TPU v7x, 32 devices: a whole 2x2x4 slice. The times are simulated.
32 devices in a mesh: blk: 16 (over z, y, core), tm: 2 (over x).
Axes of the slice: x: 2, y: 2, z: 4, core: 2. Of those that a mesh axis runs over, the one named last changes fastest.
Arguments:
- waveforms: bfloat16 [480, 16384], P(None, ('blk', 'tm')), may hold values from -60 to 60
- templates: bfloat16 [16, 480, 256], P('blk'), may hold values from -6 to 6
- station_mask: int32 [16, 160], P('blk'), may hold values 0 or 1
- channel_order: int32 [480], replicated, may hold values from 0 to 479, each once
Outputs:
- detection: float32 [16, 16384], P(None, ('blk', 'tm'))
Inputs may be any that keep to these rules, and one draw needn't show every extreme that they name: `channel_order`: each of 0 to 479 appears once.
All inputs are finite; a program needn't handle non-finite values. No bound on the sum of `station_mask` on one device may be relied on, other than what follows from the above.
Results may differ from a plain program's by a relative error of at most 0.0003.
Values may be sent and summed in bfloat16 or wider, within the bound.
No kernel may reach another device: no remote copies, remote signals or barrier semaphores. Data moves between devices by JAX's collectives and lax.ppermute only.
A program may use at most 64 MiB of HBM per device.

v0:
```python
import jax
import jax.numpy as jnp
from jax import lax
from jax.sharding import PartitionSpec as P

EPSILON = 1e-05


def shifted(block, axis, distance):
    devices = range(lax.axis_size(axis))
    route = [(i - distance, i) for i in devices if i - distance in devices]
    return lax.ppermute(block, axis, route)


def shifted_2(block, axis, distance):
    devices = range(lax.axis_size(axis))
    route = [((i - distance) % len(devices), i) for i in devices]
    return lax.ppermute(block, axis, route)


def window_sums(squares, window_len):
    running = squares
    window = 1
    while window < window_len:
        columns = running.shape[1]
        running = running[:, : columns - window] + running[:, window:]
        window = window * 2
    return running


def correlate(masked_row, extended, slab_len, window_len):
    products = lax.dot_general(
        masked_row, extended, (((0,), (0,)), ((), ())), preferred_element_type=jnp.float32
    )
    columns = extended.shape[1]
    flattened = jnp.concatenate([products.reshape(-1), jnp.zeros((window_len,), jnp.float32)])
    skewed = flattened.reshape(window_len, columns + 1)[:, :slab_len]
    return jnp.sum(skewed, axis=0)


def prepare(tpl_rows, flag_rows, onehot, window_len):
    channel_mask = jnp.dot(flag_rows.astype(jnp.float32), onehot, precision=lax.Precision.HIGHEST)
    masked = tpl_rows * channel_mask.astype(jnp.bfloat16)[:, :, None]
    tpl_norm = jnp.sqrt(jnp.sum(masked.astype(jnp.float32) ** 2, axis=(1, 2)) + EPSILON)
    live = jnp.sum(channel_mask, axis=1)
    row_scale = jnp.sqrt(window_len * live) / tpl_norm
    return (channel_mask, masked, row_scale)


def on_device(waveforms, templates, station_mask, channel_order):
    window_len = templates.shape[2]
    slab_len = waveforms.shape[1]
    group_rows = templates.shape[0]
    station_count = station_mask.shape[1]
    groups_count = lax.axis_size("blk")
    my_group = lax.axis_index("blk")
    total_rows = group_rows * groups_count
    next_edge = shifted(waveforms[:, : window_len - 1], ("blk", "tm"), -1)
    extended = jnp.concatenate([waveforms, next_edge], axis=1)
    energy = window_sums(extended.astype(jnp.float32) ** 2, window_len)
    station_of = channel_order // 3
    onehot = (jnp.arange(station_count, dtype=jnp.int32)[:, None] == station_of[None, :]).astype(
        jnp.float32
    )
    station_flags = station_mask.astype(jnp.bfloat16)

    def process(carried, tpl_rows, flag_rows, first_row):
        detect_rows, channel_rows = carried
        row_count = tpl_rows.shape[0]
        channel_mask, masked, row_scale = prepare(tpl_rows, flag_rows, onehot, window_len)
        first_row = jnp.asarray(first_row, jnp.int32)

        def one_row(row_index, detect_now):
            masked_row = lax.dynamic_index_in_dim(masked, row_index, 0, keepdims=False)
            corr_row = correlate(masked_row, extended, slab_len, window_len)
            scale_now = lax.dynamic_index_in_dim(row_scale, row_index, 0, keepdims=False)
            target = first_row + row_index
            return lax.dynamic_update_slice(
                detect_now, (corr_row * scale_now)[None, :], (target, jnp.int32(0))
            )

        detect_rows = lax.fori_loop(0, row_count, one_row, detect_rows)
        channel_rows = lax.dynamic_update_slice(
            channel_rows, channel_mask, (first_row, jnp.int32(0))
        )
        return (detect_rows, channel_rows)

    start_state = (
        jnp.zeros((total_rows, slab_len), jnp.float32),
        jnp.zeros((total_rows, extended.shape[0]), jnp.float32),
    )
    carried = process(start_state, templates, station_flags, my_group * group_rows)

    def advance(step_index, loop_state):
        carried_now, tpl_now, flag_now = loop_state
        tpl_now, flag_now = shifted_2((tpl_now, flag_now), "blk", 1)
        owner_group = (my_group - step_index) % groups_count
        carried_now = process(carried_now, tpl_now, flag_now, owner_group * group_rows)
        return (carried_now, tpl_now, flag_now)

    carried = lax.fori_loop(1, groups_count, advance, (carried, templates, station_flags))[0]
    detect_rows, channel_rows = carried
    window_energy = jnp.dot(channel_rows, energy, precision=lax.Precision.HIGHEST)
    return detect_rows / jnp.sqrt(window_energy + EPSILON)


def solution(mesh):
    placed = (P(None, ("blk", "tm")), P("blk", None, None), P("blk", None), P())
    return jax.shard_map(
        on_device, mesh=mesh, in_specs=placed, out_specs=P(None, ("blk", "tm")), check_vma=False
    )
```

profile of v0, /device:TPU:0, one launch (start us, length us, event | category | flops | bytes accessed | tf_op | source)
XLA Modules:
  0.0 219.2 jit_solution(5954258509317159606)
XLA Ops:
  2.0 1.3 collective-permute-start.2
  8.7 4.1 %collective-permute-done.2 = bf16[480,255]{1,0:T(8,128)(2,1)S(1)} collective-permute-done((bf16[480,255]{1,0:T(8,128)(2,1)S(1)}, bf16[480,255]{1,0:T(8,128)(2,1)S(1)}, u32[]{:S(2)}, u32[]{:S(2)}) %collective-permute-start.2) | collective-permute-done | bytes 244832 | tf_op jit(solution)/shard_map/ppermute | solution.py:12
  13.4 1.5 reshape.113
  14.9 1.2 concatenate.14
  17.1 1.1 slice_reduce_fusion.1
  20.9 1.4 slice_add_fusion.6
  22.4 194.0 %while.36 = (s32[]{:T(128)}, f32[16,512]{1,0:T(8,128)S(1)}, f32[16,480]{1,0:T(8,128)S(1)}, bf16[1,480,256]{2,1,0:T(8,128)(2,1)S(1)}, bf16[1,160]{1,0:T(2,128)(2,...) while((s32[]{:T(128)}, f32[16,512]{1,0:T(8,128)S(1)}, ...), condition=%wide.region_7.8_spmd.clone, body=%wide.region_3.7_spmd.clone.sunk | while | flops 190319552 | bytes 8754952 | solution.py:101
  22.5 1.9 collective-permute-start.1
  24.4 6.5 %collective-permute-done.1 = bf16[1,160]{1,0:T(2,128)(2,1)S(1)} collective-permute-done((bf16[1,160]{1,0:T(2,128)(2,1)S(1)}, bf16[1,160]{1,0:T(2,128)(2,1)S(1)}, u32[]{:S(2)}, u32[]{:S(2)}) %collective-permute-start.1) | collective-permute-done | bytes 352 | tf_op jit(solution)/shard_map/while/body/eval_jaxpr/ppermute | solution.py:18
  35.5 8.3 %collective-permute-done.1 = bf16[1,160]{1,0:T(2,128)(2,1)S(1)} collective-permute-done((bf16[1,160]{1,0:T(2,128)(2,1)S(1)}, bf16[1,160]{1,0:T(2,128)(2,1)S(1)}, u32[]{:S(2)}, u32[]{:S(2)}) %collective-permute-start.1) | collective-permute-done | bytes 352 | tf_op jit(solution)/shard_map/while/body/eval_jaxpr/ppermute | solution.py:18
  48.5 8.3 %collective-permute-done.1 = bf16[1,160]{1,0:T(2,128)(2,1)S(1)} collective-permute-done((bf16[1,160]{1,0:T(2,128)(2,1)S(1)}, bf16[1,160]{1,0:T(2,128)(2,1)S(1)}, u32[]{:S(2)}, u32[]{:S(2)}) %collective-permute-start.1) | collective-permute-done | bytes 352 | tf_op jit(solution)/shard_map/while/body/eval_jaxpr/ppermute | solution.py:18
  61.4 8.3 %collective-permute-done.1 = bf16[1,160]{1,0:T(2,128)(2,1)S(1)} collective-permute-done((bf16[1,160]{1,0:T(2,128)(2,1)S(1)}, bf16[1,160]{1,0:T(2,128)(2,1)S(1)}, u32[]{:S(2)}, u32[]{:S(2)}) %collective-permute-start.1) | collective-permute-done | bytes 352 | tf_op jit(solution)/shard_map/while/body/eval_jaxpr/ppermute | solution.py:18
  74.3 8.3 %collective-permute-done.1 = bf16[1,160]{1,0:T(2,128)(2,1)S(1)} collective-permute-done((bf16[1,160]{1,0:T(2,128)(2,1)S(1)}, bf16[1,160]{1,0:T(2,128)(2,1)S(1)}, u32[]{:S(2)}, u32[]{:S(2)}) %collective-permute-start.1) | collective-permute-done | bytes 352 | tf_op jit(solution)/shard_map/while/body/eval_jaxpr/ppermute | solution.py:18
  87.3 8.3 %collective-permute-done.1 = bf16[1,160]{1,0:T(2,128)(2,1)S(1)} collective-permute-done((bf16[1,160]{1,0:T(2,128)(2,1)S(1)}, bf16[1,160]{1,0:T(2,128)(2,1)S(1)}, u32[]{:S(2)}, u32[]{:S(2)}) %collective-permute-start.1) | collective-permute-done | bytes 352 | tf_op jit(solution)/shard_map/while/body/eval_jaxpr/ppermute | solution.py:18
  100.2 8.3 %collective-permute-done.1 = bf16[1,160]{1,0:T(2,128)(2,1)S(1)} collective-permute-done((bf16[1,160]{1,0:T(2,128)(2,1)S(1)}, bf16[1,160]{1,0:T(2,128)(2,1)S(1)}, u32[]{:S(2)}, u32[]{:S(2)}) %collective-permute-start.1) | collective-permute-done | bytes 352 | tf_op jit(solution)/shard_map/while/body/eval_jaxpr/ppermute | solution.py:18
  113.1 8.3 %collective-permute-done.1 = bf16[1,160]{1,0:T(2,128)(2,1)S(1)} collective-permute-done((bf16[1,160]{1,0:T(2,128)(2,1)S(1)}, bf16[1,160]{1,0:T(2,128)(2,1)S(1)}, u32[]{:S(2)}, u32[]{:S(2)}) %collective-permute-start.1) | collective-permute-done | bytes 352 | tf_op jit(solution)/shard_map/while/body/eval_jaxpr/ppermute | solution.py:18
  126.1 8.3 %collective-permute-done.1 = bf16[1,160]{1,0:T(2,128)(2,1)S(1)} collective-permute-done((bf16[1,160]{1,0:T(2,128)(2,1)S(1)}, bf16[1,160]{1,0:T(2,128)(2,1)S(1)}, u32[]{:S(2)}, u32[]{:S(2)}) %collective-permute-start.1) | collective-permute-done | bytes 352 | tf_op jit(solution)/shard_map/while/body/eval_jaxpr/ppermute | solution.py:18
  139.0 8.3 %collective-permute-done.1 = bf16[1,160]{1,0:T(2,128)(2,1)S(1)} collective-permute-done((bf16[1,160]{1,0:T(2,128)(2,1)S(1)}, bf16[1,160]{1,0:T(2,128)(2,1)S(1)}, u32[]{:S(2)}, u32[]{:S(2)}) %collective-permute-start.1) | collective-permute-done | bytes 352 | tf_op jit(solution)/shard_map/while/body/eval_jaxpr/ppermute | solution.py:18
  151.9 8.3 %collective-permute-done.1 = bf16[1,160]{1,0:T(2,128)(2,1)S(1)} collective-permute-done((bf16[1,160]{1,0:T(2,128)(2,1)S(1)}, bf16[1,160]{1,0:T(2,128)(2,1)S(1)}, u32[]{:S(2)}, u32[]{:S(2)}) %collective-permute-start.1) | collective-permute-done | bytes 352 | tf_op jit(solution)/shard_map/while/body/eval_jaxpr/ppermute | solution.py:18
  164.9 8.3 %collective-permute-done.1 = bf16[1,160]{1,0:T(2,128)(2,1)S(1)} collective-permute-done((bf16[1,160]{1,0:T(2,128)(2,1)S(1)}, bf16[1,160]{1,0:T(2,128)(2,1)S(1)}, u32[]{:S(2)}, u32[]{:S(2)}) %collective-permute-start.1) | collective-permute-done | bytes 352 | tf_op jit(solution)/shard_map/while/body/eval_jaxpr/ppermute | solution.py:18
  177.8 8.3 %collective-permute-done.1 = bf16[1,160]{1,0:T(2,128)(2,1)S(1)} collective-permute-done((bf16[1,160]{1,0:T(2,128)(2,1)S(1)}, bf16[1,160]{1,0:T(2,128)(2,1)S(1)}, u32[]{:S(2)}, u32[]{:S(2)}) %collective-permute-start.1) | collective-permute-done | bytes 352 | tf_op jit(solution)/shard_map/while/body/eval_jaxpr/ppermute | solution.py:18
  190.7 8.3 %collective-permute-done.1 = bf16[1,160]{1,0:T(2,128)(2,1)S(1)} collective-permute-done((bf16[1,160]{1,0:T(2,128)(2,1)S(1)}, bf16[1,160]{1,0:T(2,128)(2,1)S(1)}, u32[]{:S(2)}, u32[]{:S(2)}) %collective-permute-start.1) | collective-permute-done | bytes 352 | tf_op jit(solution)/shard_map/while/body/eval_jaxpr/ppermute | solution.py:18
  203.7 8.3 %collective-permute-done.1 = bf16[1,160]{1,0:T(2,128)(2,1)S(1)} collective-permute-done((bf16[1,160]{1,0:T(2,128)(2,1)S(1)}, bf16[1,160]{1,0:T(2,128)(2,1)S(1)}, u32[]{:S(2)}, u32[]{:S(2)}) %collective-permute-start.1) | collective-permute-done | bytes 352 | tf_op jit(solution)/shard_map/while/body/eval_jaxpr/ppermute | solution.py:18
  216.4 2.1 fusion.10
  (281 shorter events, 60.6 us)
Async XLA Ops:
  2.0 10.8 %collective-permute-start.2 = (bf16[480,255]{1,0:T(8,128)(2,1)S(1)}, bf16[480,255]{1,0:T(8,128)(2,1)S(1)}, u32[]{:S(2)}, u32[]{:S(2)}) collective-permute-start(bf16[480,255]{1,0:T(8,128)(2,1)S(1)} %slice.66), channel_id=1, source_target_pairs={{1,0},{2,1},{3,2},{4,3},{5,4},{6,5},{7,6},{8,7},{9,8},{10,9},{11,1... | collective-permute-start | bytes 734408 | tf_op jit(solution)/shard_map/ppermute | solution.py:12
  22.4 10.0 %collective-permute-start = (bf16[1,480,256]{2,1,0:T(8,128)(2,1)S(1)}, bf16[1,480,256]{2,1,0:T(8,128)(2,1)S(1)}, u32[]{:S(2)}, u32[]{:S(2)}) collective-permute-start(bf16[1,480,256]{2,1,0:T(8,128)(2,1)S(1)} %get-tuple-element.365), channel_id=1, source_target_pairs={{30,0},{0,2},{2,4},{4,6},{6,8},{8,10},{10,12},{12,14},{14,16},{16,... | collective-permute-start | bytes 737288 | tf_op jit(solution)/shard_map/while/body/eval_jaxpr/ppermute | solution.py:18
  22.5 8.4 %collective-permute-start.1 = (bf16[1,160]{1,0:T(2,128)(2,1)S(1)}, bf16[1,160]{1,0:T(2,128)(2,1)S(1)}, u32[]{:S(2)}, u32[]{:S(2)}) collective-permute-start(bf16[1,160]{1,0:T(2,128)(2,1)S(1)} %get-tuple-element.366), channel_id=1, source_target_pairs={{30,0},{0,2},{2,4},{4,6},{6,8},{8,10},{10,12},{12,14},{14,16},{16,... | collective-permute-start | bytes 968 | tf_op jit(solution)/shard_map/while/body/eval_jaxpr/ppermute | solution.py:18
  35.4 10.0 %collective-permute-start = (bf16[1,480,256]{2,1,0:T(8,128)(2,1)S(1)}, bf16[1,480,256]{2,1,0:T(8,128)(2,1)S(1)}, u32[]{:S(2)}, u32[]{:S(2)}) collective-permute-start(bf16[1,480,256]{2,1,0:T(8,128)(2,1)S(1)} %get-tuple-element.365), channel_id=1, source_target_pairs={{30,0},{0,2},{2,4},{4,6},{6,8},{8,10},{10,12},{12,14},{14,16},{16,... | collective-permute-start | bytes 737288 | tf_op jit(solution)/shard_map/while/body/eval_jaxpr/ppermute | solution.py:18
  35.4 8.4 %collective-permute-start.1 = (bf16[1,160]{1,0:T(2,128)(2,1)S(1)}, bf16[1,160]{1,0:T(2,128)(2,1)S(1)}, u32[]{:S(2)}, u32[]{:S(2)}) collective-permute-start(bf16[1,160]{1,0:T(2,128)(2,1)S(1)} %get-tuple-element.366), channel_id=1, source_target_pairs={{30,0},{0,2},{2,4},{4,6},{6,8},{8,10},{10,12},{12,14},{14,16},{16,... | collective-permute-start | bytes 968 | tf_op jit(solution)/shard_map/while/body/eval_jaxpr/ppermute | solution.py:18
  48.3 10.0 %collective-permute-start = (bf16[1,480,256]{2,1,0:T(8,128)(2,1)S(1)}, bf16[1,480,256]{2,1,0:T(8,128)(2,1)S(1)}, u32[]{:S(2)}, u32[]{:S(2)}) collective-permute-start(bf16[1,480,256]{2,1,0:T(8,128)(2,1)S(1)} %get-tuple-element.365), channel_id=1, source_target_pairs={{30,0},{0,2},{2,4},{4,6},{6,8},{8,10},{10,12},{12,14},{14,16},{16,... | collective-permute-start | bytes 737288 | tf_op jit(solution)/shard_map/while/body/eval_jaxpr/ppermute | solution.py:18
  48.4 8.4 %collective-permute-start.1 = (bf16[1,160]{1,0:T(2,128)(2,1)S(1)}, bf16[1,160]{1,0:T(2,128)(2,1)S(1)}, u32[]{:S(2)}, u32[]{:S(2)}) collective-permute-start(bf16[1,160]{1,0:T(2,128)(2,1)S(1)} %get-tuple-element.366), channel_id=1, source_target_pairs={{30,0},{0,2},{2,4},{4,6},{6,8},{8,10},{10,12},{12,14},{14,16},{16,... | collective-permute-start | bytes 968 | tf_op jit(solution)/shard_map/while/body/eval_jaxpr/ppermute | solution.py:18
  61.2 10.0 %collective-permute-start = (bf16[1,480,256]{2,1,0:T(8,128)(2,1)S(1)}, bf16[1,480,256]{2,1,0:T(8,128)(2,1)S(1)}, u32[]{:S(2)}, u32[]{:S(2)}) collective-permute-start(bf16[1,480,256]{2,1,0:T(8,128)(2,1)S(1)} %get-tuple-element.365), channel_id=1, source_target_pairs={{30,0},{0,2},{2,4},{4,6},{6,8},{8,10},{10,12},{12,14},{14,16},{16,... | collective-permute-start | bytes 737288 | tf_op jit(solution)/shard_map/while/body/eval_jaxpr/ppermute | solution.py:18
  61.3 8.4 %collective-permute-start.1 = (bf16[1,160]{1,0:T(2,128)(2,1)S(1)}, bf16[1,160]{1,0:T(2,128)(2,1)S(1)}, u32[]{:S(2)}, u32[]{:S(2)}) collective-permute-start(bf16[1,160]{1,0:T(2,128)(2,1)S(1)} %get-tuple-element.366), channel_id=1, source_target_pairs={{30,0},{0,2},{2,4},{4,6},{6,8},{8,10},{10,12},{12,14},{14,16},{16,... | collective-permute-start | bytes 968 | tf_op jit(solution)/shard_map/while/body/eval_jaxpr/ppermute | solution.py:18
  74.2 10.0 %collective-permute-start = (bf16[1,480,256]{2,1,0:T(8,128)(2,1)S(1)}, bf16[1,480,256]{2,1,0:T(8,128)(2,1)S(1)}, u32[]{:S(2)}, u32[]{:S(2)}) collective-permute-start(bf16[1,480,256]{2,1,0:T(8,128)(2,1)S(1)} %get-tuple-element.365), channel_id=1, source_target_pairs={{30,0},{0,2},{2,4},{4,6},{6,8},{8,10},{10,12},{12,14},{14,16},{16,... | collective-permute-start | bytes 737288 | tf_op jit(solution)/shard_map/while/body/eval_jaxpr/ppermute | solution.py:18
  74.2 8.4 %collective-permute-start.1 = (bf16[1,160]{1,0:T(2,128)(2,1)S(1)}, bf16[1,160]{1,0:T(2,128)(2,1)S(1)}, u32[]{:S(2)}, u32[]{:S(2)}) collective-permute-start(bf16[1,160]{1,0:T(2,128)(2,1)S(1)} %get-tuple-element.366), channel_id=1, source_target_pairs={{30,0},{0,2},{2,4},{4,6},{6,8},{8,10},{10,12},{12,14},{14,16},{16,... | collective-permute-start | bytes 968 | tf_op jit(solution)/shard_map/while/body/eval_jaxpr/ppermute | solution.py:18
  87.1 10.0 %collective-permute-start = (bf16[1,480,256]{2,1,0:T(8,128)(2,1)S(1)}, bf16[1,480,256]{2,1,0:T(8,128)(2,1)S(1)}, u32[]{:S(2)}, u32[]{:S(2)}) collective-permute-start(bf16[1,480,256]{2,1,0:T(8,128)(2,1)S(1)} %get-tuple-element.365), channel_id=1, source_target_pairs={{30,0},{0,2},{2,4},{4,6},{6,8},{8,10},{10,12},{12,14},{14,16},{16,... | collective-permute-start | bytes 737288 | tf_op jit(solution)/shard_map/while/body/eval_jaxpr/ppermute | solution.py:18
  87.2 8.4 %collective-permute-start.1 = (bf16[1,160]{1,0:T(2,128)(2,1)S(1)}, bf16[1,160]{1,0:T(2,128)(2,1)S(1)}, u32[]{:S(2)}, u32[]{:S(2)}) collective-permute-start(bf16[1,160]{1,0:T(2,128)(2,1)S(1)} %get-tuple-element.366), channel_id=1, source_target_pairs={{30,0},{0,2},{2,4},{4,6},{6,8},{8,10},{10,12},{12,14},{14,16},{16,... | collective-permute-start | bytes 968 | tf_op jit(solution)/shard_map/while/body/eval_jaxpr/ppermute | solution.py:18
  100.0 10.0 %collective-permute-start = (bf16[1,480,256]{2,1,0:T(8,128)(2,1)S(1)}, bf16[1,480,256]{2,1,0:T(8,128)(2,1)S(1)}, u32[]{:S(2)}, u32[]{:S(2)}) collective-permute-start(bf16[1,480,256]{2,1,0:T(8,128)(2,1)S(1)} %get-tuple-element.365), channel_id=1, source_target_pairs={{30,0},{0,2},{2,4},{4,6},{6,8},{8,10},{10,12},{12,14},{14,16},{16,... | collective-permute-start | bytes 737288 | tf_op jit(solution)/shard_map/while/body/eval_jaxpr/ppermute | solution.py:18
  100.1 8.4 %collective-permute-start.1 = (bf16[1,160]{1,0:T(2,128)(2,1)S(1)}, bf16[1,160]{1,0:T(2,128)(2,1)S(1)}, u32[]{:S(2)}, u32[]{:S(2)}) collective-permute-start(bf16[1,160]{1,0:T(2,128)(2,1)S(1)} %get-tuple-element.366), channel_id=1, source_target_pairs={{30,0},{0,2},{2,4},{4,6},{6,8},{8,10},{10,12},{12,14},{14,16},{16,... | collective-permute-start | bytes 968 | tf_op jit(solution)/shard_map/while/body/eval_jaxpr/ppermute | solution.py:18
  113.0 10.0 %collective-permute-start = (bf16[1,480,256]{2,1,0:T(8,128)(2,1)S(1)}, bf16[1,480,256]{2,1,0:T(8,128)(2,1)S(1)}, u32[]{:S(2)}, u32[]{:S(2)}) collective-permute-start(bf16[1,480,256]{2,1,0:T(8,128)(2,1)S(1)} %get-tuple-element.365), channel_id=1, source_target_pairs={{30,0},{0,2},{2,4},{4,6},{6,8},{8,10},{10,12},{12,14},{14,16},{16,... | collective-permute-start | bytes 737288 | tf_op jit(solution)/shard_map/while/body/eval_jaxpr/ppermute | solution.py:18
  113.0 8.4 %collective-permute-start.1 = (bf16[1,160]{1,0:T(2,128)(2,1)S(1)}, bf16[1,160]{1,0:T(2,128)(2,1)S(1)}, u32[]{:S(2)}, u32[]{:S(2)}) collective-permute-start(bf16[1,160]{1,0:T(2,128)(2,1)S(1)} %get-tuple-element.366), channel_id=1, source_target_pairs={{30,0},{0,2},{2,4},{4,6},{6,8},{8,10},{10,12},{12,14},{14,16},{16,... | collective-permute-start | bytes 968 | tf_op jit(solution)/shard_map/while/body/eval_jaxpr/ppermute | solution.py:18
  125.9 10.0 %collective-permute-start = (bf16[1,480,256]{2,1,0:T(8,128)(2,1)S(1)}, bf16[1,480,256]{2,1,0:T(8,128)(2,1)S(1)}, u32[]{:S(2)}, u32[]{:S(2)}) collective-permute-start(bf16[1,480,256]{2,1,0:T(8,128)(2,1)S(1)} %get-tuple-element.365), channel_id=1, source_target_pairs={{30,0},{0,2},{2,4},{4,6},{6,8},{8,10},{10,12},{12,14},{14,16},{16,... | collective-permute-start | bytes 737288 | tf_op jit(solution)/shard_map/while/body/eval_jaxpr/ppermute | solution.py:18
  138.8 10.0 %collective-permute-start = (bf16[1,480,256]{2,1,0:T(8,128)(2,1)S(1)}, bf16[1,480,256]{2,1,0:T(8,128)(2,1)S(1)}, u32[]{:S(2)}, u32[]{:S(2)}) collective-permute-start(bf16[1,480,256]{2,1,0:T(8,128)(2,1)S(1)} %get-tuple-element.365), channel_id=1, source_target_pairs={{30,0},{0,2},{2,4},{4,6},{6,8},{8,10},{10,12},{12,14},{14,16},{16,... | collective-permute-start | bytes 737288 | tf_op jit(solution)/shard_map/while/body/eval_jaxpr/ppermute | solution.py:18
  151.8 10.0 %collective-permute-start = (bf16[1,480,256]{2,1,0:T(8,128)(2,1)S(1)}, bf16[1,480,256]{2,1,0:T(8,128)(2,1)S(1)}, u32[]{:S(2)}, u32[]{:S(2)}) collective-permute-start(bf16[1,480,256]{2,1,0:T(8,128)(2,1)S(1)} %get-tuple-element.365), channel_id=1, source_target_pairs={{30,0},{0,2},{2,4},{4,6},{6,8},{8,10},{10,12},{12,14},{14,16},{16,... | collective-permute-start | bytes 737288 | tf_op jit(solution)/shard_map/while/body/eval_jaxpr/ppermute | solution.py:18
  164.7 10.0 %collective-permute-start = (bf16[1,480,256]{2,1,0:T(8,128)(2,1)S(1)}, bf16[1,480,256]{2,1,0:T(8,128)(2,1)S(1)}, u32[]{:S(2)}, u32[]{:S(2)}) collective-permute-start(bf16[1,480,256]{2,1,0:T(8,128)(2,1)S(1)} %get-tuple-element.365), channel_id=1, source_target_pairs={{30,0},{0,2},{2,4},{4,6},{6,8},{8,10},{10,12},{12,14},{14,16},{16,... | collective-permute-start | bytes 737288 | tf_op jit(solution)/shard_map/while/body/eval_jaxpr/ppermute | solution.py:18
  177.6 10.0 %collective-permute-start = (bf16[1,480,256]{2,1,0:T(8,128)(2,1)S(1)}, bf16[1,480,256]{2,1,0:T(8,128)(2,1)S(1)}, u32[]{:S(2)}, u32[]{:S(2)}) collective-permute-start(bf16[1,480,256]{2,1,0:T(8,128)(2,1)S(1)} %get-tuple-element.365), channel_id=1, source_target_pairs={{30,0},{0,2},{2,4},{4,6},{6,8},{8,10},{10,12},{12,14},{14,16},{16,... | collective-permute-start | bytes 737288 | tf_op jit(solution)/shard_map/while/body/eval_jaxpr/ppermute | solution.py:18
  190.6 10.0 %collective-permute-start = (bf16[1,480,256]{2,1,0:T(8,128)(2,1)S(1)}, bf16[1,480,256]{2,1,0:T(8,128)(2,1)S(1)}, u32[]{:S(2)}, u32[]{:S(2)}) collective-permute-start(bf16[1,480,256]{2,1,0:T(8,128)(2,1)S(1)} %get-tuple-element.365), channel_id=1, source_target_pairs={{30,0},{0,2},{2,4},{4,6},{6,8},{8,10},{10,12},{12,14},{14,16},{16,... | collective-permute-start | bytes 737288 | tf_op jit(solution)/shard_map/while/body/eval_jaxpr/ppermute | solution.py:18
  203.5 10.0 %collective-permute-start = (bf16[1,480,256]{2,1,0:T(8,128)(2,1)S(1)}, bf16[1,480,256]{2,1,0:T(8,128)(2,1)S(1)}, u32[]{:S(2)}, u32[]{:S(2)}) collective-permute-start(bf16[1,480,256]{2,1,0:T(8,128)(2,1)S(1)} %get-tuple-element.365), channel_id=1, source_target_pairs={{30,0},{0,2},{2,4},{4,6},{6,8},{8,10},{10,12},{12,14},{14,16},{16,... | collective-permute-start | bytes 737288 | tf_op jit(solution)/shard_map/while/body/eval_jaxpr/ppermute | solution.py:18
  (8 other events, 67.1 us)
where the time goes:
time: 220 us; the launch traced here: 219 us
  waiting for transfers between devices  126 us (57%)
  other arithmetic  30.6 us (14%)
  local copies, waits for them, and re-layouts  20.6 us (9%)
  loops' own time  20.3 us (9%)
  matrix products  14.9 us (7%)
  starting transfers between devices  4.83 us (2%)
    ppermute x30, waiting for transfers between devices, shifted_2(): return lax.ppermute(block, axis, route)  122 us
    another operation x1, loops' own time, on_device(): lax.fori_loop(1, groups_count, advance, (carried, templates, station_flags))  20.3 us
    reduce_sum x16, other arithmetic, prepare(): jnp.sum(masked.astype(jnp.float32) ** 2, axis=(1, 2)) + EPSILON  12.7 us
    reshape x16, local copies, waits for them, and re-layouts, correlate(): products.reshape(-1)  11 us
    reduce_sum x16, other arithmetic, prepare(): live = jnp.sum(channel_mask, axis=1)  9.59 us
    dot_general x16, matrix products, correlate(): lax.dot_general(masked_row, extended, (((0,), (0,)), ((), ())), preferred...  8.1 us
    dot_general x16, matrix products, prepare(): jnp.dot(flag_rows.astype(jnp.float32), onehot, precision=lax.Precision.HI...  4.65 us
  transfers between devices with their start and end apart: 31, of which 16 were waited for; matrix products, arithmetic and copies ran while one was open for 8% of the time, Pallas kernels for 0%

commit v1 on v0

v1 whole, which is shorter than its diff:
```python
import functools

import jax
import jax.numpy as jnp
from jax import lax
from jax.experimental import pallas as pl
from jax.experimental.pallas import tpu as pltpu
from jax.sharding import PartitionSpec as P

EPSILON = 1e-05
LANES = 128
INNER = 4
FINE = 16
VMEM_BYTES = 40 * 1024 * 1024

BF16 = jnp.bfloat16
F32 = jnp.float32


def call(kernel, out_shape, scratch=(), flops=0, bytes_accessed=0):
    return pl.pallas_call(
        kernel,
        out_shape=out_shape,
        scratch_shapes=list(scratch),
        compiler_params=pltpu.CompilerParams(vmem_limit_bytes=VMEM_BYTES),
        cost_estimate=pl.CostEstimate(
            flops=flops, bytes_accessed=bytes_accessed, transcendentals=0
        ),
    )


def one_hot(order_row, station_count):
    columns = order_row.shape[1]
    first = 3 * lax.broadcasted_iota(jnp.int32, (station_count, columns), 0)
    hit = (order_row >= first) & (order_row < first + 3)
    return jnp.where(hit, 1.0, 0.0).astype(BF16)


def template_kernel(tm_count, tpl_ref, flag_ref, order_ref, *refs):
    outs, meta_ref = refs[:INNER], refs[INNER]
    tpl_pad, order_pad, turned = refs[INNER + 1 :]
    channels, window = tpl_ref.shape[1:]
    stations = flag_ref.shape[1]
    padded = tpl_pad.shape[0]
    part = LANES // tm_count
    tpl_pad[channels:, :] = jnp.zeros((padded - channels, window), BF16)
    tpl_pad[:channels, :] = tpl_ref[0]
    order_pad[...] = jnp.full((1, padded), -1, jnp.int32)
    order_pad[:, :channels] = order_ref[...]
    flags = jnp.broadcast_to(flag_ref[...].astype(F32), (8, stations))
    mask = jnp.dot(
        flags.astype(BF16), one_hot(order_pad[...], stations), preferred_element_type=F32
    )
    masked = tpl_pad[...].T * mask[:1].astype(BF16)
    turned[...] = masked
    wide = masked.astype(F32)
    norm = jnp.sqrt(jnp.sum(wide * wide, keepdims=True) + EPSILON)
    live = jnp.sum(mask[:1], keepdims=True)
    meta_ref[...] = jnp.broadcast_to(jnp.sqrt(window * live) / norm, meta_ref.shape)
    meta_ref[:, :stations] = flags[:1]
    my_inner = lax.rem(lax.axis_index("blk"), INNER)
    my_tm = lax.axis_index("tm")
    spot = lax.broadcasted_iota(jnp.int32, (FINE, LANES), 1) // part
    for flip in range(INNER):
        start = pl.multiple_of((my_inner ^ flip) * LANES, LANES)
        for step in range(window // (FINE * tm_count)):
            tile = jnp.zeros((FINE, LANES), F32)
            for within in range(tm_count):
                row = FINE * (step * tm_count + within)
                chunk = turned[row : row + FINE, pl.ds(start, LANES)].astype(F32)
                turn = lax.rem(part * (within - my_tm) + LANES, LANES)
                tile = jnp.where(spot == within, pltpu.roll(chunk, turn, 1), tile)
            outs[flip][FINE * step : FINE * (step + 1), :] = tile.astype(BF16)


def wave_kernel(group, tm_count, wave_ref, *refs):
    outs, wave_pad = refs[:group], refs[group]
    channels, slab = wave_ref.shape
    padded = wave_pad.shape[0]
    part = padded // group
    wave_pad[channels:, :] = jnp.zeros((padded - channels, slab), BF16)
    wave_pad[:channels, :] = wave_ref[...]
    me = lax.rem(lax.axis_index("blk"), INNER) * tm_count + lax.axis_index("tm")
    for flip in range(group):
        start = pl.multiple_of((me ^ flip) * part, part)
        outs[flip][...] = wave_pad[pl.ds(start, part), :]


def head_kernel(group, tm_count, *refs):
    parts, out_ref = refs[:group], refs[group]
    me = lax.rem(lax.axis_index("blk"), INNER) * tm_count + lax.axis_index("tm")
    for flip in range(group):

        @pl.when(me == flip)
        def _():
            out_ref[...] = parts[flip][:, : out_ref.shape[1]]


def shift_kernel(group, tm_count, *refs):
    parts, halo_ref, out_ref, joined = refs[:group], refs[group], refs[group + 1], refs[group + 2]
    part, slab = parts[0].shape
    me = lax.rem(lax.axis_index("blk"), INNER) * tm_count + lax.axis_index("tm")
    for flip in range(group):
        start = pl.multiple_of((me ^ flip) * slab, slab)
        joined[:, pl.ds(start, slab)] = parts[flip][...].astype(F32)
    joined[:, group * slab :] = halo_ref[...].astype(F32)
    columns = joined.shape[1]
    for copy in range(LANES // FINE):
        rows = slice(copy * part, (copy + 1) * part)
        if copy == 0:
            out_ref[rows, :] = joined[...].astype(BF16)
        else:
            out_ref[rows, :] = pltpu.roll(joined[...], columns - FINE * copy, 1).astype(BF16)


def dots_kernel(group, tm_count, *refs):
    count = lax.axis_size("blk")
    tpls, shifts, outs = refs[:count], refs[count], refs[count + 1 : count + 1 + group]
    left, products, gathered = refs[count + 1 + group :]
    my_blk = lax.axis_index("blk")
    me = lax.rem(my_blk, INNER) * tm_count + lax.axis_index("tm")
    per_half = left.shape[2] // LANES
    for flip in range(count):
        row = pl.multiple_of((my_blk ^ flip) * FINE, FINE)
        for step in range(2 * per_half):
            lane = (step % per_half) * LANES
            left[step // per_half, pl.ds(row, FINE), lane : lane + LANES] = tpls[flip][
                FINE * step : FINE * (step + 1), :
            ]
    slab = gathered.shape[2]
    tiles = products.shape[0]
    span = (tiles - 1) * LANES
    per_block = span // slab

    def block(index, carry):
        start = pl.multiple_of(index * span, span)
        product = jnp.dot(
            left[0], shifts[:, pl.ds(start, span + LANES)], preferred_element_type=F32
        ) + jnp.dot(
            left[1],
            shifts[:, pl.ds(pl.multiple_of(start + LANES, LANES), span + LANES)],
            preferred_element_type=F32,
        )
        for tile in range(tiles):
            products[tile] = product[:, tile * LANES : (tile + 1) * LANES]

        def fine_rows(fine):
            return jnp.concatenate(
                [products[tile, pl.ds(fine, count, stride=FINE), :] for tile in range(tiles)],
                axis=1,
            )

        total = fine_rows(FINE - 1)
        for fine in reversed(range(FINE - 1)):
            total = fine_rows(fine) + pltpu.roll(total, span + LANES - 1, 1)
        for piece in range(per_block):
            gathered[index * per_block + piece] = total[:, piece * slab : (piece + 1) * slab]
        return carry

    lax.fori_loop(0, group // per_block, block, 0)
    for flip in range(group):
        outs[flip][...] = gathered[me ^ flip]


def power_kernel(wave_ref, meta_ref, order_ref, out_ref, head_ref):
    stations = meta_ref.shape[1]
    mask = jnp.dot(
        meta_ref[...].astype(BF16), one_hot(order_ref[...], stations), preferred_element_type=F32
    ).astype(BF16)
    wave = wave_ref[...].astype(F32)
    squares = wave * wave
    high = squares.astype(BF16)
    low = (squares - high.astype(F32)).astype(BF16)
    power = jnp.dot(mask, high, preferred_element_type=F32) + jnp.dot(
        mask, low, preferred_element_type=F32
    )
    out_ref[...] = power
    head_ref[...] = power[:, : head_ref.shape[1]]


def factor_kernel(power_ref, halo_ref, scale_ref, out_ref, joined):
    slab, window = power_ref.shape[1], halo_ref.shape[1]
    joined[:, :slab] = power_ref[...]
    joined[:, slab:] = halo_ref[...]
    running = joined[...]
    columns = running.shape[1]
    width = 1
    while width < window:
        running = running + pltpu.roll(running, columns - width, 1)
        width *= 2
    out_ref[...] = scale_ref[:, :1] / jnp.sqrt(running[:, :slab] + EPSILON)


def finish_kernel(*refs):
    parts, factor_ref, out_ref = refs[:-2], refs[-2], refs[-1]
    total = parts[0][...]
    for part in parts[1:]:
        total = total + part[...]
    out_ref[...] = total * factor_ref[...]


def on_device(waveforms, templates, station_mask, channel_order):
    channels, slab = waveforms.shape
    rows, _, window = templates.shape
    stations = station_mask.shape[1]
    blk_count, tm_count = lax.axis_size("blk"), lax.axis_size("tm")
    assert rows == 1 and LANES % tm_count == 0
    group = INNER * tm_count
    padded = INNER * LANES
    part = padded // group
    chunk = group * slab
    span = 2 * slab
    both = ("blk", "tm")
    sds = jax.ShapeDtypeStruct
    order_row = channel_order[None, :]

    *tpl_parts, meta = call(
        functools.partial(template_kernel, tm_count),
        [sds((window * part // LANES, LANES), BF16)] * INNER + [sds((1, 2 * LANES), F32)],
        [
            pltpu.VMEM((padded, window), BF16),
            pltpu.VMEM((1, padded), jnp.int32),
            pltpu.VMEM((window, padded), BF16),
        ],
        bytes_accessed=channels * window * 2,
    )(templates, station_mask, order_row)
    tpls = [tpl_parts[0]]
    for flip in range(1, blk_count):
        route = [(b, b ^ flip) for b in range(blk_count)]
        tpls.append(lax.ppermute(tpl_parts[flip % INNER], "blk", route))

    wave_parts = call(
        functools.partial(wave_kernel, group, tm_count),
        [sds((part, slab), BF16)] * group,
        [pltpu.VMEM((padded, slab), BF16)],
        bytes_accessed=channels * slab * 4,
    )(waveforms)
    total = blk_count * tm_count
    routes = [[(i, i ^ flip) for i in range(total)] for flip in range(group)]
    waves = [wave_parts[0]]
    for flip in range(1, group):
        waves.append(lax.ppermute(wave_parts[flip], both, routes[flip]))

    meta_all = lax.all_gather(meta, "blk", axis=0, tiled=True)
    power, power_head = call(
        power_kernel,
        [sds((blk_count, slab), F32), sds((blk_count, window), F32)],
        flops=4 * blk_count * channels * slab,
        bytes_accessed=channels * slab * 2,
    )(waveforms, meta_all[:, :stations], order_row)
    power_halo = lax.ppermute(power_head, both, [(i, i - 1) for i in range(1, total)])
    factor = call(
        factor_kernel,
        sds((blk_count, slab), F32),
        [pltpu.VMEM((blk_count, slab + window), F32)],
        bytes_accessed=blk_count * slab * 8,
    )(power, power_halo, meta_all[:, stations:])

    head = call(
        functools.partial(head_kernel, group, tm_count),
        sds((part, window), BF16),
        bytes_accessed=chunk * part * 2,
    )(*waves)
    halo = lax.ppermute(head, "blk", [(b, b - INNER) for b in range(INNER, blk_count)])
    copies = LANES // FINE
    shifts = call(
        functools.partial(shift_kernel, group, tm_count),
        sds((copies * part, chunk + window), BF16),
        [pltpu.VMEM((part, chunk + window), F32)],
        bytes_accessed=chunk * part * 2 * (copies + 1),
    )(*waves, halo)

    partials = call(
        functools.partial(dots_kernel, group, tm_count),
        [sds((blk_count, slab), F32)] * group,
        [
            pltpu.VMEM((2, blk_count * FINE, copies * part), BF16),
            pltpu.VMEM((span // LANES + 1, blk_count * FINE, LANES), F32),
            pltpu.VMEM((group, blk_count, slab), F32),
        ],
        flops=2 * blk_count * window * part * chunk,
        bytes_accessed=copies * part * chunk * 2,
    )(*tpls, shifts)
    sums = [partials[0]]
    for flip in range(1, group):
        sums.append(lax.ppermute(partials[flip], both, routes[flip]))
    return call(
        finish_kernel, sds((blk_count, slab), F32), bytes_accessed=blk_count * slab * 4 * (group + 2)
    )(*sums, factor)


def solution(mesh):
    placed = (P(None, ("blk", "tm")), P("blk", None, None), P("blk", None), P())
    return jax.shard_map(
        on_device, mesh=mesh, in_specs=placed, out_specs=P(None, ("blk", "tm")), check_vma=False
    )
```

time: 220 us -> 82.6 us (0.38)
  waiting for transfers between devices: 126 us -> 6.71 us
  starting transfers between devices: 4.83 us -> 41.2 us
  other arithmetic: 30.6 us -> 0 us
  loops' own time: 20.3 us -> 0 us
  blocking collectives: 0 us -> 19.7 us
  local copies, waits for them, and re-layouts: 20.6 us -> 3.42 us
  matrix products: 14.9 us -> 0 us
  Pallas kernels: 0 us -> 11.1 us
    ppermute x31, waiting for transfers between devices: 126 us -> 6.71 us  [the longest x7 2.76 us: on_device(): sums.append(lax.ppermute(partials[flip], both, routes[flip]))]
    ppermute x31, starting transfers between devices: 4.83 us -> 41.2 us  [the longest x15 23.7 us: on_device(): tpls.append(lax.ppermute(tpl_parts[flip % INNER], 'blk', route))]
    reduce_sum x48 -> x0, other arithmetic: 24.3 us -> none  [the longest x16 12.7 us: prepare(): jnp.sum(masked.astype(jnp.float32) ** 2, axis=(1, 2)) + EPSILON]
    another operation x1 -> x0, loops' own time: 20.3 us -> none  [on_device(): lax.fori_loop(1, groups_count, advance, (carried, templates, station_flags))]
    all_gather x0 -> x1, blocking collectives: none -> 19.7 us  [on_device(): meta_all = lax.all_gather(meta, 'blk', axis=0, tiled=True)]
    dot_general x33 -> x0, matrix products: 14.9 us -> none  [the longest x16 8.1 us: correlate(): lax.dot_general(masked_row, extended, (((0,), (0,)), ((), ())), preferred...]
    reshape x32 -> x0, local copies, waits for them, and re-layouts: 14.3 us -> none  [the longest x16 11 us: correlate(): products.reshape(-1)]
    pallas_call x0 -> x8, Pallas kernels: none -> 11.1 us  [the longest x1 7.9 us: on_device(): call(functools.partial(dots_kernel, group, tm_count), [sds((blk_count, sl...]
  transfers between devices with their start and end apart: 31 -> 31, of which waited for: 16 -> 5; matrix products, arithmetic and copies ran while one was open for 8% -> 0% of each run, Pallas kernels for 0% -> 3%
where the time goes in v1:
time: 82.6 us; the launch traced here: 82.4 us
  starting transfers between devices  41.2 us (50%)
  blocking collectives  19.7 us (24%)
  Pallas kernels  11.1 us (13%)
  waiting for transfers between devices  6.71 us (8%)
  local copies, waits for them, and re-layouts  3.42 us (4%)
    ppermute x15, starting transfers between devices, on_device(): tpls.append(lax.ppermute(tpl_parts[flip % INNER], 'blk', route))  23.7 us
    all_gather x1, blocking collectives, on_device(): meta_all = lax.all_gather(meta, 'blk', axis=0, tiled=True)  19.7 us
    ppermute x7, starting transfers between devices, on_device(): waves.append(lax.ppermute(wave_parts[flip], both, routes[flip]))  8.03 us
    pallas_call x1, Pallas kernels, on_device(): call(functools.partial(dots_kernel, group, tm_count), [sds((blk_count, sl...  7.9 us
    ppermute x7, starting transfers between devices, on_device(): sums.append(lax.ppermute(partials[flip], both, routes[flip]))  6.94 us
    unnamed x13, local copies, waits for them, and re-layouts  3.35 us
    ppermute x7, waiting for transfers between devices, on_device(): sums.append(lax.ppermute(partials[flip], both, routes[flip]))  2.76 us
    ppermute x15, waiting for transfers between devices, on_device(): tpls.append(lax.ppermute(tpl_parts[flip % INNER], 'blk', route))  2 us
  transfers between devices with their start and end apart: 31, of which 5 were waited for; matrix products, arithmetic and copies ran while one was open for 0% of the time, Pallas kernels for 3%

profile of v1, /device:TPU:0, one launch (start us, length us, event | category | flops | bytes accessed | tf_op | source)
XLA Modules:
  0.0 82.4 jit_solution(9917604901708100364)
XLA Ops:
  1.1 3.0 %collective-permute-start.15 = (bf16[64,512]{1,0:T(8,128)(2,1)S(1)}, bf16[64,512]{1,0:T(8,128)(2,1)S(1)}, u32[]{:S(2)}, u32[]{:S(2)}) collective-permute-start(bf16[64,512]{1,0:T(8,128)(2,1)S(1)} %get-tuple-element.33), channel_id=1, source_target_pairs={{0,1},{1,0},{2,3},{3,2},{4,5},{5,4},{6,7},{7,6},{8,9},{9,8},{10,11... | collective-permute-start | bytes 196616 | tf_op jit(solution)/shard_map/ppermute | solution.py:242
  7.5 1.7 %collective-permute-start.18 = (bf16[64,512]{1,0:T(8,128)(2,1)S(1)}, bf16[64,512]{1,0:T(8,128)(2,1)S(1)}, u32[]{:S(2)}, u32[]{:S(2)}) collective-permute-start(bf16[64,512]{1,0:T(8,128)(2,1)S(1)} %get-tuple-element.36), channel_id=1, source_target_pairs={{0,4},{1,5},{2,6},{3,7},{4,0},{5,1},{6,2},{7,3},{8,12},{9,13},{10,... | collective-permute-start | bytes 196616 | tf_op jit(solution)/shard_map/ppermute | solution.py:242
  9.2 1.4 %collective-permute-start.19 = (bf16[64,512]{1,0:T(8,128)(2,1)S(1)}, bf16[64,512]{1,0:T(8,128)(2,1)S(1)}, u32[]{:S(2)}, u32[]{:S(2)}) collective-permute-start(bf16[64,512]{1,0:T(8,128)(2,1)S(1)} %get-tuple-element.37), channel_id=1, source_target_pairs={{0,5},{1,4},{2,7},{3,6},{4,1},{5,0},{6,3},{7,2},{8,13},{9,12},{10,... | collective-permute-start | bytes 196616 | tf_op jit(solution)/shard_map/ppermute | solution.py:242
  12.5 1.4 %collective-permute-start.1 = (bf16[128,128]{1,0:T(8,128)(2,1)S(1)}, bf16[128,128]{1,0:T(8,128)(2,1)S(1)}, u32[]{:S(2)}, u32[]{:S(2)}) collective-permute-start(bf16[128,128]{1,0:T(8,128)(2,1)S(1)} %get-tuple-element.30), channel_id=1, source_target_pairs={{0,4},{2,6},{4,0},{6,2},{8,12},{10,14},{12,8},{14,10},{16,20},{18,... | collective-permute-start | bytes 98312 | tf_op jit(solution)/shard_map/ppermute | solution.py:230
  13.9 2.1 %collective-permute-start.10 = (bf16[128,128]{1,0:T(8,128)(2,1)S(1)}, bf16[128,128]{1,0:T(8,128)(2,1)S(1)}, u32[]{:S(2)}, u32[]{:S(2)}) collective-permute-start(bf16[128,128]{1,0:T(8,128)(2,1)S(1)} %get-tuple-element.31), channel_id=1, source_target_pairs={{0,22},{2,20},{4,18},{6,16},{8,30},{10,28},{12,26},{14,24},{16,6},... | collective-permute-start | bytes 98312 | tf_op jit(solution)/shard_map/ppermute | solution.py:230
  15.9 2.1 %collective-permute-start.11 = (bf16[128,128]{1,0:T(8,128)(2,1)S(1)}, bf16[128,128]{1,0:T(8,128)(2,1)S(1)}, u32[]{:S(2)}, u32[]{:S(2)}) collective-permute-start(bf16[128,128]{1,0:T(8,128)(2,1)S(1)} %get-tuple-element.28.refs_0_), channel_id=1, source_target_pairs={{0,24},{2,26},{4,28},{6,30},{8,16},{10,18},{12,20},{14,22},{16,8},... | collective-permute-start | bytes 98312 | tf_op jit(solution)/shard_map/ppermute | solution.py:230
  18.1 2.1 %collective-permute-start.12 = (bf16[128,128]{1,0:T(8,128)(2,1)S(1)}, bf16[128,128]{1,0:T(8,128)(2,1)S(1)}, u32[]{:S(2)}, u32[]{:S(2)}) collective-permute-start(bf16[128,128]{1,0:T(8,128)(2,1)S(1)} %get-tuple-element.29), channel_id=1, source_target_pairs={{0,26},{2,24},{4,30},{6,28},{8,18},{10,16},{12,22},{14,20},{16,10}... | collective-permute-start | bytes 98312 | tf_op jit(solution)/shard_map/ppermute | solution.py:230
  20.2 1.8 %collective-permute-start.13 = (bf16[128,128]{1,0:T(8,128)(2,1)S(1)}, bf16[128,128]{1,0:T(8,128)(2,1)S(1)}, u32[]{:S(2)}, u32[]{:S(2)}) collective-permute-start(bf16[128,128]{1,0:T(8,128)(2,1)S(1)} %get-tuple-element.30), channel_id=1, source_target_pairs={{0,28},{2,30},{4,24},{6,26},{8,20},{10,22},{12,16},{14,18},{16,12}... | collective-permute-start | bytes 98312 | tf_op jit(solution)/shard_map/ppermute | solution.py:230
  22.0 2.3 %collective-permute-start.14 = (bf16[128,128]{1,0:T(8,128)(2,1)S(1)}, bf16[128,128]{1,0:T(8,128)(2,1)S(1)}, u32[]{:S(2)}, u32[]{:S(2)}) collective-permute-start(bf16[128,128]{1,0:T(8,128)(2,1)S(1)} %get-tuple-element.31), channel_id=1, source_target_pairs={{0,30},{2,28},{4,26},{6,24},{8,22},{10,20},{12,18},{14,16},{16,14}... | collective-permute-start | bytes 98312 | tf_op jit(solution)/shard_map/ppermute | solution.py:230
  24.3 1.3 %collective-permute-start.2 = (bf16[128,128]{1,0:T(8,128)(2,1)S(1)}, bf16[128,128]{1,0:T(8,128)(2,1)S(1)}, u32[]{:S(2)}, u32[]{:S(2)}) collective-permute-start(bf16[128,128]{1,0:T(8,128)(2,1)S(1)} %get-tuple-element.31), channel_id=1, source_target_pairs={{0,6},{2,4},{4,2},{6,0},{8,14},{10,12},{12,10},{14,8},{16,22},{18,... | collective-permute-start | bytes 98312 | tf_op jit(solution)/shard_map/ppermute | solution.py:230
  25.7 1.5 %collective-permute-start.4 = (bf16[128,128]{1,0:T(8,128)(2,1)S(1)}, bf16[128,128]{1,0:T(8,128)(2,1)S(1)}, u32[]{:S(2)}, u32[]{:S(2)}) collective-permute-start(bf16[128,128]{1,0:T(8,128)(2,1)S(1)} %get-tuple-element.29), channel_id=1, source_target_pairs={{0,10},{2,8},{4,14},{6,12},{8,2},{10,0},{12,6},{14,4},{16,26},{18,... | collective-permute-start | bytes 98312 | tf_op jit(solution)/shard_map/ppermute | solution.py:230
  27.2 1.3 %collective-permute-start.22 = (bf16[64,256]{1,0:T(8,128)(2,1)S(1)}, bf16[64,256]{1,0:T(8,128)(2,1)S(1)}, u32[]{:S(2)}, u32[]{:S(2)}) collective-permute-start(bf16[64,256]{1,0:T(8,128)(2,1)S(1)} %shard_map.48), channel_id=1, source_target_pairs={{8,0},{10,2},{12,4},{14,6},{16,8},{18,10},{20,12},{22,14},{24,16},... | collective-permute-start | bytes 98312 | tf_op jit(solution)/shard_map/ppermute | solution.py:264
  28.5 2.8 %collective-permute-start.5 = (bf16[128,128]{1,0:T(8,128)(2,1)S(1)}, bf16[128,128]{1,0:T(8,128)(2,1)S(1)}, u32[]{:S(2)}, u32[]{:S(2)}) collective-permute-start(bf16[128,128]{1,0:T(8,128)(2,1)S(1)} %get-tuple-element.30), channel_id=1, source_target_pairs={{0,12},{2,14},{4,8},{6,10},{8,4},{10,6},{12,0},{14,2},{16,28},{18,... | collective-permute-start | bytes 98312 | tf_op jit(solution)/shard_map/ppermute | solution.py:230
  31.7 1.6 %collective-permute-start.7 = (bf16[128,128]{1,0:T(8,128)(2,1)S(1)}, bf16[128,128]{1,0:T(8,128)(2,1)S(1)}, u32[]{:S(2)}, u32[]{:S(2)}) collective-permute-start(bf16[128,128]{1,0:T(8,128)(2,1)S(1)} %get-tuple-element.28.refs_0_), channel_id=1, source_target_pairs={{0,16},{2,18},{4,20},{6,22},{8,24},{10,26},{12,28},{14,30},{16,0},... | collective-permute-start | bytes 98312 | tf_op jit(solution)/shard_map/ppermute | solution.py:230
  34.1 2.9 %collective-permute-start.9 = (bf16[128,128]{1,0:T(8,128)(2,1)S(1)}, bf16[128,128]{1,0:T(8,128)(2,1)S(1)}, u32[]{:S(2)}, u32[]{:S(2)}) collective-permute-start(bf16[128,128]{1,0:T(8,128)(2,1)S(1)} %get-tuple-element.30), channel_id=1, source_target_pairs={{0,20},{2,22},{4,16},{6,18},{8,28},{10,30},{12,24},{14,26},{16,4},... | collective-permute-start | bytes 98312 | tf_op jit(solution)/shard_map/ppermute | solution.py:230
  40.1 7.9 %shard_map.50 = (f32[16,512]{1,0:T(8,128)S(1)}, f32[16,512]{1,0:T(8,128)S(1)}, f32[16,512]{1,0:T(8,128)S(1)}, f32[16,512]{1,0:T(8,128)S(1)}, f32[16,512]{1,0:T(8...) custom-call(bf16[128,128]{1,0:T(8,128)(2,1)S(1)} %get-tuple-element.28.refs_0_, ...), custom_call_target="tpu_custom_call" | custom-call | flops 2147483648 | bytes 4194304 | tf_op jit(solution)/shard_map/pallas_call | solution.py:273
  48.0 1.8 %collective-permute-start.23 = (f32[16,512]{1,0:T(8,128)S(1)}, f32[16,512]{1,0:T(8,128)S(1)}, u32[]{:S(2)}, u32[]{:S(2)}) collective-permute-start(f32[16,512]{1,0:T(8,128)S(1)} %get-tuple-element.41), channel_id=1, source_target_pairs={{0,1},{1,0},{2,3},{3,2},{4,5},{5,4},{6,7},{7,6},{8,9},{9,8},{10,11... | collective-permute-start | bytes 98312 | tf_op jit(solution)/shard_map/ppermute | solution.py:286
  49.9 19.7 %all-gather = f32[16,1,256]{2,1,0:T(1,128)S(1)} all-gather(f32[1,1,256]{2,1,0:T(1,128)S(1)} %bitcast.10), channel_id=1, replica_groups=mesh['blk'=16,'tm'=2] {'blk'}, dimensions={0}, use_global_device_ids=true | all-gather | bytes 17408 | tf_op jit(solution)/shard_map/all_gather | solution.py:244
  70.0 1.3 %collective-permute-start.30 = (f32[16,256]{1,0:T(8,128)S(1)}, f32[16,256]{1,0:T(8,128)S(1)}, u32[]{:S(2)}, u32[]{:S(2)}) collective-permute-start(f32[16,256]{1,0:T(8,128)S(1)} %get-tuple-element.50), channel_id=1, source_target_pairs={{1,0},{2,1},{3,2},{4,3},{5,4},{6,5},{7,6},{8,7},{9,8},{10,9},{11,1... | collective-permute-start | bytes 49160 | tf_op jit(solution)/shard_map/ppermute | solution.py:251
  71.3 2.4 %collective-permute-start.25 = (f32[16,512]{1,0:T(8,128)S(1)}, f32[16,512]{1,0:T(8,128)S(1)}, u32[]{:S(2)}, u32[]{:S(2)}) collective-permute-start(f32[16,512]{1,0:T(8,128)S(1)} %get-tuple-element.43), channel_id=1, source_target_pairs={{0,3},{1,2},{2,1},{3,0},{4,7},{5,6},{6,5},{7,4},{8,11},{9,10},{10,... | collective-permute-start | bytes 98312 | tf_op jit(solution)/shard_map/ppermute | solution.py:286
  73.7 1.9 %collective-permute-done.30.halo_ref = f32[16,256]{1,0:T(8,128)S(1)} collective-permute-done((f32[16,256]{1,0:T(8,128)S(1)}, f32[16,256]{1,0:T(8,128)S(1)}, u32[]{:S(2)}, u32[]{:S(2)}) %collective-permute-start.30) | collective-permute-done | bytes 16416 | tf_op jit(solution)/shard_map/ppermute | solution.py:251
  75.6 1.7 %collective-permute-start.28 = (f32[16,512]{1,0:T(8,128)S(1)}, f32[16,512]{1,0:T(8,128)S(1)}, u32[]{:S(2)}, u32[]{:S(2)}) collective-permute-start(f32[16,512]{1,0:T(8,128)S(1)} %get-tuple-element.46), channel_id=1, source_target_pairs={{0,6},{1,7},{2,4},{3,5},{4,2},{5,3},{6,0},{7,1},{8,14},{9,15},{10,... | collective-permute-start | bytes 98312 | tf_op jit(solution)/shard_map/ppermute | solution.py:286
  79.0 1.5 %collective-permute-done.27.refs_5_ = f32[16,512]{1,0:T(8,128)S(1)} collective-permute-done((f32[16,512]{1,0:T(8,128)S(1)}, f32[16,512]{1,0:T(8,128)S(1)}, u32[]{:S(2)}, u32[]{:S(2)}) %collective-permute-start.27) | collective-permute-done | bytes 32800 | tf_op jit(solution)/shard_map/ppermute | solution.py:286
  80.5 1.3 %collective-permute-done.29.refs_7_ = f32[16,512]{1,0:T(8,128)S(1)} collective-permute-done((f32[16,512]{1,0:T(8,128)S(1)}, f32[16,512]{1,0:T(8,128)S(1)}, u32[]{:S(2)}, u32[]{:S(2)}) %collective-permute-start.29) | collective-permute-done | bytes 32800 | tf_op jit(solution)/shard_map/ppermute | solution.py:286
  (61 shorter events, 13.4 us)
Async XLA Ops:
  1.1 9.5 %collective-permute-start.15 = (bf16[64,512]{1,0:T(8,128)(2,1)S(1)}, bf16[64,512]{1,0:T(8,128)(2,1)S(1)}, u32[]{:S(2)}, u32[]{:S(2)}) collective-permute-start(bf16[64,512]{1,0:T(8,128)(2,1)S(1)} %get-tuple-element.33), channel_id=1, source_target_pairs={{0,1},{1,0},{2,3},{3,2},{4,5},{5,4},{6,7},{7,6},{8,9},{9,8},{10,11... | collective-permute-start | bytes 196616 | tf_op jit(solution)/shard_map/ppermute | solution.py:242
  4.1 7.5 %collective-permute-start.16 = (bf16[64,512]{1,0:T(8,128)(2,1)S(1)}, bf16[64,512]{1,0:T(8,128)(2,1)S(1)}, u32[]{:S(2)}, u32[]{:S(2)}) collective-permute-start(bf16[64,512]{1,0:T(8,128)(2,1)S(1)} %get-tuple-element.34), channel_id=1, source_target_pairs={{0,2},{1,3},{2,0},{3,1},{4,6},{5,7},{6,4},{7,5},{8,10},{9,11},{10,... | collective-permute-start | bytes 196616 | tf_op jit(solution)/shard_map/ppermute | solution.py:242
  7.5 6.4 %collective-permute-start.18 = (bf16[64,512]{1,0:T(8,128)(2,1)S(1)}, bf16[64,512]{1,0:T(8,128)(2,1)S(1)}, u32[]{:S(2)}, u32[]{:S(2)}) collective-permute-start(bf16[64,512]{1,0:T(8,128)(2,1)S(1)} %get-tuple-element.36), channel_id=1, source_target_pairs={{0,4},{1,5},{2,6},{3,7},{4,0},{5,1},{6,2},{7,3},{8,12},{9,13},{10,... | collective-permute-start | bytes 196616 | tf_op jit(solution)/shard_map/ppermute | solution.py:242
  9.2 6.7 %collective-permute-start.19 = (bf16[64,512]{1,0:T(8,128)(2,1)S(1)}, bf16[64,512]{1,0:T(8,128)(2,1)S(1)}, u32[]{:S(2)}, u32[]{:S(2)}) collective-permute-start(bf16[64,512]{1,0:T(8,128)(2,1)S(1)} %get-tuple-element.37), channel_id=1, source_target_pairs={{0,5},{1,4},{2,7},{3,6},{4,1},{5,0},{6,3},{7,2},{8,13},{9,12},{10,... | collective-permute-start | bytes 196616 | tf_op jit(solution)/shard_map/ppermute | solution.py:242
  10.6 7.4 %collective-permute-start.20 = (bf16[64,512]{1,0:T(8,128)(2,1)S(1)}, bf16[64,512]{1,0:T(8,128)(2,1)S(1)}, u32[]{:S(2)}, u32[]{:S(2)}) collective-permute-start(bf16[64,512]{1,0:T(8,128)(2,1)S(1)} %get-tuple-element.38), channel_id=1, source_target_pairs={{0,6},{1,7},{2,4},{3,5},{4,2},{5,3},{6,0},{7,1},{8,14},{9,15},{10,... | collective-permute-start | bytes 196616 | tf_op jit(solution)/shard_map/ppermute | solution.py:242
  11.6 8.6 %collective-permute-start.21 = (bf16[64,512]{1,0:T(8,128)(2,1)S(1)}, bf16[64,512]{1,0:T(8,128)(2,1)S(1)}, u32[]{:S(2)}, u32[]{:S(2)}) collective-permute-start(bf16[64,512]{1,0:T(8,128)(2,1)S(1)} %get-tuple-element.39), channel_id=1, source_target_pairs={{0,7},{1,6},{2,5},{3,4},{4,3},{5,2},{6,1},{7,0},{8,15},{9,14},{10,... | collective-permute-start | bytes 196616 | tf_op jit(solution)/shard_map/ppermute | solution.py:242
  12.5 9.5 %collective-permute-start.1 = (bf16[128,128]{1,0:T(8,128)(2,1)S(1)}, bf16[128,128]{1,0:T(8,128)(2,1)S(1)}, u32[]{:S(2)}, u32[]{:S(2)}) collective-permute-start(bf16[128,128]{1,0:T(8,128)(2,1)S(1)} %get-tuple-element.30), channel_id=1, source_target_pairs={{0,4},{2,6},{4,0},{6,2},{8,12},{10,14},{12,8},{14,10},{16,20},{18,... | collective-permute-start | bytes 98312 | tf_op jit(solution)/shard_map/ppermute | solution.py:230
  13.9 10.5 %collective-permute-start.10 = (bf16[128,128]{1,0:T(8,128)(2,1)S(1)}, bf16[128,128]{1,0:T(8,128)(2,1)S(1)}, u32[]{:S(2)}, u32[]{:S(2)}) collective-permute-start(bf16[128,128]{1,0:T(8,128)(2,1)S(1)} %get-tuple-element.31), channel_id=1, source_target_pairs={{0,22},{2,20},{4,18},{6,16},{8,30},{10,28},{12,26},{14,24},{16,6},... | collective-permute-start | bytes 98312 | tf_op jit(solution)/shard_map/ppermute | solution.py:230
  15.9 9.7 %collective-permute-start.11 = (bf16[128,128]{1,0:T(8,128)(2,1)S(1)}, bf16[128,128]{1,0:T(8,128)(2,1)S(1)}, u32[]{:S(2)}, u32[]{:S(2)}) collective-permute-start(bf16[128,128]{1,0:T(8,128)(2,1)S(1)} %get-tuple-element.28.refs_0_), channel_id=1, source_target_pairs={{0,24},{2,26},{4,28},{6,30},{8,16},{10,18},{12,20},{14,22},{16,8},... | collective-permute-start | bytes 98312 | tf_op jit(solution)/shard_map/ppermute | solution.py:230
  18.1 7.6 %collective-permute-start.12 = (bf16[128,128]{1,0:T(8,128)(2,1)S(1)}, bf16[128,128]{1,0:T(8,128)(2,1)S(1)}, u32[]{:S(2)}, u32[]{:S(2)}) collective-permute-start(bf16[128,128]{1,0:T(8,128)(2,1)S(1)} %get-tuple-element.29), channel_id=1, source_target_pairs={{0,26},{2,24},{4,30},{6,28},{8,18},{10,16},{12,22},{14,20},{16,10}... | collective-permute-start | bytes 98312 | tf_op jit(solution)/shard_map/ppermute | solution.py:230
  20.2 7.0 %collective-permute-start.13 = (bf16[128,128]{1,0:T(8,128)(2,1)S(1)}, bf16[128,128]{1,0:T(8,128)(2,1)S(1)}, u32[]{:S(2)}, u32[]{:S(2)}) collective-permute-start(bf16[128,128]{1,0:T(8,128)(2,1)S(1)} %get-tuple-element.30), channel_id=1, source_target_pairs={{0,28},{2,30},{4,24},{6,26},{8,20},{10,22},{12,16},{14,18},{16,12}... | collective-permute-start | bytes 98312 | tf_op jit(solution)/shard_map/ppermute | solution.py:230
  22.0 6.5 %collective-permute-start.14 = (bf16[128,128]{1,0:T(8,128)(2,1)S(1)}, bf16[128,128]{1,0:T(8,128)(2,1)S(1)}, u32[]{:S(2)}, u32[]{:S(2)}) collective-permute-start(bf16[128,128]{1,0:T(8,128)(2,1)S(1)} %get-tuple-element.31), channel_id=1, source_target_pairs={{0,30},{2,28},{4,26},{6,24},{8,22},{10,20},{12,18},{14,16},{16,14}... | collective-permute-start | bytes 98312 | tf_op jit(solution)/shard_map/ppermute | solution.py:230
  24.3 7.0 %collective-permute-start.2 = (bf16[128,128]{1,0:T(8,128)(2,1)S(1)}, bf16[128,128]{1,0:T(8,128)(2,1)S(1)}, u32[]{:S(2)}, u32[]{:S(2)}) collective-permute-start(bf16[128,128]{1,0:T(8,128)(2,1)S(1)} %get-tuple-element.31), channel_id=1, source_target_pairs={{0,6},{2,4},{4,2},{6,0},{8,14},{10,12},{12,10},{14,8},{16,22},{18,... | collective-permute-start | bytes 98312 | tf_op jit(solution)/shard_map/ppermute | solution.py:230
  25.7 6.0 %collective-permute-start.3 = (bf16[128,128]{1,0:T(8,128)(2,1)S(1)}, bf16[128,128]{1,0:T(8,128)(2,1)S(1)}, u32[]{:S(2)}, u32[]{:S(2)}) collective-permute-start(bf16[128,128]{1,0:T(8,128)(2,1)S(1)} %get-tuple-element.28.refs_0_), channel_id=1, source_target_pairs={{0,8},{2,10},{4,12},{6,14},{8,0},{10,2},{12,4},{14,6},{16,24},{18,... | collective-permute-start | bytes 98312 | tf_op jit(solution)/shard_map/ppermute | solution.py:230
  25.7 7.6 %collective-permute-start.4 = (bf16[128,128]{1,0:T(8,128)(2,1)S(1)}, bf16[128,128]{1,0:T(8,128)(2,1)S(1)}, u32[]{:S(2)}, u32[]{:S(2)}) collective-permute-start(bf16[128,128]{1,0:T(8,128)(2,1)S(1)} %get-tuple-element.29), channel_id=1, source_target_pairs={{0,10},{2,8},{4,14},{6,12},{8,2},{10,0},{12,6},{14,4},{16,26},{18,... | collective-permute-start | bytes 98312 | tf_op jit(solution)/shard_map/ppermute | solution.py:230
  27.2 6.9 %collective-permute-start.22 = (bf16[64,256]{1,0:T(8,128)(2,1)S(1)}, bf16[64,256]{1,0:T(8,128)(2,1)S(1)}, u32[]{:S(2)}, u32[]{:S(2)}) collective-permute-start(bf16[64,256]{1,0:T(8,128)(2,1)S(1)} %shard_map.48), channel_id=1, source_target_pairs={{8,0},{10,2},{12,4},{14,6},{16,8},{18,10},{20,12},{22,14},{24,16},... | collective-permute-start | bytes 98312 | tf_op jit(solution)/shard_map/ppermute | solution.py:264
  28.5 9.6 %collective-permute-start.5 = (bf16[128,128]{1,0:T(8,128)(2,1)S(1)}, bf16[128,128]{1,0:T(8,128)(2,1)S(1)}, u32[]{:S(2)}, u32[]{:S(2)}) collective-permute-start(bf16[128,128]{1,0:T(8,128)(2,1)S(1)} %get-tuple-element.30), channel_id=1, source_target_pairs={{0,12},{2,14},{4,8},{6,10},{8,4},{10,6},{12,0},{14,2},{16,28},{18,... | collective-permute-start | bytes 98312 | tf_op jit(solution)/shard_map/ppermute | solution.py:230
  31.3 6.9 %collective-permute-start.6 = (bf16[128,128]{1,0:T(8,128)(2,1)S(1)}, bf16[128,128]{1,0:T(8,128)(2,1)S(1)}, u32[]{:S(2)}, u32[]{:S(2)}) collective-permute-start(bf16[128,128]{1,0:T(8,128)(2,1)S(1)} %get-tuple-element.31), channel_id=1, source_target_pairs={{0,14},{2,12},{4,10},{6,8},{8,6},{10,4},{12,2},{14,0},{16,30},{18,... | collective-permute-start | bytes 98312 | tf_op jit(solution)/shard_map/ppermute | solution.py:230
  31.7 6.4 %collective-permute-start.7 = (bf16[128,128]{1,0:T(8,128)(2,1)S(1)}, bf16[128,128]{1,0:T(8,128)(2,1)S(1)}, u32[]{:S(2)}, u32[]{:S(2)}) collective-permute-start(bf16[128,128]{1,0:T(8,128)(2,1)S(1)} %get-tuple-element.28.refs_0_), channel_id=1, source_target_pairs={{0,16},{2,18},{4,20},{6,22},{8,24},{10,26},{12,28},{14,30},{16,0},... | collective-permute-start | bytes 98312 | tf_op jit(solution)/shard_map/ppermute | solution.py:230
  33.3 5.9 %collective-permute-start.8 = (bf16[128,128]{1,0:T(8,128)(2,1)S(1)}, bf16[128,128]{1,0:T(8,128)(2,1)S(1)}, u32[]{:S(2)}, u32[]{:S(2)}) collective-permute-start(bf16[128,128]{1,0:T(8,128)(2,1)S(1)} %get-tuple-element.29), channel_id=1, source_target_pairs={{0,18},{2,16},{4,22},{6,20},{8,26},{10,24},{12,30},{14,28},{16,2},... | collective-permute-start | bytes 98312 | tf_op jit(solution)/shard_map/ppermute | solution.py:230
  34.1 6.1 %collective-permute-start.9 = (bf16[128,128]{1,0:T(8,128)(2,1)S(1)}, bf16[128,128]{1,0:T(8,128)(2,1)S(1)}, u32[]{:S(2)}, u32[]{:S(2)}) collective-permute-start(bf16[128,128]{1,0:T(8,128)(2,1)S(1)} %get-tuple-element.30), channel_id=1, source_target_pairs={{0,20},{2,22},{4,16},{6,18},{8,28},{10,30},{12,24},{14,26},{16,4},... | collective-permute-start | bytes 98312 | tf_op jit(solution)/shard_map/ppermute | solution.py:230
  48.0 27.6 %collective-permute-start.23 = (f32[16,512]{1,0:T(8,128)S(1)}, f32[16,512]{1,0:T(8,128)S(1)}, u32[]{:S(2)}, u32[]{:S(2)}) collective-permute-start(f32[16,512]{1,0:T(8,128)S(1)} %get-tuple-element.41), channel_id=1, source_target_pairs={{0,1},{1,0},{2,3},{3,2},{4,5},{5,4},{6,7},{7,6},{8,9},{9,8},{10,11... | collective-permute-start | bytes 98312 | tf_op jit(solution)/shard_map/ppermute | solution.py:286
  49.9 27.5 %collective-permute-start.24 = (f32[16,512]{1,0:T(8,128)S(1)}, f32[16,512]{1,0:T(8,128)S(1)}, u32[]{:S(2)}, u32[]{:S(2)}) collective-permute-start(f32[16,512]{1,0:T(8,128)S(1)} %get-tuple-element.42), channel_id=1, source_target_pairs={{0,2},{1,3},{2,0},{3,1},{4,6},{5,7},{6,4},{7,5},{8,10},{9,11},{10,... | collective-permute-start | bytes 98312 | tf_op jit(solution)/shard_map/ppermute | solution.py:286
  71.3 7.6 %collective-permute-start.25 = (f32[16,512]{1,0:T(8,128)S(1)}, f32[16,512]{1,0:T(8,128)S(1)}, u32[]{:S(2)}, u32[]{:S(2)}) collective-permute-start(f32[16,512]{1,0:T(8,128)S(1)} %get-tuple-element.43), channel_id=1, source_target_pairs={{0,3},{1,2},{2,1},{3,0},{4,7},{5,6},{6,5},{7,4},{8,11},{9,10},{10,... | collective-permute-start | bytes 98312 | tf_op jit(solution)/shard_map/ppermute | solution.py:286
  (13 other events, 98.6 us)

commit v2 on v1

v2 whole, which is shorter than its diff:
```python
import functools

import jax
import jax.numpy as jnp
from jax import lax
from jax.experimental import pallas as pl
from jax.experimental.pallas import tpu as pltpu
from jax.sharding import PartitionSpec as P

EPSILON = 1e-05
LANES = 128
INNER = 4
FINE = 16
VMEM_BYTES = 40 * 1024 * 1024

BF16 = jnp.bfloat16
F32 = jnp.float32


def call(kernel, out_shape, scratch=(), flops=0, bytes_accessed=0):
    return pl.pallas_call(
        kernel,
        out_shape=out_shape,
        scratch_shapes=list(scratch),
        compiler_params=pltpu.CompilerParams(vmem_limit_bytes=VMEM_BYTES),
        cost_estimate=pl.CostEstimate(
            flops=flops, bytes_accessed=bytes_accessed, transcendentals=0
        ),
    )


def one_hot(order_row, station_count):
    columns = order_row.shape[1]
    first = 3 * lax.broadcasted_iota(jnp.int32, (station_count, columns), 0)
    hit = (order_row >= first) & (order_row < first + 3)
    return jnp.where(hit, 1.0, 0.0).astype(BF16)


def template_kernel(tm_count, tpl_ref, flag_ref, order_ref, *refs):
    out_ref, tpl_pad, order_pad, turned = refs
    channels, window = tpl_ref.shape[1:]
    stations = flag_ref.shape[1]
    padded = tpl_pad.shape[0]
    part = LANES // tm_count
    tpl_pad[channels:, :] = jnp.zeros((padded - channels, window), BF16)
    tpl_pad[:channels, :] = tpl_ref[0]
    order_pad[...] = jnp.full((1, padded), -1, jnp.int32)
    order_pad[:, :channels] = order_ref[...]
    flags = jnp.broadcast_to(flag_ref[...].astype(F32), (8, stations))
    mask = jnp.dot(
        flags.astype(BF16), one_hot(order_pad[...], stations), preferred_element_type=F32
    )
    masked = tpl_pad[...].T * mask[:1].astype(BF16)
    turned[...] = masked
    wide = masked.astype(F32)
    norm = jnp.sqrt(jnp.sum(wide * wide, keepdims=True) + EPSILON)
    live = jnp.sum(mask[:1], keepdims=True)
    rest = jnp.broadcast_to(jnp.sqrt(window * live) / norm, (1, LANES))
    extra = [jnp.zeros((1, LANES), F32)] * FINE
    for piece in range(3):
        extra[piece] = rest.astype(BF16).astype(F32)
        rest = rest - extra[piece]
    wide_flags = jnp.concatenate(
        [flags[:1], jnp.zeros((1, -stations % LANES), F32)], axis=1
    )
    for piece in range(wide_flags.shape[1] // LANES):
        extra[3 + piece] = wide_flags[:, piece * LANES : (piece + 1) * LANES]
    extra = jnp.concatenate(extra, axis=0).astype(BF16)
    my_tm = lax.axis_index("tm")
    spot = lax.broadcasted_iota(jnp.int32, (FINE, LANES), 1) // part
    for member in range(INNER):
        start = member * LANES
        pieces = []
        for step in range(window // (FINE * tm_count)):
            tile = jnp.zeros((FINE, LANES), F32)
            for within in range(tm_count):
                row = FINE * (step * tm_count + within)
                chunk = turned[row : row + FINE, start : start + LANES].astype(F32)
                turn = lax.rem(part * (within - my_tm) + LANES, LANES)
                tile = jnp.where(spot == within, pltpu.roll(chunk, turn, 1), tile)
            pieces.append(tile.astype(BF16))
        payload = jnp.concatenate(pieces + [extra], axis=0)
        for target in range(member, out_ref.shape[0], INNER):
            out_ref[target] = payload


def shift_kernel(waves_ref, halo_ref, out_ref, joined):
    group, part, slab = waves_ref.shape
    for member in range(group):
        joined[:, member * slab : (member + 1) * slab] = waves_ref[member].astype(F32)
    joined[:, group * slab :] = halo_ref[...].astype(F32)
    columns = joined.shape[1]
    for copy in range(LANES // FINE):
        rows = slice(copy * part, (copy + 1) * part)
        if copy == 0:
            out_ref[rows, :] = joined[...].astype(BF16)
        else:
            out_ref[rows, :] = pltpu.roll(joined[...], columns - FINE * copy, 1).astype(BF16)


def dots_kernel(tpls, shifts, out_ref, left, products):
    count = tpls.shape[0]
    group, _, slab = out_ref.shape
    per_half = left.shape[2] // LANES
    for template in range(count):
        row = template * FINE
        for step in range(2 * per_half):
            lane = (step % per_half) * LANES
            left[step // per_half, row : row + FINE, lane : lane + LANES] = tpls[
                template, FINE * step : FINE * (step + 1), :
            ]
    tiles = products.shape[0]
    span = (tiles - 1) * LANES
    per_block = span // slab

    def block(index, carry):
        start = pl.multiple_of(index * span, span)
        product = jnp.dot(
            left[0], shifts[:, pl.ds(start, span + LANES)], preferred_element_type=F32
        ) + jnp.dot(
            left[1],
            shifts[:, pl.ds(pl.multiple_of(start + LANES, LANES), span + LANES)],
            preferred_element_type=F32,
        )
        for tile in range(tiles):
            products[tile] = product[:, tile * LANES : (tile + 1) * LANES]

        def fine_rows(fine):
            return jnp.concatenate(
                [products[tile, pl.ds(fine, count, stride=FINE), :] for tile in range(tiles)],
                axis=1,
            )

        total = fine_rows(FINE - 1)
        for fine in reversed(range(FINE - 1)):
            total = fine_rows(fine) + pltpu.roll(total, span + LANES - 1, 1)
        for piece in range(per_block):
            out_ref[index * per_block + piece] = total[:, piece * slab : (piece + 1) * slab]
        return carry

    lax.fori_loop(0, group // per_block, block, 0)


def power_kernel(stations, wave_ref, tpls_ref, order_ref, out_ref, head_ref, scale_ref):
    extra = tpls_ref[:, tpls_ref.shape[1] - FINE :, :].astype(F32)
    scale_ref[...] = extra[:, 0, :] + extra[:, 1, :] + extra[:, 2, :]
    tiles = -(-stations // LANES)
    flags = jnp.concatenate([extra[:, 3 + tile, :] for tile in range(tiles)], axis=1)
    mask = jnp.dot(
        flags.astype(BF16),
        one_hot(order_ref[...], tiles * LANES),
        preferred_element_type=F32,
    ).astype(BF16)
    wave = wave_ref[...].astype(F32)
    squares = wave * wave
    high = squares.astype(BF16)
    low = (squares - high.astype(F32)).astype(BF16)
    power = jnp.dot(mask, high, preferred_element_type=F32) + jnp.dot(
        mask, low, preferred_element_type=F32
    )
    out_ref[...] = power
    head_ref[...] = power[:, : head_ref.shape[1]]


def factor_kernel(power_ref, halo_ref, scale_ref, out_ref, joined):
    slab, window = power_ref.shape[1], halo_ref.shape[1]
    joined[:, :slab] = power_ref[...]
    joined[:, slab:] = halo_ref[...]
    running = joined[...]
    columns = running.shape[1]
    width = 1
    while width < window:
        running = running + pltpu.roll(running, columns - width, 1)
        width *= 2
    out_ref[...] = scale_ref[:, :1] / jnp.sqrt(running[:, :slab] + EPSILON)


def finish_kernel(parts_ref, factor_ref, out_ref):
    out_ref[...] = jnp.sum(parts_ref[...], axis=0) * factor_ref[...]


def on_device(waveforms, templates, station_mask, channel_order):
    channels, slab = waveforms.shape
    rows, _, window = templates.shape
    stations = station_mask.shape[1]
    outer_count, tm_count = lax.axis_size("outer"), lax.axis_size("tm")
    blk_count = outer_count * INNER
    assert rows == 1 and LANES % tm_count == 0
    group = INNER * tm_count
    padded = INNER * LANES
    part = padded // group
    chunk = group * slab
    span = 2 * slab
    blk, members, every = ("outer", "inner"), ("inner", "tm"), ("outer", "inner", "tm")
    sds = jax.ShapeDtypeStruct
    order_row = channel_order[None, :]

    payload = call(
        functools.partial(template_kernel, tm_count),
        sds((blk_count, window * part // LANES + FINE, LANES), BF16),
        [
            pltpu.VMEM((padded, window), BF16),
            pltpu.VMEM((1, padded), jnp.int32),
            pltpu.VMEM((window, padded), BF16),
        ],
        bytes_accessed=channels * window * 2,
    )(templates, station_mask, order_row)
    tpls = lax.all_to_all(payload, blk, 0, 0, tiled=True)

    wave_parts = jnp.pad(waveforms, ((0, padded - channels), (0, 0)))
    waves = lax.all_to_all(wave_parts.reshape(group, part, slab), members, 0, 0, tiled=True)
    halo = lax.ppermute(
        waves[0, :, :window], "outer", [(b, b - 1) for b in range(1, outer_count)]
    )
    copies = LANES // FINE
    shifts = call(
        shift_kernel,
        sds((copies * part, chunk + window), BF16),
        [pltpu.VMEM((part, chunk + window), F32)],
        bytes_accessed=chunk * part * 2 * (copies + 1),
    )(waves, halo)

    power, power_head, scale = call(
        functools.partial(power_kernel, stations),
        [
            sds((blk_count, slab), F32),
            sds((blk_count, window), F32),
            sds((blk_count, LANES), F32),
        ],
        flops=4 * blk_count * channels * slab,
        bytes_accessed=channels * slab * 2,
    )(waveforms, tpls, order_row)
    total = blk_count * tm_count
    power_halo = lax.ppermute(power_head, every, [(i, i - 1) for i in range(1, total)])
    factor = call(
        factor_kernel,
        sds((blk_count, slab), F32),
        [pltpu.VMEM((blk_count, slab + window), F32)],
        bytes_accessed=blk_count * slab * 8,
    )(power, power_halo, scale)

    partials = call(
        dots_kernel,
        sds((group, blk_count, slab), F32),
        [
            pltpu.VMEM((2, blk_count * FINE, copies * part), BF16),
            pltpu.VMEM((span // LANES + 1, blk_count * FINE, LANES), F32),
        ],
        flops=2 * blk_count * window * part * chunk,
        bytes_accessed=copies * part * chunk * 2,
    )(tpls, shifts)
    sums = lax.all_to_all(partials, members, 0, 0, tiled=True)
    return call(
        finish_kernel, sds((blk_count, slab), F32), bytes_accessed=blk_count * slab * 4 * (group + 2)
    )(sums, factor)


def solution(mesh):
    blk_count, tm_count = mesh.devices.shape
    shape = (blk_count // INNER, INNER, tm_count)
    mesh = jax.sharding.Mesh(mesh.devices.reshape(shape), ("outer", "inner", "tm"))
    blk, every = ("outer", "inner"), ("outer", "inner", "tm")
    placed = (P(None, every), P(blk, None, None), P(blk, None), P())
    return jax.shard_map(
        on_device, mesh=mesh, in_specs=placed, out_specs=P(None, every), check_vma=False
    )
```

time: 82.6 us -> 63.4 us (0.77)
  the two profiles are of different devices: /device:TPU:0 before, /device:TPU:15 now
where the time goes in v2:
time: 63.4 us; the launch traced here: 62.8 us
  waiting for transfers between devices  21.2 us (33%)
  starting transfers between devices  20.6 us (32%)
  Pallas kernels  12.6 us (20%)
  local copies, waits for them, and re-layouts  8.47 us (13%)
    ppermute x1, waiting for transfers between devices, on_device(): lax.ppermute(waves[0, :, :window], 'outer', [(b, b - 1) for b in range(1,...  13 us
    pallas_call x1, Pallas kernels, on_device(): call(dots_kernel, sds((group, blk_count, slab), F32), [pltpu.VMEM((2, blk...  8.57 us
    unnamed x14, local copies, waits for them, and re-layouts  6.61 us
    all_to_all x1, starting transfers between devices, on_device(): tpls = lax.all_to_all(payload, blk, 0, 0, tiled=True)  6.56 us
    all_to_all x1, starting transfers between devices, on_device(): sums = lax.all_to_all(partials, members, 0, 0, tiled=True)  5.13 us
    ppermute x1, waiting for transfers between devices, on_device(): lax.ppermute(power_head, every, [(i, i - 1) for i in range(1, total)])  4.66 us
    all_to_all x1, starting transfers between devices, on_device(): lax.all_to_all(wave_parts.reshape(group, part, slab), members, 0, 0, tile...  4.51 us
    all_to_all x1, waiting for transfers between devices, on_device(): lax.all_to_all(wave_parts.reshape(group, part, slab), members, 0, 0, tile...  3.46 us
  transfers between devices with their start and end apart: 5, of which 3 were waited for; matrix products, arithmetic and copies ran while one was open for 0% of the time, Pallas kernels for 5%

profile of v2, /device:TPU:15, one launch (start us, length us, event | category | flops | bytes accessed | tf_op | source)
XLA Modules:
  0.0 62.8 jit_solution(14149632566816363540)
XLA Ops:
  0.0 1.9 %pad.4 = bf16[512,512]{1,0:T(8,128)(2,1)} pad(bf16[480,512]{1,0:T(8,128)(2,1)} %wave_ref.1, bf16[]{:T(256)} %constant.2.clone.1), padding=0_32x0_0 | pad | bytes 1015810 | tf_op jit(solution)/shard_map/jit(_pad)/pad | solution.py:210
  1.9 4.5 %all-to-all-start.1 = ((bf16[8,64,512]{2,1,0:T(8,128)(2,1)}), bf16[8,64,512]{2,1,0:T(8,128)(2,1)S(1)}, u32[]{:S(2)}, u32[]{:S(2)}) async-start(bf16[8,64,512]{2,1,0:T(8,128)(2,1)} %bitcast.1), calls=%async_computation.1 | async-start | bytes 1048576 | tf_op jit(solution)/shard_map/all_to_all | solution.py:211
  6.4 0.9 %copy-done.3 = bf16[1,480,256]{2,1,0:T(8,128)(2,1)S(1)} copy-done((bf16[1,480,256]{2,1,0:T(8,128)(2,1)S(1)}, bf16[1,480,256]{2,1,0:T(8,128)(2,1)}, u32[]{:S(2)}) %copy-start.3) | copy-done | bytes 245784
  7.3 0.7 %copy-done.4 = s32[480]{0:T(512)S(1)} copy-done((s32[480]{0:T(512)S(1)}, s32[480]{0:T(512)}, u32[]{:S(2)}) %copy-start.4) | copy-done | bytes 1944
  8.0 0.7 %copy-done.6 = s32[1,160]{1,0:T(1,128)S(1)} copy-done((s32[1,160]{1,0:T(1,128)S(1)}, s32[1,160]{1,0:T(1,128)}, u32[]{:S(2)}) %copy-start.6) | copy-done | bytes 664
  8.7 1.3 %shard_map.46 = bf16[16,144,128]{2,1,0:T(8,128)(2,1)} custom-call(bf16[1,480,256]{2,1,0:T(8,128)(2,1)S(1)} %copy-done.3, s32[1,160]{1,0:T(1,128)S(1)} %copy-done.6, s32[1,480]{1,0:T(1,128)S(1)} %bitcast.4), custom_call_target="tpu_custom_call" | custom-call | bytes 245760 | tf_op jit(solution)/shard_map/pallas_call | solution.py:198
  10.0 3.5 %all-to-all-done.1.waves_ref = bf16[8,64,512]{2,1,0:T(8,128)(2,1)S(1)} async-done(((bf16[8,64,512]{2,1,0:T(8,128)(2,1)}), bf16[8,64,512]{2,1,0:T(8,128)(2,1)S(1)}, u32[]{:S(2)}, u32[]{:S(2)}) %all-to-all-start.1) | async-done | bytes 524320 | tf_op jit(solution)/shard_map/all_to_all | solution.py:211
  13.4 6.6 %all-to-all-start = ((bf16[16,144,128]{2,1,0:T(8,128)(2,1)}), bf16[16,144,128]{2,1,0:T(8,128)(2,1)S(1)}, u32[]{:S(2)}, u32[]{:S(2)}) async-start(bf16[16,144,128]{2,1,0:T(8,128)(2,1)} %shard_map.46), calls=%async_computation | async-start | bytes 1179648 | tf_op jit(solution)/shard_map/all_to_all | solution.py:208
  20.0 2.2 %collective-permute-start = (bf16[64,256]{1,0:T(8,128)(2,1)S(1)}, bf16[64,256]{1,0:T(8,128)(2,1)S(1)}, u32[]{:S(2)}, u32[]{:S(2)}) collective-permute-start(bf16[64,256]{1,0:T(8,128)(2,1)S(1)} %slice_bitcast_fusion), channel_id=1, source_target_pairs={{8,0},{16,8},{24,16},{9,1},{17,9},{25,17},{10,2},{18,10},{26,18},{... | collective-permute-start | bytes 98312 | tf_op jit(solution)/shard_map/ppermute | solution.py:212
  22.2 13.0 %collective-permute-done.halo_ref = bf16[64,256]{1,0:T(8,128)(2,1)S(1)} collective-permute-done((bf16[64,256]{1,0:T(8,128)(2,1)S(1)}, bf16[64,256]{1,0:T(8,128)(2,1)S(1)}, u32[]{:S(2)}, u32[]{:S(2)}) %collective-permute-start) | collective-permute-done | bytes 32800 | tf_op jit(solution)/shard_map/ppermute | solution.py:212
  35.2 1.1 %shard_map.47.shifts = bf16[512,4352]{1,0:T(8,128)(2,1)S(1)} custom-call(bf16[8,64,512]{2,1,0:T(8,128)(2,1)S(1)} %all-to-all-done.1.waves_ref, bf16[64,256]{1,0:T(8,128)(2,1)S(1)} %collective-permute-done.halo_ref), custom_call_target="tpu_custom_call" | custom-call | bytes 4718592 | tf_op jit(solution)/shard_map/pallas_call | solution.py:216
  36.3 0.0 copy-start
  36.4 2.0 %copy-done = bf16[512,4352]{1,0:T(8,128)(2,1)} copy-done((bf16[512,4352]{1,0:T(8,128)(2,1)}, bf16[512,4352]{1,0:T(8,128)(2,1)S(1)}, u32[]{:S(2)}) %copy-start) | copy-done | bytes 4456472
  38.4 0.0 all-to-all-done.tpls.tpls_ref
  38.4 2.3 %copy-done.1 = bf16[512,4352]{1,0:T(8,128)(2,1)S(1)} copy-done((bf16[512,4352]{1,0:T(8,128)(2,1)S(1)}, bf16[512,4352]{1,0:T(8,128)(2,1)}, u32[]{:S(2)}) %copy-start.1) | copy-done | bytes 4456472
  40.7 8.6 %shard_map.48 = f32[8,16,512]{2,1,0:T(8,128)} custom-call(bf16[16,144,128]{2,1,0:T(8,128)(2,1)S(1)} %all-to-all-done.tpls.tpls_ref, bf16[512,4352]{1,0:T(8,128)(2,1)S(1)} %copy-done.1), custom_call_target="tpu_custom_call" | custom-call | flops 2147483648 | bytes 4194304 | tf_op jit(solution)/shard_map/pallas_call | solution.py:242
  49.2 5.1 %all-to-all-start.2 = ((f32[8,16,512]{2,1,0:T(8,128)}), f32[8,16,512]{2,1,0:T(8,128)S(1)}, u32[]{:S(2)}, u32[]{:S(2)}) async-start(f32[8,16,512]{2,1,0:T(8,128)} %shard_map.48), calls=%async_computation.2 | async-start | bytes 524288 | tf_op jit(solution)/shard_map/all_to_all | solution.py:252
  54.4 0.0 copy-done.2
  54.4 0.4 shard_map.49
  54.8 2.2 %collective-permute-start.1 = (f32[16,256]{1,0:T(8,128)S(1)}, f32[16,256]{1,0:T(8,128)S(1)}, u32[]{:S(2)}, u32[]{:S(2)}) collective-permute-start(f32[16,256]{1,0:T(8,128)S(1)} %get-tuple-element.9), channel_id=1, source_target_pairs={{1,0},{2,1},{3,2},{4,3},{5,4},{6,5},{7,6},{8,7},{9,8},{10,9},{11,1... | collective-permute-start | bytes 49160 | tf_op jit(solution)/shard_map/ppermute | solution.py:234
  57.0 4.7 %collective-permute-done.1.halo_ref = f32[16,256]{1,0:T(8,128)S(1)} collective-permute-done((f32[16,256]{1,0:T(8,128)S(1)}, f32[16,256]{1,0:T(8,128)S(1)}, u32[]{:S(2)}, u32[]{:S(2)}) %collective-permute-start.1) | collective-permute-done | bytes 16416 | tf_op jit(solution)/shard_map/ppermute | solution.py:234
  61.7 0.5 shard_map.50.factor_ref
  62.2 0.0 all-to-all-done.2.parts_ref
  62.2 0.6 %shard_map.51 = f32[16,512]{1,0:T(8,128)} custom-call(f32[8,16,512]{2,1,0:T(8,128)S(1)} %all-to-all-done.2.parts_ref, f32[16,512]{1,0:T(8,128)S(1)} %shard_map.50.factor_ref), custom_call_target="tpu_custom_call" | custom-call | bytes 327680 | tf_op jit(solution)/shard_map/pallas_call | solution.py:253
  (8 shorter events, 0.0 us)
Async XLA Ops:
  1.9 11.6 %all-to-all-start.1 = ((bf16[8,64,512]{2,1,0:T(8,128)(2,1)}), bf16[8,64,512]{2,1,0:T(8,128)(2,1)S(1)}, u32[]{:S(2)}, u32[]{:S(2)}) async-start(bf16[8,64,512]{2,1,0:T(8,128)(2,1)} %bitcast.1), calls=%async_computation.1 | async-start | bytes 1048576 | tf_op jit(solution)/shard_map/all_to_all | solution.py:211
  6.4 0.9 %copy-start.3 = (bf16[1,480,256]{2,1,0:T(8,128)(2,1)S(1)}, bf16[1,480,256]{2,1,0:T(8,128)(2,1)}, u32[]{:S(2)}) copy-start(bf16[1,480,256]{2,1,0:T(8,128)(2,1)} %tpl_ref.1) | copy-start | bytes 737284
  7.3 0.7 %copy-start.4 = (s32[480]{0:T(512)S(1)}, s32[480]{0:T(512)}, u32[]{:S(2)}) copy-start(s32[480]{0:T(512)} %param.7) | copy-start | bytes 5764
  8.0 0.7 %copy-start.6 = (s32[1,160]{1,0:T(1,128)S(1)}, s32[1,160]{1,0:T(1,128)}, u32[]{:S(2)}) copy-start(s32[1,160]{1,0:T(1,128)} %flag_ref.1) | copy-start | bytes 1924
  13.4 25.0 %all-to-all-start = ((bf16[16,144,128]{2,1,0:T(8,128)(2,1)}), bf16[16,144,128]{2,1,0:T(8,128)(2,1)S(1)}, u32[]{:S(2)}, u32[]{:S(2)}) async-start(bf16[16,144,128]{2,1,0:T(8,128)(2,1)} %shard_map.46), calls=%async_computation | async-start | bytes 1179648 | tf_op jit(solution)/shard_map/all_to_all | solution.py:208
  20.0 15.2 %collective-permute-start = (bf16[64,256]{1,0:T(8,128)(2,1)S(1)}, bf16[64,256]{1,0:T(8,128)(2,1)S(1)}, u32[]{:S(2)}, u32[]{:S(2)}) collective-permute-start(bf16[64,256]{1,0:T(8,128)(2,1)S(1)} %slice_bitcast_fusion), channel_id=1, source_target_pairs={{8,0},{16,8},{24,16},{9,1},{17,9},{25,17},{10,2},{18,10},{26,18},{... | collective-permute-start | bytes 98312 | tf_op jit(solution)/shard_map/ppermute | solution.py:212
  36.3 2.0 %copy-start = (bf16[512,4352]{1,0:T(8,128)(2,1)}, bf16[512,4352]{1,0:T(8,128)(2,1)S(1)}, u32[]{:S(2)}) copy-start(bf16[512,4352]{1,0:T(8,128)(2,1)S(1)} %shard_map.47.shifts) | copy-start | bytes 13369348
  38.4 2.3 %copy-start.1 = (bf16[512,4352]{1,0:T(8,128)(2,1)S(1)}, bf16[512,4352]{1,0:T(8,128)(2,1)}, u32[]{:S(2)}) copy-start(bf16[512,4352]{1,0:T(8,128)(2,1)} %copy-done) | copy-start | bytes 13369348
  40.7 13.7 %copy-start.2 = (bf16[480,512]{1,0:T(8,128)(2,1)S(1)}, bf16[480,512]{1,0:T(8,128)(2,1)}, u32[]{:S(2)}) copy-start(bf16[480,512]{1,0:T(8,128)(2,1)} %wave_ref.1) | copy-start | bytes 1474564
  40.7 13.7 %copy-start.5 = (s32[480]{0:T(512)S(1)}, s32[480]{0:T(512)}, u32[]{:S(2)}) copy-start(s32[480]{0:T(512)} %param.7) | copy-start | bytes 5764
  49.2 13.0 %all-to-all-start.2 = ((f32[8,16,512]{2,1,0:T(8,128)}), f32[8,16,512]{2,1,0:T(8,128)S(1)}, u32[]{:S(2)}, u32[]{:S(2)}) async-start(f32[8,16,512]{2,1,0:T(8,128)} %shard_map.48), calls=%async_computation.2 | async-start | bytes 524288 | tf_op jit(solution)/shard_map/all_to_all | solution.py:252
  54.8 6.9 %collective-permute-start.1 = (f32[16,256]{1,0:T(8,128)S(1)}, f32[16,256]{1,0:T(8,128)S(1)}, u32[]{:S(2)}, u32[]{:S(2)}) collective-permute-start(f32[16,256]{1,0:T(8,128)S(1)} %get-tuple-element.9), channel_id=1, source_target_pairs={{1,0},{2,1},{3,2},{4,3},{5,4},{6,5},{7,6},{8,7},{9,8},{10,9},{11,1... | collective-permute-start | bytes 49160 | tf_op jit(solution)/shard_map/ppermute | solution.py:234

commit v3 on v2

--- a/solution.py
+++ b/solution.py
@@ -17,9 +17,16 @@
 F32 = jnp.float32
 
 
-def call(kernel, out_shape, scratch=(), flops=0, bytes_accessed=0):
+HBM = pl.BlockSpec(memory_space=pltpu.HBM)
+VMEM = pl.BlockSpec(memory_space=pltpu.VMEM)
+AFTER = pl.BlockSpec(memory_space=pl.ANY)
+
+
+def call(kernel, in_specs, out_shape, scratch=(), flops=0, bytes_accessed=0):
     return pl.pallas_call(
         kernel,
+        in_specs=in_specs,
+        out_specs=jax.tree.map(lambda _: VMEM, out_shape),
         out_shape=out_shape,
         scratch_shapes=list(scratch),
         compiler_params=pltpu.CompilerParams(vmem_limit_bytes=VMEM_BYTES),
@@ -36,20 +43,29 @@
     return jnp.where(hit, 1.0, 0.0).astype(BF16)
 
 
-def template_kernel(tm_count, tpl_ref, flag_ref, order_ref, *refs):
-    out_ref, tpl_pad, order_pad, turned = refs
-    channels, window = tpl_ref.shape[1:]
+def template_kernel(tm_count, tpl_hbm, flag_hbm, order_hbm, out_ref, *scratch):
+    tpl_pad, flag_ref, order_ref, order_pad, turned, sems = scratch
+    channels, window = tpl_hbm.shape[1:]
+    copies = [
+        pltpu.make_async_copy(flag_hbm, flag_ref, sems.at[0]),
+        pltpu.make_async_copy(order_hbm, order_ref, sems.at[1]),
+        pltpu.make_async_copy(tpl_hbm.at[0], tpl_pad.at[pl.ds(0, channels)], sems.at[2]),
+    ]
+    for copy in copies:
+        copy.start()
     stations = flag_ref.shape[1]
     padded = tpl_pad.shape[0]
     part = LANES // tm_count
     tpl_pad[channels:, :] = jnp.zeros((padded - channels, window), BF16)
-    tpl_pad[:channels, :] = tpl_ref[0]
     order_pad[...] = jnp.full((1, padded), -1, jnp.int32)
+    copies[0].wait()
+    copies[1].wait()
     order_pad[:, :channels] = order_ref[...]
     flags = jnp.broadcast_to(flag_ref[...].astype(F32), (8, stations))
     mask = jnp.dot(
         flags.astype(BF16), one_hot(order_pad[...], stations), preferred_element_type=F32
     )
+    copies[2].wait()
     masked = tpl_pad[...].T * mask[:1].astype(BF16)
     turned[...] = masked
     wide = masked.astype(F32)
@@ -84,6 +100,15 @@
             out_ref[target] = payload
 
 
+def wave_kernel(wave_hbm, after, out_ref, sem):
+    del after
+    channels, slab = wave_hbm.shape
+    copy = pltpu.make_async_copy(wave_hbm, out_ref.at[pl.ds(0, channels)], sem)
+    copy.start()
+    out_ref[channels:, :] = jnp.zeros((out_ref.shape[0] - channels, slab), BF16)
+    copy.wait()
+
+
 def shift_kernel(waves_ref, halo_ref, out_ref, joined):
     group, part, slab = waves_ref.shape
     for member in range(group):
@@ -98,7 +123,8 @@
             out_ref[rows, :] = pltpu.roll(joined[...], columns - FINE * copy, 1).astype(BF16)
 
 
-def dots_kernel(tpls, shifts, out_ref, left, products):
+def dots_kernel(tpls, shifts, after, out_ref, left, products):
+    del after
     count = tpls.shape[0]
     group, _, slab = out_ref.shape
     per_half = left.shape[2] // LANES
@@ -162,7 +188,8 @@
     head_ref[...] = power[:, : head_ref.shape[1]]
 
 
-def factor_kernel(power_ref, halo_ref, scale_ref, out_ref, joined):
+def factor_kernel(power_ref, halo_ref, scale_ref, after, out_ref, joined):
+    del after
     slab, window = power_ref.shape[1], halo_ref.shape[1]
     joined[:, :slab] = power_ref[...]
     joined[:, slab:] = halo_ref[...]
@@ -197,17 +224,27 @@
 
     payload = call(
         functools.partial(template_kernel, tm_count),
+        [HBM] * 3,
         sds((blk_count, window * part // LANES + FINE, LANES), BF16),
         [
             pltpu.VMEM((padded, window), BF16),
+            pltpu.VMEM((1, stations), jnp.int32),
+            pltpu.VMEM((1, channels), jnp.int32),
             pltpu.VMEM((1, padded), jnp.int32),
             pltpu.VMEM((window, padded), BF16),
+            pltpu.SemaphoreType.DMA((3,)),
         ],
         bytes_accessed=channels * window * 2,
     )(templates, station_mask, order_row)
     tpls = lax.all_to_all(payload, blk, 0, 0, tiled=True)
 
-    wave_parts = jnp.pad(waveforms, ((0, padded - channels), (0, 0)))
+    wave_parts = call(
+        wave_kernel,
+        [HBM, AFTER],
+        sds((padded, slab), BF16),
+        [pltpu.SemaphoreType.DMA],
+        bytes_accessed=channels * slab * 2,
+    )(waveforms, payload)
     waves = lax.all_to_all(wave_parts.reshape(group, part, slab), members, 0, 0, tiled=True)
     halo = lax.ppermute(
         waves[0, :, :window], "outer", [(b, b - 1) for b in range(1, outer_count)]
@@ -215,6 +252,7 @@
     copies = LANES // FINE
     shifts = call(
         shift_kernel,
+        [VMEM] * 2,
         sds((copies * part, chunk + window), BF16),
         [pltpu.VMEM((part, chunk + window), F32)],
         bytes_accessed=chunk * part * 2 * (copies + 1),
@@ -222,6 +260,7 @@
 
     power, power_head, scale = call(
         functools.partial(power_kernel, stations),
+        [VMEM] * 3,
         [
             sds((blk_count, slab), F32),
             sds((blk_count, window), F32),
@@ -232,15 +271,9 @@
     )(waveforms, tpls, order_row)
     total = blk_count * tm_count
     power_halo = lax.ppermute(power_head, every, [(i, i - 1) for i in range(1, total)])
-    factor = call(
-        factor_kernel,
-        sds((blk_count, slab), F32),
-        [pltpu.VMEM((blk_count, slab + window), F32)],
-        bytes_accessed=blk_count * slab * 8,
-    )(power, power_halo, scale)
-
     partials = call(
         dots_kernel,
+        [VMEM, VMEM, AFTER],
         sds((group, blk_count, slab), F32),
         [
             pltpu.VMEM((2, blk_count * FINE, copies * part), BF16),
@@ -248,10 +281,20 @@
         ],
         flops=2 * blk_count * window * part * chunk,
         bytes_accessed=copies * part * chunk * 2,
-    )(tpls, shifts)
+    )(tpls, shifts, power_head)
     sums = lax.all_to_all(partials, members, 0, 0, tiled=True)
+    factor = call(
+        factor_kernel,
+        [VMEM] * 3 + [AFTER],
+        sds((blk_count, slab), F32),
+        [pltpu.VMEM((blk_count, slab + window), F32)],
+        bytes_accessed=blk_count * slab * 8,
+    )(power, power_halo, scale, partials)
     return call(
-        finish_kernel, sds((blk_count, slab), F32), bytes_accessed=blk_count * slab * 4 * (group + 2)
+        finish_kernel,
+        [VMEM] * 2,
+        sds((blk_count, slab), F32),
+        bytes_accessed=blk_count * slab * 4 * (group + 2),
     )(sums, factor)
 
 

time: 63.4 us -> 66.7 us (1.052)
  blocking collectives: 0 us -> 11.4 us
  starting transfers between devices: 20.6 us -> 16 us
  waiting for transfers between devices: 21.2 us -> 17.7 us
  local copies, waits for them, and re-layouts: 8.47 us -> 7.64 us
  Pallas kernels: 12.6 us -> 13.3 us
    all_to_all x0 -> x1, blocking collectives: none -> 11.4 us  [on_device(): lax.all_to_all(wave_parts.reshape(group, part, slab), members, 0, 0, tile...]
    all_to_all x1 -> x0, starting transfers between devices: 4.51 us -> none  [on_device(): lax.all_to_all(wave_parts.reshape(group, part, slab), members, 0, 0, tile...]
    all_to_all x1 -> x0, waiting for transfers between devices: 3.46 us -> none  [on_device(): lax.all_to_all(wave_parts.reshape(group, part, slab), members, 0, 0, tile...]
    pad x1 -> x0, local copies, waits for them, and re-layouts: 1.85 us -> none  [on_device(): wave_parts = jnp.pad(waveforms, ((0, padded - channels), (0, 0)))]
    unnamed x14 -> x16, local copies, waits for them, and re-layouts: 6.61 us -> 7.63 us
    pallas_call x6 -> x7, Pallas kernels: 12.6 us -> 13.3 us  [the longest x1 8.58 us: on_device(): call(dots_kernel, [VMEM, VMEM, AFTER], sds((group, blk_count, slab), F32)...]
  transfers between devices with their start and end apart: 5 -> 4, of which waited for: 3 -> 2; matrix products, arithmetic and copies ran while one was open for 0% -> 0% of each run, Pallas kernels for 5% -> 2%
where the time goes in v3:
time: 66.7 us; the launch traced here: 66.1 us
  waiting for transfers between devices  17.7 us (27%)
  starting transfers between devices  16 us (24%)
  Pallas kernels  13.3 us (20%)
  blocking collectives  11.4 us (17%)
  local copies, waits for them, and re-layouts  7.64 us (11%)
    ppermute x1, waiting for transfers between devices, on_device(): lax.ppermute(waves[0, :, :window], 'outer', [(b, b - 1) for b in range(1,...  13 us
    all_to_all x1, blocking collectives, on_device(): lax.all_to_all(wave_parts.reshape(group, part, slab), members, 0, 0, tile...  11.4 us
    pallas_call x1, Pallas kernels, on_device(): call(dots_kernel, [VMEM, VMEM, AFTER], sds((group, blk_count, slab), F32)...  8.58 us
    unnamed x16, local copies, waits for them, and re-layouts  7.63 us
    all_to_all x1, starting transfers between devices, on_device(): tpls = lax.all_to_all(payload, blk, 0, 0, tiled=True)  6.55 us
    all_to_all x1, starting transfers between devices, on_device(): sums = lax.all_to_all(partials, members, 0, 0, tiled=True)  5.13 us
    ppermute x1, waiting for transfers between devices, on_device(): lax.ppermute(power_head, every, [(i, i - 1) for i in range(1, total)])  4.66 us
    ppermute x1, starting transfers between devices, on_device(): lax.ppermute(waves[0, :, :window], 'outer', [(b, b - 1) for b in range(1,...  2.19 us
  transfers between devices with their start and end apart: 4, of which 2 were waited for; matrix products, arithmetic and copies ran while one was open for 0% of the time, Pallas kernels for 2%

profile of v3, /device:TPU:15, one launch (start us, length us, event | category | flops | bytes accessed | tf_op | source)
XLA Modules:
  0.0 66.1 jit_solution(4367203363706524226)
XLA Ops:
  0.0 0.9 %copy-done.4 = bf16[1,480,256]{2,1,0:T(8,128)(2,1)S(1)} copy-done((bf16[1,480,256]{2,1,0:T(8,128)(2,1)S(1)}, bf16[1,480,256]{2,1,0:T(8,128)(2,1)}, u32[]{:S(2)}) %copy-start.4) | copy-done | bytes 245784
  0.9 0.7 %copy-done.5 = s32[480]{0:T(512)S(1)} copy-done((s32[480]{0:T(512)S(1)}, s32[480]{0:T(512)}, u32[]{:S(2)}) %copy-start.5) | copy-done | bytes 1944
  1.6 0.7 %copy-done.7 = s32[1,160]{1,0:T(1,128)S(1)} copy-done((s32[1,160]{1,0:T(1,128)S(1)}, s32[1,160]{1,0:T(1,128)}, u32[]{:S(2)}) %copy-start.7) | copy-done | bytes 664
  2.3 1.7 %shard_map.46.after = bf16[16,144,128]{2,1,0:T(8,128)(2,1)} custom-call(bf16[1,480,256]{2,1,0:T(8,128)(2,1)S(1)} %copy-done.4, s32[1,160]{1,0:T(1,128)S(1)} %copy-done.7, s32[1,480]{1,0:T(1,128)S(1)} %bitcast.5), custom_call_target="tpu_custom_call" | custom-call | bytes 245760 | tf_op jit(solution)/shard_map/pallas_call | solution.py:225
  4.0 0.0 copy-start.2
  4.0 1.0 %copy-done.2 = bf16[480,512]{1,0:T(8,128)(2,1)S(1)} copy-done((bf16[480,512]{1,0:T(8,128)(2,1)S(1)}, bf16[480,512]{1,0:T(8,128)(2,1)}, u32[]{:S(2)}) %copy-start.2) | copy-done | bytes 491544
  5.1 0.3 shard_map.47
  5.4 11.4 %all_to_all.15.waves_ref = bf16[8,64,512]{2,1,0:T(8,128)(2,1)S(1)} all-to-all(bf16[8,64,512]{2,1,0:T(8,128)(2,1)S(1)} %bitcast.4), channel_id=1, replica_groups=mesh['outer'=4,'inner'=4,'tm'=2] {'inner','tm'}, dimensions={0} | all-to-all | bytes 1048576 | tf_op jit(solution)/shard_map/all_to_all | solution.py:248
  16.8 6.5 %all-to-all-start = ((bf16[16,144,128]{2,1,0:T(8,128)(2,1)}), bf16[16,144,128]{2,1,0:T(8,128)(2,1)S(1)}, u32[]{:S(2)}, u32[]{:S(2)}) async-start(bf16[16,144,128]{2,1,0:T(8,128)(2,1)} %shard_map.46.after), calls=%async_computation | async-start | bytes 1179648 | tf_op jit(solution)/shard_map/all_to_all | solution.py:239
  23.3 2.2 %collective-permute-start = (bf16[64,256]{1,0:T(8,128)(2,1)S(1)}, bf16[64,256]{1,0:T(8,128)(2,1)S(1)}, u32[]{:S(2)}, u32[]{:S(2)}) collective-permute-start(bf16[64,256]{1,0:T(8,128)(2,1)S(1)} %slice_bitcast_fusion), channel_id=1, source_target_pairs={{8,0},{16,8},{24,16},{9,1},{17,9},{25,17},{10,2},{18,10},{26,18},{... | collective-permute-start | bytes 98312 | tf_op jit(solution)/shard_map/ppermute | solution.py:249
  25.5 13.0 %collective-permute-done.halo_ref = bf16[64,256]{1,0:T(8,128)(2,1)S(1)} collective-permute-done((bf16[64,256]{1,0:T(8,128)(2,1)S(1)}, bf16[64,256]{1,0:T(8,128)(2,1)S(1)}, u32[]{:S(2)}, u32[]{:S(2)}) %collective-permute-start) | collective-permute-done | bytes 32800 | tf_op jit(solution)/shard_map/ppermute | solution.py:249
  38.6 1.1 %shard_map.48.shifts = bf16[512,4352]{1,0:T(8,128)(2,1)S(1)} custom-call(bf16[8,64,512]{2,1,0:T(8,128)(2,1)S(1)} %all_to_all.15.waves_ref, bf16[64,256]{1,0:T(8,128)(2,1)S(1)} %collective-permute-done.halo_ref), custom_call_target="tpu_custom_call" | custom-call | bytes 4718592 | tf_op jit(solution)/shard_map/pallas_call | solution.py:253
  39.7 0.0 copy-start
  39.7 2.0 %copy-done = bf16[512,4352]{1,0:T(8,128)(2,1)} copy-done((bf16[512,4352]{1,0:T(8,128)(2,1)}, bf16[512,4352]{1,0:T(8,128)(2,1)S(1)}, u32[]{:S(2)}) %copy-start) | copy-done | bytes 4456472
  41.7 0.0 all-to-all-done.tpls_ref.tpls
  41.7 0.4 shard_map.49
  42.2 2.3 %copy-done.1 = bf16[512,4352]{1,0:T(8,128)(2,1)S(1)} copy-done((bf16[512,4352]{1,0:T(8,128)(2,1)S(1)}, bf16[512,4352]{1,0:T(8,128)(2,1)}, u32[]{:S(2)}) %copy-start.1) | copy-done | bytes 4456472
  44.4 8.6 %shard_map.50.after = f32[8,16,512]{2,1,0:T(8,128)} custom-call(bf16[16,144,128]{2,1,0:T(8,128)(2,1)S(1)} %all-to-all-done.tpls_ref.tpls, bf16[512,4352]{1,0:T(8,128)(2,1)S(1)} %copy-done.1, f32[16,256]{1,0:T(8,128)S(1)} %get-tuple-element.8.after), custom_call_target="tpu_custom_call" | custom-call | flops 2147483648 | bytes 4194304 | tf_op jit(solution)/shard_map/pallas_call | solution.py:274
  53.0 5.1 %all-to-all-start.2 = ((f32[8,16,512]{2,1,0:T(8,128)}), f32[8,16,512]{2,1,0:T(8,128)S(1)}, u32[]{:S(2)}, u32[]{:S(2)}) async-start(f32[8,16,512]{2,1,0:T(8,128)} %shard_map.50.after), calls=%async_computation.2 | async-start | bytes 524288 | tf_op jit(solution)/shard_map/all_to_all | solution.py:285
  58.1 2.2 %collective-permute-start.1 = (f32[16,256]{1,0:T(8,128)S(1)}, f32[16,256]{1,0:T(8,128)S(1)}, u32[]{:S(2)}, u32[]{:S(2)}) collective-permute-start(f32[16,256]{1,0:T(8,128)S(1)} %get-tuple-element.8.after), channel_id=1, source_target_pairs={{1,0},{2,1},{3,2},{4,3},{5,4},{6,5},{7,6},{8,7},{9,8},{10,9},{11,1... | collective-permute-start | bytes 49160 | tf_op jit(solution)/shard_map/ppermute | solution.py:273
  60.3 4.7 %collective-permute-done.1.halo_ref = f32[16,256]{1,0:T(8,128)S(1)} collective-permute-done((f32[16,256]{1,0:T(8,128)S(1)}, f32[16,256]{1,0:T(8,128)S(1)}, u32[]{:S(2)}, u32[]{:S(2)}) %collective-permute-start.1) | collective-permute-done | bytes 16416 | tf_op jit(solution)/shard_map/ppermute | solution.py:273
  65.0 0.5 shard_map.51.factor_ref
  65.5 0.0 all-to-all-done.2.parts_ref
  65.5 0.6 shard_map.52
  (9 shorter events, 0.0 us)
Async XLA Ops:
  0.0 0.9 %copy-start.4 = (bf16[1,480,256]{2,1,0:T(8,128)(2,1)S(1)}, bf16[1,480,256]{2,1,0:T(8,128)(2,1)}, u32[]{:S(2)}) copy-start(bf16[1,480,256]{2,1,0:T(8,128)(2,1)} %tpl_hbm.1) | copy-start | bytes 737284
  0.9 0.7 %copy-start.5 = (s32[480]{0:T(512)S(1)}, s32[480]{0:T(512)}, u32[]{:S(2)}) copy-start(s32[480]{0:T(512)} %param.7) | copy-start | bytes 5764
  1.6 0.7 %copy-start.7 = (s32[1,160]{1,0:T(1,128)S(1)}, s32[1,160]{1,0:T(1,128)}, u32[]{:S(2)}) copy-start(s32[1,160]{1,0:T(1,128)} %flag_hbm.1) | copy-start | bytes 1924
  4.0 1.0 %copy-start.2 = (bf16[480,512]{1,0:T(8,128)(2,1)S(1)}, bf16[480,512]{1,0:T(8,128)(2,1)}, u32[]{:S(2)}) copy-start(bf16[480,512]{1,0:T(8,128)(2,1)} %wave_ref.1) | copy-start | bytes 1474564
  5.0 36.7 %copy-start.3 = (bf16[480,512]{1,0:T(8,128)(2,1)S(1)}, bf16[480,512]{1,0:T(8,128)(2,1)}, u32[]{:S(2)}) copy-start(bf16[480,512]{1,0:T(8,128)(2,1)} %wave_ref.1) | copy-start | bytes 1474564
  5.1 36.7 %copy-start.6 = (s32[480]{0:T(512)S(1)}, s32[480]{0:T(512)}, u32[]{:S(2)}) copy-start(s32[480]{0:T(512)} %param.7) | copy-start | bytes 5764
  16.8 24.9 %all-to-all-start = ((bf16[16,144,128]{2,1,0:T(8,128)(2,1)}), bf16[16,144,128]{2,1,0:T(8,128)(2,1)S(1)}, u32[]{:S(2)}, u32[]{:S(2)}) async-start(bf16[16,144,128]{2,1,0:T(8,128)(2,1)} %shard_map.46.after), calls=%async_computation | async-start | bytes 1179648 | tf_op jit(solution)/shard_map/all_to_all | solution.py:239
  23.3 15.2 %collective-permute-start = (bf16[64,256]{1,0:T(8,128)(2,1)S(1)}, bf16[64,256]{1,0:T(8,128)(2,1)S(1)}, u32[]{:S(2)}, u32[]{:S(2)}) collective-permute-start(bf16[64,256]{1,0:T(8,128)(2,1)S(1)} %slice_bitcast_fusion), channel_id=1, source_target_pairs={{8,0},{16,8},{24,16},{9,1},{17,9},{25,17},{10,2},{18,10},{26,18},{... | collective-permute-start | bytes 98312 | tf_op jit(solution)/shard_map/ppermute | solution.py:249
  39.7 2.0 %copy-start = (bf16[512,4352]{1,0:T(8,128)(2,1)}, bf16[512,4352]{1,0:T(8,128)(2,1)S(1)}, u32[]{:S(2)}) copy-start(bf16[512,4352]{1,0:T(8,128)(2,1)S(1)} %shard_map.48.shifts) | copy-start | bytes 13369348
  42.2 2.3 %copy-start.1 = (bf16[512,4352]{1,0:T(8,128)(2,1)S(1)}, bf16[512,4352]{1,0:T(8,128)(2,1)}, u32[]{:S(2)}) copy-start(bf16[512,4352]{1,0:T(8,128)(2,1)} %copy-done) | copy-start | bytes 13369348
  53.0 12.5 %all-to-all-start.2 = ((f32[8,16,512]{2,1,0:T(8,128)}), f32[8,16,512]{2,1,0:T(8,128)S(1)}, u32[]{:S(2)}, u32[]{:S(2)}) async-start(f32[8,16,512]{2,1,0:T(8,128)} %shard_map.50.after), calls=%async_computation.2 | async-start | bytes 524288 | tf_op jit(solution)/shard_map/all_to_all | solution.py:285
  58.1 6.8 %collective-permute-start.1 = (f32[16,256]{1,0:T(8,128)S(1)}, f32[16,256]{1,0:T(8,128)S(1)}, u32[]{:S(2)}, u32[]{:S(2)}) collective-permute-start(f32[16,256]{1,0:T(8,128)S(1)} %get-tuple-element.8.after), channel_id=1, source_target_pairs={{1,0},{2,1},{3,2},{4,3},{5,4},{6,5},{7,6},{8,7},{9,8},{10,9},{11,1... | collective-permute-start | bytes 49160 | tf_op jit(solution)/shard_map/ppermute | solution.py:273

commit v4 on v3

--- a/solution.py
+++ b/solution.py
@@ -10,8 +10,9 @@
 EPSILON = 1e-05
 LANES = 128
 INNER = 4
+META = 16
 FINE = 16
-VMEM_BYTES = 40 * 1024 * 1024
+MIB = 1024 * 1024
 
 BF16 = jnp.bfloat16
 F32 = jnp.float32
@@ -22,14 +23,14 @@
 AFTER = pl.BlockSpec(memory_space=pl.ANY)
 
 
-def call(kernel, in_specs, out_shape, scratch=(), flops=0, bytes_accessed=0):
+def call(kernel, in_specs, out_shape, scratch=(), flops=0, bytes_accessed=0, vmem=24):
     return pl.pallas_call(
         kernel,
         in_specs=in_specs,
         out_specs=jax.tree.map(lambda _: VMEM, out_shape),
         out_shape=out_shape,
         scratch_shapes=list(scratch),
-        compiler_params=pltpu.CompilerParams(vmem_limit_bytes=VMEM_BYTES),
+        compiler_params=pltpu.CompilerParams(vmem_limit_bytes=vmem * MIB),
         cost_estimate=pl.CostEstimate(
             flops=flops, bytes_accessed=bytes_accessed, transcendentals=0
         ),
@@ -43,19 +44,26 @@
     return jnp.where(hit, 1.0, 0.0).astype(BF16)
 
 
-def template_kernel(tm_count, tpl_hbm, flag_hbm, order_hbm, out_ref, *scratch):
-    tpl_pad, flag_ref, order_ref, order_pad, turned, sems = scratch
+def side_major(inner):
+    return (inner % 2) * (INNER // 2) + inner // 2
+
+
+def prologue_kernel(tm_count, tpl_hbm, flag_hbm, order_hbm, wave_hbm, *refs):
+    out_ref, send_ref, keep_ref = refs[:3]
+    tpl_pad, flag_ref, order_ref, order_pad, wave_pad, turned, sems = refs[3:]
     channels, window = tpl_hbm.shape[1:]
     copies = [
         pltpu.make_async_copy(flag_hbm, flag_ref, sems.at[0]),
         pltpu.make_async_copy(order_hbm, order_ref, sems.at[1]),
         pltpu.make_async_copy(tpl_hbm.at[0], tpl_pad.at[pl.ds(0, channels)], sems.at[2]),
+        pltpu.make_async_copy(wave_hbm, wave_pad.at[pl.ds(0, channels)], sems.at[3]),
     ]
     for copy in copies:
         copy.start()
     stations = flag_ref.shape[1]
     padded = tpl_pad.shape[0]
     part = LANES // tm_count
+    wave_pad[channels:, :] = jnp.zeros((padded - channels, wave_pad.shape[1]), BF16)
     tpl_pad[channels:, :] = jnp.zeros((padded - channels, window), BF16)
     order_pad[...] = jnp.full((1, padded), -1, jnp.int32)
     copies[0].wait()
@@ -72,7 +80,7 @@
     norm = jnp.sqrt(jnp.sum(wide * wide, keepdims=True) + EPSILON)
     live = jnp.sum(mask[:1], keepdims=True)
     rest = jnp.broadcast_to(jnp.sqrt(window * live) / norm, (1, LANES))
-    extra = [jnp.zeros((1, LANES), F32)] * FINE
+    extra = [jnp.zeros((1, LANES), F32)] * META
     for piece in range(3):
         extra[piece] = rest.astype(BF16).astype(F32)
         rest = rest - extra[piece]
@@ -85,7 +93,7 @@
     my_tm = lax.axis_index("tm")
     spot = lax.broadcasted_iota(jnp.int32, (FINE, LANES), 1) // part
     for member in range(INNER):
-        start = member * LANES
+        start = side_major(member) * LANES
         pieces = []
         for step in range(window // (FINE * tm_count)):
             tile = jnp.zeros((FINE, LANES), F32)
@@ -98,41 +106,52 @@
         payload = jnp.concatenate(pieces + [extra], axis=0)
         for target in range(member, out_ref.shape[0], INNER):
             out_ref[target] = payload
-
-
-def wave_kernel(wave_hbm, after, out_ref, sem):
-    del after
-    channels, slab = wave_hbm.shape
-    copy = pltpu.make_async_copy(wave_hbm, out_ref.at[pl.ds(0, channels)], sem)
-    copy.start()
-    out_ref[channels:, :] = jnp.zeros((out_ref.shape[0] - channels, slab), BF16)
-    copy.wait()
-
-
-def shift_kernel(waves_ref, halo_ref, out_ref, joined):
-    group, part, slab = waves_ref.shape
-    for member in range(group):
-        joined[:, member * slab : (member + 1) * slab] = waves_ref[member].astype(F32)
-    joined[:, group * slab :] = halo_ref[...].astype(F32)
-    columns = joined.shape[1]
-    for copy in range(LANES // FINE):
-        rows = slice(copy * part, (copy + 1) * part)
-        if copy == 0:
-            out_ref[rows, :] = joined[...].astype(BF16)
-        else:
-            out_ref[rows, :] = pltpu.roll(joined[...], columns - FINE * copy, 1).astype(BF16)
-
-
-def dots_kernel(tpls, shifts, after, out_ref, left, products):
-    del after
+    copies[3].wait()
+    core = lax.rem(lax.axis_index("inner"), 2)
+    half = padded // 2
+    keep_ref[...] = wave_pad[pl.ds(pl.multiple_of(core * half, half), half), :]
+    send_ref[...] = wave_pad[pl.ds(pl.multiple_of((1 - core) * half, half), half), :]
+
+
+def split_kernel(tm_count, keep_ref, got_ref, *outs):
+    my_inner = lax.axis_index("inner")
+    core = lax.rem(my_inner, 2)
+    me = lax.div(my_inner, 2) * tm_count + lax.axis_index("tm")
+    part = outs[0].shape[1]
+    for flip, out_ref in enumerate(outs):
+        rows = pl.ds(pl.multiple_of((me ^ flip) * part, part), part)
+        out_ref[core] = keep_ref[rows, :]
+        out_ref[1 - core] = got_ref[rows, :]
+
+
+def join_kernel(tm_count, *refs):
+    parts, out_ref, head_ref = refs[:-2], refs[-2], refs[-1]
+    me = lax.div(lax.axis_index("inner"), 2) * tm_count + lax.axis_index("tm")
+    slab = parts[0].shape[2]
+    for flip, part in enumerate(parts):
+        other = me ^ flip
+        y, tm = lax.div(other, tm_count), lax.rem(other, tm_count)
+        for core in range(2):
+            place = (y * 2 + core) * tm_count + tm
+            out_ref[:, pl.ds(pl.multiple_of(place * slab, slab), slab)] = part[core]
+    head_ref[...] = out_ref[:, : head_ref.shape[1]]
+
+
+def correlate(tpls, samples, out_ref, first, left, shifts, products):
     count = tpls.shape[0]
-    group, _, slab = out_ref.shape
-    per_half = left.shape[2] // LANES
+    slab = out_ref.shape[2]
+    part, columns = samples.shape
+    copies = shifts.shape[0] // part
+    for copy in range(copies):
+        turned = samples if copy == 0 else pltpu.roll(samples, columns - FINE * copy, 1)
+        shifts[copy * part : (copy + 1) * part, :] = turned
+    parts, _, depth = left.shape
+    steps = depth // LANES
     for template in range(count):
         row = template * FINE
-        for step in range(2 * per_half):
-            lane = (step % per_half) * LANES
-            left[step // per_half, row : row + FINE, lane : lane + LANES] = tpls[
+        for step in range(parts * steps):
+            lane = (step % steps) * LANES
+            left[step // steps, row : row + FINE, lane : lane + LANES] = tpls[
                 template, FINE * step : FINE * (step + 1), :
             ]
     tiles = products.shape[0]
@@ -141,13 +160,11 @@
 
     def block(index, carry):
         start = pl.multiple_of(index * span, span)
-        product = jnp.dot(
-            left[0], shifts[:, pl.ds(start, span + LANES)], preferred_element_type=F32
-        ) + jnp.dot(
-            left[1],
-            shifts[:, pl.ds(pl.multiple_of(start + LANES, LANES), span + LANES)],
-            preferred_element_type=F32,
-        )
+        product = None
+        for piece in range(parts):
+            here = pl.ds(pl.multiple_of(start + piece * copies * FINE, LANES), span + LANES)
+            term = jnp.dot(left[piece], shifts[:, here], preferred_element_type=F32)
+            product = term if product is None else product + term
         for tile in range(tiles):
             products[tile] = product[:, tile * LANES : (tile + 1) * LANES]
 
@@ -161,14 +178,29 @@
         for fine in reversed(range(FINE - 1)):
             total = fine_rows(fine) + pltpu.roll(total, span + LANES - 1, 1)
         for piece in range(per_block):
-            out_ref[index * per_block + piece] = total[:, piece * slab : (piece + 1) * slab]
+            out_ref[first + index * per_block + piece] = total[:, piece * slab : (piece + 1) * slab]
         return carry
 
-    lax.fori_loop(0, group // per_block, block, 0)
+    blocks = (columns - 2 * LANES) // span
+    lax.fori_loop(0, blocks, block, 0)
+
+
+def first_dots_kernel(tpls, samples_ref, out_ref, left, shifts, products):
+    columns = shifts.shape[1]
+    correlate(tpls, samples_ref[:, :columns], out_ref, 0, left, shifts, products)
+
+
+def last_dots_kernel(tpls, samples_ref, halo_ref, done_ref, after, out_ref, *scratch):
+    del after
+    rest = samples_ref.shape[1] + halo_ref.shape[1] - scratch[1].shape[1]
+    samples = jnp.concatenate([samples_ref[:, rest:], halo_ref[...]], axis=1)
+    first = done_ref.shape[0]
+    out_ref[:first] = done_ref[...]
+    correlate(tpls, samples, out_ref, first, *scratch)
 
 
 def power_kernel(stations, wave_ref, tpls_ref, order_ref, out_ref, head_ref, scale_ref):
-    extra = tpls_ref[:, tpls_ref.shape[1] - FINE :, :].astype(F32)
+    extra = tpls_ref[:, tpls_ref.shape[1] - META :, :].astype(F32)
     scale_ref[...] = extra[:, 0, :] + extra[:, 1, :] + extra[:, 2, :]
     tiles = -(-stations // LANES)
     flags = jnp.concatenate([extra[:, 3 + tile, :] for tile in range(tiles)], axis=1)
@@ -218,45 +250,53 @@
     part = padded // group
     chunk = group * slab
     span = 2 * slab
+    total = blk_count * tm_count
     blk, members, every = ("outer", "inner"), ("inner", "tm"), ("outer", "inner", "tm")
     sds = jax.ShapeDtypeStruct
     order_row = channel_order[None, :]
 
-    payload = call(
-        functools.partial(template_kernel, tm_count),
-        [HBM] * 3,
-        sds((blk_count, window * part // LANES + FINE, LANES), BF16),
+    payload, send, keep = call(
+        functools.partial(prologue_kernel, tm_count),
+        [HBM] * 4,
+        [
+            sds((blk_count, window * part // LANES + META, LANES), BF16),
+            sds((padded // 2, slab), BF16),
+            sds((padded // 2, slab), BF16),
+        ],
         [
             pltpu.VMEM((padded, window), BF16),
             pltpu.VMEM((1, stations), jnp.int32),
             pltpu.VMEM((1, channels), jnp.int32),
             pltpu.VMEM((1, padded), jnp.int32),
+            pltpu.VMEM((padded, slab), BF16),
             pltpu.VMEM((window, padded), BF16),
-            pltpu.SemaphoreType.DMA((3,)),
+            pltpu.SemaphoreType.DMA((4,)),
         ],
-        bytes_accessed=channels * window * 2,
-    )(templates, station_mask, order_row)
+        bytes_accessed=channels * (window + slab) * 2,
+        vmem=60,
+    )(templates, station_mask, order_row, waveforms)
     tpls = lax.all_to_all(payload, blk, 0, 0, tiled=True)
 
-    wave_parts = call(
-        wave_kernel,
-        [HBM, AFTER],
-        sds((padded, slab), BF16),
-        [pltpu.SemaphoreType.DMA],
-        bytes_accessed=channels * slab * 2,
-    )(waveforms, payload)
-    waves = lax.all_to_all(wave_parts.reshape(group, part, slab), members, 0, 0, tiled=True)
-    halo = lax.ppermute(
-        waves[0, :, :window], "outer", [(b, b - 1) for b in range(1, outer_count)]
-    )
-    copies = LANES // FINE
-    shifts = call(
-        shift_kernel,
+    got = lax.ppermute(send, "inner", [(b, b ^ 1) for b in range(INNER)])
+    half = group // 2
+    parts = call(
+        functools.partial(split_kernel, tm_count),
         [VMEM] * 2,
-        sds((copies * part, chunk + window), BF16),
-        [pltpu.VMEM((part, chunk + window), F32)],
-        bytes_accessed=chunk * part * 2 * (copies + 1),
-    )(waves, halo)
+        [sds((2, part, slab), BF16)] * half,
+        bytes_accessed=padded * slab * 2,
+    )(keep, got)
+    waves = [parts[0]]
+    for flip in range(1, half):
+        y, tm = flip // tm_count, flip % tm_count
+        route = [(i, i ^ (2 * tm_count * y + tm)) for i in range(total)]
+        waves.append(lax.ppermute(parts[flip], every, route))
+    samples, head = call(
+        functools.partial(join_kernel, tm_count),
+        [VMEM] * half,
+        [sds((part, chunk), BF16), sds((part, window), BF16)],
+        bytes_accessed=part * chunk * 4,
+    )(*waves)
+    halo = lax.ppermute(head, "outer", [(b, b - 1) for b in range(1, outer_count)])
 
     power, power_head, scale = call(
         functools.partial(power_kernel, stations),
@@ -269,19 +309,36 @@
         flops=4 * blk_count * channels * slab,
         bytes_accessed=channels * slab * 2,
     )(waveforms, tpls, order_row)
-    total = blk_count * tm_count
     power_halo = lax.ppermute(power_head, every, [(i, i - 1) for i in range(1, total)])
+
+    copies = max(LANES // FINE, tm_count)
+    coarse = window // FINE
+
+    def scratch(columns):
+        return [
+            pltpu.VMEM((coarse // copies, blk_count * FINE, copies * part), BF16),
+            pltpu.VMEM((copies * part, columns), BF16),
+            pltpu.VMEM((span // LANES + 1, blk_count * FINE, LANES), F32),
+        ]
+
+    blocks = group // 2
+    work = 2 * blk_count * window * part * span
     partials = call(
-        dots_kernel,
-        [VMEM, VMEM, AFTER],
+        first_dots_kernel,
+        [VMEM] * 2,
+        sds((2 * (blocks - 1), blk_count, slab), F32),
+        scratch((blocks - 1) * span + window),
+        flops=work * (blocks - 1),
+        bytes_accessed=part * chunk * 2,
+    )(tpls, samples)
+    partials = call(
+        last_dots_kernel,
+        [VMEM] * 4 + [AFTER],
         sds((group, blk_count, slab), F32),
-        [
-            pltpu.VMEM((2, blk_count * FINE, copies * part), BF16),
-            pltpu.VMEM((span // LANES + 1, blk_count * FINE, LANES), F32),
-        ],
-        flops=2 * blk_count * window * part * chunk,
-        bytes_accessed=copies * part * chunk * 2,
-    )(tpls, shifts, power_head)
+        scratch(span + window),
+        flops=work,
+        bytes_accessed=part * chunk * 2,
+    )(tpls, samples, halo, partials, power_halo)
     sums = lax.all_to_all(partials, members, 0, 0, tiled=True)
     factor = call(
         factor_kernel,

time: 66.7 us -> 50.3 us (0.75)
  the two profiles are of different devices: /device:TPU:15 before, /device:TPU:0 now
where the time goes in v4:
time: 50.3 us; the launch traced here: 49.9 us
  starting transfers between devices  20.1 us (40%)
  waiting for transfers between devices  16 us (32%)
  Pallas kernels  13.7 us (27%)
    ppermute x3, waiting for transfers between devices, on_device(): waves.append(lax.ppermute(parts[flip], every, route))  8.89 us
    all_to_all x1, starting transfers between devices, on_device(): tpls = lax.all_to_all(payload, blk, 0, 0, tiled=True)  7.53 us
    pallas_call x1, Pallas kernels, on_device(): call(first_dots_kernel, [VMEM] * 2, sds((2 * (blocks - 1), blk_count, sla...  6.72 us
    all_to_all x1, starting transfers between devices, on_device(): sums = lax.all_to_all(partials, members, 0, 0, tiled=True)  5.96 us
    all_to_all x1, waiting for transfers between devices, on_device(): sums = lax.all_to_all(partials, members, 0, 0, tiled=True)  5.93 us
    ppermute x3, starting transfers between devices, on_device(): waves.append(lax.ppermute(parts[flip], every, route))  3.57 us
    pallas_call x1, Pallas kernels, on_device(): call(last_dots_kernel, [VMEM] * 4 + [AFTER], sds((group, blk_count, slab)...  2.9 us
    pallas_call x1, Pallas kernels, on_device(): call(functools.partial(prologue_kernel, tm_count), [HBM] * 4, [sds((blk_c...  2.39 us
  transfers between devices with their start and end apart: 8, of which 4 were waited for; matrix products, arithmetic and copies ran while one was open for 0% of the time, Pallas kernels for 16%

profile of v4, /device:TPU:0, one launch (start us, length us, event | category | flops | bytes accessed | tf_op | source)
XLA Modules:
  0.0 49.9 jit_solution(1630967210537806162)
XLA Ops:
  0.0 2.4 %shard_map.46 = (bf16[16,144,128]{2,1,0:T(8,128)(2,1)}, bf16[256,512]{1,0:T(8,128)(2,1)}, bf16[256,512]{1,0:T(8,128)(2,1)}) custom-call(bf16[1,480,256]{2,1,0:T(8,128)(2,1)} %tpl_hbm.1, s32[1,160]{1,0:T(1,128)} %flag_hbm.1, s32[1,480]{1,0:T(1,128)} %bitcast.1, bf16[480,512]{1,0:T(8,128)(2,1)} %wave_ref.1), custom_call_target="tpu_custom_call" | custom-call | bytes 737280 | tf_op jit(solution)/shard_map/pallas_call | solution.py:258
  2.4 0.0 copy-start.3
  2.4 7.5 %all-to-all-start = ((bf16[16,144,128]{2,1,0:T(8,128)(2,1)}), bf16[16,144,128]{2,1,0:T(8,128)(2,1)S(1)}, u32[]{:S(2)}, u32[]{:S(2)}) async-start(bf16[16,144,128]{2,1,0:T(8,128)(2,1)} %get-tuple-element.17), calls=%async_computation | async-start | bytes 1179648 | tf_op jit(solution)/shard_map/all_to_all | solution.py:278
  10.0 0.5 collective-permute-start
  10.4 1.2 %collective-permute-done.got_ref = bf16[256,512]{1,0:T(8,128)(2,1)S(1)} collective-permute-done((bf16[256,512]{1,0:T(8,128)(2,1)S(1)}, bf16[256,512]{1,0:T(8,128)(2,1)S(1)}, u32[]{:S(2)}, u32[]{:S(2)}) %collective-permute-start) | collective-permute-done | bytes 262176 | tf_op jit(solution)/shard_map/ppermute | solution.py:280
  11.6 1.6 %collective-permute-start.1 = (bf16[2,64,512]{2,1,0:T(8,128)(2,1)S(1)}, bf16[2,64,512]{2,1,0:T(8,128)(2,1)S(1)}, u32[]{:S(2)}, u32[]{:S(2)}) collective-permute-start(bf16[2,64,512]{2,1,0:T(8,128)(2,1)S(1)} %get-tuple-element.21), channel_id=1, source_target_pairs={{0,1},{1,0},{2,3},{3,2},{4,5},{5,4},{6,7},{7,6},{8,9},{9,8},{10,11... | collective-permute-start | bytes 393224 | tf_op jit(solution)/shard_map/ppermute | solution.py:292
  13.2 1.9 %collective-permute-start.2 = (bf16[2,64,512]{2,1,0:T(8,128)(2,1)S(1)}, bf16[2,64,512]{2,1,0:T(8,128)(2,1)S(1)}, u32[]{:S(2)}, u32[]{:S(2)}) collective-permute-start(bf16[2,64,512]{2,1,0:T(8,128)(2,1)S(1)} %get-tuple-element.22), channel_id=1, source_target_pairs={{0,4},{1,5},{2,6},{3,7},{4,0},{5,1},{6,2},{7,3},{8,12},{9,13},{10,... | collective-permute-start | bytes 393224 | tf_op jit(solution)/shard_map/ppermute | solution.py:292
  15.1 0.1 collective-permute-start.3
  15.2 2.6 %collective-permute-done.1.refs_1_ = bf16[2,64,512]{2,1,0:T(8,128)(2,1)S(1)} collective-permute-done((bf16[2,64,512]{2,1,0:T(8,128)(2,1)S(1)}, bf16[2,64,512]{2,1,0:T(8,128)(2,1)S(1)}, u32[]{:S(2)}, u32[]{:S(2)}) %collective-permute-start.1) | collective-permute-done | bytes 131104 | tf_op jit(solution)/shard_map/ppermute | solution.py:292
  17.8 6.3 %collective-permute-done.2.refs_2_ = bf16[2,64,512]{2,1,0:T(8,128)(2,1)S(1)} collective-permute-done((bf16[2,64,512]{2,1,0:T(8,128)(2,1)S(1)}, bf16[2,64,512]{2,1,0:T(8,128)(2,1)S(1)}, u32[]{:S(2)}, u32[]{:S(2)}) %collective-permute-start.2) | collective-permute-done | bytes 131104 | tf_op jit(solution)/shard_map/ppermute | solution.py:292
  24.1 0.0 collective-permute-done.3.refs_3_
  24.1 0.1 shard_map.48
  24.2 1.3 %collective-permute-start.4 = (bf16[64,256]{1,0:T(8,128)(2,1)S(1)}, bf16[64,256]{1,0:T(8,128)(2,1)S(1)}, u32[]{:S(2)}, u32[]{:S(2)}) collective-permute-start(bf16[64,256]{1,0:T(8,128)(2,1)S(1)} %get-tuple-element.25), channel_id=1, source_target_pairs={{8,0},{16,8},{24,16},{9,1},{17,9},{25,17},{10,2},{18,10},{26,18},{... | collective-permute-start | bytes 98312 | tf_op jit(solution)/shard_map/ppermute | solution.py:299
  25.5 0.0 all-to-all-done.tpls.tpls_ref
  25.5 0.4 shard_map.50
  26.0 1.3 %collective-permute-start.5 = (f32[16,256]{1,0:T(8,128)S(1)}, f32[16,256]{1,0:T(8,128)S(1)}, u32[]{:S(2)}, u32[]{:S(2)}) collective-permute-start(f32[16,256]{1,0:T(8,128)S(1)} %get-tuple-element.26), channel_id=1, source_target_pairs={{1,0},{2,1},{3,2},{4,3},{5,4},{6,5},{7,6},{8,7},{9,8},{10,9},{11,1... | collective-permute-start | bytes 49160 | tf_op jit(solution)/shard_map/ppermute | solution.py:312
  27.2 6.7 %shard_map.49.done_ref = f32[6,16,512]{2,1,0:T(8,128)S(1)} custom-call(bf16[16,144,128]{2,1,0:T(8,128)(2,1)S(1)} %all-to-all-done.tpls.tpls_ref, bf16[64,4096]{1,0:T(8,128)(2,1)S(1)} %get-tuple-element.24.samples_ref), custom_call_target="tpu_custom_call" | custom-call | flops 1610612736 | bytes 524288 | tf_op jit(solution)/shard_map/pallas_call | solution.py:326
  34.0 0.0 collective-permute-done.4.halo_ref
  34.0 0.0 collective-permute-done.5.after.halo_ref
  34.0 2.9 %shard_map.51.after = f32[8,16,512]{2,1,0:T(8,128)} custom-call(bf16[16,144,128]{2,1,0:T(8,128)(2,1)S(1)} %all-to-all-done.tpls.tpls_ref, bf16[64,4096]{1,0:T(8,128)(2,1)S(1)} %get-tuple-element.24.samples_ref, bf16[64,256]{1,0:T(8,128)(2,1)S(1)} %collective-permute-done.4.halo_ref, f32[6,16,512]{2,1,0:T(8,128)S(1)} %shard_map.49.done_ref, ...), custom_call_target="tpu_custom_call" | custom-call | flops 536870912 | bytes 524288 | tf_op jit(solution)/shard_map/pallas_call | solution.py:334
  36.9 6.0 %all-to-all-start.1 = ((f32[8,16,512]{2,1,0:T(8,128)}), f32[8,16,512]{2,1,0:T(8,128)S(1)}, u32[]{:S(2)}, u32[]{:S(2)}) async-start(f32[8,16,512]{2,1,0:T(8,128)} %shard_map.51.after), calls=%async_computation.1 | async-start | bytes 524288 | tf_op jit(solution)/shard_map/all_to_all | solution.py:342
  42.9 0.5 %shard_map.52.factor_ref = f32[16,512]{1,0:T(8,128)S(1)} custom-call(f32[16,512]{1,0:T(8,128)S(1)} %get-tuple-element.27.power_ref, f32[16,256]{1,0:T(8,128)S(1)} %collective-permute-done.5.after.halo_ref, f32[16,128]{1,0:T(8,128)S(1)} %get-tuple-element.28.scale_ref, f32[8,16,512]{2,1,0:T(8,128)} %shard_map.51.after), custom_call_target="tpu_custom_call" | custom-call | bytes 65536 | tf_op jit(solution)/shard_map/pallas_call | solution.py:343
  43.4 5.9 %all-to-all-done.1.parts_ref = f32[8,16,512]{2,1,0:T(8,128)S(1)} async-done(((f32[8,16,512]{2,1,0:T(8,128)}), f32[8,16,512]{2,1,0:T(8,128)S(1)}, u32[]{:S(2)}, u32[]{:S(2)}) %all-to-all-start.1) | async-done | bytes 262176 | tf_op jit(solution)/shard_map/all_to_all | solution.py:342
  49.3 0.6 %shard_map.53 = f32[16,512]{1,0:T(8,128)} custom-call(f32[8,16,512]{2,1,0:T(8,128)S(1)} %all-to-all-done.1.parts_ref, f32[16,512]{1,0:T(8,128)S(1)} %shard_map.52.factor_ref), custom_call_target="tpu_custom_call" | custom-call | bytes 327680 | tf_op jit(solution)/shard_map/pallas_call | solution.py:350
  (8 shorter events, 0.0 us)
Async XLA Ops:
  2.4 7.6 %copy-start.3 = (bf16[256,512]{1,0:T(8,128)(2,1)S(1)}, bf16[256,512]{1,0:T(8,128)(2,1)}, u32[]{:S(2)}) copy-start(bf16[256,512]{1,0:T(8,128)(2,1)} %get-tuple-element.19) | copy-start | bytes 786436
  2.4 9.2 %copy-start.1 = (bf16[256,512]{1,0:T(8,128)(2,1)S(1)}, bf16[256,512]{1,0:T(8,128)(2,1)}, u32[]{:S(2)}) copy-start(bf16[256,512]{1,0:T(8,128)(2,1)} %get-tuple-element.18.keep_ref) | copy-start | bytes 786436
  2.4 23.1 %all-to-all-start = ((bf16[16,144,128]{2,1,0:T(8,128)(2,1)}), bf16[16,144,128]{2,1,0:T(8,128)(2,1)S(1)}, u32[]{:S(2)}, u32[]{:S(2)}) async-start(bf16[16,144,128]{2,1,0:T(8,128)(2,1)} %get-tuple-element.17), calls=%async_computation | async-start | bytes 1179648 | tf_op jit(solution)/shard_map/all_to_all | solution.py:278
  10.0 1.6 %collective-permute-start = (bf16[256,512]{1,0:T(8,128)(2,1)S(1)}, bf16[256,512]{1,0:T(8,128)(2,1)S(1)}, u32[]{:S(2)}, u32[]{:S(2)}) collective-permute-start(bf16[256,512]{1,0:T(8,128)(2,1)S(1)} %copy-done.3), channel_id=1, source_target_pairs={{0,2},{2,0},{4,6},{6,4},{1,3},{3,1},{5,7},{7,5},{8,10},{10,8},{12,... | collective-permute-start | bytes 786440 | tf_op jit(solution)/shard_map/ppermute | solution.py:280
  11.6 13.9 %copy-start = (bf16[480,512]{1,0:T(8,128)(2,1)S(1)}, bf16[480,512]{1,0:T(8,128)(2,1)}, u32[]{:S(2)}) copy-start(bf16[480,512]{1,0:T(8,128)(2,1)} %wave_ref.1) | copy-start | bytes 1474564
  11.6 6.2 %collective-permute-start.1 = (bf16[2,64,512]{2,1,0:T(8,128)(2,1)S(1)}, bf16[2,64,512]{2,1,0:T(8,128)(2,1)S(1)}, u32[]{:S(2)}, u32[]{:S(2)}) collective-permute-start(bf16[2,64,512]{2,1,0:T(8,128)(2,1)S(1)} %get-tuple-element.21), channel_id=1, source_target_pairs={{0,1},{1,0},{2,3},{3,2},{4,5},{5,4},{6,7},{7,6},{8,9},{9,8},{10,11... | collective-permute-start | bytes 393224 | tf_op jit(solution)/shard_map/ppermute | solution.py:292
  13.2 10.9 %collective-permute-start.2 = (bf16[2,64,512]{2,1,0:T(8,128)(2,1)S(1)}, bf16[2,64,512]{2,1,0:T(8,128)(2,1)S(1)}, u32[]{:S(2)}, u32[]{:S(2)}) collective-permute-start(bf16[2,64,512]{2,1,0:T(8,128)(2,1)S(1)} %get-tuple-element.22), channel_id=1, source_target_pairs={{0,4},{1,5},{2,6},{3,7},{4,0},{5,1},{6,2},{7,3},{8,12},{9,13},{10,... | collective-permute-start | bytes 393224 | tf_op jit(solution)/shard_map/ppermute | solution.py:292
  15.1 9.0 %collective-permute-start.3 = (bf16[2,64,512]{2,1,0:T(8,128)(2,1)S(1)}, bf16[2,64,512]{2,1,0:T(8,128)(2,1)S(1)}, u32[]{:S(2)}, u32[]{:S(2)}) collective-permute-start(bf16[2,64,512]{2,1,0:T(8,128)(2,1)S(1)} %get-tuple-element.23), channel_id=1, source_target_pairs={{0,5},{1,4},{2,7},{3,6},{4,1},{5,0},{6,3},{7,2},{8,13},{9,12},{10,... | collective-permute-start | bytes 393224 | tf_op jit(solution)/shard_map/ppermute | solution.py:292
  24.1 1.4 %copy-start.2 = (s32[480]{0:T(512)S(1)}, s32[480]{0:T(512)}, u32[]{:S(2)}) copy-start(s32[480]{0:T(512)} %param.7) | copy-start | bytes 5764
  24.2 9.8 %collective-permute-start.4 = (bf16[64,256]{1,0:T(8,128)(2,1)S(1)}, bf16[64,256]{1,0:T(8,128)(2,1)S(1)}, u32[]{:S(2)}, u32[]{:S(2)}) collective-permute-start(bf16[64,256]{1,0:T(8,128)(2,1)S(1)} %get-tuple-element.25), channel_id=1, source_target_pairs={{8,0},{16,8},{24,16},{9,1},{17,9},{25,17},{10,2},{18,10},{26,18},{... | collective-permute-start | bytes 98312 | tf_op jit(solution)/shard_map/ppermute | solution.py:299
  26.0 8.0 %collective-permute-start.5 = (f32[16,256]{1,0:T(8,128)S(1)}, f32[16,256]{1,0:T(8,128)S(1)}, u32[]{:S(2)}, u32[]{:S(2)}) collective-permute-start(f32[16,256]{1,0:T(8,128)S(1)} %get-tuple-element.26), channel_id=1, source_target_pairs={{1,0},{2,1},{3,2},{4,3},{5,4},{6,5},{7,6},{8,7},{9,8},{10,9},{11,1... | collective-permute-start | bytes 49160 | tf_op jit(solution)/shard_map/ppermute | solution.py:312
  36.9 12.4 %all-to-all-start.1 = ((f32[8,16,512]{2,1,0:T(8,128)}), f32[8,16,512]{2,1,0:T(8,128)S(1)}, u32[]{:S(2)}, u32[]{:S(2)}) async-start(f32[8,16,512]{2,1,0:T(8,128)} %shard_map.51.after), calls=%async_computation.1 | async-start | bytes 524288 | tf_op jit(solution)/shard_map/all_to_all | solution.py:342

commit v5 on v4

--- a/solution.py
+++ b/solution.py
@@ -190,13 +190,28 @@
     correlate(tpls, samples_ref[:, :columns], out_ref, 0, left, shifts, products)
 
 
-def last_dots_kernel(tpls, samples_ref, halo_ref, done_ref, after, out_ref, *scratch):
+def last_dots_kernel(tpls, samples_ref, halo_ref, done_ref, after, *refs):
     del after
+    keep_ref, send_ref, out_ref = refs[:3]
+    scratch = refs[3:]
     rest = samples_ref.shape[1] + halo_ref.shape[1] - scratch[1].shape[1]
     samples = jnp.concatenate([samples_ref[:, rest:], halo_ref[...]], axis=1)
     first = done_ref.shape[0]
     out_ref[:first] = done_ref[...]
     correlate(tpls, samples, out_ref, first, *scratch)
+    core = lax.rem(lax.axis_index("inner"), 2)
+    half = keep_ref.shape[0]
+    run = half // 2
+    for y in range(2):
+        for tm in range(run):
+            keep_ref[y * run + tm] = out_ref[(2 * y + core) * run + tm]
+            send_ref[y * run + tm] = out_ref[(2 * y + 1 - core) * run + tm]
+
+
+def add_kernel(tm_count, keep_ref, got_ref, *outs):
+    me = lax.div(lax.axis_index("inner"), 2) * tm_count + lax.axis_index("tm")
+    for flip, out_ref in enumerate(outs):
+        out_ref[...] = keep_ref[me ^ flip] + got_ref[me ^ flip]
 
 
 def power_kernel(stations, wave_ref, tpls_ref, order_ref, out_ref, head_ref, scale_ref):
@@ -234,8 +249,12 @@
     out_ref[...] = scale_ref[:, :1] / jnp.sqrt(running[:, :slab] + EPSILON)
 
 
-def finish_kernel(parts_ref, factor_ref, out_ref):
-    out_ref[...] = jnp.sum(parts_ref[...], axis=0) * factor_ref[...]
+def finish_kernel(*refs):
+    parts, factor_ref, out_ref = refs[:-2], refs[-2], refs[-1]
+    total = parts[0][...]
+    for part in parts[1:]:
+        total = total + part[...]
+    out_ref[...] = total * factor_ref[...]
 
 
 def on_device(waveforms, templates, station_mask, channel_order):
@@ -251,7 +270,7 @@
     chunk = group * slab
     span = 2 * slab
     total = blk_count * tm_count
-    blk, members, every = ("outer", "inner"), ("inner", "tm"), ("outer", "inner", "tm")
+    blk, every = ("outer", "inner"), ("outer", "inner", "tm")
     sds = jax.ShapeDtypeStruct
     order_row = channel_order[None, :]
 
@@ -285,11 +304,13 @@
         [sds((2, part, slab), BF16)] * half,
         bytes_accessed=padded * slab * 2,
     )(keep, got)
-    waves = [parts[0]]
-    for flip in range(1, half):
+
+    def swap(part, flip):
         y, tm = flip // tm_count, flip % tm_count
         route = [(i, i ^ (2 * tm_count * y + tm)) for i in range(total)]
-        waves.append(lax.ppermute(parts[flip], every, route))
+        return lax.ppermute(part, every, route)
+
+    waves = [parts[0]] + [swap(parts[flip], flip) for flip in range(1, half)]
     samples, head = call(
         functools.partial(join_kernel, tm_count),
         [VMEM] * half,
@@ -331,28 +352,35 @@
         flops=work * (blocks - 1),
         bytes_accessed=part * chunk * 2,
     )(tpls, samples)
-    partials = call(
+    keep, send = call(
         last_dots_kernel,
         [VMEM] * 4 + [AFTER],
-        sds((group, blk_count, slab), F32),
-        scratch(span + window),
+        [sds((half, blk_count, slab), F32)] * 2,
+        [pltpu.VMEM((group, blk_count, slab), F32)] + scratch(span + window),
         flops=work,
         bytes_accessed=part * chunk * 2,
     )(tpls, samples, halo, partials, power_halo)
-    sums = lax.all_to_all(partials, members, 0, 0, tiled=True)
+    got = lax.ppermute(send, "inner", [(b, b ^ 1) for b in range(INNER)])
     factor = call(
         factor_kernel,
         [VMEM] * 3 + [AFTER],
         sds((blk_count, slab), F32),
         [pltpu.VMEM((blk_count, slab + window), F32)],
         bytes_accessed=blk_count * slab * 8,
-    )(power, power_halo, scale, partials)
+    )(power, power_halo, scale, send)
+    sums = call(
+        functools.partial(add_kernel, tm_count),
+        [VMEM] * 2,
+        [sds((blk_count, slab), F32)] * half,
+        bytes_accessed=blk_count * slab * 12 * half,
+    )(keep, got)
+    sums = [sums[0]] + [swap(sums[flip], flip) for flip in range(1, half)]
     return call(
         finish_kernel,
-        [VMEM] * 2,
+        [VMEM] * (half + 1),
         sds((blk_count, slab), F32),
-        bytes_accessed=blk_count * slab * 4 * (group + 2),
-    )(sums, factor)
+        bytes_accessed=blk_count * slab * 4 * (half + 2),
+    )(*sums, factor)
 
 
 def solution(mesh):

time: 50.3 us -> 48.7 us (0.968)
  waiting for transfers between devices: 16 us -> 15.2 us
  Pallas kernels: 13.7 us -> 13.1 us
    all_to_all x1 -> x0, starting transfers between devices: 5.96 us -> none  [on_device(): sums = lax.all_to_all(partials, members, 0, 0, tiled=True)]
    all_to_all x1 -> x0, waiting for transfers between devices: 5.93 us -> none  [on_device(): sums = lax.all_to_all(partials, members, 0, 0, tiled=True)]
    ppermute x3 -> x6, waiting for transfers between devices: 8.89 us -> 13 us  [swap(): return lax.ppermute(part, every, route)]
    ppermute x3 -> x6, starting transfers between devices: 3.57 us -> 7.13 us  [swap(): return lax.ppermute(part, every, route)]
    ppermute x1 -> x2, starting transfers between devices: 0.47 us -> 2.75 us  [on_device(): got = lax.ppermute(send, 'inner', [(b, b ^ 1) for b in range(INNER)])]
    ppermute x1 -> x2, waiting for transfers between devices: 1.16 us -> 2.15 us  [on_device(): got = lax.ppermute(send, 'inner', [(b, b ^ 1) for b in range(INNER)])]
    pallas_call x2 -> x3, Pallas kernels: 3.53 us -> 2.88 us  [the longest x1 2.24 us: on_device(): call(last_dots_kernel, [VMEM] * 4 + [AFTER], [sds((half, blk_count, slab)...]
  transfers between devices with their start and end apart: 8 -> 11, of which waited for: 4 -> 6; matrix products, arithmetic and copies ran while one was open for 0% -> 0% of each run, Pallas kernels for 16% -> 16%
where the time goes in v5:
time: 48.7 us; the launch traced here: 48.4 us
  starting transfers between devices  20 us (41%)
  waiting for transfers between devices  15.2 us (31%)
  Pallas kernels  13.1 us (27%)
    ppermute x6, waiting for transfers between devices, swap(): return lax.ppermute(part, every, route)  13 us
    all_to_all x1, starting transfers between devices, on_device(): tpls = lax.all_to_all(payload, blk, 0, 0, tiled=True)  7.53 us
    ppermute x6, starting transfers between devices, swap(): return lax.ppermute(part, every, route)  7.13 us
    pallas_call x1, Pallas kernels, on_device(): call(first_dots_kernel, [VMEM] * 2, sds((2 * (blocks - 1), blk_count, sla...  6.72 us
    ppermute x2, starting transfers between devices, on_device(): got = lax.ppermute(send, 'inner', [(b, b ^ 1) for b in range(INNER)])  2.75 us
    pallas_call x1, Pallas kernels, on_device(): call(functools.partial(prologue_kernel, tm_count), [HBM] * 4, [sds((blk_c...  2.41 us
    pallas_call x1, Pallas kernels, on_device(): call(last_dots_kernel, [VMEM] * 4 + [AFTER], [sds((half, blk_count, slab)...  2.24 us
    ppermute x2, waiting for transfers between devices, on_device(): got = lax.ppermute(send, 'inner', [(b, b ^ 1) for b in range(INNER)])  2.15 us
  transfers between devices with their start and end apart: 11, of which 6 were waited for; matrix products, arithmetic and copies ran while one was open for 0% of the time, Pallas kernels for 16%

profile of v5, /device:TPU:0, one launch (start us, length us, event | category | flops | bytes accessed | tf_op | source)
XLA Modules:
  0.0 48.4 jit_solution(6175104678521742558)
XLA Ops:
  0.0 2.4 %shard_map.46 = (bf16[16,144,128]{2,1,0:T(8,128)(2,1)}, bf16[256,512]{1,0:T(8,128)(2,1)}, bf16[256,512]{1,0:T(8,128)(2,1)}) custom-call(bf16[1,480,256]{2,1,0:T(8,128)(2,1)} %tpl_hbm.1, s32[1,160]{1,0:T(1,128)} %flag_hbm.1, s32[1,480]{1,0:T(1,128)} %bitcast.1, bf16[480,512]{1,0:T(8,128)(2,1)} %wave_ref.1), custom_call_target="tpu_custom_call" | custom-call | bytes 737280 | tf_op jit(solution)/shard_map/pallas_call | solution.py:277
  2.4 7.5 %all-to-all-start = ((bf16[16,144,128]{2,1,0:T(8,128)(2,1)}), bf16[16,144,128]{2,1,0:T(8,128)(2,1)S(1)}, u32[]{:S(2)}, u32[]{:S(2)}) async-start(bf16[16,144,128]{2,1,0:T(8,128)(2,1)} %get-tuple-element.23), calls=%async_computation | async-start | bytes 1179648 | tf_op jit(solution)/shard_map/all_to_all | solution.py:297
  10.0 0.5 collective-permute-start
  10.5 1.2 %collective-permute-done.got_ref = bf16[256,512]{1,0:T(8,128)(2,1)S(1)} collective-permute-done((bf16[256,512]{1,0:T(8,128)(2,1)S(1)}, bf16[256,512]{1,0:T(8,128)(2,1)S(1)}, u32[]{:S(2)}, u32[]{:S(2)}) %collective-permute-start) | collective-permute-done | bytes 262176 | tf_op jit(solution)/shard_map/ppermute | solution.py:299
  11.7 1.6 %collective-permute-start.1 = (bf16[2,64,512]{2,1,0:T(8,128)(2,1)S(1)}, bf16[2,64,512]{2,1,0:T(8,128)(2,1)S(1)}, u32[]{:S(2)}, u32[]{:S(2)}) collective-permute-start(bf16[2,64,512]{2,1,0:T(8,128)(2,1)S(1)} %get-tuple-element.27), channel_id=1, source_target_pairs={{0,1},{1,0},{2,3},{3,2},{4,5},{5,4},{6,7},{7,6},{8,9},{9,8},{10,11... | collective-permute-start | bytes 393224 | tf_op jit(solution)/shard_map/ppermute | solution.py:311
  13.2 1.9 %collective-permute-start.2 = (bf16[2,64,512]{2,1,0:T(8,128)(2,1)S(1)}, bf16[2,64,512]{2,1,0:T(8,128)(2,1)S(1)}, u32[]{:S(2)}, u32[]{:S(2)}) collective-permute-start(bf16[2,64,512]{2,1,0:T(8,128)(2,1)S(1)} %get-tuple-element.28), channel_id=1, source_target_pairs={{0,4},{1,5},{2,6},{3,7},{4,0},{5,1},{6,2},{7,3},{8,12},{9,13},{10,... | collective-permute-start | bytes 393224 | tf_op jit(solution)/shard_map/ppermute | solution.py:311
  15.1 0.1 collective-permute-start.3
  15.2 2.6 %collective-permute-done.1.refs_1_ = bf16[2,64,512]{2,1,0:T(8,128)(2,1)S(1)} collective-permute-done((bf16[2,64,512]{2,1,0:T(8,128)(2,1)S(1)}, bf16[2,64,512]{2,1,0:T(8,128)(2,1)S(1)}, u32[]{:S(2)}, u32[]{:S(2)}) %collective-permute-start.1) | collective-permute-done | bytes 131104 | tf_op jit(solution)/shard_map/ppermute | solution.py:311
  17.9 6.3 %collective-permute-done.2.refs_2_ = bf16[2,64,512]{2,1,0:T(8,128)(2,1)S(1)} collective-permute-done((bf16[2,64,512]{2,1,0:T(8,128)(2,1)S(1)}, bf16[2,64,512]{2,1,0:T(8,128)(2,1)S(1)}, u32[]{:S(2)}, u32[]{:S(2)}) %collective-permute-start.2) | collective-permute-done | bytes 131104 | tf_op jit(solution)/shard_map/ppermute | solution.py:311
  24.1 0.1 shard_map.48
  24.2 1.3 %collective-permute-start.4 = (bf16[64,256]{1,0:T(8,128)(2,1)S(1)}, bf16[64,256]{1,0:T(8,128)(2,1)S(1)}, u32[]{:S(2)}, u32[]{:S(2)}) collective-permute-start(bf16[64,256]{1,0:T(8,128)(2,1)S(1)} %get-tuple-element.31), channel_id=1, source_target_pairs={{8,0},{16,8},{24,16},{9,1},{17,9},{25,17},{10,2},{18,10},{26,18},{... | collective-permute-start | bytes 98312 | tf_op jit(solution)/shard_map/ppermute | solution.py:320
  25.5 0.4 shard_map.50
  26.0 1.3 %collective-permute-start.5 = (f32[16,256]{1,0:T(8,128)S(1)}, f32[16,256]{1,0:T(8,128)S(1)}, u32[]{:S(2)}, u32[]{:S(2)}) collective-permute-start(f32[16,256]{1,0:T(8,128)S(1)} %get-tuple-element.32), channel_id=1, source_target_pairs={{1,0},{2,1},{3,2},{4,3},{5,4},{6,5},{7,6},{8,7},{9,8},{10,9},{11,1... | collective-permute-start | bytes 49160 | tf_op jit(solution)/shard_map/ppermute | solution.py:333
  27.3 6.7 %shard_map.49.done_ref = f32[6,16,512]{2,1,0:T(8,128)S(1)} custom-call(bf16[16,144,128]{2,1,0:T(8,128)(2,1)S(1)} %all-to-all-done.tpls.tpls_ref, bf16[64,4096]{1,0:T(8,128)(2,1)S(1)} %get-tuple-element.30.samples_ref), custom_call_target="tpu_custom_call" | custom-call | flops 1610612736 | bytes 524288 | tf_op jit(solution)/shard_map/pallas_call | solution.py:347
  34.0 2.2 %shard_map.51 = (f32[4,16,512]{2,1,0:T(8,128)S(1)}, f32[4,16,512]{2,1,0:T(8,128)S(1)}) custom-call(bf16[16,144,128]{2,1,0:T(8,128)(2,1)S(1)} %all-to-all-done.tpls.tpls_ref, bf16[64,4096]{1,0:T(8,128)(2,1)S(1)} %get-tuple-element.30.samples_ref, bf16[64,256]{1,0:T(8,128)(2,1)S(1)} %collective-permute-done.4.halo_ref, f32[6,16,512]{2,1,0:T(8,128)S(1)} %shard_map.49.done_ref, ...), custom_call_target="tpu_custom_call" | custom-call | flops 536870912 | bytes 524288 | tf_op jit(solution)/shard_map/pallas_call | solution.py:355
  36.2 2.3 %collective-permute-start.6 = (f32[4,16,512]{2,1,0:T(8,128)S(1)}, f32[4,16,512]{2,1,0:T(8,128)S(1)}, u32[]{:S(2)}, u32[]{:S(2)}) collective-permute-start(f32[4,16,512]{2,1,0:T(8,128)S(1)} %get-tuple-element.34.after), channel_id=1, source_target_pairs={{0,2},{2,0},{4,6},{6,4},{1,3},{3,1},{5,7},{7,5},{8,10},{10,8},{12,... | collective-permute-start | bytes 393224 | tf_op jit(solution)/shard_map/ppermute | solution.py:363
  38.5 1.0 %collective-permute-done.6.got_ref = f32[4,16,512]{2,1,0:T(8,128)S(1)} collective-permute-done((f32[4,16,512]{2,1,0:T(8,128)S(1)}, f32[4,16,512]{2,1,0:T(8,128)S(1)}, u32[]{:S(2)}, u32[]{:S(2)}) %collective-permute-start.6) | collective-permute-done | bytes 131104 | tf_op jit(solution)/shard_map/ppermute | solution.py:363
  39.5 0.9 %collective-permute-start.7 = (f32[16,512]{1,0:T(8,128)S(1)}, f32[16,512]{1,0:T(8,128)S(1)}, u32[]{:S(2)}, u32[]{:S(2)}) collective-permute-start(f32[16,512]{1,0:T(8,128)S(1)} %get-tuple-element.36), channel_id=1, source_target_pairs={{0,1},{1,0},{2,3},{3,2},{4,5},{5,4},{6,7},{7,6},{8,9},{9,8},{10,11... | collective-permute-start | bytes 98312 | tf_op jit(solution)/shard_map/ppermute | solution.py:311
  40.4 2.6 %collective-permute-start.8 = (f32[16,512]{1,0:T(8,128)S(1)}, f32[16,512]{1,0:T(8,128)S(1)}, u32[]{:S(2)}, u32[]{:S(2)}) collective-permute-start(f32[16,512]{1,0:T(8,128)S(1)} %get-tuple-element.37), channel_id=1, source_target_pairs={{0,4},{1,5},{2,6},{3,7},{4,0},{5,1},{6,2},{7,3},{8,12},{9,13},{10,... | collective-permute-start | bytes 98312 | tf_op jit(solution)/shard_map/ppermute | solution.py:311
  43.0 0.1 collective-permute-start.9
  43.1 0.5 %shard_map.53.refs_4_ = f32[16,512]{1,0:T(8,128)S(1)} custom-call(f32[16,512]{1,0:T(8,128)S(1)} %get-tuple-element.39.power_ref, f32[16,256]{1,0:T(8,128)S(1)} %collective-permute-done.5.after.halo_ref, f32[16,128]{1,0:T(8,128)S(1)} %get-tuple-element.40.scale_ref, f32[4,16,512]{2,1,0:T(8,128)S(1)} %get-tuple-element.34.after), custom_call_target="tpu_custom_call" | custom-call | bytes 65536 | tf_op jit(solution)/shard_map/pallas_call | solution.py:364
  43.6 1.2 %collective-permute-done.8.refs_2_ = f32[16,512]{1,0:T(8,128)S(1)} collective-permute-done((f32[16,512]{1,0:T(8,128)S(1)}, f32[16,512]{1,0:T(8,128)S(1)}, u32[]{:S(2)}, u32[]{:S(2)}) %collective-permute-start.8) | collective-permute-done | bytes 32800 | tf_op jit(solution)/shard_map/ppermute | solution.py:311
  44.9 2.9 %collective-permute-done.9.refs_3_ = f32[16,512]{1,0:T(8,128)S(1)} collective-permute-done((f32[16,512]{1,0:T(8,128)S(1)}, f32[16,512]{1,0:T(8,128)S(1)}, u32[]{:S(2)}, u32[]{:S(2)}) %collective-permute-start.9) | collective-permute-done | bytes 32800 | tf_op jit(solution)/shard_map/ppermute | solution.py:311
  47.8 0.6 %shard_map.54 = f32[16,512]{1,0:T(8,128)} custom-call(f32[16,512]{1,0:T(8,128)S(1)} %get-tuple-element.35.refs_0_, f32[16,512]{1,0:T(8,128)S(1)} %collective-permute-done.7.refs_1_, f32[16,512]{1,0:T(8,128)S(1)} %collective-permute-done.8.refs_2_, f32[16,512]{1,0:T(8,128)S(1)} %collective-permute-done.9.refs_3_, f32[16,512]{1,0:T(8,128)S(1)} %shard_map.53.refs_4_), custom_call_target="tpu_custom_call" | custom-call | bytes 196608 | tf_op jit(solution)/shard_map/pallas_call | solution.py:378
  (15 shorter events, 0.1 us)
Async XLA Ops:
  2.4 7.6 %copy-start.3 = (bf16[256,512]{1,0:T(8,128)(2,1)S(1)}, bf16[256,512]{1,0:T(8,128)(2,1)}, u32[]{:S(2)}) copy-start(bf16[256,512]{1,0:T(8,128)(2,1)} %get-tuple-element.25) | copy-start | bytes 786436
  2.4 9.2 %copy-start.1 = (bf16[256,512]{1,0:T(8,128)(2,1)S(1)}, bf16[256,512]{1,0:T(8,128)(2,1)}, u32[]{:S(2)}) copy-start(bf16[256,512]{1,0:T(8,128)(2,1)} %get-tuple-element.24.keep_ref) | copy-start | bytes 786436
  2.4 23.1 %all-to-all-start = ((bf16[16,144,128]{2,1,0:T(8,128)(2,1)}), bf16[16,144,128]{2,1,0:T(8,128)(2,1)S(1)}, u32[]{:S(2)}, u32[]{:S(2)}) async-start(bf16[16,144,128]{2,1,0:T(8,128)(2,1)} %get-tuple-element.23), calls=%async_computation | async-start | bytes 1179648 | tf_op jit(solution)/shard_map/all_to_all | solution.py:297
  10.0 1.6 %collective-permute-start = (bf16[256,512]{1,0:T(8,128)(2,1)S(1)}, bf16[256,512]{1,0:T(8,128)(2,1)S(1)}, u32[]{:S(2)}, u32[]{:S(2)}) collective-permute-start(bf16[256,512]{1,0:T(8,128)(2,1)S(1)} %copy-done.3), channel_id=1, source_target_pairs={{0,2},{2,0},{4,6},{6,4},{1,3},{3,1},{5,7},{7,5},{8,10},{10,8},{12,... | collective-permute-start | bytes 786440 | tf_op jit(solution)/shard_map/ppermute | solution.py:299
  11.6 13.9 %copy-start = (bf16[480,512]{1,0:T(8,128)(2,1)S(1)}, bf16[480,512]{1,0:T(8,128)(2,1)}, u32[]{:S(2)}) copy-start(bf16[480,512]{1,0:T(8,128)(2,1)} %wave_ref.1) | copy-start | bytes 1474564
  11.7 6.2 %collective-permute-start.1 = (bf16[2,64,512]{2,1,0:T(8,128)(2,1)S(1)}, bf16[2,64,512]{2,1,0:T(8,128)(2,1)S(1)}, u32[]{:S(2)}, u32[]{:S(2)}) collective-permute-start(bf16[2,64,512]{2,1,0:T(8,128)(2,1)S(1)} %get-tuple-element.27), channel_id=1, source_target_pairs={{0,1},{1,0},{2,3},{3,2},{4,5},{5,4},{6,7},{7,6},{8,9},{9,8},{10,11... | collective-permute-start | bytes 393224 | tf_op jit(solution)/shard_map/ppermute | solution.py:311
  13.2 10.9 %collective-permute-start.2 = (bf16[2,64,512]{2,1,0:T(8,128)(2,1)S(1)}, bf16[2,64,512]{2,1,0:T(8,128)(2,1)S(1)}, u32[]{:S(2)}, u32[]{:S(2)}) collective-permute-start(bf16[2,64,512]{2,1,0:T(8,128)(2,1)S(1)} %get-tuple-element.28), channel_id=1, source_target_pairs={{0,4},{1,5},{2,6},{3,7},{4,0},{5,1},{6,2},{7,3},{8,12},{9,13},{10,... | collective-permute-start | bytes 393224 | tf_op jit(solution)/shard_map/ppermute | solution.py:311
  15.1 9.0 %collective-permute-start.3 = (bf16[2,64,512]{2,1,0:T(8,128)(2,1)S(1)}, bf16[2,64,512]{2,1,0:T(8,128)(2,1)S(1)}, u32[]{:S(2)}, u32[]{:S(2)}) collective-permute-start(bf16[2,64,512]{2,1,0:T(8,128)(2,1)S(1)} %get-tuple-element.29), channel_id=1, source_target_pairs={{0,5},{1,4},{2,7},{3,6},{4,1},{5,0},{6,3},{7,2},{8,13},{9,12},{10,... | collective-permute-start | bytes 393224 | tf_op jit(solution)/shard_map/ppermute | solution.py:311
  24.1 1.4 %copy-start.2 = (s32[480]{0:T(512)S(1)}, s32[480]{0:T(512)}, u32[]{:S(2)}) copy-start(s32[480]{0:T(512)} %param.7) | copy-start | bytes 5764
  24.2 9.8 %collective-permute-start.4 = (bf16[64,256]{1,0:T(8,128)(2,1)S(1)}, bf16[64,256]{1,0:T(8,128)(2,1)S(1)}, u32[]{:S(2)}, u32[]{:S(2)}) collective-permute-start(bf16[64,256]{1,0:T(8,128)(2,1)S(1)} %get-tuple-element.31), channel_id=1, source_target_pairs={{8,0},{16,8},{24,16},{9,1},{17,9},{25,17},{10,2},{18,10},{26,18},{... | collective-permute-start | bytes 98312 | tf_op jit(solution)/shard_map/ppermute | solution.py:320
  26.0 8.0 %collective-permute-start.5 = (f32[16,256]{1,0:T(8,128)S(1)}, f32[16,256]{1,0:T(8,128)S(1)}, u32[]{:S(2)}, u32[]{:S(2)}) collective-permute-start(f32[16,256]{1,0:T(8,128)S(1)} %get-tuple-element.32), channel_id=1, source_target_pairs={{1,0},{2,1},{3,2},{4,3},{5,4},{6,5},{7,6},{8,7},{9,8},{10,9},{11,1... | collective-permute-start | bytes 49160 | tf_op jit(solution)/shard_map/ppermute | solution.py:333
  36.2 3.3 %collective-permute-start.6 = (f32[4,16,512]{2,1,0:T(8,128)S(1)}, f32[4,16,512]{2,1,0:T(8,128)S(1)}, u32[]{:S(2)}, u32[]{:S(2)}) collective-permute-start(f32[4,16,512]{2,1,0:T(8,128)S(1)} %get-tuple-element.34.after), channel_id=1, source_target_pairs={{0,2},{2,0},{4,6},{6,4},{1,3},{3,1},{5,7},{7,5},{8,10},{10,8},{12,... | collective-permute-start | bytes 393224 | tf_op jit(solution)/shard_map/ppermute | solution.py:363
  39.5 4.1 %collective-permute-start.7 = (f32[16,512]{1,0:T(8,128)S(1)}, f32[16,512]{1,0:T(8,128)S(1)}, u32[]{:S(2)}, u32[]{:S(2)}) collective-permute-start(f32[16,512]{1,0:T(8,128)S(1)} %get-tuple-element.36), channel_id=1, source_target_pairs={{0,1},{1,0},{2,3},{3,2},{4,5},{5,4},{6,7},{7,6},{8,9},{9,8},{10,11... | collective-permute-start | bytes 98312 | tf_op jit(solution)/shard_map/ppermute | solution.py:311
  40.4 4.5 %collective-permute-start.8 = (f32[16,512]{1,0:T(8,128)S(1)}, f32[16,512]{1,0:T(8,128)S(1)}, u32[]{:S(2)}, u32[]{:S(2)}) collective-permute-start(f32[16,512]{1,0:T(8,128)S(1)} %get-tuple-element.37), channel_id=1, source_target_pairs={{0,4},{1,5},{2,6},{3,7},{4,0},{5,1},{6,2},{7,3},{8,12},{9,13},{10,... | collective-permute-start | bytes 98312 | tf_op jit(solution)/shard_map/ppermute | solution.py:311
  43.0 4.8 %collective-permute-start.9 = (f32[16,512]{1,0:T(8,128)S(1)}, f32[16,512]{1,0:T(8,128)S(1)}, u32[]{:S(2)}, u32[]{:S(2)}) collective-permute-start(f32[16,512]{1,0:T(8,128)S(1)} %get-tuple-element.38), channel_id=1, source_target_pairs={{0,5},{1,4},{2,7},{3,6},{4,1},{5,0},{6,3},{7,2},{8,13},{9,12},{10,... | collective-permute-start | bytes 98312 | tf_op jit(solution)/shard_map/ppermute | solution.py:311

commit v6 on v5

--- a/solution.py
+++ b/solution.py
@@ -45,12 +45,12 @@
 
 
 def side_major(inner):
-    return (inner % 2) * (INNER // 2) + inner // 2
+    return lax.rem(inner, 2) * (INNER // 2) + lax.div(inner, 2)
 
 
 def prologue_kernel(tm_count, tpl_hbm, flag_hbm, order_hbm, wave_hbm, *refs):
-    out_ref, send_ref, keep_ref = refs[:3]
-    tpl_pad, flag_ref, order_ref, order_pad, wave_pad, turned, sems = refs[3:]
+    outs, send_ref, keep_ref = refs[:INNER], refs[INNER], refs[INNER + 1]
+    tpl_pad, flag_ref, order_ref, order_pad, wave_pad, turned, sems = refs[INNER + 2 :]
     channels, window = tpl_hbm.shape[1:]
     copies = [
         pltpu.make_async_copy(flag_hbm, flag_ref, sems.at[0]),
@@ -92,25 +92,30 @@
     extra = jnp.concatenate(extra, axis=0).astype(BF16)
     my_tm = lax.axis_index("tm")
     spot = lax.broadcasted_iota(jnp.int32, (FINE, LANES), 1) // part
-    for member in range(INNER):
-        start = side_major(member) * LANES
-        pieces = []
+    inner = lax.axis_index("inner")
+    for flip in range(INNER):
+        start = pl.multiple_of(side_major(inner ^ flip) * LANES, LANES)
         for step in range(window // (FINE * tm_count)):
             tile = jnp.zeros((FINE, LANES), F32)
             for within in range(tm_count):
                 row = FINE * (step * tm_count + within)
-                chunk = turned[row : row + FINE, start : start + LANES].astype(F32)
+                chunk = turned[row : row + FINE, pl.ds(start, LANES)].astype(F32)
                 turn = lax.rem(part * (within - my_tm) + LANES, LANES)
                 tile = jnp.where(spot == within, pltpu.roll(chunk, turn, 1), tile)
-            pieces.append(tile.astype(BF16))
-        payload = jnp.concatenate(pieces + [extra], axis=0)
-        for target in range(member, out_ref.shape[0], INNER):
-            out_ref[target] = payload
+            outs[flip][FINE * step : FINE * (step + 1), :] = tile.astype(BF16)
+        outs[flip][window * part // LANES :, :] = extra
     copies[3].wait()
-    core = lax.rem(lax.axis_index("inner"), 2)
+    core = lax.rem(inner, 2)
     half = padded // 2
     keep_ref[...] = wave_pad[pl.ds(pl.multiple_of(core * half, half), half), :]
     send_ref[...] = wave_pad[pl.ds(pl.multiple_of((1 - core) * half, half), half), :]
+
+
+def pack_kernel(*refs):
+    parts, out_ref = refs[:-1], refs[-1]
+    inner = lax.axis_index("inner")
+    for flip, part in enumerate(parts):
+        out_ref[inner ^ flip] = part[...]
 
 
 def split_kernel(tm_count, keep_ref, got_ref, *outs):
@@ -138,35 +143,37 @@
 
 
 def correlate(tpls, samples, out_ref, first, left, shifts, products):
-    count = tpls.shape[0]
     slab = out_ref.shape[2]
     part, columns = samples.shape
-    copies = shifts.shape[0] // part
-    for copy in range(copies):
-        turned = samples if copy == 0 else pltpu.roll(samples, columns - FINE * copy, 1)
-        shifts[copy * part : (copy + 1) * part, :] = turned
-    parts, _, depth = left.shape
+    depth = left.shape[1]
+    copies = LANES // FINE
+    usable = columns - 2 * LANES
+    for copy in range(depth // part):
+        tile, turn = copy // copies * LANES, copy % copies * FINE
+        turned = samples if turn == 0 else pltpu.roll(samples, columns - turn, 1)
+        shifts[copy * part : (copy + 1) * part, :] = turned[:, tile : tile + usable + LANES]
     steps = depth // LANES
-    for template in range(count):
-        row = template * FINE
-        for step in range(parts * steps):
-            lane = (step % steps) * LANES
-            left[step // steps, row : row + FINE, lane : lane + LANES] = tpls[
-                template, FINE * step : FINE * (step + 1), :
-            ]
+    outer = lax.axis_index("outer")
+    for flip, pack in enumerate(tpls):
+        for inner in range(INNER):
+            row = pl.multiple_of(((outer ^ flip) * INNER + inner) * FINE, FINE)
+            for step in range(steps):
+                left[pl.ds(row, FINE), step * LANES : (step + 1) * LANES] = pack[
+                    inner, FINE * step : FINE * (step + 1), :
+                ]
+    count = len(tpls) * INNER
     tiles = products.shape[0]
     span = (tiles - 1) * LANES
     per_block = span // slab
 
     def block(index, carry):
         start = pl.multiple_of(index * span, span)
-        product = None
-        for piece in range(parts):
-            here = pl.ds(pl.multiple_of(start + piece * copies * FINE, LANES), span + LANES)
-            term = jnp.dot(left[piece], shifts[:, here], preferred_element_type=F32)
-            product = term if product is None else product + term
-        for tile in range(tiles):
-            products[tile] = product[:, tile * LANES : (tile + 1) * LANES]
+        for tile in range(0, tiles, 2):
+            width = min(2, tiles - tile)
+            here = pl.ds(pl.multiple_of(start + tile * LANES, LANES), width * LANES)
+            product = jnp.dot(left[...], shifts[:, here], preferred_element_type=F32)
+            for piece in range(width):
+                products[tile + piece] = product[:, piece * LANES : (piece + 1) * LANES]
 
         def fine_rows(fine):
             return jnp.concatenate(
@@ -181,20 +188,20 @@
             out_ref[first + index * per_block + piece] = total[:, piece * slab : (piece + 1) * slab]
         return carry
 
-    blocks = (columns - 2 * LANES) // span
-    lax.fori_loop(0, blocks, block, 0)
-
-
-def first_dots_kernel(tpls, samples_ref, out_ref, left, shifts, products):
-    columns = shifts.shape[1]
-    correlate(tpls, samples_ref[:, :columns], out_ref, 0, left, shifts, products)
-
-
-def last_dots_kernel(tpls, samples_ref, halo_ref, done_ref, after, *refs):
-    del after
-    keep_ref, send_ref, out_ref = refs[:3]
-    scratch = refs[3:]
-    rest = samples_ref.shape[1] + halo_ref.shape[1] - scratch[1].shape[1]
+    lax.fori_loop(0, usable // span, block, 0)
+
+
+def first_dots_kernel(count, *refs):
+    tpls, samples_ref, out_ref, scratch = refs[:count], refs[count], refs[count + 1], refs[count + 2 :]
+    columns = scratch[1].shape[1] + LANES
+    correlate(tpls, samples_ref[:, :columns], out_ref, 0, *scratch)
+
+
+def last_dots_kernel(count, *refs):
+    tpls, (samples_ref, halo_ref, done_ref, _) = refs[:count], refs[count : count + 4]
+    keep_ref, send_ref, out_ref = refs[count + 4 : count + 7]
+    scratch = refs[count + 7 :]
+    rest = samples_ref.shape[1] + halo_ref.shape[1] - scratch[1].shape[1] - LANES
     samples = jnp.concatenate([samples_ref[:, rest:], halo_ref[...]], axis=1)
     first = done_ref.shape[0]
     out_ref[:first] = done_ref[...]
@@ -214,8 +221,13 @@
         out_ref[...] = keep_ref[me ^ flip] + got_ref[me ^ flip]
 
 
-def power_kernel(stations, wave_ref, tpls_ref, order_ref, out_ref, head_ref, scale_ref):
-    extra = tpls_ref[:, tpls_ref.shape[1] - META :, :].astype(F32)
+def power_kernel(stations, wave_ref, order_ref, *refs):
+    tpls, (out_ref, head_ref, scale_ref, gathered) = refs[:-4], refs[-4:]
+    outer = lax.axis_index("outer")
+    for flip, pack in enumerate(tpls):
+        place = pl.ds((outer ^ flip) * INNER, INNER)
+        gathered[place] = pack[:, pack.shape[1] - META :, :].astype(F32)
+    extra = gathered[...]
     scale_ref[...] = extra[:, 0, :] + extra[:, 1, :] + extra[:, 2, :]
     tiles = -(-stations // LANES)
     flags = jnp.concatenate([extra[:, 3 + tile, :] for tile in range(tiles)], axis=1)
@@ -259,26 +271,27 @@
 
 def on_device(waveforms, templates, station_mask, channel_order):
     channels, slab = waveforms.shape
-    rows, _, window = templates.shape
+    group_rows, _, window = templates.shape
     stations = station_mask.shape[1]
     outer_count, tm_count = lax.axis_size("outer"), lax.axis_size("tm")
     blk_count = outer_count * INNER
-    assert rows == 1 and LANES % tm_count == 0
+    assert group_rows == 1 and LANES % tm_count == 0
     group = INNER * tm_count
     padded = INNER * LANES
     part = padded // group
     chunk = group * slab
     span = 2 * slab
     total = blk_count * tm_count
-    blk, every = ("outer", "inner"), ("outer", "inner", "tm")
+    every = ("outer", "inner", "tm")
     sds = jax.ShapeDtypeStruct
     order_row = channel_order[None, :]
 
-    payload, send, keep = call(
+    rows = window * part // LANES + META
+    *pieces, send, keep = call(
         functools.partial(prologue_kernel, tm_count),
         [HBM] * 4,
         [
-            sds((blk_count, window * part // LANES + META, LANES), BF16),
+            *[sds((rows, LANES), BF16)] * INNER,
             sds((padded // 2, slab), BF16),
             sds((padded // 2, slab), BF16),
         ],
@@ -294,7 +307,16 @@
         bytes_accessed=channels * (window + slab) * 2,
         vmem=60,
     )(templates, station_mask, order_row, waveforms)
-    tpls = lax.all_to_all(payload, blk, 0, 0, tiled=True)
+
+    plane = [pieces[0]] + [
+        lax.ppermute(pieces[flip], "inner", [(b, b ^ flip) for b in range(INNER)])
+        for flip in range(1, INNER)
+    ]
+    pack = call(pack_kernel, [VMEM] * INNER, sds((INNER, rows, LANES), BF16))(*plane)
+    tpls = [pack] + [
+        lax.ppermute(pack, "outer", [(b, b ^ flip) for b in range(outer_count)])
+        for flip in range(1, outer_count)
+    ]
 
     got = lax.ppermute(send, "inner", [(b, b ^ 1) for b in range(INNER)])
     half = group // 2
@@ -321,45 +343,45 @@
 
     power, power_head, scale = call(
         functools.partial(power_kernel, stations),
-        [VMEM] * 3,
+        [VMEM] * (outer_count + 2),
         [
             sds((blk_count, slab), F32),
             sds((blk_count, window), F32),
             sds((blk_count, LANES), F32),
         ],
+        [pltpu.VMEM((blk_count, META, LANES), F32)],
         flops=4 * blk_count * channels * slab,
         bytes_accessed=channels * slab * 2,
-    )(waveforms, tpls, order_row)
+    )(waveforms, order_row, *tpls)
     power_halo = lax.ppermute(power_head, every, [(i, i - 1) for i in range(1, total)])
 
-    copies = max(LANES // FINE, tm_count)
-    coarse = window // FINE
+    depth = window // FINE * part
 
     def scratch(columns):
         return [
-            pltpu.VMEM((coarse // copies, blk_count * FINE, copies * part), BF16),
-            pltpu.VMEM((copies * part, columns), BF16),
+            pltpu.VMEM((blk_count * FINE, depth), BF16),
+            pltpu.VMEM((depth, columns + LANES), BF16),
             pltpu.VMEM((span // LANES + 1, blk_count * FINE, LANES), F32),
         ]
 
     blocks = group // 2
     work = 2 * blk_count * window * part * span
     partials = call(
-        first_dots_kernel,
-        [VMEM] * 2,
+        functools.partial(first_dots_kernel, outer_count),
+        [VMEM] * (outer_count + 1),
         sds((2 * (blocks - 1), blk_count, slab), F32),
-        scratch((blocks - 1) * span + window),
+        scratch((blocks - 1) * span),
         flops=work * (blocks - 1),
         bytes_accessed=part * chunk * 2,
-    )(tpls, samples)
+    )(*tpls, samples)
     keep, send = call(
-        last_dots_kernel,
-        [VMEM] * 4 + [AFTER],
+        functools.partial(last_dots_kernel, outer_count),
+        [VMEM] * (outer_count + 3) + [AFTER],
         [sds((half, blk_count, slab), F32)] * 2,
-        [pltpu.VMEM((group, blk_count, slab), F32)] + scratch(span + window),
+        [pltpu.VMEM((group, blk_count, slab), F32)] + scratch(span),
         flops=work,
         bytes_accessed=part * chunk * 2,
-    )(tpls, samples, halo, partials, power_halo)
+    )(*tpls, samples, halo, partials, power_halo)
     got = lax.ppermute(send, "inner", [(b, b ^ 1) for b in range(INNER)])
     factor = call(
         factor_kernel,

time: 48.7 us -> 49.5 us (1.016)
  the two profiles are of different devices: /device:TPU:0 before, /device:TPU:16 now
where the time goes in v6:
time: 49.5 us; the launch traced here: 49.3 us
  starting transfers between devices  18.6 us (38%)
  waiting for transfers between devices  15.8 us (32%)
  Pallas kernels  13 us (26%)
  local copies, waits for them, and re-layouts  1.73 us (3%)
    ppermute x3, waiting for transfers between devices, on_device(): lax.ppermute(pack, 'outer', [(b, b ^ flip) for b in range(outer_count)])  8.38 us
    ppermute x6, starting transfers between devices, swap(): return lax.ppermute(part, every, route)  7.24 us
    pallas_call x1, Pallas kernels, on_device(): call(functools.partial(first_dots_kernel, outer_count), [VMEM] * (outer_c...  6.87 us
    ppermute x3, waiting for transfers between devices, on_device(): lax.ppermute(pieces[flip], 'inner', [(b, b ^ flip) for b in range(INNER)])  3.96 us
    ppermute x3, starting transfers between devices, on_device(): lax.ppermute(pack, 'outer', [(b, b ^ flip) for b in range(outer_count)])  3.55 us
    ppermute x6, waiting for transfers between devices, swap(): return lax.ppermute(part, every, route)  2.49 us
    pallas_call x1, Pallas kernels, on_device(): call(functools.partial(prologue_kernel, tm_count), [HBM] * 4, [*[sds((row...  2.26 us
    ppermute x1, starting transfers between devices, on_device(): lax.ppermute(head, 'outer', [(b, b - 1) for b in range(1, outer_count)])  2.18 us
  transfers between devices with their start and end apart: 16, of which 8 were waited for; matrix products, arithmetic and copies ran while one was open for 0% of the time, Pallas kernels for 16%

profile of v6, /device:TPU:16, one launch (start us, length us, event | category | flops | bytes accessed | tf_op | source)
XLA Modules:
  0.0 49.3 jit_solution(2664576897279556048)
XLA Ops:
  0.0 2.3 %shard_map.46 = (bf16[144,128]{1,0:T(8,128)(2,1)}, bf16[144,128]{1,0:T(8,128)(2,1)}, bf16[144,128]{1,0:T(8,128)(2,1)}, bf16[144,128]{1,0:T(8,128)(2,1)}, bf16[25...) custom-call(bf16[1,480,256]{2,1,0:T(8,128)(2,1)} %tpl_hbm.1, s32[1,160]{1,0:T(1,128)} %flag_hbm.1, s32[1,480]{1,0:T(1,128)} %bitcast.1, ...), custom_call_target="tpu_custom_call" | custom-call | bytes 737280 | tf_op jit(solution)/shard_map/pallas_call | solution.py:290
  2.9 1.5 %collective-permute-start.1 = (bf16[144,128]{1,0:T(8,128)(2,1)}, bf16[144,128]{1,0:T(8,128)(2,1)S(1)}, u32[]{:S(2)}, u32[]{:S(2)}) collective-permute-start(bf16[144,128]{1,0:T(8,128)(2,1)} %get-tuple-element.28), channel_id=1, source_target_pairs={{0,4},{2,6},{4,0},{6,2},{1,5},{3,7},{5,1},{7,3},{8,12},{10,14},{12... | collective-permute-start | bytes 110600 | tf_op jit(solution)/shard_map/ppermute | solution.py:312
  4.4 2.6 %collective-permute-done.1.refs_2_ = bf16[144,128]{1,0:T(8,128)(2,1)S(1)} collective-permute-done((bf16[144,128]{1,0:T(8,128)(2,1)}, bf16[144,128]{1,0:T(8,128)(2,1)S(1)}, u32[]{:S(2)}, u32[]{:S(2)}) %collective-permute-start.1) | collective-permute-done | bytes 36896 | tf_op jit(solution)/shard_map/ppermute | solution.py:312
  7.0 1.3 %collective-permute-done.2.refs_3_ = bf16[144,128]{1,0:T(8,128)(2,1)S(1)} collective-permute-done((bf16[144,128]{1,0:T(8,128)(2,1)}, bf16[144,128]{1,0:T(8,128)(2,1)S(1)}, u32[]{:S(2)}, u32[]{:S(2)}) %collective-permute-start.2) | collective-permute-done | bytes 36896 | tf_op jit(solution)/shard_map/ppermute | solution.py:312
  8.3 0.8 %copy-done.2 = bf16[144,128]{1,0:T(8,128)(2,1)S(1)} copy-done((bf16[144,128]{1,0:T(8,128)(2,1)S(1)}, bf16[144,128]{1,0:T(8,128)(2,1)}, u32[]{:S(2)}) %copy-start.2) | copy-done | bytes 36888
  9.1 1.6 %collective-permute-start.3 = (bf16[4,144,128]{2,1,0:T(8,128)(2,1)S(1)}, bf16[4,144,128]{2,1,0:T(8,128)(2,1)S(1)}, u32[]{:S(2)}, u32[]{:S(2)}) collective-permute-start(bf16[4,144,128]{2,1,0:T(8,128)(2,1)S(1)} %shard_map.47.refs_0_), channel_id=1, source_target_pairs={{0,8},{8,0},{16,24},{24,16},{1,9},{9,1},{17,25},{25,17},{2,10},{10... | collective-permute-start | bytes 442376 | tf_op jit(solution)/shard_map/ppermute | solution.py:317
  11.1 1.6 %collective-permute-start.5 = (bf16[4,144,128]{2,1,0:T(8,128)(2,1)S(1)}, bf16[4,144,128]{2,1,0:T(8,128)(2,1)S(1)}, u32[]{:S(2)}, u32[]{:S(2)}) collective-permute-start(bf16[4,144,128]{2,1,0:T(8,128)(2,1)S(1)} %shard_map.47.refs_0_), channel_id=1, source_target_pairs={{0,24},{8,16},{16,8},{24,0},{1,25},{9,17},{17,9},{25,1},{2,26},{10... | collective-permute-start | bytes 442376 | tf_op jit(solution)/shard_map/ppermute | solution.py:317
  12.7 0.9 %copy-done.1 = bf16[256,512]{1,0:T(8,128)(2,1)S(1)} copy-done((bf16[256,512]{1,0:T(8,128)(2,1)S(1)}, bf16[256,512]{1,0:T(8,128)(2,1)}, u32[]{:S(2)}) %copy-start.1) | copy-done | bytes 262168
  13.7 1.6 %collective-permute-start.7 = (bf16[2,64,512]{2,1,0:T(8,128)(2,1)S(1)}, bf16[2,64,512]{2,1,0:T(8,128)(2,1)S(1)}, u32[]{:S(2)}, u32[]{:S(2)}) collective-permute-start(bf16[2,64,512]{2,1,0:T(8,128)(2,1)S(1)} %get-tuple-element.33), channel_id=1, source_target_pairs={{0,1},{1,0},{2,3},{3,2},{4,5},{5,4},{6,7},{7,6},{8,9},{9,8},{10,11... | collective-permute-start | bytes 393224 | tf_op jit(solution)/shard_map/ppermute | solution.py:333
  16.1 1.6 %collective-permute-start.9 = (bf16[2,64,512]{2,1,0:T(8,128)(2,1)S(1)}, bf16[2,64,512]{2,1,0:T(8,128)(2,1)S(1)}, u32[]{:S(2)}, u32[]{:S(2)}) collective-permute-start(bf16[2,64,512]{2,1,0:T(8,128)(2,1)S(1)} %get-tuple-element.35), channel_id=1, source_target_pairs={{0,5},{1,4},{2,7},{3,6},{4,1},{5,0},{6,3},{7,2},{8,13},{9,12},{10,... | collective-permute-start | bytes 393224 | tf_op jit(solution)/shard_map/ppermute | solution.py:333
  17.6 4.1 %collective-permute-done.4.refs_2_ = bf16[4,144,128]{2,1,0:T(8,128)(2,1)S(1)} collective-permute-done((bf16[4,144,128]{2,1,0:T(8,128)(2,1)S(1)}, bf16[4,144,128]{2,1,0:T(8,128)(2,1)S(1)}, u32[]{:S(2)}, u32[]{:S(2)}) %collective-permute-start.4) | collective-permute-done | bytes 147488 | tf_op jit(solution)/shard_map/ppermute | solution.py:317
  21.7 4.1 %collective-permute-done.5.refs_3_ = bf16[4,144,128]{2,1,0:T(8,128)(2,1)S(1)} collective-permute-done((bf16[4,144,128]{2,1,0:T(8,128)(2,1)S(1)}, bf16[4,144,128]{2,1,0:T(8,128)(2,1)S(1)}, u32[]{:S(2)}, u32[]{:S(2)}) %collective-permute-start.5) | collective-permute-done | bytes 147488 | tf_op jit(solution)/shard_map/ppermute | solution.py:317
  26.2 2.1 %collective-permute-start.11 = (f32[16,256]{1,0:T(8,128)S(1)}, f32[16,256]{1,0:T(8,128)S(1)}, u32[]{:S(2)}, u32[]{:S(2)}) collective-permute-start(f32[16,256]{1,0:T(8,128)S(1)} %get-tuple-element.38), channel_id=1, source_target_pairs={{1,0},{2,1},{3,2},{4,3},{5,4},{6,5},{7,6},{8,7},{9,8},{10,9},{11,1... | collective-permute-start | bytes 49160 | tf_op jit(solution)/shard_map/ppermute | solution.py:356
  28.4 2.2 %collective-permute-start.10 = (bf16[64,256]{1,0:T(8,128)(2,1)S(1)}, bf16[64,256]{1,0:T(8,128)(2,1)S(1)}, u32[]{:S(2)}, u32[]{:S(2)}) collective-permute-start(bf16[64,256]{1,0:T(8,128)(2,1)S(1)} %get-tuple-element.37), channel_id=1, source_target_pairs={{8,0},{16,8},{24,16},{9,1},{17,9},{25,17},{10,2},{18,10},{26,18},{... | collective-permute-start | bytes 98312 | tf_op jit(solution)/shard_map/ppermute | solution.py:342
  30.6 6.9 %shard_map.50.refs_6_ = f32[6,16,512]{2,1,0:T(8,128)S(1)} custom-call(bf16[4,144,128]{2,1,0:T(8,128)(2,1)S(1)} %shard_map.47.refs_0_, bf16[4,144,128]{2,1,0:T(8,128)(2,1)S(1)} %collective-permute-done.3.refs_1_, bf16[4,144,128]{2,1,0:T(8,128)(2,1)S(1)} %collective-permute-done.4.refs_2_, bf16[4,144,128]{2,1,0:T(8,128)(2,1)S(1)} %collective-permute-done.5.refs_3_, ...), custom_call_target="tpu_custom_call" | custom-call | flops 1610612736 | bytes 524288 | tf_op jit(solution)/shard_map/pallas_call | solution.py:369
  37.5 2.1 %shard_map.52 = (f32[4,16,512]{2,1,0:T(8,128)S(1)}, f32[4,16,512]{2,1,0:T(8,128)S(1)}) custom-call(bf16[4,144,128]{2,1,0:T(8,128)(2,1)S(1)} %shard_map.47.refs_0_, bf16[4,144,128]{2,1,0:T(8,128)(2,1)S(1)} %collective-permute-done.3.refs_1_, bf16[4,144,128]{2,1,0:T(8,128)(2,1)S(1)} %collective-permute-done.4.refs_2_, ...), custom_call_target="tpu_custom_call" | custom-call | flops 536870912 | bytes 524288 | tf_op jit(solution)/shard_map/pallas_call | solution.py:377
  39.6 1.4 %collective-permute-start.12 = (f32[4,16,512]{2,1,0:T(8,128)S(1)}, f32[4,16,512]{2,1,0:T(8,128)S(1)}, u32[]{:S(2)}, u32[]{:S(2)}) collective-permute-start(f32[4,16,512]{2,1,0:T(8,128)S(1)} %get-tuple-element.40.after), channel_id=1, source_target_pairs={{0,2},{2,0},{4,6},{6,4},{1,3},{3,1},{5,7},{7,5},{8,10},{10,8},{12,... | collective-permute-start | bytes 393224 | tf_op jit(solution)/shard_map/ppermute | solution.py:385
  41.0 1.0 %collective-permute-done.12.got_ref = f32[4,16,512]{2,1,0:T(8,128)S(1)} collective-permute-done((f32[4,16,512]{2,1,0:T(8,128)S(1)}, f32[4,16,512]{2,1,0:T(8,128)S(1)}, u32[]{:S(2)}, u32[]{:S(2)}) %collective-permute-start.12) | collective-permute-done | bytes 131104 | tf_op jit(solution)/shard_map/ppermute | solution.py:385
  42.1 1.1 %collective-permute-start.13 = (f32[16,512]{1,0:T(8,128)S(1)}, f32[16,512]{1,0:T(8,128)S(1)}, u32[]{:S(2)}, u32[]{:S(2)}) collective-permute-start(f32[16,512]{1,0:T(8,128)S(1)} %get-tuple-element.42), channel_id=1, source_target_pairs={{0,1},{1,0},{2,3},{3,2},{4,5},{5,4},{6,7},{7,6},{8,9},{9,8},{10,11... | collective-permute-start | bytes 98312 | tf_op jit(solution)/shard_map/ppermute | solution.py:333
  43.2 0.7 %collective-permute-start.14 = (f32[16,512]{1,0:T(8,128)S(1)}, f32[16,512]{1,0:T(8,128)S(1)}, u32[]{:S(2)}, u32[]{:S(2)}) collective-permute-start(f32[16,512]{1,0:T(8,128)S(1)} %get-tuple-element.43), channel_id=1, source_target_pairs={{0,4},{1,5},{2,6},{3,7},{4,0},{5,1},{6,2},{7,3},{8,12},{9,13},{10,... | collective-permute-start | bytes 98312 | tf_op jit(solution)/shard_map/ppermute | solution.py:333
  43.8 1.8 %collective-permute-start.15 = (f32[16,512]{1,0:T(8,128)S(1)}, f32[16,512]{1,0:T(8,128)S(1)}, u32[]{:S(2)}, u32[]{:S(2)}) collective-permute-start(f32[16,512]{1,0:T(8,128)S(1)} %get-tuple-element.44), channel_id=1, source_target_pairs={{0,5},{1,4},{2,7},{3,6},{4,1},{5,0},{6,3},{7,2},{8,13},{9,12},{10,... | collective-permute-start | bytes 98312 | tf_op jit(solution)/shard_map/ppermute | solution.py:333
  46.2 1.3 %collective-permute-done.14.refs_2_ = f32[16,512]{1,0:T(8,128)S(1)} collective-permute-done((f32[16,512]{1,0:T(8,128)S(1)}, f32[16,512]{1,0:T(8,128)S(1)}, u32[]{:S(2)}, u32[]{:S(2)}) %collective-permute-start.14) | collective-permute-done | bytes 32800 | tf_op jit(solution)/shard_map/ppermute | solution.py:333
  47.4 1.2 %collective-permute-done.15.refs_3_ = f32[16,512]{1,0:T(8,128)S(1)} collective-permute-done((f32[16,512]{1,0:T(8,128)S(1)}, f32[16,512]{1,0:T(8,128)S(1)}, u32[]{:S(2)}, u32[]{:S(2)}) %collective-permute-start.15) | collective-permute-done | bytes 32800 | tf_op jit(solution)/shard_map/ppermute | solution.py:333
  48.6 0.6 %shard_map.55 = f32[16,512]{1,0:T(8,128)} custom-call(f32[16,512]{1,0:T(8,128)S(1)} %get-tuple-element.41.refs_0_, f32[16,512]{1,0:T(8,128)S(1)} %collective-permute-done.13.refs_1_, f32[16,512]{1,0:T(8,128)S(1)} %collective-permute-done.14.refs_2_, f32[16,512]{1,0:T(8,128)S(1)} %collective-permute-done.15.refs_3_, f32[16,512]{1,0:T(8,128)S(1)} %shard_map.54.refs_4_), custom_call_target="tpu_custom_call" | custom-call | bytes 196608 | tf_op jit(solution)/shard_map/pallas_call | solution.py:400
  (26 shorter events, 2.8 us)
Async XLA Ops:
  2.3 23.5 %copy-start = (bf16[480,512]{1,0:T(8,128)(2,1)S(1)}, bf16[480,512]{1,0:T(8,128)(2,1)}, u32[]{:S(2)}) copy-start(bf16[480,512]{1,0:T(8,128)(2,1)} %wave_ref.1) | copy-start | bytes 1474564
  2.3 10.4 %collective-permute-start.6 = (bf16[256,512]{1,0:T(8,128)(2,1)}, bf16[256,512]{1,0:T(8,128)(2,1)S(1)}, u32[]{:S(2)}, u32[]{:S(2)}) collective-permute-start(bf16[256,512]{1,0:T(8,128)(2,1)} %get-tuple-element.31), channel_id=1, source_target_pairs={{0,2},{2,0},{4,6},{6,4},{1,3},{3,1},{5,7},{7,5},{8,10},{10,8},{12,... | collective-permute-start | bytes 786440 | tf_op jit(solution)/shard_map/ppermute | solution.py:321
  2.4 2.0 %collective-permute-start = (bf16[144,128]{1,0:T(8,128)(2,1)}, bf16[144,128]{1,0:T(8,128)(2,1)S(1)}, u32[]{:S(2)}, u32[]{:S(2)}) collective-permute-start(bf16[144,128]{1,0:T(8,128)(2,1)} %get-tuple-element.27), channel_id=1, source_target_pairs={{0,2},{2,0},{4,6},{6,4},{1,3},{3,1},{5,7},{7,5},{8,10},{10,8},{12,... | collective-permute-start | bytes 110600 | tf_op jit(solution)/shard_map/ppermute | solution.py:312
  2.9 4.2 %collective-permute-start.1 = (bf16[144,128]{1,0:T(8,128)(2,1)}, bf16[144,128]{1,0:T(8,128)(2,1)S(1)}, u32[]{:S(2)}, u32[]{:S(2)}) collective-permute-start(bf16[144,128]{1,0:T(8,128)(2,1)} %get-tuple-element.28), channel_id=1, source_target_pairs={{0,4},{2,6},{4,0},{6,2},{1,5},{3,7},{5,1},{7,3},{8,12},{10,14},{12... | collective-permute-start | bytes 110600 | tf_op jit(solution)/shard_map/ppermute | solution.py:312
  4.4 4.0 %collective-permute-start.2 = (bf16[144,128]{1,0:T(8,128)(2,1)}, bf16[144,128]{1,0:T(8,128)(2,1)S(1)}, u32[]{:S(2)}, u32[]{:S(2)}) collective-permute-start(bf16[144,128]{1,0:T(8,128)(2,1)} %get-tuple-element.29), channel_id=1, source_target_pairs={{0,6},{2,4},{4,2},{6,0},{1,7},{3,5},{5,3},{7,1},{8,14},{10,12},{12... | collective-permute-start | bytes 110600 | tf_op jit(solution)/shard_map/ppermute | solution.py:312
  8.3 0.8 %copy-start.2 = (bf16[144,128]{1,0:T(8,128)(2,1)S(1)}, bf16[144,128]{1,0:T(8,128)(2,1)}, u32[]{:S(2)}) copy-start(bf16[144,128]{1,0:T(8,128)(2,1)} %get-tuple-element.26.refs_0_) | copy-start | bytes 110596
  9.1 6.9 %collective-permute-start.3 = (bf16[4,144,128]{2,1,0:T(8,128)(2,1)S(1)}, bf16[4,144,128]{2,1,0:T(8,128)(2,1)S(1)}, u32[]{:S(2)}, u32[]{:S(2)}) collective-permute-start(bf16[4,144,128]{2,1,0:T(8,128)(2,1)S(1)} %shard_map.47.refs_0_), channel_id=1, source_target_pairs={{0,8},{8,0},{16,24},{24,16},{1,9},{9,1},{17,25},{25,17},{2,10},{10... | collective-permute-start | bytes 442376 | tf_op jit(solution)/shard_map/ppermute | solution.py:317
  10.8 10.9 %collective-permute-start.4 = (bf16[4,144,128]{2,1,0:T(8,128)(2,1)S(1)}, bf16[4,144,128]{2,1,0:T(8,128)(2,1)S(1)}, u32[]{:S(2)}, u32[]{:S(2)}) collective-permute-start(bf16[4,144,128]{2,1,0:T(8,128)(2,1)S(1)} %shard_map.47.refs_0_), channel_id=1, source_target_pairs={{0,16},{8,24},{16,0},{24,8},{1,17},{9,25},{17,1},{25,9},{2,18},{10... | collective-permute-start | bytes 442376 | tf_op jit(solution)/shard_map/ppermute | solution.py:317
  11.1 14.6 %collective-permute-start.5 = (bf16[4,144,128]{2,1,0:T(8,128)(2,1)S(1)}, bf16[4,144,128]{2,1,0:T(8,128)(2,1)S(1)}, u32[]{:S(2)}, u32[]{:S(2)}) collective-permute-start(bf16[4,144,128]{2,1,0:T(8,128)(2,1)S(1)} %shard_map.47.refs_0_), channel_id=1, source_target_pairs={{0,24},{8,16},{16,8},{24,0},{1,25},{9,17},{17,9},{25,1},{2,26},{10... | collective-permute-start | bytes 442376 | tf_op jit(solution)/shard_map/ppermute | solution.py:317
  12.7 1.0 %copy-start.1 = (bf16[256,512]{1,0:T(8,128)(2,1)S(1)}, bf16[256,512]{1,0:T(8,128)(2,1)}, u32[]{:S(2)}) copy-start(bf16[256,512]{1,0:T(8,128)(2,1)} %get-tuple-element.30.keep_ref) | copy-start | bytes 786436
  13.7 12.1 %copy-start.3 = (s32[480]{0:T(512)S(1)}, s32[480]{0:T(512)}, u32[]{:S(2)}) copy-start(s32[480]{0:T(512)} %param.7) | copy-start | bytes 5764
  13.7 14.6 %collective-permute-start.7 = (bf16[2,64,512]{2,1,0:T(8,128)(2,1)S(1)}, bf16[2,64,512]{2,1,0:T(8,128)(2,1)S(1)}, u32[]{:S(2)}, u32[]{:S(2)}) collective-permute-start(bf16[2,64,512]{2,1,0:T(8,128)(2,1)S(1)} %get-tuple-element.33), channel_id=1, source_target_pairs={{0,1},{1,0},{2,3},{3,2},{4,5},{5,4},{6,7},{7,6},{8,9},{9,8},{10,11... | collective-permute-start | bytes 393224 | tf_op jit(solution)/shard_map/ppermute | solution.py:333
  15.2 13.1 %collective-permute-start.8 = (bf16[2,64,512]{2,1,0:T(8,128)(2,1)S(1)}, bf16[2,64,512]{2,1,0:T(8,128)(2,1)S(1)}, u32[]{:S(2)}, u32[]{:S(2)}) collective-permute-start(bf16[2,64,512]{2,1,0:T(8,128)(2,1)S(1)} %get-tuple-element.34), channel_id=1, source_target_pairs={{0,4},{1,5},{2,6},{3,7},{4,0},{5,1},{6,2},{7,3},{8,12},{9,13},{10,... | collective-permute-start | bytes 393224 | tf_op jit(solution)/shard_map/ppermute | solution.py:333
  16.1 12.3 %collective-permute-start.9 = (bf16[2,64,512]{2,1,0:T(8,128)(2,1)S(1)}, bf16[2,64,512]{2,1,0:T(8,128)(2,1)S(1)}, u32[]{:S(2)}, u32[]{:S(2)}) collective-permute-start(bf16[2,64,512]{2,1,0:T(8,128)(2,1)S(1)} %get-tuple-element.35), channel_id=1, source_target_pairs={{0,5},{1,4},{2,7},{3,6},{4,1},{5,0},{6,3},{7,2},{8,13},{9,12},{10,... | collective-permute-start | bytes 393224 | tf_op jit(solution)/shard_map/ppermute | solution.py:333
  26.2 11.3 %collective-permute-start.11 = (f32[16,256]{1,0:T(8,128)S(1)}, f32[16,256]{1,0:T(8,128)S(1)}, u32[]{:S(2)}, u32[]{:S(2)}) collective-permute-start(f32[16,256]{1,0:T(8,128)S(1)} %get-tuple-element.38), channel_id=1, source_target_pairs={{1,0},{2,1},{3,2},{4,3},{5,4},{6,5},{7,6},{8,7},{9,8},{10,9},{11,1... | collective-permute-start | bytes 49160 | tf_op jit(solution)/shard_map/ppermute | solution.py:356
  28.4 9.1 %collective-permute-start.10 = (bf16[64,256]{1,0:T(8,128)(2,1)S(1)}, bf16[64,256]{1,0:T(8,128)(2,1)S(1)}, u32[]{:S(2)}, u32[]{:S(2)}) collective-permute-start(bf16[64,256]{1,0:T(8,128)(2,1)S(1)} %get-tuple-element.37), channel_id=1, source_target_pairs={{8,0},{16,8},{24,16},{9,1},{17,9},{25,17},{10,2},{18,10},{26,18},{... | collective-permute-start | bytes 98312 | tf_op jit(solution)/shard_map/ppermute | solution.py:342
  39.6 2.4 %collective-permute-start.12 = (f32[4,16,512]{2,1,0:T(8,128)S(1)}, f32[4,16,512]{2,1,0:T(8,128)S(1)}, u32[]{:S(2)}, u32[]{:S(2)}) collective-permute-start(f32[4,16,512]{2,1,0:T(8,128)S(1)} %get-tuple-element.40.after), channel_id=1, source_target_pairs={{0,2},{2,0},{4,6},{6,4},{1,3},{3,1},{5,7},{7,5},{8,10},{10,8},{12,... | collective-permute-start | bytes 393224 | tf_op jit(solution)/shard_map/ppermute | solution.py:385
  42.1 4.1 %collective-permute-start.13 = (f32[16,512]{1,0:T(8,128)S(1)}, f32[16,512]{1,0:T(8,128)S(1)}, u32[]{:S(2)}, u32[]{:S(2)}) collective-permute-start(f32[16,512]{1,0:T(8,128)S(1)} %get-tuple-element.42), channel_id=1, source_target_pairs={{0,1},{1,0},{2,3},{3,2},{4,5},{5,4},{6,7},{7,6},{8,9},{9,8},{10,11... | collective-permute-start | bytes 98312 | tf_op jit(solution)/shard_map/ppermute | solution.py:333
  43.2 4.3 %collective-permute-start.14 = (f32[16,512]{1,0:T(8,128)S(1)}, f32[16,512]{1,0:T(8,128)S(1)}, u32[]{:S(2)}, u32[]{:S(2)}) collective-permute-start(f32[16,512]{1,0:T(8,128)S(1)} %get-tuple-element.43), channel_id=1, source_target_pairs={{0,4},{1,5},{2,6},{3,7},{4,0},{5,1},{6,2},{7,3},{8,12},{9,13},{10,... | collective-permute-start | bytes 98312 | tf_op jit(solution)/shard_map/ppermute | solution.py:333
  43.8 4.8 %collective-permute-start.15 = (f32[16,512]{1,0:T(8,128)S(1)}, f32[16,512]{1,0:T(8,128)S(1)}, u32[]{:S(2)}, u32[]{:S(2)}) collective-permute-start(f32[16,512]{1,0:T(8,128)S(1)} %get-tuple-element.44), channel_id=1, source_target_pairs={{0,5},{1,4},{2,7},{3,6},{4,1},{5,0},{6,3},{7,2},{8,13},{9,12},{10,... | collective-permute-start | bytes 98312 | tf_op jit(solution)/shard_map/ppermute | solution.py:333

commit v7 on v5

--- a/solution.py
+++ b/solution.py
@@ -20,7 +20,6 @@
 
 HBM = pl.BlockSpec(memory_space=pltpu.HBM)
 VMEM = pl.BlockSpec(memory_space=pltpu.VMEM)
-AFTER = pl.BlockSpec(memory_space=pl.ANY)
 
 
 def call(kernel, in_specs, out_shape, scratch=(), flops=0, bytes_accessed=0, vmem=24):
@@ -45,7 +44,7 @@
 
 
 def side_major(inner):
-    return (inner % 2) * (INNER // 2) + inner // 2
+    return lax.rem(inner, 2) * (INNER // 2) + lax.div(inner, 2)
 
 
 def prologue_kernel(tm_count, tpl_hbm, flag_hbm, order_hbm, wave_hbm, *refs):
@@ -93,7 +92,7 @@
     my_tm = lax.axis_index("tm")
     spot = lax.broadcasted_iota(jnp.int32, (FINE, LANES), 1) // part
     for member in range(INNER):
-        start = side_major(member) * LANES
+        start = (member % 2 * (INNER // 2) + member // 2) * LANES
         pieces = []
         for step in range(window // (FINE * tm_count)):
             tile = jnp.zeros((FINE, LANES), F32)
@@ -138,74 +137,88 @@
 
 
 def correlate(tpls, samples, out_ref, first, left, shifts, products):
-    count = tpls.shape[0]
     slab = out_ref.shape[2]
     part, columns = samples.shape
-    copies = shifts.shape[0] // part
-    for copy in range(copies):
-        turned = samples if copy == 0 else pltpu.roll(samples, columns - FINE * copy, 1)
-        shifts[copy * part : (copy + 1) * part, :] = turned
-    parts, _, depth = left.shape
-    steps = depth // LANES
-    for template in range(count):
-        row = template * FINE
-        for step in range(parts * steps):
-            lane = (step % steps) * LANES
-            left[step // steps, row : row + FINE, lane : lane + LANES] = tpls[
-                template, FINE * step : FINE * (step + 1), :
-            ]
-    tiles = products.shape[0]
+    size, depth = left.shape
+    copies = LANES // FINE
+    usable = columns - 2 * LANES
+    for copy in range(depth // part):
+        tile, turn = copy // copies * LANES, copy % copies * FINE
+        turned = samples if turn == 0 else pltpu.roll(samples, columns - turn, 1)
+        shifts[copy * part : (copy + 1) * part, :] = turned[:, tile : tile + usable + LANES]
+    count = tpls.shape[0]
+    row = lax.broadcasted_iota(jnp.int32, (size, size), 0)
+    column = lax.broadcasted_iota(jnp.int32, (size, size), 1)
+    source = lax.rem(row, count) * FINE + lax.div(row, count)
+    order = jnp.where(column == source, 1.0, 0.0).astype(BF16)
+    for step in range(depth // LANES):
+        rows = tpls[:, FINE * step : FINE * (step + 1), :].reshape(size, LANES)
+        left[:, step * LANES : (step + 1) * LANES] = jnp.dot(
+            order, rows, preferred_element_type=F32
+        ).astype(BF16)
+    tiles = products.shape[1] // LANES
     span = (tiles - 1) * LANES
     per_block = span // slab
 
     def block(index, carry):
         start = pl.multiple_of(index * span, span)
-        product = None
-        for piece in range(parts):
-            here = pl.ds(pl.multiple_of(start + piece * copies * FINE, LANES), span + LANES)
-            term = jnp.dot(left[piece], shifts[:, here], preferred_element_type=F32)
-            product = term if product is None else product + term
-        for tile in range(tiles):
-            products[tile] = product[:, tile * LANES : (tile + 1) * LANES]
-
-        def fine_rows(fine):
-            return jnp.concatenate(
-                [products[tile, pl.ds(fine, count, stride=FINE), :] for tile in range(tiles)],
-                axis=1,
+        for tile in range(0, tiles, 2):
+            width = min(2, tiles - tile) * LANES
+            here = pl.ds(pl.multiple_of(start + tile * LANES, LANES), width)
+            products[:, tile * LANES : tile * LANES + width] = jnp.dot(
+                left[...], shifts[:, here], preferred_element_type=F32
             )
-
-        total = fine_rows(FINE - 1)
+        total = products[(FINE - 1) * count :, :]
         for fine in reversed(range(FINE - 1)):
-            total = fine_rows(fine) + pltpu.roll(total, span + LANES - 1, 1)
+            total = products[fine * count : (fine + 1) * count, :] + pltpu.roll(
+                total, span + LANES - 1, 1
+            )
         for piece in range(per_block):
             out_ref[first + index * per_block + piece] = total[:, piece * slab : (piece + 1) * slab]
         return carry
 
-    blocks = (columns - 2 * LANES) // span
-    lax.fori_loop(0, blocks, block, 0)
+    lax.fori_loop(0, usable // span, block, 0)
 
 
 def first_dots_kernel(tpls, samples_ref, out_ref, left, shifts, products):
-    columns = shifts.shape[1]
+    columns = shifts.shape[1] + LANES
     correlate(tpls, samples_ref[:, :columns], out_ref, 0, left, shifts, products)
 
 
-def last_dots_kernel(tpls, samples_ref, halo_ref, done_ref, after, *refs):
-    del after
+def last_dots_kernel(tpls, samples_ref, halo_ref, mask_ref, done_ref, *refs):
     keep_ref, send_ref, out_ref = refs[:3]
     scratch = refs[3:]
-    rest = samples_ref.shape[1] + halo_ref.shape[1] - scratch[1].shape[1]
+    first, slab = done_ref.shape[0], done_ref.shape[2]
+    half = keep_ref.shape[0]
+    run = half // 2
+    core = lax.rem(lax.axis_index("inner"), 2)
+
+    def powers(member, out):
+        start = (member + 1) * slab
+        if start < samples_ref.shape[1]:
+            wave = samples_ref[:, start : start + halo_ref.shape[1]]
+        else:
+            wave = halo_ref[...]
+        out[...] = masked_squares(mask_ref[...], wave)
+
+    for y in range(2):
+        for side in range(2):
+            for tm in range(run):
+                member = (2 * y + side) * run + tm
+                for owner, out in ((core, keep_ref), (1 - core, send_ref)):
+
+                    @pl.when(owner == side)
+                    def _():
+                        powers(member, out.at[y * run + tm, :, pl.ds(slab, halo_ref.shape[1])])
+
+    rest = samples_ref.shape[1] + halo_ref.shape[1] - scratch[1].shape[1] - LANES
     samples = jnp.concatenate([samples_ref[:, rest:], halo_ref[...]], axis=1)
-    first = done_ref.shape[0]
     out_ref[:first] = done_ref[...]
     correlate(tpls, samples, out_ref, first, *scratch)
-    core = lax.rem(lax.axis_index("inner"), 2)
-    half = keep_ref.shape[0]
-    run = half // 2
     for y in range(2):
         for tm in range(run):
-            keep_ref[y * run + tm] = out_ref[(2 * y + core) * run + tm]
-            send_ref[y * run + tm] = out_ref[(2 * y + 1 - core) * run + tm]
+            keep_ref[y * run + tm, :, :slab] = out_ref[(2 * y + core) * run + tm]
+            send_ref[y * run + tm, :, :slab] = out_ref[(2 * y + 1 - core) * run + tm]
 
 
 def add_kernel(tm_count, keep_ref, got_ref, *outs):
@@ -214,47 +227,52 @@
         out_ref[...] = keep_ref[me ^ flip] + got_ref[me ^ flip]
 
 
-def power_kernel(stations, wave_ref, tpls_ref, order_ref, out_ref, head_ref, scale_ref):
+def masked_squares(mask, wave):
+    wave = wave.astype(F32)
+    squares = wave * wave
+    high = squares.astype(BF16)
+    low = (squares - high.astype(F32)).astype(BF16)
+    return jnp.dot(mask, high, preferred_element_type=F32) + jnp.dot(
+        mask, low, preferred_element_type=F32
+    )
+
+
+def power_kernel(stations, tm_count, wave_ref, tpls_ref, order_ref, *refs):
+    out_ref, scale_ref, mask_ref, order_pad = refs
     extra = tpls_ref[:, tpls_ref.shape[1] - META :, :].astype(F32)
     scale_ref[...] = extra[:, 0, :] + extra[:, 1, :] + extra[:, 2, :]
     tiles = -(-stations // LANES)
     flags = jnp.concatenate([extra[:, 3 + tile, :] for tile in range(tiles)], axis=1)
+    channels = wave_ref.shape[0]
+    padded = order_pad.shape[1]
+    order_pad[...] = jnp.full((1, padded), -1, jnp.int32)
+    order_pad[:, :channels] = order_ref[...]
     mask = jnp.dot(
         flags.astype(BF16),
-        one_hot(order_ref[...], tiles * LANES),
+        one_hot(order_pad[...], tiles * LANES),
         preferred_element_type=F32,
-    ).astype(BF16)
-    wave = wave_ref[...].astype(F32)
-    squares = wave * wave
-    high = squares.astype(BF16)
-    low = (squares - high.astype(F32)).astype(BF16)
-    power = jnp.dot(mask, high, preferred_element_type=F32) + jnp.dot(
-        mask, low, preferred_element_type=F32
-    )
-    out_ref[...] = power
-    head_ref[...] = power[:, : head_ref.shape[1]]
-
-
-def factor_kernel(power_ref, halo_ref, scale_ref, after, out_ref, joined):
-    del after
-    slab, window = power_ref.shape[1], halo_ref.shape[1]
+    )
+    out_ref[...] = masked_squares(mask[:, :channels].astype(BF16), wave_ref[...])
+    part = LANES // tm_count
+    mine = side_major(lax.axis_index("inner")) * LANES + lax.axis_index("tm") * part
+    mask_ref[...] = pltpu.roll(mask, lax.rem(padded - mine, padded), 1)[:, :part].astype(BF16)
+
+
+def finish_kernel(*refs):
+    parts, (power_ref, scale_ref, out_ref, joined) = refs[:-4], refs[-4:]
+    slab = power_ref.shape[1]
+    total = parts[0][...]
+    for part in parts[1:]:
+        total = total + part[...]
     joined[:, :slab] = power_ref[...]
-    joined[:, slab:] = halo_ref[...]
+    joined[:, slab:] = total[:, slab:]
     running = joined[...]
     columns = running.shape[1]
     width = 1
-    while width < window:
+    while width < columns - slab:
         running = running + pltpu.roll(running, columns - width, 1)
         width *= 2
-    out_ref[...] = scale_ref[:, :1] / jnp.sqrt(running[:, :slab] + EPSILON)
-
-
-def finish_kernel(*refs):
-    parts, factor_ref, out_ref = refs[:-2], refs[-2], refs[-1]
-    total = parts[0][...]
-    for part in parts[1:]:
-        total = total + part[...]
-    out_ref[...] = total * factor_ref[...]
+    out_ref[...] = total[:, :slab] * (scale_ref[:, :1] / jnp.sqrt(running[:, :slab] + EPSILON))
 
 
 def on_device(waveforms, templates, station_mask, channel_order):
@@ -319,27 +337,26 @@
     )(*waves)
     halo = lax.ppermute(head, "outer", [(b, b - 1) for b in range(1, outer_count)])
 
-    power, power_head, scale = call(
-        functools.partial(power_kernel, stations),
+    power, scale, mask = call(
+        functools.partial(power_kernel, stations, tm_count),
         [VMEM] * 3,
         [
             sds((blk_count, slab), F32),
-            sds((blk_count, window), F32),
             sds((blk_count, LANES), F32),
+            sds((blk_count, part), BF16),
         ],
+        [pltpu.VMEM((1, padded), jnp.int32)],
         flops=4 * blk_count * channels * slab,
         bytes_accessed=channels * slab * 2,
     )(waveforms, tpls, order_row)
-    power_halo = lax.ppermute(power_head, every, [(i, i - 1) for i in range(1, total)])
-
-    copies = max(LANES // FINE, tm_count)
-    coarse = window // FINE
+
+    depth = window // FINE * part
 
     def scratch(columns):
         return [
-            pltpu.VMEM((coarse // copies, blk_count * FINE, copies * part), BF16),
-            pltpu.VMEM((copies * part, columns), BF16),
-            pltpu.VMEM((span // LANES + 1, blk_count * FINE, LANES), F32),
+            pltpu.VMEM((blk_count * FINE, depth), BF16),
+            pltpu.VMEM((depth, columns + LANES), BF16),
+            pltpu.VMEM((blk_count * FINE, span + LANES), F32),
         ]
 
     blocks = group // 2
@@ -348,39 +365,33 @@
         first_dots_kernel,
         [VMEM] * 2,
         sds((2 * (blocks - 1), blk_count, slab), F32),
-        scratch((blocks - 1) * span + window),
+        scratch((blocks - 1) * span),
         flops=work * (blocks - 1),
         bytes_accessed=part * chunk * 2,
     )(tpls, samples)
     keep, send = call(
         last_dots_kernel,
-        [VMEM] * 4 + [AFTER],
-        [sds((half, blk_count, slab), F32)] * 2,
-        [pltpu.VMEM((group, blk_count, slab), F32)] + scratch(span + window),
+        [VMEM] * 5,
+        [sds((half, blk_count, slab + window), F32)] * 2,
+        [pltpu.VMEM((group, blk_count, slab), F32)] + scratch(span),
         flops=work,
         bytes_accessed=part * chunk * 2,
-    )(tpls, samples, halo, partials, power_halo)
+    )(tpls, samples, halo, mask, partials)
     got = lax.ppermute(send, "inner", [(b, b ^ 1) for b in range(INNER)])
-    factor = call(
-        factor_kernel,
-        [VMEM] * 3 + [AFTER],
-        sds((blk_count, slab), F32),
-        [pltpu.VMEM((blk_count, slab + window), F32)],
-        bytes_accessed=blk_count * slab * 8,
-    )(power, power_halo, scale, send)
     sums = call(
         functools.partial(add_kernel, tm_count),
         [VMEM] * 2,
-        [sds((blk_count, slab), F32)] * half,
+        [sds((blk_count, slab + window), F32)] * half,
         bytes_accessed=blk_count * slab * 12 * half,
     )(keep, got)
     sums = [sums[0]] + [swap(sums[flip], flip) for flip in range(1, half)]
     return call(
         finish_kernel,
-        [VMEM] * (half + 1),
+        [VMEM] * (half + 2),
         sds((blk_count, slab), F32),
+        [pltpu.VMEM((blk_count, slab + window), F32)],
         bytes_accessed=blk_count * slab * 4 * (half + 2),
-    )(*sums, factor)
+    )(*sums, power, scale)
 
 
 def solution(mesh):

time: 48.7 us -> 47.1 us (0.967)
  starting transfers between devices: 20 us -> 17.1 us
  Pallas kernels: 13.1 us -> 14.2 us
    ppermute x2, starting transfers between devices: 2.75 us -> 0.56 us  [on_device(): got = lax.ppermute(send, 'inner', [(b, b ^ 1) for b in range(INNER)])]
    ppermute x1 -> x0, starting transfers between devices: 1.29 us -> none  [on_device(): lax.ppermute(power_head, every, [(i, i - 1) for i in range(1, total)])]
    pallas_call x4 -> x3, Pallas kernels: 3.82 us -> 4.93 us  [the longest x1 3.35 us: on_device(): call(last_dots_kernel, [VMEM] * 5, [sds((half, blk_count, slab + window),...]
    ppermute x6, starting transfers between devices: 7.13 us -> 7.72 us  [swap(): return lax.ppermute(part, every, route)]
  transfers between devices with their start and end apart: 11 -> 10, of which waited for: 6 -> 6; matrix products, arithmetic and copies ran while one was open for 0% -> 0% of each run, Pallas kernels for 16% -> 15%
where the time goes in v7:
time: 47.1 us; the launch traced here: 46.8 us
  starting transfers between devices  17.1 us (36%)
  waiting for transfers between devices  15.5 us (33%)
  Pallas kernels  14.2 us (30%)
    ppermute x6, waiting for transfers between devices, swap(): return lax.ppermute(part, every, route)  12.8 us
    ppermute x6, starting transfers between devices, swap(): return lax.ppermute(part, every, route)  7.72 us
    all_to_all x1, starting transfers between devices, on_device(): tpls = lax.all_to_all(payload, blk, 0, 0, tiled=True)  7.53 us
    pallas_call x1, Pallas kernels, on_device(): call(first_dots_kernel, [VMEM] * 2, sds((2 * (blocks - 1), blk_count, sla...  6.72 us
    pallas_call x1, Pallas kernels, on_device(): call(last_dots_kernel, [VMEM] * 5, [sds((half, blk_count, slab + window),...  3.35 us
    ppermute x2, waiting for transfers between devices, on_device(): got = lax.ppermute(send, 'inner', [(b, b ^ 1) for b in range(INNER)])  2.58 us
    pallas_call x1, Pallas kernels, on_device(): call(functools.partial(prologue_kernel, tm_count), [HBM] * 4, [sds((blk_c...  2.4 us
    ppermute x1, starting transfers between devices, on_device(): lax.ppermute(head, 'outer', [(b, b - 1) for b in range(1, outer_count)])  1.29 us
  transfers between devices with their start and end apart: 10, of which 6 were waited for; matrix products, arithmetic and copies ran while one was open for 0% of the time, Pallas kernels for 15%

profile of v7, /device:TPU:0, one launch (start us, length us, event | category | flops | bytes accessed | tf_op | source)
XLA Modules:
  0.0 46.8 jit_solution(17510448426750594794)
XLA Ops:
  0.0 2.4 %shard_map.46 = (bf16[16,144,128]{2,1,0:T(8,128)(2,1)}, bf16[256,512]{1,0:T(8,128)(2,1)}, bf16[256,512]{1,0:T(8,128)(2,1)}) custom-call(bf16[1,480,256]{2,1,0:T(8,128)(2,1)} %tpl_hbm.1, s32[1,160]{1,0:T(1,128)} %flag_hbm.1, s32[1,480]{1,0:T(1,128)} %bitcast.1, bf16[480,512]{1,0:T(8,128)(2,1)} %wave_ref.1), custom_call_target="tpu_custom_call" | custom-call | bytes 737280 | tf_op jit(solution)/shard_map/pallas_call | solution.py:295
  2.4 7.5 %all-to-all-start = ((bf16[16,144,128]{2,1,0:T(8,128)(2,1)}), bf16[16,144,128]{2,1,0:T(8,128)(2,1)S(1)}, u32[]{:S(2)}, u32[]{:S(2)}) async-start(bf16[16,144,128]{2,1,0:T(8,128)(2,1)} %get-tuple-element.23), calls=%async_computation | async-start | bytes 1179648 | tf_op jit(solution)/shard_map/all_to_all | solution.py:315
  10.0 0.5 %collective-permute-start = (bf16[256,512]{1,0:T(8,128)(2,1)S(1)}, bf16[256,512]{1,0:T(8,128)(2,1)S(1)}, u32[]{:S(2)}, u32[]{:S(2)}) collective-permute-start(bf16[256,512]{1,0:T(8,128)(2,1)S(1)} %copy-done.3), channel_id=1, source_target_pairs={{0,2},{2,0},{4,6},{6,4},{1,3},{3,1},{5,7},{7,5},{8,10},{10,8},{12,... | collective-permute-start | bytes 786440 | tf_op jit(solution)/shard_map/ppermute | solution.py:317
  10.4 1.2 %collective-permute-done.got_ref = bf16[256,512]{1,0:T(8,128)(2,1)S(1)} collective-permute-done((bf16[256,512]{1,0:T(8,128)(2,1)S(1)}, bf16[256,512]{1,0:T(8,128)(2,1)S(1)}, u32[]{:S(2)}, u32[]{:S(2)}) %collective-permute-start) | collective-permute-done | bytes 262176 | tf_op jit(solution)/shard_map/ppermute | solution.py:317
  11.6 1.6 %collective-permute-start.1 = (bf16[2,64,512]{2,1,0:T(8,128)(2,1)S(1)}, bf16[2,64,512]{2,1,0:T(8,128)(2,1)S(1)}, u32[]{:S(2)}, u32[]{:S(2)}) collective-permute-start(bf16[2,64,512]{2,1,0:T(8,128)(2,1)S(1)} %get-tuple-element.27), channel_id=1, source_target_pairs={{0,1},{1,0},{2,3},{3,2},{4,5},{5,4},{6,7},{7,6},{8,9},{9,8},{10,11... | collective-permute-start | bytes 393224 | tf_op jit(solution)/shard_map/ppermute | solution.py:329
  13.2 1.9 %collective-permute-start.2 = (bf16[2,64,512]{2,1,0:T(8,128)(2,1)S(1)}, bf16[2,64,512]{2,1,0:T(8,128)(2,1)S(1)}, u32[]{:S(2)}, u32[]{:S(2)}) collective-permute-start(bf16[2,64,512]{2,1,0:T(8,128)(2,1)S(1)} %get-tuple-element.28), channel_id=1, source_target_pairs={{0,4},{1,5},{2,6},{3,7},{4,0},{5,1},{6,2},{7,3},{8,12},{9,13},{10,... | collective-permute-start | bytes 393224 | tf_op jit(solution)/shard_map/ppermute | solution.py:329
  15.1 0.1 collective-permute-start.3
  15.2 2.6 %collective-permute-done.1.refs_1_ = bf16[2,64,512]{2,1,0:T(8,128)(2,1)S(1)} collective-permute-done((bf16[2,64,512]{2,1,0:T(8,128)(2,1)S(1)}, bf16[2,64,512]{2,1,0:T(8,128)(2,1)S(1)}, u32[]{:S(2)}, u32[]{:S(2)}) %collective-permute-start.1) | collective-permute-done | bytes 131104 | tf_op jit(solution)/shard_map/ppermute | solution.py:329
  17.8 6.3 %collective-permute-done.2.refs_2_ = bf16[2,64,512]{2,1,0:T(8,128)(2,1)S(1)} collective-permute-done((bf16[2,64,512]{2,1,0:T(8,128)(2,1)S(1)}, bf16[2,64,512]{2,1,0:T(8,128)(2,1)S(1)}, u32[]{:S(2)}, u32[]{:S(2)}) %collective-permute-start.2) | collective-permute-done | bytes 131104 | tf_op jit(solution)/shard_map/ppermute | solution.py:329
  24.1 0.0 collective-permute-done.3.refs_3_
  24.1 0.1 shard_map.48
  24.2 1.3 %collective-permute-start.4 = (bf16[64,256]{1,0:T(8,128)(2,1)S(1)}, bf16[64,256]{1,0:T(8,128)(2,1)S(1)}, u32[]{:S(2)}, u32[]{:S(2)}) collective-permute-start(bf16[64,256]{1,0:T(8,128)(2,1)S(1)} %get-tuple-element.31), channel_id=1, source_target_pairs={{8,0},{16,8},{24,16},{9,1},{17,9},{25,17},{10,2},{18,10},{26,18},{... | collective-permute-start | bytes 98312 | tf_op jit(solution)/shard_map/ppermute | solution.py:338
  25.5 0.0 all-to-all-done.tpls_ref.tpls
  25.5 6.7 %shard_map.50.done_ref = f32[6,16,512]{2,1,0:T(8,128)S(1)} custom-call(bf16[16,144,128]{2,1,0:T(8,128)(2,1)S(1)} %all-to-all-done.tpls_ref.tpls, bf16[64,4096]{1,0:T(8,128)(2,1)S(1)} %get-tuple-element.30.samples_ref), custom_call_target="tpu_custom_call" | custom-call | flops 1610612736 | bytes 524288 | tf_op jit(solution)/shard_map/pallas_call | solution.py:364
  32.3 0.4 shard_map.49
  32.7 3.3 %shard_map.51 = (f32[4,16,768]{2,1,0:T(8,128)S(1)}, f32[4,16,768]{2,1,0:T(8,128)S(1)}) custom-call(bf16[16,144,128]{2,1,0:T(8,128)(2,1)S(1)} %all-to-all-done.tpls_ref.tpls, bf16[64,4096]{1,0:T(8,128)(2,1)S(1)} %get-tuple-element.30.samples_ref, bf16[64,256]{1,0:T(8,128)(2,1)S(1)} %collective-permute-done.4.halo_ref, ...), custom_call_target="tpu_custom_call" | custom-call | flops 536870912 | bytes 524288 | tf_op jit(solution)/shard_map/pallas_call | solution.py:372
  36.1 0.1 collective-permute-start.5
  36.1 1.4 %collective-permute-done.5.got_ref = f32[4,16,768]{2,1,0:T(8,128)S(1)} collective-permute-done((f32[4,16,768]{2,1,0:T(8,128)S(1)}, f32[4,16,768]{2,1,0:T(8,128)S(1)}, u32[]{:S(2)}, u32[]{:S(2)}) %collective-permute-start.5) | collective-permute-done | bytes 196640 | tf_op jit(solution)/shard_map/ppermute | solution.py:380
  37.6 1.6 %collective-permute-start.6 = (f32[16,768]{1,0:T(8,128)S(1)}, f32[16,768]{1,0:T(8,128)S(1)}, u32[]{:S(2)}, u32[]{:S(2)}) collective-permute-start(f32[16,768]{1,0:T(8,128)S(1)} %get-tuple-element.36), channel_id=1, source_target_pairs={{0,1},{1,0},{2,3},{3,2},{4,5},{5,4},{6,7},{7,6},{8,9},{9,8},{10,11... | collective-permute-start | bytes 147464 | tf_op jit(solution)/shard_map/ppermute | solution.py:329
  39.1 1.6 %collective-permute-start.7 = (f32[16,768]{1,0:T(8,128)S(1)}, f32[16,768]{1,0:T(8,128)S(1)}, u32[]{:S(2)}, u32[]{:S(2)}) collective-permute-start(f32[16,768]{1,0:T(8,128)S(1)} %get-tuple-element.37), channel_id=1, source_target_pairs={{0,4},{1,5},{2,6},{3,7},{4,0},{5,1},{6,2},{7,3},{8,12},{9,13},{10,... | collective-permute-start | bytes 147464 | tf_op jit(solution)/shard_map/ppermute | solution.py:329
  40.7 1.0 %collective-permute-start.8 = (f32[16,768]{1,0:T(8,128)S(1)}, f32[16,768]{1,0:T(8,128)S(1)}, u32[]{:S(2)}, u32[]{:S(2)}) collective-permute-start(f32[16,768]{1,0:T(8,128)S(1)} %get-tuple-element.38), channel_id=1, source_target_pairs={{0,5},{1,4},{2,7},{3,6},{4,1},{5,0},{6,3},{7,2},{8,13},{9,12},{10,... | collective-permute-start | bytes 147464 | tf_op jit(solution)/shard_map/ppermute | solution.py:329
  41.8 1.5 %collective-permute-done.7.refs_2_ = f32[16,768]{1,0:T(8,128)S(1)} collective-permute-done((f32[16,768]{1,0:T(8,128)S(1)}, f32[16,768]{1,0:T(8,128)S(1)}, u32[]{:S(2)}, u32[]{:S(2)}) %collective-permute-start.7) | collective-permute-done | bytes 49184 | tf_op jit(solution)/shard_map/ppermute | solution.py:329
  43.2 2.5 %collective-permute-done.8.refs_3_ = f32[16,768]{1,0:T(8,128)S(1)} collective-permute-done((f32[16,768]{1,0:T(8,128)S(1)}, f32[16,768]{1,0:T(8,128)S(1)}, u32[]{:S(2)}, u32[]{:S(2)}) %collective-permute-start.8) | collective-permute-done | bytes 49184 | tf_op jit(solution)/shard_map/ppermute | solution.py:329
  45.7 1.1 %shard_map.53 = f32[16,512]{1,0:T(8,128)} custom-call(f32[16,768]{1,0:T(8,128)S(1)} %get-tuple-element.35.refs_0_, f32[16,768]{1,0:T(8,128)S(1)} %collective-permute-done.6.refs_1_, f32[16,768]{1,0:T(8,128)S(1)} %collective-permute-done.7.refs_2_, f32[16,768]{1,0:T(8,128)S(1)} %collective-permute-done.8.refs_3_, f32[16,512]{1,0:T(8,128)S(1)} %get-tuple-element.39.refs_4_, ...), custom_call_target="tpu_custom_call" | custom-call | bytes 196608 | tf_op jit(solution)/shard_map/pallas_call | solution.py:388
  (12 shorter events, 0.1 us)
Async XLA Ops:
  2.4 7.6 %copy-start.3 = (bf16[256,512]{1,0:T(8,128)(2,1)S(1)}, bf16[256,512]{1,0:T(8,128)(2,1)}, u32[]{:S(2)}) copy-start(bf16[256,512]{1,0:T(8,128)(2,1)} %get-tuple-element.25) | copy-start | bytes 786436
  2.4 9.2 %copy-start.1 = (bf16[256,512]{1,0:T(8,128)(2,1)S(1)}, bf16[256,512]{1,0:T(8,128)(2,1)}, u32[]{:S(2)}) copy-start(bf16[256,512]{1,0:T(8,128)(2,1)} %get-tuple-element.24.keep_ref) | copy-start | bytes 786436
  2.4 23.1 %all-to-all-start = ((bf16[16,144,128]{2,1,0:T(8,128)(2,1)}), bf16[16,144,128]{2,1,0:T(8,128)(2,1)S(1)}, u32[]{:S(2)}, u32[]{:S(2)}) async-start(bf16[16,144,128]{2,1,0:T(8,128)(2,1)} %get-tuple-element.23), calls=%async_computation | async-start | bytes 1179648 | tf_op jit(solution)/shard_map/all_to_all | solution.py:315
  10.0 1.6 %collective-permute-start = (bf16[256,512]{1,0:T(8,128)(2,1)S(1)}, bf16[256,512]{1,0:T(8,128)(2,1)S(1)}, u32[]{:S(2)}, u32[]{:S(2)}) collective-permute-start(bf16[256,512]{1,0:T(8,128)(2,1)S(1)} %copy-done.3), channel_id=1, source_target_pairs={{0,2},{2,0},{4,6},{6,4},{1,3},{3,1},{5,7},{7,5},{8,10},{10,8},{12,... | collective-permute-start | bytes 786440 | tf_op jit(solution)/shard_map/ppermute | solution.py:317
  11.6 6.2 %collective-permute-start.1 = (bf16[2,64,512]{2,1,0:T(8,128)(2,1)S(1)}, bf16[2,64,512]{2,1,0:T(8,128)(2,1)S(1)}, u32[]{:S(2)}, u32[]{:S(2)}) collective-permute-start(bf16[2,64,512]{2,1,0:T(8,128)(2,1)S(1)} %get-tuple-element.27), channel_id=1, source_target_pairs={{0,1},{1,0},{2,3},{3,2},{4,5},{5,4},{6,7},{7,6},{8,9},{9,8},{10,11... | collective-permute-start | bytes 393224 | tf_op jit(solution)/shard_map/ppermute | solution.py:329
  13.2 10.9 %collective-permute-start.2 = (bf16[2,64,512]{2,1,0:T(8,128)(2,1)S(1)}, bf16[2,64,512]{2,1,0:T(8,128)(2,1)S(1)}, u32[]{:S(2)}, u32[]{:S(2)}) collective-permute-start(bf16[2,64,512]{2,1,0:T(8,128)(2,1)S(1)} %get-tuple-element.28), channel_id=1, source_target_pairs={{0,4},{1,5},{2,6},{3,7},{4,0},{5,1},{6,2},{7,3},{8,12},{9,13},{10,... | collective-permute-start | bytes 393224 | tf_op jit(solution)/shard_map/ppermute | solution.py:329
  15.1 9.0 %collective-permute-start.3 = (bf16[2,64,512]{2,1,0:T(8,128)(2,1)S(1)}, bf16[2,64,512]{2,1,0:T(8,128)(2,1)S(1)}, u32[]{:S(2)}, u32[]{:S(2)}) collective-permute-start(bf16[2,64,512]{2,1,0:T(8,128)(2,1)S(1)} %get-tuple-element.29), channel_id=1, source_target_pairs={{0,5},{1,4},{2,7},{3,6},{4,1},{5,0},{6,3},{7,2},{8,13},{9,12},{10,... | collective-permute-start | bytes 393224 | tf_op jit(solution)/shard_map/ppermute | solution.py:329
  24.2 8.5 %collective-permute-start.4 = (bf16[64,256]{1,0:T(8,128)(2,1)S(1)}, bf16[64,256]{1,0:T(8,128)(2,1)S(1)}, u32[]{:S(2)}, u32[]{:S(2)}) collective-permute-start(bf16[64,256]{1,0:T(8,128)(2,1)S(1)} %get-tuple-element.31), channel_id=1, source_target_pairs={{8,0},{16,8},{24,16},{9,1},{17,9},{25,17},{10,2},{18,10},{26,18},{... | collective-permute-start | bytes 98312 | tf_op jit(solution)/shard_map/ppermute | solution.py:338
  25.5 6.7 %copy-start = (bf16[480,512]{1,0:T(8,128)(2,1)S(1)}, bf16[480,512]{1,0:T(8,128)(2,1)}, u32[]{:S(2)}) copy-start(bf16[480,512]{1,0:T(8,128)(2,1)} %wave_ref.1) | copy-start | bytes 1474564
  25.5 6.7 %copy-start.2 = (s32[480]{0:T(512)S(1)}, s32[480]{0:T(512)}, u32[]{:S(2)}) copy-start(s32[480]{0:T(512)} %param.7) | copy-start | bytes 5764
  36.1 1.5 %collective-permute-start.5 = (f32[4,16,768]{2,1,0:T(8,128)S(1)}, f32[4,16,768]{2,1,0:T(8,128)S(1)}, u32[]{:S(2)}, u32[]{:S(2)}) collective-permute-start(f32[4,16,768]{2,1,0:T(8,128)S(1)} %get-tuple-element.34), channel_id=1, source_target_pairs={{0,2},{2,0},{4,6},{6,4},{1,3},{3,1},{5,7},{7,5},{8,10},{10,8},{12,... | collective-permute-start | bytes 589832 | tf_op jit(solution)/shard_map/ppermute | solution.py:380
  37.6 4.2 %collective-permute-start.6 = (f32[16,768]{1,0:T(8,128)S(1)}, f32[16,768]{1,0:T(8,128)S(1)}, u32[]{:S(2)}, u32[]{:S(2)}) collective-permute-start(f32[16,768]{1,0:T(8,128)S(1)} %get-tuple-element.36), channel_id=1, source_target_pairs={{0,1},{1,0},{2,3},{3,2},{4,5},{5,4},{6,7},{7,6},{8,9},{9,8},{10,11... | collective-permute-start | bytes 147464 | tf_op jit(solution)/shard_map/ppermute | solution.py:329
  39.1 4.1 %collective-permute-start.7 = (f32[16,768]{1,0:T(8,128)S(1)}, f32[16,768]{1,0:T(8,128)S(1)}, u32[]{:S(2)}, u32[]{:S(2)}) collective-permute-start(f32[16,768]{1,0:T(8,128)S(1)} %get-tuple-element.37), channel_id=1, source_target_pairs={{0,4},{1,5},{2,6},{3,7},{4,0},{5,1},{6,2},{7,3},{8,12},{9,13},{10,... | collective-permute-start | bytes 147464 | tf_op jit(solution)/shard_map/ppermute | solution.py:329
  40.7 5.0 %collective-permute-start.8 = (f32[16,768]{1,0:T(8,128)S(1)}, f32[16,768]{1,0:T(8,128)S(1)}, u32[]{:S(2)}, u32[]{:S(2)}) collective-permute-start(f32[16,768]{1,0:T(8,128)S(1)} %get-tuple-element.38), channel_id=1, source_target_pairs={{0,5},{1,4},{2,7},{3,6},{4,1},{5,0},{6,3},{7,2},{8,13},{9,12},{10,... | collective-permute-start | bytes 147464 | tf_op jit(solution)/shard_map/ppermute | solution.py:329

commit v8 on v7

--- a/solution.py
+++ b/solution.py
@@ -156,28 +156,46 @@
         left[:, step * LANES : (step + 1) * LANES] = jnp.dot(
             order, rows, preferred_element_type=F32
         ).astype(BF16)
-    tiles = products.shape[1] // LANES
+    tiles = products.shape[2] // LANES
     span = (tiles - 1) * LANES
     per_block = span // slab
-
-    def block(index, carry):
+    blocks = usable // span
+
+    def multiply(index, slot):
         start = pl.multiple_of(index * span, span)
         for tile in range(0, tiles, 2):
             width = min(2, tiles - tile) * LANES
             here = pl.ds(pl.multiple_of(start + tile * LANES, LANES), width)
-            products[:, tile * LANES : tile * LANES + width] = jnp.dot(
+            products[slot, :, tile * LANES : tile * LANES + width] = jnp.dot(
                 left[...], shifts[:, here], preferred_element_type=F32
             )
-        total = products[(FINE - 1) * count :, :]
-        for fine in reversed(range(FINE - 1)):
-            total = products[fine * count : (fine + 1) * count, :] + pltpu.roll(
-                total, span + LANES - 1, 1
-            )
+
+    def gather(index, slot):
+        def tree(first, number):
+            if number == 1:
+                return products[slot, first * count : (first + 1) * count, :]
+            half = number // 2
+            later = pltpu.roll(tree(first + half, half), span + LANES - half, 1)
+            return tree(first, half) + later
+
+        total = tree(0, FINE)
         for piece in range(per_block):
             out_ref[first + index * per_block + piece] = total[:, piece * slab : (piece + 1) * slab]
-        return carry
-
-    lax.fori_loop(0, usable // span, block, 0)
+
+    multiply(0, 0)
+    if blocks <= 4:
+        for index in range(1, blocks):
+            multiply(index, index % 2)
+            gather(index - 1, (index - 1) % 2)
+    else:
+
+        def step(index, carry):
+            multiply(index, lax.rem(index, 2))
+            gather(index - 1, lax.rem(index + 1, 2))
+            return carry
+
+        lax.fori_loop(1, blocks, step, 0)
+    gather(blocks - 1, (blocks - 1) % 2)
 
 
 def first_dots_kernel(tpls, samples_ref, out_ref, left, shifts, products):
@@ -186,39 +204,34 @@
 
 
 def last_dots_kernel(tpls, samples_ref, halo_ref, mask_ref, done_ref, *refs):
-    keep_ref, send_ref, out_ref = refs[:3]
-    scratch = refs[3:]
+    keep_ref, send_ref, out_ref, edges = refs[:4]
+    scratch = refs[4:]
     first, slab = done_ref.shape[0], done_ref.shape[2]
-    half = keep_ref.shape[0]
-    run = half // 2
-    core = lax.rem(lax.axis_index("inner"), 2)
-
-    def powers(member, out):
-        start = (member + 1) * slab
-        if start < samples_ref.shape[1]:
-            wave = samples_ref[:, start : start + halo_ref.shape[1]]
-        else:
-            wave = halo_ref[...]
-        out[...] = masked_squares(mask_ref[...], wave)
-
-    for y in range(2):
-        for side in range(2):
-            for tm in range(run):
-                member = (2 * y + side) * run + tm
-                for owner, out in ((core, keep_ref), (1 - core, send_ref)):
-
-                    @pl.when(owner == side)
-                    def _():
-                        powers(member, out.at[y * run + tm, :, pl.ds(slab, halo_ref.shape[1])])
-
-    rest = samples_ref.shape[1] + halo_ref.shape[1] - scratch[1].shape[1] - LANES
+    group = edges.shape[0]
+    window = halo_ref.shape[1]
+    after = [samples_ref[:, (m + 1) * slab : (m + 1) * slab + window] for m in range(group - 1)]
+    squares = masked_squares(mask_ref[...], jnp.concatenate(after + [halo_ref[...]], axis=1))
+    column = lax.broadcasted_iota(jnp.int32, squares.shape, 1) % window
+    reach = 1
+    while reach < window:
+        earlier = pltpu.roll(squares, reach, 1)
+        squares = squares + jnp.where(column >= reach, earlier, 0.0)
+        reach *= 2
+    squares = jnp.where(column >= 1, pltpu.roll(squares, 1, 1), 0.0)
+    for member in range(group):
+        edges[member] = squares[:, member * window : (member + 1) * window]
+    rest = samples_ref.shape[1] + window - scratch[1].shape[1] - LANES
     samples = jnp.concatenate([samples_ref[:, rest:], halo_ref[...]], axis=1)
     out_ref[:first] = done_ref[...]
     correlate(tpls, samples, out_ref, first, *scratch)
+    core = lax.rem(lax.axis_index("inner"), 2)
+    run = keep_ref.shape[0] // 2
     for y in range(2):
         for tm in range(run):
-            keep_ref[y * run + tm, :, :slab] = out_ref[(2 * y + core) * run + tm]
-            send_ref[y * run + tm, :, :slab] = out_ref[(2 * y + 1 - core) * run + tm]
+            for ref, side in ((keep_ref, core), (send_ref, 1 - core)):
+                member = (2 * y + side) * run + tm
+                ref[y * run + tm, :, :slab] = out_ref[member]
+                ref[y * run + tm, :, slab:] = edges[member]
 
 
 def add_kernel(tm_count, keep_ref, got_ref, *outs):
@@ -237,7 +250,7 @@
     )
 
 
-def power_kernel(stations, tm_count, wave_ref, tpls_ref, order_ref, *refs):
+def power_kernel(stations, window, tm_count, wave_ref, tpls_ref, order_ref, *refs):
     out_ref, scale_ref, mask_ref, order_pad = refs
     extra = tpls_ref[:, tpls_ref.shape[1] - META :, :].astype(F32)
     scale_ref[...] = extra[:, 0, :] + extra[:, 1, :] + extra[:, 2, :]
@@ -252,27 +265,32 @@
         one_hot(order_pad[...], tiles * LANES),
         preferred_element_type=F32,
     )
-    out_ref[...] = masked_squares(mask[:, :channels].astype(BF16), wave_ref[...])
+    power = masked_squares(mask[:, :channels].astype(BF16), wave_ref[...])
+    columns = power.shape[1]
+    column = lax.broadcasted_iota(jnp.int32, power.shape, 1)
+    reach = 1
+    while reach < window:
+        later = pltpu.roll(power, columns - reach, 1)
+        power = power + jnp.where(column < columns - reach, later, 0.0)
+        reach *= 2
+    out_ref[...] = power
     part = LANES // tm_count
     mine = side_major(lax.axis_index("inner")) * LANES + lax.axis_index("tm") * part
     mask_ref[...] = pltpu.roll(mask, lax.rem(padded - mine, padded), 1)[:, :part].astype(BF16)
 
 
 def finish_kernel(*refs):
-    parts, (power_ref, scale_ref, out_ref, joined) = refs[:-4], refs[-4:]
+    parts, (power_ref, scale_ref, out_ref) = refs[:-3], refs[-3:]
     slab = power_ref.shape[1]
     total = parts[0][...]
     for part in parts[1:]:
         total = total + part[...]
-    joined[:, :slab] = power_ref[...]
-    joined[:, slab:] = total[:, slab:]
-    running = joined[...]
-    columns = running.shape[1]
-    width = 1
-    while width < columns - slab:
-        running = running + pltpu.roll(running, columns - width, 1)
-        width *= 2
-    out_ref[...] = total[:, :slab] * (scale_ref[:, :1] / jnp.sqrt(running[:, :slab] + EPSILON))
+    dots, edge = total[:, :slab], total[:, slab:]
+    inside = slab - edge.shape[1]
+    energy = jnp.concatenate(
+        [power_ref[:, :inside], power_ref[:, inside:] + edge], axis=1
+    )
+    out_ref[...] = dots * (scale_ref[:, :1] / jnp.sqrt(energy + EPSILON))
 
 
 def on_device(waveforms, templates, station_mask, channel_order):
@@ -338,7 +356,7 @@
     halo = lax.ppermute(head, "outer", [(b, b - 1) for b in range(1, outer_count)])
 
     power, scale, mask = call(
-        functools.partial(power_kernel, stations, tm_count),
+        functools.partial(power_kernel, stations, window, tm_count),
         [VMEM] * 3,
         [
             sds((blk_count, slab), F32),
@@ -356,7 +374,7 @@
         return [
             pltpu.VMEM((blk_count * FINE, depth), BF16),
             pltpu.VMEM((depth, columns + LANES), BF16),
-            pltpu.VMEM((blk_count * FINE, span + LANES), F32),
+            pltpu.VMEM((2, blk_count * FINE, span + LANES), F32),
         ]
 
     blocks = group // 2
@@ -373,7 +391,11 @@
         last_dots_kernel,
         [VMEM] * 5,
         [sds((half, blk_count, slab + window), F32)] * 2,
-        [pltpu.VMEM((group, blk_count, slab), F32)] + scratch(span),
+        [
+            pltpu.VMEM((group, blk_count, slab), F32),
+            pltpu.VMEM((group, blk_count, window), F32),
+        ]
+        + scratch(span),
         flops=work,
         bytes_accessed=part * chunk * 2,
     )(tpls, samples, halo, mask, partials)
@@ -389,7 +411,6 @@
         finish_kernel,
         [VMEM] * (half + 2),
         sds((blk_count, slab), F32),
-        [pltpu.VMEM((blk_count, slab + window), F32)],
         bytes_accessed=blk_count * slab * 4 * (half + 2),
     )(*sums, power, scale)
 

time: 47.1 us -> 42.4 us (0.900)
  Pallas kernels: 14.2 us -> 9.33 us
  waiting for transfers between devices: 15.5 us -> 16.2 us
  starting transfers between devices: 17.1 us -> 16.5 us
    pallas_call x1, Pallas kernels: 6.72 us -> 3.31 us  [on_device(): call(first_dots_kernel, [VMEM] * 2, sds((2 * (blocks - 1), blk_count, sla...]
    pallas_call x1, Pallas kernels: 3.35 us -> 1.86 us  [on_device(): call(last_dots_kernel, [VMEM] * 5, [sds((half, blk_count, slab + window),...]
    ppermute x1, waiting for transfers between devices: 0.01 us -> 1.3 us  [on_device(): lax.ppermute(head, 'outer', [(b, b - 1) for b in range(1, outer_count)])]
    ppermute x6, starting transfers between devices: 7.72 us -> 7.12 us  [swap(): return lax.ppermute(part, every, route)]
    ppermute x6, waiting for transfers between devices: 12.8 us -> 12.3 us  [swap(): return lax.ppermute(part, every, route)]
  transfers between devices with their start and end apart: 10 -> 10, of which waited for: 6 -> 8; matrix products, arithmetic and copies ran while one was open for 0% -> 0% of each run, Pallas kernels for 15% -> 10%
where the time goes in v8:
time: 42.4 us; the launch traced here: 42.2 us
  starting transfers between devices  16.5 us (39%)
  waiting for transfers between devices  16.2 us (38%)
  Pallas kernels  9.33 us (22%)
    ppermute x6, waiting for transfers between devices, swap(): return lax.ppermute(part, every, route)  12.3 us
    all_to_all x1, starting transfers between devices, on_device(): tpls = lax.all_to_all(payload, blk, 0, 0, tiled=True)  7.53 us
    ppermute x6, starting transfers between devices, swap(): return lax.ppermute(part, every, route)  7.12 us
    pallas_call x1, Pallas kernels, on_device(): call(first_dots_kernel, [VMEM] * 2, sds((2 * (blocks - 1), blk_count, sla...  3.31 us
    ppermute x2, waiting for transfers between devices, on_device(): got = lax.ppermute(send, 'inner', [(b, b ^ 1) for b in range(INNER)])  2.59 us
    pallas_call x1, Pallas kernels, on_device(): call(functools.partial(prologue_kernel, tm_count), [HBM] * 4, [sds((blk_c...  2.4 us
    pallas_call x1, Pallas kernels, on_device(): call(last_dots_kernel, [VMEM] * 5, [sds((half, blk_count, slab + window),...  1.86 us
    ppermute x1, waiting for transfers between devices, on_device(): lax.ppermute(head, 'outer', [(b, b - 1) for b in range(1, outer_count)])  1.3 us
  transfers between devices with their start and end apart: 10, of which 8 were waited for; matrix products, arithmetic and copies ran while one was open for 0% of the time, Pallas kernels for 10%

profile of v8, /device:TPU:0, one launch (start us, length us, event | category | flops | bytes accessed | tf_op | source)
XLA Modules:
  0.0 42.2 jit_solution(5345350659215722926)
XLA Ops:
  0.0 2.4 %shard_map.46 = (bf16[16,144,128]{2,1,0:T(8,128)(2,1)}, bf16[256,512]{1,0:T(8,128)(2,1)}, bf16[256,512]{1,0:T(8,128)(2,1)}) custom-call(bf16[1,480,256]{2,1,0:T(8,128)(2,1)} %tpl_hbm.1, s32[1,160]{1,0:T(1,128)} %flag_hbm.1, s32[1,480]{1,0:T(1,128)} %bitcast.1, bf16[480,512]{1,0:T(8,128)(2,1)} %wave_ref.1), custom_call_target="tpu_custom_call" | custom-call | bytes 737280 | tf_op jit(solution)/shard_map/pallas_call | solution.py:313
  2.4 7.5 %all-to-all-start = ((bf16[16,144,128]{2,1,0:T(8,128)(2,1)}), bf16[16,144,128]{2,1,0:T(8,128)(2,1)S(1)}, u32[]{:S(2)}, u32[]{:S(2)}) async-start(bf16[16,144,128]{2,1,0:T(8,128)(2,1)} %get-tuple-element.23), calls=%async_computation | async-start | bytes 1179648 | tf_op jit(solution)/shard_map/all_to_all | solution.py:333
  10.0 0.5 %collective-permute-start = (bf16[256,512]{1,0:T(8,128)(2,1)S(1)}, bf16[256,512]{1,0:T(8,128)(2,1)S(1)}, u32[]{:S(2)}, u32[]{:S(2)}) collective-permute-start(bf16[256,512]{1,0:T(8,128)(2,1)S(1)} %copy-done.3), channel_id=1, source_target_pairs={{0,2},{2,0},{4,6},{6,4},{1,3},{3,1},{5,7},{7,5},{8,10},{10,8},{12,... | collective-permute-start | bytes 786440 | tf_op jit(solution)/shard_map/ppermute | solution.py:335
  10.4 1.2 %collective-permute-done.got_ref = bf16[256,512]{1,0:T(8,128)(2,1)S(1)} collective-permute-done((bf16[256,512]{1,0:T(8,128)(2,1)S(1)}, bf16[256,512]{1,0:T(8,128)(2,1)S(1)}, u32[]{:S(2)}, u32[]{:S(2)}) %collective-permute-start) | collective-permute-done | bytes 262176 | tf_op jit(solution)/shard_map/ppermute | solution.py:335
  11.6 1.6 %collective-permute-start.1 = (bf16[2,64,512]{2,1,0:T(8,128)(2,1)S(1)}, bf16[2,64,512]{2,1,0:T(8,128)(2,1)S(1)}, u32[]{:S(2)}, u32[]{:S(2)}) collective-permute-start(bf16[2,64,512]{2,1,0:T(8,128)(2,1)S(1)} %get-tuple-element.27), channel_id=1, source_target_pairs={{0,1},{1,0},{2,3},{3,2},{4,5},{5,4},{6,7},{7,6},{8,9},{9,8},{10,11... | collective-permute-start | bytes 393224 | tf_op jit(solution)/shard_map/ppermute | solution.py:347
  13.2 1.9 %collective-permute-start.2 = (bf16[2,64,512]{2,1,0:T(8,128)(2,1)S(1)}, bf16[2,64,512]{2,1,0:T(8,128)(2,1)S(1)}, u32[]{:S(2)}, u32[]{:S(2)}) collective-permute-start(bf16[2,64,512]{2,1,0:T(8,128)(2,1)S(1)} %get-tuple-element.28), channel_id=1, source_target_pairs={{0,4},{1,5},{2,6},{3,7},{4,0},{5,1},{6,2},{7,3},{8,12},{9,13},{10,... | collective-permute-start | bytes 393224 | tf_op jit(solution)/shard_map/ppermute | solution.py:347
  15.1 0.1 collective-permute-start.3
  15.2 2.6 %collective-permute-done.1.refs_1_ = bf16[2,64,512]{2,1,0:T(8,128)(2,1)S(1)} collective-permute-done((bf16[2,64,512]{2,1,0:T(8,128)(2,1)S(1)}, bf16[2,64,512]{2,1,0:T(8,128)(2,1)S(1)}, u32[]{:S(2)}, u32[]{:S(2)}) %collective-permute-start.1) | collective-permute-done | bytes 131104 | tf_op jit(solution)/shard_map/ppermute | solution.py:347
  17.8 6.3 %collective-permute-done.2.refs_2_ = bf16[2,64,512]{2,1,0:T(8,128)(2,1)S(1)} collective-permute-done((bf16[2,64,512]{2,1,0:T(8,128)(2,1)S(1)}, bf16[2,64,512]{2,1,0:T(8,128)(2,1)S(1)}, u32[]{:S(2)}, u32[]{:S(2)}) %collective-permute-start.2) | collective-permute-done | bytes 131104 | tf_op jit(solution)/shard_map/ppermute | solution.py:347
  24.1 0.1 shard_map.48
  24.2 1.3 %collective-permute-start.4 = (bf16[64,256]{1,0:T(8,128)(2,1)S(1)}, bf16[64,256]{1,0:T(8,128)(2,1)S(1)}, u32[]{:S(2)}, u32[]{:S(2)}) collective-permute-start(bf16[64,256]{1,0:T(8,128)(2,1)S(1)} %get-tuple-element.31), channel_id=1, source_target_pairs={{8,0},{16,8},{24,16},{9,1},{17,9},{25,17},{10,2},{18,10},{26,18},{... | collective-permute-start | bytes 98312 | tf_op jit(solution)/shard_map/ppermute | solution.py:356
  25.5 3.3 %shard_map.50.done_ref = f32[6,16,512]{2,1,0:T(8,128)S(1)} custom-call(bf16[16,144,128]{2,1,0:T(8,128)(2,1)S(1)} %all-to-all-done.tpls_ref.tpls, bf16[64,4096]{1,0:T(8,128)(2,1)S(1)} %get-tuple-element.30.samples_ref), custom_call_target="tpu_custom_call" | custom-call | flops 1610612736 | bytes 524288 | tf_op jit(solution)/shard_map/pallas_call | solution.py:382
  28.8 1.0 %shard_map.49 = (f32[16,512]{1,0:T(8,128)S(1)}, f32[16,128]{1,0:T(8,128)S(1)}, bf16[16,64]{1,0:T(8,128)(2,1)S(1)}) custom-call(bf16[480,512]{1,0:T(8,128)(2,1)S(1)} %copy-done, bf16[16,144,128]{2,1,0:T(8,128)(2,1)S(1)} %all-to-all-done.tpls_ref.tpls, s32[1,480]{1,0:T(1,128)S(1)} %bitcast.2), custom_call_target="tpu_custom_call" | custom-call | flops 15728640 | bytes 491520 | tf_op jit(solution)/shard_map/pallas_call | solution.py:358
  29.8 1.3 %collective-permute-done.4.halo_ref = bf16[64,256]{1,0:T(8,128)(2,1)S(1)} collective-permute-done((bf16[64,256]{1,0:T(8,128)(2,1)S(1)}, bf16[64,256]{1,0:T(8,128)(2,1)S(1)}, u32[]{:S(2)}, u32[]{:S(2)}) %collective-permute-start.4) | collective-permute-done | bytes 32800 | tf_op jit(solution)/shard_map/ppermute | solution.py:356
  31.1 1.9 %shard_map.51 = (f32[4,16,768]{2,1,0:T(8,128)S(1)}, f32[4,16,768]{2,1,0:T(8,128)S(1)}) custom-call(bf16[16,144,128]{2,1,0:T(8,128)(2,1)S(1)} %all-to-all-done.tpls_ref.tpls, bf16[64,4096]{1,0:T(8,128)(2,1)S(1)} %get-tuple-element.30.samples_ref, bf16[64,256]{1,0:T(8,128)(2,1)S(1)} %collective-permute-done.4.halo_ref, ...), custom_call_target="tpu_custom_call" | custom-call | flops 536870912 | bytes 524288 | tf_op jit(solution)/shard_map/pallas_call | solution.py:390
  33.0 0.1 collective-permute-start.5
  33.1 1.4 %collective-permute-done.5.got_ref = f32[4,16,768]{2,1,0:T(8,128)S(1)} collective-permute-done((f32[4,16,768]{2,1,0:T(8,128)S(1)}, f32[4,16,768]{2,1,0:T(8,128)S(1)}, u32[]{:S(2)}, u32[]{:S(2)}) %collective-permute-start.5) | collective-permute-done | bytes 196640 | tf_op jit(solution)/shard_map/ppermute | solution.py:402
  34.5 0.5 %collective-permute-start.6 = (f32[16,768]{1,0:T(8,128)S(1)}, f32[16,768]{1,0:T(8,128)S(1)}, u32[]{:S(2)}, u32[]{:S(2)}) collective-permute-start(f32[16,768]{1,0:T(8,128)S(1)} %get-tuple-element.36), channel_id=1, source_target_pairs={{0,1},{1,0},{2,3},{3,2},{4,5},{5,4},{6,7},{7,6},{8,9},{9,8},{10,11... | collective-permute-start | bytes 147464 | tf_op jit(solution)/shard_map/ppermute | solution.py:347
  35.0 1.4 %collective-permute-start.7 = (f32[16,768]{1,0:T(8,128)S(1)}, f32[16,768]{1,0:T(8,128)S(1)}, u32[]{:S(2)}, u32[]{:S(2)}) collective-permute-start(f32[16,768]{1,0:T(8,128)S(1)} %get-tuple-element.37), channel_id=1, source_target_pairs={{0,4},{1,5},{2,6},{3,7},{4,0},{5,1},{6,2},{7,3},{8,12},{9,13},{10,... | collective-permute-start | bytes 147464 | tf_op jit(solution)/shard_map/ppermute | solution.py:347
  36.5 1.6 %collective-permute-start.8 = (f32[16,768]{1,0:T(8,128)S(1)}, f32[16,768]{1,0:T(8,128)S(1)}, u32[]{:S(2)}, u32[]{:S(2)}) collective-permute-start(f32[16,768]{1,0:T(8,128)S(1)} %get-tuple-element.38), channel_id=1, source_target_pairs={{0,5},{1,4},{2,7},{3,6},{4,1},{5,0},{6,3},{7,2},{8,13},{9,12},{10,... | collective-permute-start | bytes 147464 | tf_op jit(solution)/shard_map/ppermute | solution.py:347
  38.1 0.6 %collective-permute-done.6.refs_1_ = f32[16,768]{1,0:T(8,128)S(1)} collective-permute-done((f32[16,768]{1,0:T(8,128)S(1)}, f32[16,768]{1,0:T(8,128)S(1)}, u32[]{:S(2)}, u32[]{:S(2)}) %collective-permute-start.6) | collective-permute-done | bytes 49184 | tf_op jit(solution)/shard_map/ppermute | solution.py:347
  38.7 0.5 %collective-permute-done.7.refs_2_ = f32[16,768]{1,0:T(8,128)S(1)} collective-permute-done((f32[16,768]{1,0:T(8,128)S(1)}, f32[16,768]{1,0:T(8,128)S(1)}, u32[]{:S(2)}, u32[]{:S(2)}) %collective-permute-start.7) | collective-permute-done | bytes 49184 | tf_op jit(solution)/shard_map/ppermute | solution.py:347
  39.1 2.3 %collective-permute-done.8.refs_3_ = f32[16,768]{1,0:T(8,128)S(1)} collective-permute-done((f32[16,768]{1,0:T(8,128)S(1)}, f32[16,768]{1,0:T(8,128)S(1)}, u32[]{:S(2)}, u32[]{:S(2)}) %collective-permute-start.8) | collective-permute-done | bytes 49184 | tf_op jit(solution)/shard_map/ppermute | solution.py:347
  41.5 0.7 %shard_map.53 = f32[16,512]{1,0:T(8,128)} custom-call(f32[16,768]{1,0:T(8,128)S(1)} %get-tuple-element.35.refs_0_, f32[16,768]{1,0:T(8,128)S(1)} %collective-permute-done.6.refs_1_, f32[16,768]{1,0:T(8,128)S(1)} %collective-permute-done.7.refs_2_, f32[16,768]{1,0:T(8,128)S(1)} %collective-permute-done.8.refs_3_, f32[16,512]{1,0:T(8,128)S(1)} %get-tuple-element.39.refs_4_, ...), custom_call_target="tpu_custom_call" | custom-call | bytes 196608 | tf_op jit(solution)/shard_map/pallas_call | solution.py:410
  (12 shorter events, 0.1 us)
Async XLA Ops:
  2.4 7.6 %copy-start.3 = (bf16[256,512]{1,0:T(8,128)(2,1)S(1)}, bf16[256,512]{1,0:T(8,128)(2,1)}, u32[]{:S(2)}) copy-start(bf16[256,512]{1,0:T(8,128)(2,1)} %get-tuple-element.25) | copy-start | bytes 786436
  2.4 9.2 %copy-start.1 = (bf16[256,512]{1,0:T(8,128)(2,1)S(1)}, bf16[256,512]{1,0:T(8,128)(2,1)}, u32[]{:S(2)}) copy-start(bf16[256,512]{1,0:T(8,128)(2,1)} %get-tuple-element.24.keep_ref) | copy-start | bytes 786436
  2.4 23.1 %all-to-all-start = ((bf16[16,144,128]{2,1,0:T(8,128)(2,1)}), bf16[16,144,128]{2,1,0:T(8,128)(2,1)S(1)}, u32[]{:S(2)}, u32[]{:S(2)}) async-start(bf16[16,144,128]{2,1,0:T(8,128)(2,1)} %get-tuple-element.23), calls=%async_computation | async-start | bytes 1179648 | tf_op jit(solution)/shard_map/all_to_all | solution.py:333
  10.0 1.6 %collective-permute-start = (bf16[256,512]{1,0:T(8,128)(2,1)S(1)}, bf16[256,512]{1,0:T(8,128)(2,1)S(1)}, u32[]{:S(2)}, u32[]{:S(2)}) collective-permute-start(bf16[256,512]{1,0:T(8,128)(2,1)S(1)} %copy-done.3), channel_id=1, source_target_pairs={{0,2},{2,0},{4,6},{6,4},{1,3},{3,1},{5,7},{7,5},{8,10},{10,8},{12,... | collective-permute-start | bytes 786440 | tf_op jit(solution)/shard_map/ppermute | solution.py:335
  11.6 6.2 %collective-permute-start.1 = (bf16[2,64,512]{2,1,0:T(8,128)(2,1)S(1)}, bf16[2,64,512]{2,1,0:T(8,128)(2,1)S(1)}, u32[]{:S(2)}, u32[]{:S(2)}) collective-permute-start(bf16[2,64,512]{2,1,0:T(8,128)(2,1)S(1)} %get-tuple-element.27), channel_id=1, source_target_pairs={{0,1},{1,0},{2,3},{3,2},{4,5},{5,4},{6,7},{7,6},{8,9},{9,8},{10,11... | collective-permute-start | bytes 393224 | tf_op jit(solution)/shard_map/ppermute | solution.py:347
  13.2 10.9 %collective-permute-start.2 = (bf16[2,64,512]{2,1,0:T(8,128)(2,1)S(1)}, bf16[2,64,512]{2,1,0:T(8,128)(2,1)S(1)}, u32[]{:S(2)}, u32[]{:S(2)}) collective-permute-start(bf16[2,64,512]{2,1,0:T(8,128)(2,1)S(1)} %get-tuple-element.28), channel_id=1, source_target_pairs={{0,4},{1,5},{2,6},{3,7},{4,0},{5,1},{6,2},{7,3},{8,12},{9,13},{10,... | collective-permute-start | bytes 393224 | tf_op jit(solution)/shard_map/ppermute | solution.py:347
  15.1 9.0 %collective-permute-start.3 = (bf16[2,64,512]{2,1,0:T(8,128)(2,1)S(1)}, bf16[2,64,512]{2,1,0:T(8,128)(2,1)S(1)}, u32[]{:S(2)}, u32[]{:S(2)}) collective-permute-start(bf16[2,64,512]{2,1,0:T(8,128)(2,1)S(1)} %get-tuple-element.29), channel_id=1, source_target_pairs={{0,5},{1,4},{2,7},{3,6},{4,1},{5,0},{6,3},{7,2},{8,13},{9,12},{10,... | collective-permute-start | bytes 393224 | tf_op jit(solution)/shard_map/ppermute | solution.py:347
  24.2 7.0 %collective-permute-start.4 = (bf16[64,256]{1,0:T(8,128)(2,1)S(1)}, bf16[64,256]{1,0:T(8,128)(2,1)S(1)}, u32[]{:S(2)}, u32[]{:S(2)}) collective-permute-start(bf16[64,256]{1,0:T(8,128)(2,1)S(1)} %get-tuple-element.31), channel_id=1, source_target_pairs={{8,0},{16,8},{24,16},{9,1},{17,9},{25,17},{10,2},{18,10},{26,18},{... | collective-permute-start | bytes 98312 | tf_op jit(solution)/shard_map/ppermute | solution.py:356
  25.5 3.3 %copy-start = (bf16[480,512]{1,0:T(8,128)(2,1)S(1)}, bf16[480,512]{1,0:T(8,128)(2,1)}, u32[]{:S(2)}) copy-start(bf16[480,512]{1,0:T(8,128)(2,1)} %wave_ref.1) | copy-start | bytes 1474564
  25.5 3.3 %copy-start.2 = (s32[480]{0:T(512)S(1)}, s32[480]{0:T(512)}, u32[]{:S(2)}) copy-start(s32[480]{0:T(512)} %param.7) | copy-start | bytes 5764
  33.0 1.5 %collective-permute-start.5 = (f32[4,16,768]{2,1,0:T(8,128)S(1)}, f32[4,16,768]{2,1,0:T(8,128)S(1)}, u32[]{:S(2)}, u32[]{:S(2)}) collective-permute-start(f32[4,16,768]{2,1,0:T(8,128)S(1)} %get-tuple-element.34), channel_id=1, source_target_pairs={{0,2},{2,0},{4,6},{6,4},{1,3},{3,1},{5,7},{7,5},{8,10},{10,8},{12,... | collective-permute-start | bytes 589832 | tf_op jit(solution)/shard_map/ppermute | solution.py:402
  34.5 4.2 %collective-permute-start.6 = (f32[16,768]{1,0:T(8,128)S(1)}, f32[16,768]{1,0:T(8,128)S(1)}, u32[]{:S(2)}, u32[]{:S(2)}) collective-permute-start(f32[16,768]{1,0:T(8,128)S(1)} %get-tuple-element.36), channel_id=1, source_target_pairs={{0,1},{1,0},{2,3},{3,2},{4,5},{5,4},{6,7},{7,6},{8,9},{9,8},{10,11... | collective-permute-start | bytes 147464 | tf_op jit(solution)/shard_map/ppermute | solution.py:347
  35.0 4.1 %collective-permute-start.7 = (f32[16,768]{1,0:T(8,128)S(1)}, f32[16,768]{1,0:T(8,128)S(1)}, u32[]{:S(2)}, u32[]{:S(2)}) collective-permute-start(f32[16,768]{1,0:T(8,128)S(1)} %get-tuple-element.37), channel_id=1, source_target_pairs={{0,4},{1,5},{2,6},{3,7},{4,0},{5,1},{6,2},{7,3},{8,12},{9,13},{10,... | collective-permute-start | bytes 147464 | tf_op jit(solution)/shard_map/ppermute | solution.py:347
  36.5 5.0 %collective-permute-start.8 = (f32[16,768]{1,0:T(8,128)S(1)}, f32[16,768]{1,0:T(8,128)S(1)}, u32[]{:S(2)}, u32[]{:S(2)}) collective-permute-start(f32[16,768]{1,0:T(8,128)S(1)} %get-tuple-element.38), channel_id=1, source_target_pairs={{0,5},{1,4},{2,7},{3,6},{4,1},{5,0},{6,3},{7,2},{8,13},{9,12},{10,... | collective-permute-start | bytes 147464 | tf_op jit(solution)/shard_map/ppermute | solution.py:347

commit v9 on v8

--- a/solution.py
+++ b/solution.py
@@ -10,7 +10,6 @@
 EPSILON = 1e-05
 LANES = 128
 INNER = 4
-META = 16
 FINE = 16
 MIB = 1024 * 1024
 
@@ -20,6 +19,7 @@
 
 HBM = pl.BlockSpec(memory_space=pltpu.HBM)
 VMEM = pl.BlockSpec(memory_space=pltpu.VMEM)
+AFTER = pl.BlockSpec(memory_space=pl.ANY)
 
 
 def call(kernel, in_specs, out_shape, scratch=(), flops=0, bytes_accessed=0, vmem=24):
@@ -47,48 +47,86 @@
     return lax.rem(inner, 2) * (INNER // 2) + lax.div(inner, 2)
 
 
-def prologue_kernel(tm_count, tpl_hbm, flag_hbm, order_hbm, wave_hbm, *refs):
-    out_ref, send_ref, keep_ref = refs[:3]
-    tpl_pad, flag_ref, order_ref, order_pad, wave_pad, turned, sems = refs[3:]
+def regroup(channels, padded, part, transposed):
+    real = part * channels // padded
+    shape = (channels, padded) if transposed else (padded, channels)
+    channel = lax.broadcasted_iota(jnp.int32, shape, 0 if transposed else 1)
+    place = lax.broadcasted_iota(jnp.int32, shape, 1 if transposed else 0)
+    within = place % part
+    hit = (channel == lax.div(place, part) * real + within) & (within < real)
+    return jnp.where(hit, 1.0, 0.0).astype(BF16)
+
+
+def spare_lanes(part, real):
+    slots = LANES // part * (part - real)
+    slot = lax.broadcasted_iota(jnp.int32, (8, LANES), 0)
+    lane = lax.broadcasted_iota(jnp.int32, (8, LANES), 1)
+    home = lax.div(slot, part - real) * part + real + lax.rem(slot, part - real)
+    return jnp.where((lane == home) & (slot < slots), 1.0, 0.0).astype(BF16)
+
+
+def sample_kernel(part, wave_hbm, send_ref, keep_ref, wave_ref, grouped, sem):
+    copy = pltpu.make_async_copy(wave_hbm, wave_ref, sem)
+    copy.start()
+    padded = grouped.shape[0]
+    order = regroup(wave_ref.shape[0], padded, part, False)
+    copy.wait()
+    grouped[...] = jnp.dot(order, wave_ref[...], preferred_element_type=F32).astype(BF16)
+    core = lax.rem(lax.axis_index("inner"), 2)
+    half = padded // 2
+    keep_ref[...] = grouped[pl.ds(pl.multiple_of(core * half, half), half), :]
+    send_ref[...] = grouped[pl.ds(pl.multiple_of((1 - core) * half, half), half), :]
+
+
+def template_kernel(tm_count, tpl_hbm, flag_hbm, order_hbm, after, out_ref, *scratch):
+    del after
+    tpl_ref, flag_ref, order_ref, turned, sems = scratch
     channels, window = tpl_hbm.shape[1:]
     copies = [
         pltpu.make_async_copy(flag_hbm, flag_ref, sems.at[0]),
         pltpu.make_async_copy(order_hbm, order_ref, sems.at[1]),
-        pltpu.make_async_copy(tpl_hbm.at[0], tpl_pad.at[pl.ds(0, channels)], sems.at[2]),
-        pltpu.make_async_copy(wave_hbm, wave_pad.at[pl.ds(0, channels)], sems.at[3]),
+        pltpu.make_async_copy(tpl_hbm.at[0], tpl_ref, sems.at[2]),
     ]
     for copy in copies:
         copy.start()
     stations = flag_ref.shape[1]
-    padded = tpl_pad.shape[0]
+    padded = turned.shape[1]
     part = LANES // tm_count
-    wave_pad[channels:, :] = jnp.zeros((padded - channels, wave_pad.shape[1]), BF16)
-    tpl_pad[channels:, :] = jnp.zeros((padded - channels, window), BF16)
-    order_pad[...] = jnp.full((1, padded), -1, jnp.int32)
+    rows = out_ref.shape[1]
+    groups = regroup(channels, padded, part, True)
     copies[0].wait()
     copies[1].wait()
-    order_pad[:, :channels] = order_ref[...]
     flags = jnp.broadcast_to(flag_ref[...].astype(F32), (8, stations))
     mask = jnp.dot(
-        flags.astype(BF16), one_hot(order_pad[...], stations), preferred_element_type=F32
-    )
+        flags.astype(BF16), one_hot(order_ref[...], stations), preferred_element_type=F32
+    )
+    live = jnp.sum(mask[:1], keepdims=True)
+    mask = jnp.dot(mask.astype(BF16), groups, preferred_element_type=F32)[:1]
     copies[2].wait()
-    masked = tpl_pad[...].T * mask[:1].astype(BF16)
+    masked = mask * lax.dot_general(
+        tpl_ref[...], groups, (((0,), (0,)), ((), ())), preferred_element_type=F32
+    )
     turned[...] = masked
-    wide = masked.astype(F32)
-    norm = jnp.sqrt(jnp.sum(wide * wide, keepdims=True) + EPSILON)
-    live = jnp.sum(mask[:1], keepdims=True)
-    rest = jnp.broadcast_to(jnp.sqrt(window * live) / norm, (1, LANES))
-    extra = [jnp.zeros((1, LANES), F32)] * META
+    norm = jnp.sqrt(jnp.sum(masked * masked, keepdims=True) + EPSILON)
+    rest = jnp.broadcast_to(jnp.sqrt(window * live) / norm, (1, rows))
+    row = lax.broadcasted_iota(jnp.int32, (1, rows), 1)
+    scale = jnp.zeros((1, rows), F32)
     for piece in range(3):
-        extra[piece] = rest.astype(BF16).astype(F32)
-        rest = rest - extra[piece]
-    wide_flags = jnp.concatenate(
-        [flags[:1], jnp.zeros((1, -stations % LANES), F32)], axis=1
-    )
-    for piece in range(wide_flags.shape[1] // LANES):
-        extra[3 + piece] = wide_flags[:, piece * LANES : (piece + 1) * LANES]
-    extra = jnp.concatenate(extra, axis=0).astype(BF16)
+        now = rest.astype(BF16).astype(F32)
+        scale = jnp.where(row == piece, now, scale)
+        rest = rest - now
+    slots = -(-stations // rows)
+    wide = flags[:1]
+    if stations % rows:
+        wide = jnp.concatenate([wide, jnp.zeros((1, rows - stations % rows), F32)], axis=1)
+    meta = [wide[:, slot * rows : (slot + 1) * rows] for slot in range(slots)] + [scale]
+    meta = jnp.concatenate(meta + [jnp.zeros((8 - len(meta), rows), F32)], axis=0)
+    meta = lax.dot_general(
+        meta.astype(BF16),
+        spare_lanes(part, part * channels // padded),
+        (((0,), (0,)), ((), ())),
+        preferred_element_type=F32,
+    )
     my_tm = lax.axis_index("tm")
     spot = lax.broadcasted_iota(jnp.int32, (FINE, LANES), 1) // part
     for member in range(INNER):
@@ -98,18 +136,13 @@
             tile = jnp.zeros((FINE, LANES), F32)
             for within in range(tm_count):
                 row = FINE * (step * tm_count + within)
-                chunk = turned[row : row + FINE, start : start + LANES].astype(F32)
+                chunk = turned[row : row + FINE, start : start + LANES]
                 turn = lax.rem(part * (within - my_tm) + LANES, LANES)
                 tile = jnp.where(spot == within, pltpu.roll(chunk, turn, 1), tile)
-            pieces.append(tile.astype(BF16))
-        payload = jnp.concatenate(pieces + [extra], axis=0)
+            pieces.append(tile)
+        payload = (jnp.concatenate(pieces, axis=0) + meta).astype(BF16)
         for target in range(member, out_ref.shape[0], INNER):
             out_ref[target] = payload
-    copies[3].wait()
-    core = lax.rem(lax.axis_index("inner"), 2)
-    half = padded // 2
-    keep_ref[...] = wave_pad[pl.ds(pl.multiple_of(core * half, half), half), :]
-    send_ref[...] = wave_pad[pl.ds(pl.multiple_of((1 - core) * half, half), half), :]
 
 
 def split_kernel(tm_count, keep_ref, got_ref, *outs):
@@ -251,21 +284,31 @@
 
 
 def power_kernel(stations, window, tm_count, wave_ref, tpls_ref, order_ref, *refs):
-    out_ref, scale_ref, mask_ref, order_pad = refs
-    extra = tpls_ref[:, tpls_ref.shape[1] - META :, :].astype(F32)
-    scale_ref[...] = extra[:, 0, :] + extra[:, 1, :] + extra[:, 2, :]
-    tiles = -(-stations // LANES)
-    flags = jnp.concatenate([extra[:, 3 + tile, :] for tile in range(tiles)], axis=1)
+    out_ref, scale_ref, mask_ref = refs
+    count, rows, _ = tpls_ref.shape
     channels = wave_ref.shape[0]
-    padded = order_pad.shape[1]
-    order_pad[...] = jnp.full((1, padded), -1, jnp.int32)
-    order_pad[:, :channels] = order_ref[...]
+    padded = INNER * LANES
+    part = LANES // tm_count
+    meta = lax.dot_general(
+        spare_lanes(part, part * channels // padded),
+        tpls_ref[...].reshape(count * rows, LANES),
+        (((1,), (1,)), ((), ())),
+        preferred_element_type=F32,
+    )
+    slots = -(-stations // rows)
+
+    def read(slot):
+        return jnp.concatenate(
+            [meta[slot : slot + 1, t * rows : (t + 1) * rows] for t in range(count)], axis=0
+        )
+
+    scale = jnp.sum(read(slots)[:, :3], axis=1, keepdims=True)
+    scale_ref[...] = jnp.broadcast_to(scale, scale_ref.shape)
+    flags = jnp.concatenate([read(slot) for slot in range(slots)], axis=1)[:, :stations]
     mask = jnp.dot(
-        flags.astype(BF16),
-        one_hot(order_pad[...], tiles * LANES),
-        preferred_element_type=F32,
-    )
-    power = masked_squares(mask[:, :channels].astype(BF16), wave_ref[...])
+        flags.astype(BF16), one_hot(order_ref[...], stations), preferred_element_type=F32
+    ).astype(BF16)
+    power = masked_squares(mask, wave_ref[...])
     columns = power.shape[1]
     column = lax.broadcasted_iota(jnp.int32, power.shape, 1)
     reach = 1
@@ -274,7 +317,9 @@
         power = power + jnp.where(column < columns - reach, later, 0.0)
         reach *= 2
     out_ref[...] = power
-    part = LANES // tm_count
+    mask = jnp.dot(
+        mask, regroup(channels, padded, part, True), preferred_element_type=F32
+    )
     mine = side_major(lax.axis_index("inner")) * LANES + lax.axis_index("tm") * part
     mask_ref[...] = pltpu.roll(mask, lax.rem(padded - mine, padded), 1)[:, :part].astype(BF16)
 
@@ -310,26 +355,32 @@
     sds = jax.ShapeDtypeStruct
     order_row = channel_order[None, :]
 
-    payload, send, keep = call(
-        functools.partial(prologue_kernel, tm_count),
-        [HBM] * 4,
+    send, keep = call(
+        functools.partial(sample_kernel, part),
+        [HBM],
+        [sds((padded // 2, slab), BF16)] * 2,
         [
-            sds((blk_count, window * part // LANES + META, LANES), BF16),
-            sds((padded // 2, slab), BF16),
-            sds((padded // 2, slab), BF16),
+            pltpu.VMEM((channels, slab), BF16),
+            pltpu.VMEM((padded, slab), BF16),
+            pltpu.SemaphoreType.DMA,
         ],
+        bytes_accessed=channels * slab * 2,
+        vmem=60,
+    )(waveforms)
+    payload = call(
+        functools.partial(template_kernel, tm_count),
+        [HBM] * 3 + [AFTER],
+        sds((blk_count, window * part // LANES, LANES), BF16),
         [
-            pltpu.VMEM((padded, window), BF16),
+            pltpu.VMEM((channels, window), BF16),
             pltpu.VMEM((1, stations), jnp.int32),
             pltpu.VMEM((1, channels), jnp.int32),
-            pltpu.VMEM((1, padded), jnp.int32),
-            pltpu.VMEM((padded, slab), BF16),
-            pltpu.VMEM((window, padded), BF16),
-            pltpu.SemaphoreType.DMA((4,)),
+            pltpu.VMEM((window, padded), F32),
+            pltpu.SemaphoreType.DMA((3,)),
         ],
-        bytes_accessed=channels * (window + slab) * 2,
+        bytes_accessed=channels * window * 2,
         vmem=60,
-    )(templates, station_mask, order_row, waveforms)
+    )(templates, station_mask, order_row, keep)
     tpls = lax.all_to_all(payload, blk, 0, 0, tiled=True)
 
     got = lax.ppermute(send, "inner", [(b, b ^ 1) for b in range(INNER)])
@@ -363,7 +414,6 @@
             sds((blk_count, LANES), F32),
             sds((blk_count, part), BF16),
         ],
-        [pltpu.VMEM((1, padded), jnp.int32)],
         flops=4 * blk_count * channels * slab,
         bytes_accessed=channels * slab * 2,
     )(waveforms, tpls, order_row)

time: 42.4 us -> 45 us (1.061)
  Pallas kernels: 9.33 us -> 12 us
    pallas_call x1 -> x2, Pallas kernels: 2.4 us -> 4.92 us  [the longest x1 2.61 us: on_device(): call(functools.partial(template_kernel, tm_count), [HBM] * 3 + [AFTER], s...]
    ppermute x1, waiting for transfers between devices: 1.3 us -> 0.6 us  [on_device(): lax.ppermute(head, 'outer', [(b, b - 1) for b in range(1, outer_count)])]
    ppermute x6, waiting for transfers between devices: 12.3 us -> 12.9 us  [swap(): return lax.ppermute(part, every, route)]
where the time goes in v9:
time: 45 us; the launch traced here: 44.7 us
  starting transfers between devices  16.5 us (37%)
  waiting for transfers between devices  16.1 us (36%)
  Pallas kernels  12 us (27%)
    ppermute x6, waiting for transfers between devices, swap(): return lax.ppermute(part, every, route)  12.9 us
    all_to_all x1, starting transfers between devices, on_device(): tpls = lax.all_to_all(payload, blk, 0, 0, tiled=True)  7.53 us
    ppermute x6, starting transfers between devices, swap(): return lax.ppermute(part, every, route)  7.12 us
    pallas_call x1, Pallas kernels, on_device(): call(first_dots_kernel, [VMEM] * 2, sds((2 * (blocks - 1), blk_count, sla...  3.31 us
    pallas_call x1, Pallas kernels, on_device(): call(functools.partial(template_kernel, tm_count), [HBM] * 3 + [AFTER], s...  2.61 us
    ppermute x2, waiting for transfers between devices, on_device(): got = lax.ppermute(send, 'inner', [(b, b ^ 1) for b in range(INNER)])  2.59 us
    pallas_call x1, Pallas kernels, on_device(): call(functools.partial(sample_kernel, part), [HBM], [sds((padded // 2, sl...  2.31 us
    pallas_call x1, Pallas kernels, on_device(): call(last_dots_kernel, [VMEM] * 5, [sds((half, blk_count, slab + window),...  1.86 us
  transfers between devices with their start and end apart: 10, of which 8 were waited for; matrix products, arithmetic and copies ran while one was open for 0% of the time, Pallas kernels for 10%

profile of v9, /device:TPU:0, one launch (start us, length us, event | category | flops | bytes accessed | tf_op | source)
XLA Modules:
  0.0 44.7 jit_solution(3888208375629923808)
XLA Ops:
  0.0 2.3 %shard_map.46 = (bf16[256,512]{1,0:T(8,128)(2,1)}, bf16[256,512]{1,0:T(8,128)(2,1)}) custom-call(bf16[480,512]{1,0:T(8,128)(2,1)} %wave_ref.1), custom_call_target="tpu_custom_call" | custom-call | bytes 491520 | tf_op jit(solution)/shard_map/pallas_call | solution.py:358
  2.3 2.6 %shard_map.47 = bf16[16,128,128]{2,1,0:T(8,128)(2,1)} custom-call(bf16[1,480,256]{2,1,0:T(8,128)(2,1)} %tpl_hbm.1, s32[1,160]{1,0:T(1,128)} %flag_hbm.1, s32[1,480]{1,0:T(1,128)} %bitcast.1, bf16[256,512]{1,0:T(8,128)(2,1)} %get-tuple-element.22.after.keep_ref), custom_call_target="tpu_custom_call" | custom-call | bytes 245760 | tf_op jit(solution)/shard_map/pallas_call | solution.py:370
  5.0 7.5 %all-to-all-start = ((bf16[16,128,128]{2,1,0:T(8,128)(2,1)}), bf16[16,128,128]{2,1,0:T(8,128)(2,1)S(1)}, u32[]{:S(2)}, u32[]{:S(2)}) async-start(bf16[16,128,128]{2,1,0:T(8,128)(2,1)} %shard_map.47), calls=%async_computation | async-start | bytes 1048576 | tf_op jit(solution)/shard_map/all_to_all | solution.py:384
  12.5 0.5 %collective-permute-start = (bf16[256,512]{1,0:T(8,128)(2,1)S(1)}, bf16[256,512]{1,0:T(8,128)(2,1)S(1)}, u32[]{:S(2)}, u32[]{:S(2)}) collective-permute-start(bf16[256,512]{1,0:T(8,128)(2,1)S(1)} %copy-done.3), channel_id=1, source_target_pairs={{0,2},{2,0},{4,6},{6,4},{1,3},{3,1},{5,7},{7,5},{8,10},{10,8},{12,... | collective-permute-start | bytes 786440 | tf_op jit(solution)/shard_map/ppermute | solution.py:386
  13.0 1.2 %collective-permute-done.got_ref = bf16[256,512]{1,0:T(8,128)(2,1)S(1)} collective-permute-done((bf16[256,512]{1,0:T(8,128)(2,1)S(1)}, bf16[256,512]{1,0:T(8,128)(2,1)S(1)}, u32[]{:S(2)}, u32[]{:S(2)}) %collective-permute-start) | collective-permute-done | bytes 262176 | tf_op jit(solution)/shard_map/ppermute | solution.py:386
  14.2 1.6 %collective-permute-start.1 = (bf16[2,64,512]{2,1,0:T(8,128)(2,1)S(1)}, bf16[2,64,512]{2,1,0:T(8,128)(2,1)S(1)}, u32[]{:S(2)}, u32[]{:S(2)}) collective-permute-start(bf16[2,64,512]{2,1,0:T(8,128)(2,1)S(1)} %get-tuple-element.25), channel_id=1, source_target_pairs={{0,1},{1,0},{2,3},{3,2},{4,5},{5,4},{6,7},{7,6},{8,9},{9,8},{10,11... | collective-permute-start | bytes 393224 | tf_op jit(solution)/shard_map/ppermute | solution.py:398
  15.7 1.9 %collective-permute-start.2 = (bf16[2,64,512]{2,1,0:T(8,128)(2,1)S(1)}, bf16[2,64,512]{2,1,0:T(8,128)(2,1)S(1)}, u32[]{:S(2)}, u32[]{:S(2)}) collective-permute-start(bf16[2,64,512]{2,1,0:T(8,128)(2,1)S(1)} %get-tuple-element.26), channel_id=1, source_target_pairs={{0,4},{1,5},{2,6},{3,7},{4,0},{5,1},{6,2},{7,3},{8,12},{9,13},{10,... | collective-permute-start | bytes 393224 | tf_op jit(solution)/shard_map/ppermute | solution.py:398
  17.6 0.1 collective-permute-start.3
  17.7 2.6 %collective-permute-done.1.refs_1_ = bf16[2,64,512]{2,1,0:T(8,128)(2,1)S(1)} collective-permute-done((bf16[2,64,512]{2,1,0:T(8,128)(2,1)S(1)}, bf16[2,64,512]{2,1,0:T(8,128)(2,1)S(1)}, u32[]{:S(2)}, u32[]{:S(2)}) %collective-permute-start.1) | collective-permute-done | bytes 131104 | tf_op jit(solution)/shard_map/ppermute | solution.py:398
  20.4 6.6 %collective-permute-done.2.refs_2_ = bf16[2,64,512]{2,1,0:T(8,128)(2,1)S(1)} collective-permute-done((bf16[2,64,512]{2,1,0:T(8,128)(2,1)S(1)}, bf16[2,64,512]{2,1,0:T(8,128)(2,1)S(1)}, u32[]{:S(2)}, u32[]{:S(2)}) %collective-permute-start.2) | collective-permute-done | bytes 131104 | tf_op jit(solution)/shard_map/ppermute | solution.py:398
  27.0 1.3 %collective-permute-start.4 = (bf16[64,256]{1,0:T(8,128)(2,1)S(1)}, bf16[64,256]{1,0:T(8,128)(2,1)S(1)}, u32[]{:S(2)}, u32[]{:S(2)}) collective-permute-start(bf16[64,256]{1,0:T(8,128)(2,1)S(1)} %get-tuple-element.29), channel_id=1, source_target_pairs={{8,0},{16,8},{24,16},{9,1},{17,9},{25,17},{10,2},{18,10},{26,18},{... | collective-permute-start | bytes 98312 | tf_op jit(solution)/shard_map/ppermute | solution.py:407
  28.3 3.3 %shard_map.51.done_ref = f32[6,16,512]{2,1,0:T(8,128)S(1)} custom-call(bf16[16,128,128]{2,1,0:T(8,128)(2,1)S(1)} %all-to-all-done.tpls_ref.tpls, bf16[64,4096]{1,0:T(8,128)(2,1)S(1)} %get-tuple-element.28.samples_ref), custom_call_target="tpu_custom_call" | custom-call | flops 1610612736 | bytes 524288 | tf_op jit(solution)/shard_map/pallas_call | solution.py:432
  31.7 1.1 %shard_map.50 = (f32[16,512]{1,0:T(8,128)S(1)}, f32[16,128]{1,0:T(8,128)S(1)}, bf16[16,64]{1,0:T(8,128)(2,1)S(1)}) custom-call(bf16[480,512]{1,0:T(8,128)(2,1)S(1)} %copy-done, bf16[16,128,128]{2,1,0:T(8,128)(2,1)S(1)} %all-to-all-done.tpls_ref.tpls, s32[1,480]{1,0:T(1,128)S(1)} %bitcast.2), custom_call_target="tpu_custom_call" | custom-call | flops 15728640 | bytes 491520 | tf_op jit(solution)/shard_map/pallas_call | solution.py:409
  32.8 0.6 %collective-permute-done.4.halo_ref = bf16[64,256]{1,0:T(8,128)(2,1)S(1)} collective-permute-done((bf16[64,256]{1,0:T(8,128)(2,1)S(1)}, bf16[64,256]{1,0:T(8,128)(2,1)S(1)}, u32[]{:S(2)}, u32[]{:S(2)}) %collective-permute-start.4) | collective-permute-done | bytes 32800 | tf_op jit(solution)/shard_map/ppermute | solution.py:407
  33.4 1.9 %shard_map.52 = (f32[4,16,768]{2,1,0:T(8,128)S(1)}, f32[4,16,768]{2,1,0:T(8,128)S(1)}) custom-call(bf16[16,128,128]{2,1,0:T(8,128)(2,1)S(1)} %all-to-all-done.tpls_ref.tpls, bf16[64,4096]{1,0:T(8,128)(2,1)S(1)} %get-tuple-element.28.samples_ref, bf16[64,256]{1,0:T(8,128)(2,1)S(1)} %collective-permute-done.4.halo_ref, ...), custom_call_target="tpu_custom_call" | custom-call | flops 536870912 | bytes 524288 | tf_op jit(solution)/shard_map/pallas_call | solution.py:440
  35.2 0.1 collective-permute-start.5
  35.3 1.4 %collective-permute-done.5.got_ref = f32[4,16,768]{2,1,0:T(8,128)S(1)} collective-permute-done((f32[4,16,768]{2,1,0:T(8,128)S(1)}, f32[4,16,768]{2,1,0:T(8,128)S(1)}, u32[]{:S(2)}, u32[]{:S(2)}) %collective-permute-start.5) | collective-permute-done | bytes 196640 | tf_op jit(solution)/shard_map/ppermute | solution.py:452
  36.8 0.9 %collective-permute-start.6 = (f32[16,768]{1,0:T(8,128)S(1)}, f32[16,768]{1,0:T(8,128)S(1)}, u32[]{:S(2)}, u32[]{:S(2)}) collective-permute-start(f32[16,768]{1,0:T(8,128)S(1)} %get-tuple-element.34), channel_id=1, source_target_pairs={{0,1},{1,0},{2,3},{3,2},{4,5},{5,4},{6,7},{7,6},{8,9},{9,8},{10,11... | collective-permute-start | bytes 147464 | tf_op jit(solution)/shard_map/ppermute | solution.py:398
  37.7 1.3 %collective-permute-start.7 = (f32[16,768]{1,0:T(8,128)S(1)}, f32[16,768]{1,0:T(8,128)S(1)}, u32[]{:S(2)}, u32[]{:S(2)}) collective-permute-start(f32[16,768]{1,0:T(8,128)S(1)} %get-tuple-element.35), channel_id=1, source_target_pairs={{0,4},{1,5},{2,6},{3,7},{4,0},{5,1},{6,2},{7,3},{8,12},{9,13},{10,... | collective-permute-start | bytes 147464 | tf_op jit(solution)/shard_map/ppermute | solution.py:398
  39.0 1.3 %collective-permute-start.8 = (f32[16,768]{1,0:T(8,128)S(1)}, f32[16,768]{1,0:T(8,128)S(1)}, u32[]{:S(2)}, u32[]{:S(2)}) collective-permute-start(f32[16,768]{1,0:T(8,128)S(1)} %get-tuple-element.36), channel_id=1, source_target_pairs={{0,5},{1,4},{2,7},{3,6},{4,1},{5,0},{6,3},{7,2},{8,13},{9,12},{10,... | collective-permute-start | bytes 147464 | tf_op jit(solution)/shard_map/ppermute | solution.py:398
  40.3 0.6 %collective-permute-done.6.refs_1_ = f32[16,768]{1,0:T(8,128)S(1)} collective-permute-done((f32[16,768]{1,0:T(8,128)S(1)}, f32[16,768]{1,0:T(8,128)S(1)}, u32[]{:S(2)}, u32[]{:S(2)}) %collective-permute-start.6) | collective-permute-done | bytes 49184 | tf_op jit(solution)/shard_map/ppermute | solution.py:398
  40.9 0.9 %collective-permute-done.7.refs_2_ = f32[16,768]{1,0:T(8,128)S(1)} collective-permute-done((f32[16,768]{1,0:T(8,128)S(1)}, f32[16,768]{1,0:T(8,128)S(1)}, u32[]{:S(2)}, u32[]{:S(2)}) %collective-permute-start.7) | collective-permute-done | bytes 49184 | tf_op jit(solution)/shard_map/ppermute | solution.py:398
  41.8 2.2 %collective-permute-done.8.refs_3_ = f32[16,768]{1,0:T(8,128)S(1)} collective-permute-done((f32[16,768]{1,0:T(8,128)S(1)}, f32[16,768]{1,0:T(8,128)S(1)}, u32[]{:S(2)}, u32[]{:S(2)}) %collective-permute-start.8) | collective-permute-done | bytes 49184 | tf_op jit(solution)/shard_map/ppermute | solution.py:398
  44.0 0.7 %shard_map.54 = f32[16,512]{1,0:T(8,128)} custom-call(f32[16,768]{1,0:T(8,128)S(1)} %get-tuple-element.33.refs_0_, f32[16,768]{1,0:T(8,128)S(1)} %collective-permute-done.6.refs_1_, f32[16,768]{1,0:T(8,128)S(1)} %collective-permute-done.7.refs_2_, f32[16,768]{1,0:T(8,128)S(1)} %collective-permute-done.8.refs_3_, f32[16,512]{1,0:T(8,128)S(1)} %get-tuple-element.37.refs_4_, ...), custom_call_target="tpu_custom_call" | custom-call | bytes 196608 | tf_op jit(solution)/shard_map/pallas_call | solution.py:460
  (13 shorter events, 0.1 us)
Async XLA Ops:
  4.9 7.6 %copy-start.3 = (bf16[256,512]{1,0:T(8,128)(2,1)S(1)}, bf16[256,512]{1,0:T(8,128)(2,1)}, u32[]{:S(2)}) copy-start(bf16[256,512]{1,0:T(8,128)(2,1)} %get-tuple-element.23) | copy-start | bytes 786436
  4.9 9.2 %copy-start.1 = (bf16[256,512]{1,0:T(8,128)(2,1)S(1)}, bf16[256,512]{1,0:T(8,128)(2,1)}, u32[]{:S(2)}) copy-start(bf16[256,512]{1,0:T(8,128)(2,1)} %get-tuple-element.22.after.keep_ref) | copy-start | bytes 786436
  5.0 23.4 %all-to-all-start = ((bf16[16,128,128]{2,1,0:T(8,128)(2,1)}), bf16[16,128,128]{2,1,0:T(8,128)(2,1)S(1)}, u32[]{:S(2)}, u32[]{:S(2)}) async-start(bf16[16,128,128]{2,1,0:T(8,128)(2,1)} %shard_map.47), calls=%async_computation | async-start | bytes 1048576 | tf_op jit(solution)/shard_map/all_to_all | solution.py:384
  12.5 1.6 %collective-permute-start = (bf16[256,512]{1,0:T(8,128)(2,1)S(1)}, bf16[256,512]{1,0:T(8,128)(2,1)S(1)}, u32[]{:S(2)}, u32[]{:S(2)}) collective-permute-start(bf16[256,512]{1,0:T(8,128)(2,1)S(1)} %copy-done.3), channel_id=1, source_target_pairs={{0,2},{2,0},{4,6},{6,4},{1,3},{3,1},{5,7},{7,5},{8,10},{10,8},{12,... | collective-permute-start | bytes 786440 | tf_op jit(solution)/shard_map/ppermute | solution.py:386
  14.2 6.2 %collective-permute-start.1 = (bf16[2,64,512]{2,1,0:T(8,128)(2,1)S(1)}, bf16[2,64,512]{2,1,0:T(8,128)(2,1)S(1)}, u32[]{:S(2)}, u32[]{:S(2)}) collective-permute-start(bf16[2,64,512]{2,1,0:T(8,128)(2,1)S(1)} %get-tuple-element.25), channel_id=1, source_target_pairs={{0,1},{1,0},{2,3},{3,2},{4,5},{5,4},{6,7},{7,6},{8,9},{9,8},{10,11... | collective-permute-start | bytes 393224 | tf_op jit(solution)/shard_map/ppermute | solution.py:398
  15.7 11.2 %collective-permute-start.2 = (bf16[2,64,512]{2,1,0:T(8,128)(2,1)S(1)}, bf16[2,64,512]{2,1,0:T(8,128)(2,1)S(1)}, u32[]{:S(2)}, u32[]{:S(2)}) collective-permute-start(bf16[2,64,512]{2,1,0:T(8,128)(2,1)S(1)} %get-tuple-element.26), channel_id=1, source_target_pairs={{0,4},{1,5},{2,6},{3,7},{4,0},{5,1},{6,2},{7,3},{8,12},{9,13},{10,... | collective-permute-start | bytes 393224 | tf_op jit(solution)/shard_map/ppermute | solution.py:398
  17.6 9.3 %collective-permute-start.3 = (bf16[2,64,512]{2,1,0:T(8,128)(2,1)S(1)}, bf16[2,64,512]{2,1,0:T(8,128)(2,1)S(1)}, u32[]{:S(2)}, u32[]{:S(2)}) collective-permute-start(bf16[2,64,512]{2,1,0:T(8,128)(2,1)S(1)} %get-tuple-element.27), channel_id=1, source_target_pairs={{0,5},{1,4},{2,7},{3,6},{4,1},{5,0},{6,3},{7,2},{8,13},{9,12},{10,... | collective-permute-start | bytes 393224 | tf_op jit(solution)/shard_map/ppermute | solution.py:398
  27.0 6.4 %collective-permute-start.4 = (bf16[64,256]{1,0:T(8,128)(2,1)S(1)}, bf16[64,256]{1,0:T(8,128)(2,1)S(1)}, u32[]{:S(2)}, u32[]{:S(2)}) collective-permute-start(bf16[64,256]{1,0:T(8,128)(2,1)S(1)} %get-tuple-element.29), channel_id=1, source_target_pairs={{8,0},{16,8},{24,16},{9,1},{17,9},{25,17},{10,2},{18,10},{26,18},{... | collective-permute-start | bytes 98312 | tf_op jit(solution)/shard_map/ppermute | solution.py:407
  28.3 3.3 %copy-start = (bf16[480,512]{1,0:T(8,128)(2,1)S(1)}, bf16[480,512]{1,0:T(8,128)(2,1)}, u32[]{:S(2)}) copy-start(bf16[480,512]{1,0:T(8,128)(2,1)} %wave_ref.1) | copy-start | bytes 1474564
  28.3 3.3 %copy-start.2 = (s32[480]{0:T(512)S(1)}, s32[480]{0:T(512)}, u32[]{:S(2)}) copy-start(s32[480]{0:T(512)} %param.7) | copy-start | bytes 5764
  35.2 1.5 %collective-permute-start.5 = (f32[4,16,768]{2,1,0:T(8,128)S(1)}, f32[4,16,768]{2,1,0:T(8,128)S(1)}, u32[]{:S(2)}, u32[]{:S(2)}) collective-permute-start(f32[4,16,768]{2,1,0:T(8,128)S(1)} %get-tuple-element.32), channel_id=1, source_target_pairs={{0,2},{2,0},{4,6},{6,4},{1,3},{3,1},{5,7},{7,5},{8,10},{10,8},{12,... | collective-permute-start | bytes 589832 | tf_op jit(solution)/shard_map/ppermute | solution.py:452
  36.8 4.2 %collective-permute-start.6 = (f32[16,768]{1,0:T(8,128)S(1)}, f32[16,768]{1,0:T(8,128)S(1)}, u32[]{:S(2)}, u32[]{:S(2)}) collective-permute-start(f32[16,768]{1,0:T(8,128)S(1)} %get-tuple-element.34), channel_id=1, source_target_pairs={{0,1},{1,0},{2,3},{3,2},{4,5},{5,4},{6,7},{7,6},{8,9},{9,8},{10,11... | collective-permute-start | bytes 147464 | tf_op jit(solution)/shard_map/ppermute | solution.py:398
  37.7 4.1 %collective-permute-start.7 = (f32[16,768]{1,0:T(8,128)S(1)}, f32[16,768]{1,0:T(8,128)S(1)}, u32[]{:S(2)}, u32[]{:S(2)}) collective-permute-start(f32[16,768]{1,0:T(8,128)S(1)} %get-tuple-element.35), channel_id=1, source_target_pairs={{0,4},{1,5},{2,6},{3,7},{4,0},{5,1},{6,2},{7,3},{8,12},{9,13},{10,... | collective-permute-start | bytes 147464 | tf_op jit(solution)/shard_map/ppermute | solution.py:398
  39.0 5.0 %collective-permute-start.8 = (f32[16,768]{1,0:T(8,128)S(1)}, f32[16,768]{1,0:T(8,128)S(1)}, u32[]{:S(2)}, u32[]{:S(2)}) collective-permute-start(f32[16,768]{1,0:T(8,128)S(1)} %get-tuple-element.36), channel_id=1, source_target_pairs={{0,5},{1,4},{2,7},{3,6},{4,1},{5,0},{6,3},{7,2},{8,13},{9,12},{10,... | collective-permute-start | bytes 147464 | tf_op jit(solution)/shard_map/ppermute | solution.py:398

commit v10 on v9

--- a/solution.py
+++ b/solution.py
@@ -65,35 +65,24 @@
     return jnp.where((lane == home) & (slot < slots), 1.0, 0.0).astype(BF16)
 
 
-def sample_kernel(part, wave_hbm, send_ref, keep_ref, wave_ref, grouped, sem):
-    copy = pltpu.make_async_copy(wave_hbm, wave_ref, sem)
-    copy.start()
-    padded = grouped.shape[0]
-    order = regroup(wave_ref.shape[0], padded, part, False)
-    copy.wait()
-    grouped[...] = jnp.dot(order, wave_ref[...], preferred_element_type=F32).astype(BF16)
-    core = lax.rem(lax.axis_index("inner"), 2)
-    half = padded // 2
-    keep_ref[...] = grouped[pl.ds(pl.multiple_of(core * half, half), half), :]
-    send_ref[...] = grouped[pl.ds(pl.multiple_of((1 - core) * half, half), half), :]
-
-
-def template_kernel(tm_count, tpl_hbm, flag_hbm, order_hbm, after, out_ref, *scratch):
-    del after
-    tpl_ref, flag_ref, order_ref, turned, sems = scratch
+def prologue_kernel(tm_count, wave_hbm, tpl_hbm, flag_hbm, order_hbm, *refs):
+    send_ref, samples_ref, tpls_ref = refs[:3]
+    wave_ref, grouped, tpl_ref, flag_ref, order_ref, turned, sems = refs[3:]
     channels, window = tpl_hbm.shape[1:]
     copies = [
         pltpu.make_async_copy(flag_hbm, flag_ref, sems.at[0]),
         pltpu.make_async_copy(order_hbm, order_ref, sems.at[1]),
         pltpu.make_async_copy(tpl_hbm.at[0], tpl_ref, sems.at[2]),
+        pltpu.make_async_copy(wave_hbm, wave_ref, sems.at[3]),
     ]
     for copy in copies:
         copy.start()
     stations = flag_ref.shape[1]
     padded = turned.shape[1]
     part = LANES // tm_count
-    rows = out_ref.shape[1]
+    rows = tpls_ref.shape[1]
     groups = regroup(channels, padded, part, True)
+    order = regroup(channels, padded, part, False)
     copies[0].wait()
     copies[1].wait()
     flags = jnp.broadcast_to(flag_ref[...].astype(F32), (8, stations))
@@ -128,6 +117,8 @@
         preferred_element_type=F32,
     )
     my_tm = lax.axis_index("tm")
+    my_core = lax.rem(lax.axis_index("inner"), 2)
+    first = send_ref.shape[0] - 2 * rows
     spot = lax.broadcasted_iota(jnp.int32, (FINE, LANES), 1) // part
     for member in range(INNER):
         start = (member % 2 * (INNER // 2) + member // 2) * LANES
@@ -141,8 +132,49 @@
                 tile = jnp.where(spot == within, pltpu.roll(chunk, turn, 1), tile)
             pieces.append(tile)
         payload = (jnp.concatenate(pieces, axis=0) + meta).astype(BF16)
-        for target in range(member, out_ref.shape[0], INNER):
-            out_ref[target] = payload
+        y, core = member // 2, member % 2
+
+        @pl.when(core == my_core)
+        def _():
+            tpls_ref[y] = payload
+
+        @pl.when(core != my_core)
+        def _():
+            send_ref[first + y * rows : first + (y + 1) * rows, :] = payload
+
+    copies[3].wait()
+    grouped[...] = jnp.dot(order, wave_ref[...], preferred_element_type=F32).astype(BF16)
+    half = padded // 2
+    samples_ref[...] = grouped[pl.ds(pl.multiple_of(my_core * half, half), half), :]
+    theirs = pl.ds(pl.multiple_of((1 - my_core) * half, half), half)
+    for tile in range(first // half):
+        columns = slice(tile * LANES, (tile + 1) * LANES)
+        send_ref[tile * half : (tile + 1) * half, :] = grouped[theirs, columns]
+
+
+def plane_kernel(tpls_ref, got_ref, keep_ref, send_ref):
+    y, core = lax.div(lax.axis_index("inner"), 2), lax.rem(lax.axis_index("inner"), 2)
+    rows = tpls_ref.shape[1]
+    first = got_ref.shape[0] - 2 * rows
+    for side in range(2):
+        got = got_ref[first + side * rows : first + (side + 1) * rows, :]
+
+        @pl.when(side == y)
+        def _():
+            keep_ref[core] = tpls_ref[side]
+            keep_ref[1 - core] = got
+
+        @pl.when(side != y)
+        def _():
+            send_ref[core] = tpls_ref[side]
+            send_ref[1 - core] = got
+
+
+def pack_kernel(keep_ref, got_ref, out_ref):
+    y = lax.div(lax.axis_index("inner"), 2)
+    for core in range(2):
+        out_ref[2 * y + core] = keep_ref[core]
+        out_ref[2 * (1 - y) + core] = got_ref[core]
 
 
 def split_kernel(tm_count, keep_ref, got_ref, *outs):
@@ -150,10 +182,13 @@
     core = lax.rem(my_inner, 2)
     me = lax.div(my_inner, 2) * tm_count + lax.axis_index("tm")
     part = outs[0].shape[1]
+    half, slab = keep_ref.shape
     for flip, out_ref in enumerate(outs):
-        rows = pl.ds(pl.multiple_of((me ^ flip) * part, part), part)
-        out_ref[core] = keep_ref[rows, :]
-        out_ref[1 - core] = got_ref[rows, :]
+        start = (me ^ flip) * part
+        out_ref[core] = keep_ref[pl.ds(pl.multiple_of(start, part), part), :]
+        for tile in range(slab // LANES):
+            rows = pl.ds(pl.multiple_of(tile * half + start, part), part)
+            out_ref[1 - core, :, tile * LANES : (tile + 1) * LANES] = got_ref[rows, :]
 
 
 def join_kernel(tm_count, *refs):
@@ -169,6 +204,11 @@
     head_ref[...] = out_ref[:, : head_ref.shape[1]]
 
 
+def arrival(template):
+    outer = lax.div(template, INNER) ^ lax.axis_index("outer")
+    return outer * INNER + lax.rem(template, INNER)
+
+
 def correlate(tpls, samples, out_ref, first, left, shifts, products):
     slab = out_ref.shape[2]
     part, columns = samples.shape
@@ -179,15 +219,18 @@
         tile, turn = copy // copies * LANES, copy % copies * FINE
         turned = samples if turn == 0 else pltpu.roll(samples, columns - turn, 1)
         shifts[copy * part : (copy + 1) * part, :] = turned[:, tile : tile + usable + LANES]
-    count = tpls.shape[0]
+    count = len(tpls) * INNER
     row = lax.broadcasted_iota(jnp.int32, (size, size), 0)
     column = lax.broadcasted_iota(jnp.int32, (size, size), 1)
-    source = lax.rem(row, count) * FINE + lax.div(row, count)
+    source = arrival(lax.rem(row, count)) * FINE + lax.div(row, count)
     order = jnp.where(column == source, 1.0, 0.0).astype(BF16)
     for step in range(depth // LANES):
-        rows = tpls[:, FINE * step : FINE * (step + 1), :].reshape(size, LANES)
+        rows = [
+            pack[:, FINE * step : FINE * (step + 1), :].reshape(INNER * FINE, LANES)
+            for pack in tpls
+        ]
         left[:, step * LANES : (step + 1) * LANES] = jnp.dot(
-            order, rows, preferred_element_type=F32
+            order, jnp.concatenate(rows, axis=0), preferred_element_type=F32
         ).astype(BF16)
     tiles = products.shape[2] // LANES
     span = (tiles - 1) * LANES
@@ -231,14 +274,15 @@
     gather(blocks - 1, (blocks - 1) % 2)
 
 
-def first_dots_kernel(tpls, samples_ref, out_ref, left, shifts, products):
+def first_dots_kernel(*refs):
+    tpls, (samples_ref, out_ref, left, shifts, products) = refs[:-5], refs[-5:]
     columns = shifts.shape[1] + LANES
     correlate(tpls, samples_ref[:, :columns], out_ref, 0, left, shifts, products)
 
 
-def last_dots_kernel(tpls, samples_ref, halo_ref, mask_ref, done_ref, *refs):
-    keep_ref, send_ref, out_ref, edges = refs[:4]
-    scratch = refs[4:]
+def last_dots_kernel(*refs):
+    tpls, (samples_ref, halo_ref, mask_ref, done_ref) = refs[:-11], refs[-11:-7]
+    (keep_ref, send_ref), (out_ref, edges, *scratch) = refs[-7:-5], refs[-5:]
     first, slab = done_ref.shape[0], done_ref.shape[2]
     group = edges.shape[0]
     window = halo_ref.shape[1]
@@ -283,18 +327,21 @@
     )
 
 
-def power_kernel(stations, window, tm_count, wave_ref, tpls_ref, order_ref, *refs):
-    out_ref, scale_ref, mask_ref = refs
-    count, rows, _ = tpls_ref.shape
-    channels = wave_ref.shape[0]
+def mask_kernel(stations, channels, tm_count, *refs):
+    tpls, (order_ref, scale_ref, mask_ref, part_ref) = refs[:-4], refs[-4:]
+    rows = tpls[0].shape[1]
+    count = len(tpls) * INNER
     padded = INNER * LANES
     part = LANES // tm_count
     meta = lax.dot_general(
         spare_lanes(part, part * channels // padded),
-        tpls_ref[...].reshape(count * rows, LANES),
+        jnp.concatenate([pack[...].reshape(INNER * rows, LANES) for pack in tpls], axis=0),
         (((1,), (1,)), ((), ())),
         preferred_element_type=F32,
     )
+    template = lax.broadcasted_iota(jnp.int32, (count, count), 0)
+    place = lax.broadcasted_iota(jnp.int32, (count, count), 1)
+    sort = jnp.where(place == arrival(template), 1.0, 0.0).astype(BF16)
     slots = -(-stations // rows)
 
     def read(slot):
@@ -302,13 +349,25 @@
             [meta[slot : slot + 1, t * rows : (t + 1) * rows] for t in range(count)], axis=0
         )
 
-    scale = jnp.sum(read(slots)[:, :3], axis=1, keepdims=True)
+    values = jnp.concatenate([read(slot) for slot in range(slots + 1)], axis=1)
+    values = jnp.dot(sort, values.astype(BF16), preferred_element_type=F32)
+    start = slots * rows
+    scale = jnp.sum(values[:, start : start + 3], axis=1, keepdims=True)
     scale_ref[...] = jnp.broadcast_to(scale, scale_ref.shape)
-    flags = jnp.concatenate([read(slot) for slot in range(slots)], axis=1)[:, :stations]
     mask = jnp.dot(
-        flags.astype(BF16), one_hot(order_ref[...], stations), preferred_element_type=F32
+        values[:, :stations].astype(BF16),
+        one_hot(order_ref[...], stations),
+        preferred_element_type=F32,
     ).astype(BF16)
-    power = masked_squares(mask, wave_ref[...])
+    mask_ref[...] = mask
+    grouped = jnp.dot(mask, regroup(channels, padded, part, True), preferred_element_type=F32)
+    mine = side_major(lax.axis_index("inner")) * LANES + lax.axis_index("tm") * part
+    part_ref[...] = pltpu.roll(grouped, lax.rem(padded - mine, padded), 1)[:, :part].astype(BF16)
+
+
+def power_kernel(window, wave_ref, mask_ref, after, out_ref):
+    del after
+    power = masked_squares(mask_ref[...], wave_ref[...])
     columns = power.shape[1]
     column = lax.broadcasted_iota(jnp.int32, power.shape, 1)
     reach = 1
@@ -317,11 +376,6 @@
         power = power + jnp.where(column < columns - reach, later, 0.0)
         reach *= 2
     out_ref[...] = power
-    mask = jnp.dot(
-        mask, regroup(channels, padded, part, True), preferred_element_type=F32
-    )
-    mine = side_major(lax.axis_index("inner")) * LANES + lax.axis_index("tm") * part
-    mask_ref[...] = pltpu.roll(mask, lax.rem(padded - mine, padded), 1)[:, :part].astype(BF16)
 
 
 def finish_kernel(*refs):
@@ -355,35 +409,40 @@
     sds = jax.ShapeDtypeStruct
     order_row = channel_order[None, :]
 
-    send, keep = call(
-        functools.partial(sample_kernel, part),
-        [HBM],
-        [sds((padded // 2, slab), BF16)] * 2,
+    rows = window * part // LANES
+    send, keep, pieces = call(
+        functools.partial(prologue_kernel, tm_count),
+        [HBM] * 4,
+        [
+            sds((padded // 2 * slab // LANES + 2 * rows, LANES), BF16),
+            sds((padded // 2, slab), BF16),
+            sds((2, rows, LANES), BF16),
+        ],
         [
             pltpu.VMEM((channels, slab), BF16),
             pltpu.VMEM((padded, slab), BF16),
-            pltpu.SemaphoreType.DMA,
-        ],
-        bytes_accessed=channels * slab * 2,
-        vmem=60,
-    )(waveforms)
-    payload = call(
-        functools.partial(template_kernel, tm_count),
-        [HBM] * 3 + [AFTER],
-        sds((blk_count, window * part // LANES, LANES), BF16),
-        [
             pltpu.VMEM((channels, window), BF16),
             pltpu.VMEM((1, stations), jnp.int32),
             pltpu.VMEM((1, channels), jnp.int32),
             pltpu.VMEM((window, padded), F32),
-            pltpu.SemaphoreType.DMA((3,)),
+            pltpu.SemaphoreType.DMA((4,)),
         ],
-        bytes_accessed=channels * window * 2,
+        bytes_accessed=channels * (window + slab) * 2,
         vmem=60,
-    )(templates, station_mask, order_row, keep)
-    tpls = lax.all_to_all(payload, blk, 0, 0, tiled=True)
+    )(waveforms, templates, station_mask, order_row)
 
     got = lax.ppermute(send, "inner", [(b, b ^ 1) for b in range(INNER)])
+
+    ours, theirs = call(
+        plane_kernel, [VMEM] * 2, [sds((2, rows, LANES), BF16)] * 2, bytes_accessed=rows * LANES * 8
+    )(pieces, got)
+    others = lax.ppermute(theirs, "inner", [(b, b ^ 2) for b in range(INNER)])
+    pack = call(pack_kernel, [VMEM] * 2, sds((INNER, rows, LANES), BF16))(ours, others)
+    tpls = [pack] + [
+        lax.ppermute(pack, "outer", [(b, b ^ flip) for b in range(outer_count)])
+        for flip in range(1, outer_count)
+    ]
+
     half = group // 2
     parts = call(
         functools.partial(split_kernel, tm_count),
@@ -406,17 +465,16 @@
     )(*waves)
     halo = lax.ppermute(head, "outer", [(b, b - 1) for b in range(1, outer_count)])
 
-    power, scale, mask = call(
-        functools.partial(power_kernel, stations, window, tm_count),
-        [VMEM] * 3,
+    scale, mask, mask_part = call(
+        functools.partial(mask_kernel, stations, channels, tm_count),
+        [VMEM] * (outer_count + 1),
         [
-            sds((blk_count, slab), F32),
             sds((blk_count, LANES), F32),
+            sds((blk_count, channels), BF16),
             sds((blk_count, part), BF16),
         ],
-        flops=4 * blk_count * channels * slab,
-        bytes_accessed=channels * slab * 2,
-    )(waveforms, tpls, order_row)
+        bytes_accessed=blk_count * rows * LANES * 2,
+    )(*tpls, order_row)
 
     depth = window // FINE * part
 
@@ -431,15 +489,15 @@
     work = 2 * blk_count * window * part * span
     partials = call(
         first_dots_kernel,
-        [VMEM] * 2,
+        [VMEM] * (outer_count + 1),
         sds((2 * (blocks - 1), blk_count, slab), F32),
         scratch((blocks - 1) * span),
         flops=work * (blocks - 1),
         bytes_accessed=part * chunk * 2,
-    )(tpls, samples)
+    )(*tpls, samples)
     keep, send = call(
         last_dots_kernel,
-        [VMEM] * 5,
+        [VMEM] * (outer_count + 4),
         [sds((half, blk_count, slab + window), F32)] * 2,
         [
             pltpu.VMEM((group, blk_count, slab), F32),
@@ -448,8 +506,15 @@
         + scratch(span),
         flops=work,
         bytes_accessed=part * chunk * 2,
-    )(tpls, samples, halo, mask, partials)
+    )(*tpls, samples, halo, mask_part, partials)
     got = lax.ppermute(send, "inner", [(b, b ^ 1) for b in range(INNER)])
+    power = call(
+        functools.partial(power_kernel, window),
+        [VMEM, VMEM, AFTER],
+        sds((blk_count, slab), F32),
+        flops=4 * blk_count * channels * slab,
+        bytes_accessed=channels * slab * 2,
+    )(waveforms, mask, send)
     sums = call(
         functools.partial(add_kernel, tm_count),
         [VMEM] * 2,

time: 45 us -> 44 us (0.978)
  waiting for transfers between devices: 16.1 us -> 15 us
  local copies, waits for them, and re-layouts: 0.02 us -> 0.96 us
  Pallas kernels: 12 us -> 11.1 us
    ppermute x6, waiting for transfers between devices: 12.9 us -> 3.69 us  [swap(): return lax.ppermute(part, every, route)]
    ppermute x0 -> x4, waiting for transfers between devices: none -> 8.46 us  [the longest x3 7.3 us: on_device(): lax.ppermute(pack, 'outer', [(b, b ^ flip) for b in range(outer_count)])]
    all_to_all x1 -> x0, starting transfers between devices: 7.53 us -> none  [on_device(): tpls = lax.all_to_all(payload, blk, 0, 0, tiled=True)]
    ppermute x0 -> x4, starting transfers between devices: none -> 6.03 us  [the longest x3 4.45 us: on_device(): lax.ppermute(pack, 'outer', [(b, b ^ flip) for b in range(outer_count)])]
    ppermute x6, starting transfers between devices: 7.12 us -> 8.65 us  [swap(): return lax.ppermute(part, every, route)]
    unnamed x8, local copies, waits for them, and re-layouts: 0.02 us -> 0.96 us
    pallas_call x5 -> x7, Pallas kernels: 11.2 us -> 10.3 us  [the longest x1 3.49 us: on_device(): call(functools.partial(prologue_kernel, tm_count), [HBM] * 4, [sds((padde...]
    ppermute x1, waiting for transfers between devices: 0.6 us -> 0.01 us  [on_device(): lax.ppermute(head, 'outer', [(b, b - 1) for b in range(1, outer_count)])]
  transfers between devices with their start and end apart: 10 -> 13, of which waited for: 8 -> 8; matrix products, arithmetic and copies ran while one was open for 0% -> 0% of each run, Pallas kernels for 10% -> 11%
where the time goes in v10:
time: 44 us; the launch traced here: 43.8 us
  starting transfers between devices  16.6 us (38%)
  waiting for transfers between devices  15 us (34%)
  Pallas kernels  11.1 us (25%)
  local copies, waits for them, and re-layouts  0.96 us (2%)
    ppermute x6, starting transfers between devices, swap(): return lax.ppermute(part, every, route)  8.65 us
    ppermute x3, waiting for transfers between devices, on_device(): lax.ppermute(pack, 'outer', [(b, b ^ flip) for b in range(outer_count)])  7.3 us
    ppermute x3, starting transfers between devices, on_device(): lax.ppermute(pack, 'outer', [(b, b ^ flip) for b in range(outer_count)])  4.45 us
    ppermute x6, waiting for transfers between devices, swap(): return lax.ppermute(part, every, route)  3.69 us
    pallas_call x1, Pallas kernels, on_device(): call(functools.partial(prologue_kernel, tm_count), [HBM] * 4, [sds((padde...  3.49 us
    pallas_call x1, Pallas kernels, on_device(): call(first_dots_kernel, [VMEM] * (outer_count + 1), sds((2 * (blocks - 1)...  3.32 us
    ppermute x2, waiting for transfers between devices, on_device(): got = lax.ppermute(send, 'inner', [(b, b ^ 1) for b in range(INNER)])  2.89 us
    pallas_call x1, Pallas kernels, on_device(): call(last_dots_kernel, [VMEM] * (outer_count + 4), [sds((half, blk_count,...  1.87 us
  transfers between devices with their start and end apart: 13, of which 8 were waited for; matrix products, arithmetic and copies ran while one was open for 0% of the time, Pallas kernels for 11%

profile of v10, /device:TPU:0, one launch (start us, length us, event | category | flops | bytes accessed | tf_op | source)
XLA Modules:
  0.0 43.8 jit_solution(16754486507054957901)
XLA Ops:
  0.0 3.5 %shard_map.46 = (bf16[1280,128]{1,0:T(8,128)(2,1)}, bf16[256,512]{1,0:T(8,128)(2,1)}, bf16[2,128,128]{2,1,0:T(8,128)(2,1)}) custom-call(bf16[480,512]{1,0:T(8,128)(2,1)} %wave_ref.1, bf16[1,480,256]{2,1,0:T(8,128)(2,1)} %tpl_hbm.1, s32[1,160]{1,0:T(1,128)} %flag_hbm.1, s32[1,480]{1,0:T(1,128)} %bitcast.1), custom_call_target="tpu_custom_call" | custom-call | bytes 737280 | tf_op jit(solution)/shard_map/pallas_call | solution.py:413
  4.0 1.5 %collective-permute-done.got_ref = bf16[1280,128]{1,0:T(8,128)(2,1)S(1)} collective-permute-done((bf16[1280,128]{1,0:T(8,128)(2,1)}, bf16[1280,128]{1,0:T(8,128)(2,1)S(1)}, u32[]{:S(2)}, u32[]{:S(2)}) %collective-permute-start) | collective-permute-done | bytes 327712 | tf_op jit(solution)/shard_map/ppermute | solution.py:434
  5.5 0.9 %copy-done.1 = bf16[256,512]{1,0:T(8,128)(2,1)S(1)} copy-done((bf16[256,512]{1,0:T(8,128)(2,1)S(1)}, bf16[256,512]{1,0:T(8,128)(2,1)}, u32[]{:S(2)}) %copy-start.1) | copy-done | bytes 262168
  6.5 2.9 %collective-permute-start.5 = (bf16[2,64,512]{2,1,0:T(8,128)(2,1)S(1)}, bf16[2,64,512]{2,1,0:T(8,128)(2,1)S(1)}, u32[]{:S(2)}, u32[]{:S(2)}) collective-permute-start(bf16[2,64,512]{2,1,0:T(8,128)(2,1)S(1)} %get-tuple-element.31), channel_id=1, source_target_pairs={{0,1},{1,0},{2,3},{3,2},{4,5},{5,4},{6,7},{7,6},{8,9},{9,8},{10,11... | collective-permute-start | bytes 393224 | tf_op jit(solution)/shard_map/ppermute | solution.py:457
  9.5 1.6 %collective-permute-start.1 = (bf16[2,128,128]{2,1,0:T(8,128)(2,1)S(1)}, bf16[2,128,128]{2,1,0:T(8,128)(2,1)S(1)}, u32[]{:S(2)}, u32[]{:S(2)}) collective-permute-start(bf16[2,128,128]{2,1,0:T(8,128)(2,1)S(1)} %get-tuple-element.28), channel_id=1, source_target_pairs={{0,4},{2,6},{4,0},{6,2},{1,5},{3,7},{5,1},{7,3},{8,12},{10,14},{12... | collective-permute-start | bytes 196616 | tf_op jit(solution)/shard_map/ppermute | solution.py:439
  11.6 1.7 %collective-permute-start.7 = (bf16[2,64,512]{2,1,0:T(8,128)(2,1)S(1)}, bf16[2,64,512]{2,1,0:T(8,128)(2,1)S(1)}, u32[]{:S(2)}, u32[]{:S(2)}) collective-permute-start(bf16[2,64,512]{2,1,0:T(8,128)(2,1)S(1)} %get-tuple-element.33), channel_id=1, source_target_pairs={{0,5},{1,4},{2,7},{3,6},{4,1},{5,0},{6,3},{7,2},{8,13},{9,12},{10,... | collective-permute-start | bytes 393224 | tf_op jit(solution)/shard_map/ppermute | solution.py:457
  13.2 1.2 %collective-permute-done.1.got_ref = bf16[2,128,128]{2,1,0:T(8,128)(2,1)S(1)} collective-permute-done((bf16[2,128,128]{2,1,0:T(8,128)(2,1)S(1)}, bf16[2,128,128]{2,1,0:T(8,128)(2,1)S(1)}, u32[]{:S(2)}, u32[]{:S(2)}) %collective-permute-start.1) | collective-permute-done | bytes 65568 | tf_op jit(solution)/shard_map/ppermute | solution.py:439
  14.4 3.7 %collective-permute-start.4 = (bf16[4,128,128]{2,1,0:T(8,128)(2,1)S(1)}, bf16[4,128,128]{2,1,0:T(8,128)(2,1)S(1)}, u32[]{:S(2)}, u32[]{:S(2)}) collective-permute-start(bf16[4,128,128]{2,1,0:T(8,128)(2,1)S(1)} %shard_map.48.refs_0_), channel_id=1, source_target_pairs={{0,24},{8,16},{16,8},{24,0},{1,25},{9,17},{17,9},{25,1},{2,26},{10... | collective-permute-start | bytes 393224 | tf_op jit(solution)/shard_map/ppermute | solution.py:442
  18.1 0.8 %collective-permute-start.2 = (bf16[4,128,128]{2,1,0:T(8,128)(2,1)S(1)}, bf16[4,128,128]{2,1,0:T(8,128)(2,1)S(1)}, u32[]{:S(2)}, u32[]{:S(2)}) collective-permute-start(bf16[4,128,128]{2,1,0:T(8,128)(2,1)S(1)} %shard_map.48.refs_0_), channel_id=1, source_target_pairs={{0,8},{8,0},{16,24},{24,16},{1,9},{9,1},{17,25},{25,17},{2,10},{10... | collective-permute-start | bytes 393224 | tf_op jit(solution)/shard_map/ppermute | solution.py:442
  18.9 0.6 %collective-permute-done.6.refs_2_ = bf16[2,64,512]{2,1,0:T(8,128)(2,1)S(1)} collective-permute-done((bf16[2,64,512]{2,1,0:T(8,128)(2,1)S(1)}, bf16[2,64,512]{2,1,0:T(8,128)(2,1)S(1)}, u32[]{:S(2)}, u32[]{:S(2)}) %collective-permute-start.6) | collective-permute-done | bytes 131104 | tf_op jit(solution)/shard_map/ppermute | solution.py:457
  19.5 1.3 %collective-permute-start.8 = (bf16[64,256]{1,0:T(8,128)(2,1)S(1)}, bf16[64,256]{1,0:T(8,128)(2,1)S(1)}, u32[]{:S(2)}, u32[]{:S(2)}) collective-permute-start(bf16[64,256]{1,0:T(8,128)(2,1)S(1)} %get-tuple-element.35), channel_id=1, source_target_pairs={{8,0},{16,8},{24,16},{9,1},{17,9},{25,17},{10,2},{18,10},{26,18},{... | collective-permute-start | bytes 98312 | tf_op jit(solution)/shard_map/ppermute | solution.py:466
  20.8 1.5 %collective-permute-done.4.refs_3_ = bf16[4,128,128]{2,1,0:T(8,128)(2,1)S(1)} collective-permute-done((bf16[4,128,128]{2,1,0:T(8,128)(2,1)S(1)}, bf16[4,128,128]{2,1,0:T(8,128)(2,1)S(1)}, u32[]{:S(2)}, u32[]{:S(2)}) %collective-permute-start.4) | collective-permute-done | bytes 131104 | tf_op jit(solution)/shard_map/ppermute | solution.py:442
  22.3 5.8 %collective-permute-done.3.refs_2_ = bf16[4,128,128]{2,1,0:T(8,128)(2,1)S(1)} collective-permute-done((bf16[4,128,128]{2,1,0:T(8,128)(2,1)S(1)}, bf16[4,128,128]{2,1,0:T(8,128)(2,1)S(1)}, u32[]{:S(2)}, u32[]{:S(2)}) %collective-permute-start.3) | collective-permute-done | bytes 131104 | tf_op jit(solution)/shard_map/ppermute | solution.py:442
  28.1 3.3 %shard_map.52.refs_7_ = f32[6,16,512]{2,1,0:T(8,128)S(1)} custom-call(bf16[4,128,128]{2,1,0:T(8,128)(2,1)S(1)} %shard_map.48.refs_0_, bf16[4,128,128]{2,1,0:T(8,128)(2,1)S(1)} %collective-permute-done.2.refs_1_, bf16[4,128,128]{2,1,0:T(8,128)(2,1)S(1)} %collective-permute-done.3.refs_2_, bf16[4,128,128]{2,1,0:T(8,128)(2,1)S(1)} %collective-permute-done.4.refs_3_, ...), custom_call_target="tpu_custom_call" | custom-call | flops 1610612736 | bytes 524288 | tf_op jit(solution)/shard_map/pallas_call | solution.py:490
  31.4 0.7 %shard_map.51 = (f32[16,128]{1,0:T(8,128)S(1)}, bf16[16,480]{1,0:T(8,128)(2,1)S(1)}, bf16[16,64]{1,0:T(8,128)(2,1)S(1)}) custom-call(bf16[4,128,128]{2,1,0:T(8,128)(2,1)S(1)} %shard_map.48.refs_0_, bf16[4,128,128]{2,1,0:T(8,128)(2,1)S(1)} %collective-permute-done.2.refs_1_, bf16[4,128,128]{2,1,0:T(8,128)(2,1)S(1)} %collective-permute-done.3.refs_2_, ...), custom_call_target="tpu_custom_call" | custom-call | bytes 524288 | tf_op jit(solution)/shard_map/pallas_call | solution.py:468
  32.2 1.9 %shard_map.53 = (f32[4,16,768]{2,1,0:T(8,128)S(1)}, f32[4,16,768]{2,1,0:T(8,128)S(1)}) custom-call(bf16[4,128,128]{2,1,0:T(8,128)(2,1)S(1)} %shard_map.48.refs_0_, bf16[4,128,128]{2,1,0:T(8,128)(2,1)S(1)} %collective-permute-done.2.refs_1_, bf16[4,128,128]{2,1,0:T(8,128)(2,1)S(1)} %collective-permute-done.3.refs_2_, ...), custom_call_target="tpu_custom_call" | custom-call | flops 536870912 | bytes 524288 | tf_op jit(solution)/shard_map/pallas_call | solution.py:498
  34.1 1.4 %collective-permute-done.9.got_ref = f32[4,16,768]{2,1,0:T(8,128)S(1)} collective-permute-done((f32[4,16,768]{2,1,0:T(8,128)S(1)}, f32[4,16,768]{2,1,0:T(8,128)S(1)}, u32[]{:S(2)}, u32[]{:S(2)}) %collective-permute-start.9) | collective-permute-done | bytes 196640 | tf_op jit(solution)/shard_map/ppermute | solution.py:510
  35.6 1.0 %collective-permute-start.10 = (f32[16,768]{1,0:T(8,128)S(1)}, f32[16,768]{1,0:T(8,128)S(1)}, u32[]{:S(2)}, u32[]{:S(2)}) collective-permute-start(f32[16,768]{1,0:T(8,128)S(1)} %get-tuple-element.40), channel_id=1, source_target_pairs={{0,1},{1,0},{2,3},{3,2},{4,5},{5,4},{6,7},{7,6},{8,9},{9,8},{10,11... | collective-permute-start | bytes 147464 | tf_op jit(solution)/shard_map/ppermute | solution.py:457
  36.6 1.5 %collective-permute-start.11 = (f32[16,768]{1,0:T(8,128)S(1)}, f32[16,768]{1,0:T(8,128)S(1)}, u32[]{:S(2)}, u32[]{:S(2)}) collective-permute-start(f32[16,768]{1,0:T(8,128)S(1)} %get-tuple-element.41), channel_id=1, source_target_pairs={{0,4},{1,5},{2,6},{3,7},{4,0},{5,1},{6,2},{7,3},{8,12},{9,13},{10,... | collective-permute-start | bytes 147464 | tf_op jit(solution)/shard_map/ppermute | solution.py:457
  38.1 1.0 %collective-permute-start.12 = (f32[16,768]{1,0:T(8,128)S(1)}, f32[16,768]{1,0:T(8,128)S(1)}, u32[]{:S(2)}, u32[]{:S(2)}) collective-permute-start(f32[16,768]{1,0:T(8,128)S(1)} %get-tuple-element.42), channel_id=1, source_target_pairs={{0,5},{1,4},{2,7},{3,6},{4,1},{5,0},{6,3},{7,2},{8,13},{9,12},{10,... | collective-permute-start | bytes 147464 | tf_op jit(solution)/shard_map/ppermute | solution.py:457
  39.1 0.9 %shard_map.55.refs_4_ = f32[16,512]{1,0:T(8,128)S(1)} custom-call(bf16[480,512]{1,0:T(8,128)(2,1)S(1)} %copy-done, bf16[16,480]{1,0:T(8,128)(2,1)S(1)} %get-tuple-element.43.mask_ref, f32[4,16,768]{2,1,0:T(8,128)S(1)} %get-tuple-element.38.after), custom_call_target="tpu_custom_call" | custom-call | flops 15728640 | bytes 491520 | tf_op jit(solution)/shard_map/pallas_call | solution.py:511
  40.0 0.7 %collective-permute-done.11.refs_2_ = f32[16,768]{1,0:T(8,128)S(1)} collective-permute-done((f32[16,768]{1,0:T(8,128)S(1)}, f32[16,768]{1,0:T(8,128)S(1)}, u32[]{:S(2)}, u32[]{:S(2)}) %collective-permute-start.11) | collective-permute-done | bytes 49184 | tf_op jit(solution)/shard_map/ppermute | solution.py:457
  40.7 2.4 %collective-permute-done.12.refs_3_ = f32[16,768]{1,0:T(8,128)S(1)} collective-permute-done((f32[16,768]{1,0:T(8,128)S(1)}, f32[16,768]{1,0:T(8,128)S(1)}, u32[]{:S(2)}, u32[]{:S(2)}) %collective-permute-start.12) | collective-permute-done | bytes 49184 | tf_op jit(solution)/shard_map/ppermute | solution.py:457
  43.1 0.7 %shard_map.56 = f32[16,512]{1,0:T(8,128)} custom-call(f32[16,768]{1,0:T(8,128)S(1)} %get-tuple-element.39.refs_0_, f32[16,768]{1,0:T(8,128)S(1)} %collective-permute-done.10.refs_1_, f32[16,768]{1,0:T(8,128)S(1)} %collective-permute-done.11.refs_2_, f32[16,768]{1,0:T(8,128)S(1)} %collective-permute-done.12.refs_3_, f32[16,512]{1,0:T(8,128)S(1)} %shard_map.55.refs_4_, ...), custom_call_target="tpu_custom_call" | custom-call | bytes 196608 | tf_op jit(solution)/shard_map/pallas_call | solution.py:525
  (21 shorter events, 1.3 us)
Async XLA Ops:
  3.5 2.0 %collective-permute-start = (bf16[1280,128]{1,0:T(8,128)(2,1)}, bf16[1280,128]{1,0:T(8,128)(2,1)S(1)}, u32[]{:S(2)}, u32[]{:S(2)}) collective-permute-start(bf16[1280,128]{1,0:T(8,128)(2,1)} %get-tuple-element.26), channel_id=1, source_target_pairs={{0,2},{2,0},{4,6},{6,4},{1,3},{3,1},{5,7},{7,5},{8,10},{10,8},{12,... | collective-permute-start | bytes 983048 | tf_op jit(solution)/shard_map/ppermute | solution.py:434
  5.5 0.9 %copy-start.1 = (bf16[256,512]{1,0:T(8,128)(2,1)S(1)}, bf16[256,512]{1,0:T(8,128)(2,1)}, u32[]{:S(2)}) copy-start(bf16[256,512]{1,0:T(8,128)(2,1)} %get-tuple-element.29.keep_ref) | copy-start | bytes 786436
  6.4 3.0 %copy-start.2 = (bf16[2,128,128]{2,1,0:T(8,128)(2,1)S(1)}, bf16[2,128,128]{2,1,0:T(8,128)(2,1)}, u32[]{:S(2)}) copy-start(bf16[2,128,128]{2,1,0:T(8,128)(2,1)} %get-tuple-element.25.tpls_ref) | copy-start | bytes 196612
  6.5 11.6 %collective-permute-start.5 = (bf16[2,64,512]{2,1,0:T(8,128)(2,1)S(1)}, bf16[2,64,512]{2,1,0:T(8,128)(2,1)S(1)}, u32[]{:S(2)}, u32[]{:S(2)}) collective-permute-start(bf16[2,64,512]{2,1,0:T(8,128)(2,1)S(1)} %get-tuple-element.31), channel_id=1, source_target_pairs={{0,1},{1,0},{2,3},{3,2},{4,5},{5,4},{6,7},{7,6},{8,9},{9,8},{10,11... | collective-permute-start | bytes 393224 | tf_op jit(solution)/shard_map/ppermute | solution.py:457
  9.5 4.9 %collective-permute-start.1 = (bf16[2,128,128]{2,1,0:T(8,128)(2,1)S(1)}, bf16[2,128,128]{2,1,0:T(8,128)(2,1)S(1)}, u32[]{:S(2)}, u32[]{:S(2)}) collective-permute-start(bf16[2,128,128]{2,1,0:T(8,128)(2,1)S(1)} %get-tuple-element.28), channel_id=1, source_target_pairs={{0,4},{2,6},{4,0},{6,2},{1,5},{3,7},{5,1},{7,3},{8,12},{10,14},{12... | collective-permute-start | bytes 196616 | tf_op jit(solution)/shard_map/ppermute | solution.py:439
  11.0 8.4 %collective-permute-start.6 = (bf16[2,64,512]{2,1,0:T(8,128)(2,1)S(1)}, bf16[2,64,512]{2,1,0:T(8,128)(2,1)S(1)}, u32[]{:S(2)}, u32[]{:S(2)}) collective-permute-start(bf16[2,64,512]{2,1,0:T(8,128)(2,1)S(1)} %get-tuple-element.32), channel_id=1, source_target_pairs={{0,4},{1,5},{2,6},{3,7},{4,0},{5,1},{6,2},{7,3},{8,12},{9,13},{10,... | collective-permute-start | bytes 393224 | tf_op jit(solution)/shard_map/ppermute | solution.py:457
  11.6 7.9 %collective-permute-start.7 = (bf16[2,64,512]{2,1,0:T(8,128)(2,1)S(1)}, bf16[2,64,512]{2,1,0:T(8,128)(2,1)S(1)}, u32[]{:S(2)}, u32[]{:S(2)}) collective-permute-start(bf16[2,64,512]{2,1,0:T(8,128)(2,1)S(1)} %get-tuple-element.33), channel_id=1, source_target_pairs={{0,5},{1,4},{2,7},{3,6},{4,1},{5,0},{6,3},{7,2},{8,13},{9,12},{10,... | collective-permute-start | bytes 393224 | tf_op jit(solution)/shard_map/ppermute | solution.py:457
  14.4 7.9 %collective-permute-start.4 = (bf16[4,128,128]{2,1,0:T(8,128)(2,1)S(1)}, bf16[4,128,128]{2,1,0:T(8,128)(2,1)S(1)}, u32[]{:S(2)}, u32[]{:S(2)}) collective-permute-start(bf16[4,128,128]{2,1,0:T(8,128)(2,1)S(1)} %shard_map.48.refs_0_), channel_id=1, source_target_pairs={{0,24},{8,16},{16,8},{24,0},{1,25},{9,17},{17,9},{25,1},{2,26},{10... | collective-permute-start | bytes 393224 | tf_op jit(solution)/shard_map/ppermute | solution.py:442
  18.1 10.0 %collective-permute-start.3 = (bf16[4,128,128]{2,1,0:T(8,128)(2,1)S(1)}, bf16[4,128,128]{2,1,0:T(8,128)(2,1)S(1)}, u32[]{:S(2)}, u32[]{:S(2)}) collective-permute-start(bf16[4,128,128]{2,1,0:T(8,128)(2,1)S(1)} %shard_map.48.refs_0_), channel_id=1, source_target_pairs={{0,16},{8,24},{16,0},{24,8},{1,17},{9,25},{17,1},{25,9},{2,18},{10... | collective-permute-start | bytes 393224 | tf_op jit(solution)/shard_map/ppermute | solution.py:442
  18.1 10.0 %collective-permute-start.2 = (bf16[4,128,128]{2,1,0:T(8,128)(2,1)S(1)}, bf16[4,128,128]{2,1,0:T(8,128)(2,1)S(1)}, u32[]{:S(2)}, u32[]{:S(2)}) collective-permute-start(bf16[4,128,128]{2,1,0:T(8,128)(2,1)S(1)} %shard_map.48.refs_0_), channel_id=1, source_target_pairs={{0,8},{8,0},{16,24},{24,16},{1,9},{9,1},{17,25},{25,17},{2,10},{10... | collective-permute-start | bytes 393224 | tf_op jit(solution)/shard_map/ppermute | solution.py:442
  19.5 12.7 %collective-permute-start.8 = (bf16[64,256]{1,0:T(8,128)(2,1)S(1)}, bf16[64,256]{1,0:T(8,128)(2,1)S(1)}, u32[]{:S(2)}, u32[]{:S(2)}) collective-permute-start(bf16[64,256]{1,0:T(8,128)(2,1)S(1)} %get-tuple-element.35), channel_id=1, source_target_pairs={{8,0},{16,8},{24,16},{9,1},{17,9},{25,17},{10,2},{18,10},{26,18},{... | collective-permute-start | bytes 98312 | tf_op jit(solution)/shard_map/ppermute | solution.py:466
  28.1 3.3 %copy-start.3 = (s32[480]{0:T(512)S(1)}, s32[480]{0:T(512)}, u32[]{:S(2)}) copy-start(s32[480]{0:T(512)} %param.7) | copy-start | bytes 5764
  32.1 7.0 %copy-start = (bf16[480,512]{1,0:T(8,128)(2,1)S(1)}, bf16[480,512]{1,0:T(8,128)(2,1)}, u32[]{:S(2)}) copy-start(bf16[480,512]{1,0:T(8,128)(2,1)} %wave_ref.1) | copy-start | bytes 1474564
  34.0 1.5 %collective-permute-start.9 = (f32[4,16,768]{2,1,0:T(8,128)S(1)}, f32[4,16,768]{2,1,0:T(8,128)S(1)}, u32[]{:S(2)}, u32[]{:S(2)}) collective-permute-start(f32[4,16,768]{2,1,0:T(8,128)S(1)} %get-tuple-element.38.after), channel_id=1, source_target_pairs={{0,2},{2,0},{4,6},{6,4},{1,3},{3,1},{5,7},{7,5},{8,10},{10,8},{12,... | collective-permute-start | bytes 589832 | tf_op jit(solution)/shard_map/ppermute | solution.py:510
  35.6 4.4 %collective-permute-start.10 = (f32[16,768]{1,0:T(8,128)S(1)}, f32[16,768]{1,0:T(8,128)S(1)}, u32[]{:S(2)}, u32[]{:S(2)}) collective-permute-start(f32[16,768]{1,0:T(8,128)S(1)} %get-tuple-element.40), channel_id=1, source_target_pairs={{0,1},{1,0},{2,3},{3,2},{4,5},{5,4},{6,7},{7,6},{8,9},{9,8},{10,11... | collective-permute-start | bytes 147464 | tf_op jit(solution)/shard_map/ppermute | solution.py:457
  36.6 4.1 %collective-permute-start.11 = (f32[16,768]{1,0:T(8,128)S(1)}, f32[16,768]{1,0:T(8,128)S(1)}, u32[]{:S(2)}, u32[]{:S(2)}) collective-permute-start(f32[16,768]{1,0:T(8,128)S(1)} %get-tuple-element.41), channel_id=1, source_target_pairs={{0,4},{1,5},{2,6},{3,7},{4,0},{5,1},{6,2},{7,3},{8,12},{9,13},{10,... | collective-permute-start | bytes 147464 | tf_op jit(solution)/shard_map/ppermute | solution.py:457
  38.1 5.0 %collective-permute-start.12 = (f32[16,768]{1,0:T(8,128)S(1)}, f32[16,768]{1,0:T(8,128)S(1)}, u32[]{:S(2)}, u32[]{:S(2)}) collective-permute-start(f32[16,768]{1,0:T(8,128)S(1)} %get-tuple-element.42), channel_id=1, source_target_pairs={{0,5},{1,4},{2,7},{3,6},{4,1},{5,0},{6,3},{7,2},{8,13},{9,12},{10,... | collective-permute-start | bytes 147464 | tf_op jit(solution)/shard_map/ppermute | solution.py:457

commit v11 on v10

--- a/solution.py
+++ b/solution.py
@@ -47,27 +47,53 @@
     return lax.rem(inner, 2) * (INNER // 2) + lax.div(inner, 2)
 
 
-def regroup(channels, padded, part, transposed):
-    real = part * channels // padded
-    shape = (channels, padded) if transposed else (padded, channels)
-    channel = lax.broadcasted_iota(jnp.int32, shape, 0 if transposed else 1)
-    place = lax.broadcasted_iota(jnp.int32, shape, 1 if transposed else 0)
-    within = place % part
-    hit = (channel == lax.div(place, part) * real + within) & (within < real)
-    return jnp.where(hit, 1.0, 0.0).astype(BF16)
+def place_of(real, part):
+    base = real // FINE * FINE
+    return base, real - base
+
+
+def regroup_rows(source, target, part):
+    channels, width = source.shape
+    groups = target.shape[0] // part
+    real = channels // groups
+    base, extra = place_of(real, part)
+    rest = source[groups * base :, :].astype(F32)
+    fill = jnp.zeros((part - real, width), F32)
+    for group in range(groups):
+        if base:
+            run = source[group * base : (group + 1) * base, :]
+            target[group * part : group * part + base, :] = run
+        piece = [rest[group * extra : (group + 1) * extra], fill]
+        target[group * part + base : (group + 1) * part, :] = jnp.concatenate(
+            piece, axis=0
+        ).astype(BF16)
+
+
+def regroup(channels, padded, part):
+    groups = padded // part
+    real = channels // groups
+    base, extra = place_of(real, part)
+    channel = lax.broadcasted_iota(jnp.int32, (channels, padded), 0)
+    place = lax.broadcasted_iota(jnp.int32, (1, padded), 1)
+    group, within = place >> (part.bit_length() - 1), place & (part - 1)
+    rest = groups * base + extra * group + within - base
+    source = jnp.where(within < base, base * group + within, rest)
+    source = jnp.where(within < real, source, -1)
+    return jnp.where(channel == source, 1.0, 0.0).astype(BF16)
 
 
 def spare_lanes(part, real):
     slots = LANES // part * (part - real)
     slot = lax.broadcasted_iota(jnp.int32, (8, LANES), 0)
     lane = lax.broadcasted_iota(jnp.int32, (8, LANES), 1)
-    home = lax.div(slot, part - real) * part + real + lax.rem(slot, part - real)
+    spare = part - real
+    home = lax.div(slot, spare) * part + real + lax.rem(slot, spare)
     return jnp.where((lane == home) & (slot < slots), 1.0, 0.0).astype(BF16)
 
 
 def prologue_kernel(tm_count, wave_hbm, tpl_hbm, flag_hbm, order_hbm, *refs):
     send_ref, samples_ref, tpls_ref = refs[:3]
-    wave_ref, grouped, tpl_ref, flag_ref, order_ref, turned, sems = refs[3:]
+    wave_ref, grouped, tpl_ref, tpl_grouped, flag_ref, order_ref, turned, sems = refs[3:]
     channels, window = tpl_hbm.shape[1:]
     copies = [
         pltpu.make_async_copy(flag_hbm, flag_ref, sems.at[0]),
@@ -81,8 +107,7 @@
     padded = turned.shape[1]
     part = LANES // tm_count
     rows = tpls_ref.shape[1]
-    groups = regroup(channels, padded, part, True)
-    order = regroup(channels, padded, part, False)
+    groups = regroup(channels, padded, part)
     copies[0].wait()
     copies[1].wait()
     flags = jnp.broadcast_to(flag_ref[...].astype(F32), (8, stations))
@@ -92,9 +117,8 @@
     live = jnp.sum(mask[:1], keepdims=True)
     mask = jnp.dot(mask.astype(BF16), groups, preferred_element_type=F32)[:1]
     copies[2].wait()
-    masked = mask * lax.dot_general(
-        tpl_ref[...], groups, (((0,), (0,)), ((), ())), preferred_element_type=F32
-    )
+    regroup_rows(tpl_ref, tpl_grouped, part)
+    masked = tpl_grouped[...].T.astype(F32) * mask
     turned[...] = masked
     norm = jnp.sqrt(jnp.sum(masked * masked, keepdims=True) + EPSILON)
     rest = jnp.broadcast_to(jnp.sqrt(window * live) / norm, (1, rows))
@@ -119,7 +143,7 @@
     my_tm = lax.axis_index("tm")
     my_core = lax.rem(lax.axis_index("inner"), 2)
     first = send_ref.shape[0] - 2 * rows
-    spot = lax.broadcasted_iota(jnp.int32, (FINE, LANES), 1) // part
+    spot = lax.broadcasted_iota(jnp.int32, (FINE, LANES), 1) >> (part.bit_length() - 1)
     for member in range(INNER):
         start = (member % 2 * (INNER // 2) + member // 2) * LANES
         pieces = []
@@ -143,7 +167,7 @@
             send_ref[first + y * rows : first + (y + 1) * rows, :] = payload
 
     copies[3].wait()
-    grouped[...] = jnp.dot(order, wave_ref[...], preferred_element_type=F32).astype(BF16)
+    regroup_rows(wave_ref, grouped, part)
     half = padded // 2
     samples_ref[...] = grouped[pl.ds(pl.multiple_of(my_core * half, half), half), :]
     theirs = pl.ds(pl.multiple_of((1 - my_core) * half, half), half)
@@ -177,13 +201,14 @@
         out_ref[2 * (1 - y) + core] = got_ref[core]
 
 
-def split_kernel(tm_count, keep_ref, got_ref, *outs):
+def split_kernel(tm_count, flips, keep_ref, got_ref, after, *outs):
+    del after
     my_inner = lax.axis_index("inner")
     core = lax.rem(my_inner, 2)
     me = lax.div(my_inner, 2) * tm_count + lax.axis_index("tm")
     part = outs[0].shape[1]
     half, slab = keep_ref.shape
-    for flip, out_ref in enumerate(outs):
+    for flip, out_ref in zip(flips, outs):
         start = (me ^ flip) * part
         out_ref[core] = keep_ref[pl.ds(pl.multiple_of(start, part), part), :]
         for tile in range(slab // LANES):
@@ -205,8 +230,7 @@
 
 
 def arrival(template):
-    outer = lax.div(template, INNER) ^ lax.axis_index("outer")
-    return outer * INNER + lax.rem(template, INNER)
+    return template ^ (lax.axis_index("outer") * INNER)
 
 
 def correlate(tpls, samples, out_ref, first, left, shifts, products):
@@ -222,7 +246,8 @@
     count = len(tpls) * INNER
     row = lax.broadcasted_iota(jnp.int32, (size, size), 0)
     column = lax.broadcasted_iota(jnp.int32, (size, size), 1)
-    source = arrival(lax.rem(row, count)) * FINE + lax.div(row, count)
+    shift = count.bit_length() - 1
+    source = arrival(row & (count - 1)) * FINE + (row >> shift)
     order = jnp.where(column == source, 1.0, 0.0).astype(BF16)
     for step in range(depth // LANES):
         rows = [
@@ -288,7 +313,7 @@
     window = halo_ref.shape[1]
     after = [samples_ref[:, (m + 1) * slab : (m + 1) * slab + window] for m in range(group - 1)]
     squares = masked_squares(mask_ref[...], jnp.concatenate(after + [halo_ref[...]], axis=1))
-    column = lax.broadcasted_iota(jnp.int32, squares.shape, 1) % window
+    column = lax.broadcasted_iota(jnp.int32, squares.shape, 1) & (window - 1)
     reach = 1
     while reach < window:
         earlier = pltpu.roll(squares, reach, 1)
@@ -360,7 +385,7 @@
         preferred_element_type=F32,
     ).astype(BF16)
     mask_ref[...] = mask
-    grouped = jnp.dot(mask, regroup(channels, padded, part, True), preferred_element_type=F32)
+    grouped = jnp.dot(mask, regroup(channels, padded, part), preferred_element_type=F32)
     mine = side_major(lax.axis_index("inner")) * LANES + lax.axis_index("tm") * part
     part_ref[...] = pltpu.roll(grouped, lax.rem(padded - mine, padded), 1)[:, :part].astype(BF16)
 
@@ -410,6 +435,10 @@
     order_row = channel_order[None, :]
 
     rows = window * part // LANES
+    held = [
+        pltpu.with_memory_space_constraint(x, pltpu.HBM)
+        for x in (waveforms, templates, station_mask, order_row)
+    ]
     send, keep, pieces = call(
         functools.partial(prologue_kernel, tm_count),
         [HBM] * 4,
@@ -422,14 +451,14 @@
             pltpu.VMEM((channels, slab), BF16),
             pltpu.VMEM((padded, slab), BF16),
             pltpu.VMEM((channels, window), BF16),
+            pltpu.VMEM((padded, window), BF16),
             pltpu.VMEM((1, stations), jnp.int32),
             pltpu.VMEM((1, channels), jnp.int32),
             pltpu.VMEM((window, padded), F32),
             pltpu.SemaphoreType.DMA((4,)),
         ],
         bytes_accessed=channels * (window + slab) * 2,
-        vmem=60,
-    )(waveforms, templates, station_mask, order_row)
+    )(*held)
 
     got = lax.ppermute(send, "inner", [(b, b ^ 1) for b in range(INNER)])
 
@@ -444,12 +473,15 @@
     ]
 
     half = group // 2
-    parts = call(
-        functools.partial(split_kernel, tm_count),
-        [VMEM] * 2,
-        [sds((2, part, slab), BF16)] * half,
-        bytes_accessed=padded * slab * 2,
-    )(keep, got)
+    def split(flips, after):
+        return call(
+            functools.partial(split_kernel, tm_count, flips),
+            [VMEM, VMEM, AFTER],
+            [sds((2, part, slab), BF16)] * len(flips),
+            bytes_accessed=padded * slab * 2,
+        )(keep, got, after)
+
+    parts = split(range(tm_count), theirs) + split(range(tm_count, half), pack)
 
     def swap(part, flip):
         y, tm = flip // tm_count, flip % tm_count

time: 44 us -> 42.7 us (0.970)
  waiting for transfers between devices: 15 us -> 16.7 us
  Pallas kernels: 11.1 us -> 9.61 us
  local copies, waits for them, and re-layouts: 0.96 us -> 0.01 us
  starting transfers between devices: 16.6 us -> 16.1 us
    ppermute x1, waiting for transfers between devices: 1.16 us -> 2.75 us  [on_device(): others = lax.ppermute(theirs, 'inner', [(b, b ^ 2) for b in range(INNER)])]
    ppermute x6, waiting for transfers between devices: 3.69 us -> 5.25 us  [swap(): return lax.ppermute(part, every, route)]
    pallas_call x1, Pallas kernels: 3.49 us -> 2 us  [on_device(): call(functools.partial(prologue_kernel, tm_count), [HBM] * 4, [sds((padde...]
    ppermute x3, waiting for transfers between devices: 7.3 us -> 6.04 us  [on_device(): lax.ppermute(pack, 'outer', [(b, b ^ flip) for b in range(outer_count)])]
    unnamed x8 -> x4, local copies, waits for them, and re-layouts: 0.96 us -> 0.01 us
    ppermute x6, starting transfers between devices: 8.65 us -> 8.11 us  [swap(): return lax.ppermute(part, every, route)]
  transfers between devices with their start and end apart: 13 -> 13, of which waited for: 8 -> 7; matrix products, arithmetic and copies ran while one was open for 0% -> 0% of each run, Pallas kernels for 11% -> 12%
where the time goes in v11:
time: 42.7 us; the launch traced here: 42.6 us
  waiting for transfers between devices  16.7 us (39%)
  starting transfers between devices  16.1 us (38%)
  Pallas kernels  9.61 us (23%)
    ppermute x6, starting transfers between devices, swap(): return lax.ppermute(part, every, route)  8.11 us
    ppermute x3, waiting for transfers between devices, on_device(): lax.ppermute(pack, 'outer', [(b, b ^ flip) for b in range(outer_count)])  6.04 us
    ppermute x6, waiting for transfers between devices, swap(): return lax.ppermute(part, every, route)  5.25 us
    ppermute x3, starting transfers between devices, on_device(): lax.ppermute(pack, 'outer', [(b, b ^ flip) for b in range(outer_count)])  4.6 us
    pallas_call x1, Pallas kernels, on_device(): call(first_dots_kernel, [VMEM] * (outer_count + 1), sds((2 * (blocks - 1)...  3.29 us
    ppermute x1, waiting for transfers between devices, on_device(): others = lax.ppermute(theirs, 'inner', [(b, b ^ 2) for b in range(INNER)])  2.75 us
    ppermute x2, waiting for transfers between devices, on_device(): got = lax.ppermute(send, 'inner', [(b, b ^ 1) for b in range(INNER)])  2.68 us
    pallas_call x1, Pallas kernels, on_device(): call(functools.partial(prologue_kernel, tm_count), [HBM] * 4, [sds((padde...  2 us
  transfers between devices with their start and end apart: 13, of which 7 were waited for; matrix products, arithmetic and copies ran while one was open for 0% of the time, Pallas kernels for 12%

profile of v11, /device:TPU:0, one launch (start us, length us, event | category | flops | bytes accessed | tf_op | source)
XLA Modules:
  0.0 42.6 jit_solution(10490705847233178789)
XLA Ops:
  0.0 2.0 %shard_map.46 = (bf16[1280,128]{1,0:T(8,128)(2,1)S(1)}, bf16[256,512]{1,0:T(8,128)(2,1)S(1)}, bf16[2,128,128]{2,1,0:T(8,128)(2,1)S(1)}) custom-call(bf16[480,512]{1,0:T(8,128)(2,1)} %wave_ref.1, bf16[1,480,256]{2,1,0:T(8,128)(2,1)} %tpl_hbm.1, s32[1,160]{1,0:T(1,128)} %flag_hbm.1, s32[1,480]{1,0:T(1,128)} %bitcast.1), custom_call_target="tpu_custom_call" | custom-call | bytes 737280 | tf_op jit(solution)/shard_map/pallas_call | solution.py:442
  2.0 0.5 %collective-permute-start = (bf16[1280,128]{1,0:T(8,128)(2,1)S(1)}, bf16[1280,128]{1,0:T(8,128)(2,1)S(1)}, u32[]{:S(2)}, u32[]{:S(2)}) collective-permute-start(bf16[1280,128]{1,0:T(8,128)(2,1)S(1)} %get-tuple-element.26), channel_id=1, source_target_pairs={{0,2},{2,0},{4,6},{6,4},{1,3},{3,1},{5,7},{7,5},{8,10},{10,8},{12,... | collective-permute-start | bytes 983048 | tf_op jit(solution)/shard_map/ppermute | solution.py:463
  2.5 1.3 %collective-permute-done.got_ref = bf16[1280,128]{1,0:T(8,128)(2,1)S(1)} collective-permute-done((bf16[1280,128]{1,0:T(8,128)(2,1)S(1)}, bf16[1280,128]{1,0:T(8,128)(2,1)S(1)}, u32[]{:S(2)}, u32[]{:S(2)}) %collective-permute-start) | collective-permute-done | bytes 327712 | tf_op jit(solution)/shard_map/ppermute | solution.py:463
  3.9 2.9 %collective-permute-start.5 = (bf16[2,64,512]{2,1,0:T(8,128)(2,1)S(1)}, bf16[2,64,512]{2,1,0:T(8,128)(2,1)S(1)}, u32[]{:S(2)}, u32[]{:S(2)}) collective-permute-start(bf16[2,64,512]{2,1,0:T(8,128)(2,1)S(1)} %get-tuple-element.31), channel_id=1, source_target_pairs={{0,1},{1,0},{2,3},{3,2},{4,5},{5,4},{6,7},{7,6},{8,9},{9,8},{10,11... | collective-permute-start | bytes 393224 | tf_op jit(solution)/shard_map/ppermute | solution.py:489
  6.8 1.5 %collective-permute-start.1 = (bf16[2,128,128]{2,1,0:T(8,128)(2,1)S(1)}, bf16[2,128,128]{2,1,0:T(8,128)(2,1)S(1)}, u32[]{:S(2)}, u32[]{:S(2)}) collective-permute-start(bf16[2,128,128]{2,1,0:T(8,128)(2,1)S(1)} %get-tuple-element.28.after), channel_id=1, source_target_pairs={{0,4},{2,6},{4,0},{6,2},{1,5},{3,7},{5,1},{7,3},{8,12},{10,14},{12... | collective-permute-start | bytes 196616 | tf_op jit(solution)/shard_map/ppermute | solution.py:468
  8.3 2.8 %collective-permute-done.1.got_ref = bf16[2,128,128]{2,1,0:T(8,128)(2,1)S(1)} collective-permute-done((bf16[2,128,128]{2,1,0:T(8,128)(2,1)S(1)}, bf16[2,128,128]{2,1,0:T(8,128)(2,1)S(1)}, u32[]{:S(2)}, u32[]{:S(2)}) %collective-permute-start.1) | collective-permute-done | bytes 65568 | tf_op jit(solution)/shard_map/ppermute | solution.py:468
  11.1 1.6 %collective-permute-start.6 = (bf16[2,64,512]{2,1,0:T(8,128)(2,1)S(1)}, bf16[2,64,512]{2,1,0:T(8,128)(2,1)S(1)}, u32[]{:S(2)}, u32[]{:S(2)}) collective-permute-start(bf16[2,64,512]{2,1,0:T(8,128)(2,1)S(1)} %get-tuple-element.32), channel_id=1, source_target_pairs={{0,4},{1,5},{2,6},{3,7},{4,0},{5,1},{6,2},{7,3},{8,12},{9,13},{10,... | collective-permute-start | bytes 393224 | tf_op jit(solution)/shard_map/ppermute | solution.py:489
  12.8 2.0 %collective-permute-start.2 = (bf16[4,128,128]{2,1,0:T(8,128)(2,1)S(1)}, bf16[4,128,128]{2,1,0:T(8,128)(2,1)S(1)}, u32[]{:S(2)}, u32[]{:S(2)}) collective-permute-start(bf16[4,128,128]{2,1,0:T(8,128)(2,1)S(1)} %shard_map.48.after.refs_0_), channel_id=1, source_target_pairs={{0,8},{8,0},{16,24},{24,16},{1,9},{9,1},{17,25},{25,17},{2,10},{10... | collective-permute-start | bytes 393224 | tf_op jit(solution)/shard_map/ppermute | solution.py:471
  14.8 2.6 %collective-permute-start.3 = (bf16[4,128,128]{2,1,0:T(8,128)(2,1)S(1)}, bf16[4,128,128]{2,1,0:T(8,128)(2,1)S(1)}, u32[]{:S(2)}, u32[]{:S(2)}) collective-permute-start(bf16[4,128,128]{2,1,0:T(8,128)(2,1)S(1)} %shard_map.48.after.refs_0_), channel_id=1, source_target_pairs={{0,16},{8,24},{16,0},{24,8},{1,17},{9,25},{17,1},{25,9},{2,18},{10... | collective-permute-start | bytes 393224 | tf_op jit(solution)/shard_map/ppermute | solution.py:471
  17.4 1.6 %collective-permute-done.6.refs_2_ = bf16[2,64,512]{2,1,0:T(8,128)(2,1)S(1)} collective-permute-done((bf16[2,64,512]{2,1,0:T(8,128)(2,1)S(1)}, bf16[2,64,512]{2,1,0:T(8,128)(2,1)S(1)}, u32[]{:S(2)}, u32[]{:S(2)}) %collective-permute-start.6) | collective-permute-done | bytes 131104 | tf_op jit(solution)/shard_map/ppermute | solution.py:489
  19.1 1.3 %collective-permute-start.8 = (bf16[64,256]{1,0:T(8,128)(2,1)S(1)}, bf16[64,256]{1,0:T(8,128)(2,1)S(1)}, u32[]{:S(2)}, u32[]{:S(2)}) collective-permute-start(bf16[64,256]{1,0:T(8,128)(2,1)S(1)} %get-tuple-element.35), channel_id=1, source_target_pairs={{8,0},{16,8},{24,16},{9,1},{17,9},{25,17},{10,2},{18,10},{26,18},{... | collective-permute-start | bytes 98312 | tf_op jit(solution)/shard_map/ppermute | solution.py:498
  20.4 6.0 %collective-permute-done.3.refs_2_ = bf16[4,128,128]{2,1,0:T(8,128)(2,1)S(1)} collective-permute-done((bf16[4,128,128]{2,1,0:T(8,128)(2,1)S(1)}, bf16[4,128,128]{2,1,0:T(8,128)(2,1)S(1)}, u32[]{:S(2)}, u32[]{:S(2)}) %collective-permute-start.3) | collective-permute-done | bytes 131104 | tf_op jit(solution)/shard_map/ppermute | solution.py:471
  26.4 3.3 %shard_map.53.refs_7_ = f32[6,16,512]{2,1,0:T(8,128)S(1)} custom-call(bf16[4,128,128]{2,1,0:T(8,128)(2,1)S(1)} %shard_map.48.after.refs_0_, bf16[4,128,128]{2,1,0:T(8,128)(2,1)S(1)} %collective-permute-done.2.refs_1_, bf16[4,128,128]{2,1,0:T(8,128)(2,1)S(1)} %collective-permute-done.3.refs_2_, bf16[4,128,128]{2,1,0:T(8,128)(2,1)S(1)} %collective-permute-done.4.refs_3_, ...), custom_call_target="tpu_custom_call" | custom-call | flops 1610612736 | bytes 524288 | tf_op jit(solution)/shard_map/pallas_call | solution.py:522
  29.7 0.7 %shard_map.52 = (f32[16,128]{1,0:T(8,128)S(1)}, bf16[16,480]{1,0:T(8,128)(2,1)S(1)}, bf16[16,64]{1,0:T(8,128)(2,1)S(1)}) custom-call(bf16[4,128,128]{2,1,0:T(8,128)(2,1)S(1)} %shard_map.48.after.refs_0_, bf16[4,128,128]{2,1,0:T(8,128)(2,1)S(1)} %collective-permute-done.2.refs_1_, bf16[4,128,128]{2,1,0:T(8,128)(2,1)S(1)} %collective-permute-done.3.refs_2_, ...), custom_call_target="tpu_custom_call" | custom-call | bytes 524288 | tf_op jit(solution)/shard_map/pallas_call | solution.py:500
  30.4 1.9 %shard_map.54 = (f32[4,16,768]{2,1,0:T(8,128)S(1)}, f32[4,16,768]{2,1,0:T(8,128)S(1)}) custom-call(bf16[4,128,128]{2,1,0:T(8,128)(2,1)S(1)} %shard_map.48.after.refs_0_, bf16[4,128,128]{2,1,0:T(8,128)(2,1)S(1)} %collective-permute-done.2.refs_1_, bf16[4,128,128]{2,1,0:T(8,128)(2,1)S(1)} %collective-permute-done.3.refs_2_, ...), custom_call_target="tpu_custom_call" | custom-call | flops 536870912 | bytes 524288 | tf_op jit(solution)/shard_map/pallas_call | solution.py:530
  32.3 0.1 collective-permute-start.9
  32.4 1.4 %collective-permute-done.9.got_ref = f32[4,16,768]{2,1,0:T(8,128)S(1)} collective-permute-done((f32[4,16,768]{2,1,0:T(8,128)S(1)}, f32[4,16,768]{2,1,0:T(8,128)S(1)}, u32[]{:S(2)}, u32[]{:S(2)}) %collective-permute-start.9) | collective-permute-done | bytes 196640 | tf_op jit(solution)/shard_map/ppermute | solution.py:542
  33.8 1.6 %collective-permute-start.10 = (f32[16,768]{1,0:T(8,128)S(1)}, f32[16,768]{1,0:T(8,128)S(1)}, u32[]{:S(2)}, u32[]{:S(2)}) collective-permute-start(f32[16,768]{1,0:T(8,128)S(1)} %get-tuple-element.40), channel_id=1, source_target_pairs={{0,1},{1,0},{2,3},{3,2},{4,5},{5,4},{6,7},{7,6},{8,9},{9,8},{10,11... | collective-permute-start | bytes 147464 | tf_op jit(solution)/shard_map/ppermute | solution.py:489
  35.4 1.5 %collective-permute-start.11 = (f32[16,768]{1,0:T(8,128)S(1)}, f32[16,768]{1,0:T(8,128)S(1)}, u32[]{:S(2)}, u32[]{:S(2)}) collective-permute-start(f32[16,768]{1,0:T(8,128)S(1)} %get-tuple-element.41), channel_id=1, source_target_pairs={{0,4},{1,5},{2,6},{3,7},{4,0},{5,1},{6,2},{7,3},{8,12},{9,13},{10,... | collective-permute-start | bytes 147464 | tf_op jit(solution)/shard_map/ppermute | solution.py:489
  36.9 0.5 %collective-permute-start.12 = (f32[16,768]{1,0:T(8,128)S(1)}, f32[16,768]{1,0:T(8,128)S(1)}, u32[]{:S(2)}, u32[]{:S(2)}) collective-permute-start(f32[16,768]{1,0:T(8,128)S(1)} %get-tuple-element.42), channel_id=1, source_target_pairs={{0,5},{1,4},{2,7},{3,6},{4,1},{5,0},{6,3},{7,2},{8,13},{9,12},{10,... | collective-permute-start | bytes 147464 | tf_op jit(solution)/shard_map/ppermute | solution.py:489
  37.4 0.9 %shard_map.56.refs_4_ = f32[16,512]{1,0:T(8,128)S(1)} custom-call(bf16[480,512]{1,0:T(8,128)(2,1)S(1)} %copy-done, bf16[16,480]{1,0:T(8,128)(2,1)S(1)} %get-tuple-element.43.mask_ref, f32[4,16,768]{2,1,0:T(8,128)S(1)} %get-tuple-element.38.after), custom_call_target="tpu_custom_call" | custom-call | flops 15728640 | bytes 491520 | tf_op jit(solution)/shard_map/pallas_call | solution.py:543
  38.3 1.2 %collective-permute-done.11.refs_2_ = f32[16,768]{1,0:T(8,128)S(1)} collective-permute-done((f32[16,768]{1,0:T(8,128)S(1)}, f32[16,768]{1,0:T(8,128)S(1)}, u32[]{:S(2)}, u32[]{:S(2)}) %collective-permute-start.11) | collective-permute-done | bytes 49184 | tf_op jit(solution)/shard_map/ppermute | solution.py:489
  39.5 2.4 %collective-permute-done.12.refs_3_ = f32[16,768]{1,0:T(8,128)S(1)} collective-permute-done((f32[16,768]{1,0:T(8,128)S(1)}, f32[16,768]{1,0:T(8,128)S(1)}, u32[]{:S(2)}, u32[]{:S(2)}) %collective-permute-start.12) | collective-permute-done | bytes 49184 | tf_op jit(solution)/shard_map/ppermute | solution.py:489
  41.9 0.7 %shard_map.57 = f32[16,512]{1,0:T(8,128)} custom-call(f32[16,768]{1,0:T(8,128)S(1)} %get-tuple-element.39.refs_0_, f32[16,768]{1,0:T(8,128)S(1)} %collective-permute-done.10.refs_1_, f32[16,768]{1,0:T(8,128)S(1)} %collective-permute-done.11.refs_2_, f32[16,768]{1,0:T(8,128)S(1)} %collective-permute-done.12.refs_3_, f32[16,512]{1,0:T(8,128)S(1)} %shard_map.56.refs_4_, ...), custom_call_target="tpu_custom_call" | custom-call | bytes 196608 | tf_op jit(solution)/shard_map/pallas_call | solution.py:557
  (18 shorter events, 0.3 us)
Async XLA Ops:
  2.0 1.8 %collective-permute-start = (bf16[1280,128]{1,0:T(8,128)(2,1)S(1)}, bf16[1280,128]{1,0:T(8,128)(2,1)S(1)}, u32[]{:S(2)}, u32[]{:S(2)}) collective-permute-start(bf16[1280,128]{1,0:T(8,128)(2,1)S(1)} %get-tuple-element.26), channel_id=1, source_target_pairs={{0,2},{2,0},{4,6},{6,4},{1,3},{3,1},{5,7},{7,5},{8,10},{10,8},{12,... | collective-permute-start | bytes 983048 | tf_op jit(solution)/shard_map/ppermute | solution.py:463
  3.9 13.5 %collective-permute-start.5 = (bf16[2,64,512]{2,1,0:T(8,128)(2,1)S(1)}, bf16[2,64,512]{2,1,0:T(8,128)(2,1)S(1)}, u32[]{:S(2)}, u32[]{:S(2)}) collective-permute-start(bf16[2,64,512]{2,1,0:T(8,128)(2,1)S(1)} %get-tuple-element.31), channel_id=1, source_target_pairs={{0,1},{1,0},{2,3},{3,2},{4,5},{5,4},{6,7},{7,6},{8,9},{9,8},{10,11... | collective-permute-start | bytes 393224 | tf_op jit(solution)/shard_map/ppermute | solution.py:489
  6.8 4.3 %collective-permute-start.1 = (bf16[2,128,128]{2,1,0:T(8,128)(2,1)S(1)}, bf16[2,128,128]{2,1,0:T(8,128)(2,1)S(1)}, u32[]{:S(2)}, u32[]{:S(2)}) collective-permute-start(bf16[2,128,128]{2,1,0:T(8,128)(2,1)S(1)} %get-tuple-element.28.after), channel_id=1, source_target_pairs={{0,4},{2,6},{4,0},{6,2},{1,5},{3,7},{5,1},{7,3},{8,12},{10,14},{12... | collective-permute-start | bytes 196616 | tf_op jit(solution)/shard_map/ppermute | solution.py:468
  11.1 7.8 %collective-permute-start.6 = (bf16[2,64,512]{2,1,0:T(8,128)(2,1)S(1)}, bf16[2,64,512]{2,1,0:T(8,128)(2,1)S(1)}, u32[]{:S(2)}, u32[]{:S(2)}) collective-permute-start(bf16[2,64,512]{2,1,0:T(8,128)(2,1)S(1)} %get-tuple-element.32), channel_id=1, source_target_pairs={{0,4},{1,5},{2,6},{3,7},{4,0},{5,1},{6,2},{7,3},{8,12},{9,13},{10,... | collective-permute-start | bytes 393224 | tf_op jit(solution)/shard_map/ppermute | solution.py:489
  12.7 6.3 %collective-permute-start.7 = (bf16[2,64,512]{2,1,0:T(8,128)(2,1)S(1)}, bf16[2,64,512]{2,1,0:T(8,128)(2,1)S(1)}, u32[]{:S(2)}, u32[]{:S(2)}) collective-permute-start(bf16[2,64,512]{2,1,0:T(8,128)(2,1)S(1)} %get-tuple-element.33), channel_id=1, source_target_pairs={{0,5},{1,4},{2,7},{3,6},{4,1},{5,0},{6,3},{7,2},{8,13},{9,12},{10,... | collective-permute-start | bytes 393224 | tf_op jit(solution)/shard_map/ppermute | solution.py:489
  12.8 7.6 %collective-permute-start.2 = (bf16[4,128,128]{2,1,0:T(8,128)(2,1)S(1)}, bf16[4,128,128]{2,1,0:T(8,128)(2,1)S(1)}, u32[]{:S(2)}, u32[]{:S(2)}) collective-permute-start(bf16[4,128,128]{2,1,0:T(8,128)(2,1)S(1)} %shard_map.48.after.refs_0_), channel_id=1, source_target_pairs={{0,8},{8,0},{16,24},{24,16},{1,9},{9,1},{17,25},{25,17},{2,10},{10... | collective-permute-start | bytes 393224 | tf_op jit(solution)/shard_map/ppermute | solution.py:471
  14.8 11.6 %collective-permute-start.3 = (bf16[4,128,128]{2,1,0:T(8,128)(2,1)S(1)}, bf16[4,128,128]{2,1,0:T(8,128)(2,1)S(1)}, u32[]{:S(2)}, u32[]{:S(2)}) collective-permute-start(bf16[4,128,128]{2,1,0:T(8,128)(2,1)S(1)} %shard_map.48.after.refs_0_), channel_id=1, source_target_pairs={{0,16},{8,24},{16,0},{24,8},{1,17},{9,25},{17,1},{25,9},{2,18},{10... | collective-permute-start | bytes 393224 | tf_op jit(solution)/shard_map/ppermute | solution.py:471
  17.4 9.0 %collective-permute-start.4 = (bf16[4,128,128]{2,1,0:T(8,128)(2,1)S(1)}, bf16[4,128,128]{2,1,0:T(8,128)(2,1)S(1)}, u32[]{:S(2)}, u32[]{:S(2)}) collective-permute-start(bf16[4,128,128]{2,1,0:T(8,128)(2,1)S(1)} %shard_map.48.after.refs_0_), channel_id=1, source_target_pairs={{0,24},{8,16},{16,8},{24,0},{1,25},{9,17},{17,9},{25,1},{2,26},{10... | collective-permute-start | bytes 393224 | tf_op jit(solution)/shard_map/ppermute | solution.py:471
  19.1 11.4 %collective-permute-start.8 = (bf16[64,256]{1,0:T(8,128)(2,1)S(1)}, bf16[64,256]{1,0:T(8,128)(2,1)S(1)}, u32[]{:S(2)}, u32[]{:S(2)}) collective-permute-start(bf16[64,256]{1,0:T(8,128)(2,1)S(1)} %get-tuple-element.35), channel_id=1, source_target_pairs={{8,0},{16,8},{24,16},{9,1},{17,9},{25,17},{10,2},{18,10},{26,18},{... | collective-permute-start | bytes 98312 | tf_op jit(solution)/shard_map/ppermute | solution.py:498
  26.4 3.3 %copy-start.1 = (s32[480]{0:T(512)S(1)}, s32[480]{0:T(512)}, u32[]{:S(2)}) copy-start(s32[480]{0:T(512)} %param.7) | copy-start | bytes 5764
  30.4 7.0 %copy-start = (bf16[480,512]{1,0:T(8,128)(2,1)S(1)}, bf16[480,512]{1,0:T(8,128)(2,1)}, u32[]{:S(2)}) copy-start(bf16[480,512]{1,0:T(8,128)(2,1)} %wave_ref.1) | copy-start | bytes 1474564
  32.3 1.5 %collective-permute-start.9 = (f32[4,16,768]{2,1,0:T(8,128)S(1)}, f32[4,16,768]{2,1,0:T(8,128)S(1)}, u32[]{:S(2)}, u32[]{:S(2)}) collective-permute-start(f32[4,16,768]{2,1,0:T(8,128)S(1)} %get-tuple-element.38.after), channel_id=1, source_target_pairs={{0,2},{2,0},{4,6},{6,4},{1,3},{3,1},{5,7},{7,5},{8,10},{10,8},{12,... | collective-permute-start | bytes 589832 | tf_op jit(solution)/shard_map/ppermute | solution.py:542
  33.8 4.4 %collective-permute-start.10 = (f32[16,768]{1,0:T(8,128)S(1)}, f32[16,768]{1,0:T(8,128)S(1)}, u32[]{:S(2)}, u32[]{:S(2)}) collective-permute-start(f32[16,768]{1,0:T(8,128)S(1)} %get-tuple-element.40), channel_id=1, source_target_pairs={{0,1},{1,0},{2,3},{3,2},{4,5},{5,4},{6,7},{7,6},{8,9},{9,8},{10,11... | collective-permute-start | bytes 147464 | tf_op jit(solution)/shard_map/ppermute | solution.py:489
  35.4 4.1 %collective-permute-start.11 = (f32[16,768]{1,0:T(8,128)S(1)}, f32[16,768]{1,0:T(8,128)S(1)}, u32[]{:S(2)}, u32[]{:S(2)}) collective-permute-start(f32[16,768]{1,0:T(8,128)S(1)} %get-tuple-element.41), channel_id=1, source_target_pairs={{0,4},{1,5},{2,6},{3,7},{4,0},{5,1},{6,2},{7,3},{8,12},{9,13},{10,... | collective-permute-start | bytes 147464 | tf_op jit(solution)/shard_map/ppermute | solution.py:489
  36.9 5.0 %collective-permute-start.12 = (f32[16,768]{1,0:T(8,128)S(1)}, f32[16,768]{1,0:T(8,128)S(1)}, u32[]{:S(2)}, u32[]{:S(2)}) collective-permute-start(f32[16,768]{1,0:T(8,128)S(1)} %get-tuple-element.42), channel_id=1, source_target_pairs={{0,5},{1,4},{2,7},{3,6},{4,1},{5,0},{6,3},{7,2},{8,13},{9,12},{10,... | collective-permute-start | bytes 147464 | tf_op jit(solution)/shard_map/ppermute | solution.py:489

commit v12 on v11

--- a/solution.py
+++ b/solution.py
@@ -92,8 +92,8 @@
 
 
 def prologue_kernel(tm_count, wave_hbm, tpl_hbm, flag_hbm, order_hbm, *refs):
-    send_ref, samples_ref, tpls_ref = refs[:3]
-    wave_ref, grouped, tpl_ref, tpl_grouped, flag_ref, order_ref, turned, sems = refs[3:]
+    send_ref, samples_ref, *outs = refs[: INNER + 1]
+    wave_ref, grouped, tpl_ref, tpl_grouped, flag_ref, order_ref, turned, sems = refs[INNER + 1 :]
     channels, window = tpl_hbm.shape[1:]
     copies = [
         pltpu.make_async_copy(flag_hbm, flag_ref, sems.at[0]),
@@ -106,7 +106,7 @@
     stations = flag_ref.shape[1]
     padded = turned.shape[1]
     part = LANES // tm_count
-    rows = tpls_ref.shape[1]
+    rows = outs[0].shape[0]
     groups = regroup(channels, padded, part)
     copies[0].wait()
     copies[1].wait()
@@ -141,30 +141,26 @@
         preferred_element_type=F32,
     )
     my_tm = lax.axis_index("tm")
-    my_core = lax.rem(lax.axis_index("inner"), 2)
-    first = send_ref.shape[0] - 2 * rows
+    my_inner = lax.axis_index("inner")
+    my_core = lax.rem(my_inner, 2)
+    first = send_ref.shape[0] - rows
     spot = lax.broadcasted_iota(jnp.int32, (FINE, LANES), 1) >> (part.bit_length() - 1)
-    for member in range(INNER):
-        start = (member % 2 * (INNER // 2) + member // 2) * LANES
+    for flip in range(INNER):
+        start = pl.multiple_of(side_major(my_inner ^ flip) * LANES, LANES)
         pieces = []
         for step in range(window // (FINE * tm_count)):
             tile = jnp.zeros((FINE, LANES), F32)
             for within in range(tm_count):
                 row = FINE * (step * tm_count + within)
-                chunk = turned[row : row + FINE, start : start + LANES]
+                chunk = turned[row : row + FINE, pl.ds(start, LANES)]
                 turn = lax.rem(part * (within - my_tm) + LANES, LANES)
                 tile = jnp.where(spot == within, pltpu.roll(chunk, turn, 1), tile)
             pieces.append(tile)
         payload = (jnp.concatenate(pieces, axis=0) + meta).astype(BF16)
-        y, core = member // 2, member % 2
-
-        @pl.when(core == my_core)
-        def _():
-            tpls_ref[y] = payload
-
-        @pl.when(core != my_core)
-        def _():
-            send_ref[first + y * rows : first + (y + 1) * rows, :] = payload
+        if flip == 1:
+            send_ref[first:, :] = payload
+        else:
+            outs[flip - (flip > 1)][...] = payload
 
     copies[3].wait()
     regroup_rows(wave_ref, grouped, part)
@@ -176,29 +172,13 @@
         send_ref[tile * half : (tile + 1) * half, :] = grouped[theirs, columns]
 
 
-def plane_kernel(tpls_ref, got_ref, keep_ref, send_ref):
-    y, core = lax.div(lax.axis_index("inner"), 2), lax.rem(lax.axis_index("inner"), 2)
-    rows = tpls_ref.shape[1]
-    first = got_ref.shape[0] - 2 * rows
-    for side in range(2):
-        got = got_ref[first + side * rows : first + (side + 1) * rows, :]
-
-        @pl.when(side == y)
-        def _():
-            keep_ref[core] = tpls_ref[side]
-            keep_ref[1 - core] = got
-
-        @pl.when(side != y)
-        def _():
-            send_ref[core] = tpls_ref[side]
-            send_ref[1 - core] = got
-
-
-def pack_kernel(keep_ref, got_ref, out_ref):
-    y = lax.div(lax.axis_index("inner"), 2)
-    for core in range(2):
-        out_ref[2 * y + core] = keep_ref[core]
-        out_ref[2 * (1 - y) + core] = got_ref[core]
+def pack_kernel(mine_ref, core_ref, y_ref, both_ref, out_ref):
+    inner = lax.axis_index("inner")
+    rows = mine_ref.shape[0]
+    out_ref[inner] = mine_ref[...]
+    out_ref[inner ^ 1] = core_ref[core_ref.shape[0] - rows :, :]
+    out_ref[inner ^ 2] = y_ref[...]
+    out_ref[inner ^ 3] = both_ref[...]
 
 
 def split_kernel(tm_count, flips, keep_ref, got_ref, after, *outs):
@@ -229,8 +209,9 @@
     head_ref[...] = out_ref[:, : head_ref.shape[1]]
 
 
-def arrival(template):
-    return template ^ (lax.axis_index("outer") * INNER)
+def arrival(template, count):
+    inner = template & (INNER - 1)
+    return ((lax.axis_index("outer") * INNER - (template - inner)) & (count - 1)) + inner
 
 
 def correlate(tpls, samples, out_ref, first, left, shifts, products):
@@ -247,7 +228,7 @@
     row = lax.broadcasted_iota(jnp.int32, (size, size), 0)
     column = lax.broadcasted_iota(jnp.int32, (size, size), 1)
     shift = count.bit_length() - 1
-    source = arrival(row & (count - 1)) * FINE + (row >> shift)
+    source = arrival(row & (count - 1), count) * FINE + (row >> shift)
     order = jnp.where(column == source, 1.0, 0.0).astype(BF16)
     for step in range(depth // LANES):
         rows = [
@@ -366,7 +347,7 @@
     )
     template = lax.broadcasted_iota(jnp.int32, (count, count), 0)
     place = lax.broadcasted_iota(jnp.int32, (count, count), 1)
-    sort = jnp.where(place == arrival(template), 1.0, 0.0).astype(BF16)
+    sort = jnp.where(place == arrival(template, count), 1.0, 0.0).astype(BF16)
     slots = -(-stations // rows)
 
     def read(slot):
@@ -439,13 +420,13 @@
         pltpu.with_memory_space_constraint(x, pltpu.HBM)
         for x in (waveforms, templates, station_mask, order_row)
     ]
-    send, keep, pieces = call(
+    send, keep, *pieces = call(
         functools.partial(prologue_kernel, tm_count),
         [HBM] * 4,
         [
-            sds((padded // 2 * slab // LANES + 2 * rows, LANES), BF16),
+            sds((padded // 2 * slab // LANES + rows, LANES), BF16),
             sds((padded // 2, slab), BF16),
-            sds((2, rows, LANES), BF16),
+            *[sds((rows, LANES), BF16)] * (INNER - 1),
         ],
         [
             pltpu.VMEM((channels, slab), BF16),
@@ -460,17 +441,21 @@
         bytes_accessed=channels * (window + slab) * 2,
     )(*held)
 
-    got = lax.ppermute(send, "inner", [(b, b ^ 1) for b in range(INNER)])
-
-    ours, theirs = call(
-        plane_kernel, [VMEM] * 2, [sds((2, rows, LANES), BF16)] * 2, bytes_accessed=rows * LANES * 8
-    )(pieces, got)
-    others = lax.ppermute(theirs, "inner", [(b, b ^ 2) for b in range(INNER)])
-    pack = call(pack_kernel, [VMEM] * 2, sds((INNER, rows, LANES), BF16))(ours, others)
-    tpls = [pack] + [
-        lax.ppermute(pack, "outer", [(b, b ^ flip) for b in range(outer_count)])
-        for flip in range(1, outer_count)
-    ]
+    def plane(part, flip):
+        return lax.ppermute(part, "inner", [(b, b ^ flip) for b in range(INNER)])
+
+    got = plane(send, 1)
+    others = [plane(pieces[1], 2), plane(pieces[2], 3)]
+    pack = call(
+        pack_kernel, [VMEM] * INNER, sds((INNER, rows, LANES), BF16), bytes_accessed=rows * LANES * 8
+    )(pieces[0], got, *others)
+
+    def shift(distance):
+        return lax.ppermute(
+            pack, "outer", [(b, (b + distance) % outer_count) for b in range(outer_count)]
+        )
+
+    tpls = [pack] + [shift(distance) for distance in range(1, outer_count)]
 
     half = group // 2
     def split(flips, after):
@@ -481,7 +466,7 @@
             bytes_accessed=padded * slab * 2,
         )(keep, got, after)
 
-    parts = split(range(tm_count), theirs) + split(range(tm_count, half), pack)
+    parts = split(range(tm_count), got) + split(range(tm_count, half), tpls[1])
 
     def swap(part, flip):
         y, tm = flip // tm_count, flip % tm_count

time: 42.7 us -> 43.2 us (1.012)
  starting transfers between devices: 16.1 us -> 17.3 us
  waiting for transfers between devices: 16.7 us -> 16.2 us
    ppermute x6, waiting for transfers between devices: 5.25 us -> 3.32 us  [swap(): return lax.ppermute(part, every, route)]
    ppermute x4 -> x6, starting transfers between devices: 6.12 us -> 7.85 us  [the longest x3 4.67 us: shift(): lax.ppermute(pack, 'outer', [(b, (b + distance) % outer_count) for b in r...]
    ppermute x1, waiting for transfers between devices: 0.01 us -> 1.64 us  [on_device(): lax.ppermute(head, 'outer', [(b, b - 1) for b in range(1, outer_count)])]
    ppermute x2 -> x1, waiting for transfers between devices: 2.68 us -> 1.43 us  [on_device(): got = lax.ppermute(send, 'inner', [(b, b ^ 1) for b in range(INNER)])]
    ppermute x4 -> x6, waiting for transfers between devices: 8.79 us -> 9.85 us  [the longest x3 6.58 us: shift(): lax.ppermute(pack, 'outer', [(b, (b + distance) % outer_count) for b in r...]
    ppermute x2 -> x1, starting transfers between devices: 0.59 us -> 0.07 us  [on_device(): got = lax.ppermute(send, 'inner', [(b, b ^ 1) for b in range(INNER)])]
  transfers between devices with their start and end apart: 13 -> 14, of which waited for: 7 -> 8; matrix products, arithmetic and copies ran while one was open for 0% -> 0% of each run, Pallas kernels for 12% -> 11%
where the time goes in v12:
time: 43.2 us; the launch traced here: 43 us
  starting transfers between devices  17.3 us (40%)
  waiting for transfers between devices  16.2 us (38%)
  Pallas kernels  9.27 us (21%)
    ppermute x6, starting transfers between devices, swap(): return lax.ppermute(part, every, route)  8.13 us
    ppermute x3, waiting for transfers between devices, shift(): lax.ppermute(pack, 'outer', [(b, (b + distance) % outer_count) for b in r...  6.58 us
    ppermute x3, starting transfers between devices, shift(): lax.ppermute(pack, 'outer', [(b, (b + distance) % outer_count) for b in r...  4.67 us
    ppermute x6, waiting for transfers between devices, swap(): return lax.ppermute(part, every, route)  3.32 us
    pallas_call x1, Pallas kernels, on_device(): call(first_dots_kernel, [VMEM] * (outer_count + 1), sds((2 * (blocks - 1)...  3.29 us
    ppermute x3, waiting for transfers between devices, plane(): return lax.ppermute(part, 'inner', [(b, b ^ flip) for b in range(INNER)])  3.28 us
    ppermute x3, starting transfers between devices, plane(): return lax.ppermute(part, 'inner', [(b, b ^ flip) for b in range(INNER)])  3.18 us
    pallas_call x1, Pallas kernels, on_device(): call(last_dots_kernel, [VMEM] * (outer_count + 4), [sds((half, blk_count,...  1.87 us
  transfers between devices with their start and end apart: 14, of which 8 were waited for; matrix products, arithmetic and copies ran while one was open for 0% of the time, Pallas kernels for 11%

profile of v12, /device:TPU:0, one launch (start us, length us, event | category | flops | bytes accessed | tf_op | source)
XLA Modules:
  0.0 43.0 jit_solution(1893563544698489973)
XLA Ops:
  0.0 1.7 %shard_map.46 = (bf16[1152,128]{1,0:T(8,128)(2,1)S(1)}, bf16[256,512]{1,0:T(8,128)(2,1)S(1)}, bf16[128,128]{1,0:T(8,128)(2,1)S(1)}, bf16[128,128]{1,0:T(8,128)(2,1)S(1)}, bf16[128,128]{1,0:T(8,128)(2,1)S(1)}) custom-call(bf16[480,512]{1,0:T(8,128)(2,1)} %wave_ref.1, bf16[1,480,256]{2,1,0:T(8,128)(2,1)} %tpl_hbm.1, s32[1,160]{1,0:T(1,128)} %flag_hbm.1, ...), custom_call_target="tpu_custom_call" | custom-call | bytes 737280 | tf_op jit(solution)/shard_map/pallas_call | solution.py:423
  2.2 2.6 %collective-permute-start.1 = (bf16[128,128]{1,0:T(8,128)(2,1)S(1)}, bf16[128,128]{1,0:T(8,128)(2,1)S(1)}, u32[]{:S(2)}, u32[]{:S(2)}) collective-permute-start(bf16[128,128]{1,0:T(8,128)(2,1)S(1)} %get-tuple-element.27), channel_id=1, source_target_pairs={{0,4},{2,6},{4,0},{6,2},{1,5},{3,7},{5,1},{7,3},{8,12},{10,14},{12... | collective-permute-start | bytes 98312 | tf_op jit(solution)/shard_map/ppermute | solution.py:445
  4.9 1.9 %collective-permute-done.1.y_ref = bf16[128,128]{1,0:T(8,128)(2,1)S(1)} collective-permute-done((bf16[128,128]{1,0:T(8,128)(2,1)S(1)}, bf16[128,128]{1,0:T(8,128)(2,1)S(1)}, u32[]{:S(2)}, u32[]{:S(2)}) %collective-permute-start.1) | collective-permute-done | bytes 32800 | tf_op jit(solution)/shard_map/ppermute | solution.py:445
  6.8 1.4 %collective-permute-done.2.both_ref = bf16[128,128]{1,0:T(8,128)(2,1)S(1)} collective-permute-done((bf16[128,128]{1,0:T(8,128)(2,1)S(1)}, bf16[128,128]{1,0:T(8,128)(2,1)S(1)}, u32[]{:S(2)}, u32[]{:S(2)}) %collective-permute-start.2) | collective-permute-done | bytes 32800 | tf_op jit(solution)/shard_map/ppermute | solution.py:445
  8.2 1.6 %collective-permute-start.3 = (bf16[4,128,128]{2,1,0:T(8,128)(2,1)S(1)}, bf16[4,128,128]{2,1,0:T(8,128)(2,1)S(1)}, u32[]{:S(2)}, u32[]{:S(2)}) collective-permute-start(bf16[4,128,128]{2,1,0:T(8,128)(2,1)S(1)} %shard_map.47.refs_0_), channel_id=1, source_target_pairs={{0,8},{8,16},{16,24},{24,0},{1,9},{9,17},{17,25},{25,1},{2,10},{10... | collective-permute-start | bytes 393224 | tf_op jit(solution)/shard_map/ppermute | solution.py:454
  9.8 2.2 %collective-permute-start.5 = (bf16[4,128,128]{2,1,0:T(8,128)(2,1)S(1)}, bf16[4,128,128]{2,1,0:T(8,128)(2,1)S(1)}, u32[]{:S(2)}, u32[]{:S(2)}) collective-permute-start(bf16[4,128,128]{2,1,0:T(8,128)(2,1)S(1)} %shard_map.47.refs_0_), channel_id=1, source_target_pairs={{0,24},{8,0},{16,8},{24,16},{1,25},{9,1},{17,9},{25,17},{2,26},{10... | collective-permute-start | bytes 393224 | tf_op jit(solution)/shard_map/ppermute | solution.py:454
  12.1 0.8 %collective-permute-start.4 = (bf16[4,128,128]{2,1,0:T(8,128)(2,1)S(1)}, bf16[4,128,128]{2,1,0:T(8,128)(2,1)S(1)}, u32[]{:S(2)}, u32[]{:S(2)}) collective-permute-start(bf16[4,128,128]{2,1,0:T(8,128)(2,1)S(1)} %shard_map.47.refs_0_), channel_id=1, source_target_pairs={{0,16},{8,24},{16,0},{24,8},{1,17},{9,25},{17,1},{25,9},{2,18},{10... | collective-permute-start | bytes 393224 | tf_op jit(solution)/shard_map/ppermute | solution.py:454
  12.9 1.6 %collective-permute-start.6 = (bf16[2,64,512]{2,1,0:T(8,128)(2,1)S(1)}, bf16[2,64,512]{2,1,0:T(8,128)(2,1)S(1)}, u32[]{:S(2)}, u32[]{:S(2)}) collective-permute-start(bf16[2,64,512]{2,1,0:T(8,128)(2,1)S(1)} %get-tuple-element.31), channel_id=1, source_target_pairs={{0,1},{1,0},{2,3},{3,2},{4,5},{5,4},{6,7},{7,6},{8,9},{9,8},{10,11... | collective-permute-start | bytes 393224 | tf_op jit(solution)/shard_map/ppermute | solution.py:474
  14.4 1.9 %collective-permute-done.3.after.refs_1_ = bf16[4,128,128]{2,1,0:T(8,128)(2,1)S(1)} collective-permute-done((bf16[4,128,128]{2,1,0:T(8,128)(2,1)S(1)}, bf16[4,128,128]{2,1,0:T(8,128)(2,1)S(1)}, u32[]{:S(2)}, u32[]{:S(2)}) %collective-permute-start.3) | collective-permute-done | bytes 131104 | tf_op jit(solution)/shard_map/ppermute | solution.py:454
  16.4 0.8 %collective-permute-start.7 = (bf16[2,64,512]{2,1,0:T(8,128)(2,1)S(1)}, bf16[2,64,512]{2,1,0:T(8,128)(2,1)S(1)}, u32[]{:S(2)}, u32[]{:S(2)}) collective-permute-start(bf16[2,64,512]{2,1,0:T(8,128)(2,1)S(1)} %get-tuple-element.32), channel_id=1, source_target_pairs={{0,4},{1,5},{2,6},{3,7},{4,0},{5,1},{6,2},{7,3},{8,12},{9,13},{10,... | collective-permute-start | bytes 393224 | tf_op jit(solution)/shard_map/ppermute | solution.py:474
  17.3 2.2 %collective-permute-start.8 = (bf16[2,64,512]{2,1,0:T(8,128)(2,1)S(1)}, bf16[2,64,512]{2,1,0:T(8,128)(2,1)S(1)}, u32[]{:S(2)}, u32[]{:S(2)}) collective-permute-start(bf16[2,64,512]{2,1,0:T(8,128)(2,1)S(1)} %get-tuple-element.33), channel_id=1, source_target_pairs={{0,5},{1,4},{2,7},{3,6},{4,1},{5,0},{6,3},{7,2},{8,13},{9,12},{10,... | collective-permute-start | bytes 393224 | tf_op jit(solution)/shard_map/ppermute | solution.py:474
  19.5 4.6 %collective-permute-done.4.refs_2_ = bf16[4,128,128]{2,1,0:T(8,128)(2,1)S(1)} collective-permute-done((bf16[4,128,128]{2,1,0:T(8,128)(2,1)S(1)}, bf16[4,128,128]{2,1,0:T(8,128)(2,1)S(1)}, u32[]{:S(2)}, u32[]{:S(2)}) %collective-permute-start.4) | collective-permute-done | bytes 131104 | tf_op jit(solution)/shard_map/ppermute | solution.py:454
  24.1 0.7 %shard_map.51 = (f32[16,128]{1,0:T(8,128)S(1)}, bf16[16,480]{1,0:T(8,128)(2,1)S(1)}, bf16[16,64]{1,0:T(8,128)(2,1)S(1)}) custom-call(bf16[4,128,128]{2,1,0:T(8,128)(2,1)S(1)} %shard_map.47.refs_0_, bf16[4,128,128]{2,1,0:T(8,128)(2,1)S(1)} %collective-permute-done.3.after.refs_1_, bf16[4,128,128]{2,1,0:T(8,128)(2,1)S(1)} %collective-permute-done.4.refs_2_, ...), custom_call_target="tpu_custom_call" | custom-call | bytes 524288 | tf_op jit(solution)/shard_map/pallas_call | solution.py:485
  24.9 1.3 %collective-permute-start.9 = (bf16[64,256]{1,0:T(8,128)(2,1)S(1)}, bf16[64,256]{1,0:T(8,128)(2,1)S(1)}, u32[]{:S(2)}, u32[]{:S(2)}) collective-permute-start(bf16[64,256]{1,0:T(8,128)(2,1)S(1)} %get-tuple-element.35), channel_id=1, source_target_pairs={{8,0},{16,8},{24,16},{9,1},{17,9},{25,17},{10,2},{18,10},{26,18},{... | collective-permute-start | bytes 98312 | tf_op jit(solution)/shard_map/ppermute | solution.py:483
  26.2 3.3 %shard_map.52.refs_7_ = f32[6,16,512]{2,1,0:T(8,128)S(1)} custom-call(bf16[4,128,128]{2,1,0:T(8,128)(2,1)S(1)} %shard_map.47.refs_0_, bf16[4,128,128]{2,1,0:T(8,128)(2,1)S(1)} %collective-permute-done.3.after.refs_1_, bf16[4,128,128]{2,1,0:T(8,128)(2,1)S(1)} %collective-permute-done.4.refs_2_, bf16[4,128,128]{2,1,0:T(8,128)(2,1)S(1)} %collective-permute-done.5.refs_3_, ...), custom_call_target="tpu_custom_call" | custom-call | flops 1610612736 | bytes 524288 | tf_op jit(solution)/shard_map/pallas_call | solution.py:507
  29.5 1.6 %collective-permute-done.9.refs_5_ = bf16[64,256]{1,0:T(8,128)(2,1)S(1)} collective-permute-done((bf16[64,256]{1,0:T(8,128)(2,1)S(1)}, bf16[64,256]{1,0:T(8,128)(2,1)S(1)}, u32[]{:S(2)}, u32[]{:S(2)}) %collective-permute-start.9) | collective-permute-done | bytes 32800 | tf_op jit(solution)/shard_map/ppermute | solution.py:483
  31.1 1.9 %shard_map.53 = (f32[4,16,768]{2,1,0:T(8,128)S(1)}, f32[4,16,768]{2,1,0:T(8,128)S(1)}) custom-call(bf16[4,128,128]{2,1,0:T(8,128)(2,1)S(1)} %shard_map.47.refs_0_, bf16[4,128,128]{2,1,0:T(8,128)(2,1)S(1)} %collective-permute-done.3.after.refs_1_, bf16[4,128,128]{2,1,0:T(8,128)(2,1)S(1)} %collective-permute-done.4.refs_2_, ...), custom_call_target="tpu_custom_call" | custom-call | flops 536870912 | bytes 524288 | tf_op jit(solution)/shard_map/pallas_call | solution.py:515
  33.1 1.4 %collective-permute-done.10.got_ref = f32[4,16,768]{2,1,0:T(8,128)S(1)} collective-permute-done((f32[4,16,768]{2,1,0:T(8,128)S(1)}, f32[4,16,768]{2,1,0:T(8,128)S(1)}, u32[]{:S(2)}, u32[]{:S(2)}) %collective-permute-start.10) | collective-permute-done | bytes 196640 | tf_op jit(solution)/shard_map/ppermute | solution.py:527
  34.6 1.6 %collective-permute-start.11 = (f32[16,768]{1,0:T(8,128)S(1)}, f32[16,768]{1,0:T(8,128)S(1)}, u32[]{:S(2)}, u32[]{:S(2)}) collective-permute-start(f32[16,768]{1,0:T(8,128)S(1)} %get-tuple-element.40), channel_id=1, source_target_pairs={{0,1},{1,0},{2,3},{3,2},{4,5},{5,4},{6,7},{7,6},{8,9},{9,8},{10,11... | collective-permute-start | bytes 147464 | tf_op jit(solution)/shard_map/ppermute | solution.py:474
  36.1 1.2 %collective-permute-start.12 = (f32[16,768]{1,0:T(8,128)S(1)}, f32[16,768]{1,0:T(8,128)S(1)}, u32[]{:S(2)}, u32[]{:S(2)}) collective-permute-start(f32[16,768]{1,0:T(8,128)S(1)} %get-tuple-element.41), channel_id=1, source_target_pairs={{0,4},{1,5},{2,6},{3,7},{4,0},{5,1},{6,2},{7,3},{8,12},{9,13},{10,... | collective-permute-start | bytes 147464 | tf_op jit(solution)/shard_map/ppermute | solution.py:474
  37.3 0.8 %collective-permute-start.13 = (f32[16,768]{1,0:T(8,128)S(1)}, f32[16,768]{1,0:T(8,128)S(1)}, u32[]{:S(2)}, u32[]{:S(2)}) collective-permute-start(f32[16,768]{1,0:T(8,128)S(1)} %get-tuple-element.42), channel_id=1, source_target_pairs={{0,5},{1,4},{2,7},{3,6},{4,1},{5,0},{6,3},{7,2},{8,13},{9,12},{10,... | collective-permute-start | bytes 147464 | tf_op jit(solution)/shard_map/ppermute | solution.py:474
  38.1 0.9 %shard_map.55.refs_4_ = f32[16,512]{1,0:T(8,128)S(1)} custom-call(bf16[480,512]{1,0:T(8,128)(2,1)S(1)} %copy-done, bf16[16,480]{1,0:T(8,128)(2,1)S(1)} %get-tuple-element.43.mask_ref, f32[4,16,768]{2,1,0:T(8,128)S(1)} %get-tuple-element.38.after), custom_call_target="tpu_custom_call" | custom-call | flops 15728640 | bytes 491520 | tf_op jit(solution)/shard_map/pallas_call | solution.py:528
  39.0 1.2 %collective-permute-done.12.refs_2_ = f32[16,768]{1,0:T(8,128)S(1)} collective-permute-done((f32[16,768]{1,0:T(8,128)S(1)}, f32[16,768]{1,0:T(8,128)S(1)}, u32[]{:S(2)}, u32[]{:S(2)}) %collective-permute-start.12) | collective-permute-done | bytes 49184 | tf_op jit(solution)/shard_map/ppermute | solution.py:474
  40.2 2.1 %collective-permute-done.13.refs_3_ = f32[16,768]{1,0:T(8,128)S(1)} collective-permute-done((f32[16,768]{1,0:T(8,128)S(1)}, f32[16,768]{1,0:T(8,128)S(1)}, u32[]{:S(2)}, u32[]{:S(2)}) %collective-permute-start.13) | collective-permute-done | bytes 49184 | tf_op jit(solution)/shard_map/ppermute | solution.py:474
  (19 shorter events, 1.5 us)
Async XLA Ops:
  1.7 6.5 %collective-permute-start = (bf16[1152,128]{1,0:T(8,128)(2,1)S(1)}, bf16[1152,128]{1,0:T(8,128)(2,1)S(1)}, u32[]{:S(2)}, u32[]{:S(2)}) collective-permute-start(bf16[1152,128]{1,0:T(8,128)(2,1)S(1)} %get-tuple-element.26), channel_id=1, source_target_pairs={{0,2},{2,0},{4,6},{6,4},{1,3},{3,1},{5,7},{7,5},{8,10},{10,8},{12,... | collective-permute-start | bytes 884744 | tf_op jit(solution)/shard_map/ppermute | solution.py:445
  2.2 4.6 %collective-permute-start.1 = (bf16[128,128]{1,0:T(8,128)(2,1)S(1)}, bf16[128,128]{1,0:T(8,128)(2,1)S(1)}, u32[]{:S(2)}, u32[]{:S(2)}) collective-permute-start(bf16[128,128]{1,0:T(8,128)(2,1)S(1)} %get-tuple-element.27), channel_id=1, source_target_pairs={{0,4},{2,6},{4,0},{6,2},{1,5},{3,7},{5,1},{7,3},{8,12},{10,14},{12... | collective-permute-start | bytes 98312 | tf_op jit(solution)/shard_map/ppermute | solution.py:445
  4.8 3.3 %collective-permute-start.2 = (bf16[128,128]{1,0:T(8,128)(2,1)S(1)}, bf16[128,128]{1,0:T(8,128)(2,1)S(1)}, u32[]{:S(2)}, u32[]{:S(2)}) collective-permute-start(bf16[128,128]{1,0:T(8,128)(2,1)S(1)} %get-tuple-element.28), channel_id=1, source_target_pairs={{0,6},{2,4},{4,2},{6,0},{1,7},{3,5},{5,3},{7,1},{8,14},{10,12},{12... | collective-permute-start | bytes 98312 | tf_op jit(solution)/shard_map/ppermute | solution.py:445
  8.2 8.2 %collective-permute-start.3 = (bf16[4,128,128]{2,1,0:T(8,128)(2,1)S(1)}, bf16[4,128,128]{2,1,0:T(8,128)(2,1)S(1)}, u32[]{:S(2)}, u32[]{:S(2)}) collective-permute-start(bf16[4,128,128]{2,1,0:T(8,128)(2,1)S(1)} %shard_map.47.refs_0_), channel_id=1, source_target_pairs={{0,8},{8,16},{16,24},{24,0},{1,9},{9,17},{17,25},{25,1},{2,10},{10... | collective-permute-start | bytes 393224 | tf_op jit(solution)/shard_map/ppermute | solution.py:454
  9.8 9.6 %collective-permute-start.5 = (bf16[4,128,128]{2,1,0:T(8,128)(2,1)S(1)}, bf16[4,128,128]{2,1,0:T(8,128)(2,1)S(1)}, u32[]{:S(2)}, u32[]{:S(2)}) collective-permute-start(bf16[4,128,128]{2,1,0:T(8,128)(2,1)S(1)} %shard_map.47.refs_0_), channel_id=1, source_target_pairs={{0,24},{8,0},{16,8},{24,16},{1,25},{9,1},{17,9},{25,17},{2,26},{10... | collective-permute-start | bytes 393224 | tf_op jit(solution)/shard_map/ppermute | solution.py:454
  12.1 12.0 %collective-permute-start.4 = (bf16[4,128,128]{2,1,0:T(8,128)(2,1)S(1)}, bf16[4,128,128]{2,1,0:T(8,128)(2,1)S(1)}, u32[]{:S(2)}, u32[]{:S(2)}) collective-permute-start(bf16[4,128,128]{2,1,0:T(8,128)(2,1)S(1)} %shard_map.47.refs_0_), channel_id=1, source_target_pairs={{0,16},{8,24},{16,0},{24,8},{1,17},{9,25},{17,1},{25,9},{2,18},{10... | collective-permute-start | bytes 393224 | tf_op jit(solution)/shard_map/ppermute | solution.py:454
  12.9 11.9 %collective-permute-start.6 = (bf16[2,64,512]{2,1,0:T(8,128)(2,1)S(1)}, bf16[2,64,512]{2,1,0:T(8,128)(2,1)S(1)}, u32[]{:S(2)}, u32[]{:S(2)}) collective-permute-start(bf16[2,64,512]{2,1,0:T(8,128)(2,1)S(1)} %get-tuple-element.31), channel_id=1, source_target_pairs={{0,1},{1,0},{2,3},{3,2},{4,5},{5,4},{6,7},{7,6},{8,9},{9,8},{10,11... | collective-permute-start | bytes 393224 | tf_op jit(solution)/shard_map/ppermute | solution.py:474
  16.4 7.7 %copy-start.1 = (s32[480]{0:T(512)S(1)}, s32[480]{0:T(512)}, u32[]{:S(2)}) copy-start(s32[480]{0:T(512)} %param.7) | copy-start | bytes 5764
  16.4 8.4 %collective-permute-start.7 = (bf16[2,64,512]{2,1,0:T(8,128)(2,1)S(1)}, bf16[2,64,512]{2,1,0:T(8,128)(2,1)S(1)}, u32[]{:S(2)}, u32[]{:S(2)}) collective-permute-start(bf16[2,64,512]{2,1,0:T(8,128)(2,1)S(1)} %get-tuple-element.32), channel_id=1, source_target_pairs={{0,4},{1,5},{2,6},{3,7},{4,0},{5,1},{6,2},{7,3},{8,12},{9,13},{10,... | collective-permute-start | bytes 393224 | tf_op jit(solution)/shard_map/ppermute | solution.py:474
  17.3 7.6 %collective-permute-start.8 = (bf16[2,64,512]{2,1,0:T(8,128)(2,1)S(1)}, bf16[2,64,512]{2,1,0:T(8,128)(2,1)S(1)}, u32[]{:S(2)}, u32[]{:S(2)}) collective-permute-start(bf16[2,64,512]{2,1,0:T(8,128)(2,1)S(1)} %get-tuple-element.33), channel_id=1, source_target_pairs={{0,5},{1,4},{2,7},{3,6},{4,1},{5,0},{6,3},{7,2},{8,13},{9,12},{10,... | collective-permute-start | bytes 393224 | tf_op jit(solution)/shard_map/ppermute | solution.py:474
  24.9 6.2 %collective-permute-start.9 = (bf16[64,256]{1,0:T(8,128)(2,1)S(1)}, bf16[64,256]{1,0:T(8,128)(2,1)S(1)}, u32[]{:S(2)}, u32[]{:S(2)}) collective-permute-start(bf16[64,256]{1,0:T(8,128)(2,1)S(1)} %get-tuple-element.35), channel_id=1, source_target_pairs={{8,0},{16,8},{24,16},{9,1},{17,9},{25,17},{10,2},{18,10},{26,18},{... | collective-permute-start | bytes 98312 | tf_op jit(solution)/shard_map/ppermute | solution.py:483
  31.1 7.0 %copy-start = (bf16[480,512]{1,0:T(8,128)(2,1)S(1)}, bf16[480,512]{1,0:T(8,128)(2,1)}, u32[]{:S(2)}) copy-start(bf16[480,512]{1,0:T(8,128)(2,1)} %wave_ref.1) | copy-start | bytes 1474564
  33.0 1.5 %collective-permute-start.10 = (f32[4,16,768]{2,1,0:T(8,128)S(1)}, f32[4,16,768]{2,1,0:T(8,128)S(1)}, u32[]{:S(2)}, u32[]{:S(2)}) collective-permute-start(f32[4,16,768]{2,1,0:T(8,128)S(1)} %get-tuple-element.38.after), channel_id=1, source_target_pairs={{0,2},{2,0},{4,6},{6,4},{1,3},{3,1},{5,7},{7,5},{8,10},{10,8},{12,... | collective-permute-start | bytes 589832 | tf_op jit(solution)/shard_map/ppermute | solution.py:527
  34.6 4.4 %collective-permute-start.11 = (f32[16,768]{1,0:T(8,128)S(1)}, f32[16,768]{1,0:T(8,128)S(1)}, u32[]{:S(2)}, u32[]{:S(2)}) collective-permute-start(f32[16,768]{1,0:T(8,128)S(1)} %get-tuple-element.40), channel_id=1, source_target_pairs={{0,1},{1,0},{2,3},{3,2},{4,5},{5,4},{6,7},{7,6},{8,9},{9,8},{10,11... | collective-permute-start | bytes 147464 | tf_op jit(solution)/shard_map/ppermute | solution.py:474
  36.1 4.1 %collective-permute-start.12 = (f32[16,768]{1,0:T(8,128)S(1)}, f32[16,768]{1,0:T(8,128)S(1)}, u32[]{:S(2)}, u32[]{:S(2)}) collective-permute-start(f32[16,768]{1,0:T(8,128)S(1)} %get-tuple-element.41), channel_id=1, source_target_pairs={{0,4},{1,5},{2,6},{3,7},{4,0},{5,1},{6,2},{7,3},{8,12},{9,13},{10,... | collective-permute-start | bytes 147464 | tf_op jit(solution)/shard_map/ppermute | solution.py:474
  37.3 5.0 %collective-permute-start.13 = (f32[16,768]{1,0:T(8,128)S(1)}, f32[16,768]{1,0:T(8,128)S(1)}, u32[]{:S(2)}, u32[]{:S(2)}) collective-permute-start(f32[16,768]{1,0:T(8,128)S(1)} %get-tuple-element.42), channel_id=1, source_target_pairs={{0,5},{1,4},{2,7},{3,6},{4,1},{5,0},{6,3},{7,2},{8,13},{9,12},{10,... | collective-permute-start | bytes 147464 | tf_op jit(solution)/shard_map/ppermute | solution.py:474

commit v13 on v12

--- a/solution.py
+++ b/solution.py
@@ -466,14 +466,15 @@
             bytes_accessed=padded * slab * 2,
         )(keep, got, after)
 
-    parts = split(range(tm_count), got) + split(range(tm_count, half), tpls[1])
-
     def swap(part, flip):
         y, tm = flip // tm_count, flip % tm_count
         route = [(i, i ^ (2 * tm_count * y + tm)) for i in range(total)]
         return lax.ppermute(part, every, route)
 
-    waves = [parts[0]] + [swap(parts[flip], flip) for flip in range(1, half)]
+    parts = split(range(tm_count), pack)
+    waves = [parts[0]] + [swap(parts[flip], flip) for flip in range(1, tm_count)]
+    parts += split(range(tm_count, half), waves[1])
+    waves += [swap(parts[flip], flip) for flip in range(tm_count, half)]
     samples, head = call(
         functools.partial(join_kernel, tm_count),
         [VMEM] * half,

time: 43.2 us -> 42 us (0.972)
  starting transfers between devices: 17.3 us -> 16.7 us
  waiting for transfers between devices: 16.2 us -> 15.7 us
    ppermute x6, waiting for transfers between devices: 3.32 us -> 2.02 us  [swap(): return lax.ppermute(part, every, route)]
    ppermute x3, waiting for transfers between devices: 6.58 us -> 7.74 us  [shift(): lax.ppermute(pack, 'outer', [(b, (b + distance) % outer_count) for b in r...]
    ppermute x6, starting transfers between devices: 8.13 us -> 7.58 us  [swap(): return lax.ppermute(part, every, route)]
    ppermute x1, waiting for transfers between devices: 1.64 us -> 1.21 us  [on_device(): lax.ppermute(head, 'outer', [(b, b - 1) for b in range(1, outer_count)])]
  transfers between devices with their start and end apart: 14 -> 14, of which waited for: 8 -> 8; matrix products, arithmetic and copies ran while one was open for 0% -> 0% of each run, Pallas kernels for 11% -> 12%
where the time goes in v13:
time: 42 us; the launch traced here: 41.8 us
  starting transfers between devices  16.7 us (40%)
  waiting for transfers between devices  15.7 us (37%)
  Pallas kernels  9.3 us (22%)
    ppermute x3, waiting for transfers between devices, shift(): lax.ppermute(pack, 'outer', [(b, (b + distance) % outer_count) for b in r...  7.74 us
    ppermute x6, starting transfers between devices, swap(): return lax.ppermute(part, every, route)  7.58 us
    ppermute x3, starting transfers between devices, shift(): lax.ppermute(pack, 'outer', [(b, (b + distance) % outer_count) for b in r...  4.62 us
    pallas_call x1, Pallas kernels, on_device(): call(first_dots_kernel, [VMEM] * (outer_count + 1), sds((2 * (blocks - 1)...  3.3 us
    ppermute x3, waiting for transfers between devices, plane(): return lax.ppermute(part, 'inner', [(b, b ^ flip) for b in range(INNER)])  3.28 us
    ppermute x3, starting transfers between devices, plane(): return lax.ppermute(part, 'inner', [(b, b ^ flip) for b in range(INNER)])  3.18 us
    ppermute x6, waiting for transfers between devices, swap(): return lax.ppermute(part, every, route)  2.02 us
    pallas_call x1, Pallas kernels, on_device(): call(last_dots_kernel, [VMEM] * (outer_count + 4), [sds((half, blk_count,...  1.88 us
  transfers between devices with their start and end apart: 14, of which 8 were waited for; matrix products, arithmetic and copies ran while one was open for 0% of the time, Pallas kernels for 12%

profile of v13, /device:TPU:0, one launch (start us, length us, event | category | flops | bytes accessed | tf_op | source)
XLA Modules:
  0.0 41.8 jit_solution(5221908989748113302)
XLA Ops:
  0.0 1.7 %shard_map.46 = (bf16[1152,128]{1,0:T(8,128)(2,1)S(1)}, bf16[256,512]{1,0:T(8,128)(2,1)S(1)}, bf16[128,128]{1,0:T(8,128)(2,1)S(1)}, bf16[128,128]{1,0:T(8,128)(2,1)S(1)}, bf16[128,128]{1,0:T(8,128)(2,1)S(1)}) custom-call(bf16[480,512]{1,0:T(8,128)(2,1)} %wave_ref.1, bf16[1,480,256]{2,1,0:T(8,128)(2,1)} %tpl_hbm.1, s32[1,160]{1,0:T(1,128)} %flag_hbm.1, ...), custom_call_target="tpu_custom_call" | custom-call | bytes 737280 | tf_op jit(solution)/shard_map/pallas_call | solution.py:423
  1.7 0.5 %collective-permute-start = (bf16[1152,128]{1,0:T(8,128)(2,1)S(1)}, bf16[1152,128]{1,0:T(8,128)(2,1)S(1)}, u32[]{:S(2)}, u32[]{:S(2)}) collective-permute-start(bf16[1152,128]{1,0:T(8,128)(2,1)S(1)} %get-tuple-element.26), channel_id=1, source_target_pairs={{0,2},{2,0},{4,6},{6,4},{1,3},{3,1},{5,7},{7,5},{8,10},{10,8},{12,... | collective-permute-start | bytes 884744 | tf_op jit(solution)/shard_map/ppermute | solution.py:445
  2.2 2.6 %collective-permute-start.1 = (bf16[128,128]{1,0:T(8,128)(2,1)S(1)}, bf16[128,128]{1,0:T(8,128)(2,1)S(1)}, u32[]{:S(2)}, u32[]{:S(2)}) collective-permute-start(bf16[128,128]{1,0:T(8,128)(2,1)S(1)} %get-tuple-element.27), channel_id=1, source_target_pairs={{0,4},{2,6},{4,0},{6,2},{1,5},{3,7},{5,1},{7,3},{8,12},{10,14},{12... | collective-permute-start | bytes 98312 | tf_op jit(solution)/shard_map/ppermute | solution.py:445
  4.9 1.9 %collective-permute-done.1.y_ref = bf16[128,128]{1,0:T(8,128)(2,1)S(1)} collective-permute-done((bf16[128,128]{1,0:T(8,128)(2,1)S(1)}, bf16[128,128]{1,0:T(8,128)(2,1)S(1)}, u32[]{:S(2)}, u32[]{:S(2)}) %collective-permute-start.1) | collective-permute-done | bytes 32800 | tf_op jit(solution)/shard_map/ppermute | solution.py:445
  6.8 1.4 %collective-permute-done.2.both_ref = bf16[128,128]{1,0:T(8,128)(2,1)S(1)} collective-permute-done((bf16[128,128]{1,0:T(8,128)(2,1)S(1)}, bf16[128,128]{1,0:T(8,128)(2,1)S(1)}, u32[]{:S(2)}, u32[]{:S(2)}) %collective-permute-start.2) | collective-permute-done | bytes 32800 | tf_op jit(solution)/shard_map/ppermute | solution.py:445
  8.2 1.6 %collective-permute-start.6 = (bf16[2,64,512]{2,1,0:T(8,128)(2,1)S(1)}, bf16[2,64,512]{2,1,0:T(8,128)(2,1)S(1)}, u32[]{:S(2)}, u32[]{:S(2)}) collective-permute-start(bf16[2,64,512]{2,1,0:T(8,128)(2,1)S(1)} %get-tuple-element.31), channel_id=1, source_target_pairs={{0,1},{1,0},{2,3},{3,2},{4,5},{5,4},{6,7},{7,6},{8,9},{9,8},{10,11... | collective-permute-start | bytes 393224 | tf_op jit(solution)/shard_map/ppermute | solution.py:472
  9.8 3.6 %collective-permute-start.5 = (bf16[4,128,128]{2,1,0:T(8,128)(2,1)S(1)}, bf16[4,128,128]{2,1,0:T(8,128)(2,1)S(1)}, u32[]{:S(2)}, u32[]{:S(2)}) collective-permute-start(bf16[4,128,128]{2,1,0:T(8,128)(2,1)S(1)} %shard_map.47.after.refs_0_), channel_id=1, source_target_pairs={{0,24},{8,0},{16,8},{24,16},{1,25},{9,1},{17,9},{25,17},{2,26},{10... | collective-permute-start | bytes 393224 | tf_op jit(solution)/shard_map/ppermute | solution.py:454
  13.4 1.0 %collective-permute-start.3 = (bf16[4,128,128]{2,1,0:T(8,128)(2,1)S(1)}, bf16[4,128,128]{2,1,0:T(8,128)(2,1)S(1)}, u32[]{:S(2)}, u32[]{:S(2)}) collective-permute-start(bf16[4,128,128]{2,1,0:T(8,128)(2,1)S(1)} %shard_map.47.after.refs_0_), channel_id=1, source_target_pairs={{0,8},{8,16},{16,24},{24,0},{1,9},{9,17},{17,25},{25,1},{2,10},{10... | collective-permute-start | bytes 393224 | tf_op jit(solution)/shard_map/ppermute | solution.py:454
  14.5 0.9 %collective-permute-start.7 = (bf16[2,64,512]{2,1,0:T(8,128)(2,1)S(1)}, bf16[2,64,512]{2,1,0:T(8,128)(2,1)S(1)}, u32[]{:S(2)}, u32[]{:S(2)}) collective-permute-start(bf16[2,64,512]{2,1,0:T(8,128)(2,1)S(1)} %get-tuple-element.32), channel_id=1, source_target_pairs={{0,4},{1,5},{2,6},{3,7},{4,0},{5,1},{6,2},{7,3},{8,12},{9,13},{10,... | collective-permute-start | bytes 393224 | tf_op jit(solution)/shard_map/ppermute | solution.py:472
  15.4 1.6 %collective-permute-start.8 = (bf16[2,64,512]{2,1,0:T(8,128)(2,1)S(1)}, bf16[2,64,512]{2,1,0:T(8,128)(2,1)S(1)}, u32[]{:S(2)}, u32[]{:S(2)}) collective-permute-start(bf16[2,64,512]{2,1,0:T(8,128)(2,1)S(1)} %get-tuple-element.33), channel_id=1, source_target_pairs={{0,5},{1,4},{2,7},{3,6},{4,1},{5,0},{6,3},{7,2},{8,13},{9,12},{10,... | collective-permute-start | bytes 393224 | tf_op jit(solution)/shard_map/ppermute | solution.py:472
  17.3 7.4 %collective-permute-done.4.refs_2_ = bf16[4,128,128]{2,1,0:T(8,128)(2,1)S(1)} collective-permute-done((bf16[4,128,128]{2,1,0:T(8,128)(2,1)S(1)}, bf16[4,128,128]{2,1,0:T(8,128)(2,1)S(1)}, u32[]{:S(2)}, u32[]{:S(2)}) %collective-permute-start.4) | collective-permute-done | bytes 131104 | tf_op jit(solution)/shard_map/ppermute | solution.py:454
  24.7 0.7 %shard_map.51 = (f32[16,128]{1,0:T(8,128)S(1)}, bf16[16,480]{1,0:T(8,128)(2,1)S(1)}, bf16[16,64]{1,0:T(8,128)(2,1)S(1)}) custom-call(bf16[4,128,128]{2,1,0:T(8,128)(2,1)S(1)} %shard_map.47.after.refs_0_, bf16[4,128,128]{2,1,0:T(8,128)(2,1)S(1)} %collective-permute-done.3.refs_1_, bf16[4,128,128]{2,1,0:T(8,128)(2,1)S(1)} %collective-permute-done.4.refs_2_, ...), custom_call_target="tpu_custom_call" | custom-call | bytes 524288 | tf_op jit(solution)/shard_map/pallas_call | solution.py:486
  25.5 1.3 %collective-permute-start.9 = (bf16[64,256]{1,0:T(8,128)(2,1)S(1)}, bf16[64,256]{1,0:T(8,128)(2,1)S(1)}, u32[]{:S(2)}, u32[]{:S(2)}) collective-permute-start(bf16[64,256]{1,0:T(8,128)(2,1)S(1)} %get-tuple-element.35), channel_id=1, source_target_pairs={{8,0},{16,8},{24,16},{9,1},{17,9},{25,17},{10,2},{18,10},{26,18},{... | collective-permute-start | bytes 98312 | tf_op jit(solution)/shard_map/ppermute | solution.py:484
  26.8 3.3 %shard_map.52.refs_7_ = f32[6,16,512]{2,1,0:T(8,128)S(1)} custom-call(bf16[4,128,128]{2,1,0:T(8,128)(2,1)S(1)} %shard_map.47.after.refs_0_, bf16[4,128,128]{2,1,0:T(8,128)(2,1)S(1)} %collective-permute-done.3.refs_1_, bf16[4,128,128]{2,1,0:T(8,128)(2,1)S(1)} %collective-permute-done.4.refs_2_, bf16[4,128,128]{2,1,0:T(8,128)(2,1)S(1)} %collective-permute-done.5.refs_3_, ...), custom_call_target="tpu_custom_call" | custom-call | flops 1610612736 | bytes 524288 | tf_op jit(solution)/shard_map/pallas_call | solution.py:508
  30.1 1.2 %collective-permute-done.9.refs_5_ = bf16[64,256]{1,0:T(8,128)(2,1)S(1)} collective-permute-done((bf16[64,256]{1,0:T(8,128)(2,1)S(1)}, bf16[64,256]{1,0:T(8,128)(2,1)S(1)}, u32[]{:S(2)}, u32[]{:S(2)}) %collective-permute-start.9) | collective-permute-done | bytes 32800 | tf_op jit(solution)/shard_map/ppermute | solution.py:484
  31.3 1.9 %shard_map.53 = (f32[4,16,768]{2,1,0:T(8,128)S(1)}, f32[4,16,768]{2,1,0:T(8,128)S(1)}) custom-call(bf16[4,128,128]{2,1,0:T(8,128)(2,1)S(1)} %shard_map.47.after.refs_0_, bf16[4,128,128]{2,1,0:T(8,128)(2,1)S(1)} %collective-permute-done.3.refs_1_, bf16[4,128,128]{2,1,0:T(8,128)(2,1)S(1)} %collective-permute-done.4.refs_2_, ...), custom_call_target="tpu_custom_call" | custom-call | flops 536870912 | bytes 524288 | tf_op jit(solution)/shard_map/pallas_call | solution.py:516
  33.3 1.4 %collective-permute-done.10.got_ref = f32[4,16,768]{2,1,0:T(8,128)S(1)} collective-permute-done((f32[4,16,768]{2,1,0:T(8,128)S(1)}, f32[4,16,768]{2,1,0:T(8,128)S(1)}, u32[]{:S(2)}, u32[]{:S(2)}) %collective-permute-start.10) | collective-permute-done | bytes 196640 | tf_op jit(solution)/shard_map/ppermute | solution.py:528
  34.7 0.6 %collective-permute-start.11 = (f32[16,768]{1,0:T(8,128)S(1)}, f32[16,768]{1,0:T(8,128)S(1)}, u32[]{:S(2)}, u32[]{:S(2)}) collective-permute-start(f32[16,768]{1,0:T(8,128)S(1)} %get-tuple-element.40), channel_id=1, source_target_pairs={{0,1},{1,0},{2,3},{3,2},{4,5},{5,4},{6,7},{7,6},{8,9},{9,8},{10,11... | collective-permute-start | bytes 147464 | tf_op jit(solution)/shard_map/ppermute | solution.py:472
  35.3 0.8 %collective-permute-start.12 = (f32[16,768]{1,0:T(8,128)S(1)}, f32[16,768]{1,0:T(8,128)S(1)}, u32[]{:S(2)}, u32[]{:S(2)}) collective-permute-start(f32[16,768]{1,0:T(8,128)S(1)} %get-tuple-element.41), channel_id=1, source_target_pairs={{0,4},{1,5},{2,6},{3,7},{4,0},{5,1},{6,2},{7,3},{8,12},{9,13},{10,... | collective-permute-start | bytes 147464 | tf_op jit(solution)/shard_map/ppermute | solution.py:472
  36.2 2.1 %collective-permute-start.13 = (f32[16,768]{1,0:T(8,128)S(1)}, f32[16,768]{1,0:T(8,128)S(1)}, u32[]{:S(2)}, u32[]{:S(2)}) collective-permute-start(f32[16,768]{1,0:T(8,128)S(1)} %get-tuple-element.42), channel_id=1, source_target_pairs={{0,5},{1,4},{2,7},{3,6},{4,1},{5,0},{6,3},{7,2},{8,13},{9,12},{10,... | collective-permute-start | bytes 147464 | tf_op jit(solution)/shard_map/ppermute | solution.py:472
  38.3 0.9 %shard_map.55.refs_4_ = f32[16,512]{1,0:T(8,128)S(1)} custom-call(bf16[480,512]{1,0:T(8,128)(2,1)S(1)} %copy-done, bf16[16,480]{1,0:T(8,128)(2,1)S(1)} %get-tuple-element.43.mask_ref, f32[4,16,768]{2,1,0:T(8,128)S(1)} %get-tuple-element.38.after), custom_call_target="tpu_custom_call" | custom-call | flops 15728640 | bytes 491520 | tf_op jit(solution)/shard_map/pallas_call | solution.py:529
  39.1 0.8 %collective-permute-done.12.refs_2_ = f32[16,768]{1,0:T(8,128)S(1)} collective-permute-done((f32[16,768]{1,0:T(8,128)S(1)}, f32[16,768]{1,0:T(8,128)S(1)}, u32[]{:S(2)}, u32[]{:S(2)}) %collective-permute-start.12) | collective-permute-done | bytes 49184 | tf_op jit(solution)/shard_map/ppermute | solution.py:472
  39.9 1.2 %collective-permute-done.13.refs_3_ = f32[16,768]{1,0:T(8,128)S(1)} collective-permute-done((f32[16,768]{1,0:T(8,128)S(1)}, f32[16,768]{1,0:T(8,128)S(1)}, u32[]{:S(2)}, u32[]{:S(2)}) %collective-permute-start.13) | collective-permute-done | bytes 49184 | tf_op jit(solution)/shard_map/ppermute | solution.py:472
  41.2 0.7 %shard_map.56 = f32[16,512]{1,0:T(8,128)} custom-call(f32[16,768]{1,0:T(8,128)S(1)} %get-tuple-element.39.refs_0_, f32[16,768]{1,0:T(8,128)S(1)} %collective-permute-done.11.refs_1_, f32[16,768]{1,0:T(8,128)S(1)} %collective-permute-done.12.refs_2_, f32[16,768]{1,0:T(8,128)S(1)} %collective-permute-done.13.refs_3_, f32[16,512]{1,0:T(8,128)S(1)} %shard_map.55.refs_4_, ...), custom_call_target="tpu_custom_call" | custom-call | bytes 196608 | tf_op jit(solution)/shard_map/pallas_call | solution.py:543
  (19 shorter events, 0.7 us)
Async XLA Ops:
  1.7 6.5 %collective-permute-start = (bf16[1152,128]{1,0:T(8,128)(2,1)S(1)}, bf16[1152,128]{1,0:T(8,128)(2,1)S(1)}, u32[]{:S(2)}, u32[]{:S(2)}) collective-permute-start(bf16[1152,128]{1,0:T(8,128)(2,1)S(1)} %get-tuple-element.26), channel_id=1, source_target_pairs={{0,2},{2,0},{4,6},{6,4},{1,3},{3,1},{5,7},{7,5},{8,10},{10,8},{12,... | collective-permute-start | bytes 884744 | tf_op jit(solution)/shard_map/ppermute | solution.py:445
  2.2 4.6 %collective-permute-start.1 = (bf16[128,128]{1,0:T(8,128)(2,1)S(1)}, bf16[128,128]{1,0:T(8,128)(2,1)S(1)}, u32[]{:S(2)}, u32[]{:S(2)}) collective-permute-start(bf16[128,128]{1,0:T(8,128)(2,1)S(1)} %get-tuple-element.27), channel_id=1, source_target_pairs={{0,4},{2,6},{4,0},{6,2},{1,5},{3,7},{5,1},{7,3},{8,12},{10,14},{12... | collective-permute-start | bytes 98312 | tf_op jit(solution)/shard_map/ppermute | solution.py:445
  4.8 3.3 %collective-permute-start.2 = (bf16[128,128]{1,0:T(8,128)(2,1)S(1)}, bf16[128,128]{1,0:T(8,128)(2,1)S(1)}, u32[]{:S(2)}, u32[]{:S(2)}) collective-permute-start(bf16[128,128]{1,0:T(8,128)(2,1)S(1)} %get-tuple-element.28), channel_id=1, source_target_pairs={{0,6},{2,4},{4,2},{6,0},{1,7},{3,5},{5,3},{7,1},{8,14},{10,12},{12... | collective-permute-start | bytes 98312 | tf_op jit(solution)/shard_map/ppermute | solution.py:445
  8.2 6.2 %collective-permute-start.6 = (bf16[2,64,512]{2,1,0:T(8,128)(2,1)S(1)}, bf16[2,64,512]{2,1,0:T(8,128)(2,1)S(1)}, u32[]{:S(2)}, u32[]{:S(2)}) collective-permute-start(bf16[2,64,512]{2,1,0:T(8,128)(2,1)S(1)} %get-tuple-element.31), channel_id=1, source_target_pairs={{0,1},{1,0},{2,3},{3,2},{4,5},{5,4},{6,7},{7,6},{8,9},{9,8},{10,11... | collective-permute-start | bytes 393224 | tf_op jit(solution)/shard_map/ppermute | solution.py:472
  9.8 7.5 %collective-permute-start.5 = (bf16[4,128,128]{2,1,0:T(8,128)(2,1)S(1)}, bf16[4,128,128]{2,1,0:T(8,128)(2,1)S(1)}, u32[]{:S(2)}, u32[]{:S(2)}) collective-permute-start(bf16[4,128,128]{2,1,0:T(8,128)(2,1)S(1)} %shard_map.47.after.refs_0_), channel_id=1, source_target_pairs={{0,24},{8,0},{16,8},{24,16},{1,25},{9,1},{17,9},{25,17},{2,26},{10... | collective-permute-start | bytes 393224 | tf_op jit(solution)/shard_map/ppermute | solution.py:454
  13.4 11.3 %collective-permute-start.4 = (bf16[4,128,128]{2,1,0:T(8,128)(2,1)S(1)}, bf16[4,128,128]{2,1,0:T(8,128)(2,1)S(1)}, u32[]{:S(2)}, u32[]{:S(2)}) collective-permute-start(bf16[4,128,128]{2,1,0:T(8,128)(2,1)S(1)} %shard_map.47.after.refs_0_), channel_id=1, source_target_pairs={{0,16},{8,24},{16,0},{24,8},{1,17},{9,25},{17,1},{25,9},{2,18},{10... | collective-permute-start | bytes 393224 | tf_op jit(solution)/shard_map/ppermute | solution.py:454
  13.4 11.3 %collective-permute-start.3 = (bf16[4,128,128]{2,1,0:T(8,128)(2,1)S(1)}, bf16[4,128,128]{2,1,0:T(8,128)(2,1)S(1)}, u32[]{:S(2)}, u32[]{:S(2)}) collective-permute-start(bf16[4,128,128]{2,1,0:T(8,128)(2,1)S(1)} %shard_map.47.after.refs_0_), channel_id=1, source_target_pairs={{0,8},{8,16},{16,24},{24,0},{1,9},{9,17},{17,25},{25,1},{2,10},{10... | collective-permute-start | bytes 393224 | tf_op jit(solution)/shard_map/ppermute | solution.py:454
  14.5 10.2 %copy-start.1 = (s32[480]{0:T(512)S(1)}, s32[480]{0:T(512)}, u32[]{:S(2)}) copy-start(s32[480]{0:T(512)} %param.7) | copy-start | bytes 5764
  14.5 10.9 %collective-permute-start.7 = (bf16[2,64,512]{2,1,0:T(8,128)(2,1)S(1)}, bf16[2,64,512]{2,1,0:T(8,128)(2,1)S(1)}, u32[]{:S(2)}, u32[]{:S(2)}) collective-permute-start(bf16[2,64,512]{2,1,0:T(8,128)(2,1)S(1)} %get-tuple-element.32), channel_id=1, source_target_pairs={{0,4},{1,5},{2,6},{3,7},{4,0},{5,1},{6,2},{7,3},{8,12},{9,13},{10,... | collective-permute-start | bytes 393224 | tf_op jit(solution)/shard_map/ppermute | solution.py:472
  15.4 10.0 %collective-permute-start.8 = (bf16[2,64,512]{2,1,0:T(8,128)(2,1)S(1)}, bf16[2,64,512]{2,1,0:T(8,128)(2,1)S(1)}, u32[]{:S(2)}, u32[]{:S(2)}) collective-permute-start(bf16[2,64,512]{2,1,0:T(8,128)(2,1)S(1)} %get-tuple-element.33), channel_id=1, source_target_pairs={{0,5},{1,4},{2,7},{3,6},{4,1},{5,0},{6,3},{7,2},{8,13},{9,12},{10,... | collective-permute-start | bytes 393224 | tf_op jit(solution)/shard_map/ppermute | solution.py:472
  25.5 5.8 %collective-permute-start.9 = (bf16[64,256]{1,0:T(8,128)(2,1)S(1)}, bf16[64,256]{1,0:T(8,128)(2,1)S(1)}, u32[]{:S(2)}, u32[]{:S(2)}) collective-permute-start(bf16[64,256]{1,0:T(8,128)(2,1)S(1)} %get-tuple-element.35), channel_id=1, source_target_pairs={{8,0},{16,8},{24,16},{9,1},{17,9},{25,17},{10,2},{18,10},{26,18},{... | collective-permute-start | bytes 98312 | tf_op jit(solution)/shard_map/ppermute | solution.py:484
  31.3 7.0 %copy-start = (bf16[480,512]{1,0:T(8,128)(2,1)S(1)}, bf16[480,512]{1,0:T(8,128)(2,1)}, u32[]{:S(2)}) copy-start(bf16[480,512]{1,0:T(8,128)(2,1)} %wave_ref.1) | copy-start | bytes 1474564
  33.2 1.5 %collective-permute-start.10 = (f32[4,16,768]{2,1,0:T(8,128)S(1)}, f32[4,16,768]{2,1,0:T(8,128)S(1)}, u32[]{:S(2)}, u32[]{:S(2)}) collective-permute-start(f32[4,16,768]{2,1,0:T(8,128)S(1)} %get-tuple-element.38.after), channel_id=1, source_target_pairs={{0,2},{2,0},{4,6},{6,4},{1,3},{3,1},{5,7},{7,5},{8,10},{10,8},{12,... | collective-permute-start | bytes 589832 | tf_op jit(solution)/shard_map/ppermute | solution.py:528
  34.7 4.4 %collective-permute-start.11 = (f32[16,768]{1,0:T(8,128)S(1)}, f32[16,768]{1,0:T(8,128)S(1)}, u32[]{:S(2)}, u32[]{:S(2)}) collective-permute-start(f32[16,768]{1,0:T(8,128)S(1)} %get-tuple-element.40), channel_id=1, source_target_pairs={{0,1},{1,0},{2,3},{3,2},{4,5},{5,4},{6,7},{7,6},{8,9},{9,8},{10,11... | collective-permute-start | bytes 147464 | tf_op jit(solution)/shard_map/ppermute | solution.py:472
  35.3 4.6 %collective-permute-start.12 = (f32[16,768]{1,0:T(8,128)S(1)}, f32[16,768]{1,0:T(8,128)S(1)}, u32[]{:S(2)}, u32[]{:S(2)}) collective-permute-start(f32[16,768]{1,0:T(8,128)S(1)} %get-tuple-element.41), channel_id=1, source_target_pairs={{0,4},{1,5},{2,6},{3,7},{4,0},{5,1},{6,2},{7,3},{8,12},{9,13},{10,... | collective-permute-start | bytes 147464 | tf_op jit(solution)/shard_map/ppermute | solution.py:472
  36.2 5.0 %collective-permute-start.13 = (f32[16,768]{1,0:T(8,128)S(1)}, f32[16,768]{1,0:T(8,128)S(1)}, u32[]{:S(2)}, u32[]{:S(2)}) collective-permute-start(f32[16,768]{1,0:T(8,128)S(1)} %get-tuple-element.42), channel_id=1, source_target_pairs={{0,5},{1,4},{2,7},{3,6},{4,1},{5,0},{6,3},{7,2},{8,13},{9,12},{10,... | collective-permute-start | bytes 147464 | tf_op jit(solution)/shard_map/ppermute | solution.py:472

commit v14 on v13

--- a/solution.py
+++ b/solution.py
@@ -209,26 +209,17 @@
     head_ref[...] = out_ref[:, : head_ref.shape[1]]
 
 
-def arrival(template, count):
-    inner = template & (INNER - 1)
-    return ((lax.axis_index("outer") * INNER - (template - inner)) & (count - 1)) + inner
-
-
-def correlate(tpls, samples, out_ref, first, left, shifts, products):
-    slab = out_ref.shape[2]
-    part, columns = samples.shape
+def arrival(template):
+    return template ^ (lax.axis_index("outer") * INNER)
+
+
+def arrange(tpls, left):
     size, depth = left.shape
-    copies = LANES // FINE
-    usable = columns - 2 * LANES
-    for copy in range(depth // part):
-        tile, turn = copy // copies * LANES, copy % copies * FINE
-        turned = samples if turn == 0 else pltpu.roll(samples, columns - turn, 1)
-        shifts[copy * part : (copy + 1) * part, :] = turned[:, tile : tile + usable + LANES]
     count = len(tpls) * INNER
     row = lax.broadcasted_iota(jnp.int32, (size, size), 0)
     column = lax.broadcasted_iota(jnp.int32, (size, size), 1)
     shift = count.bit_length() - 1
-    source = arrival(row & (count - 1), count) * FINE + (row >> shift)
+    source = arrival(row & (count - 1)) * FINE + (row >> shift)
     order = jnp.where(column == source, 1.0, 0.0).astype(BF16)
     for step in range(depth // LANES):
         rows = [
@@ -238,21 +229,38 @@
         left[:, step * LANES : (step + 1) * LANES] = jnp.dot(
             order, jnp.concatenate(rows, axis=0), preferred_element_type=F32
         ).astype(BF16)
+
+
+def correlate(left, full, out_ref, slab, side, shifts, products):
+    part = full.shape[0]
+    size, depth = left.shape
+    count = size // FINE
+    copies = LANES // FINE
+    run = out_ref.shape[0] // 2
+    width = run * slab
+    for y in range(2):
+        columns = width + 2 * LANES
+        start = pl.multiple_of((2 * y + side) * width, width)
+        samples = full[:, pl.ds(start, columns)]
+        for copy in range(depth // part):
+            tile, turn = copy // copies * LANES, copy % copies * FINE
+            turned = samples if turn == 0 else pltpu.roll(samples, columns - turn, 1)
+            shifts[y, copy * part : (copy + 1) * part, :] = turned[:, tile : tile + width + LANES]
     tiles = products.shape[2] // LANES
     span = (tiles - 1) * LANES
     per_block = span // slab
-    blocks = usable // span
-
-    def multiply(index, slot):
-        start = pl.multiple_of(index * span, span)
+    blocks = [(y, index) for y in range(2) for index in range(width // span)]
+
+    def multiply(place, slot):
+        y, index = place
         for tile in range(0, tiles, 2):
-            width = min(2, tiles - tile) * LANES
-            here = pl.ds(pl.multiple_of(start + tile * LANES, LANES), width)
-            products[slot, :, tile * LANES : tile * LANES + width] = jnp.dot(
-                left[...], shifts[:, here], preferred_element_type=F32
+            start = index * span + tile * LANES
+            lanes = min(2, tiles - tile) * LANES
+            products[slot, :, tile * LANES : tile * LANES + lanes] = jnp.dot(
+                left[...], shifts[y, :, start : start + lanes], preferred_element_type=F32
             )
 
-    def gather(index, slot):
+    def gather(place, slot):
         def tree(first, number):
             if number == 1:
                 return products[slot, first * count : (first + 1) * count, :]
@@ -261,39 +269,34 @@
             return tree(first, half) + later
 
         total = tree(0, FINE)
+        y, index = place
         for piece in range(per_block):
-            out_ref[first + index * per_block + piece] = total[:, piece * slab : (piece + 1) * slab]
-
-    multiply(0, 0)
-    if blocks <= 4:
-        for index in range(1, blocks):
-            multiply(index, index % 2)
-            gather(index - 1, (index - 1) % 2)
-    else:
-
-        def step(index, carry):
-            multiply(index, lax.rem(index, 2))
-            gather(index - 1, lax.rem(index + 1, 2))
-            return carry
-
-        lax.fori_loop(1, blocks, step, 0)
-    gather(blocks - 1, (blocks - 1) % 2)
-
-
-def first_dots_kernel(*refs):
-    tpls, (samples_ref, out_ref, left, shifts, products) = refs[:-5], refs[-5:]
-    columns = shifts.shape[1] + LANES
-    correlate(tpls, samples_ref[:, :columns], out_ref, 0, left, shifts, products)
-
-
-def last_dots_kernel(*refs):
-    tpls, (samples_ref, halo_ref, mask_ref, done_ref) = refs[:-11], refs[-11:-7]
-    (keep_ref, send_ref), (out_ref, edges, *scratch) = refs[-7:-5], refs[-5:]
-    first, slab = done_ref.shape[0], done_ref.shape[2]
-    group = edges.shape[0]
-    window = halo_ref.shape[1]
-    after = [samples_ref[:, (m + 1) * slab : (m + 1) * slab + window] for m in range(group - 1)]
-    squares = masked_squares(mask_ref[...], jnp.concatenate(after + [halo_ref[...]], axis=1))
+            out_ref[y * run + index * per_block + piece, :, :slab] = total[
+                :, piece * slab : (piece + 1) * slab
+            ]
+
+    multiply(blocks[0], 0)
+    for number in range(1, len(blocks)):
+        multiply(blocks[number], number % 2)
+        gather(blocks[number - 1], (number - 1) % 2)
+    gather(blocks[-1], (len(blocks) - 1) % 2)
+
+
+def first_dots_kernel(stations, channels, tm_count, *refs):
+    tpls, (order_ref, samples_ref, halo_ref) = refs[:-12], refs[-12:-9]
+    send_ref, edges_ref, left, scale_ref, mask_ref = refs[-9:-4]
+    full, edges, shifts, products = refs[-4:]
+    core = lax.rem(lax.axis_index("inner"), 2)
+    group, _, window = edges.shape
+    chunk = samples_ref.shape[1]
+    slab = chunk // group
+    full[:, :chunk] = samples_ref[...]
+    full[:, chunk:] = halo_ref[...]
+    arrange(tpls, left)
+    correlate(left, full, send_ref, slab, 1 - core, shifts, products)
+    part_mask = read_masks(stations, channels, tm_count, tpls, order_ref, scale_ref, mask_ref)
+    after = [full[:, (m + 1) * slab : (m + 1) * slab + window] for m in range(group)]
+    squares = masked_squares(part_mask, jnp.concatenate(after, axis=1))
     column = lax.broadcasted_iota(jnp.int32, squares.shape, 1) & (window - 1)
     reach = 1
     while reach < window:
@@ -303,18 +306,23 @@
     squares = jnp.where(column >= 1, pltpu.roll(squares, 1, 1), 0.0)
     for member in range(group):
         edges[member] = squares[:, member * window : (member + 1) * window]
-    rest = samples_ref.shape[1] + window - scratch[1].shape[1] - LANES
-    samples = jnp.concatenate([samples_ref[:, rest:], halo_ref[...]], axis=1)
-    out_ref[:first] = done_ref[...]
-    correlate(tpls, samples, out_ref, first, *scratch)
-    core = lax.rem(lax.axis_index("inner"), 2)
-    run = keep_ref.shape[0] // 2
+    run = group // 4
     for y in range(2):
         for tm in range(run):
-            for ref, side in ((keep_ref, core), (send_ref, 1 - core)):
-                member = (2 * y + side) * run + tm
-                ref[y * run + tm, :, :slab] = out_ref[member]
-                ref[y * run + tm, :, slab:] = edges[member]
+            send_ref[y * run + tm, :, slab:] = edges[(2 * y + 1 - core) * run + tm]
+            edges_ref[y * run + tm] = edges[(2 * y + core) * run + tm]
+
+
+def second_dots_kernel(left, samples_ref, halo_ref, edges_ref, after, keep_ref, *scratch):
+    del after
+    full, shifts, products = scratch
+    chunk = samples_ref.shape[1]
+    full[:, :chunk] = samples_ref[...]
+    full[:, chunk:] = halo_ref[...]
+    core = lax.rem(lax.axis_index("inner"), 2)
+    slab = keep_ref.shape[2] - edges_ref.shape[2]
+    correlate(left, full, keep_ref, slab, core, shifts, products)
+    keep_ref[:, :, slab:] = edges_ref[...]
 
 
 def add_kernel(tm_count, keep_ref, got_ref, *outs):
@@ -333,8 +341,7 @@
     )
 
 
-def mask_kernel(stations, channels, tm_count, *refs):
-    tpls, (order_ref, scale_ref, mask_ref, part_ref) = refs[:-4], refs[-4:]
+def read_masks(stations, channels, tm_count, tpls, order_ref, scale_ref, mask_ref):
     rows = tpls[0].shape[1]
     count = len(tpls) * INNER
     padded = INNER * LANES
@@ -347,7 +354,7 @@
     )
     template = lax.broadcasted_iota(jnp.int32, (count, count), 0)
     place = lax.broadcasted_iota(jnp.int32, (count, count), 1)
-    sort = jnp.where(place == arrival(template, count), 1.0, 0.0).astype(BF16)
+    sort = jnp.where(place == arrival(template), 1.0, 0.0).astype(BF16)
     slots = -(-stations // rows)
 
     def read(slot):
@@ -368,7 +375,7 @@
     mask_ref[...] = mask
     grouped = jnp.dot(mask, regroup(channels, padded, part), preferred_element_type=F32)
     mine = side_major(lax.axis_index("inner")) * LANES + lax.axis_index("tm") * part
-    part_ref[...] = pltpu.roll(grouped, lax.rem(padded - mine, padded), 1)[:, :part].astype(BF16)
+    return pltpu.roll(grouped, lax.rem(padded - mine, padded), 1)[:, :part].astype(BF16)
 
 
 def power_kernel(window, wave_ref, mask_ref, after, out_ref):
@@ -450,12 +457,10 @@
         pack_kernel, [VMEM] * INNER, sds((INNER, rows, LANES), BF16), bytes_accessed=rows * LANES * 8
     )(pieces[0], got, *others)
 
-    def shift(distance):
-        return lax.ppermute(
-            pack, "outer", [(b, (b + distance) % outer_count) for b in range(outer_count)]
-        )
-
-    tpls = [pack] + [shift(distance) for distance in range(1, outer_count)]
+    tpls = [pack] + [
+        lax.ppermute(pack, "outer", [(b, b ^ flip) for b in range(outer_count)])
+        for flip in range(1, outer_count)
+    ]
 
     half = group // 2
     def split(flips, after):
@@ -473,7 +478,7 @@
 
     parts = split(range(tm_count), pack)
     waves = [parts[0]] + [swap(parts[flip], flip) for flip in range(1, tm_count)]
-    parts += split(range(tm_count, half), waves[1])
+    parts += split(range(tm_count, half), tpls[1])
     waves += [swap(parts[flip], flip) for flip in range(tm_count, half)]
     samples, head = call(
         functools.partial(join_kernel, tm_count),
@@ -483,48 +488,44 @@
     )(*waves)
     halo = lax.ppermute(head, "outer", [(b, b - 1) for b in range(1, outer_count)])
 
-    scale, mask, mask_part = call(
-        functools.partial(mask_kernel, stations, channels, tm_count),
-        [VMEM] * (outer_count + 1),
+    depth = window // FINE * part
+    count = blk_count
+    work = 2 * count * window * part * chunk // 2
+
+    def scratch():
+        return [
+            pltpu.VMEM((2, depth, chunk // 4 + LANES), BF16),
+            pltpu.VMEM((2, count * FINE, span + LANES), F32),
+        ]
+
+    send, edges, left, scale, mask = call(
+        functools.partial(first_dots_kernel, stations, channels, tm_count),
+        [VMEM] * (outer_count + 3),
         [
-            sds((blk_count, LANES), F32),
-            sds((blk_count, channels), BF16),
-            sds((blk_count, part), BF16),
+            sds((half, count, slab + window), F32),
+            sds((half, count, window), F32),
+            sds((count * FINE, depth), BF16),
+            sds((count, LANES), F32),
+            sds((count, channels), BF16),
         ],
-        bytes_accessed=blk_count * rows * LANES * 2,
-    )(*tpls, order_row)
-
-    depth = window // FINE * part
-
-    def scratch(columns):
-        return [
-            pltpu.VMEM((blk_count * FINE, depth), BF16),
-            pltpu.VMEM((depth, columns + LANES), BF16),
-            pltpu.VMEM((2, blk_count * FINE, span + LANES), F32),
+        [
+            pltpu.VMEM((part, chunk + window), BF16),
+            pltpu.VMEM((group, count, window), F32),
         ]
-
-    blocks = group // 2
-    work = 2 * blk_count * window * part * span
-    partials = call(
-        first_dots_kernel,
-        [VMEM] * (outer_count + 1),
-        sds((2 * (blocks - 1), blk_count, slab), F32),
-        scratch((blocks - 1) * span),
-        flops=work * (blocks - 1),
-        bytes_accessed=part * chunk * 2,
-    )(*tpls, samples)
-    keep, send = call(
-        last_dots_kernel,
-        [VMEM] * (outer_count + 4),
-        [sds((half, blk_count, slab + window), F32)] * 2,
-        [
-            pltpu.VMEM((group, blk_count, slab), F32),
-            pltpu.VMEM((group, blk_count, window), F32),
-        ]
-        + scratch(span),
+        + scratch(),
         flops=work,
         bytes_accessed=part * chunk * 2,
-    )(*tpls, samples, halo, mask_part, partials)
+        vmem=36,
+    )(*tpls, order_row, samples, halo)
+    keep = call(
+        second_dots_kernel,
+        [VMEM] * 4 + [AFTER],
+        sds((half, count, slab + window), F32),
+        [pltpu.VMEM((part, chunk + window), BF16)] + scratch(),
+        flops=work,
+        bytes_accessed=part * chunk * 2,
+        vmem=36,
+    )(left, samples, halo, edges, send)
     got = lax.ppermute(send, "inner", [(b, b ^ 1) for b in range(INNER)])
     power = call(
         functools.partial(power_kernel, window),
@@ -532,7 +533,7 @@
         sds((blk_count, slab), F32),
         flops=4 * blk_count * channels * slab,
         bytes_accessed=channels * slab * 2,
-    )(waveforms, mask, send)
+    )(waveforms, mask, keep)
     sums = call(
         functools.partial(add_kernel, tm_count),
         [VMEM] * 2,

time: 42 us -> 44.5 us (1.060)
  starting transfers between devices: 16.7 us -> 17.9 us
  waiting for transfers between devices: 15.7 us -> 16.7 us
    ppermute x3, waiting for transfers between devices: 7.74 us -> 10.4 us  [on_device(): lax.ppermute(pack, 'outer', [(b, b ^ flip) for b in range(outer_count)])]
    ppermute x1, waiting for transfers between devices: 1.43 us -> 0.01 us  [on_device(): got = lax.ppermute(send, 'inner', [(b, b ^ 1) for b in range(INNER)])]
    ppermute x1, waiting for transfers between devices: 1.21 us -> 0.01 us  [on_device(): lax.ppermute(head, 'outer', [(b, b - 1) for b in range(1, outer_count)])]
    ppermute x6, waiting for transfers between devices: 2.02 us -> 3 us  [swap(): return lax.ppermute(part, every, route)]
    ppermute x3, starting transfers between devices: 4.62 us -> 5.25 us  [on_device(): lax.ppermute(pack, 'outer', [(b, b ^ flip) for b in range(outer_count)])]
    ppermute x6, starting transfers between devices: 7.58 us -> 8.13 us  [swap(): return lax.ppermute(part, every, route)]
    pallas_call x3 -> x2, Pallas kernels: 5.88 us -> 6.15 us  [the longest x1 3.73 us: on_device(): call(functools.partial(first_dots_kernel, stations, channels, tm_count),...]
  transfers between devices with their start and end apart: 14 -> 14, of which waited for: 8 -> 8; matrix products, arithmetic and copies ran while one was open for 0% -> 0% of each run, Pallas kernels for 12% -> 8%
where the time goes in v14:
time: 44.5 us; the launch traced here: 44.3 us
  starting transfers between devices  17.9 us (40%)
  waiting for transfers between devices  16.7 us (38%)
  Pallas kernels  9.55 us (21%)
    ppermute x3, waiting for transfers between devices, on_device(): lax.ppermute(pack, 'outer', [(b, b ^ flip) for b in range(outer_count)])  10.4 us
    ppermute x6, starting transfers between devices, swap(): return lax.ppermute(part, every, route)  8.13 us
    ppermute x3, starting transfers between devices, on_device(): lax.ppermute(pack, 'outer', [(b, b ^ flip) for b in range(outer_count)])  5.25 us
    pallas_call x1, Pallas kernels, on_device(): call(functools.partial(first_dots_kernel, stations, channels, tm_count),...  3.73 us
    ppermute x3, waiting for transfers between devices, plane(): return lax.ppermute(part, 'inner', [(b, b ^ flip) for b in range(INNER)])  3.28 us
    ppermute x3, starting transfers between devices, plane(): return lax.ppermute(part, 'inner', [(b, b ^ flip) for b in range(INNER)])  3.18 us
    ppermute x6, waiting for transfers between devices, swap(): return lax.ppermute(part, every, route)  3 us
    pallas_call x1, Pallas kernels, on_device(): call(second_dots_kernel, [VMEM] * 4 + [AFTER], sds((half, count, slab + w...  2.42 us
  transfers between devices with their start and end apart: 14, of which 8 were waited for; matrix products, arithmetic and copies ran while one was open for 0% of the time, Pallas kernels for 8%

profile of v14, /device:TPU:0, one launch (start us, length us, event | category | flops | bytes accessed | tf_op | source)
XLA Modules:
  0.0 44.3 jit_solution(8634196634144228603)
XLA Ops:
  0.0 1.7 %shard_map.46 = (bf16[1152,128]{1,0:T(8,128)(2,1)S(1)}, bf16[256,512]{1,0:T(8,128)(2,1)S(1)}, bf16[128,128]{1,0:T(8,128)(2,1)S(1)}, bf16[128,128]{1,0:T(8,128)(2,1)S(1)}, bf16[128,128]{1,0:T(8,128)(2,1)S(1)}) custom-call(bf16[480,512]{1,0:T(8,128)(2,1)} %wave_ref.1, bf16[1,480,256]{2,1,0:T(8,128)(2,1)} %tpl_hbm.1, s32[1,160]{1,0:T(1,128)} %flag_hbm.1, ...), custom_call_target="tpu_custom_call" | custom-call | bytes 737280 | tf_op jit(solution)/shard_map/pallas_call | solution.py:430
  1.7 0.5 %collective-permute-start = (bf16[1152,128]{1,0:T(8,128)(2,1)S(1)}, bf16[1152,128]{1,0:T(8,128)(2,1)S(1)}, u32[]{:S(2)}, u32[]{:S(2)}) collective-permute-start(bf16[1152,128]{1,0:T(8,128)(2,1)S(1)} %get-tuple-element.26), channel_id=1, source_target_pairs={{0,2},{2,0},{4,6},{6,4},{1,3},{3,1},{5,7},{7,5},{8,10},{10,8},{12,... | collective-permute-start | bytes 884744 | tf_op jit(solution)/shard_map/ppermute | solution.py:452
  2.2 2.6 %collective-permute-start.1 = (bf16[128,128]{1,0:T(8,128)(2,1)S(1)}, bf16[128,128]{1,0:T(8,128)(2,1)S(1)}, u32[]{:S(2)}, u32[]{:S(2)}) collective-permute-start(bf16[128,128]{1,0:T(8,128)(2,1)S(1)} %get-tuple-element.27), channel_id=1, source_target_pairs={{0,4},{2,6},{4,0},{6,2},{1,5},{3,7},{5,1},{7,3},{8,12},{10,14},{12... | collective-permute-start | bytes 98312 | tf_op jit(solution)/shard_map/ppermute | solution.py:452
  4.9 1.9 %collective-permute-done.1.y_ref = bf16[128,128]{1,0:T(8,128)(2,1)S(1)} collective-permute-done((bf16[128,128]{1,0:T(8,128)(2,1)S(1)}, bf16[128,128]{1,0:T(8,128)(2,1)S(1)}, u32[]{:S(2)}, u32[]{:S(2)}) %collective-permute-start.1) | collective-permute-done | bytes 32800 | tf_op jit(solution)/shard_map/ppermute | solution.py:452
  6.8 1.4 %collective-permute-done.2.both_ref = bf16[128,128]{1,0:T(8,128)(2,1)S(1)} collective-permute-done((bf16[128,128]{1,0:T(8,128)(2,1)S(1)}, bf16[128,128]{1,0:T(8,128)(2,1)S(1)}, u32[]{:S(2)}, u32[]{:S(2)}) %collective-permute-start.2) | collective-permute-done | bytes 32800 | tf_op jit(solution)/shard_map/ppermute | solution.py:452
  8.2 1.6 %collective-permute-start.3 = (bf16[4,128,128]{2,1,0:T(8,128)(2,1)S(1)}, bf16[4,128,128]{2,1,0:T(8,128)(2,1)S(1)}, u32[]{:S(2)}, u32[]{:S(2)}) collective-permute-start(bf16[4,128,128]{2,1,0:T(8,128)(2,1)S(1)} %shard_map.47.after.refs_0_), channel_id=1, source_target_pairs={{0,8},{8,0},{16,24},{24,16},{1,9},{9,1},{17,25},{25,17},{2,10},{10... | collective-permute-start | bytes 393224 | tf_op jit(solution)/shard_map/ppermute | solution.py:461
  9.9 1.6 %collective-permute-start.6 = (bf16[2,64,512]{2,1,0:T(8,128)(2,1)S(1)}, bf16[2,64,512]{2,1,0:T(8,128)(2,1)S(1)}, u32[]{:S(2)}, u32[]{:S(2)}) collective-permute-start(bf16[2,64,512]{2,1,0:T(8,128)(2,1)S(1)} %get-tuple-element.31), channel_id=1, source_target_pairs={{0,1},{1,0},{2,3},{3,2},{4,5},{5,4},{6,7},{7,6},{8,9},{9,8},{10,11... | collective-permute-start | bytes 393224 | tf_op jit(solution)/shard_map/ppermute | solution.py:477
  11.4 2.4 %collective-permute-done.3.after.refs_1_ = bf16[4,128,128]{2,1,0:T(8,128)(2,1)S(1)} collective-permute-done((bf16[4,128,128]{2,1,0:T(8,128)(2,1)S(1)}, bf16[4,128,128]{2,1,0:T(8,128)(2,1)S(1)}, u32[]{:S(2)}, u32[]{:S(2)}) %collective-permute-start.3) | collective-permute-done | bytes 131104 | tf_op jit(solution)/shard_map/ppermute | solution.py:461
  13.9 0.8 %collective-permute-start.7 = (bf16[2,64,512]{2,1,0:T(8,128)(2,1)S(1)}, bf16[2,64,512]{2,1,0:T(8,128)(2,1)S(1)}, u32[]{:S(2)}, u32[]{:S(2)}) collective-permute-start(bf16[2,64,512]{2,1,0:T(8,128)(2,1)S(1)} %get-tuple-element.32), channel_id=1, source_target_pairs={{0,4},{1,5},{2,6},{3,7},{4,0},{5,1},{6,2},{7,3},{8,12},{9,13},{10,... | collective-permute-start | bytes 393224 | tf_op jit(solution)/shard_map/ppermute | solution.py:477
  14.7 2.2 %collective-permute-start.8 = (bf16[2,64,512]{2,1,0:T(8,128)(2,1)S(1)}, bf16[2,64,512]{2,1,0:T(8,128)(2,1)S(1)}, u32[]{:S(2)}, u32[]{:S(2)}) collective-permute-start(bf16[2,64,512]{2,1,0:T(8,128)(2,1)S(1)} %get-tuple-element.33), channel_id=1, source_target_pairs={{0,5},{1,4},{2,7},{3,6},{4,1},{5,0},{6,3},{7,2},{8,13},{9,12},{10,... | collective-permute-start | bytes 393224 | tf_op jit(solution)/shard_map/ppermute | solution.py:477
  16.9 3.6 %collective-permute-start.5 = (bf16[4,128,128]{2,1,0:T(8,128)(2,1)S(1)}, bf16[4,128,128]{2,1,0:T(8,128)(2,1)S(1)}, u32[]{:S(2)}, u32[]{:S(2)}) collective-permute-start(bf16[4,128,128]{2,1,0:T(8,128)(2,1)S(1)} %shard_map.47.after.refs_0_), channel_id=1, source_target_pairs={{0,24},{8,16},{16,8},{24,0},{1,25},{9,17},{17,9},{25,1},{2,26},{10... | collective-permute-start | bytes 393224 | tf_op jit(solution)/shard_map/ppermute | solution.py:461
  20.5 1.0 %collective-permute-done.7.refs_2_ = bf16[2,64,512]{2,1,0:T(8,128)(2,1)S(1)} collective-permute-done((bf16[2,64,512]{2,1,0:T(8,128)(2,1)S(1)}, bf16[2,64,512]{2,1,0:T(8,128)(2,1)S(1)}, u32[]{:S(2)}, u32[]{:S(2)}) %collective-permute-start.7) | collective-permute-done | bytes 131104 | tf_op jit(solution)/shard_map/ppermute | solution.py:477
  21.5 1.3 %collective-permute-start.9 = (bf16[64,256]{1,0:T(8,128)(2,1)S(1)}, bf16[64,256]{1,0:T(8,128)(2,1)S(1)}, u32[]{:S(2)}, u32[]{:S(2)}) collective-permute-start(bf16[64,256]{1,0:T(8,128)(2,1)S(1)} %get-tuple-element.35), channel_id=1, source_target_pairs={{8,0},{16,8},{24,16},{9,1},{17,9},{25,17},{10,2},{18,10},{26,18},{... | collective-permute-start | bytes 98312 | tf_op jit(solution)/shard_map/ppermute | solution.py:489
  22.8 1.7 %collective-permute-done.5.refs_3_ = bf16[4,128,128]{2,1,0:T(8,128)(2,1)S(1)} collective-permute-done((bf16[4,128,128]{2,1,0:T(8,128)(2,1)S(1)}, bf16[4,128,128]{2,1,0:T(8,128)(2,1)S(1)}, u32[]{:S(2)}, u32[]{:S(2)}) %collective-permute-start.5) | collective-permute-done | bytes 131104 | tf_op jit(solution)/shard_map/ppermute | solution.py:461
  24.5 6.3 %collective-permute-done.4.refs_2_ = bf16[4,128,128]{2,1,0:T(8,128)(2,1)S(1)} collective-permute-done((bf16[4,128,128]{2,1,0:T(8,128)(2,1)S(1)}, bf16[4,128,128]{2,1,0:T(8,128)(2,1)S(1)}, u32[]{:S(2)}, u32[]{:S(2)}) %collective-permute-start.4) | collective-permute-done | bytes 131104 | tf_op jit(solution)/shard_map/ppermute | solution.py:461
  30.9 3.7 %shard_map.51 = (f32[4,16,768]{2,1,0:T(8,128)S(1)}, f32[4,16,256]{2,1,0:T(8,128)S(1)}, bf16[256,1024]{1,0:T(8,128)(2,1)S(1)}, f32[16,128]{1,0:T(8,128)S(1)}, bf16[16,480]{1,0:T(8,128)(2,1)S(1)}) custom-call(bf16[4,128,128]{2,1,0:T(8,128)(2,1)S(1)} %shard_map.47.after.refs_0_, bf16[4,128,128]{2,1,0:T(8,128)(2,1)S(1)} %collective-permute-done.3.after.refs_1_, ...), custom_call_target="tpu_custom_call" | custom-call | flops 1073741824 | bytes 524288 | tf_op jit(solution)/shard_map/pallas_call | solution.py:501
  34.7 2.4 %shard_map.52.keep_ref.after = f32[4,16,768]{2,1,0:T(8,128)S(1)} custom-call(bf16[256,1024]{1,0:T(8,128)(2,1)S(1)} %get-tuple-element.36.left, bf16[64,4096]{1,0:T(8,128)(2,1)S(1)} %get-tuple-element.34.refs_5_.samples_ref, bf16[64,256]{1,0:T(8,128)(2,1)S(1)} %collective-permute-done.9.refs_6_.halo_ref, f32[4,16,256]{2,1,0:T(8,128)S(1)} %get-tuple-element.37.edges_ref, ...), custom_call_target="tpu_custom_call" | custom-call | flops 1073741824 | bytes 524288 | tf_op jit(solution)/shard_map/pallas_call | solution.py:520
  37.2 0.6 %collective-permute-start.11 = (f32[16,768]{1,0:T(8,128)S(1)}, f32[16,768]{1,0:T(8,128)S(1)}, u32[]{:S(2)}, u32[]{:S(2)}) collective-permute-start(f32[16,768]{1,0:T(8,128)S(1)} %get-tuple-element.40), channel_id=1, source_target_pairs={{0,1},{1,0},{2,3},{3,2},{4,5},{5,4},{6,7},{7,6},{8,9},{9,8},{10,11... | collective-permute-start | bytes 147464 | tf_op jit(solution)/shard_map/ppermute | solution.py:477
  37.8 0.8 %collective-permute-start.12 = (f32[16,768]{1,0:T(8,128)S(1)}, f32[16,768]{1,0:T(8,128)S(1)}, u32[]{:S(2)}, u32[]{:S(2)}) collective-permute-start(f32[16,768]{1,0:T(8,128)S(1)} %get-tuple-element.41), channel_id=1, source_target_pairs={{0,4},{1,5},{2,6},{3,7},{4,0},{5,1},{6,2},{7,3},{8,12},{9,13},{10,... | collective-permute-start | bytes 147464 | tf_op jit(solution)/shard_map/ppermute | solution.py:477
  38.6 2.1 %collective-permute-start.13 = (f32[16,768]{1,0:T(8,128)S(1)}, f32[16,768]{1,0:T(8,128)S(1)}, u32[]{:S(2)}, u32[]{:S(2)}) collective-permute-start(f32[16,768]{1,0:T(8,128)S(1)} %get-tuple-element.42), channel_id=1, source_target_pairs={{0,5},{1,4},{2,7},{3,6},{4,1},{5,0},{6,3},{7,2},{8,13},{9,12},{10,... | collective-permute-start | bytes 147464 | tf_op jit(solution)/shard_map/ppermute | solution.py:477
  40.7 0.9 %shard_map.54.refs_4_ = f32[16,512]{1,0:T(8,128)S(1)} custom-call(bf16[480,512]{1,0:T(8,128)(2,1)S(1)} %copy-done, bf16[16,480]{1,0:T(8,128)(2,1)S(1)} %get-tuple-element.43.mask_ref, f32[4,16,768]{2,1,0:T(8,128)S(1)} %shard_map.52.keep_ref.after), custom_call_target="tpu_custom_call" | custom-call | flops 15728640 | bytes 491520 | tf_op jit(solution)/shard_map/pallas_call | solution.py:530
  41.6 0.3 collective-permute-done.12.refs_2_
  41.9 1.7 %collective-permute-done.13.refs_3_ = f32[16,768]{1,0:T(8,128)S(1)} collective-permute-done((f32[16,768]{1,0:T(8,128)S(1)}, f32[16,768]{1,0:T(8,128)S(1)}, u32[]{:S(2)}, u32[]{:S(2)}) %collective-permute-start.13) | collective-permute-done | bytes 49184 | tf_op jit(solution)/shard_map/ppermute | solution.py:477
  43.6 0.7 %shard_map.55 = f32[16,512]{1,0:T(8,128)} custom-call(f32[16,768]{1,0:T(8,128)S(1)} %get-tuple-element.39.refs_0_, f32[16,768]{1,0:T(8,128)S(1)} %collective-permute-done.11.refs_1_, f32[16,768]{1,0:T(8,128)S(1)} %collective-permute-done.12.refs_2_, f32[16,768]{1,0:T(8,128)S(1)} %collective-permute-done.13.refs_3_, f32[16,512]{1,0:T(8,128)S(1)} %shard_map.54.refs_4_, ...), custom_call_target="tpu_custom_call" | custom-call | bytes 196608 | tf_op jit(solution)/shard_map/pallas_call | solution.py:544
  (18 shorter events, 0.3 us)
Async XLA Ops:
  1.7 6.5 %collective-permute-start = (bf16[1152,128]{1,0:T(8,128)(2,1)S(1)}, bf16[1152,128]{1,0:T(8,128)(2,1)S(1)}, u32[]{:S(2)}, u32[]{:S(2)}) collective-permute-start(bf16[1152,128]{1,0:T(8,128)(2,1)S(1)} %get-tuple-element.26), channel_id=1, source_target_pairs={{0,2},{2,0},{4,6},{6,4},{1,3},{3,1},{5,7},{7,5},{8,10},{10,8},{12,... | collective-permute-start | bytes 884744 | tf_op jit(solution)/shard_map/ppermute | solution.py:452
  2.2 4.6 %collective-permute-start.1 = (bf16[128,128]{1,0:T(8,128)(2,1)S(1)}, bf16[128,128]{1,0:T(8,128)(2,1)S(1)}, u32[]{:S(2)}, u32[]{:S(2)}) collective-permute-start(bf16[128,128]{1,0:T(8,128)(2,1)S(1)} %get-tuple-element.27), channel_id=1, source_target_pairs={{0,4},{2,6},{4,0},{6,2},{1,5},{3,7},{5,1},{7,3},{8,12},{10,14},{12... | collective-permute-start | bytes 98312 | tf_op jit(solution)/shard_map/ppermute | solution.py:452
  4.8 3.3 %collective-permute-start.2 = (bf16[128,128]{1,0:T(8,128)(2,1)S(1)}, bf16[128,128]{1,0:T(8,128)(2,1)S(1)}, u32[]{:S(2)}, u32[]{:S(2)}) collective-permute-start(bf16[128,128]{1,0:T(8,128)(2,1)S(1)} %get-tuple-element.28), channel_id=1, source_target_pairs={{0,6},{2,4},{4,2},{6,0},{1,7},{3,5},{5,3},{7,1},{8,14},{10,12},{12... | collective-permute-start | bytes 98312 | tf_op jit(solution)/shard_map/ppermute | solution.py:452
  8.2 5.6 %collective-permute-start.3 = (bf16[4,128,128]{2,1,0:T(8,128)(2,1)S(1)}, bf16[4,128,128]{2,1,0:T(8,128)(2,1)S(1)}, u32[]{:S(2)}, u32[]{:S(2)}) collective-permute-start(bf16[4,128,128]{2,1,0:T(8,128)(2,1)S(1)} %shard_map.47.after.refs_0_), channel_id=1, source_target_pairs={{0,8},{8,0},{16,24},{24,16},{1,9},{9,1},{17,25},{25,17},{2,10},{10... | collective-permute-start | bytes 393224 | tf_op jit(solution)/shard_map/ppermute | solution.py:461
  9.9 10.6 %collective-permute-start.6 = (bf16[2,64,512]{2,1,0:T(8,128)(2,1)S(1)}, bf16[2,64,512]{2,1,0:T(8,128)(2,1)S(1)}, u32[]{:S(2)}, u32[]{:S(2)}) collective-permute-start(bf16[2,64,512]{2,1,0:T(8,128)(2,1)S(1)} %get-tuple-element.31), channel_id=1, source_target_pairs={{0,1},{1,0},{2,3},{3,2},{4,5},{5,4},{6,7},{7,6},{8,9},{9,8},{10,11... | collective-permute-start | bytes 393224 | tf_op jit(solution)/shard_map/ppermute | solution.py:477
  13.9 7.6 %collective-permute-start.7 = (bf16[2,64,512]{2,1,0:T(8,128)(2,1)S(1)}, bf16[2,64,512]{2,1,0:T(8,128)(2,1)S(1)}, u32[]{:S(2)}, u32[]{:S(2)}) collective-permute-start(bf16[2,64,512]{2,1,0:T(8,128)(2,1)S(1)} %get-tuple-element.32), channel_id=1, source_target_pairs={{0,4},{1,5},{2,6},{3,7},{4,0},{5,1},{6,2},{7,3},{8,12},{9,13},{10,... | collective-permute-start | bytes 393224 | tf_op jit(solution)/shard_map/ppermute | solution.py:477
  14.7 6.8 %collective-permute-start.8 = (bf16[2,64,512]{2,1,0:T(8,128)(2,1)S(1)}, bf16[2,64,512]{2,1,0:T(8,128)(2,1)S(1)}, u32[]{:S(2)}, u32[]{:S(2)}) collective-permute-start(bf16[2,64,512]{2,1,0:T(8,128)(2,1)S(1)} %get-tuple-element.33), channel_id=1, source_target_pairs={{0,5},{1,4},{2,7},{3,6},{4,1},{5,0},{6,3},{7,2},{8,13},{9,12},{10,... | collective-permute-start | bytes 393224 | tf_op jit(solution)/shard_map/ppermute | solution.py:477
  16.9 7.7 %collective-permute-start.5 = (bf16[4,128,128]{2,1,0:T(8,128)(2,1)S(1)}, bf16[4,128,128]{2,1,0:T(8,128)(2,1)S(1)}, u32[]{:S(2)}, u32[]{:S(2)}) collective-permute-start(bf16[4,128,128]{2,1,0:T(8,128)(2,1)S(1)} %shard_map.47.after.refs_0_), channel_id=1, source_target_pairs={{0,24},{8,16},{16,8},{24,0},{1,25},{9,17},{17,9},{25,1},{2,26},{10... | collective-permute-start | bytes 393224 | tf_op jit(solution)/shard_map/ppermute | solution.py:461
  20.5 10.4 %collective-permute-start.4 = (bf16[4,128,128]{2,1,0:T(8,128)(2,1)S(1)}, bf16[4,128,128]{2,1,0:T(8,128)(2,1)S(1)}, u32[]{:S(2)}, u32[]{:S(2)}) collective-permute-start(bf16[4,128,128]{2,1,0:T(8,128)(2,1)S(1)} %shard_map.47.after.refs_0_), channel_id=1, source_target_pairs={{0,16},{8,24},{16,0},{24,8},{1,17},{9,25},{17,1},{25,9},{2,18},{10... | collective-permute-start | bytes 393224 | tf_op jit(solution)/shard_map/ppermute | solution.py:461
  21.5 9.3 %copy-start.1 = (s32[480]{0:T(512)S(1)}, s32[480]{0:T(512)}, u32[]{:S(2)}) copy-start(s32[480]{0:T(512)} %param.7) | copy-start | bytes 5764
  21.5 9.3 %collective-permute-start.9 = (bf16[64,256]{1,0:T(8,128)(2,1)S(1)}, bf16[64,256]{1,0:T(8,128)(2,1)S(1)}, u32[]{:S(2)}, u32[]{:S(2)}) collective-permute-start(bf16[64,256]{1,0:T(8,128)(2,1)S(1)} %get-tuple-element.35), channel_id=1, source_target_pairs={{8,0},{16,8},{24,16},{9,1},{17,9},{25,17},{10,2},{18,10},{26,18},{... | collective-permute-start | bytes 98312 | tf_op jit(solution)/shard_map/ppermute | solution.py:489
  34.6 2.5 %collective-permute-start.10 = (f32[4,16,768]{2,1,0:T(8,128)S(1)}, f32[4,16,768]{2,1,0:T(8,128)S(1)}, u32[]{:S(2)}, u32[]{:S(2)}) collective-permute-start(f32[4,16,768]{2,1,0:T(8,128)S(1)} %get-tuple-element.38.after), channel_id=1, source_target_pairs={{0,2},{2,0},{4,6},{6,4},{1,3},{3,1},{5,7},{7,5},{8,10},{10,8},{12,... | collective-permute-start | bytes 589832 | tf_op jit(solution)/shard_map/ppermute | solution.py:529
  34.7 6.0 %copy-start = (bf16[480,512]{1,0:T(8,128)(2,1)S(1)}, bf16[480,512]{1,0:T(8,128)(2,1)}, u32[]{:S(2)}) copy-start(bf16[480,512]{1,0:T(8,128)(2,1)} %wave_ref.1) | copy-start | bytes 1474564
  37.2 4.4 %collective-permute-start.11 = (f32[16,768]{1,0:T(8,128)S(1)}, f32[16,768]{1,0:T(8,128)S(1)}, u32[]{:S(2)}, u32[]{:S(2)}) collective-permute-start(f32[16,768]{1,0:T(8,128)S(1)} %get-tuple-element.40), channel_id=1, source_target_pairs={{0,1},{1,0},{2,3},{3,2},{4,5},{5,4},{6,7},{7,6},{8,9},{9,8},{10,11... | collective-permute-start | bytes 147464 | tf_op jit(solution)/shard_map/ppermute | solution.py:477
  37.8 4.1 %collective-permute-start.12 = (f32[16,768]{1,0:T(8,128)S(1)}, f32[16,768]{1,0:T(8,128)S(1)}, u32[]{:S(2)}, u32[]{:S(2)}) collective-permute-start(f32[16,768]{1,0:T(8,128)S(1)} %get-tuple-element.41), channel_id=1, source_target_pairs={{0,4},{1,5},{2,6},{3,7},{4,0},{5,1},{6,2},{7,3},{8,12},{9,13},{10,... | collective-permute-start | bytes 147464 | tf_op jit(solution)/shard_map/ppermute | solution.py:477
  38.6 5.0 %collective-permute-start.13 = (f32[16,768]{1,0:T(8,128)S(1)}, f32[16,768]{1,0:T(8,128)S(1)}, u32[]{:S(2)}, u32[]{:S(2)}) collective-permute-start(f32[16,768]{1,0:T(8,128)S(1)} %get-tuple-element.42), channel_id=1, source_target_pairs={{0,5},{1,4},{2,7},{3,6},{4,1},{5,0},{6,3},{7,2},{8,13},{9,12},{10,... | collective-permute-start | bytes 147464 | tf_op jit(solution)/shard_map/ppermute | solution.py:477

commit v15 on v14

--- a/solution.py
+++ b/solution.py
@@ -181,14 +181,13 @@
     out_ref[inner ^ 3] = both_ref[...]
 
 
-def split_kernel(tm_count, flips, keep_ref, got_ref, after, *outs):
-    del after
+def split_kernel(tm_count, keep_ref, got_ref, *outs):
     my_inner = lax.axis_index("inner")
     core = lax.rem(my_inner, 2)
     me = lax.div(my_inner, 2) * tm_count + lax.axis_index("tm")
     part = outs[0].shape[1]
     half, slab = keep_ref.shape
-    for flip, out_ref in zip(flips, outs):
+    for flip, out_ref in enumerate(outs):
         start = (me ^ flip) * part
         out_ref[core] = keep_ref[pl.ds(pl.multiple_of(start, part), part), :]
         for tile in range(slab // LANES):
@@ -463,23 +462,19 @@
     ]
 
     half = group // 2
-    def split(flips, after):
-        return call(
-            functools.partial(split_kernel, tm_count, flips),
-            [VMEM, VMEM, AFTER],
-            [sds((2, part, slab), BF16)] * len(flips),
-            bytes_accessed=padded * slab * 2,
-        )(keep, got, after)
 
     def swap(part, flip):
         y, tm = flip // tm_count, flip % tm_count
         route = [(i, i ^ (2 * tm_count * y + tm)) for i in range(total)]
         return lax.ppermute(part, every, route)
 
-    parts = split(range(tm_count), pack)
-    waves = [parts[0]] + [swap(parts[flip], flip) for flip in range(1, tm_count)]
-    parts += split(range(tm_count, half), tpls[1])
-    waves += [swap(parts[flip], flip) for flip in range(tm_count, half)]
+    parts = call(
+        functools.partial(split_kernel, tm_count),
+        [VMEM] * 2,
+        [sds((2, part, slab), BF16)] * half,
+        bytes_accessed=padded * slab * 2,
+    )(keep, got)
+    waves = [parts[0]] + [swap(parts[flip], flip) for flip in range(1, half)]
     samples, head = call(
         functools.partial(join_kernel, tm_count),
         [VMEM] * half,

time: 44.5 us -> 40.7 us (0.915)
  waiting for transfers between devices: 16.7 us -> 14.5 us
  starting transfers between devices: 17.9 us -> 16.4 us
    ppermute x3, waiting for transfers between devices: 10.4 us -> 8.15 us  [on_device(): lax.ppermute(pack, 'outer', [(b, b ^ flip) for b in range(outer_count)])]
    ppermute x3, starting transfers between devices: 3.18 us -> 2.04 us  [plane(): return lax.ppermute(part, 'inner', [(b, b ^ flip) for b in range(INNER)])]
    ppermute x3, starting transfers between devices: 5.25 us -> 4.45 us  [on_device(): lax.ppermute(pack, 'outer', [(b, b ^ flip) for b in range(outer_count)])]
    ppermute x6, waiting for transfers between devices: 3 us -> 3.67 us  [swap(): return lax.ppermute(part, every, route)]
    ppermute x3, waiting for transfers between devices: 3.28 us -> 2.62 us  [plane(): return lax.ppermute(part, 'inner', [(b, b ^ flip) for b in range(INNER)])]
where the time goes in v15:
time: 40.7 us; the launch traced here: 40.5 us
  starting transfers between devices  16.4 us (40%)
  waiting for transfers between devices  14.5 us (36%)
  Pallas kernels  9.55 us (23%)
    ppermute x6, starting transfers between devices, swap(): return lax.ppermute(part, every, route)  8.51 us
    ppermute x3, waiting for transfers between devices, on_device(): lax.ppermute(pack, 'outer', [(b, b ^ flip) for b in range(outer_count)])  8.15 us
    ppermute x3, starting transfers between devices, on_device(): lax.ppermute(pack, 'outer', [(b, b ^ flip) for b in range(outer_count)])  4.45 us
    pallas_call x1, Pallas kernels, on_device(): call(functools.partial(first_dots_kernel, stations, channels, tm_count),...  3.72 us
    ppermute x6, waiting for transfers between devices, swap(): return lax.ppermute(part, every, route)  3.67 us
    ppermute x3, waiting for transfers between devices, plane(): return lax.ppermute(part, 'inner', [(b, b ^ flip) for b in range(INNER)])  2.62 us
    pallas_call x1, Pallas kernels, on_device(): call(second_dots_kernel, [VMEM] * 4 + [AFTER], sds((half, count, slab + w...  2.42 us
    ppermute x3, starting transfers between devices, plane(): return lax.ppermute(part, 'inner', [(b, b ^ flip) for b in range(INNER)])  2.04 us
  transfers between devices with their start and end apart: 14, of which 8 were waited for; matrix products, arithmetic and copies ran while one was open for 0% of the time, Pallas kernels for 8%

profile of v15, /device:TPU:0, one launch (start us, length us, event | category | flops | bytes accessed | tf_op | source)
XLA Modules:
  0.0 40.5 jit_solution(742954218149410136)
XLA Ops:
  0.0 1.7 %shard_map.46 = (bf16[1152,128]{1,0:T(8,128)(2,1)S(1)}, bf16[256,512]{1,0:T(8,128)(2,1)S(1)}, bf16[128,128]{1,0:T(8,128)(2,1)S(1)}, bf16[128,128]{1,0:T(8,128)(2,1)S(1)}, bf16[128,128]{1,0:T(8,128)(2,1)S(1)}) custom-call(bf16[480,512]{1,0:T(8,128)(2,1)} %wave_ref.1, bf16[1,480,256]{2,1,0:T(8,128)(2,1)} %tpl_hbm.1, s32[1,160]{1,0:T(1,128)} %flag_hbm.1, ...), custom_call_target="tpu_custom_call" | custom-call | bytes 737280 | tf_op jit(solution)/shard_map/pallas_call | solution.py:429
  1.7 0.5 %collective-permute-start = (bf16[1152,128]{1,0:T(8,128)(2,1)S(1)}, bf16[1152,128]{1,0:T(8,128)(2,1)S(1)}, u32[]{:S(2)}, u32[]{:S(2)}) collective-permute-start(bf16[1152,128]{1,0:T(8,128)(2,1)S(1)} %get-tuple-element.26), channel_id=1, source_target_pairs={{0,2},{2,0},{4,6},{6,4},{1,3},{3,1},{5,7},{7,5},{8,10},{10,8},{12,... | collective-permute-start | bytes 884744 | tf_op jit(solution)/shard_map/ppermute | solution.py:451
  2.2 1.2 %collective-permute-done.core_ref.got_ref = bf16[1152,128]{1,0:T(8,128)(2,1)S(1)} collective-permute-done((bf16[1152,128]{1,0:T(8,128)(2,1)S(1)}, bf16[1152,128]{1,0:T(8,128)(2,1)S(1)}, u32[]{:S(2)}, u32[]{:S(2)}) %collective-permute-start) | collective-permute-done | bytes 294944 | tf_op jit(solution)/shard_map/ppermute | solution.py:451
  3.5 2.9 %collective-permute-start.6 = (bf16[2,64,512]{2,1,0:T(8,128)(2,1)S(1)}, bf16[2,64,512]{2,1,0:T(8,128)(2,1)S(1)}, u32[]{:S(2)}, u32[]{:S(2)}) collective-permute-start(bf16[2,64,512]{2,1,0:T(8,128)(2,1)S(1)} %get-tuple-element.31), channel_id=1, source_target_pairs={{0,1},{1,0},{2,3},{3,2},{4,5},{5,4},{6,7},{7,6},{8,9},{9,8},{10,11... | collective-permute-start | bytes 393224 | tf_op jit(solution)/shard_map/ppermute | solution.py:469
  6.4 1.5 %collective-permute-start.1 = (bf16[128,128]{1,0:T(8,128)(2,1)S(1)}, bf16[128,128]{1,0:T(8,128)(2,1)S(1)}, u32[]{:S(2)}, u32[]{:S(2)}) collective-permute-start(bf16[128,128]{1,0:T(8,128)(2,1)S(1)} %get-tuple-element.27), channel_id=1, source_target_pairs={{0,4},{2,6},{4,0},{6,2},{1,5},{3,7},{5,1},{7,3},{8,12},{10,14},{12... | collective-permute-start | bytes 98312 | tf_op jit(solution)/shard_map/ppermute | solution.py:451
  7.9 1.2 %collective-permute-start.7 = (bf16[2,64,512]{2,1,0:T(8,128)(2,1)S(1)}, bf16[2,64,512]{2,1,0:T(8,128)(2,1)S(1)}, u32[]{:S(2)}, u32[]{:S(2)}) collective-permute-start(bf16[2,64,512]{2,1,0:T(8,128)(2,1)S(1)} %get-tuple-element.32), channel_id=1, source_target_pairs={{0,4},{1,5},{2,6},{3,7},{4,0},{5,1},{6,2},{7,3},{8,12},{9,13},{10,... | collective-permute-start | bytes 393224 | tf_op jit(solution)/shard_map/ppermute | solution.py:469
  9.2 0.8 %collective-permute-start.8 = (bf16[2,64,512]{2,1,0:T(8,128)(2,1)S(1)}, bf16[2,64,512]{2,1,0:T(8,128)(2,1)S(1)}, u32[]{:S(2)}, u32[]{:S(2)}) collective-permute-start(bf16[2,64,512]{2,1,0:T(8,128)(2,1)S(1)} %get-tuple-element.33), channel_id=1, source_target_pairs={{0,5},{1,4},{2,7},{3,6},{4,1},{5,0},{6,3},{7,2},{8,13},{9,12},{10,... | collective-permute-start | bytes 393224 | tf_op jit(solution)/shard_map/ppermute | solution.py:469
  10.0 0.4 collective-permute-done.1.y_ref
  10.3 1.1 %collective-permute-done.2.both_ref = bf16[128,128]{1,0:T(8,128)(2,1)S(1)} collective-permute-done((bf16[128,128]{1,0:T(8,128)(2,1)S(1)}, bf16[128,128]{1,0:T(8,128)(2,1)S(1)}, u32[]{:S(2)}, u32[]{:S(2)}) %collective-permute-start.2) | collective-permute-done | bytes 32800 | tf_op jit(solution)/shard_map/ppermute | solution.py:451
  11.4 3.7 %collective-permute-start.5 = (bf16[4,128,128]{2,1,0:T(8,128)(2,1)S(1)}, bf16[4,128,128]{2,1,0:T(8,128)(2,1)S(1)}, u32[]{:S(2)}, u32[]{:S(2)}) collective-permute-start(bf16[4,128,128]{2,1,0:T(8,128)(2,1)S(1)} %shard_map.47.refs_0_), channel_id=1, source_target_pairs={{0,24},{8,16},{16,8},{24,0},{1,25},{9,17},{17,9},{25,1},{2,26},{10... | collective-permute-start | bytes 393224 | tf_op jit(solution)/shard_map/ppermute | solution.py:460
  15.1 0.8 %collective-permute-start.3 = (bf16[4,128,128]{2,1,0:T(8,128)(2,1)S(1)}, bf16[4,128,128]{2,1,0:T(8,128)(2,1)S(1)}, u32[]{:S(2)}, u32[]{:S(2)}) collective-permute-start(bf16[4,128,128]{2,1,0:T(8,128)(2,1)S(1)} %shard_map.47.refs_0_), channel_id=1, source_target_pairs={{0,8},{8,0},{16,24},{24,16},{1,9},{9,1},{17,25},{25,17},{2,10},{10... | collective-permute-start | bytes 393224 | tf_op jit(solution)/shard_map/ppermute | solution.py:460
  15.9 1.1 %collective-permute-done.7.refs_2_ = bf16[2,64,512]{2,1,0:T(8,128)(2,1)S(1)} collective-permute-done((bf16[2,64,512]{2,1,0:T(8,128)(2,1)S(1)}, bf16[2,64,512]{2,1,0:T(8,128)(2,1)S(1)}, u32[]{:S(2)}, u32[]{:S(2)}) %collective-permute-start.7) | collective-permute-done | bytes 131104 | tf_op jit(solution)/shard_map/ppermute | solution.py:469
  17.1 1.3 %collective-permute-start.9 = (bf16[64,256]{1,0:T(8,128)(2,1)S(1)}, bf16[64,256]{1,0:T(8,128)(2,1)S(1)}, u32[]{:S(2)}, u32[]{:S(2)}) collective-permute-start(bf16[64,256]{1,0:T(8,128)(2,1)S(1)} %get-tuple-element.35), channel_id=1, source_target_pairs={{8,0},{16,8},{24,16},{9,1},{17,9},{25,17},{10,2},{18,10},{26,18},{... | collective-permute-start | bytes 98312 | tf_op jit(solution)/shard_map/ppermute | solution.py:484
  18.4 1.3 %collective-permute-done.5.refs_3_ = bf16[4,128,128]{2,1,0:T(8,128)(2,1)S(1)} collective-permute-done((bf16[4,128,128]{2,1,0:T(8,128)(2,1)S(1)}, bf16[4,128,128]{2,1,0:T(8,128)(2,1)S(1)}, u32[]{:S(2)}, u32[]{:S(2)}) %collective-permute-start.5) | collective-permute-done | bytes 131104 | tf_op jit(solution)/shard_map/ppermute | solution.py:460
  19.7 6.8 %collective-permute-done.4.refs_2_ = bf16[4,128,128]{2,1,0:T(8,128)(2,1)S(1)} collective-permute-done((bf16[4,128,128]{2,1,0:T(8,128)(2,1)S(1)}, bf16[4,128,128]{2,1,0:T(8,128)(2,1)S(1)}, u32[]{:S(2)}, u32[]{:S(2)}) %collective-permute-start.4) | collective-permute-done | bytes 131104 | tf_op jit(solution)/shard_map/ppermute | solution.py:460
  26.6 3.7 %shard_map.50 = (f32[4,16,768]{2,1,0:T(8,128)S(1)}, f32[4,16,256]{2,1,0:T(8,128)S(1)}, bf16[256,1024]{1,0:T(8,128)(2,1)S(1)}, f32[16,128]{1,0:T(8,128)S(1)}, bf16[16,480]{1,0:T(8,128)(2,1)S(1)}) custom-call(bf16[4,128,128]{2,1,0:T(8,128)(2,1)S(1)} %shard_map.47.refs_0_, bf16[4,128,128]{2,1,0:T(8,128)(2,1)S(1)} %collective-permute-done.3.refs_1_, ...), custom_call_target="tpu_custom_call" | custom-call | flops 1073741824 | bytes 524288 | tf_op jit(solution)/shard_map/pallas_call | solution.py:496
  30.4 2.4 %shard_map.51.keep_ref.after = f32[4,16,768]{2,1,0:T(8,128)S(1)} custom-call(bf16[256,1024]{1,0:T(8,128)(2,1)S(1)} %get-tuple-element.36.left, bf16[64,4096]{1,0:T(8,128)(2,1)S(1)} %get-tuple-element.34.refs_5_.samples_ref, bf16[64,256]{1,0:T(8,128)(2,1)S(1)} %collective-permute-done.9.refs_6_.halo_ref, f32[4,16,256]{2,1,0:T(8,128)S(1)} %get-tuple-element.37.edges_ref, ...), custom_call_target="tpu_custom_call" | custom-call | flops 1073741824 | bytes 524288 | tf_op jit(solution)/shard_map/pallas_call | solution.py:515
  32.8 0.6 %collective-permute-start.11 = (f32[16,768]{1,0:T(8,128)S(1)}, f32[16,768]{1,0:T(8,128)S(1)}, u32[]{:S(2)}, u32[]{:S(2)}) collective-permute-start(f32[16,768]{1,0:T(8,128)S(1)} %get-tuple-element.40), channel_id=1, source_target_pairs={{0,1},{1,0},{2,3},{3,2},{4,5},{5,4},{6,7},{7,6},{8,9},{9,8},{10,11... | collective-permute-start | bytes 147464 | tf_op jit(solution)/shard_map/ppermute | solution.py:469
  33.5 1.4 %collective-permute-start.12 = (f32[16,768]{1,0:T(8,128)S(1)}, f32[16,768]{1,0:T(8,128)S(1)}, u32[]{:S(2)}, u32[]{:S(2)}) collective-permute-start(f32[16,768]{1,0:T(8,128)S(1)} %get-tuple-element.41), channel_id=1, source_target_pairs={{0,4},{1,5},{2,6},{3,7},{4,0},{5,1},{6,2},{7,3},{8,12},{9,13},{10,... | collective-permute-start | bytes 147464 | tf_op jit(solution)/shard_map/ppermute | solution.py:469
  34.8 1.6 %collective-permute-start.13 = (f32[16,768]{1,0:T(8,128)S(1)}, f32[16,768]{1,0:T(8,128)S(1)}, u32[]{:S(2)}, u32[]{:S(2)}) collective-permute-start(f32[16,768]{1,0:T(8,128)S(1)} %get-tuple-element.42), channel_id=1, source_target_pairs={{0,5},{1,4},{2,7},{3,6},{4,1},{5,0},{6,3},{7,2},{8,13},{9,12},{10,... | collective-permute-start | bytes 147464 | tf_op jit(solution)/shard_map/ppermute | solution.py:469
  36.4 0.9 %shard_map.53.refs_4_ = f32[16,512]{1,0:T(8,128)S(1)} custom-call(bf16[480,512]{1,0:T(8,128)(2,1)S(1)} %copy-done, bf16[16,480]{1,0:T(8,128)(2,1)S(1)} %get-tuple-element.43.mask_ref, f32[4,16,768]{2,1,0:T(8,128)S(1)} %shard_map.51.keep_ref.after), custom_call_target="tpu_custom_call" | custom-call | flops 15728640 | bytes 491520 | tf_op jit(solution)/shard_map/pallas_call | solution.py:525
  37.3 0.3 collective-permute-done.12.refs_2_
  37.5 2.2 %collective-permute-done.13.refs_3_ = f32[16,768]{1,0:T(8,128)S(1)} collective-permute-done((f32[16,768]{1,0:T(8,128)S(1)}, f32[16,768]{1,0:T(8,128)S(1)}, u32[]{:S(2)}, u32[]{:S(2)}) %collective-permute-start.13) | collective-permute-done | bytes 49184 | tf_op jit(solution)/shard_map/ppermute | solution.py:469
  39.8 0.7 %shard_map.54 = f32[16,512]{1,0:T(8,128)} custom-call(f32[16,768]{1,0:T(8,128)S(1)} %get-tuple-element.39.refs_0_, f32[16,768]{1,0:T(8,128)S(1)} %collective-permute-done.11.refs_1_, f32[16,768]{1,0:T(8,128)S(1)} %collective-permute-done.12.refs_2_, f32[16,768]{1,0:T(8,128)S(1)} %collective-permute-done.13.refs_3_, f32[16,512]{1,0:T(8,128)S(1)} %shard_map.53.refs_4_, ...), custom_call_target="tpu_custom_call" | custom-call | bytes 196608 | tf_op jit(solution)/shard_map/pallas_call | solution.py:539
  (17 shorter events, 0.3 us)
Async XLA Ops:
  1.7 1.7 %collective-permute-start = (bf16[1152,128]{1,0:T(8,128)(2,1)S(1)}, bf16[1152,128]{1,0:T(8,128)(2,1)S(1)}, u32[]{:S(2)}, u32[]{:S(2)}) collective-permute-start(bf16[1152,128]{1,0:T(8,128)(2,1)S(1)} %get-tuple-element.26), channel_id=1, source_target_pairs={{0,2},{2,0},{4,6},{6,4},{1,3},{3,1},{5,7},{7,5},{8,10},{10,8},{12,... | collective-permute-start | bytes 884744 | tf_op jit(solution)/shard_map/ppermute | solution.py:451
  3.5 11.6 %collective-permute-start.6 = (bf16[2,64,512]{2,1,0:T(8,128)(2,1)S(1)}, bf16[2,64,512]{2,1,0:T(8,128)(2,1)S(1)}, u32[]{:S(2)}, u32[]{:S(2)}) collective-permute-start(bf16[2,64,512]{2,1,0:T(8,128)(2,1)S(1)} %get-tuple-element.31), channel_id=1, source_target_pairs={{0,1},{1,0},{2,3},{3,2},{4,5},{5,4},{6,7},{7,6},{8,9},{9,8},{10,11... | collective-permute-start | bytes 393224 | tf_op jit(solution)/shard_map/ppermute | solution.py:469
  6.4 3.9 %collective-permute-start.1 = (bf16[128,128]{1,0:T(8,128)(2,1)S(1)}, bf16[128,128]{1,0:T(8,128)(2,1)S(1)}, u32[]{:S(2)}, u32[]{:S(2)}) collective-permute-start(bf16[128,128]{1,0:T(8,128)(2,1)S(1)} %get-tuple-element.27), channel_id=1, source_target_pairs={{0,4},{2,6},{4,0},{6,2},{1,5},{3,7},{5,1},{7,3},{8,12},{10,14},{12... | collective-permute-start | bytes 98312 | tf_op jit(solution)/shard_map/ppermute | solution.py:451
  7.9 3.4 %collective-permute-start.2 = (bf16[128,128]{1,0:T(8,128)(2,1)S(1)}, bf16[128,128]{1,0:T(8,128)(2,1)S(1)}, u32[]{:S(2)}, u32[]{:S(2)}) collective-permute-start(bf16[128,128]{1,0:T(8,128)(2,1)S(1)} %get-tuple-element.28), channel_id=1, source_target_pairs={{0,6},{2,4},{4,2},{6,0},{1,7},{3,5},{5,3},{7,1},{8,14},{10,12},{12... | collective-permute-start | bytes 98312 | tf_op jit(solution)/shard_map/ppermute | solution.py:451
  7.9 9.1 %collective-permute-start.7 = (bf16[2,64,512]{2,1,0:T(8,128)(2,1)S(1)}, bf16[2,64,512]{2,1,0:T(8,128)(2,1)S(1)}, u32[]{:S(2)}, u32[]{:S(2)}) collective-permute-start(bf16[2,64,512]{2,1,0:T(8,128)(2,1)S(1)} %get-tuple-element.32), channel_id=1, source_target_pairs={{0,4},{1,5},{2,6},{3,7},{4,0},{5,1},{6,2},{7,3},{8,12},{9,13},{10,... | collective-permute-start | bytes 393224 | tf_op jit(solution)/shard_map/ppermute | solution.py:469
  9.2 7.9 %collective-permute-start.8 = (bf16[2,64,512]{2,1,0:T(8,128)(2,1)S(1)}, bf16[2,64,512]{2,1,0:T(8,128)(2,1)S(1)}, u32[]{:S(2)}, u32[]{:S(2)}) collective-permute-start(bf16[2,64,512]{2,1,0:T(8,128)(2,1)S(1)} %get-tuple-element.33), channel_id=1, source_target_pairs={{0,5},{1,4},{2,7},{3,6},{4,1},{5,0},{6,3},{7,2},{8,13},{9,12},{10,... | collective-permute-start | bytes 393224 | tf_op jit(solution)/shard_map/ppermute | solution.py:469
  11.4 8.3 %collective-permute-start.5 = (bf16[4,128,128]{2,1,0:T(8,128)(2,1)S(1)}, bf16[4,128,128]{2,1,0:T(8,128)(2,1)S(1)}, u32[]{:S(2)}, u32[]{:S(2)}) collective-permute-start(bf16[4,128,128]{2,1,0:T(8,128)(2,1)S(1)} %shard_map.47.refs_0_), channel_id=1, source_target_pairs={{0,24},{8,16},{16,8},{24,0},{1,25},{9,17},{17,9},{25,1},{2,26},{10... | collective-permute-start | bytes 393224 | tf_op jit(solution)/shard_map/ppermute | solution.py:460
  15.1 11.5 %collective-permute-start.4 = (bf16[4,128,128]{2,1,0:T(8,128)(2,1)S(1)}, bf16[4,128,128]{2,1,0:T(8,128)(2,1)S(1)}, u32[]{:S(2)}, u32[]{:S(2)}) collective-permute-start(bf16[4,128,128]{2,1,0:T(8,128)(2,1)S(1)} %shard_map.47.refs_0_), channel_id=1, source_target_pairs={{0,16},{8,24},{16,0},{24,8},{1,17},{9,25},{17,1},{25,9},{2,18},{10... | collective-permute-start | bytes 393224 | tf_op jit(solution)/shard_map/ppermute | solution.py:460
  15.1 11.5 %collective-permute-start.3 = (bf16[4,128,128]{2,1,0:T(8,128)(2,1)S(1)}, bf16[4,128,128]{2,1,0:T(8,128)(2,1)S(1)}, u32[]{:S(2)}, u32[]{:S(2)}) collective-permute-start(bf16[4,128,128]{2,1,0:T(8,128)(2,1)S(1)} %shard_map.47.refs_0_), channel_id=1, source_target_pairs={{0,8},{8,0},{16,24},{24,16},{1,9},{9,1},{17,25},{25,17},{2,10},{10... | collective-permute-start | bytes 393224 | tf_op jit(solution)/shard_map/ppermute | solution.py:460
  17.1 9.5 %copy-start.1 = (s32[480]{0:T(512)S(1)}, s32[480]{0:T(512)}, u32[]{:S(2)}) copy-start(s32[480]{0:T(512)} %param.7) | copy-start | bytes 5764
  17.1 9.5 %collective-permute-start.9 = (bf16[64,256]{1,0:T(8,128)(2,1)S(1)}, bf16[64,256]{1,0:T(8,128)(2,1)S(1)}, u32[]{:S(2)}, u32[]{:S(2)}) collective-permute-start(bf16[64,256]{1,0:T(8,128)(2,1)S(1)} %get-tuple-element.35), channel_id=1, source_target_pairs={{8,0},{16,8},{24,16},{9,1},{17,9},{25,17},{10,2},{18,10},{26,18},{... | collective-permute-start | bytes 98312 | tf_op jit(solution)/shard_map/ppermute | solution.py:484
  30.3 2.5 %collective-permute-start.10 = (f32[4,16,768]{2,1,0:T(8,128)S(1)}, f32[4,16,768]{2,1,0:T(8,128)S(1)}, u32[]{:S(2)}, u32[]{:S(2)}) collective-permute-start(f32[4,16,768]{2,1,0:T(8,128)S(1)} %get-tuple-element.38.after), channel_id=1, source_target_pairs={{0,2},{2,0},{4,6},{6,4},{1,3},{3,1},{5,7},{7,5},{8,10},{10,8},{12,... | collective-permute-start | bytes 589832 | tf_op jit(solution)/shard_map/ppermute | solution.py:524
  30.4 6.0 %copy-start = (bf16[480,512]{1,0:T(8,128)(2,1)S(1)}, bf16[480,512]{1,0:T(8,128)(2,1)}, u32[]{:S(2)}) copy-start(bf16[480,512]{1,0:T(8,128)(2,1)} %wave_ref.1) | copy-start | bytes 1474564
  32.8 4.4 %collective-permute-start.11 = (f32[16,768]{1,0:T(8,128)S(1)}, f32[16,768]{1,0:T(8,128)S(1)}, u32[]{:S(2)}, u32[]{:S(2)}) collective-permute-start(f32[16,768]{1,0:T(8,128)S(1)} %get-tuple-element.40), channel_id=1, source_target_pairs={{0,1},{1,0},{2,3},{3,2},{4,5},{5,4},{6,7},{7,6},{8,9},{9,8},{10,11... | collective-permute-start | bytes 147464 | tf_op jit(solution)/shard_map/ppermute | solution.py:469
  33.5 4.1 %collective-permute-start.12 = (f32[16,768]{1,0:T(8,128)S(1)}, f32[16,768]{1,0:T(8,128)S(1)}, u32[]{:S(2)}, u32[]{:S(2)}) collective-permute-start(f32[16,768]{1,0:T(8,128)S(1)} %get-tuple-element.41), channel_id=1, source_target_pairs={{0,4},{1,5},{2,6},{3,7},{4,0},{5,1},{6,2},{7,3},{8,12},{9,13},{10,... | collective-permute-start | bytes 147464 | tf_op jit(solution)/shard_map/ppermute | solution.py:469
  34.8 5.0 %collective-permute-start.13 = (f32[16,768]{1,0:T(8,128)S(1)}, f32[16,768]{1,0:T(8,128)S(1)}, u32[]{:S(2)}, u32[]{:S(2)}) collective-permute-start(f32[16,768]{1,0:T(8,128)S(1)} %get-tuple-element.42), channel_id=1, source_target_pairs={{0,5},{1,4},{2,7},{3,6},{4,1},{5,0},{6,3},{7,2},{8,13},{9,12},{10,... | collective-permute-start | bytes 147464 | tf_op jit(solution)/shard_map/ppermute | solution.py:469

commit v16 on v15

--- a/solution.py
+++ b/solution.py
@@ -281,7 +281,7 @@
     gather(blocks[-1], (len(blocks) - 1) % 2)
 
 
-def first_dots_kernel(stations, channels, tm_count, *refs):
+def first_dots_kernel(outer_count, stations, channels, tm_count, *refs):
     tpls, (order_ref, samples_ref, halo_ref) = refs[:-12], refs[-12:-9]
     send_ref, edges_ref, left, scale_ref, mask_ref = refs[-9:-4]
     full, edges, shifts, products = refs[-4:]
@@ -291,6 +291,9 @@
     slab = chunk // group
     full[:, :chunk] = samples_ref[...]
     full[:, chunk:] = halo_ref[...]
+    tpls = [pack[...] for pack in tpls]
+    if len(tpls) > outer_count:
+        tpls = tpls[:-2] + [tpls[-2] + tpls[-1]]
     arrange(tpls, left)
     correlate(left, full, send_ref, slab, 1 - core, shifts, products)
     part_mask = read_masks(stations, channels, tm_count, tpls, order_ref, scale_ref, mask_ref)
@@ -347,7 +350,7 @@
     part = LANES // tm_count
     meta = lax.dot_general(
         spare_lanes(part, part * channels // padded),
-        jnp.concatenate([pack[...].reshape(INNER * rows, LANES) for pack in tpls], axis=0),
+        jnp.concatenate([pack.reshape(INNER * rows, LANES) for pack in tpls], axis=0),
         (((1,), (1,)), ((), ())),
         preferred_element_type=F32,
     )
@@ -456,10 +459,20 @@
         pack_kernel, [VMEM] * INNER, sds((INNER, rows, LANES), BF16), bytes_accessed=rows * LANES * 8
     )(pieces[0], got, *others)
 
-    tpls = [pack] + [
-        lax.ppermute(pack, "outer", [(b, b ^ flip) for b in range(outer_count)])
-        for flip in range(1, outer_count)
-    ]
+    def cross(part, route):
+        return lax.ppermute(part, "outer", route)
+
+    if outer_count == 4:
+        near = cross(pack, [(0, 1), (1, 0), (2, 3), (3, 2)])
+        far = cross(pack, [(0, 2), (2, 0), (1, 3), (3, 1)])
+        middle = cross(pack, [(1, 2), (2, 1)])
+        ends = cross(far, [(1, 0), (2, 3)])
+        tpls = [pack, near, far, middle, ends]
+    else:
+        tpls = [pack] + [
+            cross(pack, [(b, b ^ flip) for b in range(outer_count)])
+            for flip in range(1, outer_count)
+        ]
 
     half = group // 2
 
@@ -494,8 +507,8 @@
         ]
 
     send, edges, left, scale, mask = call(
-        functools.partial(first_dots_kernel, stations, channels, tm_count),
-        [VMEM] * (outer_count + 3),
+        functools.partial(first_dots_kernel, outer_count, stations, channels, tm_count),
+        [VMEM] * (len(tpls) + 3),
         [
             sds((half, count, slab + window), F32),
             sds((half, count, window), F32),
@@ -535,7 +548,7 @@
         [sds((blk_count, slab + window), F32)] * half,
         bytes_accessed=blk_count * slab * 12 * half,
     )(keep, got)
-    sums = [sums[0]] + [swap(sums[flip], flip) for flip in range(1, half)]
+    sums = [sums[0]] + [swap(sums[flip], flip) for flip in reversed(range(1, half))]
     return call(
         finish_kernel,
         [VMEM] * (half + 2),

time: 40.7 us -> 39.8 us (0.978)
  waiting for transfers between devices: 14.5 us -> 9.55 us
  starting transfers between devices: 16.4 us -> 20.3 us
    ppermute x3 -> x4, waiting for transfers between devices: 8.15 us -> 0.19 us  [cross(): return lax.ppermute(part, 'outer', route)]
    ppermute x1, waiting for transfers between devices: 0.01 us -> 5 us  [on_device(): lax.ppermute(head, 'outer', [(b, b - 1) for b in range(1, outer_count)])]
    ppermute x3 -> x4, starting transfers between devices: 4.45 us -> 7.48 us  [cross(): return lax.ppermute(part, 'outer', route)]
    ppermute x3, waiting for transfers between devices: 2.62 us -> 1.44 us  [plane(): return lax.ppermute(part, 'inner', [(b, b ^ flip) for b in range(INNER)])]
    ppermute x3, starting transfers between devices: 2.04 us -> 3.18 us  [plane(): return lax.ppermute(part, 'inner', [(b, b ^ flip) for b in range(INNER)])]
    ppermute x6, waiting for transfers between devices: 3.67 us -> 2.91 us  [swap(): return lax.ppermute(part, every, route)]
  transfers between devices with their start and end apart: 14 -> 15, of which waited for: 8 -> 8; matrix products, arithmetic and copies ran while one was open for 0% -> 0% of each run, Pallas kernels for 8% -> 9%
where the time goes in v16:
time: 39.8 us; the launch traced here: 39.6 us
  starting transfers between devices  20.3 us (51%)
  Pallas kernels  9.56 us (24%)
  waiting for transfers between devices  9.55 us (24%)
    ppermute x6, starting transfers between devices, swap(): return lax.ppermute(part, every, route)  8.27 us
    ppermute x4, starting transfers between devices, cross(): return lax.ppermute(part, 'outer', route)  7.48 us
    ppermute x1, waiting for transfers between devices, on_device(): lax.ppermute(head, 'outer', [(b, b - 1) for b in range(1, outer_count)])  5 us
    pallas_call x1, Pallas kernels, on_device(): call(functools.partial(first_dots_kernel, outer_count, stations, channels...  3.73 us
    ppermute x3, starting transfers between devices, plane(): return lax.ppermute(part, 'inner', [(b, b ^ flip) for b in range(INNER)])  3.18 us
    ppermute x6, waiting for transfers between devices, swap(): return lax.ppermute(part, every, route)  2.91 us
    pallas_call x1, Pallas kernels, on_device(): call(second_dots_kernel, [VMEM] * 4 + [AFTER], sds((half, count, slab + w...  2.42 us
    pallas_call x1, Pallas kernels, on_device(): call(functools.partial(prologue_kernel, tm_count), [HBM] * 4, [sds((padde...  1.7 us
  transfers between devices with their start and end apart: 15, of which 8 were waited for; matrix products, arithmetic and copies ran while one was open for 0% of the time, Pallas kernels for 9%

profile of v16, /device:TPU:0, one launch (start us, length us, event | category | flops | bytes accessed | tf_op | source)
XLA Modules:
  0.0 39.6 jit_solution(2740183289620923823)
XLA Ops:
  0.0 1.7 %shard_map.46 = (bf16[1152,128]{1,0:T(8,128)(2,1)S(1)}, bf16[256,512]{1,0:T(8,128)(2,1)S(1)}, bf16[128,128]{1,0:T(8,128)(2,1)S(1)}, bf16[128,128]{1,0:T(8,128)(2,1)S(1)}, bf16[128,128]{1,0:T(8,128)(2,1)S(1)}) custom-call(bf16[480,512]{1,0:T(8,128)(2,1)} %wave_ref.1, bf16[1,480,256]{2,1,0:T(8,128)(2,1)} %tpl_hbm.1, s32[1,160]{1,0:T(1,128)} %flag_hbm.1, ...), custom_call_target="tpu_custom_call" | custom-call | bytes 737280 | tf_op jit(solution)/shard_map/pallas_call | solution.py:432
  1.7 0.5 %collective-permute-start = (bf16[1152,128]{1,0:T(8,128)(2,1)S(1)}, bf16[1152,128]{1,0:T(8,128)(2,1)S(1)}, u32[]{:S(2)}, u32[]{:S(2)}) collective-permute-start(bf16[1152,128]{1,0:T(8,128)(2,1)S(1)} %get-tuple-element.26), channel_id=1, source_target_pairs={{0,2},{2,0},{4,6},{6,4},{1,3},{3,1},{5,7},{7,5},{8,10},{10,8},{12,... | collective-permute-start | bytes 884744 | tf_op jit(solution)/shard_map/ppermute | solution.py:454
  2.2 2.6 %collective-permute-start.1 = (bf16[128,128]{1,0:T(8,128)(2,1)S(1)}, bf16[128,128]{1,0:T(8,128)(2,1)S(1)}, u32[]{:S(2)}, u32[]{:S(2)}) collective-permute-start(bf16[128,128]{1,0:T(8,128)(2,1)S(1)} %get-tuple-element.27), channel_id=1, source_target_pairs={{0,4},{2,6},{4,0},{6,2},{1,5},{3,7},{5,1},{7,3},{8,12},{10,14},{12... | collective-permute-start | bytes 98312 | tf_op jit(solution)/shard_map/ppermute | solution.py:454
  5.0 1.8 %collective-permute-start.7 = (bf16[2,64,512]{2,1,0:T(8,128)(2,1)S(1)}, bf16[2,64,512]{2,1,0:T(8,128)(2,1)S(1)}, u32[]{:S(2)}, u32[]{:S(2)}) collective-permute-start(bf16[2,64,512]{2,1,0:T(8,128)(2,1)S(1)} %get-tuple-element.31), channel_id=1, source_target_pairs={{0,1},{1,0},{2,3},{3,2},{4,5},{5,4},{6,7},{7,6},{8,9},{9,8},{10,11... | collective-permute-start | bytes 393224 | tf_op jit(solution)/shard_map/ppermute | solution.py:482
  6.8 1.4 %collective-permute-done.2.both_ref = bf16[128,128]{1,0:T(8,128)(2,1)S(1)} collective-permute-done((bf16[128,128]{1,0:T(8,128)(2,1)S(1)}, bf16[128,128]{1,0:T(8,128)(2,1)S(1)}, u32[]{:S(2)}, u32[]{:S(2)}) %collective-permute-start.2) | collective-permute-done | bytes 32800 | tf_op jit(solution)/shard_map/ppermute | solution.py:454
  8.2 2.7 %collective-permute-start.4 = (bf16[4,128,128]{2,1,0:T(8,128)(2,1)S(1)}, bf16[4,128,128]{2,1,0:T(8,128)(2,1)S(1)}, u32[]{:S(2)}, u32[]{:S(2)}) collective-permute-start(bf16[4,128,128]{2,1,0:T(8,128)(2,1)S(1)} %shard_map.47.refs_0_), channel_id=1, source_target_pairs={{0,16},{16,0},{8,24},{24,8},{1,17},{17,1},{9,25},{25,9},{2,18},{18... | collective-permute-start | bytes 393224 | tf_op jit(solution)/shard_map/ppermute | solution.py:463
  10.8 0.9 %collective-permute-start.8 = (bf16[2,64,512]{2,1,0:T(8,128)(2,1)S(1)}, bf16[2,64,512]{2,1,0:T(8,128)(2,1)S(1)}, u32[]{:S(2)}, u32[]{:S(2)}) collective-permute-start(bf16[2,64,512]{2,1,0:T(8,128)(2,1)S(1)} %get-tuple-element.32), channel_id=1, source_target_pairs={{0,4},{1,5},{2,6},{3,7},{4,0},{5,1},{6,2},{7,3},{8,12},{9,13},{10,... | collective-permute-start | bytes 393224 | tf_op jit(solution)/shard_map/ppermute | solution.py:482
  11.7 2.1 %collective-permute-start.9 = (bf16[2,64,512]{2,1,0:T(8,128)(2,1)S(1)}, bf16[2,64,512]{2,1,0:T(8,128)(2,1)S(1)}, u32[]{:S(2)}, u32[]{:S(2)}) collective-permute-start(bf16[2,64,512]{2,1,0:T(8,128)(2,1)S(1)} %get-tuple-element.33), channel_id=1, source_target_pairs={{0,5},{1,4},{2,7},{3,6},{4,1},{5,0},{6,3},{7,2},{8,13},{9,12},{10,... | collective-permute-start | bytes 393224 | tf_op jit(solution)/shard_map/ppermute | solution.py:482
  13.8 0.7 %collective-permute-start.5 = (bf16[4,128,128]{2,1,0:T(8,128)(2,1)S(1)}, bf16[4,128,128]{2,1,0:T(8,128)(2,1)S(1)}, u32[]{:S(2)}, u32[]{:S(2)}) collective-permute-start(bf16[4,128,128]{2,1,0:T(8,128)(2,1)S(1)} %shard_map.47.refs_0_), channel_id=1, source_target_pairs={{8,16},{16,8},{9,17},{17,9},{10,18},{18,10},{11,19},{19,11},{12,20... | collective-permute-start | bytes 393224 | tf_op jit(solution)/shard_map/ppermute | solution.py:463
  14.5 2.9 %collective-permute-start.3 = (bf16[4,128,128]{2,1,0:T(8,128)(2,1)S(1)}, bf16[4,128,128]{2,1,0:T(8,128)(2,1)S(1)}, u32[]{:S(2)}, u32[]{:S(2)}) collective-permute-start(bf16[4,128,128]{2,1,0:T(8,128)(2,1)S(1)} %shard_map.47.refs_0_), channel_id=1, source_target_pairs={{0,8},{8,0},{16,24},{24,16},{1,9},{9,1},{17,25},{25,17},{2,10},{10... | collective-permute-start | bytes 393224 | tf_op jit(solution)/shard_map/ppermute | solution.py:463
  17.4 0.2 collective-permute-done.4.refs_2_
  17.5 1.3 %collective-permute-start.6 = (bf16[4,128,128]{2,1,0:T(8,128)(2,1)S(1)}, bf16[4,128,128]{2,1,0:T(8,128)(2,1)S(1)}, u32[]{:S(2)}, u32[]{:S(2)}) collective-permute-start(bf16[4,128,128]{2,1,0:T(8,128)(2,1)S(1)} %collective-permute-done.4.refs_2_), channel_id=1, source_target_pairs={{8,0},{16,24},{9,1},{17,25},{10,2},{18,26},{11,3},{19,27},{12,4},{... | collective-permute-start | bytes 393224 | tf_op jit(solution)/shard_map/ppermute | solution.py:463
  19.0 1.3 %collective-permute-start.10 = (bf16[64,256]{1,0:T(8,128)(2,1)S(1)}, bf16[64,256]{1,0:T(8,128)(2,1)S(1)}, u32[]{:S(2)}, u32[]{:S(2)}) collective-permute-start(bf16[64,256]{1,0:T(8,128)(2,1)S(1)} %get-tuple-element.35), channel_id=1, source_target_pairs={{8,0},{16,8},{24,16},{9,1},{17,9},{25,17},{10,2},{18,10},{26,18},{... | collective-permute-start | bytes 98312 | tf_op jit(solution)/shard_map/ppermute | solution.py:497
  20.3 5.0 %collective-permute-done.10.refs_7_.halo_ref = bf16[64,256]{1,0:T(8,128)(2,1)S(1)} collective-permute-done((bf16[64,256]{1,0:T(8,128)(2,1)S(1)}, bf16[64,256]{1,0:T(8,128)(2,1)S(1)}, u32[]{:S(2)}, u32[]{:S(2)}) %collective-permute-start.10) | collective-permute-done | bytes 32800 | tf_op jit(solution)/shard_map/ppermute | solution.py:497
  25.4 3.7 %shard_map.50 = (f32[4,16,768]{2,1,0:T(8,128)S(1)}, f32[4,16,256]{2,1,0:T(8,128)S(1)}, bf16[256,1024]{1,0:T(8,128)(2,1)S(1)}, f32[16,128]{1,0:T(8,128)S(1)}, bf16[16,480]{1,0:T(8,128)(2,1)S(1)}) custom-call(bf16[4,128,128]{2,1,0:T(8,128)(2,1)S(1)} %shard_map.47.refs_0_, bf16[4,128,128]{2,1,0:T(8,128)(2,1)S(1)} %collective-permute-done.3.refs_1_, ...), custom_call_target="tpu_custom_call" | custom-call | flops 1073741824 | bytes 524288 | tf_op jit(solution)/shard_map/pallas_call | solution.py:509
  29.2 2.4 %shard_map.51.keep_ref.after = f32[4,16,768]{2,1,0:T(8,128)S(1)} custom-call(bf16[256,1024]{1,0:T(8,128)(2,1)S(1)} %get-tuple-element.36.left, bf16[64,4096]{1,0:T(8,128)(2,1)S(1)} %get-tuple-element.34.refs_6_.samples_ref, bf16[64,256]{1,0:T(8,128)(2,1)S(1)} %collective-permute-done.10.refs_7_.halo_ref, f32[4,16,256]{2,1,0:T(8,128)S(1)} %get-tuple-element.37.edges_ref, ...), custom_call_target="tpu_custom_call" | custom-call | flops 1073741824 | bytes 524288 | tf_op jit(solution)/shard_map/pallas_call | solution.py:528
  31.7 1.9 %collective-permute-start.12 = (f32[16,768]{1,0:T(8,128)S(1)}, f32[16,768]{1,0:T(8,128)S(1)}, u32[]{:S(2)}, u32[]{:S(2)}) collective-permute-start(f32[16,768]{1,0:T(8,128)S(1)} %get-tuple-element.40), channel_id=1, source_target_pairs={{0,5},{1,4},{2,7},{3,6},{4,1},{5,0},{6,3},{7,2},{8,13},{9,12},{10,... | collective-permute-start | bytes 147464 | tf_op jit(solution)/shard_map/ppermute | solution.py:482
  33.6 1.2 %collective-permute-start.13 = (f32[16,768]{1,0:T(8,128)S(1)}, f32[16,768]{1,0:T(8,128)S(1)}, u32[]{:S(2)}, u32[]{:S(2)}) collective-permute-start(f32[16,768]{1,0:T(8,128)S(1)} %get-tuple-element.41), channel_id=1, source_target_pairs={{0,4},{1,5},{2,6},{3,7},{4,0},{5,1},{6,2},{7,3},{8,12},{9,13},{10,... | collective-permute-start | bytes 147464 | tf_op jit(solution)/shard_map/ppermute | solution.py:482
  34.8 0.4 %collective-permute-start.14 = (f32[16,768]{1,0:T(8,128)S(1)}, f32[16,768]{1,0:T(8,128)S(1)}, u32[]{:S(2)}, u32[]{:S(2)}) collective-permute-start(f32[16,768]{1,0:T(8,128)S(1)} %get-tuple-element.42), channel_id=1, source_target_pairs={{0,1},{1,0},{2,3},{3,2},{4,5},{5,4},{6,7},{7,6},{8,9},{9,8},{10,11... | collective-permute-start | bytes 147464 | tf_op jit(solution)/shard_map/ppermute | solution.py:482
  35.2 0.9 %shard_map.53.refs_4_ = f32[16,512]{1,0:T(8,128)S(1)} custom-call(bf16[480,512]{1,0:T(8,128)(2,1)S(1)} %copy-done, bf16[16,480]{1,0:T(8,128)(2,1)S(1)} %get-tuple-element.43.mask_ref, f32[4,16,768]{2,1,0:T(8,128)S(1)} %shard_map.51.keep_ref.after), custom_call_target="tpu_custom_call" | custom-call | flops 15728640 | bytes 491520 | tf_op jit(solution)/shard_map/pallas_call | solution.py:538
  36.1 0.7 %collective-permute-done.12.refs_1_ = f32[16,768]{1,0:T(8,128)S(1)} collective-permute-done((f32[16,768]{1,0:T(8,128)S(1)}, f32[16,768]{1,0:T(8,128)S(1)}, u32[]{:S(2)}, u32[]{:S(2)}) %collective-permute-start.12) | collective-permute-done | bytes 49184 | tf_op jit(solution)/shard_map/ppermute | solution.py:482
  36.8 1.0 %collective-permute-done.13.refs_2_ = f32[16,768]{1,0:T(8,128)S(1)} collective-permute-done((f32[16,768]{1,0:T(8,128)S(1)}, f32[16,768]{1,0:T(8,128)S(1)}, u32[]{:S(2)}, u32[]{:S(2)}) %collective-permute-start.13) | collective-permute-done | bytes 49184 | tf_op jit(solution)/shard_map/ppermute | solution.py:482
  37.8 1.0 %collective-permute-done.14.refs_3_ = f32[16,768]{1,0:T(8,128)S(1)} collective-permute-done((f32[16,768]{1,0:T(8,128)S(1)}, f32[16,768]{1,0:T(8,128)S(1)}, u32[]{:S(2)}, u32[]{:S(2)}) %collective-permute-start.14) | collective-permute-done | bytes 49184 | tf_op jit(solution)/shard_map/ppermute | solution.py:482
  38.9 0.7 %shard_map.54 = f32[16,512]{1,0:T(8,128)} custom-call(f32[16,768]{1,0:T(8,128)S(1)} %get-tuple-element.39.refs_0_, f32[16,768]{1,0:T(8,128)S(1)} %collective-permute-done.12.refs_1_, f32[16,768]{1,0:T(8,128)S(1)} %collective-permute-done.13.refs_2_, f32[16,768]{1,0:T(8,128)S(1)} %collective-permute-done.14.refs_3_, f32[16,512]{1,0:T(8,128)S(1)} %shard_map.53.refs_4_, ...), custom_call_target="tpu_custom_call" | custom-call | bytes 196608 | tf_op jit(solution)/shard_map/pallas_call | solution.py:552
  (19 shorter events, 0.6 us)
Async XLA Ops:
  1.7 3.2 %collective-permute-start = (bf16[1152,128]{1,0:T(8,128)(2,1)S(1)}, bf16[1152,128]{1,0:T(8,128)(2,1)S(1)}, u32[]{:S(2)}, u32[]{:S(2)}) collective-permute-start(bf16[1152,128]{1,0:T(8,128)(2,1)S(1)} %get-tuple-element.26), channel_id=1, source_target_pairs={{0,2},{2,0},{4,6},{6,4},{1,3},{3,1},{5,7},{7,5},{8,10},{10,8},{12,... | collective-permute-start | bytes 884744 | tf_op jit(solution)/shard_map/ppermute | solution.py:454
  2.2 4.6 %collective-permute-start.1 = (bf16[128,128]{1,0:T(8,128)(2,1)S(1)}, bf16[128,128]{1,0:T(8,128)(2,1)S(1)}, u32[]{:S(2)}, u32[]{:S(2)}) collective-permute-start(bf16[128,128]{1,0:T(8,128)(2,1)S(1)} %get-tuple-element.27), channel_id=1, source_target_pairs={{0,4},{2,6},{4,0},{6,2},{1,5},{3,7},{5,1},{7,3},{8,12},{10,14},{12... | collective-permute-start | bytes 98312 | tf_op jit(solution)/shard_map/ppermute | solution.py:454
  4.8 3.3 %collective-permute-start.2 = (bf16[128,128]{1,0:T(8,128)(2,1)S(1)}, bf16[128,128]{1,0:T(8,128)(2,1)S(1)}, u32[]{:S(2)}, u32[]{:S(2)}) collective-permute-start(bf16[128,128]{1,0:T(8,128)(2,1)S(1)} %get-tuple-element.28), channel_id=1, source_target_pairs={{0,6},{2,4},{4,2},{6,0},{1,7},{3,5},{5,3},{7,1},{8,14},{10,12},{12... | collective-permute-start | bytes 98312 | tf_op jit(solution)/shard_map/ppermute | solution.py:454
  5.0 9.5 %collective-permute-start.7 = (bf16[2,64,512]{2,1,0:T(8,128)(2,1)S(1)}, bf16[2,64,512]{2,1,0:T(8,128)(2,1)S(1)}, u32[]{:S(2)}, u32[]{:S(2)}) collective-permute-start(bf16[2,64,512]{2,1,0:T(8,128)(2,1)S(1)} %get-tuple-element.31), channel_id=1, source_target_pairs={{0,1},{1,0},{2,3},{3,2},{4,5},{5,4},{6,7},{7,6},{8,9},{9,8},{10,11... | collective-permute-start | bytes 393224 | tf_op jit(solution)/shard_map/ppermute | solution.py:482
  8.2 9.3 %collective-permute-start.4 = (bf16[4,128,128]{2,1,0:T(8,128)(2,1)S(1)}, bf16[4,128,128]{2,1,0:T(8,128)(2,1)S(1)}, u32[]{:S(2)}, u32[]{:S(2)}) collective-permute-start(bf16[4,128,128]{2,1,0:T(8,128)(2,1)S(1)} %shard_map.47.refs_0_), channel_id=1, source_target_pairs={{0,16},{16,0},{8,24},{24,8},{1,17},{17,1},{9,25},{25,9},{2,18},{18... | collective-permute-start | bytes 393224 | tf_op jit(solution)/shard_map/ppermute | solution.py:463
  10.8 8.1 %collective-permute-start.8 = (bf16[2,64,512]{2,1,0:T(8,128)(2,1)S(1)}, bf16[2,64,512]{2,1,0:T(8,128)(2,1)S(1)}, u32[]{:S(2)}, u32[]{:S(2)}) collective-permute-start(bf16[2,64,512]{2,1,0:T(8,128)(2,1)S(1)} %get-tuple-element.32), channel_id=1, source_target_pairs={{0,4},{1,5},{2,6},{3,7},{4,0},{5,1},{6,2},{7,3},{8,12},{9,13},{10,... | collective-permute-start | bytes 393224 | tf_op jit(solution)/shard_map/ppermute | solution.py:482
  11.7 7.2 %collective-permute-start.9 = (bf16[2,64,512]{2,1,0:T(8,128)(2,1)S(1)}, bf16[2,64,512]{2,1,0:T(8,128)(2,1)S(1)}, u32[]{:S(2)}, u32[]{:S(2)}) collective-permute-start(bf16[2,64,512]{2,1,0:T(8,128)(2,1)S(1)} %get-tuple-element.33), channel_id=1, source_target_pairs={{0,5},{1,4},{2,7},{3,6},{4,1},{5,0},{6,3},{7,2},{8,13},{9,12},{10,... | collective-permute-start | bytes 393224 | tf_op jit(solution)/shard_map/ppermute | solution.py:482
  13.8 6.5 %collective-permute-start.5 = (bf16[4,128,128]{2,1,0:T(8,128)(2,1)S(1)}, bf16[4,128,128]{2,1,0:T(8,128)(2,1)S(1)}, u32[]{:S(2)}, u32[]{:S(2)}) collective-permute-start(bf16[4,128,128]{2,1,0:T(8,128)(2,1)S(1)} %shard_map.47.refs_0_), channel_id=1, source_target_pairs={{8,16},{16,8},{9,17},{17,9},{10,18},{18,10},{11,19},{19,11},{12,20... | collective-permute-start | bytes 393224 | tf_op jit(solution)/shard_map/ppermute | solution.py:463
  14.5 5.9 %collective-permute-start.3 = (bf16[4,128,128]{2,1,0:T(8,128)(2,1)S(1)}, bf16[4,128,128]{2,1,0:T(8,128)(2,1)S(1)}, u32[]{:S(2)}, u32[]{:S(2)}) collective-permute-start(bf16[4,128,128]{2,1,0:T(8,128)(2,1)S(1)} %shard_map.47.refs_0_), channel_id=1, source_target_pairs={{0,8},{8,0},{16,24},{24,16},{1,9},{9,1},{17,25},{25,17},{2,10},{10... | collective-permute-start | bytes 393224 | tf_op jit(solution)/shard_map/ppermute | solution.py:463
  17.5 7.8 %collective-permute-start.6 = (bf16[4,128,128]{2,1,0:T(8,128)(2,1)S(1)}, bf16[4,128,128]{2,1,0:T(8,128)(2,1)S(1)}, u32[]{:S(2)}, u32[]{:S(2)}) collective-permute-start(bf16[4,128,128]{2,1,0:T(8,128)(2,1)S(1)} %collective-permute-done.4.refs_2_), channel_id=1, source_target_pairs={{8,0},{16,24},{9,1},{17,25},{10,2},{18,26},{11,3},{19,27},{12,4},{... | collective-permute-start | bytes 393224 | tf_op jit(solution)/shard_map/ppermute | solution.py:463
  19.0 6.4 %copy-start.1 = (s32[480]{0:T(512)S(1)}, s32[480]{0:T(512)}, u32[]{:S(2)}) copy-start(s32[480]{0:T(512)} %param.7) | copy-start | bytes 5764
  19.0 6.3 %collective-permute-start.10 = (bf16[64,256]{1,0:T(8,128)(2,1)S(1)}, bf16[64,256]{1,0:T(8,128)(2,1)S(1)}, u32[]{:S(2)}, u32[]{:S(2)}) collective-permute-start(bf16[64,256]{1,0:T(8,128)(2,1)S(1)} %get-tuple-element.35), channel_id=1, source_target_pairs={{8,0},{16,8},{24,16},{9,1},{17,9},{25,17},{10,2},{18,10},{26,18},{... | collective-permute-start | bytes 98312 | tf_op jit(solution)/shard_map/ppermute | solution.py:497
  29.1 2.5 %collective-permute-start.11 = (f32[4,16,768]{2,1,0:T(8,128)S(1)}, f32[4,16,768]{2,1,0:T(8,128)S(1)}, u32[]{:S(2)}, u32[]{:S(2)}) collective-permute-start(f32[4,16,768]{2,1,0:T(8,128)S(1)} %get-tuple-element.38.after), channel_id=1, source_target_pairs={{0,2},{2,0},{4,6},{6,4},{1,3},{3,1},{5,7},{7,5},{8,10},{10,8},{12,... | collective-permute-start | bytes 589832 | tf_op jit(solution)/shard_map/ppermute | solution.py:537
  29.2 6.1 %copy-start = (bf16[480,512]{1,0:T(8,128)(2,1)S(1)}, bf16[480,512]{1,0:T(8,128)(2,1)}, u32[]{:S(2)}) copy-start(bf16[480,512]{1,0:T(8,128)(2,1)} %wave_ref.1) | copy-start | bytes 1474564
  31.7 5.1 %collective-permute-start.12 = (f32[16,768]{1,0:T(8,128)S(1)}, f32[16,768]{1,0:T(8,128)S(1)}, u32[]{:S(2)}, u32[]{:S(2)}) collective-permute-start(f32[16,768]{1,0:T(8,128)S(1)} %get-tuple-element.40), channel_id=1, source_target_pairs={{0,5},{1,4},{2,7},{3,6},{4,1},{5,0},{6,3},{7,2},{8,13},{9,12},{10,... | collective-permute-start | bytes 147464 | tf_op jit(solution)/shard_map/ppermute | solution.py:482
  33.6 4.2 %collective-permute-start.13 = (f32[16,768]{1,0:T(8,128)S(1)}, f32[16,768]{1,0:T(8,128)S(1)}, u32[]{:S(2)}, u32[]{:S(2)}) collective-permute-start(f32[16,768]{1,0:T(8,128)S(1)} %get-tuple-element.41), channel_id=1, source_target_pairs={{0,4},{1,5},{2,6},{3,7},{4,0},{5,1},{6,2},{7,3},{8,12},{9,13},{10,... | collective-permute-start | bytes 147464 | tf_op jit(solution)/shard_map/ppermute | solution.py:482
  34.8 4.1 %collective-permute-start.14 = (f32[16,768]{1,0:T(8,128)S(1)}, f32[16,768]{1,0:T(8,128)S(1)}, u32[]{:S(2)}, u32[]{:S(2)}) collective-permute-start(f32[16,768]{1,0:T(8,128)S(1)} %get-tuple-element.42), channel_id=1, source_target_pairs={{0,1},{1,0},{2,3},{3,2},{4,5},{5,4},{6,7},{7,6},{8,9},{9,8},{10,11... | collective-permute-start | bytes 147464 | tf_op jit(solution)/shard_map/ppermute | solution.py:482

commit v17 on v16

--- a/solution.py
+++ b/solution.py
@@ -12,6 +12,7 @@
 INNER = 4
 FINE = 16
 MIB = 1024 * 1024
+RELAY_FLOPS = 6 * 10**9
 
 BF16 = jnp.bfloat16
 F32 = jnp.float32
@@ -172,6 +173,10 @@
         send_ref[tile * half : (tile + 1) * half, :] = grouped[theirs, columns]
 
 
+def relay_kernel(in_ref, out_ref):
+    out_ref[...] = in_ref[...]
+
+
 def pack_kernel(mine_ref, core_ref, y_ref, both_ref, out_ref):
     inner = lax.axis_index("inner")
     rows = mine_ref.shape[0]
@@ -181,31 +186,56 @@
     out_ref[inner ^ 3] = both_ref[...]
 
 
-def split_kernel(tm_count, keep_ref, got_ref, *outs):
+def head_kernel(keep_ref, got_ref, out_ref):
+    core = lax.rem(lax.axis_index("inner"), 2)
+    half, window = out_ref.shape
+
+    @pl.when(core == 0)
+    def _():
+        out_ref[...] = keep_ref[:, :window]
+
+    @pl.when(core == 1)
+    def _():
+        for tile in range(window // LANES):
+            out_ref[:, tile * LANES : (tile + 1) * LANES] = got_ref[
+                tile * half : (tile + 1) * half, :
+            ]
+
+
+def split_kernel(tm_count, keep_ref, got_ref, halo_ref, after, *outs):
+    del after
     my_inner = lax.axis_index("inner")
     core = lax.rem(my_inner, 2)
     me = lax.div(my_inner, 2) * tm_count + lax.axis_index("tm")
-    part = outs[0].shape[1]
+    part = outs[0].shape[0]
     half, slab = keep_ref.shape
     for flip, out_ref in enumerate(outs):
         start = (me ^ flip) * part
-        out_ref[core] = keep_ref[pl.ds(pl.multiple_of(start, part), part), :]
+        rows = pl.ds(pl.multiple_of(start, part), part)
+        out_ref[:, pl.ds(pl.multiple_of(core * slab, slab), slab)] = keep_ref[rows, :]
         for tile in range(slab // LANES):
-            rows = pl.ds(pl.multiple_of(tile * half + start, part), part)
-            out_ref[1 - core, :, tile * LANES : (tile + 1) * LANES] = got_ref[rows, :]
-
-
-def join_kernel(tm_count, *refs):
-    parts, out_ref, head_ref = refs[:-2], refs[-2], refs[-1]
+            theirs = pl.ds(pl.multiple_of(tile * half + start, part), part)
+            lanes = pl.multiple_of((1 - core) * slab + tile * LANES, LANES)
+            out_ref[:, pl.ds(lanes, LANES)] = got_ref[theirs, :]
+        out_ref[:, 2 * slab :] = halo_ref[rows, :]
+
+
+def join_kernel(tm_count, slab, *refs):
+    parts, out_ref = refs[:-1], refs[-1]
     me = lax.div(lax.axis_index("inner"), 2) * tm_count + lax.axis_index("tm")
-    slab = parts[0].shape[2]
+    count = len(parts)
     for flip, part in enumerate(parts):
         other = me ^ flip
         y, tm = lax.div(other, tm_count), lax.rem(other, tm_count)
         for core in range(2):
             place = (y * 2 + core) * tm_count + tm
-            out_ref[:, pl.ds(pl.multiple_of(place * slab, slab), slab)] = part[core]
-    head_ref[...] = out_ref[:, : head_ref.shape[1]]
+            out_ref[:, pl.ds(pl.multiple_of(place * slab, slab), slab)] = part[
+                :, core * slab : (core + 1) * slab
+            ]
+
+        @pl.when(other == 0)
+        def _():
+            out_ref[:, 2 * count * slab :] = part[:, 2 * slab :]
 
 
 def arrival(template):
@@ -282,15 +312,12 @@
 
 
 def first_dots_kernel(outer_count, stations, channels, tm_count, *refs):
-    tpls, (order_ref, samples_ref, halo_ref) = refs[:-12], refs[-12:-9]
-    send_ref, edges_ref, left, scale_ref, mask_ref = refs[-9:-4]
-    full, edges, shifts, products = refs[-4:]
+    tpls, (order_ref, full) = refs[:-10], refs[-10:-8]
+    send_ref, edges_ref, left, scale_ref, mask_ref = refs[-8:-3]
+    edges, shifts, products = refs[-3:]
     core = lax.rem(lax.axis_index("inner"), 2)
     group, _, window = edges.shape
-    chunk = samples_ref.shape[1]
-    slab = chunk // group
-    full[:, :chunk] = samples_ref[...]
-    full[:, chunk:] = halo_ref[...]
+    slab = (full.shape[1] - window) // group
     tpls = [pack[...] for pack in tpls]
     if len(tpls) > outer_count:
         tpls = tpls[:-2] + [tpls[-2] + tpls[-1]]
@@ -315,12 +342,8 @@
             edges_ref[y * run + tm] = edges[(2 * y + core) * run + tm]
 
 
-def second_dots_kernel(left, samples_ref, halo_ref, edges_ref, after, keep_ref, *scratch):
+def second_dots_kernel(left, full, edges_ref, after, keep_ref, shifts, products):
     del after
-    full, shifts, products = scratch
-    chunk = samples_ref.shape[1]
-    full[:, :chunk] = samples_ref[...]
-    full[:, chunk:] = halo_ref[...]
     core = lax.rem(lax.axis_index("inner"), 2)
     slab = keep_ref.shape[2] - edges_ref.shape[2]
     correlate(left, full, keep_ref, slab, core, shifts, products)
@@ -466,7 +489,8 @@
         near = cross(pack, [(0, 1), (1, 0), (2, 3), (3, 2)])
         far = cross(pack, [(0, 2), (2, 0), (1, 3), (3, 1)])
         middle = cross(pack, [(1, 2), (2, 1)])
-        ends = cross(far, [(1, 0), (2, 3)])
+        relay = call(relay_kernel, [VMEM], sds(pack.shape, BF16), flops=RELAY_FLOPS)
+        ends = cross(relay(far), [(1, 0), (2, 3)])
         tpls = [pack, near, far, middle, ends]
     else:
         tpls = [pack] + [
@@ -481,20 +505,24 @@
         route = [(i, i ^ (2 * tm_count * y + tm)) for i in range(total)]
         return lax.ppermute(part, every, route)
 
+    head = call(
+        head_kernel, [VMEM] * 2, sds((padded // 2, window), BF16), bytes_accessed=padded * window
+    )(keep, got)
+    from_first = [(o * INNER + core) * tm_count for o in range(1, outer_count) for core in range(2)]
+    halo = lax.ppermute(head, every, [(i, i - INNER * tm_count) for i in from_first])
     parts = call(
         functools.partial(split_kernel, tm_count),
-        [VMEM] * 2,
-        [sds((2, part, slab), BF16)] * half,
+        [VMEM] * 3 + [AFTER],
+        [sds((part, 2 * slab + window), BF16)] * half,
         bytes_accessed=padded * slab * 2,
-    )(keep, got)
+    )(keep, got, halo, pack)
     waves = [parts[0]] + [swap(parts[flip], flip) for flip in range(1, half)]
-    samples, head = call(
-        functools.partial(join_kernel, tm_count),
+    samples = call(
+        functools.partial(join_kernel, tm_count, slab),
         [VMEM] * half,
-        [sds((part, chunk), BF16), sds((part, window), BF16)],
+        sds((part, chunk + window), BF16),
         bytes_accessed=part * chunk * 4,
     )(*waves)
-    halo = lax.ppermute(head, "outer", [(b, b - 1) for b in range(1, outer_count)])
 
     depth = window // FINE * part
     count = blk_count
@@ -508,7 +536,7 @@
 
     send, edges, left, scale, mask = call(
         functools.partial(first_dots_kernel, outer_count, stations, channels, tm_count),
-        [VMEM] * (len(tpls) + 3),
+        [VMEM] * (len(tpls) + 2),
         [
             sds((half, count, slab + window), F32),
             sds((half, count, window), F32),
@@ -516,24 +544,20 @@
             sds((count, LANES), F32),
             sds((count, channels), BF16),
         ],
-        [
-            pltpu.VMEM((part, chunk + window), BF16),
-            pltpu.VMEM((group, count, window), F32),
-        ]
-        + scratch(),
+        [pltpu.VMEM((group, count, window), F32)] + scratch(),
         flops=work,
         bytes_accessed=part * chunk * 2,
         vmem=36,
-    )(*tpls, order_row, samples, halo)
+    )(*tpls, order_row, samples)
     keep = call(
         second_dots_kernel,
-        [VMEM] * 4 + [AFTER],
+        [VMEM] * 3 + [AFTER],
         sds((half, count, slab + window), F32),
-        [pltpu.VMEM((part, chunk + window), BF16)] + scratch(),
+        scratch(),
         flops=work,
         bytes_accessed=part * chunk * 2,
         vmem=36,
-    )(left, samples, halo, edges, send)
+    )(left, samples, edges, send)
     got = lax.ppermute(send, "inner", [(b, b ^ 1) for b in range(INNER)])
     power = call(
         functools.partial(power_kernel, window),

time: 39.8 us -> 41.1 us (1.033)
  waiting for transfers between devices: 9.55 us -> 13.4 us
  starting transfers between devices: 20.3 us -> 18.1 us
    ppermute x1, waiting for transfers between devices: 5 us -> 0.01 us  [on_device(): lax.ppermute(head, every, [(i, i - INNER * tm_count) for i in from_first])]
    ppermute x6, waiting for transfers between devices: 2.91 us -> 7.11 us  [swap(): return lax.ppermute(part, every, route)]
    ppermute x4, waiting for transfers between devices: 0.19 us -> 4.31 us  [cross(): return lax.ppermute(part, 'outer', route)]
    ppermute x6, starting transfers between devices: 8.27 us -> 6.05 us  [swap(): return lax.ppermute(part, every, route)]
    ppermute x3, waiting for transfers between devices: 1.44 us -> 1.96 us  [plane(): return lax.ppermute(part, 'inner', [(b, b ^ flip) for b in range(INNER)])]
    pallas_call x3 -> x5, Pallas kernels: 2.54 us -> 2.47 us  [the longest x1 2.31 us: on_device(): call(second_dots_kernel, [VMEM] * 3 + [AFTER], sds((half, count, slab + w...]
  transfers between devices with their start and end apart: 15 -> 15, of which waited for: 8 -> 10; matrix products, arithmetic and copies ran while one was open for 0% -> 0% of each run, Pallas kernels for 9% -> 8%
where the time goes in v17:
time: 41.1 us; the launch traced here: 40.9 us
  starting transfers between devices  18.1 us (44%)
  waiting for transfers between devices  13.4 us (33%)
  Pallas kernels  9.31 us (23%)
    ppermute x4, starting transfers between devices, cross(): return lax.ppermute(part, 'outer', route)  7.48 us
    ppermute x6, waiting for transfers between devices, swap(): return lax.ppermute(part, every, route)  7.11 us
    ppermute x6, starting transfers between devices, swap(): return lax.ppermute(part, every, route)  6.05 us
    ppermute x4, waiting for transfers between devices, cross(): return lax.ppermute(part, 'outer', route)  4.31 us
    pallas_call x1, Pallas kernels, on_device(): call(functools.partial(first_dots_kernel, outer_count, stations, channels...  3.55 us
    ppermute x3, starting transfers between devices, plane(): return lax.ppermute(part, 'inner', [(b, b ^ flip) for b in range(INNER)])  3.18 us
    pallas_call x1, Pallas kernels, on_device(): call(second_dots_kernel, [VMEM] * 3 + [AFTER], sds((half, count, slab + w...  2.31 us
    ppermute x3, waiting for transfers between devices, plane(): return lax.ppermute(part, 'inner', [(b, b ^ flip) for b in range(INNER)])  1.96 us
  transfers between devices with their start and end apart: 15, of which 10 were waited for; matrix products, arithmetic and copies ran while one was open for 0% of the time, Pallas kernels for 8%

profile of v17, /device:TPU:0, one launch (start us, length us, event | category | flops | bytes accessed | tf_op | source)
XLA Modules:
  0.0 40.9 jit_solution(13738818617939397272)
XLA Ops:
  0.0 1.7 %shard_map.46 = (bf16[1152,128]{1,0:T(8,128)(2,1)S(1)}, bf16[256,512]{1,0:T(8,128)(2,1)S(1)}, bf16[128,128]{1,0:T(8,128)(2,1)S(1)}, bf16[128,128]{1,0:T(8,128)(2,1)S(1)}, bf16[128,128]{1,0:T(8,128)(2,1)S(1)}) custom-call(bf16[480,512]{1,0:T(8,128)(2,1)} %wave_ref.1, bf16[1,480,256]{2,1,0:T(8,128)(2,1)} %tpl_hbm.1, s32[1,160]{1,0:T(1,128)} %flag_hbm.1, ...), custom_call_target="tpu_custom_call" | custom-call | bytes 737280 | tf_op jit(solution)/shard_map/pallas_call | solution.py:455
  2.2 2.6 %collective-permute-start.1 = (bf16[128,128]{1,0:T(8,128)(2,1)S(1)}, bf16[128,128]{1,0:T(8,128)(2,1)S(1)}, u32[]{:S(2)}, u32[]{:S(2)}) collective-permute-start(bf16[128,128]{1,0:T(8,128)(2,1)S(1)} %get-tuple-element.25), channel_id=1, source_target_pairs={{0,4},{2,6},{4,0},{6,2},{1,5},{3,7},{5,1},{7,3},{8,12},{10,14},{12... | collective-permute-start | bytes 98312 | tf_op jit(solution)/shard_map/ppermute | solution.py:477
  4.9 1.3 %collective-permute-start.7 = (bf16[256,256]{1,0:T(8,128)(2,1)S(1)}, bf16[256,256]{1,0:T(8,128)(2,1)S(1)}, u32[]{:S(2)}, u32[]{:S(2)}) collective-permute-start(bf16[256,256]{1,0:T(8,128)(2,1)S(1)} %shard_map.49), channel_id=1, source_target_pairs={{8,0},{10,2},{16,8},{18,10},{24,16},{26,18}} | collective-permute-start | bytes 393224 | tf_op jit(solution)/shard_map/ppermute | solution.py:512
  6.2 0.6 %collective-permute-done.1.y_ref = bf16[128,128]{1,0:T(8,128)(2,1)S(1)} collective-permute-done((bf16[128,128]{1,0:T(8,128)(2,1)S(1)}, bf16[128,128]{1,0:T(8,128)(2,1)S(1)}, u32[]{:S(2)}, u32[]{:S(2)}) %collective-permute-start.1) | collective-permute-done | bytes 32800 | tf_op jit(solution)/shard_map/ppermute | solution.py:477
  6.8 1.4 %collective-permute-done.2.both_ref = bf16[128,128]{1,0:T(8,128)(2,1)S(1)} collective-permute-done((bf16[128,128]{1,0:T(8,128)(2,1)S(1)}, bf16[128,128]{1,0:T(8,128)(2,1)S(1)}, u32[]{:S(2)}, u32[]{:S(2)}) %collective-permute-start.2) | collective-permute-done | bytes 32800 | tf_op jit(solution)/shard_map/ppermute | solution.py:477
  8.2 2.7 %collective-permute-start.4 = (bf16[4,128,128]{2,1,0:T(8,128)(2,1)S(1)}, bf16[4,128,128]{2,1,0:T(8,128)(2,1)S(1)}, u32[]{:S(2)}, u32[]{:S(2)}) collective-permute-start(bf16[4,128,128]{2,1,0:T(8,128)(2,1)S(1)} %shard_map.47.after.refs_0_), channel_id=1, source_target_pairs={{0,16},{16,0},{8,24},{24,8},{1,17},{17,1},{9,25},{25,9},{2,18},{18... | collective-permute-start | bytes 393224 | tf_op jit(solution)/shard_map/ppermute | solution.py:486
  10.8 0.7 %collective-permute-start.5 = (bf16[4,128,128]{2,1,0:T(8,128)(2,1)S(1)}, bf16[4,128,128]{2,1,0:T(8,128)(2,1)S(1)}, u32[]{:S(2)}, u32[]{:S(2)}) collective-permute-start(bf16[4,128,128]{2,1,0:T(8,128)(2,1)S(1)} %shard_map.47.after.refs_0_), channel_id=1, source_target_pairs={{8,16},{16,8},{9,17},{17,9},{10,18},{18,10},{11,19},{19,11},{12,20... | collective-permute-start | bytes 393224 | tf_op jit(solution)/shard_map/ppermute | solution.py:486
  11.5 2.9 %collective-permute-start.3 = (bf16[4,128,128]{2,1,0:T(8,128)(2,1)S(1)}, bf16[4,128,128]{2,1,0:T(8,128)(2,1)S(1)}, u32[]{:S(2)}, u32[]{:S(2)}) collective-permute-start(bf16[4,128,128]{2,1,0:T(8,128)(2,1)S(1)} %shard_map.47.after.refs_0_), channel_id=1, source_target_pairs={{0,8},{8,0},{16,24},{24,16},{1,9},{9,1},{17,25},{25,17},{2,10},{10... | collective-permute-start | bytes 393224 | tf_op jit(solution)/shard_map/ppermute | solution.py:486
  14.5 1.6 %collective-permute-start.8 = (bf16[64,1280]{1,0:T(8,128)(2,1)S(1)}, bf16[64,1280]{1,0:T(8,128)(2,1)S(1)}, u32[]{:S(2)}, u32[]{:S(2)}) collective-permute-start(bf16[64,1280]{1,0:T(8,128)(2,1)S(1)} %get-tuple-element.29), channel_id=1, source_target_pairs={{0,1},{1,0},{2,3},{3,2},{4,5},{5,4},{6,7},{7,6},{8,9},{9,8},{10,11... | collective-permute-start | bytes 491528 | tf_op jit(solution)/shard_map/ppermute | solution.py:506
  16.0 0.9 %collective-permute-start.9 = (bf16[64,1280]{1,0:T(8,128)(2,1)S(1)}, bf16[64,1280]{1,0:T(8,128)(2,1)S(1)}, u32[]{:S(2)}, u32[]{:S(2)}) collective-permute-start(bf16[64,1280]{1,0:T(8,128)(2,1)S(1)} %get-tuple-element.30), channel_id=1, source_target_pairs={{0,4},{1,5},{2,6},{3,7},{4,0},{5,1},{6,2},{7,3},{8,12},{9,13},{10,... | collective-permute-start | bytes 491528 | tf_op jit(solution)/shard_map/ppermute | solution.py:506
  16.9 3.1 %collective-permute-done.4.in_ref.refs_2_ = bf16[4,128,128]{2,1,0:T(8,128)(2,1)S(1)} collective-permute-done((bf16[4,128,128]{2,1,0:T(8,128)(2,1)S(1)}, bf16[4,128,128]{2,1,0:T(8,128)(2,1)S(1)}, u32[]{:S(2)}, u32[]{:S(2)}) %collective-permute-start.4) | collective-permute-done | bytes 131104 | tf_op jit(solution)/shard_map/ppermute | solution.py:486
  20.1 0.6 %collective-permute-done.8.refs_1_ = bf16[64,1280]{1,0:T(8,128)(2,1)S(1)} collective-permute-done((bf16[64,1280]{1,0:T(8,128)(2,1)S(1)}, bf16[64,1280]{1,0:T(8,128)(2,1)S(1)}, u32[]{:S(2)}, u32[]{:S(2)}) %collective-permute-start.8) | collective-permute-done | bytes 163872 | tf_op jit(solution)/shard_map/ppermute | solution.py:506
  20.7 1.3 %collective-permute-start.6 = (bf16[4,128,128]{2,1,0:T(8,128)(2,1)S(1)}, bf16[4,128,128]{2,1,0:T(8,128)(2,1)S(1)}, u32[]{:S(2)}, u32[]{:S(2)}) collective-permute-start(bf16[4,128,128]{2,1,0:T(8,128)(2,1)S(1)} %shard_map.48), channel_id=1, source_target_pairs={{8,0},{16,24},{9,1},{17,25},{10,2},{18,26},{11,3},{19,27},{12,4},{... | collective-permute-start | bytes 393224 | tf_op jit(solution)/shard_map/ppermute | solution.py:486
  22.0 1.4 %collective-permute-done.9.refs_2_ = bf16[64,1280]{1,0:T(8,128)(2,1)S(1)} collective-permute-done((bf16[64,1280]{1,0:T(8,128)(2,1)S(1)}, bf16[64,1280]{1,0:T(8,128)(2,1)S(1)}, u32[]{:S(2)}, u32[]{:S(2)}) %collective-permute-start.9) | collective-permute-done | bytes 163872 | tf_op jit(solution)/shard_map/ppermute | solution.py:506
  23.4 2.8 %collective-permute-done.10.refs_3_ = bf16[64,1280]{1,0:T(8,128)(2,1)S(1)} collective-permute-done((bf16[64,1280]{1,0:T(8,128)(2,1)S(1)}, bf16[64,1280]{1,0:T(8,128)(2,1)S(1)}, u32[]{:S(2)}, u32[]{:S(2)}) %collective-permute-start.10) | collective-permute-done | bytes 163872 | tf_op jit(solution)/shard_map/ppermute | solution.py:506
  26.3 1.2 %collective-permute-done.6.refs_4_ = bf16[4,128,128]{2,1,0:T(8,128)(2,1)S(1)} collective-permute-done((bf16[4,128,128]{2,1,0:T(8,128)(2,1)S(1)}, bf16[4,128,128]{2,1,0:T(8,128)(2,1)S(1)}, u32[]{:S(2)}, u32[]{:S(2)}) %collective-permute-start.6) | collective-permute-done | bytes 131104 | tf_op jit(solution)/shard_map/ppermute | solution.py:486
  27.5 3.5 %shard_map.52 = (f32[4,16,768]{2,1,0:T(8,128)S(1)}, f32[4,16,256]{2,1,0:T(8,128)S(1)}, bf16[256,1024]{1,0:T(8,128)(2,1)S(1)}, f32[16,128]{1,0:T(8,128)S(1)}, bf16[16,480]{1,0:T(8,128)(2,1)S(1)}) custom-call(bf16[4,128,128]{2,1,0:T(8,128)(2,1)S(1)} %shard_map.47.after.refs_0_, bf16[4,128,128]{2,1,0:T(8,128)(2,1)S(1)} %collective-permute-done.3.refs_1_, ...), custom_call_target="tpu_custom_call" | custom-call | flops 1073741824 | bytes 524288 | tf_op jit(solution)/shard_map/pallas_call | solution.py:537
  31.2 2.3 %shard_map.53.keep_ref.after = f32[4,16,768]{2,1,0:T(8,128)S(1)} custom-call(bf16[256,1024]{1,0:T(8,128)(2,1)S(1)} %get-tuple-element.32.left, bf16[64,4352]{1,0:T(8,128)(2,1)S(1)} %shard_map.51.refs_6_.full, f32[4,16,256]{2,1,0:T(8,128)S(1)} %get-tuple-element.33.edges_ref, f32[4,16,768]{2,1,0:T(8,128)S(1)} %get-tuple-element.34.after), custom_call_target="tpu_custom_call" | custom-call | flops 1073741824 | bytes 524288 | tf_op jit(solution)/shard_map/pallas_call | solution.py:552
  33.5 2.4 %collective-permute-start.12 = (f32[16,768]{1,0:T(8,128)S(1)}, f32[16,768]{1,0:T(8,128)S(1)}, u32[]{:S(2)}, u32[]{:S(2)}) collective-permute-start(f32[16,768]{1,0:T(8,128)S(1)} %get-tuple-element.36), channel_id=1, source_target_pairs={{0,5},{1,4},{2,7},{3,6},{4,1},{5,0},{6,3},{7,2},{8,13},{9,12},{10,... | collective-permute-start | bytes 147464 | tf_op jit(solution)/shard_map/ppermute | solution.py:506
  36.1 1.0 %collective-permute-start.14 = (f32[16,768]{1,0:T(8,128)S(1)}, f32[16,768]{1,0:T(8,128)S(1)}, u32[]{:S(2)}, u32[]{:S(2)}) collective-permute-start(f32[16,768]{1,0:T(8,128)S(1)} %get-tuple-element.38), channel_id=1, source_target_pairs={{0,1},{1,0},{2,3},{3,2},{4,5},{5,4},{6,7},{7,6},{8,9},{9,8},{10,11... | collective-permute-start | bytes 147464 | tf_op jit(solution)/shard_map/ppermute | solution.py:506
  37.1 0.9 %shard_map.55.refs_4_ = f32[16,512]{1,0:T(8,128)S(1)} custom-call(bf16[480,512]{1,0:T(8,128)(2,1)S(1)} %copy-done, bf16[16,480]{1,0:T(8,128)(2,1)S(1)} %get-tuple-element.39.mask_ref, f32[4,16,768]{2,1,0:T(8,128)S(1)} %shard_map.53.keep_ref.after), custom_call_target="tpu_custom_call" | custom-call | flops 15728640 | bytes 491520 | tf_op jit(solution)/shard_map/pallas_call | solution.py:562
  38.0 0.7 %collective-permute-done.12.refs_1_ = f32[16,768]{1,0:T(8,128)S(1)} collective-permute-done((f32[16,768]{1,0:T(8,128)S(1)}, f32[16,768]{1,0:T(8,128)S(1)}, u32[]{:S(2)}, u32[]{:S(2)}) %collective-permute-start.12) | collective-permute-done | bytes 49184 | tf_op jit(solution)/shard_map/ppermute | solution.py:506
  38.6 1.4 %collective-permute-done.13.refs_2_ = f32[16,768]{1,0:T(8,128)S(1)} collective-permute-done((f32[16,768]{1,0:T(8,128)S(1)}, f32[16,768]{1,0:T(8,128)S(1)}, u32[]{:S(2)}, u32[]{:S(2)}) %collective-permute-start.13) | collective-permute-done | bytes 49184 | tf_op jit(solution)/shard_map/ppermute | solution.py:506
  40.2 0.7 %shard_map.56 = f32[16,512]{1,0:T(8,128)} custom-call(f32[16,768]{1,0:T(8,128)S(1)} %get-tuple-element.35.refs_0_, f32[16,768]{1,0:T(8,128)S(1)} %collective-permute-done.12.refs_1_, f32[16,768]{1,0:T(8,128)S(1)} %collective-permute-done.13.refs_2_, f32[16,768]{1,0:T(8,128)S(1)} %collective-permute-done.14.refs_3_, f32[16,512]{1,0:T(8,128)S(1)} %shard_map.55.refs_4_, ...), custom_call_target="tpu_custom_call" | custom-call | bytes 196608 | tf_op jit(solution)/shard_map/pallas_call | solution.py:576
  (21 shorter events, 1.5 us)
Async XLA Ops:
  1.7 3.2 %collective-permute-start = (bf16[1152,128]{1,0:T(8,128)(2,1)S(1)}, bf16[1152,128]{1,0:T(8,128)(2,1)S(1)}, u32[]{:S(2)}, u32[]{:S(2)}) collective-permute-start(bf16[1152,128]{1,0:T(8,128)(2,1)S(1)} %get-tuple-element.24), channel_id=1, source_target_pairs={{0,2},{2,0},{4,6},{6,4},{1,3},{3,1},{5,7},{7,5},{8,10},{10,8},{12,... | collective-permute-start | bytes 884744 | tf_op jit(solution)/shard_map/ppermute | solution.py:477
  2.2 4.6 %collective-permute-start.1 = (bf16[128,128]{1,0:T(8,128)(2,1)S(1)}, bf16[128,128]{1,0:T(8,128)(2,1)S(1)}, u32[]{:S(2)}, u32[]{:S(2)}) collective-permute-start(bf16[128,128]{1,0:T(8,128)(2,1)S(1)} %get-tuple-element.25), channel_id=1, source_target_pairs={{0,4},{2,6},{4,0},{6,2},{1,5},{3,7},{5,1},{7,3},{8,12},{10,14},{12... | collective-permute-start | bytes 98312 | tf_op jit(solution)/shard_map/ppermute | solution.py:477
  4.8 3.3 %collective-permute-start.2 = (bf16[128,128]{1,0:T(8,128)(2,1)S(1)}, bf16[128,128]{1,0:T(8,128)(2,1)S(1)}, u32[]{:S(2)}, u32[]{:S(2)}) collective-permute-start(bf16[128,128]{1,0:T(8,128)(2,1)S(1)} %get-tuple-element.26), channel_id=1, source_target_pairs={{0,6},{2,4},{4,2},{6,0},{1,7},{3,5},{5,3},{7,1},{8,14},{10,12},{12... | collective-permute-start | bytes 98312 | tf_op jit(solution)/shard_map/ppermute | solution.py:477
  4.9 9.5 %collective-permute-start.7 = (bf16[256,256]{1,0:T(8,128)(2,1)S(1)}, bf16[256,256]{1,0:T(8,128)(2,1)S(1)}, u32[]{:S(2)}, u32[]{:S(2)}) collective-permute-start(bf16[256,256]{1,0:T(8,128)(2,1)S(1)} %shard_map.49), channel_id=1, source_target_pairs={{8,0},{10,2},{16,8},{18,10},{24,16},{26,18}} | collective-permute-start | bytes 393224 | tf_op jit(solution)/shard_map/ppermute | solution.py:512
  8.2 11.8 %collective-permute-start.4 = (bf16[4,128,128]{2,1,0:T(8,128)(2,1)S(1)}, bf16[4,128,128]{2,1,0:T(8,128)(2,1)S(1)}, u32[]{:S(2)}, u32[]{:S(2)}) collective-permute-start(bf16[4,128,128]{2,1,0:T(8,128)(2,1)S(1)} %shard_map.47.after.refs_0_), channel_id=1, source_target_pairs={{0,16},{16,0},{8,24},{24,8},{1,17},{17,1},{9,25},{25,9},{2,18},{18... | collective-permute-start | bytes 393224 | tf_op jit(solution)/shard_map/ppermute | solution.py:486
  10.8 15.5 %collective-permute-start.5 = (bf16[4,128,128]{2,1,0:T(8,128)(2,1)S(1)}, bf16[4,128,128]{2,1,0:T(8,128)(2,1)S(1)}, u32[]{:S(2)}, u32[]{:S(2)}) collective-permute-start(bf16[4,128,128]{2,1,0:T(8,128)(2,1)S(1)} %shard_map.47.after.refs_0_), channel_id=1, source_target_pairs={{8,16},{16,8},{9,17},{17,9},{10,18},{18,10},{11,19},{19,11},{12,20... | collective-permute-start | bytes 393224 | tf_op jit(solution)/shard_map/ppermute | solution.py:486
  11.5 14.8 %collective-permute-start.3 = (bf16[4,128,128]{2,1,0:T(8,128)(2,1)S(1)}, bf16[4,128,128]{2,1,0:T(8,128)(2,1)S(1)}, u32[]{:S(2)}, u32[]{:S(2)}) collective-permute-start(bf16[4,128,128]{2,1,0:T(8,128)(2,1)S(1)} %shard_map.47.after.refs_0_), channel_id=1, source_target_pairs={{0,8},{8,0},{16,24},{24,16},{1,9},{9,1},{17,25},{25,17},{2,10},{10... | collective-permute-start | bytes 393224 | tf_op jit(solution)/shard_map/ppermute | solution.py:486
  14.5 6.2 %collective-permute-start.8 = (bf16[64,1280]{1,0:T(8,128)(2,1)S(1)}, bf16[64,1280]{1,0:T(8,128)(2,1)S(1)}, u32[]{:S(2)}, u32[]{:S(2)}) collective-permute-start(bf16[64,1280]{1,0:T(8,128)(2,1)S(1)} %get-tuple-element.29), channel_id=1, source_target_pairs={{0,1},{1,0},{2,3},{3,2},{4,5},{5,4},{6,7},{7,6},{8,9},{9,8},{10,11... | collective-permute-start | bytes 491528 | tf_op jit(solution)/shard_map/ppermute | solution.py:506
  16.0 7.4 %collective-permute-start.9 = (bf16[64,1280]{1,0:T(8,128)(2,1)S(1)}, bf16[64,1280]{1,0:T(8,128)(2,1)S(1)}, u32[]{:S(2)}, u32[]{:S(2)}) collective-permute-start(bf16[64,1280]{1,0:T(8,128)(2,1)S(1)} %get-tuple-element.30), channel_id=1, source_target_pairs={{0,4},{1,5},{2,6},{3,7},{4,0},{5,1},{6,2},{7,3},{8,12},{9,13},{10,... | collective-permute-start | bytes 491528 | tf_op jit(solution)/shard_map/ppermute | solution.py:506
  20.0 6.2 %collective-permute-start.10 = (bf16[64,1280]{1,0:T(8,128)(2,1)S(1)}, bf16[64,1280]{1,0:T(8,128)(2,1)S(1)}, u32[]{:S(2)}, u32[]{:S(2)}) collective-permute-start(bf16[64,1280]{1,0:T(8,128)(2,1)S(1)} %get-tuple-element.31), channel_id=1, source_target_pairs={{0,5},{1,4},{2,7},{3,6},{4,1},{5,0},{6,3},{7,2},{8,13},{9,12},{10,... | collective-permute-start | bytes 491528 | tf_op jit(solution)/shard_map/ppermute | solution.py:506
  20.7 6.8 %collective-permute-start.6 = (bf16[4,128,128]{2,1,0:T(8,128)(2,1)S(1)}, bf16[4,128,128]{2,1,0:T(8,128)(2,1)S(1)}, u32[]{:S(2)}, u32[]{:S(2)}) collective-permute-start(bf16[4,128,128]{2,1,0:T(8,128)(2,1)S(1)} %shard_map.48), channel_id=1, source_target_pairs={{8,0},{16,24},{9,1},{17,25},{10,2},{18,26},{11,3},{19,27},{12,4},{... | collective-permute-start | bytes 393224 | tf_op jit(solution)/shard_map/ppermute | solution.py:486
  26.2 1.3 %copy-start.1 = (s32[480]{0:T(512)S(1)}, s32[480]{0:T(512)}, u32[]{:S(2)}) copy-start(s32[480]{0:T(512)} %param.7) | copy-start | bytes 5764
  31.1 2.4 %collective-permute-start.11 = (f32[4,16,768]{2,1,0:T(8,128)S(1)}, f32[4,16,768]{2,1,0:T(8,128)S(1)}, u32[]{:S(2)}, u32[]{:S(2)}) collective-permute-start(f32[4,16,768]{2,1,0:T(8,128)S(1)} %get-tuple-element.34.after), channel_id=1, source_target_pairs={{0,2},{2,0},{4,6},{6,4},{1,3},{3,1},{5,7},{7,5},{8,10},{10,8},{12,... | collective-permute-start | bytes 589832 | tf_op jit(solution)/shard_map/ppermute | solution.py:561
  31.1 5.9 %copy-start = (bf16[480,512]{1,0:T(8,128)(2,1)S(1)}, bf16[480,512]{1,0:T(8,128)(2,1)}, u32[]{:S(2)}) copy-start(bf16[480,512]{1,0:T(8,128)(2,1)} %wave_ref.1) | copy-start | bytes 1474564
  33.5 5.1 %collective-permute-start.12 = (f32[16,768]{1,0:T(8,128)S(1)}, f32[16,768]{1,0:T(8,128)S(1)}, u32[]{:S(2)}, u32[]{:S(2)}) collective-permute-start(f32[16,768]{1,0:T(8,128)S(1)} %get-tuple-element.36), channel_id=1, source_target_pairs={{0,5},{1,4},{2,7},{3,6},{4,1},{5,0},{6,3},{7,2},{8,13},{9,12},{10,... | collective-permute-start | bytes 147464 | tf_op jit(solution)/shard_map/ppermute | solution.py:506
  35.9 4.1 %collective-permute-start.13 = (f32[16,768]{1,0:T(8,128)S(1)}, f32[16,768]{1,0:T(8,128)S(1)}, u32[]{:S(2)}, u32[]{:S(2)}) collective-permute-start(f32[16,768]{1,0:T(8,128)S(1)} %get-tuple-element.37), channel_id=1, source_target_pairs={{0,4},{1,5},{2,6},{3,7},{4,0},{5,1},{6,2},{7,3},{8,12},{9,13},{10,... | collective-permute-start | bytes 147464 | tf_op jit(solution)/shard_map/ppermute | solution.py:506
  36.1 4.1 %collective-permute-start.14 = (f32[16,768]{1,0:T(8,128)S(1)}, f32[16,768]{1,0:T(8,128)S(1)}, u32[]{:S(2)}, u32[]{:S(2)}) collective-permute-start(f32[16,768]{1,0:T(8,128)S(1)} %get-tuple-element.38), channel_id=1, source_target_pairs={{0,1},{1,0},{2,3},{3,2},{4,5},{5,4},{6,7},{7,6},{8,9},{9,8},{10,11... | collective-permute-start | bytes 147464 | tf_op jit(solution)/shard_map/ppermute | solution.py:506

commit v18 on v17

--- a/solution.py
+++ b/solution.py
@@ -12,7 +12,6 @@
 INNER = 4
 FINE = 16
 MIB = 1024 * 1024
-RELAY_FLOPS = 6 * 10**9
 
 BF16 = jnp.bfloat16
 F32 = jnp.float32
@@ -171,10 +170,6 @@
     for tile in range(first // half):
         columns = slice(tile * LANES, (tile + 1) * LANES)
         send_ref[tile * half : (tile + 1) * half, :] = grouped[theirs, columns]
-
-
-def relay_kernel(in_ref, out_ref):
-    out_ref[...] = in_ref[...]
 
 
 def pack_kernel(mine_ref, core_ref, y_ref, both_ref, out_ref):
@@ -489,8 +484,7 @@
         near = cross(pack, [(0, 1), (1, 0), (2, 3), (3, 2)])
         far = cross(pack, [(0, 2), (2, 0), (1, 3), (3, 1)])
         middle = cross(pack, [(1, 2), (2, 1)])
-        relay = call(relay_kernel, [VMEM], sds(pack.shape, BF16), flops=RELAY_FLOPS)
-        ends = cross(relay(far), [(1, 0), (2, 3)])
+        ends = cross(far, [(1, 0), (2, 3)])
         tpls = [pack, near, far, middle, ends]
     else:
         tpls = [pack] + [

time: 41.1 us -> 43 us (1.046)
  waiting for transfers between devices: 13.4 us -> 16.6 us
  starting transfers between devices: 18.1 us -> 16.8 us
    ppermute x6, waiting for transfers between devices: 7.11 us -> 3.32 us  [swap(): return lax.ppermute(part, every, route)]
    ppermute x3, waiting for transfers between devices: 1.96 us -> 4.85 us  [plane(): return lax.ppermute(part, 'inner', [(b, b ^ flip) for b in range(INNER)])]
    ppermute x4, waiting for transfers between devices: 4.31 us -> 7.1 us  [cross(): return lax.ppermute(part, 'outer', route)]
    ppermute x4, starting transfers between devices: 7.48 us -> 5.34 us  [cross(): return lax.ppermute(part, 'outer', route)]
    ppermute x1, waiting for transfers between devices: 0.01 us -> 1.36 us  [on_device(): lax.ppermute(head, every, [(i, i - INNER * tm_count) for i in from_first])]
    ppermute x6, starting transfers between devices: 6.05 us -> 7.22 us  [swap(): return lax.ppermute(part, every, route)]
  transfers between devices with their start and end apart: 15 -> 15, of which waited for: 10 -> 11; matrix products, arithmetic and copies ran while one was open for 0% -> 0% of each run, Pallas kernels for 8% -> 8%
where the time goes in v18:
time: 43 us; the launch traced here: 42.8 us
  starting transfers between devices  16.8 us (39%)
  waiting for transfers between devices  16.6 us (39%)
  Pallas kernels  9.3 us (22%)
    ppermute x6, starting transfers between devices, swap(): return lax.ppermute(part, every, route)  7.22 us
    ppermute x4, waiting for transfers between devices, cross(): return lax.ppermute(part, 'outer', route)  7.1 us
    ppermute x4, starting transfers between devices, cross(): return lax.ppermute(part, 'outer', route)  5.34 us
    ppermute x3, waiting for transfers between devices, plane(): return lax.ppermute(part, 'inner', [(b, b ^ flip) for b in range(INNER)])  4.85 us
    pallas_call x1, Pallas kernels, on_device(): call(functools.partial(first_dots_kernel, outer_count, stations, channels...  3.55 us
    ppermute x6, waiting for transfers between devices, swap(): return lax.ppermute(part, every, route)  3.32 us
    ppermute x3, starting transfers between devices, plane(): return lax.ppermute(part, 'inner', [(b, b ^ flip) for b in range(INNER)])  2.85 us
    pallas_call x1, Pallas kernels, on_device(): call(second_dots_kernel, [VMEM] * 3 + [AFTER], sds((half, count, slab + w...  2.31 us
  transfers between devices with their start and end apart: 15, of which 11 were waited for; matrix products, arithmetic and copies ran while one was open for 0% of the time, Pallas kernels for 8%

profile of v18, /device:TPU:0, one launch (start us, length us, event | category | flops | bytes accessed | tf_op | source)
XLA Modules:
  0.0 42.8 jit_solution(9791447006397421255)
XLA Ops:
  0.0 1.7 %shard_map.46 = (bf16[1152,128]{1,0:T(8,128)(2,1)S(1)}, bf16[256,512]{1,0:T(8,128)(2,1)S(1)}, bf16[128,128]{1,0:T(8,128)(2,1)S(1)}, bf16[128,128]{1,0:T(8,128)(2,1)S(1)}, bf16[128,128]{1,0:T(8,128)(2,1)S(1)}) custom-call(bf16[480,512]{1,0:T(8,128)(2,1)} %wave_ref.1, bf16[1,480,256]{2,1,0:T(8,128)(2,1)} %tpl_hbm.1, s32[1,160]{1,0:T(1,128)} %flag_hbm.1, ...), custom_call_target="tpu_custom_call" | custom-call | bytes 737280 | tf_op jit(solution)/shard_map/pallas_call | solution.py:450
  2.2 1.2 %collective-permute-done.core_ref.got_ref = bf16[1152,128]{1,0:T(8,128)(2,1)S(1)} collective-permute-done((bf16[1152,128]{1,0:T(8,128)(2,1)S(1)}, bf16[1152,128]{1,0:T(8,128)(2,1)S(1)}, u32[]{:S(2)}, u32[]{:S(2)}) %collective-permute-start) | collective-permute-done | bytes 294944 | tf_op jit(solution)/shard_map/ppermute | solution.py:472
  3.4 1.3 %collective-permute-start.7 = (bf16[256,256]{1,0:T(8,128)(2,1)S(1)}, bf16[256,256]{1,0:T(8,128)(2,1)S(1)}, u32[]{:S(2)}, u32[]{:S(2)}) collective-permute-start(bf16[256,256]{1,0:T(8,128)(2,1)S(1)} %shard_map.48), channel_id=1, source_target_pairs={{8,0},{10,2},{16,8},{18,10},{24,16},{26,18}} | collective-permute-start | bytes 393224 | tf_op jit(solution)/shard_map/ppermute | solution.py:506
  4.7 2.3 %collective-permute-start.1 = (bf16[128,128]{1,0:T(8,128)(2,1)S(1)}, bf16[128,128]{1,0:T(8,128)(2,1)S(1)}, u32[]{:S(2)}, u32[]{:S(2)}) collective-permute-start(bf16[128,128]{1,0:T(8,128)(2,1)S(1)} %get-tuple-element.25), channel_id=1, source_target_pairs={{0,4},{2,6},{4,0},{6,2},{1,5},{3,7},{5,1},{7,3},{8,12},{10,14},{12... | collective-permute-start | bytes 98312 | tf_op jit(solution)/shard_map/ppermute | solution.py:472
  7.1 1.9 %collective-permute-done.1.y_ref = bf16[128,128]{1,0:T(8,128)(2,1)S(1)} collective-permute-done((bf16[128,128]{1,0:T(8,128)(2,1)S(1)}, bf16[128,128]{1,0:T(8,128)(2,1)S(1)}, u32[]{:S(2)}, u32[]{:S(2)}) %collective-permute-start.1) | collective-permute-done | bytes 32800 | tf_op jit(solution)/shard_map/ppermute | solution.py:472
  9.0 1.7 %collective-permute-done.2.both_ref = bf16[128,128]{1,0:T(8,128)(2,1)S(1)} collective-permute-done((bf16[128,128]{1,0:T(8,128)(2,1)S(1)}, bf16[128,128]{1,0:T(8,128)(2,1)S(1)}, u32[]{:S(2)}, u32[]{:S(2)}) %collective-permute-start.2) | collective-permute-done | bytes 32800 | tf_op jit(solution)/shard_map/ppermute | solution.py:472
  10.7 1.4 %collective-permute-done.7.halo_ref = bf16[256,256]{1,0:T(8,128)(2,1)S(1)} collective-permute-done((bf16[256,256]{1,0:T(8,128)(2,1)S(1)}, bf16[256,256]{1,0:T(8,128)(2,1)S(1)}, u32[]{:S(2)}, u32[]{:S(2)}) %collective-permute-start.7) | collective-permute-done | bytes 131104 | tf_op jit(solution)/shard_map/ppermute | solution.py:506
  12.4 2.6 %collective-permute-start.4 = (bf16[4,128,128]{2,1,0:T(8,128)(2,1)S(1)}, bf16[4,128,128]{2,1,0:T(8,128)(2,1)S(1)}, u32[]{:S(2)}, u32[]{:S(2)}) collective-permute-start(bf16[4,128,128]{2,1,0:T(8,128)(2,1)S(1)} %shard_map.47.after.refs_0_), channel_id=1, source_target_pairs={{0,16},{16,0},{8,24},{24,8},{1,17},{17,1},{9,25},{25,9},{2,18},{18... | collective-permute-start | bytes 393224 | tf_op jit(solution)/shard_map/ppermute | solution.py:481
  15.6 2.9 %collective-permute-start.10 = (bf16[64,1280]{1,0:T(8,128)(2,1)S(1)}, bf16[64,1280]{1,0:T(8,128)(2,1)S(1)}, u32[]{:S(2)}, u32[]{:S(2)}) collective-permute-start(bf16[64,1280]{1,0:T(8,128)(2,1)S(1)} %get-tuple-element.31), channel_id=1, source_target_pairs={{0,5},{1,4},{2,7},{3,6},{4,1},{5,0},{6,3},{7,2},{8,13},{9,12},{10,... | collective-permute-start | bytes 491528 | tf_op jit(solution)/shard_map/ppermute | solution.py:500
  19.1 2.2 %collective-permute-done.4.refs_2_ = bf16[4,128,128]{2,1,0:T(8,128)(2,1)S(1)} collective-permute-done((bf16[4,128,128]{2,1,0:T(8,128)(2,1)S(1)}, bf16[4,128,128]{2,1,0:T(8,128)(2,1)S(1)}, u32[]{:S(2)}, u32[]{:S(2)}) %collective-permute-start.4) | collective-permute-done | bytes 131104 | tf_op jit(solution)/shard_map/ppermute | solution.py:481
  21.4 0.8 %collective-permute-start.3 = (bf16[4,128,128]{2,1,0:T(8,128)(2,1)S(1)}, bf16[4,128,128]{2,1,0:T(8,128)(2,1)S(1)}, u32[]{:S(2)}, u32[]{:S(2)}) collective-permute-start(bf16[4,128,128]{2,1,0:T(8,128)(2,1)S(1)} %shard_map.47.after.refs_0_), channel_id=1, source_target_pairs={{0,8},{8,0},{16,24},{24,16},{1,9},{9,1},{17,25},{25,17},{2,10},{10... | collective-permute-start | bytes 393224 | tf_op jit(solution)/shard_map/ppermute | solution.py:481
  22.2 1.3 %collective-permute-start.6 = (bf16[4,128,128]{2,1,0:T(8,128)(2,1)S(1)}, bf16[4,128,128]{2,1,0:T(8,128)(2,1)S(1)}, u32[]{:S(2)}, u32[]{:S(2)}) collective-permute-start(bf16[4,128,128]{2,1,0:T(8,128)(2,1)S(1)} %collective-permute-done.4.refs_2_), channel_id=1, source_target_pairs={{8,0},{16,24},{9,1},{17,25},{10,2},{18,26},{11,3},{19,27},{12,4},{... | collective-permute-start | bytes 393224 | tf_op jit(solution)/shard_map/ppermute | solution.py:481
  23.4 0.8 %collective-permute-done.9.refs_2_ = bf16[64,1280]{1,0:T(8,128)(2,1)S(1)} collective-permute-done((bf16[64,1280]{1,0:T(8,128)(2,1)S(1)}, bf16[64,1280]{1,0:T(8,128)(2,1)S(1)}, u32[]{:S(2)}, u32[]{:S(2)}) %collective-permute-start.9) | collective-permute-done | bytes 163872 | tf_op jit(solution)/shard_map/ppermute | solution.py:500
  24.3 2.1 %collective-permute-done.3.refs_1_ = bf16[4,128,128]{2,1,0:T(8,128)(2,1)S(1)} collective-permute-done((bf16[4,128,128]{2,1,0:T(8,128)(2,1)S(1)}, bf16[4,128,128]{2,1,0:T(8,128)(2,1)S(1)}, u32[]{:S(2)}, u32[]{:S(2)}) %collective-permute-start.3) | collective-permute-done | bytes 131104 | tf_op jit(solution)/shard_map/ppermute | solution.py:481
  26.4 2.8 %collective-permute-done.6.refs_4_ = bf16[4,128,128]{2,1,0:T(8,128)(2,1)S(1)} collective-permute-done((bf16[4,128,128]{2,1,0:T(8,128)(2,1)S(1)}, bf16[4,128,128]{2,1,0:T(8,128)(2,1)S(1)}, u32[]{:S(2)}, u32[]{:S(2)}) %collective-permute-start.6) | collective-permute-done | bytes 131104 | tf_op jit(solution)/shard_map/ppermute | solution.py:481
  29.2 3.6 %shard_map.51 = (f32[4,16,768]{2,1,0:T(8,128)S(1)}, f32[4,16,256]{2,1,0:T(8,128)S(1)}, bf16[256,1024]{1,0:T(8,128)(2,1)S(1)}, f32[16,128]{1,0:T(8,128)S(1)}, bf16[16,480]{1,0:T(8,128)(2,1)S(1)}) custom-call(bf16[4,128,128]{2,1,0:T(8,128)(2,1)S(1)} %shard_map.47.after.refs_0_, bf16[4,128,128]{2,1,0:T(8,128)(2,1)S(1)} %collective-permute-done.3.refs_1_, ...), custom_call_target="tpu_custom_call" | custom-call | flops 1073741824 | bytes 524288 | tf_op jit(solution)/shard_map/pallas_call | solution.py:531
  32.8 2.3 %shard_map.52.keep_ref.after = f32[4,16,768]{2,1,0:T(8,128)S(1)} custom-call(bf16[256,1024]{1,0:T(8,128)(2,1)S(1)} %get-tuple-element.32.left, bf16[64,4352]{1,0:T(8,128)(2,1)S(1)} %shard_map.50.refs_6_.full, f32[4,16,256]{2,1,0:T(8,128)S(1)} %get-tuple-element.33.edges_ref, f32[4,16,768]{2,1,0:T(8,128)S(1)} %get-tuple-element.34.after), custom_call_target="tpu_custom_call" | custom-call | flops 1073741824 | bytes 524288 | tf_op jit(solution)/shard_map/pallas_call | solution.py:546
  35.2 1.7 %collective-permute-start.12 = (f32[16,768]{1,0:T(8,128)S(1)}, f32[16,768]{1,0:T(8,128)S(1)}, u32[]{:S(2)}, u32[]{:S(2)}) collective-permute-start(f32[16,768]{1,0:T(8,128)S(1)} %get-tuple-element.36), channel_id=1, source_target_pairs={{0,5},{1,4},{2,7},{3,6},{4,1},{5,0},{6,3},{7,2},{8,13},{9,12},{10,... | collective-permute-start | bytes 147464 | tf_op jit(solution)/shard_map/ppermute | solution.py:500
  36.9 1.2 %collective-permute-start.13 = (f32[16,768]{1,0:T(8,128)S(1)}, f32[16,768]{1,0:T(8,128)S(1)}, u32[]{:S(2)}, u32[]{:S(2)}) collective-permute-start(f32[16,768]{1,0:T(8,128)S(1)} %get-tuple-element.37), channel_id=1, source_target_pairs={{0,4},{1,5},{2,6},{3,7},{4,0},{5,1},{6,2},{7,3},{8,12},{9,13},{10,... | collective-permute-start | bytes 147464 | tf_op jit(solution)/shard_map/ppermute | solution.py:500
  38.7 0.9 %shard_map.54.refs_4_ = f32[16,512]{1,0:T(8,128)S(1)} custom-call(bf16[480,512]{1,0:T(8,128)(2,1)S(1)} %copy-done, bf16[16,480]{1,0:T(8,128)(2,1)S(1)} %get-tuple-element.39.mask_ref, f32[4,16,768]{2,1,0:T(8,128)S(1)} %shard_map.52.keep_ref.after), custom_call_target="tpu_custom_call" | custom-call | flops 15728640 | bytes 491520 | tf_op jit(solution)/shard_map/pallas_call | solution.py:556
  39.6 0.7 %collective-permute-done.12.refs_1_ = f32[16,768]{1,0:T(8,128)S(1)} collective-permute-done((f32[16,768]{1,0:T(8,128)S(1)}, f32[16,768]{1,0:T(8,128)S(1)}, u32[]{:S(2)}, u32[]{:S(2)}) %collective-permute-start.12) | collective-permute-done | bytes 49184 | tf_op jit(solution)/shard_map/ppermute | solution.py:500
  40.3 1.0 %collective-permute-done.13.refs_2_ = f32[16,768]{1,0:T(8,128)S(1)} collective-permute-done((f32[16,768]{1,0:T(8,128)S(1)}, f32[16,768]{1,0:T(8,128)S(1)}, u32[]{:S(2)}, u32[]{:S(2)}) %collective-permute-start.13) | collective-permute-done | bytes 49184 | tf_op jit(solution)/shard_map/ppermute | solution.py:500
  41.3 0.8 %collective-permute-done.14.refs_3_ = f32[16,768]{1,0:T(8,128)S(1)} collective-permute-done((f32[16,768]{1,0:T(8,128)S(1)}, f32[16,768]{1,0:T(8,128)S(1)}, u32[]{:S(2)}, u32[]{:S(2)}) %collective-permute-start.14) | collective-permute-done | bytes 49184 | tf_op jit(solution)/shard_map/ppermute | solution.py:500
  42.2 0.7 %shard_map.55 = f32[16,512]{1,0:T(8,128)} custom-call(f32[16,768]{1,0:T(8,128)S(1)} %get-tuple-element.35.refs_0_, f32[16,768]{1,0:T(8,128)S(1)} %collective-permute-done.12.refs_1_, f32[16,768]{1,0:T(8,128)S(1)} %collective-permute-done.13.refs_2_, f32[16,768]{1,0:T(8,128)S(1)} %collective-permute-done.14.refs_3_, f32[16,512]{1,0:T(8,128)S(1)} %shard_map.54.refs_4_, ...), custom_call_target="tpu_custom_call" | custom-call | bytes 196608 | tf_op jit(solution)/shard_map/pallas_call | solution.py:570
  (20 shorter events, 2.9 us)
Async XLA Ops:
  1.7 1.7 %collective-permute-start = (bf16[1152,128]{1,0:T(8,128)(2,1)S(1)}, bf16[1152,128]{1,0:T(8,128)(2,1)S(1)}, u32[]{:S(2)}, u32[]{:S(2)}) collective-permute-start(bf16[1152,128]{1,0:T(8,128)(2,1)S(1)} %get-tuple-element.24), channel_id=1, source_target_pairs={{0,2},{2,0},{4,6},{6,4},{1,3},{3,1},{5,7},{7,5},{8,10},{10,8},{12,... | collective-permute-start | bytes 884744 | tf_op jit(solution)/shard_map/ppermute | solution.py:472
  3.4 8.7 %collective-permute-start.7 = (bf16[256,256]{1,0:T(8,128)(2,1)S(1)}, bf16[256,256]{1,0:T(8,128)(2,1)S(1)}, u32[]{:S(2)}, u32[]{:S(2)}) collective-permute-start(bf16[256,256]{1,0:T(8,128)(2,1)S(1)} %shard_map.48), channel_id=1, source_target_pairs={{8,0},{10,2},{16,8},{18,10},{24,16},{26,18}} | collective-permute-start | bytes 393224 | tf_op jit(solution)/shard_map/ppermute | solution.py:506
  4.7 4.2 %collective-permute-start.1 = (bf16[128,128]{1,0:T(8,128)(2,1)S(1)}, bf16[128,128]{1,0:T(8,128)(2,1)S(1)}, u32[]{:S(2)}, u32[]{:S(2)}) collective-permute-start(bf16[128,128]{1,0:T(8,128)(2,1)S(1)} %get-tuple-element.25), channel_id=1, source_target_pairs={{0,4},{2,6},{4,0},{6,2},{1,5},{3,7},{5,1},{7,3},{8,12},{10,14},{12... | collective-permute-start | bytes 98312 | tf_op jit(solution)/shard_map/ppermute | solution.py:472
  7.1 3.6 %collective-permute-start.2 = (bf16[128,128]{1,0:T(8,128)(2,1)S(1)}, bf16[128,128]{1,0:T(8,128)(2,1)S(1)}, u32[]{:S(2)}, u32[]{:S(2)}) collective-permute-start(bf16[128,128]{1,0:T(8,128)(2,1)S(1)} %get-tuple-element.26), channel_id=1, source_target_pairs={{0,6},{2,4},{4,2},{6,0},{1,7},{3,5},{5,3},{7,1},{8,14},{10,12},{12... | collective-permute-start | bytes 98312 | tf_op jit(solution)/shard_map/ppermute | solution.py:472
  12.2 10.0 %collective-permute-start.8 = (bf16[64,1280]{1,0:T(8,128)(2,1)S(1)}, bf16[64,1280]{1,0:T(8,128)(2,1)S(1)}, u32[]{:S(2)}, u32[]{:S(2)}) collective-permute-start(bf16[64,1280]{1,0:T(8,128)(2,1)S(1)} %get-tuple-element.29), channel_id=1, source_target_pairs={{0,1},{1,0},{2,3},{3,2},{4,5},{5,4},{6,7},{7,6},{8,9},{9,8},{10,11... | collective-permute-start | bytes 491528 | tf_op jit(solution)/shard_map/ppermute | solution.py:500
  12.4 8.9 %collective-permute-start.4 = (bf16[4,128,128]{2,1,0:T(8,128)(2,1)S(1)}, bf16[4,128,128]{2,1,0:T(8,128)(2,1)S(1)}, u32[]{:S(2)}, u32[]{:S(2)}) collective-permute-start(bf16[4,128,128]{2,1,0:T(8,128)(2,1)S(1)} %shard_map.47.after.refs_0_), channel_id=1, source_target_pairs={{0,16},{16,0},{8,24},{24,8},{1,17},{17,1},{9,25},{25,9},{2,18},{18... | collective-permute-start | bytes 393224 | tf_op jit(solution)/shard_map/ppermute | solution.py:481
  15.1 9.1 %collective-permute-start.9 = (bf16[64,1280]{1,0:T(8,128)(2,1)S(1)}, bf16[64,1280]{1,0:T(8,128)(2,1)S(1)}, u32[]{:S(2)}, u32[]{:S(2)}) collective-permute-start(bf16[64,1280]{1,0:T(8,128)(2,1)S(1)} %get-tuple-element.30), channel_id=1, source_target_pairs={{0,4},{1,5},{2,6},{3,7},{4,0},{5,1},{6,2},{7,3},{8,12},{9,13},{10,... | collective-permute-start | bytes 491528 | tf_op jit(solution)/shard_map/ppermute | solution.py:500
  15.6 8.6 %collective-permute-start.10 = (bf16[64,1280]{1,0:T(8,128)(2,1)S(1)}, bf16[64,1280]{1,0:T(8,128)(2,1)S(1)}, u32[]{:S(2)}, u32[]{:S(2)}) collective-permute-start(bf16[64,1280]{1,0:T(8,128)(2,1)S(1)} %get-tuple-element.31), channel_id=1, source_target_pairs={{0,5},{1,4},{2,7},{3,6},{4,1},{5,0},{6,3},{7,2},{8,13},{9,12},{10,... | collective-permute-start | bytes 491528 | tf_op jit(solution)/shard_map/ppermute | solution.py:500
  18.5 5.8 %collective-permute-start.5 = (bf16[4,128,128]{2,1,0:T(8,128)(2,1)S(1)}, bf16[4,128,128]{2,1,0:T(8,128)(2,1)S(1)}, u32[]{:S(2)}, u32[]{:S(2)}) collective-permute-start(bf16[4,128,128]{2,1,0:T(8,128)(2,1)S(1)} %shard_map.47.after.refs_0_), channel_id=1, source_target_pairs={{8,16},{16,8},{9,17},{17,9},{10,18},{18,10},{11,19},{19,11},{12,20... | collective-permute-start | bytes 393224 | tf_op jit(solution)/shard_map/ppermute | solution.py:481
  21.4 5.0 %collective-permute-start.3 = (bf16[4,128,128]{2,1,0:T(8,128)(2,1)S(1)}, bf16[4,128,128]{2,1,0:T(8,128)(2,1)S(1)}, u32[]{:S(2)}, u32[]{:S(2)}) collective-permute-start(bf16[4,128,128]{2,1,0:T(8,128)(2,1)S(1)} %shard_map.47.after.refs_0_), channel_id=1, source_target_pairs={{0,8},{8,0},{16,24},{24,16},{1,9},{9,1},{17,25},{25,17},{2,10},{10... | collective-permute-start | bytes 393224 | tf_op jit(solution)/shard_map/ppermute | solution.py:481
  22.2 7.0 %collective-permute-start.6 = (bf16[4,128,128]{2,1,0:T(8,128)(2,1)S(1)}, bf16[4,128,128]{2,1,0:T(8,128)(2,1)S(1)}, u32[]{:S(2)}, u32[]{:S(2)}) collective-permute-start(bf16[4,128,128]{2,1,0:T(8,128)(2,1)S(1)} %collective-permute-done.4.refs_2_), channel_id=1, source_target_pairs={{8,0},{16,24},{9,1},{17,25},{10,2},{18,26},{11,3},{19,27},{12,4},{... | collective-permute-start | bytes 393224 | tf_op jit(solution)/shard_map/ppermute | solution.py:481
  24.2 5.0 %copy-start.1 = (s32[480]{0:T(512)S(1)}, s32[480]{0:T(512)}, u32[]{:S(2)}) copy-start(s32[480]{0:T(512)} %param.7) | copy-start | bytes 5764
  32.7 2.4 %collective-permute-start.11 = (f32[4,16,768]{2,1,0:T(8,128)S(1)}, f32[4,16,768]{2,1,0:T(8,128)S(1)}, u32[]{:S(2)}, u32[]{:S(2)}) collective-permute-start(f32[4,16,768]{2,1,0:T(8,128)S(1)} %get-tuple-element.34.after), channel_id=1, source_target_pairs={{0,2},{2,0},{4,6},{6,4},{1,3},{3,1},{5,7},{7,5},{8,10},{10,8},{12,... | collective-permute-start | bytes 589832 | tf_op jit(solution)/shard_map/ppermute | solution.py:555
  32.8 5.9 %copy-start = (bf16[480,512]{1,0:T(8,128)(2,1)S(1)}, bf16[480,512]{1,0:T(8,128)(2,1)}, u32[]{:S(2)}) copy-start(bf16[480,512]{1,0:T(8,128)(2,1)} %wave_ref.1) | copy-start | bytes 1474564
  35.2 5.1 %collective-permute-start.12 = (f32[16,768]{1,0:T(8,128)S(1)}, f32[16,768]{1,0:T(8,128)S(1)}, u32[]{:S(2)}, u32[]{:S(2)}) collective-permute-start(f32[16,768]{1,0:T(8,128)S(1)} %get-tuple-element.36), channel_id=1, source_target_pairs={{0,5},{1,4},{2,7},{3,6},{4,1},{5,0},{6,3},{7,2},{8,13},{9,12},{10,... | collective-permute-start | bytes 147464 | tf_op jit(solution)/shard_map/ppermute | solution.py:500
  36.9 4.4 %collective-permute-start.13 = (f32[16,768]{1,0:T(8,128)S(1)}, f32[16,768]{1,0:T(8,128)S(1)}, u32[]{:S(2)}, u32[]{:S(2)}) collective-permute-start(f32[16,768]{1,0:T(8,128)S(1)} %get-tuple-element.37), channel_id=1, source_target_pairs={{0,4},{1,5},{2,6},{3,7},{4,0},{5,1},{6,2},{7,3},{8,12},{9,13},{10,... | collective-permute-start | bytes 147464 | tf_op jit(solution)/shard_map/ppermute | solution.py:500
  38.1 4.1 %collective-permute-start.14 = (f32[16,768]{1,0:T(8,128)S(1)}, f32[16,768]{1,0:T(8,128)S(1)}, u32[]{:S(2)}, u32[]{:S(2)}) collective-permute-start(f32[16,768]{1,0:T(8,128)S(1)} %get-tuple-element.38), channel_id=1, source_target_pairs={{0,1},{1,0},{2,3},{3,2},{4,5},{5,4},{6,7},{7,6},{8,9},{9,8},{10,11... | collective-permute-start | bytes 147464 | tf_op jit(solution)/shard_map/ppermute | solution.py:500

commit v19 on v16

--- a/solution.py
+++ b/solution.py
@@ -208,36 +208,23 @@
     head_ref[...] = out_ref[:, : head_ref.shape[1]]
 
 
-def arrival(template):
-    return template ^ (lax.axis_index("outer") * INNER)
-
-
 def arrange(tpls, left):
-    size, depth = left.shape
-    count = len(tpls) * INNER
-    row = lax.broadcasted_iota(jnp.int32, (size, size), 0)
-    column = lax.broadcasted_iota(jnp.int32, (size, size), 1)
-    shift = count.bit_length() - 1
-    source = arrival(row & (count - 1)) * FINE + (row >> shift)
-    order = jnp.where(column == source, 1.0, 0.0).astype(BF16)
-    for step in range(depth // LANES):
-        rows = [
-            pack[:, FINE * step : FINE * (step + 1), :].reshape(INNER * FINE, LANES)
-            for pack in tpls
-        ]
-        left[:, step * LANES : (step + 1) * LANES] = jnp.dot(
-            order, jnp.concatenate(rows, axis=0), preferred_element_type=F32
-        ).astype(BF16)
-
-
-def correlate(left, full, out_ref, slab, side, shifts, products):
+    for flip, pack in enumerate(tpls):
+        for inner in range(INNER):
+            row = (flip * INNER + inner) * FINE
+            for step in range(left.shape[1] // LANES):
+                left[row : row + FINE, step * LANES : (step + 1) * LANES] = pack[
+                    inner, FINE * step : FINE * (step + 1), :
+                ]
+
+
+def correlate(left, full, slab, run, side, ys, store, shifts, products):
     part = full.shape[0]
     size, depth = left.shape
     count = size // FINE
     copies = LANES // FINE
-    run = out_ref.shape[0] // 2
     width = run * slab
-    for y in range(2):
+    for y in ys:
         columns = width + 2 * LANES
         start = pl.multiple_of((2 * y + side) * width, width)
         samples = full[:, pl.ds(start, columns)]
@@ -245,24 +232,31 @@
             tile, turn = copy // copies * LANES, copy % copies * FINE
             turned = samples if turn == 0 else pltpu.roll(samples, columns - turn, 1)
             shifts[y, copy * part : (copy + 1) * part, :] = turned[:, tile : tile + width + LANES]
-    tiles = products.shape[2] // LANES
+    tiles = products.shape[1]
     span = (tiles - 1) * LANES
     per_block = span // slab
-    blocks = [(y, index) for y in range(2) for index in range(width // span)]
+    blocks = [(y, index) for y in ys for index in range(width // span)]
 
     def multiply(place, slot):
         y, index = place
         for tile in range(0, tiles, 2):
             start = index * span + tile * LANES
-            lanes = min(2, tiles - tile) * LANES
-            products[slot, :, tile * LANES : tile * LANES + lanes] = jnp.dot(
-                left[...], shifts[y, :, start : start + lanes], preferred_element_type=F32
+            pieces = min(2, tiles - tile)
+            product = jnp.dot(
+                left[...],
+                shifts[y, :, start : start + pieces * LANES],
+                preferred_element_type=F32,
             )
+            for piece in range(pieces):
+                products[slot, tile + piece] = product[:, piece * LANES : (piece + 1) * LANES]
 
     def gather(place, slot):
         def tree(first, number):
             if number == 1:
-                return products[slot, first * count : (first + 1) * count, :]
+                rows = pl.ds(first, count, stride=FINE)
+                return jnp.concatenate(
+                    [products[slot, tile, rows, :] for tile in range(tiles)], axis=1
+                )
             half = number // 2
             later = pltpu.roll(tree(first + half, half), span + LANES - half, 1)
             return tree(first, half) + later
@@ -270,9 +264,7 @@
         total = tree(0, FINE)
         y, index = place
         for piece in range(per_block):
-            out_ref[y * run + index * per_block + piece, :, :slab] = total[
-                :, piece * slab : (piece + 1) * slab
-            ]
+            store(y, index * per_block + piece, total[:, piece * slab : (piece + 1) * slab])
 
     multiply(blocks[0], 0)
     for number in range(1, len(blocks)):
@@ -282,23 +274,38 @@
 
 
 def first_dots_kernel(outer_count, stations, channels, tm_count, *refs):
-    tpls, (order_ref, samples_ref, halo_ref) = refs[:-12], refs[-12:-9]
-    send_ref, edges_ref, left, scale_ref, mask_ref = refs[-9:-4]
-    full, edges, shifts, products = refs[-4:]
-    core = lax.rem(lax.axis_index("inner"), 2)
-    group, _, window = edges.shape
-    chunk = samples_ref.shape[1]
-    slab = chunk // group
-    full[:, :chunk] = samples_ref[...]
-    full[:, chunk:] = halo_ref[...]
+    tpls, (order_ref, samples_ref) = refs[:-9], refs[-9:-7]
+    begun_ref, left, scale_ref, mask_ref, part_ref, shifts, products = refs[-7:]
     tpls = [pack[...] for pack in tpls]
     if len(tpls) > outer_count:
         tpls = tpls[:-2] + [tpls[-2] + tpls[-1]]
     arrange(tpls, left)
-    correlate(left, full, send_ref, slab, 1 - core, shifts, products)
-    part_mask = read_masks(stations, channels, tm_count, tpls, order_ref, scale_ref, mask_ref)
+    core = lax.rem(lax.axis_index("inner"), 2)
+    run, _, slab = begun_ref.shape
+
+    def store(y, place, sums):
+        begun_ref[place] = sums
+
+    correlate(left, samples_ref, slab, run, 1 - core, [0], store, shifts, products)
+    read_masks(stations, channels, tm_count, tpls, order_ref, scale_ref, mask_ref, part_ref)
+
+
+def middle_dots_kernel(left, samples_ref, halo_ref, begun_ref, mask_ref, *refs):
+    send_ref, edges_ref, full, edges, shifts, products = refs
+    group, _, window = edges.shape
+    chunk = samples_ref.shape[1]
+    slab = chunk // group
+    run = group // 4
+    core = lax.rem(lax.axis_index("inner"), 2)
+    full[:, :chunk] = samples_ref[...]
+    full[:, chunk:] = halo_ref[...]
+
+    def store(y, place, sums):
+        send_ref[y * run + place, :, :slab] = sums
+
+    correlate(left, full, slab, run, 1 - core, [1], store, shifts, products)
     after = [full[:, (m + 1) * slab : (m + 1) * slab + window] for m in range(group)]
-    squares = masked_squares(part_mask, jnp.concatenate(after, axis=1))
+    squares = masked_squares(mask_ref[...], jnp.concatenate(after, axis=1))
     column = lax.broadcasted_iota(jnp.int32, squares.shape, 1) & (window - 1)
     reach = 1
     while reach < window:
@@ -308,22 +315,27 @@
     squares = jnp.where(column >= 1, pltpu.roll(squares, 1, 1), 0.0)
     for member in range(group):
         edges[member] = squares[:, member * window : (member + 1) * window]
-    run = group // 4
-    for y in range(2):
-        for tm in range(run):
+    for tm in range(run):
+        send_ref[tm, :, :slab] = begun_ref[tm]
+        for y in range(2):
             send_ref[y * run + tm, :, slab:] = edges[(2 * y + 1 - core) * run + tm]
             edges_ref[y * run + tm] = edges[(2 * y + core) * run + tm]
 
 
-def second_dots_kernel(left, samples_ref, halo_ref, edges_ref, after, keep_ref, *scratch):
+def last_dots_kernel(left, samples_ref, halo_ref, edges_ref, after, keep_ref, *scratch):
     del after
     full, shifts, products = scratch
     chunk = samples_ref.shape[1]
     full[:, :chunk] = samples_ref[...]
     full[:, chunk:] = halo_ref[...]
     core = lax.rem(lax.axis_index("inner"), 2)
+    run = keep_ref.shape[0] // 2
     slab = keep_ref.shape[2] - edges_ref.shape[2]
-    correlate(left, full, keep_ref, slab, core, shifts, products)
+
+    def store(y, place, sums):
+        keep_ref[y * run + place, :, :slab] = sums
+
+    correlate(left, full, slab, run, core, [0, 1], store, shifts, products)
     keep_ref[:, :, slab:] = edges_ref[...]
 
 
@@ -343,7 +355,7 @@
     )
 
 
-def read_masks(stations, channels, tm_count, tpls, order_ref, scale_ref, mask_ref):
+def read_masks(stations, channels, tm_count, tpls, order_ref, scale_ref, mask_ref, part_ref):
     rows = tpls[0].shape[1]
     count = len(tpls) * INNER
     padded = INNER * LANES
@@ -354,9 +366,6 @@
         (((1,), (1,)), ((), ())),
         preferred_element_type=F32,
     )
-    template = lax.broadcasted_iota(jnp.int32, (count, count), 0)
-    place = lax.broadcasted_iota(jnp.int32, (count, count), 1)
-    sort = jnp.where(place == arrival(template), 1.0, 0.0).astype(BF16)
     slots = -(-stations // rows)
 
     def read(slot):
@@ -365,7 +374,6 @@
         )
 
     values = jnp.concatenate([read(slot) for slot in range(slots + 1)], axis=1)
-    values = jnp.dot(sort, values.astype(BF16), preferred_element_type=F32)
     start = slots * rows
     scale = jnp.sum(values[:, start : start + 3], axis=1, keepdims=True)
     scale_ref[...] = jnp.broadcast_to(scale, scale_ref.shape)
@@ -377,7 +385,7 @@
     mask_ref[...] = mask
     grouped = jnp.dot(mask, regroup(channels, padded, part), preferred_element_type=F32)
     mine = side_major(lax.axis_index("inner")) * LANES + lax.axis_index("tm") * part
-    return pltpu.roll(grouped, lax.rem(padded - mine, padded), 1)[:, :part].astype(BF16)
+    part_ref[...] = pltpu.roll(grouped, lax.rem(padded - mine, padded), 1)[:, :part].astype(BF16)
 
 
 def power_kernel(window, wave_ref, mask_ref, after, out_ref):
@@ -404,7 +412,16 @@
     energy = jnp.concatenate(
         [power_ref[:, :inside], power_ref[:, inside:] + edge], axis=1
     )
-    out_ref[...] = dots * (scale_ref[:, :1] / jnp.sqrt(energy + EPSILON))
+    rows = dots * (scale_ref[:, :1] / jnp.sqrt(energy + EPSILON))
+    outer = lax.axis_index("outer")
+    step = INNER
+    while step < rows.shape[0]:
+        pairs = [rows[start : start + step] for start in range(0, rows.shape[0], step)]
+        swapped = [pairs[index ^ 1] for index in range(len(pairs))]
+        flipped = (outer & (step // INNER)) != 0
+        rows = jnp.where(flipped, jnp.concatenate(swapped, axis=0), rows)
+        step *= 2
+    out_ref[...] = rows
 
 
 def on_device(waveforms, templates, station_mask, channel_order):
@@ -503,33 +520,39 @@
     def scratch():
         return [
             pltpu.VMEM((2, depth, chunk // 4 + LANES), BF16),
-            pltpu.VMEM((2, count * FINE, span + LANES), F32),
+            pltpu.VMEM((2, span // LANES + 1, count * FINE, LANES), F32),
         ]
 
-    send, edges, left, scale, mask = call(
+    begun, left, scale, mask, mask_part = call(
         functools.partial(first_dots_kernel, outer_count, stations, channels, tm_count),
-        [VMEM] * (len(tpls) + 3),
+        [VMEM] * (len(tpls) + 2),
         [
-            sds((half, count, slab + window), F32),
-            sds((half, count, window), F32),
+            sds((tm_count, count, slab), F32),
             sds((count * FINE, depth), BF16),
             sds((count, LANES), F32),
             sds((count, channels), BF16),
+            sds((count, part), BF16),
         ],
-        [
-            pltpu.VMEM((part, chunk + window), BF16),
-            pltpu.VMEM((group, count, window), F32),
-        ]
-        + scratch(),
-        flops=work,
+        scratch(),
+        flops=work // 2,
         bytes_accessed=part * chunk * 2,
         vmem=36,
-    )(*tpls, order_row, samples, halo)
+    )(*tpls, order_row, samples)
+    full = pltpu.VMEM((part, chunk + window), BF16)
+    send, edges = call(
+        middle_dots_kernel,
+        [VMEM] * 5,
+        [sds((half, count, slab + window), F32), sds((half, count, window), F32)],
+        [full, pltpu.VMEM((group, count, window), F32)] + scratch(),
+        flops=work // 2,
+        bytes_accessed=part * chunk * 2,
+        vmem=36,
+    )(left, samples, halo, begun, mask_part)
     keep = call(
-        second_dots_kernel,
+        last_dots_kernel,
         [VMEM] * 4 + [AFTER],
         sds((half, count, slab + window), F32),
-        [pltpu.VMEM((part, chunk + window), BF16)] + scratch(),
+        [full] + scratch(),
         flops=work,
         bytes_accessed=part * chunk * 2,
         vmem=36,

time: 39.8 us -> 38.8 us (0.975)
  waiting for transfers between devices: 9.55 us -> 8.93 us
    ppermute x1, waiting for transfers between devices: 5 us -> 0.01 us  [on_device(): lax.ppermute(head, 'outer', [(b, b - 1) for b in range(1, outer_count)])]
    ppermute x4, waiting for transfers between devices: 0.19 us -> 4.57 us  [cross(): return lax.ppermute(part, 'outer', route)]
    pallas_call x1, Pallas kernels: 3.73 us -> 1.52 us  [on_device(): call(functools.partial(first_dots_kernel, outer_count, stations, channels...]
    pallas_call x1 -> x2, Pallas kernels: 2.42 us -> 4.28 us  [the longest x1 2.41 us: on_device(): call(last_dots_kernel, [VMEM] * 4 + [AFTER], sds((half, count, slab + win...]
  transfers between devices with their start and end apart: 15 -> 15, of which waited for: 8 -> 8; matrix products, arithmetic and copies ran while one was open for 0% -> 0% of each run, Pallas kernels for 9% -> 13%
where the time goes in v19:
time: 38.8 us; the launch traced here: 38.6 us
  starting transfers between devices  20.3 us (52%)
  Pallas kernels  9.22 us (24%)
  waiting for transfers between devices  8.93 us (23%)
    ppermute x6, starting transfers between devices, swap(): return lax.ppermute(part, every, route)  8.27 us
    ppermute x4, starting transfers between devices, cross(): return lax.ppermute(part, 'outer', route)  7.48 us
    ppermute x4, waiting for transfers between devices, cross(): return lax.ppermute(part, 'outer', route)  4.57 us
    ppermute x3, starting transfers between devices, plane(): return lax.ppermute(part, 'inner', [(b, b ^ flip) for b in range(INNER)])  3.18 us
    ppermute x6, waiting for transfers between devices, swap(): return lax.ppermute(part, every, route)  2.92 us
    pallas_call x1, Pallas kernels, on_device(): call(last_dots_kernel, [VMEM] * 4 + [AFTER], sds((half, count, slab + win...  2.41 us
    pallas_call x1, Pallas kernels, on_device(): call(middle_dots_kernel, [VMEM] * 5, [sds((half, count, slab + window), F...  1.88 us
    pallas_call x1, Pallas kernels, on_device(): call(functools.partial(prologue_kernel, tm_count), [HBM] * 4, [sds((padde...  1.7 us
  transfers between devices with their start and end apart: 15, of which 8 were waited for; matrix products, arithmetic and copies ran while one was open for 0% of the time, Pallas kernels for 13%

profile of v19, /device:TPU:0, one launch (start us, length us, event | category | flops | bytes accessed | tf_op | source)
XLA Modules:
  0.0 38.6 jit_solution(3437060128109741295)
XLA Ops:
  0.0 1.7 %shard_map.46 = (bf16[1152,128]{1,0:T(8,128)(2,1)S(1)}, bf16[256,512]{1,0:T(8,128)(2,1)S(1)}, bf16[128,128]{1,0:T(8,128)(2,1)S(1)}, bf16[128,128]{1,0:T(8,128)(2,1)S(1)}, bf16[128,128]{1,0:T(8,128)(2,1)S(1)}) custom-call(bf16[480,512]{1,0:T(8,128)(2,1)} %wave_ref.1, bf16[1,480,256]{2,1,0:T(8,128)(2,1)} %tpl_hbm.1, s32[1,160]{1,0:T(1,128)} %flag_hbm.1, ...), custom_call_target="tpu_custom_call" | custom-call | bytes 737280 | tf_op jit(solution)/shard_map/pallas_call | solution.py:449
  1.7 0.5 %collective-permute-start = (bf16[1152,128]{1,0:T(8,128)(2,1)S(1)}, bf16[1152,128]{1,0:T(8,128)(2,1)S(1)}, u32[]{:S(2)}, u32[]{:S(2)}) collective-permute-start(bf16[1152,128]{1,0:T(8,128)(2,1)S(1)} %get-tuple-element.28), channel_id=1, source_target_pairs={{0,2},{2,0},{4,6},{6,4},{1,3},{3,1},{5,7},{7,5},{8,10},{10,8},{12,... | collective-permute-start | bytes 884744 | tf_op jit(solution)/shard_map/ppermute | solution.py:471
  2.2 2.6 %collective-permute-start.1 = (bf16[128,128]{1,0:T(8,128)(2,1)S(1)}, bf16[128,128]{1,0:T(8,128)(2,1)S(1)}, u32[]{:S(2)}, u32[]{:S(2)}) collective-permute-start(bf16[128,128]{1,0:T(8,128)(2,1)S(1)} %get-tuple-element.29), channel_id=1, source_target_pairs={{0,4},{2,6},{4,0},{6,2},{1,5},{3,7},{5,1},{7,3},{8,12},{10,14},{12... | collective-permute-start | bytes 98312 | tf_op jit(solution)/shard_map/ppermute | solution.py:471
  5.0 1.8 %collective-permute-start.7 = (bf16[2,64,512]{2,1,0:T(8,128)(2,1)S(1)}, bf16[2,64,512]{2,1,0:T(8,128)(2,1)S(1)}, u32[]{:S(2)}, u32[]{:S(2)}) collective-permute-start(bf16[2,64,512]{2,1,0:T(8,128)(2,1)S(1)} %get-tuple-element.33), channel_id=1, source_target_pairs={{0,1},{1,0},{2,3},{3,2},{4,5},{5,4},{6,7},{7,6},{8,9},{9,8},{10,11... | collective-permute-start | bytes 393224 | tf_op jit(solution)/shard_map/ppermute | solution.py:499
  6.8 1.4 %collective-permute-done.2.both_ref = bf16[128,128]{1,0:T(8,128)(2,1)S(1)} collective-permute-done((bf16[128,128]{1,0:T(8,128)(2,1)S(1)}, bf16[128,128]{1,0:T(8,128)(2,1)S(1)}, u32[]{:S(2)}, u32[]{:S(2)}) %collective-permute-start.2) | collective-permute-done | bytes 32800 | tf_op jit(solution)/shard_map/ppermute | solution.py:471
  8.2 2.7 %collective-permute-start.4 = (bf16[4,128,128]{2,1,0:T(8,128)(2,1)S(1)}, bf16[4,128,128]{2,1,0:T(8,128)(2,1)S(1)}, u32[]{:S(2)}, u32[]{:S(2)}) collective-permute-start(bf16[4,128,128]{2,1,0:T(8,128)(2,1)S(1)} %shard_map.47.refs_0_), channel_id=1, source_target_pairs={{0,16},{16,0},{8,24},{24,8},{1,17},{17,1},{9,25},{25,9},{2,18},{18... | collective-permute-start | bytes 393224 | tf_op jit(solution)/shard_map/ppermute | solution.py:480
  10.8 0.9 %collective-permute-start.8 = (bf16[2,64,512]{2,1,0:T(8,128)(2,1)S(1)}, bf16[2,64,512]{2,1,0:T(8,128)(2,1)S(1)}, u32[]{:S(2)}, u32[]{:S(2)}) collective-permute-start(bf16[2,64,512]{2,1,0:T(8,128)(2,1)S(1)} %get-tuple-element.34), channel_id=1, source_target_pairs={{0,4},{1,5},{2,6},{3,7},{4,0},{5,1},{6,2},{7,3},{8,12},{9,13},{10,... | collective-permute-start | bytes 393224 | tf_op jit(solution)/shard_map/ppermute | solution.py:499
  11.7 2.1 %collective-permute-start.9 = (bf16[2,64,512]{2,1,0:T(8,128)(2,1)S(1)}, bf16[2,64,512]{2,1,0:T(8,128)(2,1)S(1)}, u32[]{:S(2)}, u32[]{:S(2)}) collective-permute-start(bf16[2,64,512]{2,1,0:T(8,128)(2,1)S(1)} %get-tuple-element.35), channel_id=1, source_target_pairs={{0,5},{1,4},{2,7},{3,6},{4,1},{5,0},{6,3},{7,2},{8,13},{9,12},{10,... | collective-permute-start | bytes 393224 | tf_op jit(solution)/shard_map/ppermute | solution.py:499
  13.8 0.7 %collective-permute-start.5 = (bf16[4,128,128]{2,1,0:T(8,128)(2,1)S(1)}, bf16[4,128,128]{2,1,0:T(8,128)(2,1)S(1)}, u32[]{:S(2)}, u32[]{:S(2)}) collective-permute-start(bf16[4,128,128]{2,1,0:T(8,128)(2,1)S(1)} %shard_map.47.refs_0_), channel_id=1, source_target_pairs={{8,16},{16,8},{9,17},{17,9},{10,18},{18,10},{11,19},{19,11},{12,20... | collective-permute-start | bytes 393224 | tf_op jit(solution)/shard_map/ppermute | solution.py:480
  14.5 2.9 %collective-permute-start.3 = (bf16[4,128,128]{2,1,0:T(8,128)(2,1)S(1)}, bf16[4,128,128]{2,1,0:T(8,128)(2,1)S(1)}, u32[]{:S(2)}, u32[]{:S(2)}) collective-permute-start(bf16[4,128,128]{2,1,0:T(8,128)(2,1)S(1)} %shard_map.47.refs_0_), channel_id=1, source_target_pairs={{0,8},{8,0},{16,24},{24,16},{1,9},{9,1},{17,25},{25,17},{2,10},{10... | collective-permute-start | bytes 393224 | tf_op jit(solution)/shard_map/ppermute | solution.py:480
  17.5 1.3 %collective-permute-start.6 = (bf16[4,128,128]{2,1,0:T(8,128)(2,1)S(1)}, bf16[4,128,128]{2,1,0:T(8,128)(2,1)S(1)}, u32[]{:S(2)}, u32[]{:S(2)}) collective-permute-start(bf16[4,128,128]{2,1,0:T(8,128)(2,1)S(1)} %collective-permute-done.4.refs_2_), channel_id=1, source_target_pairs={{8,0},{16,24},{9,1},{17,25},{10,2},{18,26},{11,3},{19,27},{12,4},{... | collective-permute-start | bytes 393224 | tf_op jit(solution)/shard_map/ppermute | solution.py:480
  19.0 1.3 %collective-permute-start.10 = (bf16[64,256]{1,0:T(8,128)(2,1)S(1)}, bf16[64,256]{1,0:T(8,128)(2,1)S(1)}, u32[]{:S(2)}, u32[]{:S(2)}) collective-permute-start(bf16[64,256]{1,0:T(8,128)(2,1)S(1)} %get-tuple-element.38), channel_id=1, source_target_pairs={{8,0},{16,8},{24,16},{9,1},{17,9},{25,17},{10,2},{18,10},{26,18},{... | collective-permute-start | bytes 98312 | tf_op jit(solution)/shard_map/ppermute | solution.py:514
  20.3 4.4 %collective-permute-done.6.refs_4_ = bf16[4,128,128]{2,1,0:T(8,128)(2,1)S(1)} collective-permute-done((bf16[4,128,128]{2,1,0:T(8,128)(2,1)S(1)}, bf16[4,128,128]{2,1,0:T(8,128)(2,1)S(1)}, u32[]{:S(2)}, u32[]{:S(2)}) %collective-permute-start.6) | collective-permute-done | bytes 131104 | tf_op jit(solution)/shard_map/ppermute | solution.py:480
  24.7 1.5 %shard_map.50 = (f32[2,16,512]{2,1,0:T(8,128)S(1)}, bf16[256,1024]{1,0:T(8,128)(2,1)S(1)}, f32[16,128]{1,0:T(8,128)S(1)}, bf16[16,480]{1,0:T(8,128)(2,1)S(1)}, bf16[16,64]{1,0:T(8,128)(2,1)S(1)}) custom-call(bf16[4,128,128]{2,1,0:T(8,128)(2,1)S(1)} %shard_map.47.refs_0_, bf16[4,128,128]{2,1,0:T(8,128)(2,1)S(1)} %collective-permute-done.3.refs_1_, ...), custom_call_target="tpu_custom_call" | custom-call | flops 536870912 | bytes 524288 | tf_op jit(solution)/shard_map/pallas_call | solution.py:526
  26.3 1.9 %shard_map.51 = (f32[4,16,768]{2,1,0:T(8,128)S(1)}, f32[4,16,256]{2,1,0:T(8,128)S(1)}) custom-call(bf16[256,1024]{1,0:T(8,128)(2,1)S(1)} %get-tuple-element.37.left, bf16[64,4096]{1,0:T(8,128)(2,1)S(1)} %get-tuple-element.36.refs_6_.samples_ref, bf16[64,256]{1,0:T(8,128)(2,1)S(1)} %collective-permute-done.10.halo_ref, ...), custom_call_target="tpu_custom_call" | custom-call | flops 536870912 | bytes 524288 | tf_op jit(solution)/shard_map/pallas_call | solution.py:542
  28.2 2.4 %shard_map.52.keep_ref.after = f32[4,16,768]{2,1,0:T(8,128)S(1)} custom-call(bf16[256,1024]{1,0:T(8,128)(2,1)S(1)} %get-tuple-element.37.left, bf16[64,4096]{1,0:T(8,128)(2,1)S(1)} %get-tuple-element.36.refs_6_.samples_ref, bf16[64,256]{1,0:T(8,128)(2,1)S(1)} %collective-permute-done.10.halo_ref, f32[4,16,256]{2,1,0:T(8,128)S(1)} %get-tuple-element.41.edges_ref, ...), custom_call_target="tpu_custom_call" | custom-call | flops 1073741824 | bytes 524288 | tf_op jit(solution)/shard_map/pallas_call | solution.py:551
  30.7 2.0 %collective-permute-start.12 = (f32[16,768]{1,0:T(8,128)S(1)}, f32[16,768]{1,0:T(8,128)S(1)}, u32[]{:S(2)}, u32[]{:S(2)}) collective-permute-start(f32[16,768]{1,0:T(8,128)S(1)} %get-tuple-element.44), channel_id=1, source_target_pairs={{0,5},{1,4},{2,7},{3,6},{4,1},{5,0},{6,3},{7,2},{8,13},{9,12},{10,... | collective-permute-start | bytes 147464 | tf_op jit(solution)/shard_map/ppermute | solution.py:499
  32.7 1.2 %collective-permute-start.13 = (f32[16,768]{1,0:T(8,128)S(1)}, f32[16,768]{1,0:T(8,128)S(1)}, u32[]{:S(2)}, u32[]{:S(2)}) collective-permute-start(f32[16,768]{1,0:T(8,128)S(1)} %get-tuple-element.45), channel_id=1, source_target_pairs={{0,4},{1,5},{2,6},{3,7},{4,0},{5,1},{6,2},{7,3},{8,12},{9,13},{10,... | collective-permute-start | bytes 147464 | tf_op jit(solution)/shard_map/ppermute | solution.py:499
  33.8 0.4 %collective-permute-start.14 = (f32[16,768]{1,0:T(8,128)S(1)}, f32[16,768]{1,0:T(8,128)S(1)}, u32[]{:S(2)}, u32[]{:S(2)}) collective-permute-start(f32[16,768]{1,0:T(8,128)S(1)} %get-tuple-element.46), channel_id=1, source_target_pairs={{0,1},{1,0},{2,3},{3,2},{4,5},{5,4},{6,7},{7,6},{8,9},{9,8},{10,11... | collective-permute-start | bytes 147464 | tf_op jit(solution)/shard_map/ppermute | solution.py:499
  34.3 0.9 %shard_map.54.refs_4_ = f32[16,512]{1,0:T(8,128)S(1)} custom-call(bf16[480,512]{1,0:T(8,128)(2,1)S(1)} %copy-done, bf16[16,480]{1,0:T(8,128)(2,1)S(1)} %get-tuple-element.47.mask_ref, f32[4,16,768]{2,1,0:T(8,128)S(1)} %shard_map.52.keep_ref.after), custom_call_target="tpu_custom_call" | custom-call | flops 15728640 | bytes 491520 | tf_op jit(solution)/shard_map/pallas_call | solution.py:561
  35.1 0.7 %collective-permute-done.12.refs_1_ = f32[16,768]{1,0:T(8,128)S(1)} collective-permute-done((f32[16,768]{1,0:T(8,128)S(1)}, f32[16,768]{1,0:T(8,128)S(1)}, u32[]{:S(2)}, u32[]{:S(2)}) %collective-permute-start.12) | collective-permute-done | bytes 49184 | tf_op jit(solution)/shard_map/ppermute | solution.py:499
  35.8 1.0 %collective-permute-done.13.refs_2_ = f32[16,768]{1,0:T(8,128)S(1)} collective-permute-done((f32[16,768]{1,0:T(8,128)S(1)}, f32[16,768]{1,0:T(8,128)S(1)}, u32[]{:S(2)}, u32[]{:S(2)}) %collective-permute-start.13) | collective-permute-done | bytes 49184 | tf_op jit(solution)/shard_map/ppermute | solution.py:499
  36.9 1.0 %collective-permute-done.14.refs_3_ = f32[16,768]{1,0:T(8,128)S(1)} collective-permute-done((f32[16,768]{1,0:T(8,128)S(1)}, f32[16,768]{1,0:T(8,128)S(1)}, u32[]{:S(2)}, u32[]{:S(2)}) %collective-permute-start.14) | collective-permute-done | bytes 49184 | tf_op jit(solution)/shard_map/ppermute | solution.py:499
  37.9 0.7 %shard_map.55 = f32[16,512]{1,0:T(8,128)} custom-call(f32[16,768]{1,0:T(8,128)S(1)} %get-tuple-element.43.refs_0_, f32[16,768]{1,0:T(8,128)S(1)} %collective-permute-done.12.refs_1_, f32[16,768]{1,0:T(8,128)S(1)} %collective-permute-done.13.refs_2_, f32[16,768]{1,0:T(8,128)S(1)} %collective-permute-done.14.refs_3_, f32[16,512]{1,0:T(8,128)S(1)} %shard_map.54.refs_4_, ...), custom_call_target="tpu_custom_call" | custom-call | bytes 196608 | tf_op jit(solution)/shard_map/pallas_call | solution.py:575
  (20 shorter events, 0.7 us)
Async XLA Ops:
  1.7 3.2 %collective-permute-start = (bf16[1152,128]{1,0:T(8,128)(2,1)S(1)}, bf16[1152,128]{1,0:T(8,128)(2,1)S(1)}, u32[]{:S(2)}, u32[]{:S(2)}) collective-permute-start(bf16[1152,128]{1,0:T(8,128)(2,1)S(1)} %get-tuple-element.28), channel_id=1, source_target_pairs={{0,2},{2,0},{4,6},{6,4},{1,3},{3,1},{5,7},{7,5},{8,10},{10,8},{12,... | collective-permute-start | bytes 884744 | tf_op jit(solution)/shard_map/ppermute | solution.py:471
  2.2 4.6 %collective-permute-start.1 = (bf16[128,128]{1,0:T(8,128)(2,1)S(1)}, bf16[128,128]{1,0:T(8,128)(2,1)S(1)}, u32[]{:S(2)}, u32[]{:S(2)}) collective-permute-start(bf16[128,128]{1,0:T(8,128)(2,1)S(1)} %get-tuple-element.29), channel_id=1, source_target_pairs={{0,4},{2,6},{4,0},{6,2},{1,5},{3,7},{5,1},{7,3},{8,12},{10,14},{12... | collective-permute-start | bytes 98312 | tf_op jit(solution)/shard_map/ppermute | solution.py:471
  4.8 3.3 %collective-permute-start.2 = (bf16[128,128]{1,0:T(8,128)(2,1)S(1)}, bf16[128,128]{1,0:T(8,128)(2,1)S(1)}, u32[]{:S(2)}, u32[]{:S(2)}) collective-permute-start(bf16[128,128]{1,0:T(8,128)(2,1)S(1)} %get-tuple-element.30), channel_id=1, source_target_pairs={{0,6},{2,4},{4,2},{6,0},{1,7},{3,5},{5,3},{7,1},{8,14},{10,12},{12... | collective-permute-start | bytes 98312 | tf_op jit(solution)/shard_map/ppermute | solution.py:471
  5.0 9.5 %collective-permute-start.7 = (bf16[2,64,512]{2,1,0:T(8,128)(2,1)S(1)}, bf16[2,64,512]{2,1,0:T(8,128)(2,1)S(1)}, u32[]{:S(2)}, u32[]{:S(2)}) collective-permute-start(bf16[2,64,512]{2,1,0:T(8,128)(2,1)S(1)} %get-tuple-element.33), channel_id=1, source_target_pairs={{0,1},{1,0},{2,3},{3,2},{4,5},{5,4},{6,7},{7,6},{8,9},{9,8},{10,11... | collective-permute-start | bytes 393224 | tf_op jit(solution)/shard_map/ppermute | solution.py:499
  8.2 9.3 %collective-permute-start.4 = (bf16[4,128,128]{2,1,0:T(8,128)(2,1)S(1)}, bf16[4,128,128]{2,1,0:T(8,128)(2,1)S(1)}, u32[]{:S(2)}, u32[]{:S(2)}) collective-permute-start(bf16[4,128,128]{2,1,0:T(8,128)(2,1)S(1)} %shard_map.47.refs_0_), channel_id=1, source_target_pairs={{0,16},{16,0},{8,24},{24,8},{1,17},{17,1},{9,25},{25,9},{2,18},{18... | collective-permute-start | bytes 393224 | tf_op jit(solution)/shard_map/ppermute | solution.py:480
  10.8 8.1 %collective-permute-start.8 = (bf16[2,64,512]{2,1,0:T(8,128)(2,1)S(1)}, bf16[2,64,512]{2,1,0:T(8,128)(2,1)S(1)}, u32[]{:S(2)}, u32[]{:S(2)}) collective-permute-start(bf16[2,64,512]{2,1,0:T(8,128)(2,1)S(1)} %get-tuple-element.34), channel_id=1, source_target_pairs={{0,4},{1,5},{2,6},{3,7},{4,0},{5,1},{6,2},{7,3},{8,12},{9,13},{10,... | collective-permute-start | bytes 393224 | tf_op jit(solution)/shard_map/ppermute | solution.py:499
  11.7 7.2 %collective-permute-start.9 = (bf16[2,64,512]{2,1,0:T(8,128)(2,1)S(1)}, bf16[2,64,512]{2,1,0:T(8,128)(2,1)S(1)}, u32[]{:S(2)}, u32[]{:S(2)}) collective-permute-start(bf16[2,64,512]{2,1,0:T(8,128)(2,1)S(1)} %get-tuple-element.35), channel_id=1, source_target_pairs={{0,5},{1,4},{2,7},{3,6},{4,1},{5,0},{6,3},{7,2},{8,13},{9,12},{10,... | collective-permute-start | bytes 393224 | tf_op jit(solution)/shard_map/ppermute | solution.py:499
  13.8 6.5 %collective-permute-start.5 = (bf16[4,128,128]{2,1,0:T(8,128)(2,1)S(1)}, bf16[4,128,128]{2,1,0:T(8,128)(2,1)S(1)}, u32[]{:S(2)}, u32[]{:S(2)}) collective-permute-start(bf16[4,128,128]{2,1,0:T(8,128)(2,1)S(1)} %shard_map.47.refs_0_), channel_id=1, source_target_pairs={{8,16},{16,8},{9,17},{17,9},{10,18},{18,10},{11,19},{19,11},{12,20... | collective-permute-start | bytes 393224 | tf_op jit(solution)/shard_map/ppermute | solution.py:480
  14.5 5.9 %collective-permute-start.3 = (bf16[4,128,128]{2,1,0:T(8,128)(2,1)S(1)}, bf16[4,128,128]{2,1,0:T(8,128)(2,1)S(1)}, u32[]{:S(2)}, u32[]{:S(2)}) collective-permute-start(bf16[4,128,128]{2,1,0:T(8,128)(2,1)S(1)} %shard_map.47.refs_0_), channel_id=1, source_target_pairs={{0,8},{8,0},{16,24},{24,16},{1,9},{9,1},{17,25},{25,17},{2,10},{10... | collective-permute-start | bytes 393224 | tf_op jit(solution)/shard_map/ppermute | solution.py:480
  17.5 7.2 %collective-permute-start.6 = (bf16[4,128,128]{2,1,0:T(8,128)(2,1)S(1)}, bf16[4,128,128]{2,1,0:T(8,128)(2,1)S(1)}, u32[]{:S(2)}, u32[]{:S(2)}) collective-permute-start(bf16[4,128,128]{2,1,0:T(8,128)(2,1)S(1)} %collective-permute-done.4.refs_2_), channel_id=1, source_target_pairs={{8,0},{16,24},{9,1},{17,25},{10,2},{18,26},{11,3},{19,27},{12,4},{... | collective-permute-start | bytes 393224 | tf_op jit(solution)/shard_map/ppermute | solution.py:480
  19.0 5.7 %copy-start.1 = (s32[480]{0:T(512)S(1)}, s32[480]{0:T(512)}, u32[]{:S(2)}) copy-start(s32[480]{0:T(512)} %param.7) | copy-start | bytes 5764
  19.0 7.2 %collective-permute-start.10 = (bf16[64,256]{1,0:T(8,128)(2,1)S(1)}, bf16[64,256]{1,0:T(8,128)(2,1)S(1)}, u32[]{:S(2)}, u32[]{:S(2)}) collective-permute-start(bf16[64,256]{1,0:T(8,128)(2,1)S(1)} %get-tuple-element.38), channel_id=1, source_target_pairs={{8,0},{16,8},{24,16},{9,1},{17,9},{25,17},{10,2},{18,10},{26,18},{... | collective-permute-start | bytes 98312 | tf_op jit(solution)/shard_map/ppermute | solution.py:514
  28.1 2.5 %collective-permute-start.11 = (f32[4,16,768]{2,1,0:T(8,128)S(1)}, f32[4,16,768]{2,1,0:T(8,128)S(1)}, u32[]{:S(2)}, u32[]{:S(2)}) collective-permute-start(f32[4,16,768]{2,1,0:T(8,128)S(1)} %get-tuple-element.42.after), channel_id=1, source_target_pairs={{0,2},{2,0},{4,6},{6,4},{1,3},{3,1},{5,7},{7,5},{8,10},{10,8},{12,... | collective-permute-start | bytes 589832 | tf_op jit(solution)/shard_map/ppermute | solution.py:560
  28.2 6.0 %copy-start = (bf16[480,512]{1,0:T(8,128)(2,1)S(1)}, bf16[480,512]{1,0:T(8,128)(2,1)}, u32[]{:S(2)}) copy-start(bf16[480,512]{1,0:T(8,128)(2,1)} %wave_ref.1) | copy-start | bytes 1474564
  30.7 5.1 %collective-permute-start.12 = (f32[16,768]{1,0:T(8,128)S(1)}, f32[16,768]{1,0:T(8,128)S(1)}, u32[]{:S(2)}, u32[]{:S(2)}) collective-permute-start(f32[16,768]{1,0:T(8,128)S(1)} %get-tuple-element.44), channel_id=1, source_target_pairs={{0,5},{1,4},{2,7},{3,6},{4,1},{5,0},{6,3},{7,2},{8,13},{9,12},{10,... | collective-permute-start | bytes 147464 | tf_op jit(solution)/shard_map/ppermute | solution.py:499
  32.7 4.2 %collective-permute-start.13 = (f32[16,768]{1,0:T(8,128)S(1)}, f32[16,768]{1,0:T(8,128)S(1)}, u32[]{:S(2)}, u32[]{:S(2)}) collective-permute-start(f32[16,768]{1,0:T(8,128)S(1)} %get-tuple-element.45), channel_id=1, source_target_pairs={{0,4},{1,5},{2,6},{3,7},{4,0},{5,1},{6,2},{7,3},{8,12},{9,13},{10,... | collective-permute-start | bytes 147464 | tf_op jit(solution)/shard_map/ppermute | solution.py:499
  33.8 4.1 %collective-permute-start.14 = (f32[16,768]{1,0:T(8,128)S(1)}, f32[16,768]{1,0:T(8,128)S(1)}, u32[]{:S(2)}, u32[]{:S(2)}) collective-permute-start(f32[16,768]{1,0:T(8,128)S(1)} %get-tuple-element.46), channel_id=1, source_target_pairs={{0,1},{1,0},{2,3},{3,2},{4,5},{5,4},{6,7},{7,6},{8,9},{9,8},{10,11... | collective-permute-start | bytes 147464 | tf_op jit(solution)/shard_map/ppermute | solution.py:499

commit v20 on v19

--- a/solution.py
+++ b/solution.py
@@ -224,18 +224,18 @@
     count = size // FINE
     copies = LANES // FINE
     width = run * slab
-    for y in ys:
+    for slot, y in enumerate(ys):
         columns = width + 2 * LANES
         start = pl.multiple_of((2 * y + side) * width, width)
         samples = full[:, pl.ds(start, columns)]
         for copy in range(depth // part):
             tile, turn = copy // copies * LANES, copy % copies * FINE
             turned = samples if turn == 0 else pltpu.roll(samples, columns - turn, 1)
-            shifts[y, copy * part : (copy + 1) * part, :] = turned[:, tile : tile + width + LANES]
+            shifts[slot, copy * part : (copy + 1) * part, :] = turned[:, tile : tile + width + LANES]
     tiles = products.shape[1]
     span = (tiles - 1) * LANES
     per_block = span // slab
-    blocks = [(y, index) for y in ys for index in range(width // span)]
+    blocks = [(y, index) for y in range(len(ys)) for index in range(width // span)]
 
     def multiply(place, slot):
         y, index = place
@@ -262,9 +262,9 @@
             return tree(first, half) + later
 
         total = tree(0, FINE)
-        y, index = place
+        _, index = place
         for piece in range(per_block):
-            store(y, index * per_block + piece, total[:, piece * slab : (piece + 1) * slab])
+            store(index * per_block + piece, total[:, piece * slab : (piece + 1) * slab])
 
     multiply(blocks[0], 0)
     for number in range(1, len(blocks)):
@@ -283,7 +283,7 @@
     core = lax.rem(lax.axis_index("inner"), 2)
     run, _, slab = begun_ref.shape
 
-    def store(y, place, sums):
+    def store(place, sums):
         begun_ref[place] = sums
 
     correlate(left, samples_ref, slab, run, 1 - core, [0], store, shifts, products)
@@ -300,8 +300,8 @@
     full[:, :chunk] = samples_ref[...]
     full[:, chunk:] = halo_ref[...]
 
-    def store(y, place, sums):
-        send_ref[y * run + place, :, :slab] = sums
+    def store(place, sums):
+        send_ref[run + place, :, :slab] = sums
 
     correlate(left, full, slab, run, 1 - core, [1], store, shifts, products)
     after = [full[:, (m + 1) * slab : (m + 1) * slab + window] for m in range(group)]
@@ -322,27 +322,32 @@
             edges_ref[y * run + tm] = edges[(2 * y + core) * run + tm]
 
 
-def last_dots_kernel(left, samples_ref, halo_ref, edges_ref, after, keep_ref, *scratch):
+def own_dots_kernel(far, left, samples_ref, halo_ref, edges_ref, after, keep_ref, *scratch):
     del after
     full, shifts, products = scratch
     chunk = samples_ref.shape[1]
     full[:, :chunk] = samples_ref[...]
     full[:, chunk:] = halo_ref[...]
     core = lax.rem(lax.axis_index("inner"), 2)
-    run = keep_ref.shape[0] // 2
+    y = lax.div(lax.axis_index("inner"), 2) ^ far
+    run = keep_ref.shape[0]
     slab = keep_ref.shape[2] - edges_ref.shape[2]
 
-    def store(y, place, sums):
-        keep_ref[y * run + place, :, :slab] = sums
-
-    correlate(left, full, slab, run, core, [0, 1], store, shifts, products)
-    keep_ref[:, :, slab:] = edges_ref[...]
-
-
-def add_kernel(tm_count, keep_ref, got_ref, *outs):
-    me = lax.div(lax.axis_index("inner"), 2) * tm_count + lax.axis_index("tm")
+    def store(place, sums):
+        keep_ref[place, :, :slab] = sums
+
+    correlate(left, full, slab, run, core, [y], store, shifts, products)
+    for tm in range(run):
+        keep_ref[tm, :, slab:] = edges_ref[y * run + tm]
+
+
+def add_kernel(far, keep_ref, got_ref, *outs):
+    y = lax.div(lax.axis_index("inner"), 2) ^ far
+    my_tm = lax.axis_index("tm")
+    run = keep_ref.shape[0]
     for flip, out_ref in enumerate(outs):
-        out_ref[...] = keep_ref[me ^ flip] + got_ref[me ^ flip]
+        tm = my_tm ^ flip
+        out_ref[...] = keep_ref[tm] + got_ref[y * run + tm]
 
 
 def masked_squares(mask, wave):
@@ -548,33 +553,40 @@
         bytes_accessed=part * chunk * 2,
         vmem=36,
     )(left, samples, halo, begun, mask_part)
-    keep = call(
-        last_dots_kernel,
-        [VMEM] * 4 + [AFTER],
-        sds((half, count, slab + window), F32),
-        [full] + scratch(),
-        flops=work,
-        bytes_accessed=part * chunk * 2,
-        vmem=36,
-    )(left, samples, halo, edges, send)
     got = lax.ppermute(send, "inner", [(b, b ^ 1) for b in range(INNER)])
+
+    def own(far, after):
+        keep = call(
+            functools.partial(own_dots_kernel, far),
+            [VMEM] * 4 + [AFTER],
+            sds((tm_count, count, slab + window), F32),
+            [full] + scratch(),
+            flops=work // 2,
+            bytes_accessed=part * chunk * 2,
+            vmem=36,
+        )(left, samples, halo, edges, after)
+        return call(
+            functools.partial(add_kernel, far),
+            [VMEM] * 2,
+            [sds((count, slab + window), F32)] * tm_count,
+            bytes_accessed=count * slab * 12 * tm_count,
+        )(keep, got)
+
+    theirs = own(1, send)
+    ours = own(0, theirs[0])
     power = call(
         functools.partial(power_kernel, window),
         [VMEM, VMEM, AFTER],
         sds((blk_count, slab), F32),
         flops=4 * blk_count * channels * slab,
         bytes_accessed=channels * slab * 2,
-    )(waveforms, mask, keep)
-    sums = call(
-        functools.partial(add_kernel, tm_count),
-        [VMEM] * 2,
-        [sds((blk_count, slab + window), F32)] * half,
-        bytes_accessed=blk_count * slab * 12 * half,
-    )(keep, got)
-    sums = [sums[0]] + [swap(sums[flip], flip) for flip in reversed(range(1, half))]
+    )(waveforms, mask, ours[0])
+    far = [swap(theirs[tm], tm_count + tm) for tm in reversed(range(tm_count))]
+    sums = [functools.reduce(jnp.add, far)]
+    sums += [swap(ours[tm], tm) for tm in range(1, tm_count)] + [ours[0]]
     return call(
         finish_kernel,
-        [VMEM] * (half + 2),
+        [VMEM] * (len(sums) + 2),
         sds((blk_count, slab), F32),
         bytes_accessed=blk_count * slab * 4 * (half + 2),
     )(*sums, power, scale)

time: 38.8 us -> 39.3 us (1.013)
  Pallas kernels: 9.22 us -> 9.64 us
    pallas_call x3 -> x5, Pallas kernels: 3.13 us -> 3.56 us  [the longest x2 2.85 us: own(): call(functools.partial(own_dots_kernel, far), [VMEM] * 4 + [AFTER], sds((...]
  transfers between devices with their start and end apart: 15 -> 15, of which waited for: 8 -> 7; matrix products, arithmetic and copies ran while one was open for 0% -> 0% of each run, Pallas kernels for 13% -> 14%
where the time goes in v20:
time: 39.3 us; the launch traced here: 39.1 us
  starting transfers between devices  20.4 us (52%)
  Pallas kernels  9.64 us (25%)
  waiting for transfers between devices  8.94 us (23%)
    ppermute x6, starting transfers between devices, swap(): return lax.ppermute(part, every, route)  8.34 us
    ppermute x4, starting transfers between devices, cross(): return lax.ppermute(part, 'outer', route)  7.48 us
    ppermute x4, waiting for transfers between devices, cross(): return lax.ppermute(part, 'outer', route)  4.57 us
    ppermute x3, starting transfers between devices, plane(): return lax.ppermute(part, 'inner', [(b, b ^ flip) for b in range(INNER)])  3.18 us
    ppermute x6, waiting for transfers between devices, swap(): return lax.ppermute(part, every, route)  2.9 us
    pallas_call x2, Pallas kernels, own(): call(functools.partial(own_dots_kernel, far), [VMEM] * 4 + [AFTER], sds((...  2.85 us
    pallas_call x1, Pallas kernels, on_device(): call(middle_dots_kernel, [VMEM] * 5, [sds((half, count, slab + window), F...  1.87 us
    pallas_call x1, Pallas kernels, on_device(): call(functools.partial(prologue_kernel, tm_count), [HBM] * 4, [sds((padde...  1.7 us
  transfers between devices with their start and end apart: 15, of which 7 were waited for; matrix products, arithmetic and copies ran while one was open for 0% of the time, Pallas kernels for 14%

profile of v20, /device:TPU:0, one launch (start us, length us, event | category | flops | bytes accessed | tf_op | source)
XLA Modules:
  0.0 39.1 jit_solution(17077838644476253352)
XLA Ops:
  0.0 1.7 %shard_map.46 = (bf16[1152,128]{1,0:T(8,128)(2,1)S(1)}, bf16[256,512]{1,0:T(8,128)(2,1)S(1)}, bf16[128,128]{1,0:T(8,128)(2,1)S(1)}, bf16[128,128]{1,0:T(8,128)(2,1)S(1)}, bf16[128,128]{1,0:T(8,128)(2,1)S(1)}) custom-call(bf16[480,512]{1,0:T(8,128)(2,1)} %wave_ref.1, bf16[1,480,256]{2,1,0:T(8,128)(2,1)} %tpl_hbm.1, s32[1,160]{1,0:T(1,128)} %flag_hbm.1, ...), custom_call_target="tpu_custom_call" | custom-call | bytes 737280 | tf_op jit(solution)/shard_map/pallas_call | solution.py:454
  1.7 0.5 %collective-permute-start = (bf16[1152,128]{1,0:T(8,128)(2,1)S(1)}, bf16[1152,128]{1,0:T(8,128)(2,1)S(1)}, u32[]{:S(2)}, u32[]{:S(2)}) collective-permute-start(bf16[1152,128]{1,0:T(8,128)(2,1)S(1)} %get-tuple-element.28), channel_id=1, source_target_pairs={{0,2},{2,0},{4,6},{6,4},{1,3},{3,1},{5,7},{7,5},{8,10},{10,8},{12,... | collective-permute-start | bytes 884744 | tf_op jit(solution)/shard_map/ppermute | solution.py:476
  2.2 2.6 %collective-permute-start.1 = (bf16[128,128]{1,0:T(8,128)(2,1)S(1)}, bf16[128,128]{1,0:T(8,128)(2,1)S(1)}, u32[]{:S(2)}, u32[]{:S(2)}) collective-permute-start(bf16[128,128]{1,0:T(8,128)(2,1)S(1)} %get-tuple-element.29), channel_id=1, source_target_pairs={{0,4},{2,6},{4,0},{6,2},{1,5},{3,7},{5,1},{7,3},{8,12},{10,14},{12... | collective-permute-start | bytes 98312 | tf_op jit(solution)/shard_map/ppermute | solution.py:476
  5.0 1.8 %collective-permute-start.7 = (bf16[2,64,512]{2,1,0:T(8,128)(2,1)S(1)}, bf16[2,64,512]{2,1,0:T(8,128)(2,1)S(1)}, u32[]{:S(2)}, u32[]{:S(2)}) collective-permute-start(bf16[2,64,512]{2,1,0:T(8,128)(2,1)S(1)} %get-tuple-element.33), channel_id=1, source_target_pairs={{0,1},{1,0},{2,3},{3,2},{4,5},{5,4},{6,7},{7,6},{8,9},{9,8},{10,11... | collective-permute-start | bytes 393224 | tf_op jit(solution)/shard_map/ppermute | solution.py:504
  6.8 1.4 %collective-permute-done.2.both_ref = bf16[128,128]{1,0:T(8,128)(2,1)S(1)} collective-permute-done((bf16[128,128]{1,0:T(8,128)(2,1)S(1)}, bf16[128,128]{1,0:T(8,128)(2,1)S(1)}, u32[]{:S(2)}, u32[]{:S(2)}) %collective-permute-start.2) | collective-permute-done | bytes 32800 | tf_op jit(solution)/shard_map/ppermute | solution.py:476
  8.2 2.7 %collective-permute-start.4 = (bf16[4,128,128]{2,1,0:T(8,128)(2,1)S(1)}, bf16[4,128,128]{2,1,0:T(8,128)(2,1)S(1)}, u32[]{:S(2)}, u32[]{:S(2)}) collective-permute-start(bf16[4,128,128]{2,1,0:T(8,128)(2,1)S(1)} %shard_map.47.refs_0_), channel_id=1, source_target_pairs={{0,16},{16,0},{8,24},{24,8},{1,17},{17,1},{9,25},{25,9},{2,18},{18... | collective-permute-start | bytes 393224 | tf_op jit(solution)/shard_map/ppermute | solution.py:485
  10.8 0.9 %collective-permute-start.8 = (bf16[2,64,512]{2,1,0:T(8,128)(2,1)S(1)}, bf16[2,64,512]{2,1,0:T(8,128)(2,1)S(1)}, u32[]{:S(2)}, u32[]{:S(2)}) collective-permute-start(bf16[2,64,512]{2,1,0:T(8,128)(2,1)S(1)} %get-tuple-element.34), channel_id=1, source_target_pairs={{0,4},{1,5},{2,6},{3,7},{4,0},{5,1},{6,2},{7,3},{8,12},{9,13},{10,... | collective-permute-start | bytes 393224 | tf_op jit(solution)/shard_map/ppermute | solution.py:504
  11.7 2.1 %collective-permute-start.9 = (bf16[2,64,512]{2,1,0:T(8,128)(2,1)S(1)}, bf16[2,64,512]{2,1,0:T(8,128)(2,1)S(1)}, u32[]{:S(2)}, u32[]{:S(2)}) collective-permute-start(bf16[2,64,512]{2,1,0:T(8,128)(2,1)S(1)} %get-tuple-element.35), channel_id=1, source_target_pairs={{0,5},{1,4},{2,7},{3,6},{4,1},{5,0},{6,3},{7,2},{8,13},{9,12},{10,... | collective-permute-start | bytes 393224 | tf_op jit(solution)/shard_map/ppermute | solution.py:504
  13.8 0.7 %collective-permute-start.5 = (bf16[4,128,128]{2,1,0:T(8,128)(2,1)S(1)}, bf16[4,128,128]{2,1,0:T(8,128)(2,1)S(1)}, u32[]{:S(2)}, u32[]{:S(2)}) collective-permute-start(bf16[4,128,128]{2,1,0:T(8,128)(2,1)S(1)} %shard_map.47.refs_0_), channel_id=1, source_target_pairs={{8,16},{16,8},{9,17},{17,9},{10,18},{18,10},{11,19},{19,11},{12,20... | collective-permute-start | bytes 393224 | tf_op jit(solution)/shard_map/ppermute | solution.py:485
  14.5 2.9 %collective-permute-start.3 = (bf16[4,128,128]{2,1,0:T(8,128)(2,1)S(1)}, bf16[4,128,128]{2,1,0:T(8,128)(2,1)S(1)}, u32[]{:S(2)}, u32[]{:S(2)}) collective-permute-start(bf16[4,128,128]{2,1,0:T(8,128)(2,1)S(1)} %shard_map.47.refs_0_), channel_id=1, source_target_pairs={{0,8},{8,0},{16,24},{24,16},{1,9},{9,1},{17,25},{25,17},{2,10},{10... | collective-permute-start | bytes 393224 | tf_op jit(solution)/shard_map/ppermute | solution.py:485
  17.5 1.3 %collective-permute-start.6 = (bf16[4,128,128]{2,1,0:T(8,128)(2,1)S(1)}, bf16[4,128,128]{2,1,0:T(8,128)(2,1)S(1)}, u32[]{:S(2)}, u32[]{:S(2)}) collective-permute-start(bf16[4,128,128]{2,1,0:T(8,128)(2,1)S(1)} %collective-permute-done.4.refs_2_), channel_id=1, source_target_pairs={{8,0},{16,24},{9,1},{17,25},{10,2},{18,26},{11,3},{19,27},{12,4},{... | collective-permute-start | bytes 393224 | tf_op jit(solution)/shard_map/ppermute | solution.py:485
  19.0 1.3 %collective-permute-start.10 = (bf16[64,256]{1,0:T(8,128)(2,1)S(1)}, bf16[64,256]{1,0:T(8,128)(2,1)S(1)}, u32[]{:S(2)}, u32[]{:S(2)}) collective-permute-start(bf16[64,256]{1,0:T(8,128)(2,1)S(1)} %get-tuple-element.38), channel_id=1, source_target_pairs={{8,0},{16,8},{24,16},{9,1},{17,9},{25,17},{10,2},{18,10},{26,18},{... | collective-permute-start | bytes 98312 | tf_op jit(solution)/shard_map/ppermute | solution.py:519
  20.3 4.4 %collective-permute-done.6.refs_4_ = bf16[4,128,128]{2,1,0:T(8,128)(2,1)S(1)} collective-permute-done((bf16[4,128,128]{2,1,0:T(8,128)(2,1)S(1)}, bf16[4,128,128]{2,1,0:T(8,128)(2,1)S(1)}, u32[]{:S(2)}, u32[]{:S(2)}) %collective-permute-start.6) | collective-permute-done | bytes 131104 | tf_op jit(solution)/shard_map/ppermute | solution.py:485
  24.7 1.5 %shard_map.50 = (f32[2,16,512]{2,1,0:T(8,128)S(1)}, bf16[256,1024]{1,0:T(8,128)(2,1)S(1)}, f32[16,128]{1,0:T(8,128)S(1)}, bf16[16,480]{1,0:T(8,128)(2,1)S(1)}, bf16[16,64]{1,0:T(8,128)(2,1)S(1)}) custom-call(bf16[4,128,128]{2,1,0:T(8,128)(2,1)S(1)} %shard_map.47.refs_0_, bf16[4,128,128]{2,1,0:T(8,128)(2,1)S(1)} %collective-permute-done.3.refs_1_, ...), custom_call_target="tpu_custom_call" | custom-call | flops 536870912 | bytes 524288 | tf_op jit(solution)/shard_map/pallas_call | solution.py:531
  26.3 1.9 %shard_map.51 = (f32[4,16,768]{2,1,0:T(8,128)S(1)}, f32[4,16,256]{2,1,0:T(8,128)S(1)}) custom-call(bf16[256,1024]{1,0:T(8,128)(2,1)S(1)} %get-tuple-element.37.left, bf16[64,4096]{1,0:T(8,128)(2,1)S(1)} %get-tuple-element.36.refs_6_.samples_ref, bf16[64,256]{1,0:T(8,128)(2,1)S(1)} %collective-permute-done.10.halo_ref, ...), custom_call_target="tpu_custom_call" | custom-call | flops 536870912 | bytes 524288 | tf_op jit(solution)/shard_map/pallas_call | solution.py:547
  28.2 1.4 %shard_map.52.keep_ref = f32[2,16,768]{2,1,0:T(8,128)S(1)} custom-call(bf16[256,1024]{1,0:T(8,128)(2,1)S(1)} %get-tuple-element.37.left, bf16[64,4096]{1,0:T(8,128)(2,1)S(1)} %get-tuple-element.36.refs_6_.samples_ref, bf16[64,256]{1,0:T(8,128)(2,1)S(1)} %collective-permute-done.10.halo_ref, f32[4,16,256]{2,1,0:T(8,128)S(1)} %get-tuple-element.41.edges_ref, ...), custom_call_target="tpu_custom_call" | custom-call | flops 536870912 | bytes 524288 | tf_op jit(solution)/shard_map/pallas_call | solution.py:559
  29.7 2.0 %collective-permute-start.12 = (f32[16,768]{1,0:T(8,128)S(1)}, f32[16,768]{1,0:T(8,128)S(1)}, u32[]{:S(2)}, u32[]{:S(2)}) collective-permute-start(f32[16,768]{1,0:T(8,128)S(1)} %get-tuple-element.43), channel_id=1, source_target_pairs={{0,5},{1,4},{2,7},{3,6},{4,1},{5,0},{6,3},{7,2},{8,13},{9,12},{10,... | collective-permute-start | bytes 147464 | tf_op jit(solution)/shard_map/ppermute | solution.py:504
  31.6 1.2 %collective-permute-start.13 = (f32[16,768]{1,0:T(8,128)S(1)}, f32[16,768]{1,0:T(8,128)S(1)}, u32[]{:S(2)}, u32[]{:S(2)}) collective-permute-start(f32[16,768]{1,0:T(8,128)S(1)} %get-tuple-element.44.after), channel_id=1, source_target_pairs={{0,4},{1,5},{2,6},{3,7},{4,0},{5,1},{6,2},{7,3},{8,12},{9,13},{10,... | collective-permute-start | bytes 147464 | tf_op jit(solution)/shard_map/ppermute | solution.py:504
  32.8 1.4 %shard_map.54.keep_ref = f32[2,16,768]{2,1,0:T(8,128)S(1)} custom-call(bf16[256,1024]{1,0:T(8,128)(2,1)S(1)} %get-tuple-element.37.left, bf16[64,4096]{1,0:T(8,128)(2,1)S(1)} %get-tuple-element.36.refs_6_.samples_ref, bf16[64,256]{1,0:T(8,128)(2,1)S(1)} %collective-permute-done.10.halo_ref, f32[4,16,256]{2,1,0:T(8,128)S(1)} %get-tuple-element.41.edges_ref, ...), custom_call_target="tpu_custom_call" | custom-call | flops 536870912 | bytes 524288 | tf_op jit(solution)/shard_map/pallas_call | solution.py:559
  34.2 0.5 %collective-permute-start.14 = (f32[16,768]{1,0:T(8,128)S(1)}, f32[16,768]{1,0:T(8,128)S(1)}, u32[]{:S(2)}, u32[]{:S(2)}) collective-permute-start(f32[16,768]{1,0:T(8,128)S(1)} %get-tuple-element.45), channel_id=1, source_target_pairs={{0,1},{1,0},{2,3},{3,2},{4,5},{5,4},{6,7},{7,6},{8,9},{9,8},{10,11... | collective-permute-start | bytes 147464 | tf_op jit(solution)/shard_map/ppermute | solution.py:504
  34.8 0.9 %shard_map.56.refs_3_ = f32[16,512]{1,0:T(8,128)S(1)} custom-call(bf16[480,512]{1,0:T(8,128)(2,1)S(1)} %copy-done, bf16[16,480]{1,0:T(8,128)(2,1)S(1)} %get-tuple-element.47.mask_ref, f32[16,768]{1,0:T(8,128)S(1)} %get-tuple-element.46.after.refs_2_), custom_call_target="tpu_custom_call" | custom-call | flops 15728640 | bytes 491520 | tf_op jit(solution)/shard_map/pallas_call | solution.py:577
  35.6 0.2 collective-permute-done.13
  35.8 2.6 %collective-permute-done.14.refs_1_ = f32[16,768]{1,0:T(8,128)S(1)} collective-permute-done((f32[16,768]{1,0:T(8,128)S(1)}, f32[16,768]{1,0:T(8,128)S(1)}, u32[]{:S(2)}, u32[]{:S(2)}) %collective-permute-start.14) | collective-permute-done | bytes 49184 | tf_op jit(solution)/shard_map/ppermute | solution.py:504
  38.4 0.7 %shard_map.57 = f32[16,512]{1,0:T(8,128)} custom-call(f32[16,768]{1,0:T(8,128)S(1)} %add.3.refs_0_, f32[16,768]{1,0:T(8,128)S(1)} %collective-permute-done.14.refs_1_, f32[16,768]{1,0:T(8,128)S(1)} %get-tuple-element.46.after.refs_2_, f32[16,512]{1,0:T(8,128)S(1)} %shard_map.56.refs_3_, f32[16,128]{1,0:T(8,128)S(1)} %get-tuple-element.48.refs_4_), custom_call_target="tpu_custom_call" | custom-call | bytes 196608 | tf_op jit(solution)/shard_map/pallas_call | solution.py:587
  (23 shorter events, 0.7 us)
Async XLA Ops:
  1.7 3.2 %collective-permute-start = (bf16[1152,128]{1,0:T(8,128)(2,1)S(1)}, bf16[1152,128]{1,0:T(8,128)(2,1)S(1)}, u32[]{:S(2)}, u32[]{:S(2)}) collective-permute-start(bf16[1152,128]{1,0:T(8,128)(2,1)S(1)} %get-tuple-element.28), channel_id=1, source_target_pairs={{0,2},{2,0},{4,6},{6,4},{1,3},{3,1},{5,7},{7,5},{8,10},{10,8},{12,... | collective-permute-start | bytes 884744 | tf_op jit(solution)/shard_map/ppermute | solution.py:476
  2.2 4.6 %collective-permute-start.1 = (bf16[128,128]{1,0:T(8,128)(2,1)S(1)}, bf16[128,128]{1,0:T(8,128)(2,1)S(1)}, u32[]{:S(2)}, u32[]{:S(2)}) collective-permute-start(bf16[128,128]{1,0:T(8,128)(2,1)S(1)} %get-tuple-element.29), channel_id=1, source_target_pairs={{0,4},{2,6},{4,0},{6,2},{1,5},{3,7},{5,1},{7,3},{8,12},{10,14},{12... | collective-permute-start | bytes 98312 | tf_op jit(solution)/shard_map/ppermute | solution.py:476
  4.8 3.3 %collective-permute-start.2 = (bf16[128,128]{1,0:T(8,128)(2,1)S(1)}, bf16[128,128]{1,0:T(8,128)(2,1)S(1)}, u32[]{:S(2)}, u32[]{:S(2)}) collective-permute-start(bf16[128,128]{1,0:T(8,128)(2,1)S(1)} %get-tuple-element.30), channel_id=1, source_target_pairs={{0,6},{2,4},{4,2},{6,0},{1,7},{3,5},{5,3},{7,1},{8,14},{10,12},{12... | collective-permute-start | bytes 98312 | tf_op jit(solution)/shard_map/ppermute | solution.py:476
  5.0 9.5 %collective-permute-start.7 = (bf16[2,64,512]{2,1,0:T(8,128)(2,1)S(1)}, bf16[2,64,512]{2,1,0:T(8,128)(2,1)S(1)}, u32[]{:S(2)}, u32[]{:S(2)}) collective-permute-start(bf16[2,64,512]{2,1,0:T(8,128)(2,1)S(1)} %get-tuple-element.33), channel_id=1, source_target_pairs={{0,1},{1,0},{2,3},{3,2},{4,5},{5,4},{6,7},{7,6},{8,9},{9,8},{10,11... | collective-permute-start | bytes 393224 | tf_op jit(solution)/shard_map/ppermute | solution.py:504
  8.2 9.3 %collective-permute-start.4 = (bf16[4,128,128]{2,1,0:T(8,128)(2,1)S(1)}, bf16[4,128,128]{2,1,0:T(8,128)(2,1)S(1)}, u32[]{:S(2)}, u32[]{:S(2)}) collective-permute-start(bf16[4,128,128]{2,1,0:T(8,128)(2,1)S(1)} %shard_map.47.refs_0_), channel_id=1, source_target_pairs={{0,16},{16,0},{8,24},{24,8},{1,17},{17,1},{9,25},{25,9},{2,18},{18... | collective-permute-start | bytes 393224 | tf_op jit(solution)/shard_map/ppermute | solution.py:485
  10.8 8.1 %collective-permute-start.8 = (bf16[2,64,512]{2,1,0:T(8,128)(2,1)S(1)}, bf16[2,64,512]{2,1,0:T(8,128)(2,1)S(1)}, u32[]{:S(2)}, u32[]{:S(2)}) collective-permute-start(bf16[2,64,512]{2,1,0:T(8,128)(2,1)S(1)} %get-tuple-element.34), channel_id=1, source_target_pairs={{0,4},{1,5},{2,6},{3,7},{4,0},{5,1},{6,2},{7,3},{8,12},{9,13},{10,... | collective-permute-start | bytes 393224 | tf_op jit(solution)/shard_map/ppermute | solution.py:504
  11.7 7.2 %collective-permute-start.9 = (bf16[2,64,512]{2,1,0:T(8,128)(2,1)S(1)}, bf16[2,64,512]{2,1,0:T(8,128)(2,1)S(1)}, u32[]{:S(2)}, u32[]{:S(2)}) collective-permute-start(bf16[2,64,512]{2,1,0:T(8,128)(2,1)S(1)} %get-tuple-element.35), channel_id=1, source_target_pairs={{0,5},{1,4},{2,7},{3,6},{4,1},{5,0},{6,3},{7,2},{8,13},{9,12},{10,... | collective-permute-start | bytes 393224 | tf_op jit(solution)/shard_map/ppermute | solution.py:504
  13.8 6.5 %collective-permute-start.5 = (bf16[4,128,128]{2,1,0:T(8,128)(2,1)S(1)}, bf16[4,128,128]{2,1,0:T(8,128)(2,1)S(1)}, u32[]{:S(2)}, u32[]{:S(2)}) collective-permute-start(bf16[4,128,128]{2,1,0:T(8,128)(2,1)S(1)} %shard_map.47.refs_0_), channel_id=1, source_target_pairs={{8,16},{16,8},{9,17},{17,9},{10,18},{18,10},{11,19},{19,11},{12,20... | collective-permute-start | bytes 393224 | tf_op jit(solution)/shard_map/ppermute | solution.py:485
  14.5 5.9 %collective-permute-start.3 = (bf16[4,128,128]{2,1,0:T(8,128)(2,1)S(1)}, bf16[4,128,128]{2,1,0:T(8,128)(2,1)S(1)}, u32[]{:S(2)}, u32[]{:S(2)}) collective-permute-start(bf16[4,128,128]{2,1,0:T(8,128)(2,1)S(1)} %shard_map.47.refs_0_), channel_id=1, source_target_pairs={{0,8},{8,0},{16,24},{24,16},{1,9},{9,1},{17,25},{25,17},{2,10},{10... | collective-permute-start | bytes 393224 | tf_op jit(solution)/shard_map/ppermute | solution.py:485
  17.5 7.2 %collective-permute-start.6 = (bf16[4,128,128]{2,1,0:T(8,128)(2,1)S(1)}, bf16[4,128,128]{2,1,0:T(8,128)(2,1)S(1)}, u32[]{:S(2)}, u32[]{:S(2)}) collective-permute-start(bf16[4,128,128]{2,1,0:T(8,128)(2,1)S(1)} %collective-permute-done.4.refs_2_), channel_id=1, source_target_pairs={{8,0},{16,24},{9,1},{17,25},{10,2},{18,26},{11,3},{19,27},{12,4},{... | collective-permute-start | bytes 393224 | tf_op jit(solution)/shard_map/ppermute | solution.py:485
  19.0 5.7 %copy-start.1 = (s32[480]{0:T(512)S(1)}, s32[480]{0:T(512)}, u32[]{:S(2)}) copy-start(s32[480]{0:T(512)} %param.7) | copy-start | bytes 5764
  19.0 7.2 %collective-permute-start.10 = (bf16[64,256]{1,0:T(8,128)(2,1)S(1)}, bf16[64,256]{1,0:T(8,128)(2,1)S(1)}, u32[]{:S(2)}, u32[]{:S(2)}) collective-permute-start(bf16[64,256]{1,0:T(8,128)(2,1)S(1)} %get-tuple-element.38), channel_id=1, source_target_pairs={{8,0},{16,8},{24,16},{9,1},{17,9},{25,17},{10,2},{18,10},{26,18},{... | collective-permute-start | bytes 98312 | tf_op jit(solution)/shard_map/ppermute | solution.py:519
  28.1 1.5 %collective-permute-start.11 = (f32[4,16,768]{2,1,0:T(8,128)S(1)}, f32[4,16,768]{2,1,0:T(8,128)S(1)}, u32[]{:S(2)}, u32[]{:S(2)}) collective-permute-start(f32[4,16,768]{2,1,0:T(8,128)S(1)} %get-tuple-element.42.after), channel_id=1, source_target_pairs={{0,2},{2,0},{4,6},{6,4},{1,3},{3,1},{5,7},{7,5},{8,10},{10,8},{12,... | collective-permute-start | bytes 589832 | tf_op jit(solution)/shard_map/ppermute | solution.py:556
  29.7 6.0 %collective-permute-start.12 = (f32[16,768]{1,0:T(8,128)S(1)}, f32[16,768]{1,0:T(8,128)S(1)}, u32[]{:S(2)}, u32[]{:S(2)}) collective-permute-start(f32[16,768]{1,0:T(8,128)S(1)} %get-tuple-element.43), channel_id=1, source_target_pairs={{0,5},{1,4},{2,7},{3,6},{4,1},{5,0},{6,3},{7,2},{8,13},{9,12},{10,... | collective-permute-start | bytes 147464 | tf_op jit(solution)/shard_map/ppermute | solution.py:504
  31.6 4.2 %collective-permute-start.13 = (f32[16,768]{1,0:T(8,128)S(1)}, f32[16,768]{1,0:T(8,128)S(1)}, u32[]{:S(2)}, u32[]{:S(2)}) collective-permute-start(f32[16,768]{1,0:T(8,128)S(1)} %get-tuple-element.44.after), channel_id=1, source_target_pairs={{0,4},{1,5},{2,6},{3,7},{4,0},{5,1},{6,2},{7,3},{8,12},{9,13},{10,... | collective-permute-start | bytes 147464 | tf_op jit(solution)/shard_map/ppermute | solution.py:504
  32.8 2.0 %copy-start = (bf16[480,512]{1,0:T(8,128)(2,1)S(1)}, bf16[480,512]{1,0:T(8,128)(2,1)}, u32[]{:S(2)}) copy-start(bf16[480,512]{1,0:T(8,128)(2,1)} %wave_ref.1) | copy-start | bytes 1474564
  34.2 4.2 %collective-permute-start.14 = (f32[16,768]{1,0:T(8,128)S(1)}, f32[16,768]{1,0:T(8,128)S(1)}, u32[]{:S(2)}, u32[]{:S(2)}) collective-permute-start(f32[16,768]{1,0:T(8,128)S(1)} %get-tuple-element.45), channel_id=1, source_target_pairs={{0,1},{1,0},{2,3},{3,2},{4,5},{5,4},{6,7},{7,6},{8,9},{9,8},{10,11... | collective-permute-start | bytes 147464 | tf_op jit(solution)/shard_map/ppermute | solution.py:504

commit v21 on v19

--- a/solution.py
+++ b/solution.py
@@ -10,7 +10,8 @@
 EPSILON = 1e-05
 LANES = 128
 INNER = 4
-FINE = 16
+ROWS = 16
+FINE = 32
 MIB = 1024 * 1024
 
 BF16 = jnp.bfloat16
@@ -48,7 +49,7 @@
 
 
 def place_of(real, part):
-    base = real // FINE * FINE
+    base = real // ROWS * ROWS
     return base, real - base
 
 

time: 38.8 us -> 41.2 us (1.062)
  Pallas kernels: 9.22 us -> 11.7 us
    pallas_call x1, Pallas kernels: 2.41 us -> 3.7 us  [on_device(): call(last_dots_kernel, [VMEM] * 4 + [AFTER], sds((half, count, slab + win...]
    pallas_call x1, Pallas kernels: 1.52 us -> 2.18 us  [on_device(): call(functools.partial(first_dots_kernel, outer_count, stations, channels...]
    pallas_call x1, Pallas kernels: 1.88 us -> 2.36 us  [on_device(): call(middle_dots_kernel, [VMEM] * 5, [sds((half, count, slab + window), F...]
  transfers between devices with their start and end apart: 15 -> 15, of which waited for: 8 -> 8; matrix products, arithmetic and copies ran while one was open for 0% -> 0% of each run, Pallas kernels for 13% -> 17%
where the time goes in v21:
time: 41.2 us; the launch traced here: 41 us
  starting transfers between devices  20.3 us (49%)
  Pallas kernels  11.7 us (28%)
  waiting for transfers between devices  8.92 us (22%)
    ppermute x6, starting transfers between devices, swap(): return lax.ppermute(part, every, route)  8.27 us
    ppermute x4, starting transfers between devices, cross(): return lax.ppermute(part, 'outer', route)  7.48 us
    ppermute x4, waiting for transfers between devices, cross(): return lax.ppermute(part, 'outer', route)  4.57 us
    pallas_call x1, Pallas kernels, on_device(): call(last_dots_kernel, [VMEM] * 4 + [AFTER], sds((half, count, slab + win...  3.7 us
    ppermute x3, starting transfers between devices, plane(): return lax.ppermute(part, 'inner', [(b, b ^ flip) for b in range(INNER)])  3.18 us
    ppermute x6, waiting for transfers between devices, swap(): return lax.ppermute(part, every, route)  2.91 us
    pallas_call x1, Pallas kernels, on_device(): call(middle_dots_kernel, [VMEM] * 5, [sds((half, count, slab + window), F...  2.36 us
    pallas_call x1, Pallas kernels, on_device(): call(functools.partial(first_dots_kernel, outer_count, stations, channels...  2.18 us
  transfers between devices with their start and end apart: 15, of which 8 were waited for; matrix products, arithmetic and copies ran while one was open for 0% of the time, Pallas kernels for 17%

profile of v21, /device:TPU:0, one launch (start us, length us, event | category | flops | bytes accessed | tf_op | source)
XLA Modules:
  0.0 41.0 jit_solution(2720464957130088757)
XLA Ops:
  0.0 1.7 %shard_map.46 = (bf16[1152,128]{1,0:T(8,128)(2,1)S(1)}, bf16[256,512]{1,0:T(8,128)(2,1)S(1)}, bf16[128,128]{1,0:T(8,128)(2,1)S(1)}, bf16[128,128]{1,0:T(8,128)(2,1)S(1)}, bf16[128,128]{1,0:T(8,128)(2,1)S(1)}) custom-call(bf16[480,512]{1,0:T(8,128)(2,1)} %wave_ref.1, bf16[1,480,256]{2,1,0:T(8,128)(2,1)} %tpl_hbm.1, s32[1,160]{1,0:T(1,128)} %flag_hbm.1, ...), custom_call_target="tpu_custom_call" | custom-call | bytes 737280 | tf_op jit(solution)/shard_map/pallas_call | solution.py:450
  1.7 0.5 %collective-permute-start = (bf16[1152,128]{1,0:T(8,128)(2,1)S(1)}, bf16[1152,128]{1,0:T(8,128)(2,1)S(1)}, u32[]{:S(2)}, u32[]{:S(2)}) collective-permute-start(bf16[1152,128]{1,0:T(8,128)(2,1)S(1)} %get-tuple-element.28), channel_id=1, source_target_pairs={{0,2},{2,0},{4,6},{6,4},{1,3},{3,1},{5,7},{7,5},{8,10},{10,8},{12,... | collective-permute-start | bytes 884744 | tf_op jit(solution)/shard_map/ppermute | solution.py:472
  2.2 2.6 %collective-permute-start.1 = (bf16[128,128]{1,0:T(8,128)(2,1)S(1)}, bf16[128,128]{1,0:T(8,128)(2,1)S(1)}, u32[]{:S(2)}, u32[]{:S(2)}) collective-permute-start(bf16[128,128]{1,0:T(8,128)(2,1)S(1)} %get-tuple-element.29), channel_id=1, source_target_pairs={{0,4},{2,6},{4,0},{6,2},{1,5},{3,7},{5,1},{7,3},{8,12},{10,14},{12... | collective-permute-start | bytes 98312 | tf_op jit(solution)/shard_map/ppermute | solution.py:472
  5.0 1.8 %collective-permute-start.7 = (bf16[2,64,512]{2,1,0:T(8,128)(2,1)S(1)}, bf16[2,64,512]{2,1,0:T(8,128)(2,1)S(1)}, u32[]{:S(2)}, u32[]{:S(2)}) collective-permute-start(bf16[2,64,512]{2,1,0:T(8,128)(2,1)S(1)} %get-tuple-element.33), channel_id=1, source_target_pairs={{0,1},{1,0},{2,3},{3,2},{4,5},{5,4},{6,7},{7,6},{8,9},{9,8},{10,11... | collective-permute-start | bytes 393224 | tf_op jit(solution)/shard_map/ppermute | solution.py:500
  6.8 1.4 %collective-permute-done.2.both_ref = bf16[128,128]{1,0:T(8,128)(2,1)S(1)} collective-permute-done((bf16[128,128]{1,0:T(8,128)(2,1)S(1)}, bf16[128,128]{1,0:T(8,128)(2,1)S(1)}, u32[]{:S(2)}, u32[]{:S(2)}) %collective-permute-start.2) | collective-permute-done | bytes 32800 | tf_op jit(solution)/shard_map/ppermute | solution.py:472
  8.2 2.7 %collective-permute-start.4 = (bf16[4,128,128]{2,1,0:T(8,128)(2,1)S(1)}, bf16[4,128,128]{2,1,0:T(8,128)(2,1)S(1)}, u32[]{:S(2)}, u32[]{:S(2)}) collective-permute-start(bf16[4,128,128]{2,1,0:T(8,128)(2,1)S(1)} %shard_map.47.refs_0_), channel_id=1, source_target_pairs={{0,16},{16,0},{8,24},{24,8},{1,17},{17,1},{9,25},{25,9},{2,18},{18... | collective-permute-start | bytes 393224 | tf_op jit(solution)/shard_map/ppermute | solution.py:481
  10.8 0.9 %collective-permute-start.8 = (bf16[2,64,512]{2,1,0:T(8,128)(2,1)S(1)}, bf16[2,64,512]{2,1,0:T(8,128)(2,1)S(1)}, u32[]{:S(2)}, u32[]{:S(2)}) collective-permute-start(bf16[2,64,512]{2,1,0:T(8,128)(2,1)S(1)} %get-tuple-element.34), channel_id=1, source_target_pairs={{0,4},{1,5},{2,6},{3,7},{4,0},{5,1},{6,2},{7,3},{8,12},{9,13},{10,... | collective-permute-start | bytes 393224 | tf_op jit(solution)/shard_map/ppermute | solution.py:500
  11.7 2.1 %collective-permute-start.9 = (bf16[2,64,512]{2,1,0:T(8,128)(2,1)S(1)}, bf16[2,64,512]{2,1,0:T(8,128)(2,1)S(1)}, u32[]{:S(2)}, u32[]{:S(2)}) collective-permute-start(bf16[2,64,512]{2,1,0:T(8,128)(2,1)S(1)} %get-tuple-element.35), channel_id=1, source_target_pairs={{0,5},{1,4},{2,7},{3,6},{4,1},{5,0},{6,3},{7,2},{8,13},{9,12},{10,... | collective-permute-start | bytes 393224 | tf_op jit(solution)/shard_map/ppermute | solution.py:500
  13.8 0.7 %collective-permute-start.5 = (bf16[4,128,128]{2,1,0:T(8,128)(2,1)S(1)}, bf16[4,128,128]{2,1,0:T(8,128)(2,1)S(1)}, u32[]{:S(2)}, u32[]{:S(2)}) collective-permute-start(bf16[4,128,128]{2,1,0:T(8,128)(2,1)S(1)} %shard_map.47.refs_0_), channel_id=1, source_target_pairs={{8,16},{16,8},{9,17},{17,9},{10,18},{18,10},{11,19},{19,11},{12,20... | collective-permute-start | bytes 393224 | tf_op jit(solution)/shard_map/ppermute | solution.py:481
  14.5 2.9 %collective-permute-start.3 = (bf16[4,128,128]{2,1,0:T(8,128)(2,1)S(1)}, bf16[4,128,128]{2,1,0:T(8,128)(2,1)S(1)}, u32[]{:S(2)}, u32[]{:S(2)}) collective-permute-start(bf16[4,128,128]{2,1,0:T(8,128)(2,1)S(1)} %shard_map.47.refs_0_), channel_id=1, source_target_pairs={{0,8},{8,0},{16,24},{24,16},{1,9},{9,1},{17,25},{25,17},{2,10},{10... | collective-permute-start | bytes 393224 | tf_op jit(solution)/shard_map/ppermute | solution.py:481
  17.5 1.3 %collective-permute-start.6 = (bf16[4,128,128]{2,1,0:T(8,128)(2,1)S(1)}, bf16[4,128,128]{2,1,0:T(8,128)(2,1)S(1)}, u32[]{:S(2)}, u32[]{:S(2)}) collective-permute-start(bf16[4,128,128]{2,1,0:T(8,128)(2,1)S(1)} %collective-permute-done.4.refs_2_), channel_id=1, source_target_pairs={{8,0},{16,24},{9,1},{17,25},{10,2},{18,26},{11,3},{19,27},{12,4},{... | collective-permute-start | bytes 393224 | tf_op jit(solution)/shard_map/ppermute | solution.py:481
  19.0 1.3 %collective-permute-start.10 = (bf16[64,256]{1,0:T(8,128)(2,1)S(1)}, bf16[64,256]{1,0:T(8,128)(2,1)S(1)}, u32[]{:S(2)}, u32[]{:S(2)}) collective-permute-start(bf16[64,256]{1,0:T(8,128)(2,1)S(1)} %get-tuple-element.38), channel_id=1, source_target_pairs={{8,0},{16,8},{24,16},{9,1},{17,9},{25,17},{10,2},{18,10},{26,18},{... | collective-permute-start | bytes 98312 | tf_op jit(solution)/shard_map/ppermute | solution.py:515
  20.3 4.4 %collective-permute-done.6.refs_4_ = bf16[4,128,128]{2,1,0:T(8,128)(2,1)S(1)} collective-permute-done((bf16[4,128,128]{2,1,0:T(8,128)(2,1)S(1)}, bf16[4,128,128]{2,1,0:T(8,128)(2,1)S(1)}, u32[]{:S(2)}, u32[]{:S(2)}) %collective-permute-start.6) | collective-permute-done | bytes 131104 | tf_op jit(solution)/shard_map/ppermute | solution.py:481
  24.7 2.2 %shard_map.50 = (f32[2,16,512]{2,1,0:T(8,128)S(1)}, bf16[512,512]{1,0:T(8,128)(2,1)S(1)}, f32[16,128]{1,0:T(8,128)S(1)}, bf16[16,480]{1,0:T(8,128)(2,1)S(1)}, bf16[16,64]{1,0:T(8,128)(2,1)S(1)}) custom-call(bf16[4,128,128]{2,1,0:T(8,128)(2,1)S(1)} %shard_map.47.refs_0_, bf16[4,128,128]{2,1,0:T(8,128)(2,1)S(1)} %collective-permute-done.3.refs_1_, ...), custom_call_target="tpu_custom_call" | custom-call | flops 536870912 | bytes 524288 | tf_op jit(solution)/shard_map/pallas_call | solution.py:527
  26.9 2.4 %shard_map.51 = (f32[4,16,768]{2,1,0:T(8,128)S(1)}, f32[4,16,256]{2,1,0:T(8,128)S(1)}) custom-call(bf16[512,512]{1,0:T(8,128)(2,1)S(1)} %get-tuple-element.37.left, bf16[64,4096]{1,0:T(8,128)(2,1)S(1)} %get-tuple-element.36.refs_6_.samples_ref, bf16[64,256]{1,0:T(8,128)(2,1)S(1)} %collective-permute-done.10.halo_ref, ...), custom_call_target="tpu_custom_call" | custom-call | flops 536870912 | bytes 524288 | tf_op jit(solution)/shard_map/pallas_call | solution.py:543
  29.4 3.7 %shard_map.52.keep_ref.after = f32[4,16,768]{2,1,0:T(8,128)S(1)} custom-call(bf16[512,512]{1,0:T(8,128)(2,1)S(1)} %get-tuple-element.37.left, bf16[64,4096]{1,0:T(8,128)(2,1)S(1)} %get-tuple-element.36.refs_6_.samples_ref, bf16[64,256]{1,0:T(8,128)(2,1)S(1)} %collective-permute-done.10.halo_ref, f32[4,16,256]{2,1,0:T(8,128)S(1)} %get-tuple-element.41.edges_ref, ...), custom_call_target="tpu_custom_call" | custom-call | flops 1073741824 | bytes 524288 | tf_op jit(solution)/shard_map/pallas_call | solution.py:552
  33.1 2.0 %collective-permute-start.12 = (f32[16,768]{1,0:T(8,128)S(1)}, f32[16,768]{1,0:T(8,128)S(1)}, u32[]{:S(2)}, u32[]{:S(2)}) collective-permute-start(f32[16,768]{1,0:T(8,128)S(1)} %get-tuple-element.44), channel_id=1, source_target_pairs={{0,5},{1,4},{2,7},{3,6},{4,1},{5,0},{6,3},{7,2},{8,13},{9,12},{10,... | collective-permute-start | bytes 147464 | tf_op jit(solution)/shard_map/ppermute | solution.py:500
  35.1 1.1 %collective-permute-start.13 = (f32[16,768]{1,0:T(8,128)S(1)}, f32[16,768]{1,0:T(8,128)S(1)}, u32[]{:S(2)}, u32[]{:S(2)}) collective-permute-start(f32[16,768]{1,0:T(8,128)S(1)} %get-tuple-element.45), channel_id=1, source_target_pairs={{0,4},{1,5},{2,6},{3,7},{4,0},{5,1},{6,2},{7,3},{8,12},{9,13},{10,... | collective-permute-start | bytes 147464 | tf_op jit(solution)/shard_map/ppermute | solution.py:500
  36.3 0.4 %collective-permute-start.14 = (f32[16,768]{1,0:T(8,128)S(1)}, f32[16,768]{1,0:T(8,128)S(1)}, u32[]{:S(2)}, u32[]{:S(2)}) collective-permute-start(f32[16,768]{1,0:T(8,128)S(1)} %get-tuple-element.46), channel_id=1, source_target_pairs={{0,1},{1,0},{2,3},{3,2},{4,5},{5,4},{6,7},{7,6},{8,9},{9,8},{10,11... | collective-permute-start | bytes 147464 | tf_op jit(solution)/shard_map/ppermute | solution.py:500
  36.7 0.9 %shard_map.54.refs_4_ = f32[16,512]{1,0:T(8,128)S(1)} custom-call(bf16[480,512]{1,0:T(8,128)(2,1)S(1)} %copy-done, bf16[16,480]{1,0:T(8,128)(2,1)S(1)} %get-tuple-element.47.mask_ref, f32[4,16,768]{2,1,0:T(8,128)S(1)} %shard_map.52.keep_ref.after), custom_call_target="tpu_custom_call" | custom-call | flops 15728640 | bytes 491520 | tf_op jit(solution)/shard_map/pallas_call | solution.py:562
  37.6 0.7 %collective-permute-done.12.refs_1_ = f32[16,768]{1,0:T(8,128)S(1)} collective-permute-done((f32[16,768]{1,0:T(8,128)S(1)}, f32[16,768]{1,0:T(8,128)S(1)}, u32[]{:S(2)}, u32[]{:S(2)}) %collective-permute-start.12) | collective-permute-done | bytes 49184 | tf_op jit(solution)/shard_map/ppermute | solution.py:500
  38.3 1.0 %collective-permute-done.13.refs_2_ = f32[16,768]{1,0:T(8,128)S(1)} collective-permute-done((f32[16,768]{1,0:T(8,128)S(1)}, f32[16,768]{1,0:T(8,128)S(1)}, u32[]{:S(2)}, u32[]{:S(2)}) %collective-permute-start.13) | collective-permute-done | bytes 49184 | tf_op jit(solution)/shard_map/ppermute | solution.py:500
  39.3 1.1 %collective-permute-done.14.refs_3_ = f32[16,768]{1,0:T(8,128)S(1)} collective-permute-done((f32[16,768]{1,0:T(8,128)S(1)}, f32[16,768]{1,0:T(8,128)S(1)}, u32[]{:S(2)}, u32[]{:S(2)}) %collective-permute-start.14) | collective-permute-done | bytes 49184 | tf_op jit(solution)/shard_map/ppermute | solution.py:500
  40.3 0.7 %shard_map.55 = f32[16,512]{1,0:T(8,128)} custom-call(f32[16,768]{1,0:T(8,128)S(1)} %get-tuple-element.43.refs_0_, f32[16,768]{1,0:T(8,128)S(1)} %collective-permute-done.12.refs_1_, f32[16,768]{1,0:T(8,128)S(1)} %collective-permute-done.13.refs_2_, f32[16,768]{1,0:T(8,128)S(1)} %collective-permute-done.14.refs_3_, f32[16,512]{1,0:T(8,128)S(1)} %shard_map.54.refs_4_, ...), custom_call_target="tpu_custom_call" | custom-call | bytes 196608 | tf_op jit(solution)/shard_map/pallas_call | solution.py:576
  (20 shorter events, 0.7 us)
Async XLA Ops:
  1.7 3.2 %collective-permute-start = (bf16[1152,128]{1,0:T(8,128)(2,1)S(1)}, bf16[1152,128]{1,0:T(8,128)(2,1)S(1)}, u32[]{:S(2)}, u32[]{:S(2)}) collective-permute-start(bf16[1152,128]{1,0:T(8,128)(2,1)S(1)} %get-tuple-element.28), channel_id=1, source_target_pairs={{0,2},{2,0},{4,6},{6,4},{1,3},{3,1},{5,7},{7,5},{8,10},{10,8},{12,... | collective-permute-start | bytes 884744 | tf_op jit(solution)/shard_map/ppermute | solution.py:472
  2.2 4.6 %collective-permute-start.1 = (bf16[128,128]{1,0:T(8,128)(2,1)S(1)}, bf16[128,128]{1,0:T(8,128)(2,1)S(1)}, u32[]{:S(2)}, u32[]{:S(2)}) collective-permute-start(bf16[128,128]{1,0:T(8,128)(2,1)S(1)} %get-tuple-element.29), channel_id=1, source_target_pairs={{0,4},{2,6},{4,0},{6,2},{1,5},{3,7},{5,1},{7,3},{8,12},{10,14},{12... | collective-permute-start | bytes 98312 | tf_op jit(solution)/shard_map/ppermute | solution.py:472
  4.8 3.3 %collective-permute-start.2 = (bf16[128,128]{1,0:T(8,128)(2,1)S(1)}, bf16[128,128]{1,0:T(8,128)(2,1)S(1)}, u32[]{:S(2)}, u32[]{:S(2)}) collective-permute-start(bf16[128,128]{1,0:T(8,128)(2,1)S(1)} %get-tuple-element.30), channel_id=1, source_target_pairs={{0,6},{2,4},{4,2},{6,0},{1,7},{3,5},{5,3},{7,1},{8,14},{10,12},{12... | collective-permute-start | bytes 98312 | tf_op jit(solution)/shard_map/ppermute | solution.py:472
  5.0 9.5 %collective-permute-start.7 = (bf16[2,64,512]{2,1,0:T(8,128)(2,1)S(1)}, bf16[2,64,512]{2,1,0:T(8,128)(2,1)S(1)}, u32[]{:S(2)}, u32[]{:S(2)}) collective-permute-start(bf16[2,64,512]{2,1,0:T(8,128)(2,1)S(1)} %get-tuple-element.33), channel_id=1, source_target_pairs={{0,1},{1,0},{2,3},{3,2},{4,5},{5,4},{6,7},{7,6},{8,9},{9,8},{10,11... | collective-permute-start | bytes 393224 | tf_op jit(solution)/shard_map/ppermute | solution.py:500
  8.2 9.3 %collective-permute-start.4 = (bf16[4,128,128]{2,1,0:T(8,128)(2,1)S(1)}, bf16[4,128,128]{2,1,0:T(8,128)(2,1)S(1)}, u32[]{:S(2)}, u32[]{:S(2)}) collective-permute-start(bf16[4,128,128]{2,1,0:T(8,128)(2,1)S(1)} %shard_map.47.refs_0_), channel_id=1, source_target_pairs={{0,16},{16,0},{8,24},{24,8},{1,17},{17,1},{9,25},{25,9},{2,18},{18... | collective-permute-start | bytes 393224 | tf_op jit(solution)/shard_map/ppermute | solution.py:481
  10.8 8.1 %collective-permute-start.8 = (bf16[2,64,512]{2,1,0:T(8,128)(2,1)S(1)}, bf16[2,64,512]{2,1,0:T(8,128)(2,1)S(1)}, u32[]{:S(2)}, u32[]{:S(2)}) collective-permute-start(bf16[2,64,512]{2,1,0:T(8,128)(2,1)S(1)} %get-tuple-element.34), channel_id=1, source_target_pairs={{0,4},{1,5},{2,6},{3,7},{4,0},{5,1},{6,2},{7,3},{8,12},{9,13},{10,... | collective-permute-start | bytes 393224 | tf_op jit(solution)/shard_map/ppermute | solution.py:500
  11.7 7.2 %collective-permute-start.9 = (bf16[2,64,512]{2,1,0:T(8,128)(2,1)S(1)}, bf16[2,64,512]{2,1,0:T(8,128)(2,1)S(1)}, u32[]{:S(2)}, u32[]{:S(2)}) collective-permute-start(bf16[2,64,512]{2,1,0:T(8,128)(2,1)S(1)} %get-tuple-element.35), channel_id=1, source_target_pairs={{0,5},{1,4},{2,7},{3,6},{4,1},{5,0},{6,3},{7,2},{8,13},{9,12},{10,... | collective-permute-start | bytes 393224 | tf_op jit(solution)/shard_map/ppermute | solution.py:500
  13.8 6.5 %collective-permute-start.5 = (bf16[4,128,128]{2,1,0:T(8,128)(2,1)S(1)}, bf16[4,128,128]{2,1,0:T(8,128)(2,1)S(1)}, u32[]{:S(2)}, u32[]{:S(2)}) collective-permute-start(bf16[4,128,128]{2,1,0:T(8,128)(2,1)S(1)} %shard_map.47.refs_0_), channel_id=1, source_target_pairs={{8,16},{16,8},{9,17},{17,9},{10,18},{18,10},{11,19},{19,11},{12,20... | collective-permute-start | bytes 393224 | tf_op jit(solution)/shard_map/ppermute | solution.py:481
  14.5 5.9 %collective-permute-start.3 = (bf16[4,128,128]{2,1,0:T(8,128)(2,1)S(1)}, bf16[4,128,128]{2,1,0:T(8,128)(2,1)S(1)}, u32[]{:S(2)}, u32[]{:S(2)}) collective-permute-start(bf16[4,128,128]{2,1,0:T(8,128)(2,1)S(1)} %shard_map.47.refs_0_), channel_id=1, source_target_pairs={{0,8},{8,0},{16,24},{24,16},{1,9},{9,1},{17,25},{25,17},{2,10},{10... | collective-permute-start | bytes 393224 | tf_op jit(solution)/shard_map/ppermute | solution.py:481
  17.5 7.2 %collective-permute-start.6 = (bf16[4,128,128]{2,1,0:T(8,128)(2,1)S(1)}, bf16[4,128,128]{2,1,0:T(8,128)(2,1)S(1)}, u32[]{:S(2)}, u32[]{:S(2)}) collective-permute-start(bf16[4,128,128]{2,1,0:T(8,128)(2,1)S(1)} %collective-permute-done.4.refs_2_), channel_id=1, source_target_pairs={{8,0},{16,24},{9,1},{17,25},{10,2},{18,26},{11,3},{19,27},{12,4},{... | collective-permute-start | bytes 393224 | tf_op jit(solution)/shard_map/ppermute | solution.py:481
  19.0 5.7 %copy-start.1 = (s32[480]{0:T(512)S(1)}, s32[480]{0:T(512)}, u32[]{:S(2)}) copy-start(s32[480]{0:T(512)} %param.7) | copy-start | bytes 5764
  19.0 7.9 %collective-permute-start.10 = (bf16[64,256]{1,0:T(8,128)(2,1)S(1)}, bf16[64,256]{1,0:T(8,128)(2,1)S(1)}, u32[]{:S(2)}, u32[]{:S(2)}) collective-permute-start(bf16[64,256]{1,0:T(8,128)(2,1)S(1)} %get-tuple-element.38), channel_id=1, source_target_pairs={{8,0},{16,8},{24,16},{9,1},{17,9},{25,17},{10,2},{18,10},{26,18},{... | collective-permute-start | bytes 98312 | tf_op jit(solution)/shard_map/ppermute | solution.py:515
  29.3 3.8 %collective-permute-start.11 = (f32[4,16,768]{2,1,0:T(8,128)S(1)}, f32[4,16,768]{2,1,0:T(8,128)S(1)}, u32[]{:S(2)}, u32[]{:S(2)}) collective-permute-start(f32[4,16,768]{2,1,0:T(8,128)S(1)} %get-tuple-element.42.after), channel_id=1, source_target_pairs={{0,2},{2,0},{4,6},{6,4},{1,3},{3,1},{5,7},{7,5},{8,10},{10,8},{12,... | collective-permute-start | bytes 589832 | tf_op jit(solution)/shard_map/ppermute | solution.py:561
  29.4 7.3 %copy-start = (bf16[480,512]{1,0:T(8,128)(2,1)S(1)}, bf16[480,512]{1,0:T(8,128)(2,1)}, u32[]{:S(2)}) copy-start(bf16[480,512]{1,0:T(8,128)(2,1)} %wave_ref.1) | copy-start | bytes 1474564
  33.1 5.1 %collective-permute-start.12 = (f32[16,768]{1,0:T(8,128)S(1)}, f32[16,768]{1,0:T(8,128)S(1)}, u32[]{:S(2)}, u32[]{:S(2)}) collective-permute-start(f32[16,768]{1,0:T(8,128)S(1)} %get-tuple-element.44), channel_id=1, source_target_pairs={{0,5},{1,4},{2,7},{3,6},{4,1},{5,0},{6,3},{7,2},{8,13},{9,12},{10,... | collective-permute-start | bytes 147464 | tf_op jit(solution)/shard_map/ppermute | solution.py:500
  35.1 4.2 %collective-permute-start.13 = (f32[16,768]{1,0:T(8,128)S(1)}, f32[16,768]{1,0:T(8,128)S(1)}, u32[]{:S(2)}, u32[]{:S(2)}) collective-permute-start(f32[16,768]{1,0:T(8,128)S(1)} %get-tuple-element.45), channel_id=1, source_target_pairs={{0,4},{1,5},{2,6},{3,7},{4,0},{5,1},{6,2},{7,3},{8,12},{9,13},{10,... | collective-permute-start | bytes 147464 | tf_op jit(solution)/shard_map/ppermute | solution.py:500
  36.3 4.1 %collective-permute-start.14 = (f32[16,768]{1,0:T(8,128)S(1)}, f32[16,768]{1,0:T(8,128)S(1)}, u32[]{:S(2)}, u32[]{:S(2)}) collective-permute-start(f32[16,768]{1,0:T(8,128)S(1)} %get-tuple-element.46), channel_id=1, source_target_pairs={{0,1},{1,0},{2,3},{3,2},{4,5},{5,4},{6,7},{7,6},{8,9},{9,8},{10,11... | collective-permute-start | bytes 147464 | tf_op jit(solution)/shard_map/ppermute | solution.py:500

commit v22 on v19

--- a/solution.py
+++ b/solution.py
@@ -278,7 +278,7 @@
     begun_ref, left, scale_ref, mask_ref, part_ref, shifts, products = refs[-7:]
     tpls = [pack[...] for pack in tpls]
     if len(tpls) > outer_count:
-        tpls = tpls[:-2] + [tpls[-2] + tpls[-1]]
+        tpls = tpls[:2] + [tpls[2] + tpls[3], tpls[4] + tpls[5]]
     arrange(tpls, left)
     core = lax.rem(lax.axis_index("inner"), 2)
     run, _, slab = begun_ref.shape
@@ -481,10 +481,11 @@
 
     if outer_count == 4:
         near = cross(pack, [(0, 1), (1, 0), (2, 3), (3, 2)])
-        far = cross(pack, [(0, 2), (2, 0), (1, 3), (3, 1)])
         middle = cross(pack, [(1, 2), (2, 1)])
-        ends = cross(far, [(1, 0), (2, 3)])
-        tpls = [pack, near, far, middle, ends]
+        inward = cross(near, [(1, 2), (2, 1)])
+        outward = cross(middle, [(1, 0), (2, 3)])
+        ends = cross(inward, [(1, 0), (2, 3)])
+        tpls = [pack, near, inward, outward, middle, ends]
     else:
         tpls = [pack] + [
             cross(pack, [(b, b ^ flip) for b in range(outer_count)])

time: 38.8 us -> 43.1 us (1.11)
  waiting for transfers between devices: 8.93 us -> 16.3 us
  starting transfers between devices: 20.3 us -> 17.2 us
    ppermute x4 -> x5, waiting for transfers between devices: 4.57 us -> 6.75 us  [cross(): return lax.ppermute(part, 'outer', route)]
    ppermute x4 -> x5, starting transfers between devices: 7.48 us -> 5.53 us  [cross(): return lax.ppermute(part, 'outer', route)]
    ppermute x3, waiting for transfers between devices: 1.44 us -> 3.28 us  [plane(): return lax.ppermute(part, 'inner', [(b, b ^ flip) for b in range(INNER)])]
    ppermute x1, waiting for transfers between devices: 0.01 us -> 1.77 us  [on_device(): lax.ppermute(head, 'outer', [(b, b - 1) for b in range(1, outer_count)])]
    ppermute x6, waiting for transfers between devices: 2.92 us -> 4.51 us  [swap(): return lax.ppermute(part, every, route)]
    ppermute x6, starting transfers between devices: 8.27 us -> 7.11 us  [swap(): return lax.ppermute(part, every, route)]
  transfers between devices with their start and end apart: 15 -> 16, of which waited for: 8 -> 10; matrix products, arithmetic and copies ran while one was open for 0% -> 0% of each run, Pallas kernels for 13% -> 11%
where the time goes in v22:
time: 43.1 us; the launch traced here: 42.9 us
  starting transfers between devices  17.2 us (40%)
  waiting for transfers between devices  16.3 us (38%)
  Pallas kernels  9.23 us (21%)
    ppermute x6, starting transfers between devices, swap(): return lax.ppermute(part, every, route)  7.11 us
    ppermute x5, waiting for transfers between devices, cross(): return lax.ppermute(part, 'outer', route)  6.75 us
    ppermute x5, starting transfers between devices, cross(): return lax.ppermute(part, 'outer', route)  5.53 us
    ppermute x6, waiting for transfers between devices, swap(): return lax.ppermute(part, every, route)  4.51 us
    ppermute x3, waiting for transfers between devices, plane(): return lax.ppermute(part, 'inner', [(b, b ^ flip) for b in range(INNER)])  3.28 us
    ppermute x3, starting transfers between devices, plane(): return lax.ppermute(part, 'inner', [(b, b ^ flip) for b in range(INNER)])  3.18 us
    pallas_call x1, Pallas kernels, on_device(): call(last_dots_kernel, [VMEM] * 4 + [AFTER], sds((half, count, slab + win...  2.4 us
    pallas_call x1, Pallas kernels, on_device(): call(middle_dots_kernel, [VMEM] * 5, [sds((half, count, slab + window), F...  1.88 us
  transfers between devices with their start and end apart: 16, of which 10 were waited for; matrix products, arithmetic and copies ran while one was open for 0% of the time, Pallas kernels for 11%

profile of v22, /device:TPU:0, one launch (start us, length us, event | category | flops | bytes accessed | tf_op | source)
XLA Modules:
  0.0 42.9 jit_solution(18267733641219286711)
XLA Ops:
  0.0 1.7 %shard_map.46 = (bf16[1152,128]{1,0:T(8,128)(2,1)S(1)}, bf16[256,512]{1,0:T(8,128)(2,1)S(1)}, bf16[128,128]{1,0:T(8,128)(2,1)S(1)}, bf16[128,128]{1,0:T(8,128)(2,1)S(1)}, bf16[128,128]{1,0:T(8,128)(2,1)S(1)}) custom-call(bf16[480,512]{1,0:T(8,128)(2,1)} %wave_ref.1, bf16[1,480,256]{2,1,0:T(8,128)(2,1)} %tpl_hbm.1, s32[1,160]{1,0:T(1,128)} %flag_hbm.1, ...), custom_call_target="tpu_custom_call" | custom-call | bytes 737280 | tf_op jit(solution)/shard_map/pallas_call | solution.py:449
  2.2 2.6 %collective-permute-start.1 = (bf16[128,128]{1,0:T(8,128)(2,1)S(1)}, bf16[128,128]{1,0:T(8,128)(2,1)S(1)}, u32[]{:S(2)}, u32[]{:S(2)}) collective-permute-start(bf16[128,128]{1,0:T(8,128)(2,1)S(1)} %get-tuple-element.29), channel_id=1, source_target_pairs={{0,4},{2,6},{4,0},{6,2},{1,5},{3,7},{5,1},{7,3},{8,12},{10,14},{12... | collective-permute-start | bytes 98312 | tf_op jit(solution)/shard_map/ppermute | solution.py:471
  4.9 1.9 %collective-permute-done.1.y_ref = bf16[128,128]{1,0:T(8,128)(2,1)S(1)} collective-permute-done((bf16[128,128]{1,0:T(8,128)(2,1)S(1)}, bf16[128,128]{1,0:T(8,128)(2,1)S(1)}, u32[]{:S(2)}, u32[]{:S(2)}) %collective-permute-start.1) | collective-permute-done | bytes 32800 | tf_op jit(solution)/shard_map/ppermute | solution.py:471
  6.8 1.4 %collective-permute-done.2.both_ref = bf16[128,128]{1,0:T(8,128)(2,1)S(1)} collective-permute-done((bf16[128,128]{1,0:T(8,128)(2,1)S(1)}, bf16[128,128]{1,0:T(8,128)(2,1)S(1)}, u32[]{:S(2)}, u32[]{:S(2)}) %collective-permute-start.2) | collective-permute-done | bytes 32800 | tf_op jit(solution)/shard_map/ppermute | solution.py:471
  8.2 1.6 %collective-permute-start.3 = (bf16[4,128,128]{2,1,0:T(8,128)(2,1)S(1)}, bf16[4,128,128]{2,1,0:T(8,128)(2,1)S(1)}, u32[]{:S(2)}, u32[]{:S(2)}) collective-permute-start(bf16[4,128,128]{2,1,0:T(8,128)(2,1)S(1)} %shard_map.47.refs_0_), channel_id=1, source_target_pairs={{0,8},{8,0},{16,24},{24,16},{1,9},{9,1},{17,25},{25,17},{2,10},{10... | collective-permute-start | bytes 393224 | tf_op jit(solution)/shard_map/ppermute | solution.py:480
  10.5 3.3 %collective-permute-done.3.refs_1_ = bf16[4,128,128]{2,1,0:T(8,128)(2,1)S(1)} collective-permute-done((bf16[4,128,128]{2,1,0:T(8,128)(2,1)S(1)}, bf16[4,128,128]{2,1,0:T(8,128)(2,1)S(1)}, u32[]{:S(2)}, u32[]{:S(2)}) %collective-permute-start.3) | collective-permute-done | bytes 131104 | tf_op jit(solution)/shard_map/ppermute | solution.py:480
  14.6 1.6 %collective-permute-start.8 = (bf16[2,64,512]{2,1,0:T(8,128)(2,1)S(1)}, bf16[2,64,512]{2,1,0:T(8,128)(2,1)S(1)}, u32[]{:S(2)}, u32[]{:S(2)}) collective-permute-start(bf16[2,64,512]{2,1,0:T(8,128)(2,1)S(1)} %get-tuple-element.33), channel_id=1, source_target_pairs={{0,1},{1,0},{2,3},{3,2},{4,5},{5,4},{6,7},{7,6},{8,9},{9,8},{10,11... | collective-permute-start | bytes 393224 | tf_op jit(solution)/shard_map/ppermute | solution.py:500
  16.1 0.9 %collective-permute-start.9 = (bf16[2,64,512]{2,1,0:T(8,128)(2,1)S(1)}, bf16[2,64,512]{2,1,0:T(8,128)(2,1)S(1)}, u32[]{:S(2)}, u32[]{:S(2)}) collective-permute-start(bf16[2,64,512]{2,1,0:T(8,128)(2,1)S(1)} %get-tuple-element.34), channel_id=1, source_target_pairs={{0,4},{1,5},{2,6},{3,7},{4,0},{5,1},{6,2},{7,3},{8,12},{9,13},{10,... | collective-permute-start | bytes 393224 | tf_op jit(solution)/shard_map/ppermute | solution.py:500
  17.0 1.1 %collective-permute-start.10 = (bf16[2,64,512]{2,1,0:T(8,128)(2,1)S(1)}, bf16[2,64,512]{2,1,0:T(8,128)(2,1)S(1)}, u32[]{:S(2)}, u32[]{:S(2)}) collective-permute-start(bf16[2,64,512]{2,1,0:T(8,128)(2,1)S(1)} %get-tuple-element.35), channel_id=1, source_target_pairs={{0,5},{1,4},{2,7},{3,6},{4,1},{5,0},{6,3},{7,2},{8,13},{9,12},{10,... | collective-permute-start | bytes 393224 | tf_op jit(solution)/shard_map/ppermute | solution.py:500
  18.1 1.3 %collective-permute-start.6 = (bf16[4,128,128]{2,1,0:T(8,128)(2,1)S(1)}, bf16[4,128,128]{2,1,0:T(8,128)(2,1)S(1)}, u32[]{:S(2)}, u32[]{:S(2)}) collective-permute-start(bf16[4,128,128]{2,1,0:T(8,128)(2,1)S(1)} %collective-permute-done.5.refs_4_), channel_id=1, source_target_pairs={{8,0},{16,24},{9,1},{17,25},{10,2},{18,26},{11,3},{19,27},{12,4},{... | collective-permute-start | bytes 393224 | tf_op jit(solution)/shard_map/ppermute | solution.py:480
  19.4 1.3 %collective-permute-start.7 = (bf16[4,128,128]{2,1,0:T(8,128)(2,1)S(1)}, bf16[4,128,128]{2,1,0:T(8,128)(2,1)S(1)}, u32[]{:S(2)}, u32[]{:S(2)}) collective-permute-start(bf16[4,128,128]{2,1,0:T(8,128)(2,1)S(1)} %collective-permute-done.4.refs_2_), channel_id=1, source_target_pairs={{8,0},{16,24},{9,1},{17,25},{10,2},{18,26},{11,3},{19,27},{12,4},{... | collective-permute-start | bytes 393224 | tf_op jit(solution)/shard_map/ppermute | solution.py:480
  20.7 2.9 %collective-permute-done.9.refs_2_ = bf16[2,64,512]{2,1,0:T(8,128)(2,1)S(1)} collective-permute-done((bf16[2,64,512]{2,1,0:T(8,128)(2,1)S(1)}, bf16[2,64,512]{2,1,0:T(8,128)(2,1)S(1)}, u32[]{:S(2)}, u32[]{:S(2)}) %collective-permute-start.9) | collective-permute-done | bytes 131104 | tf_op jit(solution)/shard_map/ppermute | solution.py:500
  23.8 1.3 %collective-permute-start.11 = (bf16[64,256]{1,0:T(8,128)(2,1)S(1)}, bf16[64,256]{1,0:T(8,128)(2,1)S(1)}, u32[]{:S(2)}, u32[]{:S(2)}) collective-permute-start(bf16[64,256]{1,0:T(8,128)(2,1)S(1)} %get-tuple-element.38), channel_id=1, source_target_pairs={{8,0},{16,8},{24,16},{9,1},{17,9},{25,17},{10,2},{18,10},{26,18},{... | collective-permute-start | bytes 98312 | tf_op jit(solution)/shard_map/ppermute | solution.py:515
  25.1 2.0 %collective-permute-done.6.refs_3_ = bf16[4,128,128]{2,1,0:T(8,128)(2,1)S(1)} collective-permute-done((bf16[4,128,128]{2,1,0:T(8,128)(2,1)S(1)}, bf16[4,128,128]{2,1,0:T(8,128)(2,1)S(1)}, u32[]{:S(2)}, u32[]{:S(2)}) %collective-permute-start.6) | collective-permute-done | bytes 131104 | tf_op jit(solution)/shard_map/ppermute | solution.py:480
  27.1 1.4 %collective-permute-done.7.refs_5_ = bf16[4,128,128]{2,1,0:T(8,128)(2,1)S(1)} collective-permute-done((bf16[4,128,128]{2,1,0:T(8,128)(2,1)S(1)}, bf16[4,128,128]{2,1,0:T(8,128)(2,1)S(1)}, u32[]{:S(2)}, u32[]{:S(2)}) %collective-permute-start.7) | collective-permute-done | bytes 131104 | tf_op jit(solution)/shard_map/ppermute | solution.py:480
  28.5 1.5 %shard_map.50 = (f32[2,16,512]{2,1,0:T(8,128)S(1)}, bf16[256,1024]{1,0:T(8,128)(2,1)S(1)}, f32[16,128]{1,0:T(8,128)S(1)}, bf16[16,480]{1,0:T(8,128)(2,1)S(1)}, bf16[16,64]{1,0:T(8,128)(2,1)S(1)}) custom-call(bf16[4,128,128]{2,1,0:T(8,128)(2,1)S(1)} %shard_map.47.refs_0_, bf16[4,128,128]{2,1,0:T(8,128)(2,1)S(1)} %collective-permute-done.3.refs_1_, ...), custom_call_target="tpu_custom_call" | custom-call | flops 536870912 | bytes 524288 | tf_op jit(solution)/shard_map/pallas_call | solution.py:527
  30.0 1.8 %collective-permute-done.11.halo_ref = bf16[64,256]{1,0:T(8,128)(2,1)S(1)} collective-permute-done((bf16[64,256]{1,0:T(8,128)(2,1)S(1)}, bf16[64,256]{1,0:T(8,128)(2,1)S(1)}, u32[]{:S(2)}, u32[]{:S(2)}) %collective-permute-start.11) | collective-permute-done | bytes 32800 | tf_op jit(solution)/shard_map/ppermute | solution.py:515
  31.8 1.9 %shard_map.51 = (f32[4,16,768]{2,1,0:T(8,128)S(1)}, f32[4,16,256]{2,1,0:T(8,128)S(1)}) custom-call(bf16[256,1024]{1,0:T(8,128)(2,1)S(1)} %get-tuple-element.37.left, bf16[64,4096]{1,0:T(8,128)(2,1)S(1)} %get-tuple-element.36.refs_7_.samples_ref, bf16[64,256]{1,0:T(8,128)(2,1)S(1)} %collective-permute-done.11.halo_ref, ...), custom_call_target="tpu_custom_call" | custom-call | flops 536870912 | bytes 524288 | tf_op jit(solution)/shard_map/pallas_call | solution.py:543
  33.8 2.4 %shard_map.52.keep_ref.after = f32[4,16,768]{2,1,0:T(8,128)S(1)} custom-call(bf16[256,1024]{1,0:T(8,128)(2,1)S(1)} %get-tuple-element.37.left, bf16[64,4096]{1,0:T(8,128)(2,1)S(1)} %get-tuple-element.36.refs_7_.samples_ref, bf16[64,256]{1,0:T(8,128)(2,1)S(1)} %collective-permute-done.11.halo_ref, f32[4,16,256]{2,1,0:T(8,128)S(1)} %get-tuple-element.41.edges_ref, ...), custom_call_target="tpu_custom_call" | custom-call | flops 1073741824 | bytes 524288 | tf_op jit(solution)/shard_map/pallas_call | solution.py:552
  36.2 0.9 %collective-permute-start.13 = (f32[16,768]{1,0:T(8,128)S(1)}, f32[16,768]{1,0:T(8,128)S(1)}, u32[]{:S(2)}, u32[]{:S(2)}) collective-permute-start(f32[16,768]{1,0:T(8,128)S(1)} %get-tuple-element.44), channel_id=1, source_target_pairs={{0,5},{1,4},{2,7},{3,6},{4,1},{5,0},{6,3},{7,2},{8,13},{9,12},{10,... | collective-permute-start | bytes 147464 | tf_op jit(solution)/shard_map/ppermute | solution.py:500
  37.1 1.0 %collective-permute-start.14 = (f32[16,768]{1,0:T(8,128)S(1)}, f32[16,768]{1,0:T(8,128)S(1)}, u32[]{:S(2)}, u32[]{:S(2)}) collective-permute-start(f32[16,768]{1,0:T(8,128)S(1)} %get-tuple-element.45), channel_id=1, source_target_pairs={{0,4},{1,5},{2,6},{3,7},{4,0},{5,1},{6,2},{7,3},{8,12},{9,13},{10,... | collective-permute-start | bytes 147464 | tf_op jit(solution)/shard_map/ppermute | solution.py:500
  38.1 1.7 %collective-permute-start.15 = (f32[16,768]{1,0:T(8,128)S(1)}, f32[16,768]{1,0:T(8,128)S(1)}, u32[]{:S(2)}, u32[]{:S(2)}) collective-permute-start(f32[16,768]{1,0:T(8,128)S(1)} %get-tuple-element.46), channel_id=1, source_target_pairs={{0,1},{1,0},{2,3},{3,2},{4,5},{5,4},{6,7},{7,6},{8,9},{9,8},{10,11... | collective-permute-start | bytes 147464 | tf_op jit(solution)/shard_map/ppermute | solution.py:500
  39.8 0.9 %shard_map.54.refs_4_ = f32[16,512]{1,0:T(8,128)S(1)} custom-call(bf16[480,512]{1,0:T(8,128)(2,1)S(1)} %copy-done, bf16[16,480]{1,0:T(8,128)(2,1)S(1)} %get-tuple-element.47.mask_ref, f32[4,16,768]{2,1,0:T(8,128)S(1)} %shard_map.52.keep_ref.after), custom_call_target="tpu_custom_call" | custom-call | flops 15728640 | bytes 491520 | tf_op jit(solution)/shard_map/pallas_call | solution.py:562
  40.6 0.9 %collective-permute-done.13.refs_1_ = f32[16,768]{1,0:T(8,128)S(1)} collective-permute-done((f32[16,768]{1,0:T(8,128)S(1)}, f32[16,768]{1,0:T(8,128)S(1)}, u32[]{:S(2)}, u32[]{:S(2)}) %collective-permute-start.13) | collective-permute-done | bytes 49184 | tf_op jit(solution)/shard_map/ppermute | solution.py:500
  (22 shorter events, 3.5 us)
Async XLA Ops:
  1.7 6.5 %collective-permute-start = (bf16[1152,128]{1,0:T(8,128)(2,1)S(1)}, bf16[1152,128]{1,0:T(8,128)(2,1)S(1)}, u32[]{:S(2)}, u32[]{:S(2)}) collective-permute-start(bf16[1152,128]{1,0:T(8,128)(2,1)S(1)} %get-tuple-element.28), channel_id=1, source_target_pairs={{0,2},{2,0},{4,6},{6,4},{1,3},{3,1},{5,7},{7,5},{8,10},{10,8},{12,... | collective-permute-start | bytes 884744 | tf_op jit(solution)/shard_map/ppermute | solution.py:471
  2.2 4.6 %collective-permute-start.1 = (bf16[128,128]{1,0:T(8,128)(2,1)S(1)}, bf16[128,128]{1,0:T(8,128)(2,1)S(1)}, u32[]{:S(2)}, u32[]{:S(2)}) collective-permute-start(bf16[128,128]{1,0:T(8,128)(2,1)S(1)} %get-tuple-element.29), channel_id=1, source_target_pairs={{0,4},{2,6},{4,0},{6,2},{1,5},{3,7},{5,1},{7,3},{8,12},{10,14},{12... | collective-permute-start | bytes 98312 | tf_op jit(solution)/shard_map/ppermute | solution.py:471
  4.8 3.3 %collective-permute-start.2 = (bf16[128,128]{1,0:T(8,128)(2,1)S(1)}, bf16[128,128]{1,0:T(8,128)(2,1)S(1)}, u32[]{:S(2)}, u32[]{:S(2)}) collective-permute-start(bf16[128,128]{1,0:T(8,128)(2,1)S(1)} %get-tuple-element.30), channel_id=1, source_target_pairs={{0,6},{2,4},{4,2},{6,0},{1,7},{3,5},{5,3},{7,1},{8,14},{10,12},{12... | collective-permute-start | bytes 98312 | tf_op jit(solution)/shard_map/ppermute | solution.py:471
  8.2 5.6 %collective-permute-start.3 = (bf16[4,128,128]{2,1,0:T(8,128)(2,1)S(1)}, bf16[4,128,128]{2,1,0:T(8,128)(2,1)S(1)}, u32[]{:S(2)}, u32[]{:S(2)}) collective-permute-start(bf16[4,128,128]{2,1,0:T(8,128)(2,1)S(1)} %shard_map.47.refs_0_), channel_id=1, source_target_pairs={{0,8},{8,0},{16,24},{24,16},{1,9},{9,1},{17,25},{25,17},{2,10},{10... | collective-permute-start | bytes 393224 | tf_op jit(solution)/shard_map/ppermute | solution.py:480
  9.8 8.3 %collective-permute-start.5 = (bf16[4,128,128]{2,1,0:T(8,128)(2,1)S(1)}, bf16[4,128,128]{2,1,0:T(8,128)(2,1)S(1)}, u32[]{:S(2)}, u32[]{:S(2)}) collective-permute-start(bf16[4,128,128]{2,1,0:T(8,128)(2,1)S(1)} %shard_map.47.refs_0_), channel_id=1, source_target_pairs={{8,16},{16,8},{9,17},{17,9},{10,18},{18,10},{11,19},{19,11},{12,20... | collective-permute-start | bytes 393224 | tf_op jit(solution)/shard_map/ppermute | solution.py:480
  13.8 5.6 %collective-permute-start.4 = (bf16[4,128,128]{2,1,0:T(8,128)(2,1)S(1)}, bf16[4,128,128]{2,1,0:T(8,128)(2,1)S(1)}, u32[]{:S(2)}, u32[]{:S(2)}) collective-permute-start(bf16[4,128,128]{2,1,0:T(8,128)(2,1)S(1)} %collective-permute-done.3.refs_1_), channel_id=1, source_target_pairs={{8,16},{16,8},{9,17},{17,9},{10,18},{18,10},{11,19},{19,11},{12,20... | collective-permute-start | bytes 393224 | tf_op jit(solution)/shard_map/ppermute | solution.py:480
  14.6 6.2 %collective-permute-start.8 = (bf16[2,64,512]{2,1,0:T(8,128)(2,1)S(1)}, bf16[2,64,512]{2,1,0:T(8,128)(2,1)S(1)}, u32[]{:S(2)}, u32[]{:S(2)}) collective-permute-start(bf16[2,64,512]{2,1,0:T(8,128)(2,1)S(1)} %get-tuple-element.33), channel_id=1, source_target_pairs={{0,1},{1,0},{2,3},{3,2},{4,5},{5,4},{6,7},{7,6},{8,9},{9,8},{10,11... | collective-permute-start | bytes 393224 | tf_op jit(solution)/shard_map/ppermute | solution.py:500
  16.1 7.5 %collective-permute-start.9 = (bf16[2,64,512]{2,1,0:T(8,128)(2,1)S(1)}, bf16[2,64,512]{2,1,0:T(8,128)(2,1)S(1)}, u32[]{:S(2)}, u32[]{:S(2)}) collective-permute-start(bf16[2,64,512]{2,1,0:T(8,128)(2,1)S(1)} %get-tuple-element.34), channel_id=1, source_target_pairs={{0,4},{1,5},{2,6},{3,7},{4,0},{5,1},{6,2},{7,3},{8,12},{9,13},{10,... | collective-permute-start | bytes 393224 | tf_op jit(solution)/shard_map/ppermute | solution.py:500
  17.0 6.7 %collective-permute-start.10 = (bf16[2,64,512]{2,1,0:T(8,128)(2,1)S(1)}, bf16[2,64,512]{2,1,0:T(8,128)(2,1)S(1)}, u32[]{:S(2)}, u32[]{:S(2)}) collective-permute-start(bf16[2,64,512]{2,1,0:T(8,128)(2,1)S(1)} %get-tuple-element.35), channel_id=1, source_target_pairs={{0,5},{1,4},{2,7},{3,6},{4,1},{5,0},{6,3},{7,2},{8,13},{9,12},{10,... | collective-permute-start | bytes 393224 | tf_op jit(solution)/shard_map/ppermute | solution.py:500
  18.1 8.9 %collective-permute-start.6 = (bf16[4,128,128]{2,1,0:T(8,128)(2,1)S(1)}, bf16[4,128,128]{2,1,0:T(8,128)(2,1)S(1)}, u32[]{:S(2)}, u32[]{:S(2)}) collective-permute-start(bf16[4,128,128]{2,1,0:T(8,128)(2,1)S(1)} %collective-permute-done.5.refs_4_), channel_id=1, source_target_pairs={{8,0},{16,24},{9,1},{17,25},{10,2},{18,26},{11,3},{19,27},{12,4},{... | collective-permute-start | bytes 393224 | tf_op jit(solution)/shard_map/ppermute | solution.py:480
  19.4 9.0 %collective-permute-start.7 = (bf16[4,128,128]{2,1,0:T(8,128)(2,1)S(1)}, bf16[4,128,128]{2,1,0:T(8,128)(2,1)S(1)}, u32[]{:S(2)}, u32[]{:S(2)}) collective-permute-start(bf16[4,128,128]{2,1,0:T(8,128)(2,1)S(1)} %collective-permute-done.4.refs_2_), channel_id=1, source_target_pairs={{8,0},{16,24},{9,1},{17,25},{10,2},{18,26},{11,3},{19,27},{12,4},{... | collective-permute-start | bytes 393224 | tf_op jit(solution)/shard_map/ppermute | solution.py:480
  23.7 4.7 %copy-start.1 = (s32[480]{0:T(512)S(1)}, s32[480]{0:T(512)}, u32[]{:S(2)}) copy-start(s32[480]{0:T(512)} %param.7) | copy-start | bytes 5764
  23.8 8.0 %collective-permute-start.11 = (bf16[64,256]{1,0:T(8,128)(2,1)S(1)}, bf16[64,256]{1,0:T(8,128)(2,1)S(1)}, u32[]{:S(2)}, u32[]{:S(2)}) collective-permute-start(bf16[64,256]{1,0:T(8,128)(2,1)S(1)} %get-tuple-element.38), channel_id=1, source_target_pairs={{8,0},{16,8},{24,16},{9,1},{17,9},{25,17},{10,2},{18,10},{26,18},{... | collective-permute-start | bytes 98312 | tf_op jit(solution)/shard_map/ppermute | solution.py:515
  33.7 2.5 %collective-permute-start.12 = (f32[4,16,768]{2,1,0:T(8,128)S(1)}, f32[4,16,768]{2,1,0:T(8,128)S(1)}, u32[]{:S(2)}, u32[]{:S(2)}) collective-permute-start(f32[4,16,768]{2,1,0:T(8,128)S(1)} %get-tuple-element.42.after), channel_id=1, source_target_pairs={{0,2},{2,0},{4,6},{6,4},{1,3},{3,1},{5,7},{7,5},{8,10},{10,8},{12,... | collective-permute-start | bytes 589832 | tf_op jit(solution)/shard_map/ppermute | solution.py:561
  33.7 6.0 %copy-start = (bf16[480,512]{1,0:T(8,128)(2,1)S(1)}, bf16[480,512]{1,0:T(8,128)(2,1)}, u32[]{:S(2)}) copy-start(bf16[480,512]{1,0:T(8,128)(2,1)} %wave_ref.1) | copy-start | bytes 1474564
  36.2 5.3 %collective-permute-start.13 = (f32[16,768]{1,0:T(8,128)S(1)}, f32[16,768]{1,0:T(8,128)S(1)}, u32[]{:S(2)}, u32[]{:S(2)}) collective-permute-start(f32[16,768]{1,0:T(8,128)S(1)} %get-tuple-element.44), channel_id=1, source_target_pairs={{0,5},{1,4},{2,7},{3,6},{4,1},{5,0},{6,3},{7,2},{8,13},{9,12},{10,... | collective-permute-start | bytes 147464 | tf_op jit(solution)/shard_map/ppermute | solution.py:500
  37.1 4.9 %collective-permute-start.14 = (f32[16,768]{1,0:T(8,128)S(1)}, f32[16,768]{1,0:T(8,128)S(1)}, u32[]{:S(2)}, u32[]{:S(2)}) collective-permute-start(f32[16,768]{1,0:T(8,128)S(1)} %get-tuple-element.45), channel_id=1, source_target_pairs={{0,4},{1,5},{2,6},{3,7},{4,0},{5,1},{6,2},{7,3},{8,12},{9,13},{10,... | collective-permute-start | bytes 147464 | tf_op jit(solution)/shard_map/ppermute | solution.py:500
  38.1 4.1 %collective-permute-start.15 = (f32[16,768]{1,0:T(8,128)S(1)}, f32[16,768]{1,0:T(8,128)S(1)}, u32[]{:S(2)}, u32[]{:S(2)}) collective-permute-start(f32[16,768]{1,0:T(8,128)S(1)} %get-tuple-element.46), channel_id=1, source_target_pairs={{0,1},{1,0},{2,3},{3,2},{4,5},{5,4},{6,7},{7,6},{8,9},{9,8},{10,11... | collective-permute-start | bytes 147464 | tf_op jit(solution)/shard_map/ppermute | solution.py:500

commit v23 on v19

--- a/solution.py
+++ b/solution.py
@@ -228,10 +228,9 @@
         columns = width + 2 * LANES
         start = pl.multiple_of((2 * y + side) * width, width)
         samples = full[:, pl.ds(start, columns)]
-        for copy in range(depth // part):
-            tile, turn = copy // copies * LANES, copy % copies * FINE
-            turned = samples if turn == 0 else pltpu.roll(samples, columns - turn, 1)
-            shifts[y, copy * part : (copy + 1) * part, :] = turned[:, tile : tile + width + LANES]
+        for copy in range(copies):
+            turned = samples if copy == 0 else pltpu.roll(samples, columns - copy * FINE, 1)
+            shifts[y, copy * part : (copy + 1) * part, :] = turned
     tiles = products.shape[1]
     span = (tiles - 1) * LANES
     per_block = span // slab
@@ -242,10 +241,10 @@
         for tile in range(0, tiles, 2):
             start = index * span + tile * LANES
             pieces = min(2, tiles - tile)
+            starts = range(start, start + depth // (copies * part) * LANES, LANES)
+            right = [shifts[y, :, first : first + pieces * LANES] for first in starts]
             product = jnp.dot(
-                left[...],
-                shifts[y, :, start : start + pieces * LANES],
-                preferred_element_type=F32,
+                left[...], jnp.concatenate(right, axis=0), preferred_element_type=F32
             )
             for piece in range(pieces):
                 products[slot, tile + piece] = product[:, piece * LANES : (piece + 1) * LANES]
@@ -519,7 +518,7 @@
 
     def scratch():
         return [
-            pltpu.VMEM((2, depth, chunk // 4 + LANES), BF16),
+            pltpu.VMEM((2, LANES // FINE * part, chunk // 4 + 2 * LANES), BF16),
             pltpu.VMEM((2, span // LANES + 1, count * FINE, LANES), F32),
         ]
 

time: 38.8 us -> 38.7 us (level)
  no operation moved by 1% of the time
where the time goes in v23:
time: 38.7 us; the launch traced here: 38.5 us
  starting transfers between devices  20.3 us (52%)
  Pallas kernels  9.15 us (24%)
  waiting for transfers between devices  8.93 us (23%)
    ppermute x6, starting transfers between devices, swap(): return lax.ppermute(part, every, route)  8.27 us
    ppermute x4, starting transfers between devices, cross(): return lax.ppermute(part, 'outer', route)  7.48 us
    ppermute x4, waiting for transfers between devices, cross(): return lax.ppermute(part, 'outer', route)  4.57 us
    ppermute x3, starting transfers between devices, plane(): return lax.ppermute(part, 'inner', [(b, b ^ flip) for b in range(INNER)])  3.18 us
    ppermute x6, waiting for transfers between devices, swap(): return lax.ppermute(part, every, route)  2.92 us
    pallas_call x1, Pallas kernels, on_device(): call(last_dots_kernel, [VMEM] * 4 + [AFTER], sds((half, count, slab + win...  2.37 us
    pallas_call x1, Pallas kernels, on_device(): call(middle_dots_kernel, [VMEM] * 5, [sds((half, count, slab + window), F...  1.85 us
    pallas_call x1, Pallas kernels, on_device(): call(functools.partial(prologue_kernel, tm_count), [HBM] * 4, [sds((padde...  1.7 us
  transfers between devices with their start and end apart: 15, of which 8 were waited for; matrix products, arithmetic and copies ran while one was open for 0% of the time, Pallas kernels for 13%

profile of v23, /device:TPU:0, one launch (start us, length us, event | category | flops | bytes accessed | tf_op | source)
XLA Modules:
  0.0 38.5 jit_solution(1321361699730709528)
XLA Ops:
  0.0 1.7 %shard_map.46 = (bf16[1152,128]{1,0:T(8,128)(2,1)S(1)}, bf16[256,512]{1,0:T(8,128)(2,1)S(1)}, bf16[128,128]{1,0:T(8,128)(2,1)S(1)}, bf16[128,128]{1,0:T(8,128)(2,1)S(1)}, bf16[128,128]{1,0:T(8,128)(2,1)S(1)}) custom-call(bf16[480,512]{1,0:T(8,128)(2,1)} %wave_ref.1, bf16[1,480,256]{2,1,0:T(8,128)(2,1)} %tpl_hbm.1, s32[1,160]{1,0:T(1,128)} %flag_hbm.1, ...), custom_call_target="tpu_custom_call" | custom-call | bytes 737280 | tf_op jit(solution)/shard_map/pallas_call | solution.py:448
  1.7 0.5 %collective-permute-start = (bf16[1152,128]{1,0:T(8,128)(2,1)S(1)}, bf16[1152,128]{1,0:T(8,128)(2,1)S(1)}, u32[]{:S(2)}, u32[]{:S(2)}) collective-permute-start(bf16[1152,128]{1,0:T(8,128)(2,1)S(1)} %get-tuple-element.28), channel_id=1, source_target_pairs={{0,2},{2,0},{4,6},{6,4},{1,3},{3,1},{5,7},{7,5},{8,10},{10,8},{12,... | collective-permute-start | bytes 884744 | tf_op jit(solution)/shard_map/ppermute | solution.py:470
  2.2 2.6 %collective-permute-start.1 = (bf16[128,128]{1,0:T(8,128)(2,1)S(1)}, bf16[128,128]{1,0:T(8,128)(2,1)S(1)}, u32[]{:S(2)}, u32[]{:S(2)}) collective-permute-start(bf16[128,128]{1,0:T(8,128)(2,1)S(1)} %get-tuple-element.29), channel_id=1, source_target_pairs={{0,4},{2,6},{4,0},{6,2},{1,5},{3,7},{5,1},{7,3},{8,12},{10,14},{12... | collective-permute-start | bytes 98312 | tf_op jit(solution)/shard_map/ppermute | solution.py:470
  5.0 1.8 %collective-permute-start.7 = (bf16[2,64,512]{2,1,0:T(8,128)(2,1)S(1)}, bf16[2,64,512]{2,1,0:T(8,128)(2,1)S(1)}, u32[]{:S(2)}, u32[]{:S(2)}) collective-permute-start(bf16[2,64,512]{2,1,0:T(8,128)(2,1)S(1)} %get-tuple-element.33), channel_id=1, source_target_pairs={{0,1},{1,0},{2,3},{3,2},{4,5},{5,4},{6,7},{7,6},{8,9},{9,8},{10,11... | collective-permute-start | bytes 393224 | tf_op jit(solution)/shard_map/ppermute | solution.py:498
  6.8 1.4 %collective-permute-done.2.both_ref = bf16[128,128]{1,0:T(8,128)(2,1)S(1)} collective-permute-done((bf16[128,128]{1,0:T(8,128)(2,1)S(1)}, bf16[128,128]{1,0:T(8,128)(2,1)S(1)}, u32[]{:S(2)}, u32[]{:S(2)}) %collective-permute-start.2) | collective-permute-done | bytes 32800 | tf_op jit(solution)/shard_map/ppermute | solution.py:470
  8.2 2.7 %collective-permute-start.4 = (bf16[4,128,128]{2,1,0:T(8,128)(2,1)S(1)}, bf16[4,128,128]{2,1,0:T(8,128)(2,1)S(1)}, u32[]{:S(2)}, u32[]{:S(2)}) collective-permute-start(bf16[4,128,128]{2,1,0:T(8,128)(2,1)S(1)} %shard_map.47.refs_0_), channel_id=1, source_target_pairs={{0,16},{16,0},{8,24},{24,8},{1,17},{17,1},{9,25},{25,9},{2,18},{18... | collective-permute-start | bytes 393224 | tf_op jit(solution)/shard_map/ppermute | solution.py:479
  10.8 0.9 %collective-permute-start.8 = (bf16[2,64,512]{2,1,0:T(8,128)(2,1)S(1)}, bf16[2,64,512]{2,1,0:T(8,128)(2,1)S(1)}, u32[]{:S(2)}, u32[]{:S(2)}) collective-permute-start(bf16[2,64,512]{2,1,0:T(8,128)(2,1)S(1)} %get-tuple-element.34), channel_id=1, source_target_pairs={{0,4},{1,5},{2,6},{3,7},{4,0},{5,1},{6,2},{7,3},{8,12},{9,13},{10,... | collective-permute-start | bytes 393224 | tf_op jit(solution)/shard_map/ppermute | solution.py:498
  11.7 2.1 %collective-permute-start.9 = (bf16[2,64,512]{2,1,0:T(8,128)(2,1)S(1)}, bf16[2,64,512]{2,1,0:T(8,128)(2,1)S(1)}, u32[]{:S(2)}, u32[]{:S(2)}) collective-permute-start(bf16[2,64,512]{2,1,0:T(8,128)(2,1)S(1)} %get-tuple-element.35), channel_id=1, source_target_pairs={{0,5},{1,4},{2,7},{3,6},{4,1},{5,0},{6,3},{7,2},{8,13},{9,12},{10,... | collective-permute-start | bytes 393224 | tf_op jit(solution)/shard_map/ppermute | solution.py:498
  13.8 0.7 %collective-permute-start.5 = (bf16[4,128,128]{2,1,0:T(8,128)(2,1)S(1)}, bf16[4,128,128]{2,1,0:T(8,128)(2,1)S(1)}, u32[]{:S(2)}, u32[]{:S(2)}) collective-permute-start(bf16[4,128,128]{2,1,0:T(8,128)(2,1)S(1)} %shard_map.47.refs_0_), channel_id=1, source_target_pairs={{8,16},{16,8},{9,17},{17,9},{10,18},{18,10},{11,19},{19,11},{12,20... | collective-permute-start | bytes 393224 | tf_op jit(solution)/shard_map/ppermute | solution.py:479
  14.5 2.9 %collective-permute-start.3 = (bf16[4,128,128]{2,1,0:T(8,128)(2,1)S(1)}, bf16[4,128,128]{2,1,0:T(8,128)(2,1)S(1)}, u32[]{:S(2)}, u32[]{:S(2)}) collective-permute-start(bf16[4,128,128]{2,1,0:T(8,128)(2,1)S(1)} %shard_map.47.refs_0_), channel_id=1, source_target_pairs={{0,8},{8,0},{16,24},{24,16},{1,9},{9,1},{17,25},{25,17},{2,10},{10... | collective-permute-start | bytes 393224 | tf_op jit(solution)/shard_map/ppermute | solution.py:479
  17.5 1.3 %collective-permute-start.6 = (bf16[4,128,128]{2,1,0:T(8,128)(2,1)S(1)}, bf16[4,128,128]{2,1,0:T(8,128)(2,1)S(1)}, u32[]{:S(2)}, u32[]{:S(2)}) collective-permute-start(bf16[4,128,128]{2,1,0:T(8,128)(2,1)S(1)} %collective-permute-done.4.refs_2_), channel_id=1, source_target_pairs={{8,0},{16,24},{9,1},{17,25},{10,2},{18,26},{11,3},{19,27},{12,4},{... | collective-permute-start | bytes 393224 | tf_op jit(solution)/shard_map/ppermute | solution.py:479
  19.0 1.3 %collective-permute-start.10 = (bf16[64,256]{1,0:T(8,128)(2,1)S(1)}, bf16[64,256]{1,0:T(8,128)(2,1)S(1)}, u32[]{:S(2)}, u32[]{:S(2)}) collective-permute-start(bf16[64,256]{1,0:T(8,128)(2,1)S(1)} %get-tuple-element.38), channel_id=1, source_target_pairs={{8,0},{16,8},{24,16},{9,1},{17,9},{25,17},{10,2},{18,10},{26,18},{... | collective-permute-start | bytes 98312 | tf_op jit(solution)/shard_map/ppermute | solution.py:513
  20.3 4.4 %collective-permute-done.6.refs_4_ = bf16[4,128,128]{2,1,0:T(8,128)(2,1)S(1)} collective-permute-done((bf16[4,128,128]{2,1,0:T(8,128)(2,1)S(1)}, bf16[4,128,128]{2,1,0:T(8,128)(2,1)S(1)}, u32[]{:S(2)}, u32[]{:S(2)}) %collective-permute-start.6) | collective-permute-done | bytes 131104 | tf_op jit(solution)/shard_map/ppermute | solution.py:479
  24.7 1.5 %shard_map.50 = (f32[2,16,512]{2,1,0:T(8,128)S(1)}, bf16[256,1024]{1,0:T(8,128)(2,1)S(1)}, f32[16,128]{1,0:T(8,128)S(1)}, bf16[16,480]{1,0:T(8,128)(2,1)S(1)}, bf16[16,64]{1,0:T(8,128)(2,1)S(1)}) custom-call(bf16[4,128,128]{2,1,0:T(8,128)(2,1)S(1)} %shard_map.47.refs_0_, bf16[4,128,128]{2,1,0:T(8,128)(2,1)S(1)} %collective-permute-done.3.refs_1_, ...), custom_call_target="tpu_custom_call" | custom-call | flops 536870912 | bytes 524288 | tf_op jit(solution)/shard_map/pallas_call | solution.py:525
  26.3 1.9 %shard_map.51 = (f32[4,16,768]{2,1,0:T(8,128)S(1)}, f32[4,16,256]{2,1,0:T(8,128)S(1)}) custom-call(bf16[256,1024]{1,0:T(8,128)(2,1)S(1)} %get-tuple-element.37.left, bf16[64,4096]{1,0:T(8,128)(2,1)S(1)} %get-tuple-element.36.refs_6_.samples_ref, bf16[64,256]{1,0:T(8,128)(2,1)S(1)} %collective-permute-done.10.halo_ref, ...), custom_call_target="tpu_custom_call" | custom-call | flops 536870912 | bytes 524288 | tf_op jit(solution)/shard_map/pallas_call | solution.py:541
  28.2 2.4 %shard_map.52.keep_ref.after = f32[4,16,768]{2,1,0:T(8,128)S(1)} custom-call(bf16[256,1024]{1,0:T(8,128)(2,1)S(1)} %get-tuple-element.37.left, bf16[64,4096]{1,0:T(8,128)(2,1)S(1)} %get-tuple-element.36.refs_6_.samples_ref, bf16[64,256]{1,0:T(8,128)(2,1)S(1)} %collective-permute-done.10.halo_ref, f32[4,16,256]{2,1,0:T(8,128)S(1)} %get-tuple-element.41.edges_ref, ...), custom_call_target="tpu_custom_call" | custom-call | flops 1073741824 | bytes 524288 | tf_op jit(solution)/shard_map/pallas_call | solution.py:550
  30.6 2.0 %collective-permute-start.12 = (f32[16,768]{1,0:T(8,128)S(1)}, f32[16,768]{1,0:T(8,128)S(1)}, u32[]{:S(2)}, u32[]{:S(2)}) collective-permute-start(f32[16,768]{1,0:T(8,128)S(1)} %get-tuple-element.44), channel_id=1, source_target_pairs={{0,5},{1,4},{2,7},{3,6},{4,1},{5,0},{6,3},{7,2},{8,13},{9,12},{10,... | collective-permute-start | bytes 147464 | tf_op jit(solution)/shard_map/ppermute | solution.py:498
  32.6 1.2 %collective-permute-start.13 = (f32[16,768]{1,0:T(8,128)S(1)}, f32[16,768]{1,0:T(8,128)S(1)}, u32[]{:S(2)}, u32[]{:S(2)}) collective-permute-start(f32[16,768]{1,0:T(8,128)S(1)} %get-tuple-element.45), channel_id=1, source_target_pairs={{0,4},{1,5},{2,6},{3,7},{4,0},{5,1},{6,2},{7,3},{8,12},{9,13},{10,... | collective-permute-start | bytes 147464 | tf_op jit(solution)/shard_map/ppermute | solution.py:498
  33.8 0.4 %collective-permute-start.14 = (f32[16,768]{1,0:T(8,128)S(1)}, f32[16,768]{1,0:T(8,128)S(1)}, u32[]{:S(2)}, u32[]{:S(2)}) collective-permute-start(f32[16,768]{1,0:T(8,128)S(1)} %get-tuple-element.46), channel_id=1, source_target_pairs={{0,1},{1,0},{2,3},{3,2},{4,5},{5,4},{6,7},{7,6},{8,9},{9,8},{10,11... | collective-permute-start | bytes 147464 | tf_op jit(solution)/shard_map/ppermute | solution.py:498
  34.2 0.9 %shard_map.54.refs_4_ = f32[16,512]{1,0:T(8,128)S(1)} custom-call(bf16[480,512]{1,0:T(8,128)(2,1)S(1)} %copy-done, bf16[16,480]{1,0:T(8,128)(2,1)S(1)} %get-tuple-element.47.mask_ref, f32[4,16,768]{2,1,0:T(8,128)S(1)} %shard_map.52.keep_ref.after), custom_call_target="tpu_custom_call" | custom-call | flops 15728640 | bytes 491520 | tf_op jit(solution)/shard_map/pallas_call | solution.py:560
  35.1 0.7 %collective-permute-done.12.refs_1_ = f32[16,768]{1,0:T(8,128)S(1)} collective-permute-done((f32[16,768]{1,0:T(8,128)S(1)}, f32[16,768]{1,0:T(8,128)S(1)}, u32[]{:S(2)}, u32[]{:S(2)}) %collective-permute-start.12) | collective-permute-done | bytes 49184 | tf_op jit(solution)/shard_map/ppermute | solution.py:498
  35.8 1.0 %collective-permute-done.13.refs_2_ = f32[16,768]{1,0:T(8,128)S(1)} collective-permute-done((f32[16,768]{1,0:T(8,128)S(1)}, f32[16,768]{1,0:T(8,128)S(1)}, u32[]{:S(2)}, u32[]{:S(2)}) %collective-permute-start.13) | collective-permute-done | bytes 49184 | tf_op jit(solution)/shard_map/ppermute | solution.py:498
  36.8 1.1 %collective-permute-done.14.refs_3_ = f32[16,768]{1,0:T(8,128)S(1)} collective-permute-done((f32[16,768]{1,0:T(8,128)S(1)}, f32[16,768]{1,0:T(8,128)S(1)}, u32[]{:S(2)}, u32[]{:S(2)}) %collective-permute-start.14) | collective-permute-done | bytes 49184 | tf_op jit(solution)/shard_map/ppermute | solution.py:498
  37.8 0.7 %shard_map.55 = f32[16,512]{1,0:T(8,128)} custom-call(f32[16,768]{1,0:T(8,128)S(1)} %get-tuple-element.43.refs_0_, f32[16,768]{1,0:T(8,128)S(1)} %collective-permute-done.12.refs_1_, f32[16,768]{1,0:T(8,128)S(1)} %collective-permute-done.13.refs_2_, f32[16,768]{1,0:T(8,128)S(1)} %collective-permute-done.14.refs_3_, f32[16,512]{1,0:T(8,128)S(1)} %shard_map.54.refs_4_, ...), custom_call_target="tpu_custom_call" | custom-call | bytes 196608 | tf_op jit(solution)/shard_map/pallas_call | solution.py:574
  (20 shorter events, 0.7 us)
Async XLA Ops:
  1.7 3.2 %collective-permute-start = (bf16[1152,128]{1,0:T(8,128)(2,1)S(1)}, bf16[1152,128]{1,0:T(8,128)(2,1)S(1)}, u32[]{:S(2)}, u32[]{:S(2)}) collective-permute-start(bf16[1152,128]{1,0:T(8,128)(2,1)S(1)} %get-tuple-element.28), channel_id=1, source_target_pairs={{0,2},{2,0},{4,6},{6,4},{1,3},{3,1},{5,7},{7,5},{8,10},{10,8},{12,... | collective-permute-start | bytes 884744 | tf_op jit(solution)/shard_map/ppermute | solution.py:470
  2.2 4.6 %collective-permute-start.1 = (bf16[128,128]{1,0:T(8,128)(2,1)S(1)}, bf16[128,128]{1,0:T(8,128)(2,1)S(1)}, u32[]{:S(2)}, u32[]{:S(2)}) collective-permute-start(bf16[128,128]{1,0:T(8,128)(2,1)S(1)} %get-tuple-element.29), channel_id=1, source_target_pairs={{0,4},{2,6},{4,0},{6,2},{1,5},{3,7},{5,1},{7,3},{8,12},{10,14},{12... | collective-permute-start | bytes 98312 | tf_op jit(solution)/shard_map/ppermute | solution.py:470
  4.8 3.3 %collective-permute-start.2 = (bf16[128,128]{1,0:T(8,128)(2,1)S(1)}, bf16[128,128]{1,0:T(8,128)(2,1)S(1)}, u32[]{:S(2)}, u32[]{:S(2)}) collective-permute-start(bf16[128,128]{1,0:T(8,128)(2,1)S(1)} %get-tuple-element.30), channel_id=1, source_target_pairs={{0,6},{2,4},{4,2},{6,0},{1,7},{3,5},{5,3},{7,1},{8,14},{10,12},{12... | collective-permute-start | bytes 98312 | tf_op jit(solution)/shard_map/ppermute | solution.py:470
  5.0 9.5 %collective-permute-start.7 = (bf16[2,64,512]{2,1,0:T(8,128)(2,1)S(1)}, bf16[2,64,512]{2,1,0:T(8,128)(2,1)S(1)}, u32[]{:S(2)}, u32[]{:S(2)}) collective-permute-start(bf16[2,64,512]{2,1,0:T(8,128)(2,1)S(1)} %get-tuple-element.33), channel_id=1, source_target_pairs={{0,1},{1,0},{2,3},{3,2},{4,5},{5,4},{6,7},{7,6},{8,9},{9,8},{10,11... | collective-permute-start | bytes 393224 | tf_op jit(solution)/shard_map/ppermute | solution.py:498
  8.2 9.3 %collective-permute-start.4 = (bf16[4,128,128]{2,1,0:T(8,128)(2,1)S(1)}, bf16[4,128,128]{2,1,0:T(8,128)(2,1)S(1)}, u32[]{:S(2)}, u32[]{:S(2)}) collective-permute-start(bf16[4,128,128]{2,1,0:T(8,128)(2,1)S(1)} %shard_map.47.refs_0_), channel_id=1, source_target_pairs={{0,16},{16,0},{8,24},{24,8},{1,17},{17,1},{9,25},{25,9},{2,18},{18... | collective-permute-start | bytes 393224 | tf_op jit(solution)/shard_map/ppermute | solution.py:479
  10.8 8.1 %collective-permute-start.8 = (bf16[2,64,512]{2,1,0:T(8,128)(2,1)S(1)}, bf16[2,64,512]{2,1,0:T(8,128)(2,1)S(1)}, u32[]{:S(2)}, u32[]{:S(2)}) collective-permute-start(bf16[2,64,512]{2,1,0:T(8,128)(2,1)S(1)} %get-tuple-element.34), channel_id=1, source_target_pairs={{0,4},{1,5},{2,6},{3,7},{4,0},{5,1},{6,2},{7,3},{8,12},{9,13},{10,... | collective-permute-start | bytes 393224 | tf_op jit(solution)/shard_map/ppermute | solution.py:498
  11.7 7.2 %collective-permute-start.9 = (bf16[2,64,512]{2,1,0:T(8,128)(2,1)S(1)}, bf16[2,64,512]{2,1,0:T(8,128)(2,1)S(1)}, u32[]{:S(2)}, u32[]{:S(2)}) collective-permute-start(bf16[2,64,512]{2,1,0:T(8,128)(2,1)S(1)} %get-tuple-element.35), channel_id=1, source_target_pairs={{0,5},{1,4},{2,7},{3,6},{4,1},{5,0},{6,3},{7,2},{8,13},{9,12},{10,... | collective-permute-start | bytes 393224 | tf_op jit(solution)/shard_map/ppermute | solution.py:498
  13.8 6.5 %collective-permute-start.5 = (bf16[4,128,128]{2,1,0:T(8,128)(2,1)S(1)}, bf16[4,128,128]{2,1,0:T(8,128)(2,1)S(1)}, u32[]{:S(2)}, u32[]{:S(2)}) collective-permute-start(bf16[4,128,128]{2,1,0:T(8,128)(2,1)S(1)} %shard_map.47.refs_0_), channel_id=1, source_target_pairs={{8,16},{16,8},{9,17},{17,9},{10,18},{18,10},{11,19},{19,11},{12,20... | collective-permute-start | bytes 393224 | tf_op jit(solution)/shard_map/ppermute | solution.py:479
  14.5 5.9 %collective-permute-start.3 = (bf16[4,128,128]{2,1,0:T(8,128)(2,1)S(1)}, bf16[4,128,128]{2,1,0:T(8,128)(2,1)S(1)}, u32[]{:S(2)}, u32[]{:S(2)}) collective-permute-start(bf16[4,128,128]{2,1,0:T(8,128)(2,1)S(1)} %shard_map.47.refs_0_), channel_id=1, source_target_pairs={{0,8},{8,0},{16,24},{24,16},{1,9},{9,1},{17,25},{25,17},{2,10},{10... | collective-permute-start | bytes 393224 | tf_op jit(solution)/shard_map/ppermute | solution.py:479
  17.5 7.2 %collective-permute-start.6 = (bf16[4,128,128]{2,1,0:T(8,128)(2,1)S(1)}, bf16[4,128,128]{2,1,0:T(8,128)(2,1)S(1)}, u32[]{:S(2)}, u32[]{:S(2)}) collective-permute-start(bf16[4,128,128]{2,1,0:T(8,128)(2,1)S(1)} %collective-permute-done.4.refs_2_), channel_id=1, source_target_pairs={{8,0},{16,24},{9,1},{17,25},{10,2},{18,26},{11,3},{19,27},{12,4},{... | collective-permute-start | bytes 393224 | tf_op jit(solution)/shard_map/ppermute | solution.py:479
  19.0 5.7 %copy-start.1 = (s32[480]{0:T(512)S(1)}, s32[480]{0:T(512)}, u32[]{:S(2)}) copy-start(s32[480]{0:T(512)} %param.7) | copy-start | bytes 5764
  19.0 7.2 %collective-permute-start.10 = (bf16[64,256]{1,0:T(8,128)(2,1)S(1)}, bf16[64,256]{1,0:T(8,128)(2,1)S(1)}, u32[]{:S(2)}, u32[]{:S(2)}) collective-permute-start(bf16[64,256]{1,0:T(8,128)(2,1)S(1)} %get-tuple-element.38), channel_id=1, source_target_pairs={{8,0},{16,8},{24,16},{9,1},{17,9},{25,17},{10,2},{18,10},{26,18},{... | collective-permute-start | bytes 98312 | tf_op jit(solution)/shard_map/ppermute | solution.py:513
  28.1 2.5 %collective-permute-start.11 = (f32[4,16,768]{2,1,0:T(8,128)S(1)}, f32[4,16,768]{2,1,0:T(8,128)S(1)}, u32[]{:S(2)}, u32[]{:S(2)}) collective-permute-start(f32[4,16,768]{2,1,0:T(8,128)S(1)} %get-tuple-element.42.after), channel_id=1, source_target_pairs={{0,2},{2,0},{4,6},{6,4},{1,3},{3,1},{5,7},{7,5},{8,10},{10,8},{12,... | collective-permute-start | bytes 589832 | tf_op jit(solution)/shard_map/ppermute | solution.py:559
  28.2 6.0 %copy-start = (bf16[480,512]{1,0:T(8,128)(2,1)S(1)}, bf16[480,512]{1,0:T(8,128)(2,1)}, u32[]{:S(2)}) copy-start(bf16[480,512]{1,0:T(8,128)(2,1)} %wave_ref.1) | copy-start | bytes 1474564
  30.6 5.1 %collective-permute-start.12 = (f32[16,768]{1,0:T(8,128)S(1)}, f32[16,768]{1,0:T(8,128)S(1)}, u32[]{:S(2)}, u32[]{:S(2)}) collective-permute-start(f32[16,768]{1,0:T(8,128)S(1)} %get-tuple-element.44), channel_id=1, source_target_pairs={{0,5},{1,4},{2,7},{3,6},{4,1},{5,0},{6,3},{7,2},{8,13},{9,12},{10,... | collective-permute-start | bytes 147464 | tf_op jit(solution)/shard_map/ppermute | solution.py:498
  32.6 4.2 %collective-permute-start.13 = (f32[16,768]{1,0:T(8,128)S(1)}, f32[16,768]{1,0:T(8,128)S(1)}, u32[]{:S(2)}, u32[]{:S(2)}) collective-permute-start(f32[16,768]{1,0:T(8,128)S(1)} %get-tuple-element.45), channel_id=1, source_target_pairs={{0,4},{1,5},{2,6},{3,7},{4,0},{5,1},{6,2},{7,3},{8,12},{9,13},{10,... | collective-permute-start | bytes 147464 | tf_op jit(solution)/shard_map/ppermute | solution.py:498
  33.8 4.1 %collective-permute-start.14 = (f32[16,768]{1,0:T(8,128)S(1)}, f32[16,768]{1,0:T(8,128)S(1)}, u32[]{:S(2)}, u32[]{:S(2)}) collective-permute-start(f32[16,768]{1,0:T(8,128)S(1)} %get-tuple-element.46), channel_id=1, source_target_pairs={{0,1},{1,0},{2,3},{3,2},{4,5},{5,4},{6,7},{7,6},{8,9},{9,8},{10,11... | collective-permute-start | bytes 147464 | tf_op jit(solution)/shard_map/ppermute | solution.py:498

commit v24 on v23

--- a/solution.py
+++ b/solution.py
@@ -250,20 +250,22 @@
                 products[slot, tile + piece] = product[:, piece * LANES : (piece + 1) * LANES]
 
     def gather(place, slot):
-        def tree(first, number):
+        def tree(first, number, here):
             if number == 1:
                 rows = pl.ds(first, count, stride=FINE)
-                return jnp.concatenate(
-                    [products[slot, tile, rows, :] for tile in range(tiles)], axis=1
-                )
+                return jnp.concatenate([products[slot, tile, rows, :] for tile in here], axis=1)
             half = number // 2
-            later = pltpu.roll(tree(first + half, half), span + LANES - half, 1)
-            return tree(first, half) + later
-
-        total = tree(0, FINE)
+            later = pltpu.roll(tree(first + half, half, here), len(here) * LANES - half, 1)
+            return tree(first, half, here) + later
+
         y, index = place
-        for piece in range(per_block):
-            store(y, index * per_block + piece, total[:, piece * slab : (piece + 1) * slab])
+        cut = tiles // 3
+        for low, high in ((0, cut), (cut, tiles - 1)):
+            total = tree(0, FINE, range(low, high + 1))
+            for tile in range(low, high):
+                member, lane = divmod(tile * LANES, slab)
+                columns = total[:, (tile - low) * LANES : (tile - low + 1) * LANES]
+                store(y, index * per_block + member, lane, columns)
 
     multiply(blocks[0], 0)
     for number in range(1, len(blocks)):
@@ -282,8 +284,8 @@
     core = lax.rem(lax.axis_index("inner"), 2)
     run, _, slab = begun_ref.shape
 
-    def store(y, place, sums):
-        begun_ref[place] = sums
+    def store(y, place, lane, sums):
+        begun_ref[place, :, lane : lane + LANES] = sums
 
     correlate(left, samples_ref, slab, run, 1 - core, [0], store, shifts, products)
     read_masks(stations, channels, tm_count, tpls, order_ref, scale_ref, mask_ref, part_ref)
@@ -299,8 +301,8 @@
     full[:, :chunk] = samples_ref[...]
     full[:, chunk:] = halo_ref[...]
 
-    def store(y, place, sums):
-        send_ref[y * run + place, :, :slab] = sums
+    def store(y, place, lane, sums):
+        send_ref[run + place, :, lane : lane + LANES] = sums
 
     correlate(left, full, slab, run, 1 - core, [1], store, shifts, products)
     after = [full[:, (m + 1) * slab : (m + 1) * slab + window] for m in range(group)]
@@ -331,8 +333,8 @@
     run = keep_ref.shape[0] // 2
     slab = keep_ref.shape[2] - edges_ref.shape[2]
 
-    def store(y, place, sums):
-        keep_ref[y * run + place, :, :slab] = sums
+    def store(y, place, lane, sums):
+        keep_ref[y * run + place, :, lane : lane + LANES] = sums
 
     correlate(left, full, slab, run, core, [0, 1], store, shifts, products)
     keep_ref[:, :, slab:] = edges_ref[...]

time: 38.7 us -> 38.9 us (level)
  no operation moved by 1% of the time
where the time goes in v24:
time: 38.9 us; the launch traced here: 38.7 us
  starting transfers between devices  20.3 us (52%)
  Pallas kernels  9.32 us (24%)
  waiting for transfers between devices  8.93 us (23%)
    ppermute x6, starting transfers between devices, swap(): return lax.ppermute(part, every, route)  8.27 us
    ppermute x4, starting transfers between devices, cross(): return lax.ppermute(part, 'outer', route)  7.48 us
    ppermute x4, waiting for transfers between devices, cross(): return lax.ppermute(part, 'outer', route)  4.57 us
    ppermute x3, starting transfers between devices, plane(): return lax.ppermute(part, 'inner', [(b, b ^ flip) for b in range(INNER)])  3.18 us
    ppermute x6, waiting for transfers between devices, swap(): return lax.ppermute(part, every, route)  2.92 us
    pallas_call x1, Pallas kernels, on_device(): call(last_dots_kernel, [VMEM] * 4 + [AFTER], sds((half, count, slab + win...  2.51 us
    pallas_call x1, Pallas kernels, on_device(): call(middle_dots_kernel, [VMEM] * 5, [sds((half, count, slab + window), F...  1.89 us
    pallas_call x1, Pallas kernels, on_device(): call(functools.partial(prologue_kernel, tm_count), [HBM] * 4, [sds((padde...  1.7 us
  transfers between devices with their start and end apart: 15, of which 8 were waited for; matrix products, arithmetic and copies ran while one was open for 0% of the time, Pallas kernels for 13%

profile of v24, /device:TPU:0, one launch (start us, length us, event | category | flops | bytes accessed | tf_op | source)
XLA Modules:
  0.0 38.7 jit_solution(3501638929754185533)
XLA Ops:
  0.0 1.7 %shard_map.46 = (bf16[1152,128]{1,0:T(8,128)(2,1)S(1)}, bf16[256,512]{1,0:T(8,128)(2,1)S(1)}, bf16[128,128]{1,0:T(8,128)(2,1)S(1)}, bf16[128,128]{1,0:T(8,128)(2,1)S(1)}, bf16[128,128]{1,0:T(8,128)(2,1)S(1)}) custom-call(bf16[480,512]{1,0:T(8,128)(2,1)} %wave_ref.1, bf16[1,480,256]{2,1,0:T(8,128)(2,1)} %tpl_hbm.1, s32[1,160]{1,0:T(1,128)} %flag_hbm.1, ...), custom_call_target="tpu_custom_call" | custom-call | bytes 737280 | tf_op jit(solution)/shard_map/pallas_call | solution.py:450
  1.7 0.5 %collective-permute-start = (bf16[1152,128]{1,0:T(8,128)(2,1)S(1)}, bf16[1152,128]{1,0:T(8,128)(2,1)S(1)}, u32[]{:S(2)}, u32[]{:S(2)}) collective-permute-start(bf16[1152,128]{1,0:T(8,128)(2,1)S(1)} %get-tuple-element.28), channel_id=1, source_target_pairs={{0,2},{2,0},{4,6},{6,4},{1,3},{3,1},{5,7},{7,5},{8,10},{10,8},{12,... | collective-permute-start | bytes 884744 | tf_op jit(solution)/shard_map/ppermute | solution.py:472
  2.2 2.6 %collective-permute-start.1 = (bf16[128,128]{1,0:T(8,128)(2,1)S(1)}, bf16[128,128]{1,0:T(8,128)(2,1)S(1)}, u32[]{:S(2)}, u32[]{:S(2)}) collective-permute-start(bf16[128,128]{1,0:T(8,128)(2,1)S(1)} %get-tuple-element.29), channel_id=1, source_target_pairs={{0,4},{2,6},{4,0},{6,2},{1,5},{3,7},{5,1},{7,3},{8,12},{10,14},{12... | collective-permute-start | bytes 98312 | tf_op jit(solution)/shard_map/ppermute | solution.py:472
  5.0 1.8 %collective-permute-start.7 = (bf16[2,64,512]{2,1,0:T(8,128)(2,1)S(1)}, bf16[2,64,512]{2,1,0:T(8,128)(2,1)S(1)}, u32[]{:S(2)}, u32[]{:S(2)}) collective-permute-start(bf16[2,64,512]{2,1,0:T(8,128)(2,1)S(1)} %get-tuple-element.33), channel_id=1, source_target_pairs={{0,1},{1,0},{2,3},{3,2},{4,5},{5,4},{6,7},{7,6},{8,9},{9,8},{10,11... | collective-permute-start | bytes 393224 | tf_op jit(solution)/shard_map/ppermute | solution.py:500
  6.8 1.4 %collective-permute-done.2.both_ref = bf16[128,128]{1,0:T(8,128)(2,1)S(1)} collective-permute-done((bf16[128,128]{1,0:T(8,128)(2,1)S(1)}, bf16[128,128]{1,0:T(8,128)(2,1)S(1)}, u32[]{:S(2)}, u32[]{:S(2)}) %collective-permute-start.2) | collective-permute-done | bytes 32800 | tf_op jit(solution)/shard_map/ppermute | solution.py:472
  8.2 2.7 %collective-permute-start.4 = (bf16[4,128,128]{2,1,0:T(8,128)(2,1)S(1)}, bf16[4,128,128]{2,1,0:T(8,128)(2,1)S(1)}, u32[]{:S(2)}, u32[]{:S(2)}) collective-permute-start(bf16[4,128,128]{2,1,0:T(8,128)(2,1)S(1)} %shard_map.47.refs_0_), channel_id=1, source_target_pairs={{0,16},{16,0},{8,24},{24,8},{1,17},{17,1},{9,25},{25,9},{2,18},{18... | collective-permute-start | bytes 393224 | tf_op jit(solution)/shard_map/ppermute | solution.py:481
  10.8 0.9 %collective-permute-start.8 = (bf16[2,64,512]{2,1,0:T(8,128)(2,1)S(1)}, bf16[2,64,512]{2,1,0:T(8,128)(2,1)S(1)}, u32[]{:S(2)}, u32[]{:S(2)}) collective-permute-start(bf16[2,64,512]{2,1,0:T(8,128)(2,1)S(1)} %get-tuple-element.34), channel_id=1, source_target_pairs={{0,4},{1,5},{2,6},{3,7},{4,0},{5,1},{6,2},{7,3},{8,12},{9,13},{10,... | collective-permute-start | bytes 393224 | tf_op jit(solution)/shard_map/ppermute | solution.py:500
  11.7 2.1 %collective-permute-start.9 = (bf16[2,64,512]{2,1,0:T(8,128)(2,1)S(1)}, bf16[2,64,512]{2,1,0:T(8,128)(2,1)S(1)}, u32[]{:S(2)}, u32[]{:S(2)}) collective-permute-start(bf16[2,64,512]{2,1,0:T(8,128)(2,1)S(1)} %get-tuple-element.35), channel_id=1, source_target_pairs={{0,5},{1,4},{2,7},{3,6},{4,1},{5,0},{6,3},{7,2},{8,13},{9,12},{10,... | collective-permute-start | bytes 393224 | tf_op jit(solution)/shard_map/ppermute | solution.py:500
  13.8 0.7 %collective-permute-start.5 = (bf16[4,128,128]{2,1,0:T(8,128)(2,1)S(1)}, bf16[4,128,128]{2,1,0:T(8,128)(2,1)S(1)}, u32[]{:S(2)}, u32[]{:S(2)}) collective-permute-start(bf16[4,128,128]{2,1,0:T(8,128)(2,1)S(1)} %shard_map.47.refs_0_), channel_id=1, source_target_pairs={{8,16},{16,8},{9,17},{17,9},{10,18},{18,10},{11,19},{19,11},{12,20... | collective-permute-start | bytes 393224 | tf_op jit(solution)/shard_map/ppermute | solution.py:481
  14.5 2.9 %collective-permute-start.3 = (bf16[4,128,128]{2,1,0:T(8,128)(2,1)S(1)}, bf16[4,128,128]{2,1,0:T(8,128)(2,1)S(1)}, u32[]{:S(2)}, u32[]{:S(2)}) collective-permute-start(bf16[4,128,128]{2,1,0:T(8,128)(2,1)S(1)} %shard_map.47.refs_0_), channel_id=1, source_target_pairs={{0,8},{8,0},{16,24},{24,16},{1,9},{9,1},{17,25},{25,17},{2,10},{10... | collective-permute-start | bytes 393224 | tf_op jit(solution)/shard_map/ppermute | solution.py:481
  17.5 1.3 %collective-permute-start.6 = (bf16[4,128,128]{2,1,0:T(8,128)(2,1)S(1)}, bf16[4,128,128]{2,1,0:T(8,128)(2,1)S(1)}, u32[]{:S(2)}, u32[]{:S(2)}) collective-permute-start(bf16[4,128,128]{2,1,0:T(8,128)(2,1)S(1)} %collective-permute-done.4.refs_2_), channel_id=1, source_target_pairs={{8,0},{16,24},{9,1},{17,25},{10,2},{18,26},{11,3},{19,27},{12,4},{... | collective-permute-start | bytes 393224 | tf_op jit(solution)/shard_map/ppermute | solution.py:481
  19.0 1.3 %collective-permute-start.10 = (bf16[64,256]{1,0:T(8,128)(2,1)S(1)}, bf16[64,256]{1,0:T(8,128)(2,1)S(1)}, u32[]{:S(2)}, u32[]{:S(2)}) collective-permute-start(bf16[64,256]{1,0:T(8,128)(2,1)S(1)} %get-tuple-element.38), channel_id=1, source_target_pairs={{8,0},{16,8},{24,16},{9,1},{17,9},{25,17},{10,2},{18,10},{26,18},{... | collective-permute-start | bytes 98312 | tf_op jit(solution)/shard_map/ppermute | solution.py:515
  20.3 4.4 %collective-permute-done.6.refs_4_ = bf16[4,128,128]{2,1,0:T(8,128)(2,1)S(1)} collective-permute-done((bf16[4,128,128]{2,1,0:T(8,128)(2,1)S(1)}, bf16[4,128,128]{2,1,0:T(8,128)(2,1)S(1)}, u32[]{:S(2)}, u32[]{:S(2)}) %collective-permute-start.6) | collective-permute-done | bytes 131104 | tf_op jit(solution)/shard_map/ppermute | solution.py:481
  24.7 1.5 %shard_map.50 = (f32[2,16,512]{2,1,0:T(8,128)S(1)}, bf16[256,1024]{1,0:T(8,128)(2,1)S(1)}, f32[16,128]{1,0:T(8,128)S(1)}, bf16[16,480]{1,0:T(8,128)(2,1)S(1)}, bf16[16,64]{1,0:T(8,128)(2,1)S(1)}) custom-call(bf16[4,128,128]{2,1,0:T(8,128)(2,1)S(1)} %shard_map.47.refs_0_, bf16[4,128,128]{2,1,0:T(8,128)(2,1)S(1)} %collective-permute-done.3.refs_1_, ...), custom_call_target="tpu_custom_call" | custom-call | flops 536870912 | bytes 524288 | tf_op jit(solution)/shard_map/pallas_call | solution.py:527
  26.3 1.9 %shard_map.51 = (f32[4,16,768]{2,1,0:T(8,128)S(1)}, f32[4,16,256]{2,1,0:T(8,128)S(1)}) custom-call(bf16[256,1024]{1,0:T(8,128)(2,1)S(1)} %get-tuple-element.37.left, bf16[64,4096]{1,0:T(8,128)(2,1)S(1)} %get-tuple-element.36.refs_6_.samples_ref, bf16[64,256]{1,0:T(8,128)(2,1)S(1)} %collective-permute-done.10.halo_ref, ...), custom_call_target="tpu_custom_call" | custom-call | flops 536870912 | bytes 524288 | tf_op jit(solution)/shard_map/pallas_call | solution.py:543
  28.2 2.5 %shard_map.52.keep_ref.after = f32[4,16,768]{2,1,0:T(8,128)S(1)} custom-call(bf16[256,1024]{1,0:T(8,128)(2,1)S(1)} %get-tuple-element.37.left, bf16[64,4096]{1,0:T(8,128)(2,1)S(1)} %get-tuple-element.36.refs_6_.samples_ref, bf16[64,256]{1,0:T(8,128)(2,1)S(1)} %collective-permute-done.10.halo_ref, f32[4,16,256]{2,1,0:T(8,128)S(1)} %get-tuple-element.41.edges_ref, ...), custom_call_target="tpu_custom_call" | custom-call | flops 1073741824 | bytes 524288 | tf_op jit(solution)/shard_map/pallas_call | solution.py:552
  30.8 1.9 %collective-permute-start.12 = (f32[16,768]{1,0:T(8,128)S(1)}, f32[16,768]{1,0:T(8,128)S(1)}, u32[]{:S(2)}, u32[]{:S(2)}) collective-permute-start(f32[16,768]{1,0:T(8,128)S(1)} %get-tuple-element.44), channel_id=1, source_target_pairs={{0,5},{1,4},{2,7},{3,6},{4,1},{5,0},{6,3},{7,2},{8,13},{9,12},{10,... | collective-permute-start | bytes 147464 | tf_op jit(solution)/shard_map/ppermute | solution.py:500
  32.8 1.2 %collective-permute-start.13 = (f32[16,768]{1,0:T(8,128)S(1)}, f32[16,768]{1,0:T(8,128)S(1)}, u32[]{:S(2)}, u32[]{:S(2)}) collective-permute-start(f32[16,768]{1,0:T(8,128)S(1)} %get-tuple-element.45), channel_id=1, source_target_pairs={{0,4},{1,5},{2,6},{3,7},{4,0},{5,1},{6,2},{7,3},{8,12},{9,13},{10,... | collective-permute-start | bytes 147464 | tf_op jit(solution)/shard_map/ppermute | solution.py:500
  33.9 0.4 %collective-permute-start.14 = (f32[16,768]{1,0:T(8,128)S(1)}, f32[16,768]{1,0:T(8,128)S(1)}, u32[]{:S(2)}, u32[]{:S(2)}) collective-permute-start(f32[16,768]{1,0:T(8,128)S(1)} %get-tuple-element.46), channel_id=1, source_target_pairs={{0,1},{1,0},{2,3},{3,2},{4,5},{5,4},{6,7},{7,6},{8,9},{9,8},{10,11... | collective-permute-start | bytes 147464 | tf_op jit(solution)/shard_map/ppermute | solution.py:500
  34.4 0.9 %shard_map.54.refs_4_ = f32[16,512]{1,0:T(8,128)S(1)} custom-call(bf16[480,512]{1,0:T(8,128)(2,1)S(1)} %copy-done, bf16[16,480]{1,0:T(8,128)(2,1)S(1)} %get-tuple-element.47.mask_ref, f32[4,16,768]{2,1,0:T(8,128)S(1)} %shard_map.52.keep_ref.after), custom_call_target="tpu_custom_call" | custom-call | flops 15728640 | bytes 491520 | tf_op jit(solution)/shard_map/pallas_call | solution.py:562
  35.2 0.7 %collective-permute-done.12.refs_1_ = f32[16,768]{1,0:T(8,128)S(1)} collective-permute-done((f32[16,768]{1,0:T(8,128)S(1)}, f32[16,768]{1,0:T(8,128)S(1)}, u32[]{:S(2)}, u32[]{:S(2)}) %collective-permute-start.12) | collective-permute-done | bytes 49184 | tf_op jit(solution)/shard_map/ppermute | solution.py:500
  35.9 1.0 %collective-permute-done.13.refs_2_ = f32[16,768]{1,0:T(8,128)S(1)} collective-permute-done((f32[16,768]{1,0:T(8,128)S(1)}, f32[16,768]{1,0:T(8,128)S(1)}, u32[]{:S(2)}, u32[]{:S(2)}) %collective-permute-start.13) | collective-permute-done | bytes 49184 | tf_op jit(solution)/shard_map/ppermute | solution.py:500
  37.0 1.0 %collective-permute-done.14.refs_3_ = f32[16,768]{1,0:T(8,128)S(1)} collective-permute-done((f32[16,768]{1,0:T(8,128)S(1)}, f32[16,768]{1,0:T(8,128)S(1)}, u32[]{:S(2)}, u32[]{:S(2)}) %collective-permute-start.14) | collective-permute-done | bytes 49184 | tf_op jit(solution)/shard_map/ppermute | solution.py:500
  38.0 0.7 %shard_map.55 = f32[16,512]{1,0:T(8,128)} custom-call(f32[16,768]{1,0:T(8,128)S(1)} %get-tuple-element.43.refs_0_, f32[16,768]{1,0:T(8,128)S(1)} %collective-permute-done.12.refs_1_, f32[16,768]{1,0:T(8,128)S(1)} %collective-permute-done.13.refs_2_, f32[16,768]{1,0:T(8,128)S(1)} %collective-permute-done.14.refs_3_, f32[16,512]{1,0:T(8,128)S(1)} %shard_map.54.refs_4_, ...), custom_call_target="tpu_custom_call" | custom-call | bytes 196608 | tf_op jit(solution)/shard_map/pallas_call | solution.py:576
  (20 shorter events, 0.7 us)
Async XLA Ops:
  1.7 3.2 %collective-permute-start = (bf16[1152,128]{1,0:T(8,128)(2,1)S(1)}, bf16[1152,128]{1,0:T(8,128)(2,1)S(1)}, u32[]{:S(2)}, u32[]{:S(2)}) collective-permute-start(bf16[1152,128]{1,0:T(8,128)(2,1)S(1)} %get-tuple-element.28), channel_id=1, source_target_pairs={{0,2},{2,0},{4,6},{6,4},{1,3},{3,1},{5,7},{7,5},{8,10},{10,8},{12,... | collective-permute-start | bytes 884744 | tf_op jit(solution)/shard_map/ppermute | solution.py:472
  2.2 4.6 %collective-permute-start.1 = (bf16[128,128]{1,0:T(8,128)(2,1)S(1)}, bf16[128,128]{1,0:T(8,128)(2,1)S(1)}, u32[]{:S(2)}, u32[]{:S(2)}) collective-permute-start(bf16[128,128]{1,0:T(8,128)(2,1)S(1)} %get-tuple-element.29), channel_id=1, source_target_pairs={{0,4},{2,6},{4,0},{6,2},{1,5},{3,7},{5,1},{7,3},{8,12},{10,14},{12... | collective-permute-start | bytes 98312 | tf_op jit(solution)/shard_map/ppermute | solution.py:472
  4.8 3.3 %collective-permute-start.2 = (bf16[128,128]{1,0:T(8,128)(2,1)S(1)}, bf16[128,128]{1,0:T(8,128)(2,1)S(1)}, u32[]{:S(2)}, u32[]{:S(2)}) collective-permute-start(bf16[128,128]{1,0:T(8,128)(2,1)S(1)} %get-tuple-element.30), channel_id=1, source_target_pairs={{0,6},{2,4},{4,2},{6,0},{1,7},{3,5},{5,3},{7,1},{8,14},{10,12},{12... | collective-permute-start | bytes 98312 | tf_op jit(solution)/shard_map/ppermute | solution.py:472
  5.0 9.5 %collective-permute-start.7 = (bf16[2,64,512]{2,1,0:T(8,128)(2,1)S(1)}, bf16[2,64,512]{2,1,0:T(8,128)(2,1)S(1)}, u32[]{:S(2)}, u32[]{:S(2)}) collective-permute-start(bf16[2,64,512]{2,1,0:T(8,128)(2,1)S(1)} %get-tuple-element.33), channel_id=1, source_target_pairs={{0,1},{1,0},{2,3},{3,2},{4,5},{5,4},{6,7},{7,6},{8,9},{9,8},{10,11... | collective-permute-start | bytes 393224 | tf_op jit(solution)/shard_map/ppermute | solution.py:500
  8.2 9.3 %collective-permute-start.4 = (bf16[4,128,128]{2,1,0:T(8,128)(2,1)S(1)}, bf16[4,128,128]{2,1,0:T(8,128)(2,1)S(1)}, u32[]{:S(2)}, u32[]{:S(2)}) collective-permute-start(bf16[4,128,128]{2,1,0:T(8,128)(2,1)S(1)} %shard_map.47.refs_0_), channel_id=1, source_target_pairs={{0,16},{16,0},{8,24},{24,8},{1,17},{17,1},{9,25},{25,9},{2,18},{18... | collective-permute-start | bytes 393224 | tf_op jit(solution)/shard_map/ppermute | solution.py:481
  10.8 8.1 %collective-permute-start.8 = (bf16[2,64,512]{2,1,0:T(8,128)(2,1)S(1)}, bf16[2,64,512]{2,1,0:T(8,128)(2,1)S(1)}, u32[]{:S(2)}, u32[]{:S(2)}) collective-permute-start(bf16[2,64,512]{2,1,0:T(8,128)(2,1)S(1)} %get-tuple-element.34), channel_id=1, source_target_pairs={{0,4},{1,5},{2,6},{3,7},{4,0},{5,1},{6,2},{7,3},{8,12},{9,13},{10,... | collective-permute-start | bytes 393224 | tf_op jit(solution)/shard_map/ppermute | solution.py:500
  11.7 7.2 %collective-permute-start.9 = (bf16[2,64,512]{2,1,0:T(8,128)(2,1)S(1)}, bf16[2,64,512]{2,1,0:T(8,128)(2,1)S(1)}, u32[]{:S(2)}, u32[]{:S(2)}) collective-permute-start(bf16[2,64,512]{2,1,0:T(8,128)(2,1)S(1)} %get-tuple-element.35), channel_id=1, source_target_pairs={{0,5},{1,4},{2,7},{3,6},{4,1},{5,0},{6,3},{7,2},{8,13},{9,12},{10,... | collective-permute-start | bytes 393224 | tf_op jit(solution)/shard_map/ppermute | solution.py:500
  13.8 6.5 %collective-permute-start.5 = (bf16[4,128,128]{2,1,0:T(8,128)(2,1)S(1)}, bf16[4,128,128]{2,1,0:T(8,128)(2,1)S(1)}, u32[]{:S(2)}, u32[]{:S(2)}) collective-permute-start(bf16[4,128,128]{2,1,0:T(8,128)(2,1)S(1)} %shard_map.47.refs_0_), channel_id=1, source_target_pairs={{8,16},{16,8},{9,17},{17,9},{10,18},{18,10},{11,19},{19,11},{12,20... | collective-permute-start | bytes 393224 | tf_op jit(solution)/shard_map/ppermute | solution.py:481
  14.5 5.9 %collective-permute-start.3 = (bf16[4,128,128]{2,1,0:T(8,128)(2,1)S(1)}, bf16[4,128,128]{2,1,0:T(8,128)(2,1)S(1)}, u32[]{:S(2)}, u32[]{:S(2)}) collective-permute-start(bf16[4,128,128]{2,1,0:T(8,128)(2,1)S(1)} %shard_map.47.refs_0_), channel_id=1, source_target_pairs={{0,8},{8,0},{16,24},{24,16},{1,9},{9,1},{17,25},{25,17},{2,10},{10... | collective-permute-start | bytes 393224 | tf_op jit(solution)/shard_map/ppermute | solution.py:481
  17.5 7.2 %collective-permute-start.6 = (bf16[4,128,128]{2,1,0:T(8,128)(2,1)S(1)}, bf16[4,128,128]{2,1,0:T(8,128)(2,1)S(1)}, u32[]{:S(2)}, u32[]{:S(2)}) collective-permute-start(bf16[4,128,128]{2,1,0:T(8,128)(2,1)S(1)} %collective-permute-done.4.refs_2_), channel_id=1, source_target_pairs={{8,0},{16,24},{9,1},{17,25},{10,2},{18,26},{11,3},{19,27},{12,4},{... | collective-permute-start | bytes 393224 | tf_op jit(solution)/shard_map/ppermute | solution.py:481
  19.0 5.7 %copy-start.1 = (s32[480]{0:T(512)S(1)}, s32[480]{0:T(512)}, u32[]{:S(2)}) copy-start(s32[480]{0:T(512)} %param.7) | copy-start | bytes 5764
  19.0 7.2 %collective-permute-start.10 = (bf16[64,256]{1,0:T(8,128)(2,1)S(1)}, bf16[64,256]{1,0:T(8,128)(2,1)S(1)}, u32[]{:S(2)}, u32[]{:S(2)}) collective-permute-start(bf16[64,256]{1,0:T(8,128)(2,1)S(1)} %get-tuple-element.38), channel_id=1, source_target_pairs={{8,0},{16,8},{24,16},{9,1},{17,9},{25,17},{10,2},{18,10},{26,18},{... | collective-permute-start | bytes 98312 | tf_op jit(solution)/shard_map/ppermute | solution.py:515
  28.1 2.6 %collective-permute-start.11 = (f32[4,16,768]{2,1,0:T(8,128)S(1)}, f32[4,16,768]{2,1,0:T(8,128)S(1)}, u32[]{:S(2)}, u32[]{:S(2)}) collective-permute-start(f32[4,16,768]{2,1,0:T(8,128)S(1)} %get-tuple-element.42.after), channel_id=1, source_target_pairs={{0,2},{2,0},{4,6},{6,4},{1,3},{3,1},{5,7},{7,5},{8,10},{10,8},{12,... | collective-permute-start | bytes 589832 | tf_op jit(solution)/shard_map/ppermute | solution.py:561
  28.2 6.1 %copy-start = (bf16[480,512]{1,0:T(8,128)(2,1)S(1)}, bf16[480,512]{1,0:T(8,128)(2,1)}, u32[]{:S(2)}) copy-start(bf16[480,512]{1,0:T(8,128)(2,1)} %wave_ref.1) | copy-start | bytes 1474564
  30.8 5.1 %collective-permute-start.12 = (f32[16,768]{1,0:T(8,128)S(1)}, f32[16,768]{1,0:T(8,128)S(1)}, u32[]{:S(2)}, u32[]{:S(2)}) collective-permute-start(f32[16,768]{1,0:T(8,128)S(1)} %get-tuple-element.44), channel_id=1, source_target_pairs={{0,5},{1,4},{2,7},{3,6},{4,1},{5,0},{6,3},{7,2},{8,13},{9,12},{10,... | collective-permute-start | bytes 147464 | tf_op jit(solution)/shard_map/ppermute | solution.py:500
  32.8 4.2 %collective-permute-start.13 = (f32[16,768]{1,0:T(8,128)S(1)}, f32[16,768]{1,0:T(8,128)S(1)}, u32[]{:S(2)}, u32[]{:S(2)}) collective-permute-start(f32[16,768]{1,0:T(8,128)S(1)} %get-tuple-element.45), channel_id=1, source_target_pairs={{0,4},{1,5},{2,6},{3,7},{4,0},{5,1},{6,2},{7,3},{8,12},{9,13},{10,... | collective-permute-start | bytes 147464 | tf_op jit(solution)/shard_map/ppermute | solution.py:500
  33.9 4.1 %collective-permute-start.14 = (f32[16,768]{1,0:T(8,128)S(1)}, f32[16,768]{1,0:T(8,128)S(1)}, u32[]{:S(2)}, u32[]{:S(2)}) collective-permute-start(f32[16,768]{1,0:T(8,128)S(1)} %get-tuple-element.46), channel_id=1, source_target_pairs={{0,1},{1,0},{2,3},{3,2},{4,5},{5,4},{6,7},{7,6},{8,9},{9,8},{10,11... | collective-permute-start | bytes 147464 | tf_op jit(solution)/shard_map/ppermute | solution.py:500

commit v25 on v23

--- a/solution.py
+++ b/solution.py
@@ -321,12 +321,8 @@
             edges_ref[y * run + tm] = edges[(2 * y + core) * run + tm]
 
 
-def last_dots_kernel(left, samples_ref, halo_ref, edges_ref, after, keep_ref, *scratch):
+def last_dots_kernel(left, full, edges_ref, after, keep_ref, shifts, products):
     del after
-    full, shifts, products = scratch
-    chunk = samples_ref.shape[1]
-    full[:, :chunk] = samples_ref[...]
-    full[:, chunk:] = halo_ref[...]
     core = lax.rem(lax.axis_index("inner"), 2)
     run = keep_ref.shape[0] // 2
     slab = keep_ref.shape[2] - edges_ref.shape[2]
@@ -537,25 +533,28 @@
         bytes_accessed=part * chunk * 2,
         vmem=36,
     )(*tpls, order_row, samples)
-    full = pltpu.VMEM((part, chunk + window), BF16)
-    send, edges = call(
+    send, edges, full = call(
         middle_dots_kernel,
         [VMEM] * 5,
-        [sds((half, count, slab + window), F32), sds((half, count, window), F32)],
-        [full, pltpu.VMEM((group, count, window), F32)] + scratch(),
+        [
+            sds((half, count, slab + window), F32),
+            sds((half, count, window), F32),
+            sds((part, chunk + window), BF16),
+        ],
+        [pltpu.VMEM((group, count, window), F32)] + scratch(),
         flops=work // 2,
         bytes_accessed=part * chunk * 2,
         vmem=36,
     )(left, samples, halo, begun, mask_part)
     keep = call(
         last_dots_kernel,
-        [VMEM] * 4 + [AFTER],
+        [VMEM] * 3 + [AFTER],
         sds((half, count, slab + window), F32),
-        [full] + scratch(),
+        scratch(),
         flops=work,
         bytes_accessed=part * chunk * 2,
         vmem=36,
-    )(left, samples, halo, edges, send)
+    )(left, full, edges, send)
     got = lax.ppermute(send, "inner", [(b, b ^ 1) for b in range(INNER)])
     power = call(
         functools.partial(power_kernel, window),

time: 38.7 us -> 38.7 us (level)
  no operation moved by 1% of the time
where the time goes in v25:
time: 38.7 us; the launch traced here: 38.5 us
  starting transfers between devices  20.3 us (52%)
  Pallas kernels  9.11 us (24%)
  waiting for transfers between devices  8.93 us (23%)
    ppermute x6, starting transfers between devices, swap(): return lax.ppermute(part, every, route)  8.27 us
    ppermute x4, starting transfers between devices, cross(): return lax.ppermute(part, 'outer', route)  7.48 us
    ppermute x4, waiting for transfers between devices, cross(): return lax.ppermute(part, 'outer', route)  4.57 us
    ppermute x3, starting transfers between devices, plane(): return lax.ppermute(part, 'inner', [(b, b ^ flip) for b in range(INNER)])  3.18 us
    ppermute x6, waiting for transfers between devices, swap(): return lax.ppermute(part, every, route)  2.92 us
    pallas_call x1, Pallas kernels, on_device(): call(last_dots_kernel, [VMEM] * 3 + [AFTER], sds((half, count, slab + win...  2.32 us
    pallas_call x1, Pallas kernels, on_device(): call(middle_dots_kernel, [VMEM] * 5, [sds((half, count, slab + window), F...  1.86 us
    pallas_call x1, Pallas kernels, on_device(): call(functools.partial(prologue_kernel, tm_count), [HBM] * 4, [sds((padde...  1.7 us
  transfers between devices with their start and end apart: 15, of which 8 were waited for; matrix products, arithmetic and copies ran while one was open for 0% of the time, Pallas kernels for 13%

profile of v25, /device:TPU:0, one launch (start us, length us, event | category | flops | bytes accessed | tf_op | source)
XLA Modules:
  0.0 38.5 jit_solution(3765745525850438536)
XLA Ops:
  0.0 1.7 %shard_map.46 = (bf16[1152,128]{1,0:T(8,128)(2,1)S(1)}, bf16[256,512]{1,0:T(8,128)(2,1)S(1)}, bf16[128,128]{1,0:T(8,128)(2,1)S(1)}, bf16[128,128]{1,0:T(8,128)(2,1)S(1)}, bf16[128,128]{1,0:T(8,128)(2,1)S(1)}) custom-call(bf16[480,512]{1,0:T(8,128)(2,1)} %wave_ref.1, bf16[1,480,256]{2,1,0:T(8,128)(2,1)} %tpl_hbm.1, s32[1,160]{1,0:T(1,128)} %flag_hbm.1, ...), custom_call_target="tpu_custom_call" | custom-call | bytes 737280 | tf_op jit(solution)/shard_map/pallas_call | solution.py:444
  1.7 0.5 %collective-permute-start = (bf16[1152,128]{1,0:T(8,128)(2,1)S(1)}, bf16[1152,128]{1,0:T(8,128)(2,1)S(1)}, u32[]{:S(2)}, u32[]{:S(2)}) collective-permute-start(bf16[1152,128]{1,0:T(8,128)(2,1)S(1)} %get-tuple-element.29), channel_id=1, source_target_pairs={{0,2},{2,0},{4,6},{6,4},{1,3},{3,1},{5,7},{7,5},{8,10},{10,8},{12,... | collective-permute-start | bytes 884744 | tf_op jit(solution)/shard_map/ppermute | solution.py:466
  2.2 2.6 %collective-permute-start.1 = (bf16[128,128]{1,0:T(8,128)(2,1)S(1)}, bf16[128,128]{1,0:T(8,128)(2,1)S(1)}, u32[]{:S(2)}, u32[]{:S(2)}) collective-permute-start(bf16[128,128]{1,0:T(8,128)(2,1)S(1)} %get-tuple-element.30), channel_id=1, source_target_pairs={{0,4},{2,6},{4,0},{6,2},{1,5},{3,7},{5,1},{7,3},{8,12},{10,14},{12... | collective-permute-start | bytes 98312 | tf_op jit(solution)/shard_map/ppermute | solution.py:466
  5.0 1.8 %collective-permute-start.7 = (bf16[2,64,512]{2,1,0:T(8,128)(2,1)S(1)}, bf16[2,64,512]{2,1,0:T(8,128)(2,1)S(1)}, u32[]{:S(2)}, u32[]{:S(2)}) collective-permute-start(bf16[2,64,512]{2,1,0:T(8,128)(2,1)S(1)} %get-tuple-element.34), channel_id=1, source_target_pairs={{0,1},{1,0},{2,3},{3,2},{4,5},{5,4},{6,7},{7,6},{8,9},{9,8},{10,11... | collective-permute-start | bytes 393224 | tf_op jit(solution)/shard_map/ppermute | solution.py:494
  6.8 1.4 %collective-permute-done.2.both_ref = bf16[128,128]{1,0:T(8,128)(2,1)S(1)} collective-permute-done((bf16[128,128]{1,0:T(8,128)(2,1)S(1)}, bf16[128,128]{1,0:T(8,128)(2,1)S(1)}, u32[]{:S(2)}, u32[]{:S(2)}) %collective-permute-start.2) | collective-permute-done | bytes 32800 | tf_op jit(solution)/shard_map/ppermute | solution.py:466
  8.2 2.7 %collective-permute-start.4 = (bf16[4,128,128]{2,1,0:T(8,128)(2,1)S(1)}, bf16[4,128,128]{2,1,0:T(8,128)(2,1)S(1)}, u32[]{:S(2)}, u32[]{:S(2)}) collective-permute-start(bf16[4,128,128]{2,1,0:T(8,128)(2,1)S(1)} %shard_map.47.refs_0_), channel_id=1, source_target_pairs={{0,16},{16,0},{8,24},{24,8},{1,17},{17,1},{9,25},{25,9},{2,18},{18... | collective-permute-start | bytes 393224 | tf_op jit(solution)/shard_map/ppermute | solution.py:475
  10.8 0.9 %collective-permute-start.8 = (bf16[2,64,512]{2,1,0:T(8,128)(2,1)S(1)}, bf16[2,64,512]{2,1,0:T(8,128)(2,1)S(1)}, u32[]{:S(2)}, u32[]{:S(2)}) collective-permute-start(bf16[2,64,512]{2,1,0:T(8,128)(2,1)S(1)} %get-tuple-element.35), channel_id=1, source_target_pairs={{0,4},{1,5},{2,6},{3,7},{4,0},{5,1},{6,2},{7,3},{8,12},{9,13},{10,... | collective-permute-start | bytes 393224 | tf_op jit(solution)/shard_map/ppermute | solution.py:494
  11.7 2.1 %collective-permute-start.9 = (bf16[2,64,512]{2,1,0:T(8,128)(2,1)S(1)}, bf16[2,64,512]{2,1,0:T(8,128)(2,1)S(1)}, u32[]{:S(2)}, u32[]{:S(2)}) collective-permute-start(bf16[2,64,512]{2,1,0:T(8,128)(2,1)S(1)} %get-tuple-element.36), channel_id=1, source_target_pairs={{0,5},{1,4},{2,7},{3,6},{4,1},{5,0},{6,3},{7,2},{8,13},{9,12},{10,... | collective-permute-start | bytes 393224 | tf_op jit(solution)/shard_map/ppermute | solution.py:494
  13.8 0.7 %collective-permute-start.5 = (bf16[4,128,128]{2,1,0:T(8,128)(2,1)S(1)}, bf16[4,128,128]{2,1,0:T(8,128)(2,1)S(1)}, u32[]{:S(2)}, u32[]{:S(2)}) collective-permute-start(bf16[4,128,128]{2,1,0:T(8,128)(2,1)S(1)} %shard_map.47.refs_0_), channel_id=1, source_target_pairs={{8,16},{16,8},{9,17},{17,9},{10,18},{18,10},{11,19},{19,11},{12,20... | collective-permute-start | bytes 393224 | tf_op jit(solution)/shard_map/ppermute | solution.py:475
  14.5 2.9 %collective-permute-start.3 = (bf16[4,128,128]{2,1,0:T(8,128)(2,1)S(1)}, bf16[4,128,128]{2,1,0:T(8,128)(2,1)S(1)}, u32[]{:S(2)}, u32[]{:S(2)}) collective-permute-start(bf16[4,128,128]{2,1,0:T(8,128)(2,1)S(1)} %shard_map.47.refs_0_), channel_id=1, source_target_pairs={{0,8},{8,0},{16,24},{24,16},{1,9},{9,1},{17,25},{25,17},{2,10},{10... | collective-permute-start | bytes 393224 | tf_op jit(solution)/shard_map/ppermute | solution.py:475
  17.5 1.3 %collective-permute-start.6 = (bf16[4,128,128]{2,1,0:T(8,128)(2,1)S(1)}, bf16[4,128,128]{2,1,0:T(8,128)(2,1)S(1)}, u32[]{:S(2)}, u32[]{:S(2)}) collective-permute-start(bf16[4,128,128]{2,1,0:T(8,128)(2,1)S(1)} %collective-permute-done.4.refs_2_), channel_id=1, source_target_pairs={{8,0},{16,24},{9,1},{17,25},{10,2},{18,26},{11,3},{19,27},{12,4},{... | collective-permute-start | bytes 393224 | tf_op jit(solution)/shard_map/ppermute | solution.py:475
  19.0 1.3 %collective-permute-start.10 = (bf16[64,256]{1,0:T(8,128)(2,1)S(1)}, bf16[64,256]{1,0:T(8,128)(2,1)S(1)}, u32[]{:S(2)}, u32[]{:S(2)}) collective-permute-start(bf16[64,256]{1,0:T(8,128)(2,1)S(1)} %get-tuple-element.39), channel_id=1, source_target_pairs={{8,0},{16,8},{24,16},{9,1},{17,9},{25,17},{10,2},{18,10},{26,18},{... | collective-permute-start | bytes 98312 | tf_op jit(solution)/shard_map/ppermute | solution.py:509
  20.3 4.4 %collective-permute-done.6.refs_4_ = bf16[4,128,128]{2,1,0:T(8,128)(2,1)S(1)} collective-permute-done((bf16[4,128,128]{2,1,0:T(8,128)(2,1)S(1)}, bf16[4,128,128]{2,1,0:T(8,128)(2,1)S(1)}, u32[]{:S(2)}, u32[]{:S(2)}) %collective-permute-start.6) | collective-permute-done | bytes 131104 | tf_op jit(solution)/shard_map/ppermute | solution.py:475
  24.7 1.5 %shard_map.50 = (f32[2,16,512]{2,1,0:T(8,128)S(1)}, bf16[256,1024]{1,0:T(8,128)(2,1)S(1)}, f32[16,128]{1,0:T(8,128)S(1)}, bf16[16,480]{1,0:T(8,128)(2,1)S(1)}, bf16[16,64]{1,0:T(8,128)(2,1)S(1)}) custom-call(bf16[4,128,128]{2,1,0:T(8,128)(2,1)S(1)} %shard_map.47.refs_0_, bf16[4,128,128]{2,1,0:T(8,128)(2,1)S(1)} %collective-permute-done.3.refs_1_, ...), custom_call_target="tpu_custom_call" | custom-call | flops 536870912 | bytes 524288 | tf_op jit(solution)/shard_map/pallas_call | solution.py:521
  26.3 1.9 %shard_map.51 = (f32[4,16,768]{2,1,0:T(8,128)S(1)}, f32[4,16,256]{2,1,0:T(8,128)S(1)}, bf16[64,4352]{1,0:T(8,128)(2,1)S(1)}) custom-call(bf16[256,1024]{1,0:T(8,128)(2,1)S(1)} %get-tuple-element.38.left, bf16[64,4096]{1,0:T(8,128)(2,1)S(1)} %get-tuple-element.37.refs_6_.samples_ref, bf16[64,256]{1,0:T(8,128)(2,1)S(1)} %collective-permute-done.10.halo_ref, ...), custom_call_target="tpu_custom_call" | custom-call | flops 536870912 | bytes 524288 | tf_op jit(solution)/shard_map/pallas_call | solution.py:536
  28.2 2.3 %shard_map.52.keep_ref.after = f32[4,16,768]{2,1,0:T(8,128)S(1)} custom-call(bf16[256,1024]{1,0:T(8,128)(2,1)S(1)} %get-tuple-element.38.left, bf16[64,4352]{1,0:T(8,128)(2,1)S(1)} %get-tuple-element.42.full, f32[4,16,256]{2,1,0:T(8,128)S(1)} %get-tuple-element.43.edges_ref, f32[4,16,768]{2,1,0:T(8,128)S(1)} %get-tuple-element.44.after), custom_call_target="tpu_custom_call" | custom-call | flops 1073741824 | bytes 524288 | tf_op jit(solution)/shard_map/pallas_call | solution.py:549
  30.6 2.0 %collective-permute-start.12 = (f32[16,768]{1,0:T(8,128)S(1)}, f32[16,768]{1,0:T(8,128)S(1)}, u32[]{:S(2)}, u32[]{:S(2)}) collective-permute-start(f32[16,768]{1,0:T(8,128)S(1)} %get-tuple-element.46), channel_id=1, source_target_pairs={{0,5},{1,4},{2,7},{3,6},{4,1},{5,0},{6,3},{7,2},{8,13},{9,12},{10,... | collective-permute-start | bytes 147464 | tf_op jit(solution)/shard_map/ppermute | solution.py:494
  32.6 1.2 %collective-permute-start.13 = (f32[16,768]{1,0:T(8,128)S(1)}, f32[16,768]{1,0:T(8,128)S(1)}, u32[]{:S(2)}, u32[]{:S(2)}) collective-permute-start(f32[16,768]{1,0:T(8,128)S(1)} %get-tuple-element.47), channel_id=1, source_target_pairs={{0,4},{1,5},{2,6},{3,7},{4,0},{5,1},{6,2},{7,3},{8,12},{9,13},{10,... | collective-permute-start | bytes 147464 | tf_op jit(solution)/shard_map/ppermute | solution.py:494
  33.7 0.4 %collective-permute-start.14 = (f32[16,768]{1,0:T(8,128)S(1)}, f32[16,768]{1,0:T(8,128)S(1)}, u32[]{:S(2)}, u32[]{:S(2)}) collective-permute-start(f32[16,768]{1,0:T(8,128)S(1)} %get-tuple-element.48), channel_id=1, source_target_pairs={{0,1},{1,0},{2,3},{3,2},{4,5},{5,4},{6,7},{7,6},{8,9},{9,8},{10,11... | collective-permute-start | bytes 147464 | tf_op jit(solution)/shard_map/ppermute | solution.py:494
  34.1 0.9 %shard_map.54.refs_4_ = f32[16,512]{1,0:T(8,128)S(1)} custom-call(bf16[480,512]{1,0:T(8,128)(2,1)S(1)} %copy-done, bf16[16,480]{1,0:T(8,128)(2,1)S(1)} %get-tuple-element.49.mask_ref, f32[4,16,768]{2,1,0:T(8,128)S(1)} %shard_map.52.keep_ref.after), custom_call_target="tpu_custom_call" | custom-call | flops 15728640 | bytes 491520 | tf_op jit(solution)/shard_map/pallas_call | solution.py:559
  35.0 0.7 %collective-permute-done.12.refs_1_ = f32[16,768]{1,0:T(8,128)S(1)} collective-permute-done((f32[16,768]{1,0:T(8,128)S(1)}, f32[16,768]{1,0:T(8,128)S(1)}, u32[]{:S(2)}, u32[]{:S(2)}) %collective-permute-start.12) | collective-permute-done | bytes 49184 | tf_op jit(solution)/shard_map/ppermute | solution.py:494
  35.7 1.0 %collective-permute-done.13.refs_2_ = f32[16,768]{1,0:T(8,128)S(1)} collective-permute-done((f32[16,768]{1,0:T(8,128)S(1)}, f32[16,768]{1,0:T(8,128)S(1)}, u32[]{:S(2)}, u32[]{:S(2)}) %collective-permute-start.13) | collective-permute-done | bytes 49184 | tf_op jit(solution)/shard_map/ppermute | solution.py:494
  36.7 1.1 %collective-permute-done.14.refs_3_ = f32[16,768]{1,0:T(8,128)S(1)} collective-permute-done((f32[16,768]{1,0:T(8,128)S(1)}, f32[16,768]{1,0:T(8,128)S(1)}, u32[]{:S(2)}, u32[]{:S(2)}) %collective-permute-start.14) | collective-permute-done | bytes 49184 | tf_op jit(solution)/shard_map/ppermute | solution.py:494
  37.8 0.7 %shard_map.55 = f32[16,512]{1,0:T(8,128)} custom-call(f32[16,768]{1,0:T(8,128)S(1)} %get-tuple-element.45.refs_0_, f32[16,768]{1,0:T(8,128)S(1)} %collective-permute-done.12.refs_1_, f32[16,768]{1,0:T(8,128)S(1)} %collective-permute-done.13.refs_2_, f32[16,768]{1,0:T(8,128)S(1)} %collective-permute-done.14.refs_3_, f32[16,512]{1,0:T(8,128)S(1)} %shard_map.54.refs_4_, ...), custom_call_target="tpu_custom_call" | custom-call | bytes 196608 | tf_op jit(solution)/shard_map/pallas_call | solution.py:573
  (20 shorter events, 0.7 us)
Async XLA Ops:
  1.7 3.2 %collective-permute-start = (bf16[1152,128]{1,0:T(8,128)(2,1)S(1)}, bf16[1152,128]{1,0:T(8,128)(2,1)S(1)}, u32[]{:S(2)}, u32[]{:S(2)}) collective-permute-start(bf16[1152,128]{1,0:T(8,128)(2,1)S(1)} %get-tuple-element.29), channel_id=1, source_target_pairs={{0,2},{2,0},{4,6},{6,4},{1,3},{3,1},{5,7},{7,5},{8,10},{10,8},{12,... | collective-permute-start | bytes 884744 | tf_op jit(solution)/shard_map/ppermute | solution.py:466
  2.2 4.6 %collective-permute-start.1 = (bf16[128,128]{1,0:T(8,128)(2,1)S(1)}, bf16[128,128]{1,0:T(8,128)(2,1)S(1)}, u32[]{:S(2)}, u32[]{:S(2)}) collective-permute-start(bf16[128,128]{1,0:T(8,128)(2,1)S(1)} %get-tuple-element.30), channel_id=1, source_target_pairs={{0,4},{2,6},{4,0},{6,2},{1,5},{3,7},{5,1},{7,3},{8,12},{10,14},{12... | collective-permute-start | bytes 98312 | tf_op jit(solution)/shard_map/ppermute | solution.py:466
  4.8 3.3 %collective-permute-start.2 = (bf16[128,128]{1,0:T(8,128)(2,1)S(1)}, bf16[128,128]{1,0:T(8,128)(2,1)S(1)}, u32[]{:S(2)}, u32[]{:S(2)}) collective-permute-start(bf16[128,128]{1,0:T(8,128)(2,1)S(1)} %get-tuple-element.31), channel_id=1, source_target_pairs={{0,6},{2,4},{4,2},{6,0},{1,7},{3,5},{5,3},{7,1},{8,14},{10,12},{12... | collective-permute-start | bytes 98312 | tf_op jit(solution)/shard_map/ppermute | solution.py:466
  5.0 9.5 %collective-permute-start.7 = (bf16[2,64,512]{2,1,0:T(8,128)(2,1)S(1)}, bf16[2,64,512]{2,1,0:T(8,128)(2,1)S(1)}, u32[]{:S(2)}, u32[]{:S(2)}) collective-permute-start(bf16[2,64,512]{2,1,0:T(8,128)(2,1)S(1)} %get-tuple-element.34), channel_id=1, source_target_pairs={{0,1},{1,0},{2,3},{3,2},{4,5},{5,4},{6,7},{7,6},{8,9},{9,8},{10,11... | collective-permute-start | bytes 393224 | tf_op jit(solution)/shard_map/ppermute | solution.py:494
  8.2 9.3 %collective-permute-start.4 = (bf16[4,128,128]{2,1,0:T(8,128)(2,1)S(1)}, bf16[4,128,128]{2,1,0:T(8,128)(2,1)S(1)}, u32[]{:S(2)}, u32[]{:S(2)}) collective-permute-start(bf16[4,128,128]{2,1,0:T(8,128)(2,1)S(1)} %shard_map.47.refs_0_), channel_id=1, source_target_pairs={{0,16},{16,0},{8,24},{24,8},{1,17},{17,1},{9,25},{25,9},{2,18},{18... | collective-permute-start | bytes 393224 | tf_op jit(solution)/shard_map/ppermute | solution.py:475
  10.8 8.1 %collective-permute-start.8 = (bf16[2,64,512]{2,1,0:T(8,128)(2,1)S(1)}, bf16[2,64,512]{2,1,0:T(8,128)(2,1)S(1)}, u32[]{:S(2)}, u32[]{:S(2)}) collective-permute-start(bf16[2,64,512]{2,1,0:T(8,128)(2,1)S(1)} %get-tuple-element.35), channel_id=1, source_target_pairs={{0,4},{1,5},{2,6},{3,7},{4,0},{5,1},{6,2},{7,3},{8,12},{9,13},{10,... | collective-permute-start | bytes 393224 | tf_op jit(solution)/shard_map/ppermute | solution.py:494
  11.7 7.2 %collective-permute-start.9 = (bf16[2,64,512]{2,1,0:T(8,128)(2,1)S(1)}, bf16[2,64,512]{2,1,0:T(8,128)(2,1)S(1)}, u32[]{:S(2)}, u32[]{:S(2)}) collective-permute-start(bf16[2,64,512]{2,1,0:T(8,128)(2,1)S(1)} %get-tuple-element.36), channel_id=1, source_target_pairs={{0,5},{1,4},{2,7},{3,6},{4,1},{5,0},{6,3},{7,2},{8,13},{9,12},{10,... | collective-permute-start | bytes 393224 | tf_op jit(solution)/shard_map/ppermute | solution.py:494
  13.8 6.5 %collective-permute-start.5 = (bf16[4,128,128]{2,1,0:T(8,128)(2,1)S(1)}, bf16[4,128,128]{2,1,0:T(8,128)(2,1)S(1)}, u32[]{:S(2)}, u32[]{:S(2)}) collective-permute-start(bf16[4,128,128]{2,1,0:T(8,128)(2,1)S(1)} %shard_map.47.refs_0_), channel_id=1, source_target_pairs={{8,16},{16,8},{9,17},{17,9},{10,18},{18,10},{11,19},{19,11},{12,20... | collective-permute-start | bytes 393224 | tf_op jit(solution)/shard_map/ppermute | solution.py:475
  14.5 5.9 %collective-permute-start.3 = (bf16[4,128,128]{2,1,0:T(8,128)(2,1)S(1)}, bf16[4,128,128]{2,1,0:T(8,128)(2,1)S(1)}, u32[]{:S(2)}, u32[]{:S(2)}) collective-permute-start(bf16[4,128,128]{2,1,0:T(8,128)(2,1)S(1)} %shard_map.47.refs_0_), channel_id=1, source_target_pairs={{0,8},{8,0},{16,24},{24,16},{1,9},{9,1},{17,25},{25,17},{2,10},{10... | collective-permute-start | bytes 393224 | tf_op jit(solution)/shard_map/ppermute | solution.py:475
  17.5 7.2 %collective-permute-start.6 = (bf16[4,128,128]{2,1,0:T(8,128)(2,1)S(1)}, bf16[4,128,128]{2,1,0:T(8,128)(2,1)S(1)}, u32[]{:S(2)}, u32[]{:S(2)}) collective-permute-start(bf16[4,128,128]{2,1,0:T(8,128)(2,1)S(1)} %collective-permute-done.4.refs_2_), channel_id=1, source_target_pairs={{8,0},{16,24},{9,1},{17,25},{10,2},{18,26},{11,3},{19,27},{12,4},{... | collective-permute-start | bytes 393224 | tf_op jit(solution)/shard_map/ppermute | solution.py:475
  19.0 5.7 %copy-start.1 = (s32[480]{0:T(512)S(1)}, s32[480]{0:T(512)}, u32[]{:S(2)}) copy-start(s32[480]{0:T(512)} %param.7) | copy-start | bytes 5764
  19.0 7.2 %collective-permute-start.10 = (bf16[64,256]{1,0:T(8,128)(2,1)S(1)}, bf16[64,256]{1,0:T(8,128)(2,1)S(1)}, u32[]{:S(2)}, u32[]{:S(2)}) collective-permute-start(bf16[64,256]{1,0:T(8,128)(2,1)S(1)} %get-tuple-element.39), channel_id=1, source_target_pairs={{8,0},{16,8},{24,16},{9,1},{17,9},{25,17},{10,2},{18,10},{26,18},{... | collective-permute-start | bytes 98312 | tf_op jit(solution)/shard_map/ppermute | solution.py:509
  28.1 2.4 %collective-permute-start.11 = (f32[4,16,768]{2,1,0:T(8,128)S(1)}, f32[4,16,768]{2,1,0:T(8,128)S(1)}, u32[]{:S(2)}, u32[]{:S(2)}) collective-permute-start(f32[4,16,768]{2,1,0:T(8,128)S(1)} %get-tuple-element.44.after), channel_id=1, source_target_pairs={{0,2},{2,0},{4,6},{6,4},{1,3},{3,1},{5,7},{7,5},{8,10},{10,8},{12,... | collective-permute-start | bytes 589832 | tf_op jit(solution)/shard_map/ppermute | solution.py:558
  28.2 6.0 %copy-start = (bf16[480,512]{1,0:T(8,128)(2,1)S(1)}, bf16[480,512]{1,0:T(8,128)(2,1)}, u32[]{:S(2)}) copy-start(bf16[480,512]{1,0:T(8,128)(2,1)} %wave_ref.1) | copy-start | bytes 1474564
  30.6 5.1 %collective-permute-start.12 = (f32[16,768]{1,0:T(8,128)S(1)}, f32[16,768]{1,0:T(8,128)S(1)}, u32[]{:S(2)}, u32[]{:S(2)}) collective-permute-start(f32[16,768]{1,0:T(8,128)S(1)} %get-tuple-element.46), channel_id=1, source_target_pairs={{0,5},{1,4},{2,7},{3,6},{4,1},{5,0},{6,3},{7,2},{8,13},{9,12},{10,... | collective-permute-start | bytes 147464 | tf_op jit(solution)/shard_map/ppermute | solution.py:494
  32.6 4.2 %collective-permute-start.13 = (f32[16,768]{1,0:T(8,128)S(1)}, f32[16,768]{1,0:T(8,128)S(1)}, u32[]{:S(2)}, u32[]{:S(2)}) collective-permute-start(f32[16,768]{1,0:T(8,128)S(1)} %get-tuple-element.47), channel_id=1, source_target_pairs={{0,4},{1,5},{2,6},{3,7},{4,0},{5,1},{6,2},{7,3},{8,12},{9,13},{10,... | collective-permute-start | bytes 147464 | tf_op jit(solution)/shard_map/ppermute | solution.py:494
  33.7 4.1 %collective-permute-start.14 = (f32[16,768]{1,0:T(8,128)S(1)}, f32[16,768]{1,0:T(8,128)S(1)}, u32[]{:S(2)}, u32[]{:S(2)}) collective-permute-start(f32[16,768]{1,0:T(8,128)S(1)} %get-tuple-element.48), channel_id=1, source_target_pairs={{0,1},{1,0},{2,3},{3,2},{4,5},{5,4},{6,7},{7,6},{8,9},{9,8},{10,11... | collective-permute-start | bytes 147464 | tf_op jit(solution)/shard_map/ppermute | solution.py:494
